TPU v7x, 32 devices: a whole 2x2x4 slice. The times are simulated.
32 devices in a mesh: parts: 2 (over y), cells: 4 (over z), blk: 4 (over x, core).
Axes of the slice: x: 2, y: 2, z: 4, core: 2. Of those that a mesh axis runs over, the one named last changes fastest.
Arguments:
- expression: bfloat16 [4096, 4096], P(('parts', 'cells'), 'blk'), parts along dimension 0, may hold values from 0.02 to 36, as said below
- cell_type: int32 [4096], P(('parts', 'cells')), parts along dimension 0, may hold values from 0 to 3, as said below
- size_factor: bfloat16 [4096], P(('parts', 'cells')), parts along dimension 0, may hold values from 0.19921875 to 5
- gene_mean: float32 [8192], P(('parts', 'blk')), parts along dimension 0, may hold values from 0.2 to 3
Outputs:
- correlation: bfloat16 [8, 4096, 4096], P(('parts', 'cells'), 'blk'), parts along dimension 0
There are 2 independent parts, one for each index of `parts`. A program takes and returns all parts, laid end to end along the dimension named above; each array names one. Nothing has to cross between parts.
Inputs may be any that keep to these rules, and one draw needn't show every extreme that they name: `cell_type`: each storage shard of 512 cells in a row holds at most 256 cells of one type and at least one cell of every type; one type has exactly 256 cells in every shard. `expression`: positive levels.
All inputs are finite; a program needn't handle non-finite values.
Results may differ from a plain program's by a relative error of at most 0.0027.
Values may be sent and summed in bfloat16 or wider, within the bound.
No kernel may reach another device: no remote copies, remote signals or barrier semaphores. Data moves between devices by JAX's collectives and lax.ppermute only.
A program may use at most 128 MiB of HBM per device.

v0:
```python
import jax
import jax.numpy as jnp
from jax import lax
from jax.sharding import PartitionSpec as P

dispersion = 100.0
epsilon = 1e-05


def standardize(values, factors, gene_mean, is_valid):
    live = is_valid[:, None]
    expected = jnp.where(live, factors[:, None] * gene_mean[None, :], 1.0)
    residual = jnp.where(
        live,
        (values.astype(jnp.float32) - expected)
        / jnp.sqrt(expected + expected * expected / dispersion),
        0.0,
    )
    live_count = jnp.sum(is_valid.astype(jnp.float32))
    center = jnp.sum(residual, axis=0) / live_count
    centered = jnp.where(live, residual - center[None, :], 0.0)
    spread = jnp.sum(centered * centered, axis=0) / live_count
    scaled = (centered * lax.rsqrt(spread + epsilon)[None, :]).astype(jnp.bfloat16)
    return (scaled, live_count)


def cross_gram(left_panel, right_panel):
    return lax.dot_general(
        left_panel, right_panel, (((0,), (0,)), ((), ())), preferred_element_type=jnp.float32
    )


def shards(expression, cell_type, size_factor, gene_mean):
    type_count = lax.axis_size("cells")
    shard_rows, panel_width = expression.shape
    capacity = 2 * shard_rows // type_count
    one_hot = (cell_type[:, None] == jnp.arange(type_count, dtype=jnp.int32)[None, :]).astype(
        jnp.int32
    )
    slot_rank = jnp.sum(jnp.cumsum(one_hot, axis=0) * one_hot, axis=1) - 1
    target = cell_type * capacity + slot_rank
    slot_total = type_count * capacity
    send_values = (
        jnp.zeros((slot_total, panel_width), jnp.bfloat16)
        .at[target]
        .set(expression)
        .reshape(type_count, capacity, panel_width)
    )
    send_factors = (
        jnp.zeros((slot_total,), jnp.bfloat16)
        .at[target]
        .set(size_factor)
        .reshape(type_count, capacity)
    )
    got_values, got_factors = (
        lax.all_to_all(send_values, "cells", split_axis=0, concat_axis=0, tiled=True),
        lax.all_to_all(send_factors, "cells", split_axis=0, concat_axis=0, tiled=True),
    )
    values = got_values.reshape(slot_total, panel_width)
    factors = got_factors.reshape(slot_total).astype(jnp.float32)
    scaled, live_count = standardize(values, factors, gene_mean, factors > 0.0)
    full_gram = cross_gram(scaled, lax.all_gather(scaled, "blk", axis=1, tiled=True))
    full_row = (full_gram / live_count).astype(jnp.bfloat16)
    return full_row[None]


def solution(mesh):
    placed = (
        P(("parts", "cells"), "blk"),
        P(("parts", "cells")),
        P(("parts", "cells")),
        P(("parts", "blk")),
    )
    return jax.shard_map(
        shards,
        mesh=mesh,
        in_specs=placed,
        out_specs=P(("parts", "cells"), "blk", None),
        check_vma=False,
    )
```

profile of v0, /device:TPU:0, one launch (start us, length us, event | category | flops | bytes accessed | tf_op | source)
XLA Modules:
  0.0 168.5 jit_solution(392267317657151299)
XLA Ops:
  6.5 0.0 copy-start
  6.5 0.7 fusion.12
  7.2 1.2 reduce-window.6
  8.4 0.2 slice_reduce_fusion
  8.7 0.2 reduce-window.9
  8.8 0.1 add_bitcast_fusion
  8.9 0.7 fusion.11
  9.6 0.7 compare_select_fusion
  10.3 3.9 %scatter_custom_fusion = bf16[1024]{0:T(1024)(128)(2,1)S(1)} fusion(s32[512]{0:T(512)S(1)} %compare_select_fusion, bf16[512]{0:T(512)(128)(2,1)} %param.6, bf16[]{:T(256)} %constant.9.clone.1), kind=kCustom, calls=%fused_computation.31 | custom fusion | bytes 2560 | tf_op jit(solution)/shard_map/scatter | solution.py:52
  14.3 0.5 broadcast.90
  14.8 0.7 reduce.5
  15.4 0.6 reshape.129
  16.0 6.3 %all-to-all-start = ((bf16[4,2,128]{2,1,0:T(2,128)(2,1)}), bf16[4,2,128]{2,1,0:T(2,128)(2,1)S(1)}, u32[]{:S(2)}, u32[]{:S(2)}) async-start(bf16[4,2,128]{2,1,0:T(2,128)(2,1)} %reshape.129), calls=%async_computation | async-start | bytes 4096 | tf_op jit(solution)/shard_map/all_to_all | solution.py:57
  22.4 4.8 %scatter_custom_fusion.1 = bf16[1024,1024]{1,0:T(8,128)(2,1)} fusion(s32[512]{0:T(512)S(1)} %compare_select_fusion, bf16[512,1024]{1,0:T(8,128)(2,1)} %param.4, bf16[]{:T(256)} %constant.9.clone.1), kind=kCustom, calls=%fused_computation.14 | custom fusion | bytes 2097664 | tf_op jit(solution)/shard_map/scatter | solution.py:46
  27.1 0.6 all-to-all-done
  27.8 4.5 %all-to-all-start.1 = ((bf16[4,256,1024]{2,1,0:T(8,128)(2,1)}), bf16[4,256,1024]{2,1,0:T(8,128)(2,1)S(1)}, u32[]{:S(2)}, u32[]{:S(2)}) async-start(bf16[4,256,1024]{2,1,0:T(8,128)(2,1)} %bitcast.44), calls=%async_computation.1 | async-start | bytes 4194304 | tf_op jit(solution)/shard_map/all_to_all | solution.py:56
  32.2 0.0 all-gather.2.cloned.1.call-start
  32.3 0.7 convert_reduce_fusion
  32.9 46.9 %all-to-all-done.1 = bf16[4,256,1024]{2,1,0:T(8,128)(2,1)S(1)} async-done(((bf16[4,256,1024]{2,1,0:T(8,128)(2,1)}), bf16[4,256,1024]{2,1,0:T(8,128)(2,1)S(1)}, u32[]{:S(2)}, u32[]{:S(2)}) %all-to-all-start.1) | async-done | bytes 2097184 | tf_op jit(solution)/shard_map/all_to_all | solution.py:56
  79.9 0.0 copy-done
  79.9 1.7 %fusion.7 = f32[1024]{0:T(1024)S(1)} fusion(f32[1024]{0:T(1024)S(1)} %copy-done, f32[4,256]{1,0:T(4,128)S(1)} %bitcast.47, pred[4,256]{1,0:T(4,128)(4,1)S(1)} %get-tuple-element.6, bf16[4,256,1024]{2,1,0:T(8,128)(2,1)S(1)} %all-to-all-done.1), kind=kLoop, calls=%fused_computation.13 | loop fusion | flops 10484736 | bytes 2110464 | tf_op jit(solution)/shard_map/reduce_sum | solution.py:20
  81.6 0.7 broadcast_divide_fusion
  82.3 2.1 %multiply_reduce_fusion = f32[1024]{0:T(1024)S(1)} fusion(f32[1024]{0:T(1024)S(1)} %broadcast_divide_fusion, pred[4,256]{1,0:T(4,128)(4,1)S(1)} %get-tuple-element.6, f32[1024]{0:T(1024)S(1)} %copy-done, f32[4,256]{1,0:T(4,128)S(1)} %bitcast.48, bf16[4,256,1024]{2,1,0:T(8,128)(2,1)S(1)} %all-to-all-done.1), kind=kLoop, calls=%fused_computation.11 | loop fusion | flops 13630464 | bytes 2114560 | tf_op jit(solution)/shard_map/reduce_sum | solution.py:22
  84.4 0.7 add_rsqrt_fusion
  85.1 3.4 %fusion.6 = bf16[1024,1024]{1,0:T(8,128)(2,1)} fusion(f32[1024]{0:T(1024)S(1)} %add_rsqrt_fusion, f32[1024]{0:T(1024)S(1)} %broadcast_divide_fusion, f32[1024]{0:T(1024)S(1)} %copy-done, f32[1024]{0:T(1024)S(1)} %bitcast.46, pred[1024]{0:T(1024)(128)(4,1)S(1)} %broadcast_compare_fusion.1, bf16[4,256,1024]{2,1,0:T(8,128)(2,1)S(1)} %all-to-all-done.1), kind=kLoop, calls=%fused_computation.10 | loop fusion | flops 13631488 | bytes 4211712 | tf_op jit(solution)/shard_map/convert_element_type | solution.py:23
  88.5 0.0 all-gather.2.cloned.1.call-update
  88.5 57.5 %all-gather.2.cloned.1.call-done = bf16[1024,4096]{1,0:T(8,128)(2,1)} async-done(((bf16[1024,1024]{1,0:T(8,128)(2,1)}), bf16[1024,4096]{1,0:T(8,128)(2,1)}) %all-gather.2.cloned.1.call-update) | async-done | bytes 8388624 | tf_op jit(solution)/shard_map/all_gather | solution.py:62
  146.1 15.6 %fusion = bf16[1,1024,4096]{2,1,0:T(8,128)(2,1)} fusion(f32[]{:T(128)} %get-tuple-element.5, bf16[1024,1024]{1,0:T(8,128)(2,1)} %fusion.6, bf16[1024,4096]{1,0:T(8,128)(2,1)} %all-gather.2.cloned.1.call-done), kind=kOutput, calls=%fused_computation.3 | convolution fusion | flops 8598323200 | bytes 18874372 | tf_op jit(solution)/shard_map/dot_general | solution.py:28
  (5 shorter events, 0.0 us)
Async XLA Ops:
  6.5 73.3 %copy-start = (f32[1024]{0:T(1024)S(1)}, f32[1024]{0:T(1024)}, u32[]{:S(2)}) copy-start(f32[1024]{0:T(1024)} %param.7) | copy-start | bytes 12292
  16.0 11.7 %all-to-all-start = ((bf16[4,2,128]{2,1,0:T(2,128)(2,1)}), bf16[4,2,128]{2,1,0:T(2,128)(2,1)S(1)}, u32[]{:S(2)}, u32[]{:S(2)}) async-start(bf16[4,2,128]{2,1,0:T(2,128)(2,1)} %reshape.129), calls=%async_computation | async-start | bytes 4096 | tf_op jit(solution)/shard_map/all_to_all | solution.py:57
  27.8 52.1 %all-to-all-start.1 = ((bf16[4,256,1024]{2,1,0:T(8,128)(2,1)}), bf16[4,256,1024]{2,1,0:T(8,128)(2,1)S(1)}, u32[]{:S(2)}, u32[]{:S(2)}) async-start(bf16[4,256,1024]{2,1,0:T(8,128)(2,1)} %bitcast.44), calls=%async_computation.1 | async-start | bytes 4194304 | tf_op jit(solution)/shard_map/all_to_all | solution.py:56
  32.2 113.8 %all-gather.2.cloned.1.call-start = ((), (), s32[]{:S(2)}) async-start(), calls=%async_computation.2 | async-start | bytes 10485760 | tf_op jit(solution)/shard_map/all_gather | solution.py:62
Sparse Core Ops, SparseCore 0:
  88.6 57.3 all-gather.1
where the time goes:
time: 169 us; the launch traced here: 168 us
  waiting for transfers between devices  105 us (62%)
  matrix products  15.6 us (9%)
  other arithmetic  13.5 us (8%)
  between operations  13.5 us (8%)
  starting transfers between devices  10.8 us (6%)
  local copies, waits for them, and re-layouts  10.1 us (6%)
    all_gather x1, waiting for transfers between devices, shards(): lax.all_gather(scaled, 'blk', axis=1, tiled=True)  57.5 us
    all_to_all x1, waiting for transfers between devices, shards(): lax.all_to_all(send_values, 'cells', split_axis=0, concat_axis=0, tiled=T...  46.9 us
    dot_general x1, matrix products, cross_gram(): lax.dot_general(left_panel, right_panel, (((0,), (0,)), ((), ())), prefer...  15.6 us
    all_to_all x1, starting transfers between devices, shards(): lax.all_to_all(send_factors, 'cells', split_axis=0, concat_axis=0, tiled=...  6.32 us
    scatter x1, local copies, waits for them, and re-layouts, shards(): send_values = jnp.zeros((slot_total, panel_width), jnp.bfloat16).at[targe...  4.79 us
    all_to_all x1, starting transfers between devices, shards(): lax.all_to_all(send_values, 'cells', split_axis=0, concat_axis=0, tiled=T...  4.49 us
    scatter x1, local copies, waits for them, and re-layouts, shards(): send_factors = jnp.zeros((slot_total,), jnp.bfloat16).at[target].set(size...  3.92 us
    convert_element_type x1, other arithmetic, standardize(): (centered * lax.rsqrt(spread + epsilon)[None, :]).astype(jnp.bfloat16)  3.4 us
  transfers between devices with their start and end apart: 3, of which 3 were waited for; matrix products, arithmetic and copies ran while one was open for 3% of the time, Pallas kernels for 0%

commit v1 on v0

v1 whole, which is shorter than its diff:
```python
import functools

import jax
import jax.numpy as jnp
from jax import lax
from jax.experimental import pallas as pl
from jax.experimental.pallas import tpu as pltpu
from jax.sharding import PartitionSpec as P

dispersion = 100.0
epsilon = 1e-05
TILE = 16
VMEM = 48 * 1024 * 1024

whole = pl.BlockSpec(memory_space=pltpu.VMEM)


def pack_kernel(types, cap, widths, home_ref, type_ref, factor_ref, expr_ref, *outs):
    rows = expr_ref.shape[0]
    home = home_ref[0]
    kind = type_ref[...]
    rel = jnp.where(kind >= home, kind - home, kind - home + types)
    lines = max(types, 8)
    hot = lax.broadcasted_iota(jnp.int32, (lines, rows), 0) == rel
    hot_f = jnp.where(hot, 1.0, 0.0)
    upper = jnp.where(
        lax.broadcasted_iota(jnp.int32, (rows, rows), 0)
        <= lax.broadcasted_iota(jnp.int32, (rows, rows), 1),
        1.0,
        0.0,
    ).astype(jnp.bfloat16)
    running = jnp.dot(hot_f.astype(jnp.bfloat16), upper, preferred_element_type=jnp.float32)
    rank = jnp.sum(hot_f * running, axis=0, keepdims=True) - 1.0
    slot = rel * cap + rank.astype(jnp.int32)
    factor = jnp.broadcast_to(factor_ref[...].astype(jnp.float32), (TILE, rows)).astype(
        jnp.bfloat16
    )
    values = expr_ref[...]
    for j in range(types):
        place = jnp.where(
            lax.broadcasted_iota(jnp.int32, (cap, rows), 0) + j * cap == slot, 1.0, 0.0
        ).astype(jnp.bfloat16)
        block = jnp.dot(place, values, preferred_element_type=jnp.float32).astype(jnp.bfloat16)
        start = 0
        for k, width in enumerate(widths):
            outs[k * types + j][0:cap, :] = block[:, start : start + width]
            start += width
        line = lax.dot_general(
            factor, place, (((1,), (1,)), ((), ())), preferred_element_type=jnp.float32
        )
        row = lax.broadcasted_iota(jnp.int32, (TILE, 1), 0)
        width = widths[0]
        tail = jnp.zeros((TILE, min(width, cap)), jnp.float32)
        for i in range(pl.cdiv(cap, width)):
            tail = jnp.where(row == i, line[:, i * width : min((i + 1) * width, cap)], tail)
        outs[j][cap : cap + TILE, 0 : min(width, cap)] = tail.astype(jnp.bfloat16)


def pack(types, cap, widths, home, cell_type, size_factor, expression):
    rows = expression.shape[0]
    shapes = [
        jax.ShapeDtypeStruct((cap + (TILE if k == 0 else 0), width), jnp.bfloat16)
        for k, width in enumerate(widths)
        for _ in range(types)
    ]
    flat = pl.pallas_call(
        functools.partial(pack_kernel, types, cap, widths),
        out_shape=shapes,
        in_specs=[pl.BlockSpec(memory_space=pltpu.SMEM), whole, whole, whole],
        out_specs=[whole] * len(shapes),
        compiler_params=pltpu.CompilerParams(vmem_limit_bytes=VMEM),
        cost_estimate=pl.CostEstimate(
            flops=2 * types * cap * rows * expression.shape[1],
            bytes_accessed=3 * types * cap * expression.shape[1],
            transcendentals=0,
        ),
        name="pack",
    )(home, cell_type.reshape(1, rows), size_factor.reshape(1, rows), expression)
    return [flat[k * types : (k + 1) * types] for k in range(len(widths))]


def standardize_kernel(types, cap, lead, separate, mean_ref, *refs):
    blocks = refs[:types]
    tails = refs[types : 2 * types] if separate else blocks
    base = 0 if separate else cap
    refs = refs[2 * types :] if separate else refs[types:]
    scaled_ref, turned_ref, count_ref, work = refs
    mean = mean_ref[...]
    width = mean.shape[1]
    piece = min(lead, cap)
    total = jnp.zeros((1, width), jnp.float32)
    count = jnp.zeros((1, 1), jnp.float32)
    alive = []
    for j in range(types):
        column = jnp.zeros((cap, 1), jnp.float32)
        for i in range(pl.cdiv(cap, lead)):
            line = tails[j][base : base + TILE, 0:piece].astype(jnp.float32)[i : i + 1, :]
            diagonal = (
                lax.broadcasted_iota(jnp.int32, (cap, piece), 0)
                == lax.broadcasted_iota(jnp.int32, (cap, piece), 1) + i * lead
            )
            column += jnp.sum(jnp.where(diagonal, line, 0.0), axis=1, keepdims=True)
        live = column > 0.0
        alive.append(live)
        count += jnp.sum(jnp.where(live, 1.0, 0.0), axis=0, keepdims=True)
        expected = jnp.where(live, column * mean, 1.0)
        values = blocks[j][0:cap, :].astype(jnp.float32)
        residual = jnp.where(
            live,
            (values - expected) * lax.rsqrt(expected + expected * expected * (1.0 / dispersion)),
            0.0,
        )
        work[j * cap : (j + 1) * cap, :] = residual
        total += jnp.sum(residual, axis=0, keepdims=True)
    center = total / count
    square = jnp.zeros((1, width), jnp.float32)
    for j in range(types):
        centered = jnp.where(alive[j], work[j * cap : (j + 1) * cap, :] - center, 0.0)
        work[j * cap : (j + 1) * cap, :] = centered
        square += jnp.sum(centered * centered, axis=0, keepdims=True)
    scale = lax.rsqrt(square / count + epsilon)
    for j in range(types):
        scaled = work[j * cap : (j + 1) * cap, :] * scale
        scaled_ref[j * cap : (j + 1) * cap, :] = scaled.astype(jnp.bfloat16)
        work[j * cap : (j + 1) * cap, :] = scaled
    turned_ref[...] = jnp.transpose(work[...]).astype(jnp.bfloat16)
    count_ref[...] = jnp.broadcast_to(count, count_ref.shape)


def standardize(types, cap, lead, mean, blocks, first):
    width = mean.shape[1]
    separate = first is not blocks
    slots = types * cap
    specs = [whole] * (1 + types)
    args = [mean, *blocks]
    if separate:
        specs += [pl.BlockSpec((TILE, lead), lambda i: (cap // TILE, 0))] * types
        args += list(first)
    return pl.pallas_call(
        functools.partial(standardize_kernel, types, cap, lead, separate),
        grid=(1,),
        out_shape=[
            jax.ShapeDtypeStruct((slots, width), jnp.bfloat16),
            jax.ShapeDtypeStruct((width, slots), jnp.bfloat16),
            jax.ShapeDtypeStruct((8, 128), jnp.float32),
        ],
        in_specs=specs,
        out_specs=[whole] * 3,
        scratch_shapes=[pltpu.VMEM((slots, width), jnp.float32)],
        compiler_params=pltpu.CompilerParams(vmem_limit_bytes=VMEM),
        cost_estimate=pl.CostEstimate(
            flops=20 * slots * width,
            bytes_accessed=6 * slots * width,
            transcendentals=slots * width,
        ),
        name="standardize",
    )(*args)


def gram_kernel(parts, panels, aliased, place_ref, count_ref, *refs):
    left = refs[:parts]
    right = refs[parts : parts + panels]
    out_ref = refs[parts + panels + (1 if aliased else 0)]
    inverse = 1.0 / count_ref[0:1, 0:1]
    step = pl.program_id(0)
    for j in range(panels):

        @pl.when(step == j)
        def _(j=j):
            start = 0
            for piece in left:
                size = piece.shape[0]
                product = jnp.dot(piece[...], right[j][...], preferred_element_type=jnp.float32)
                out_ref[0, start : start + size, :] = (product * inverse).astype(jnp.bfloat16)
                start += size


def gram(shape, places, count, left, right, before):
    rows, columns = shape[1:]
    width = right[0].shape[1]
    slots = right[0].shape[0]
    aliased = before is not None
    args = [places, count, *left, *right] + ([before] if aliased else [])
    hold = pl.BlockSpec(memory_space=pltpu.VMEM)
    specs = [hold] * (1 + len(left) + len(right))
    specs += [pl.BlockSpec(memory_space=pl.ANY)] if aliased else []
    return pl.pallas_call(
        functools.partial(gram_kernel, len(left), len(right), aliased),
        grid_spec=pltpu.PrefetchScalarGridSpec(
            num_scalar_prefetch=1,
            grid=(len(right),),
            in_specs=specs,
            out_specs=pl.BlockSpec((1, rows, width), lambda i, place: (0, 0, place[i])),
        ),
        out_shape=jax.ShapeDtypeStruct(shape, jnp.bfloat16),
        input_output_aliases={len(args) - 1: 0} if aliased else {},
        compiler_params=pltpu.CompilerParams(vmem_limit_bytes=VMEM),
        cost_estimate=pl.CostEstimate(
            flops=2 * slots * rows * width * len(right),
            bytes_accessed=2 * (slots + rows) * width * len(right) + 2 * slots * rows,
            transcendentals=0,
        ),
        name="gram",
    )(*args)


def shards(expression, cell_type, size_factor, gene_mean):
    types = lax.axis_size("cells")
    blocks = lax.axis_size("blk")
    shard_rows, panel = expression.shape
    cap = 2 * shard_rows // types
    width = 256
    widths = [width] * (panel // width)
    chunks = len(widths)
    home = lax.axis_index("cells").astype(jnp.int32)
    me = lax.axis_index("blk").astype(jnp.int32)
    cores = 2
    chips = blocks // cores

    packed = pack(types, cap, widths, home[None], cell_type, size_factor, expression)

    def shift(block, by):
        return lax.ppermute(block, "cells", [(s, (s + by) % types) for s in range(types)])

    def across(panel_, by):
        return lax.ppermute(panel_, "blk", [(b, (b + by * cores) % blocks) for b in range(blocks)])

    def sibling(panel_):
        return lax.ppermute(panel_, "blk", [(b, b ^ 1) for b in range(blocks)])

    arrived = [
        [packed[k][0]] + [shift(packed[k][j], j) for j in range(1, types)] for k in range(chunks)
    ]
    mean = gene_mean.reshape(1, panel)
    left, panels, count = [], [], None
    for k in range(chunks):
        own, turned, count = standardize(
            types, cap, width, mean[:, k * width : (k + 1) * width], arrived[k], arrived[0]
        )
        left.append(turned)
        near = [own] + [across(own, d) for d in range(1, chips)]
        panels.append(near + [sibling(p) for p in near])

    out = None
    shape = (1, panel, panel * blocks)
    for k in range(chunks):
        sources = [(me + blocks - d * cores) % blocks for d in range(chips)]
        sources += [s ^ 1 for s in sources]
        places = jnp.stack(sources) * chunks + k
        out = gram(shape, places.astype(jnp.int32), count, left, panels[k], out)
    return out


def solution(mesh):
    placed = (
        P(("parts", "cells"), "blk"),
        P(("parts", "cells")),
        P(("parts", "cells")),
        P(("parts", "blk")),
    )
    return jax.shard_map(
        shards,
        mesh=mesh,
        in_specs=placed,
        out_specs=P(("parts", "cells"), "blk", None),
        check_vma=False,
    )
```

time: 169 us -> 112 us (0.66)
  waiting for transfers between devices: 105 us -> 31.8 us
  starting transfers between devices: 10.8 us -> 43.4 us
  Pallas kernels: 0 us -> 30.1 us
  matrix products: 15.6 us -> 0 us
  between operations: 13.5 us -> 0.05 us
  other arithmetic: 13.5 us -> 0.08 us
  local copies, waits for them, and re-layouts: 10.1 us -> 5.15 us
    all_gather x1 -> x0, waiting for transfers between devices: 57.5 us -> none  [shards(): lax.all_gather(scaled, 'blk', axis=1, tiled=True)]
    all_to_all x2 -> x0, waiting for transfers between devices: 47.5 us -> none  [the longest x1 46.9 us: shards(): lax.all_to_all(send_values, 'cells', split_axis=0, concat_axis=0, tiled=T...]
    ppermute x0 -> x24, starting transfers between devices: none -> 43.4 us  [the longest x12 37.3 us: shift(): lax.ppermute(block, 'cells', [(s, (s + by) % types) for s in range(types)])]
    ppermute x0 -> x24, waiting for transfers between devices: none -> 31.8 us  [the longest x4 27.2 us: across(): lax.ppermute(panel_, 'blk', [(b, (b + by * cores) % blocks) for b in rang...]
    pallas_call x0 -> x9, Pallas kernels: none -> 30.1 us  [the longest x4 22.3 us: gram(): pl.pallas_call(functools.partial(gram_kernel, len(left), len(right), alia...]
    dot_general x1 -> x0, matrix products: 15.6 us -> none  [cross_gram(): lax.dot_general(left_panel, right_panel, (((0,), (0,)), ((), ())), prefer...]
    all_to_all x2 -> x0, starting transfers between devices: 10.8 us -> none  [the longest x1 6.32 us: shards(): lax.all_to_all(send_factors, 'cells', split_axis=0, concat_axis=0, tiled=...]
    scatter x2 -> x0, local copies, waits for them, and re-layouts: 8.71 us -> none  [the longest x1 4.79 us: shards(): send_values = jnp.zeros((slot_total, panel_width), jnp.bfloat16).at[targe...]
  transfers between devices with their start and end apart: 3 -> 24, of which waited for: 3 -> 6; matrix products, arithmetic and copies ran while one was open for 3% -> 1% of each run, Pallas kernels for 0% -> 21%
where the time goes in v1:
time: 112 us; the launch traced here: 111 us
  starting transfers between devices  43.4 us (39%)
  waiting for transfers between devices  31.8 us (28%)
  Pallas kernels  30.1 us (27%)
  local copies, waits for them, and re-layouts  5.15 us (5%)
    ppermute x12, starting transfers between devices, shift(): lax.ppermute(block, 'cells', [(s, (s + by) % types) for s in range(types)])  37.3 us
    ppermute x4, waiting for transfers between devices, across(): lax.ppermute(panel_, 'blk', [(b, (b + by * cores) % blocks) for b in rang...  27.2 us
    pallas_call x4, Pallas kernels, gram(): pl.pallas_call(functools.partial(gram_kernel, len(left), len(right), alia...  22.3 us
    pallas_call x4, Pallas kernels, standardize(): pl.pallas_call(functools.partial(standardize_kernel, types, cap, lead, se...  6.17 us
    ppermute x4, starting transfers between devices, across(): lax.ppermute(panel_, 'blk', [(b, (b + by * cores) % blocks) for b in rang...  5.02 us
    ppermute x12, waiting for transfers between devices, shift(): lax.ppermute(block, 'cells', [(s, (s + by) % types) for s in range(types)])  4.53 us
    unnamed x8, local copies, waits for them, and re-layouts  3.74 us
  transfers between devices with their start and end apart: 24, of which 6 were waited for; matrix products, arithmetic and copies ran while one was open for 1% of the time, Pallas kernels for 21%

profile of v1, /device:TPU:0, one launch (start us, length us, event | category | flops | bytes accessed | tf_op | source)
XLA Modules:
  0.0 110.6 jit_solution(4824674286680450272)
XLA Ops:
  0.0 0.7 reshape.11.factor_ref
  0.7 1.2 %copy-done.2 = bf16[512,1024]{1,0:T(8,128)(2,1)S(1)} copy-done((bf16[512,1024]{1,0:T(8,128)(2,1)S(1)}, bf16[512,1024]{1,0:T(8,128)(2,1)}, u32[]{:S(2)}) %copy-start.2) | copy-done | bytes 1048600
  1.9 0.7 copy-done.3
  2.6 1.7 %pack.1 = (bf16[272,256]{1,0:T(8,128)(2,1)S(1)}, bf16[272,256]{1,0:T(8,128)(2,1)S(1)}, bf16[272,256]{1,0:T(8,128)(2,1)S(1)}, bf16[272,256]{1,0:T(8,128)(2,1)S(1)...) custom-call(s32[1]{0:T(128)} %bitcast.5.home_ref, ...), custom_call_target="tpu_custom_call" | custom-call | flops 1073741824 | bytes 3145728 | tf_op jit(solution)/shard_map/pack/pallas_call | solution.py:66
  4.3 3.1 %collective-permute-start.3 = (bf16[272,256]{1,0:T(8,128)(2,1)S(1)}, bf16[272,256]{1,0:T(8,128)(2,1)S(1)}, u32[]{:S(2)}, u32[]{:S(2)}) collective-permute-start(bf16[272,256]{1,0:T(8,128)(2,1)S(1)} %get-tuple-element.35), channel_id=1, source_target_pairs={{0,4},{4,8},{8,12},{12,0},{1,5},{5,9},{9,13},{13,1},{2,6},{6,10},{... | collective-permute-start | bytes 417800 | tf_op jit(solution)/shard_map/ppermute | solution.py:223
  7.4 2.6 %collective-permute-start.4 = (bf16[272,256]{1,0:T(8,128)(2,1)S(1)}, bf16[272,256]{1,0:T(8,128)(2,1)S(1)}, u32[]{:S(2)}, u32[]{:S(2)}) collective-permute-start(bf16[272,256]{1,0:T(8,128)(2,1)S(1)} %get-tuple-element.36), channel_id=1, source_target_pairs={{0,8},{4,12},{8,0},{12,4},{1,9},{5,13},{9,1},{13,5},{2,10},{6,14},... | collective-permute-start | bytes 417800 | tf_op jit(solution)/shard_map/ppermute | solution.py:223
  10.0 1.4 %collective-permute-start.5 = (bf16[272,256]{1,0:T(8,128)(2,1)S(1)}, bf16[272,256]{1,0:T(8,128)(2,1)S(1)}, u32[]{:S(2)}, u32[]{:S(2)}) collective-permute-start(bf16[272,256]{1,0:T(8,128)(2,1)S(1)} %get-tuple-element.37), channel_id=1, source_target_pairs={{0,12},{4,0},{8,4},{12,8},{1,13},{5,1},{9,5},{13,9},{2,14},{6,2},{... | collective-permute-start | bytes 417800 | tf_op jit(solution)/shard_map/ppermute | solution.py:223
  11.3 0.2 collective-permute-start.10
  11.5 2.8 %collective-permute-start.11 = (bf16[256,256]{1,0:T(8,128)(2,1)S(1)}, bf16[256,256]{1,0:T(8,128)(2,1)S(1)}, u32[]{:S(2)}, u32[]{:S(2)}) collective-permute-start(bf16[256,256]{1,0:T(8,128)(2,1)S(1)} %get-tuple-element.48), channel_id=1, source_target_pairs={{0,12},{4,0},{8,4},{12,8},{1,13},{5,1},{9,5},{13,9},{2,14},{6,2},{... | collective-permute-start | bytes 393224 | tf_op jit(solution)/shard_map/ppermute | solution.py:223
  14.4 10.2 %collective-permute-start.9 = (bf16[256,256]{1,0:T(8,128)(2,1)S(1)}, bf16[256,256]{1,0:T(8,128)(2,1)S(1)}, u32[]{:S(2)}, u32[]{:S(2)}) collective-permute-start(bf16[256,256]{1,0:T(8,128)(2,1)S(1)} %get-tuple-element.46), channel_id=1, source_target_pairs={{0,4},{4,8},{8,12},{12,0},{1,5},{5,9},{9,13},{13,1},{2,6},{6,10},{... | collective-permute-start | bytes 393224 | tf_op jit(solution)/shard_map/ppermute | solution.py:223
  24.5 0.0 collective-permute-done.4.refs_6_.refs_2_
  24.5 3.1 %collective-permute-start.6 = (bf16[256,256]{1,0:T(8,128)(2,1)S(1)}, bf16[256,256]{1,0:T(8,128)(2,1)S(1)}, u32[]{:S(2)}, u32[]{:S(2)}) collective-permute-start(bf16[256,256]{1,0:T(8,128)(2,1)S(1)} %get-tuple-element.41), channel_id=1, source_target_pairs={{0,4},{4,8},{8,12},{12,0},{1,5},{5,9},{9,13},{13,1},{2,6},{6,10},{... | collective-permute-start | bytes 393224 | tf_op jit(solution)/shard_map/ppermute | solution.py:223
  27.7 0.7 fusion
  28.4 0.0 collective-permute-done.5.refs_7_.refs_3_
  28.4 1.4 %standardize.5 = (bf16[1024,256]{1,0:T(8,128)(2,1)S(1)}, bf16[256,1024]{1,0:T(8,128)(2,1)S(1)}, f32[8,128]{1,0:T(8,128)}) custom-call(f32[1,256]{1,0:T(1,128)S(1)} %get-tuple-element.59.mean_ref, bf16[272,256]{1,0:T(8,128)(2,1)S(1)} %get-tuple-element.34.refs_4_.refs_0_, bf16[272,256]{1,0:T(8,128)(2,1)S(1)} %collective-permute-done.3.refs_5_.refs_1_, ...), custom_call_target="tpu_custom_call" | custom-call | flops 5242880 | bytes 1572864 | tf_op jit(solution)/shard_map/standardize/pallas_call | solution.py:139
  29.8 1.5 %collective-permute-start.21 = (bf16[1024,256]{1,0:T(8,128)(2,1)S(1)}, bf16[1024,256]{1,0:T(8,128)(2,1)S(1)}, u32[]{:S(2)}, u32[]{:S(2)}) collective-permute-start(bf16[1024,256]{1,0:T(8,128)(2,1)S(1)} %get-tuple-element.54.refs_4_), channel_id=1, source_target_pairs={{0,2},{1,3},{2,0},{3,1},{4,6},{5,7},{6,4},{7,5},{8,10},{9,11},{10,... | collective-permute-start | bytes 1572872 | tf_op jit(solution)/shard_map/ppermute | solution.py:226
  31.3 0.7 collective-permute-done.10.refs_2_
  32.0 0.0 collective-permute-start.22
  32.0 0.0 collective-permute-done.11.refs_3_
  32.0 3.7 %collective-permute-start.7 = (bf16[256,256]{1,0:T(8,128)(2,1)S(1)}, bf16[256,256]{1,0:T(8,128)(2,1)S(1)}, u32[]{:S(2)}, u32[]{:S(2)}) collective-permute-start(bf16[256,256]{1,0:T(8,128)(2,1)S(1)} %get-tuple-element.42), channel_id=1, source_target_pairs={{0,8},{4,12},{8,0},{12,4},{1,9},{5,13},{9,1},{13,5},{2,10},{6,14},... | collective-permute-start | bytes 393224 | tf_op jit(solution)/shard_map/ppermute | solution.py:223
  35.7 0.0 collective-permute-done.9.refs_1_
  35.7 3.4 %collective-permute-start.8 = (bf16[256,256]{1,0:T(8,128)(2,1)S(1)}, bf16[256,256]{1,0:T(8,128)(2,1)S(1)}, u32[]{:S(2)}, u32[]{:S(2)}) collective-permute-start(bf16[256,256]{1,0:T(8,128)(2,1)S(1)} %get-tuple-element.43), channel_id=1, source_target_pairs={{0,12},{4,0},{8,4},{12,8},{1,13},{5,1},{9,5},{13,9},{2,14},{6,2},{... | collective-permute-start | bytes 393224 | tf_op jit(solution)/shard_map/ppermute | solution.py:223
  39.1 2.9 %collective-permute-done.7.refs_2_ = bf16[256,256]{1,0:T(8,128)(2,1)S(1)} collective-permute-done((bf16[256,256]{1,0:T(8,128)(2,1)S(1)}, bf16[256,256]{1,0:T(8,128)(2,1)S(1)}, u32[]{:S(2)}, u32[]{:S(2)}) %collective-permute-start.7) | collective-permute-done | bytes 131104 | tf_op jit(solution)/shard_map/ppermute | solution.py:223
  41.9 0.1 collective-permute-start.1
  42.1 0.9 collective-permute-done.8.refs_3_
  43.0 6.8 %collective-permute-start.2 = (bf16[256,256]{1,0:T(8,128)(2,1)S(1)}, bf16[256,256]{1,0:T(8,128)(2,1)S(1)}, u32[]{:S(2)}, u32[]{:S(2)}) collective-permute-start(bf16[256,256]{1,0:T(8,128)(2,1)S(1)} %get-tuple-element.33), channel_id=1, source_target_pairs={{0,12},{4,0},{8,4},{12,8},{1,13},{5,1},{9,5},{13,9},{2,14},{6,2},{... | collective-permute-start | bytes 393224 | tf_op jit(solution)/shard_map/ppermute | solution.py:223
  49.8 1.6 %standardize.6 = (bf16[1024,256]{1,0:T(8,128)(2,1)}, bf16[256,1024]{1,0:T(8,128)(2,1)S(1)}, f32[8,128]{1,0:T(8,128)}) custom-call(f32[1,256]{1,0:T(1,128)S(1)} %get-tuple-element.58.mean_ref, bf16[256,256]{1,0:T(8,128)(2,1)S(1)} %get-tuple-element.40.refs_0_, bf16[256,256]{1,0:T(8,128)(2,1)S(1)} %collective-permute-done.6.refs_1_, ...), custom_call_target="tpu_custom_call" | custom-call | flops 5242880 | bytes 1572864 | tf_op jit(solution)/shard_map/standardize/pallas_call | solution.py:139
  51.3 0.0 collective-permute-done.refs_1_
  51.3 1.5 %collective-permute-start.18 = (bf16[1024,256]{1,0:T(8,128)(2,1)}, bf16[1024,256]{1,0:T(8,128)(2,1)}, u32[]{:S(2)}, u32[]{:S(2)}) collective-permute-start(bf16[1024,256]{1,0:T(8,128)(2,1)} %get-tuple-element.53.refs_4_), channel_id=1, source_target_pairs={{0,2},{1,3},{2,0},{3,1},{4,6},{5,7},{6,4},{7,5},{8,10},{9,11},{10,... | collective-permute-start | bytes 1572872 | tf_op jit(solution)/shard_map/ppermute | solution.py:226
  52.8 1.6 %standardize.7 = (bf16[1024,256]{1,0:T(8,128)(2,1)}, bf16[256,1024]{1,0:T(8,128)(2,1)S(1)}, f32[8,128]{1,0:T(8,128)}) custom-call(f32[1,256]{1,0:T(1,128)S(1)} %get-tuple-element.57.mean_ref, bf16[256,256]{1,0:T(8,128)(2,1)S(1)} %get-tuple-element.45.refs_0_, bf16[256,256]{1,0:T(8,128)(2,1)S(1)} %collective-permute-done.9.refs_1_, ...), custom_call_target="tpu_custom_call" | custom-call | flops 5242880 | bytes 1572864 | tf_op jit(solution)/shard_map/standardize/pallas_call | solution.py:139
  54.4 0.0 collective-permute-done.1.refs_2_
  54.4 0.0 collective-permute-start.19
  54.4 0.0 collective-permute-done.2.refs_3_
  54.4 0.8 collective-permute-start.15
  55.2 1.6 %standardize.4 = (bf16[1024,256]{1,0:T(8,128)(2,1)}, bf16[256,1024]{1,0:T(8,128)(2,1)S(1)}, f32[8,128]{1,0:T(8,128)S(1)}) custom-call(f32[1,256]{1,0:T(1,128)S(1)} %get-tuple-element.60.mean_ref, bf16[256,256]{1,0:T(8,128)(2,1)S(1)} %get-tuple-element.30.refs_0_, bf16[256,256]{1,0:T(8,128)(2,1)S(1)} %collective-permute-done.refs_1_, ...), custom_call_target="tpu_custom_call" | custom-call | flops 5242880 | bytes 1572864 | tf_op jit(solution)/shard_map/standardize/pallas_call | solution.py:139
  56.8 1.3 %collective-permute-start.12 = (bf16[1024,256]{1,0:T(8,128)(2,1)}, bf16[1024,256]{1,0:T(8,128)(2,1)}, u32[]{:S(2)}, u32[]{:S(2)}) collective-permute-start(bf16[1024,256]{1,0:T(8,128)(2,1)} %get-tuple-element.51.refs_4_), channel_id=1, source_target_pairs={{0,2},{1,3},{2,0},{3,1},{4,6},{5,7},{6,4},{7,5},{8,10},{9,11},{10,... | collective-permute-start | bytes 1572872 | tf_op jit(solution)/shard_map/ppermute | solution.py:226
  58.1 0.8 copy-done
  58.9 7.6 %collective-permute-done.18.refs_5_ = bf16[1024,256]{1,0:T(8,128)(2,1)} collective-permute-done((bf16[1024,256]{1,0:T(8,128)(2,1)}, bf16[1024,256]{1,0:T(8,128)(2,1)}, u32[]{:S(2)}, u32[]{:S(2)}) %collective-permute-start.18) | collective-permute-done | bytes 524320 | tf_op jit(solution)/shard_map/ppermute | solution.py:226
  66.5 0.1 broadcast_add_fusion
  66.6 0.5 collective-permute-start.16
  67.1 10.6 %collective-permute-done.15.refs_5_ = bf16[1024,256]{1,0:T(8,128)(2,1)} collective-permute-done((bf16[1024,256]{1,0:T(8,128)(2,1)}, bf16[1024,256]{1,0:T(8,128)(2,1)}, u32[]{:S(2)}, u32[]{:S(2)}) %collective-permute-start.15) | collective-permute-done | bytes 524320 | tf_op jit(solution)/shard_map/ppermute | solution.py:226
  77.8 9.0 %collective-permute-done.12.refs_5_ = bf16[1024,256]{1,0:T(8,128)(2,1)} collective-permute-done((bf16[1024,256]{1,0:T(8,128)(2,1)}, bf16[1024,256]{1,0:T(8,128)(2,1)}, u32[]{:S(2)}, u32[]{:S(2)}) %collective-permute-start.12) | collective-permute-done | bytes 524320 | tf_op jit(solution)/shard_map/ppermute | solution.py:226
  86.8 0.5 collective-permute-start.14
  87.3 1.0 copy-done.1
  88.3 5.4 %gram.4.refs_8_ = bf16[1,1024,4096]{2,1,0:T(8,128)(2,1)} custom-call(s32[4]{0:T(128)S(1)} %get-tuple-element.56.place_ref, f32[8,128]{1,0:T(8,128)S(1)} %get-tuple-element.38.count_ref, bf16[256,1024]{1,0:T(8,128)(2,1)S(1)} %get-tuple-element.39.refs_0_, bf16[256,1024]{1,0:T(8,128)(2,1)S(1)} %get-tuple-element.44.refs_1_, ...), custom_call_target="tpu_custom_call" | custom-call | flops 2147483648 | bytes 6291456 | tf_op jit(solution)/shard_map/gram/pallas_call | solution.py:187
  93.7 5.7 %gram.5.refs_8_ = bf16[1,1024,4096]{2,1,0:T(8,128)(2,1)} custom-call(s32[4]{0:T(128)S(1)} %get-tuple-element.55.place_ref, f32[8,128]{1,0:T(8,128)S(1)} %get-tuple-element.38.count_ref, bf16[256,1024]{1,0:T(8,128)(2,1)S(1)} %get-tuple-element.39.refs_0_, bf16[256,1024]{1,0:T(8,128)(2,1)S(1)} %get-tuple-element.44.refs_1_, ...), custom_call_target="tpu_custom_call", output_to_operand_aliasing={{}: (10, {})} | custom-call | flops 2147483648 | bytes 6291456 | tf_op jit(solution)/shard_map/gram/pallas_call | solution.py:187
  99.4 5.6 %gram.6.refs_8_ = bf16[1,1024,4096]{2,1,0:T(8,128)(2,1)} custom-call(s32[4]{0:T(128)S(1)} %get-tuple-element.61.place_ref, f32[8,128]{1,0:T(8,128)S(1)} %get-tuple-element.38.count_ref, bf16[256,1024]{1,0:T(8,128)(2,1)S(1)} %get-tuple-element.39.refs_0_, bf16[256,1024]{1,0:T(8,128)(2,1)S(1)} %get-tuple-element.44.refs_1_, ...), custom_call_target="tpu_custom_call", output_to_operand_aliasing={{}: (10, {})} | custom-call | flops 2147483648 | bytes 6291456 | tf_op jit(solution)/shard_map/gram/pallas_call | solution.py:187
  105.0 5.6 %gram.7 = bf16[1,1024,4096]{2,1,0:T(8,128)(2,1)} custom-call(s32[4]{0:T(128)S(1)} %get-tuple-element.62.place_ref, f32[8,128]{1,0:T(8,128)S(1)} %get-tuple-element.38.count_ref, bf16[256,1024]{1,0:T(8,128)(2,1)S(1)} %get-tuple-element.39.refs_0_, bf16[256,1024]{1,0:T(8,128)(2,1)S(1)} %get-tuple-element.44.refs_1_, ...), custom_call_target="tpu_custom_call", output_to_operand_aliasing={{}: (10, {})} | custom-call | flops 2147483648 | bytes 6291456 | tf_op jit(solution)/shard_map/gram/pallas_call | solution.py:187
  (21 shorter events, 0.1 us)
Async XLA Ops:
  0.7 1.2 %copy-start.2 = (bf16[512,1024]{1,0:T(8,128)(2,1)S(1)}, bf16[512,1024]{1,0:T(8,128)(2,1)}, u32[]{:S(2)}) copy-start(bf16[512,1024]{1,0:T(8,128)(2,1)} %expr_ref.1) | copy-start | bytes 3145732
  1.9 0.7 copy-start.3
  4.3 10.1 %collective-permute-start.3 = (bf16[272,256]{1,0:T(8,128)(2,1)S(1)}, bf16[272,256]{1,0:T(8,128)(2,1)S(1)}, u32[]{:S(2)}, u32[]{:S(2)}) collective-permute-start(bf16[272,256]{1,0:T(8,128)(2,1)S(1)} %get-tuple-element.35), channel_id=1, source_target_pairs={{0,4},{4,8},{8,12},{12,0},{1,5},{5,9},{9,13},{13,1},{2,6},{6,10},{... | collective-permute-start | bytes 417800 | tf_op jit(solution)/shard_map/ppermute | solution.py:223
  7.4 17.2 %collective-permute-start.4 = (bf16[272,256]{1,0:T(8,128)(2,1)S(1)}, bf16[272,256]{1,0:T(8,128)(2,1)S(1)}, u32[]{:S(2)}, u32[]{:S(2)}) collective-permute-start(bf16[272,256]{1,0:T(8,128)(2,1)S(1)} %get-tuple-element.36), channel_id=1, source_target_pairs={{0,8},{4,12},{8,0},{12,4},{1,9},{5,13},{9,1},{13,5},{2,10},{6,14},... | collective-permute-start | bytes 417800 | tf_op jit(solution)/shard_map/ppermute | solution.py:223
  10.0 18.4 %collective-permute-start.5 = (bf16[272,256]{1,0:T(8,128)(2,1)S(1)}, bf16[272,256]{1,0:T(8,128)(2,1)S(1)}, u32[]{:S(2)}, u32[]{:S(2)}) collective-permute-start(bf16[272,256]{1,0:T(8,128)(2,1)S(1)} %get-tuple-element.37), channel_id=1, source_target_pairs={{0,12},{4,0},{8,4},{12,8},{1,13},{5,1},{9,5},{13,9},{2,14},{6,2},{... | collective-permute-start | bytes 417800 | tf_op jit(solution)/shard_map/ppermute | solution.py:223
  11.3 20.7 %collective-permute-start.10 = (bf16[256,256]{1,0:T(8,128)(2,1)S(1)}, bf16[256,256]{1,0:T(8,128)(2,1)S(1)}, u32[]{:S(2)}, u32[]{:S(2)}) collective-permute-start(bf16[256,256]{1,0:T(8,128)(2,1)S(1)} %get-tuple-element.47), channel_id=1, source_target_pairs={{0,8},{4,12},{8,0},{12,4},{1,9},{5,13},{9,1},{13,5},{2,10},{6,14},... | collective-permute-start | bytes 393224 | tf_op jit(solution)/shard_map/ppermute | solution.py:223
  11.5 20.5 %collective-permute-start.11 = (bf16[256,256]{1,0:T(8,128)(2,1)S(1)}, bf16[256,256]{1,0:T(8,128)(2,1)S(1)}, u32[]{:S(2)}, u32[]{:S(2)}) collective-permute-start(bf16[256,256]{1,0:T(8,128)(2,1)S(1)} %get-tuple-element.48), channel_id=1, source_target_pairs={{0,12},{4,0},{8,4},{12,8},{1,13},{5,1},{9,5},{13,9},{2,14},{6,2},{... | collective-permute-start | bytes 393224 | tf_op jit(solution)/shard_map/ppermute | solution.py:223
  14.4 21.3 %collective-permute-start.9 = (bf16[256,256]{1,0:T(8,128)(2,1)S(1)}, bf16[256,256]{1,0:T(8,128)(2,1)S(1)}, u32[]{:S(2)}, u32[]{:S(2)}) collective-permute-start(bf16[256,256]{1,0:T(8,128)(2,1)S(1)} %get-tuple-element.46), channel_id=1, source_target_pairs={{0,4},{4,8},{8,12},{12,0},{1,5},{5,9},{9,13},{13,1},{2,6},{6,10},{... | collective-permute-start | bytes 393224 | tf_op jit(solution)/shard_map/ppermute | solution.py:223
  24.5 14.5 %collective-permute-start.6 = (bf16[256,256]{1,0:T(8,128)(2,1)S(1)}, bf16[256,256]{1,0:T(8,128)(2,1)S(1)}, u32[]{:S(2)}, u32[]{:S(2)}) collective-permute-start(bf16[256,256]{1,0:T(8,128)(2,1)S(1)} %get-tuple-element.41), channel_id=1, source_target_pairs={{0,4},{4,8},{8,12},{12,0},{1,5},{5,9},{9,13},{13,1},{2,6},{6,10},{... | collective-permute-start | bytes 393224 | tf_op jit(solution)/shard_map/ppermute | solution.py:223
  29.8 27.0 %collective-permute-start.21 = (bf16[1024,256]{1,0:T(8,128)(2,1)S(1)}, bf16[1024,256]{1,0:T(8,128)(2,1)S(1)}, u32[]{:S(2)}, u32[]{:S(2)}) collective-permute-start(bf16[1024,256]{1,0:T(8,128)(2,1)S(1)} %get-tuple-element.54.refs_4_), channel_id=1, source_target_pairs={{0,2},{1,3},{2,0},{3,1},{4,6},{5,7},{6,4},{7,5},{8,10},{9,11},{10,... | collective-permute-start | bytes 1572872 | tf_op jit(solution)/shard_map/ppermute | solution.py:226
  32.0 26.1 %collective-permute-start.22 = (bf16[1024,256]{1,0:T(8,128)(2,1)S(1)}, bf16[1024,256]{1,0:T(8,128)(2,1)S(1)}, u32[]{:S(2)}, u32[]{:S(2)}) collective-permute-start(bf16[1024,256]{1,0:T(8,128)(2,1)S(1)} %get-tuple-element.54.refs_4_), channel_id=1, source_target_pairs={{0,1},{1,0},{2,3},{3,2},{4,5},{5,4},{6,7},{7,6},{8,9},{9,8},{10,11... | collective-permute-start | bytes 1572872 | tf_op jit(solution)/shard_map/ppermute | solution.py:229
  32.0 9.9 %collective-permute-start.7 = (bf16[256,256]{1,0:T(8,128)(2,1)S(1)}, bf16[256,256]{1,0:T(8,128)(2,1)S(1)}, u32[]{:S(2)}, u32[]{:S(2)}) collective-permute-start(bf16[256,256]{1,0:T(8,128)(2,1)S(1)} %get-tuple-element.42), channel_id=1, source_target_pairs={{0,8},{4,12},{8,0},{12,4},{1,9},{5,13},{9,1},{13,5},{2,10},{6,14},... | collective-permute-start | bytes 393224 | tf_op jit(solution)/shard_map/ppermute | solution.py:223
  35.7 7.3 %collective-permute-start.8 = (bf16[256,256]{1,0:T(8,128)(2,1)S(1)}, bf16[256,256]{1,0:T(8,128)(2,1)S(1)}, u32[]{:S(2)}, u32[]{:S(2)}) collective-permute-start(bf16[256,256]{1,0:T(8,128)(2,1)S(1)} %get-tuple-element.43), channel_id=1, source_target_pairs={{0,12},{4,0},{8,4},{12,8},{1,13},{5,1},{9,5},{13,9},{2,14},{6,2},{... | collective-permute-start | bytes 393224 | tf_op jit(solution)/shard_map/ppermute | solution.py:223
  39.0 12.3 %collective-permute-start = (bf16[256,256]{1,0:T(8,128)(2,1)S(1)}, bf16[256,256]{1,0:T(8,128)(2,1)S(1)}, u32[]{:S(2)}, u32[]{:S(2)}) collective-permute-start(bf16[256,256]{1,0:T(8,128)(2,1)S(1)} %get-tuple-element.31), channel_id=1, source_target_pairs={{0,4},{4,8},{8,12},{12,0},{1,5},{5,9},{9,13},{13,1},{2,6},{6,10},{... | collective-permute-start | bytes 393224 | tf_op jit(solution)/shard_map/ppermute | solution.py:223
  41.9 12.4 %collective-permute-start.1 = (bf16[256,256]{1,0:T(8,128)(2,1)S(1)}, bf16[256,256]{1,0:T(8,128)(2,1)S(1)}, u32[]{:S(2)}, u32[]{:S(2)}) collective-permute-start(bf16[256,256]{1,0:T(8,128)(2,1)S(1)} %get-tuple-element.32), channel_id=1, source_target_pairs={{0,8},{4,12},{8,0},{12,4},{1,9},{5,13},{9,1},{13,5},{2,10},{6,14},... | collective-permute-start | bytes 393224 | tf_op jit(solution)/shard_map/ppermute | solution.py:223
  43.0 11.4 %collective-permute-start.2 = (bf16[256,256]{1,0:T(8,128)(2,1)S(1)}, bf16[256,256]{1,0:T(8,128)(2,1)S(1)}, u32[]{:S(2)}, u32[]{:S(2)}) collective-permute-start(bf16[256,256]{1,0:T(8,128)(2,1)S(1)} %get-tuple-element.33), channel_id=1, source_target_pairs={{0,12},{4,0},{8,4},{12,8},{1,13},{5,1},{9,5},{13,9},{2,14},{6,2},{... | collective-permute-start | bytes 393224 | tf_op jit(solution)/shard_map/ppermute | solution.py:223
  51.3 15.2 %collective-permute-start.18 = (bf16[1024,256]{1,0:T(8,128)(2,1)}, bf16[1024,256]{1,0:T(8,128)(2,1)}, u32[]{:S(2)}, u32[]{:S(2)}) collective-permute-start(bf16[1024,256]{1,0:T(8,128)(2,1)} %get-tuple-element.53.refs_4_), channel_id=1, source_target_pairs={{0,2},{1,3},{2,0},{3,1},{4,6},{5,7},{6,4},{7,5},{8,10},{9,11},{10,... | collective-permute-start | bytes 1572872 | tf_op jit(solution)/shard_map/ppermute | solution.py:226
  54.4 12.2 %collective-permute-start.19 = (bf16[1024,256]{1,0:T(8,128)(2,1)}, bf16[1024,256]{1,0:T(8,128)(2,1)}, u32[]{:S(2)}, u32[]{:S(2)}) collective-permute-start(bf16[1024,256]{1,0:T(8,128)(2,1)} %get-tuple-element.53.refs_4_), channel_id=1, source_target_pairs={{0,1},{1,0},{2,3},{3,2},{4,5},{5,4},{6,7},{7,6},{8,9},{9,8},{10,11... | collective-permute-start | bytes 1572872 | tf_op jit(solution)/shard_map/ppermute | solution.py:229
  54.4 23.4 %collective-permute-start.15 = (bf16[1024,256]{1,0:T(8,128)(2,1)}, bf16[1024,256]{1,0:T(8,128)(2,1)}, u32[]{:S(2)}, u32[]{:S(2)}) collective-permute-start(bf16[1024,256]{1,0:T(8,128)(2,1)} %get-tuple-element.52.refs_4_), channel_id=1, source_target_pairs={{0,2},{1,3},{2,0},{3,1},{4,6},{5,7},{6,4},{7,5},{8,10},{9,11},{10,... | collective-permute-start | bytes 1572872 | tf_op jit(solution)/shard_map/ppermute | solution.py:226
  56.8 30.0 %collective-permute-start.12 = (bf16[1024,256]{1,0:T(8,128)(2,1)}, bf16[1024,256]{1,0:T(8,128)(2,1)}, u32[]{:S(2)}, u32[]{:S(2)}) collective-permute-start(bf16[1024,256]{1,0:T(8,128)(2,1)} %get-tuple-element.51.refs_4_), channel_id=1, source_target_pairs={{0,2},{1,3},{2,0},{3,1},{4,6},{5,7},{6,4},{7,5},{8,10},{9,11},{10,... | collective-permute-start | bytes 1572872 | tf_op jit(solution)/shard_map/ppermute | solution.py:226
  58.1 0.8 copy-start
  58.9 27.9 %collective-permute-start.23 = (bf16[1024,256]{1,0:T(8,128)(2,1)S(1)}, bf16[1024,256]{1,0:T(8,128)(2,1)}, u32[]{:S(2)}, u32[]{:S(2)}) collective-permute-start(bf16[1024,256]{1,0:T(8,128)(2,1)S(1)} %collective-permute-done.21.refs_5_), channel_id=1, source_target_pairs={{0,1},{1,0},{2,3},{3,2},{4,5},{5,4},{6,7},{7,6},{8,9},{9,8},{10,11... | collective-permute-start | bytes 1572872 | tf_op jit(solution)/shard_map/ppermute | solution.py:229
  66.5 27.2 %collective-permute-start.20 = (bf16[1024,256]{1,0:T(8,128)(2,1)}, bf16[1024,256]{1,0:T(8,128)(2,1)S(1)}, u32[]{:S(2)}, u32[]{:S(2)}) collective-permute-start(bf16[1024,256]{1,0:T(8,128)(2,1)} %collective-permute-done.18.refs_5_), channel_id=1, source_target_pairs={{0,1},{1,0},{2,3},{3,2},{4,5},{5,4},{6,7},{7,6},{8,9},{9,8},{10,11... | collective-permute-start | bytes 1572872 | tf_op jit(solution)/shard_map/ppermute | solution.py:229
  66.6 32.8 %collective-permute-start.16 = (bf16[1024,256]{1,0:T(8,128)(2,1)}, bf16[1024,256]{1,0:T(8,128)(2,1)S(1)}, u32[]{:S(2)}, u32[]{:S(2)}) collective-permute-start(bf16[1024,256]{1,0:T(8,128)(2,1)} %get-tuple-element.52.refs_4_), channel_id=1, source_target_pairs={{0,1},{1,0},{2,3},{3,2},{4,5},{5,4},{6,7},{7,6},{8,9},{9,8},{10,11... | collective-permute-start | bytes 1572872 | tf_op jit(solution)/shard_map/ppermute | solution.py:229
  77.8 21.7 %collective-permute-start.17 = (bf16[1024,256]{1,0:T(8,128)(2,1)}, bf16[1024,256]{1,0:T(8,128)(2,1)S(1)}, u32[]{:S(2)}, u32[]{:S(2)}) collective-permute-start(bf16[1024,256]{1,0:T(8,128)(2,1)} %collective-permute-done.15.refs_5_), channel_id=1, source_target_pairs={{0,1},{1,0},{2,3},{3,2},{4,5},{5,4},{6,7},{7,6},{8,9},{9,8},{10,11... | collective-permute-start | bytes 1572872 | tf_op jit(solution)/shard_map/ppermute | solution.py:229
  86.8 18.3 %collective-permute-start.13 = (bf16[1024,256]{1,0:T(8,128)(2,1)}, bf16[1024,256]{1,0:T(8,128)(2,1)S(1)}, u32[]{:S(2)}, u32[]{:S(2)}) collective-permute-start(bf16[1024,256]{1,0:T(8,128)(2,1)} %get-tuple-element.51.refs_4_), channel_id=1, source_target_pairs={{0,1},{1,0},{2,3},{3,2},{4,5},{5,4},{6,7},{7,6},{8,9},{9,8},{10,11... | collective-permute-start | bytes 1572872 | tf_op jit(solution)/shard_map/ppermute | solution.py:229
  86.8 18.3 %collective-permute-start.14 = (bf16[1024,256]{1,0:T(8,128)(2,1)}, bf16[1024,256]{1,0:T(8,128)(2,1)S(1)}, u32[]{:S(2)}, u32[]{:S(2)}) collective-permute-start(bf16[1024,256]{1,0:T(8,128)(2,1)} %collective-permute-done.12.refs_5_), channel_id=1, source_target_pairs={{0,1},{1,0},{2,3},{3,2},{4,5},{5,4},{6,7},{7,6},{8,9},{9,8},{10,11... | collective-permute-start | bytes 1572872 | tf_op jit(solution)/shard_map/ppermute | solution.py:229
  87.3 1.0 copy-start.1

commit v2 on v1

--- a/solution.py
+++ b/solution.py
@@ -10,8 +10,9 @@
 dispersion = 100.0
 epsilon = 1e-05
 TILE = 16
-VMEM = 48 * 1024 * 1024
-
+VMEM = 24 * 1024 * 1024
+
+brief = pl.CostEstimate(flops=1024, bytes_accessed=1024, transcendentals=0)
 whole = pl.BlockSpec(memory_space=pltpu.VMEM)
 
 
@@ -19,7 +20,7 @@
     rows = expr_ref.shape[0]
     home = home_ref[0]
     kind = type_ref[...]
-    rel = jnp.where(kind >= home, kind - home, kind - home + types)
+    rel = jnp.bitwise_xor(kind, home)
     lines = max(types, 8)
     hot = lax.broadcasted_iota(jnp.int32, (lines, rows), 0) == rel
     hot_f = jnp.where(hot, 1.0, 0.0)
@@ -69,11 +70,7 @@
         in_specs=[pl.BlockSpec(memory_space=pltpu.SMEM), whole, whole, whole],
         out_specs=[whole] * len(shapes),
         compiler_params=pltpu.CompilerParams(vmem_limit_bytes=VMEM),
-        cost_estimate=pl.CostEstimate(
-            flops=2 * types * cap * rows * expression.shape[1],
-            bytes_accessed=3 * types * cap * expression.shape[1],
-            transcendentals=0,
-        ),
+        cost_estimate=brief,
         name="pack",
     )(home, cell_type.reshape(1, rows), size_factor.reshape(1, rows), expression)
     return [flat[k * types : (k + 1) * types] for k in range(len(widths))]
@@ -148,41 +145,39 @@
         out_specs=[whole] * 3,
         scratch_shapes=[pltpu.VMEM((slots, width), jnp.float32)],
         compiler_params=pltpu.CompilerParams(vmem_limit_bytes=VMEM),
-        cost_estimate=pl.CostEstimate(
-            flops=20 * slots * width,
-            bytes_accessed=6 * slots * width,
-            transcendentals=slots * width,
-        ),
+        cost_estimate=brief,
         name="standardize",
     )(*args)
 
 
 def gram_kernel(parts, panels, aliased, place_ref, count_ref, *refs):
-    left = refs[:parts]
+    pieces = refs[:parts]
     right = refs[parts : parts + panels]
-    out_ref = refs[parts + panels + (1 if aliased else 0)]
+    out_ref, left = refs[parts + panels + (1 if aliased else 0) :]
     inverse = 1.0 / count_ref[0:1, 0:1]
     step = pl.program_id(0)
+
+    @pl.when(step == 0)
+    def _():
+        start = 0
+        for piece in pieces:
+            left[start : start + piece.shape[0], :] = piece[...]
+            start += piece.shape[0]
+
     for j in range(panels):
 
         @pl.when(step == j)
         def _(j=j):
-            start = 0
-            for piece in left:
-                size = piece.shape[0]
-                product = jnp.dot(piece[...], right[j][...], preferred_element_type=jnp.float32)
-                out_ref[0, start : start + size, :] = (product * inverse).astype(jnp.bfloat16)
-                start += size
+            product = jnp.dot(left[...], right[j][...], preferred_element_type=jnp.float32)
+            out_ref[0] = (product * inverse).astype(jnp.bfloat16)
 
 
 def gram(shape, places, count, left, right, before):
-    rows, columns = shape[1:]
-    width = right[0].shape[1]
-    slots = right[0].shape[0]
+    rows = shape[1]
+    slots, width = right[0].shape
     aliased = before is not None
     args = [places, count, *left, *right] + ([before] if aliased else [])
-    hold = pl.BlockSpec(memory_space=pltpu.VMEM)
-    specs = [hold] * (1 + len(left) + len(right))
+    specs = [whole] * (1 + len(left) + len(right))
     specs += [pl.BlockSpec(memory_space=pl.ANY)] if aliased else []
     return pl.pallas_call(
         functools.partial(gram_kernel, len(left), len(right), aliased),
@@ -191,17 +186,18 @@
             grid=(len(right),),
             in_specs=specs,
             out_specs=pl.BlockSpec((1, rows, width), lambda i, place: (0, 0, place[i])),
+            scratch_shapes=[pltpu.VMEM((rows, slots), jnp.bfloat16)],
         ),
         out_shape=jax.ShapeDtypeStruct(shape, jnp.bfloat16),
         input_output_aliases={len(args) - 1: 0} if aliased else {},
         compiler_params=pltpu.CompilerParams(vmem_limit_bytes=VMEM),
-        cost_estimate=pl.CostEstimate(
-            flops=2 * slots * rows * width * len(right),
-            bytes_accessed=2 * (slots + rows) * width * len(right) + 2 * slots * rows,
-            transcendentals=0,
-        ),
+        cost_estimate=brief,
         name="gram",
     )(*args)
+
+
+def after(value, *others):
+    return lax.optimization_barrier((value, *others))[0]
 
 
 def shards(expression, cell_type, size_factor, gene_mean):
@@ -209,6 +205,7 @@
     blocks = lax.axis_size("blk")
     shard_rows, panel = expression.shape
     cap = 2 * shard_rows // types
+    assert types & (types - 1) == 0
     width = 256
     widths = [width] * (panel // width)
     chunks = len(widths)
@@ -216,11 +213,12 @@
     me = lax.axis_index("blk").astype(jnp.int32)
     cores = 2
     chips = blocks // cores
+    window = 3
 
     packed = pack(types, cap, widths, home[None], cell_type, size_factor, expression)
 
-    def shift(block, by):
-        return lax.ppermute(block, "cells", [(s, (s + by) % types) for s in range(types)])
+    def swap(block, by):
+        return lax.ppermute(block, "cells", [(s, s ^ by) for s in range(types)])
 
     def across(panel_, by):
         return lax.ppermute(panel_, "blk", [(b, (b + by * cores) % blocks) for b in range(blocks)])
@@ -228,26 +226,60 @@
     def sibling(panel_):
         return lax.ppermute(panel_, "blk", [(b, b ^ 1) for b in range(blocks)])
 
-    arrived = [
-        [packed[k][0]] + [shift(packed[k][j], j) for j in range(1, types)] for k in range(chunks)
-    ]
     mean = gene_mean.reshape(1, panel)
-    left, panels, count = [], [], None
+    order = sorted(range(1, types), key=lambda j: (j == types - 1, -j))
+    flights, first = [], None
+    left, own, near, far, far_near = [], [], [], [], []
     for k in range(chunks):
-        own, turned, count = standardize(
-            types, cap, width, mean[:, k * width : (k + 1) * width], arrived[k], arrived[0]
+        arrived = [packed[k][0]] + [None] * (types - 1)
+        for j in order:
+            waits = flights[-window:][:1] if len(flights) >= window else []
+            if j == order[-1] and k >= 2:
+                waits = waits + far[k - 2]
+            arrived[j] = swap(after(packed[k][j], *waits) if waits else packed[k][j], j)
+            flights.append(arrived[j])
+        if k >= 2:
+            far_near.append([sibling(got) for got in far[k - 2]])
+        done = near[-1:] + (far_near[-1] if k >= 2 else [])
+        if done:
+            arrived[0] = after(arrived[0], *done)
+        first = first or arrived
+        scaled, turned, count = standardize(
+            types, cap, width, mean[:, k * width : (k + 1) * width], arrived, first
         )
         left.append(turned)
-        near = [own] + [across(own, d) for d in range(1, chips)]
-        panels.append(near + [sibling(p) for p in near])
-
-    out = None
+        own.append(scaled)
+        far.append([across(scaled, d) for d in range(1, chips)])
+        near.append(sibling(scaled))
+
+    column = lambda source, k: source * chunks + k
+    distant = [(me + blocks - d * cores) % blocks for d in range(1, chips)]
     shape = (1, panel, panel * blocks)
+
+    def far_panels(k):
+        panels, places = [], []
+        for source, got, other in zip(distant, far[k], far_near[k]):
+            panels += [got, other]
+            places += [column(source, k), column(source ^ 1, k)]
+        return panels, places
+
+    panels, places = [], []
     for k in range(chunks):
-        sources = [(me + blocks - d * cores) % blocks for d in range(chips)]
-        sources += [s ^ 1 for s in sources]
-        places = jnp.stack(sources) * chunks + k
-        out = gram(shape, places.astype(jnp.int32), count, left, panels[k], out)
+        panels += [own[k], near[k]]
+        places += [column(me, k), column(me ^ 1, k)]
+    for k in range(chunks - 2):
+        more, at = far_panels(k)
+        panels += more
+        places += at
+    late = max(chunks - 2, 0)
+    panels[0] = after(panels[0], *far[late])
+    far_near.append([sibling(got) for got in far[late]])
+    out = gram(shape, jnp.stack(places).astype(jnp.int32), count, left, panels, None)
+    for k in range(late, chunks):
+        if k > late:
+            far_near.append([sibling(after(got, out)) for got in far[k]])
+        panels, places = far_panels(k)
+        out = gram(shape, jnp.stack(places).astype(jnp.int32), count, left, panels, out)
     return out
 
 

time: 112 us -> 111 us (level)
  starting transfers between devices: 43.4 us -> 25.5 us
  waiting for transfers between devices: 31.8 us -> 41.7 us
  local copies, waits for them, and re-layouts: 5.15 us -> 15 us
  Pallas kernels: 30.1 us -> 27.8 us
    ppermute x12, waiting for transfers between devices: 4.53 us -> 27.5 us  [swap(): return lax.ppermute(block, 'cells', [(s, s ^ by) for s in range(types)])]
    ppermute x12, starting transfers between devices: 37.3 us -> 20.8 us  [swap(): return lax.ppermute(block, 'cells', [(s, s ^ by) for s in range(types)])]
    ppermute x4, waiting for transfers between devices: 27.2 us -> 11.2 us  [across(): lax.ppermute(panel_, 'blk', [(b, (b + by * cores) % blocks) for b in rang...]
    unnamed x8 -> x36, local copies, waits for them, and re-layouts: 3.74 us -> 13.5 us
    ppermute x8, waiting for transfers between devices: 0.02 us -> 2.95 us  [sibling(): return lax.ppermute(panel_, 'blk', [(b, b ^ 1) for b in range(blocks)])]
    pallas_call x4 -> x3, Pallas kernels: 22.3 us -> 20.3 us  [gram(): pl.pallas_call(functools.partial(gram_kernel, len(left), len(right), alia...]
  transfers between devices with their start and end apart: 24 -> 24, of which waited for: 6 -> 10; matrix products, arithmetic and copies ran while one was open for 1% -> 1% of each run, Pallas kernels for 21% -> 19%
where the time goes in v2:
time: 111 us; the launch traced here: 110 us
  waiting for transfers between devices  41.7 us (38%)
  Pallas kernels  27.8 us (25%)
  starting transfers between devices  25.5 us (23%)
  local copies, waits for them, and re-layouts  15 us (14%)
    ppermute x12, waiting for transfers between devices, swap(): return lax.ppermute(block, 'cells', [(s, s ^ by) for s in range(types)])  27.5 us
    ppermute x12, starting transfers between devices, swap(): return lax.ppermute(block, 'cells', [(s, s ^ by) for s in range(types)])  20.8 us
    pallas_call x3, Pallas kernels, gram(): pl.pallas_call(functools.partial(gram_kernel, len(left), len(right), alia...  20.3 us
    unnamed x36, local copies, waits for them, and re-layouts  13.5 us
    ppermute x4, waiting for transfers between devices, across(): lax.ppermute(panel_, 'blk', [(b, (b + by * cores) % blocks) for b in rang...  11.2 us
    pallas_call x4, Pallas kernels, standardize(): pl.pallas_call(functools.partial(standardize_kernel, types, cap, lead, se...  5.78 us
    ppermute x4, starting transfers between devices, across(): lax.ppermute(panel_, 'blk', [(b, (b + by * cores) % blocks) for b in rang...  4.07 us
    ppermute x8, waiting for transfers between devices, sibling(): return lax.ppermute(panel_, 'blk', [(b, b ^ 1) for b in range(blocks)])  2.95 us
  transfers between devices with their start and end apart: 24, of which 10 were waited for; matrix products, arithmetic and copies ran while one was open for 1% of the time, Pallas kernels for 19%

profile of v2, /device:TPU:0, one launch (start us, length us, event | category | flops | bytes accessed | tf_op | source)
XLA Modules:
  0.0 110.1 jit_solution(12925705083766923436)
XLA Ops:
  0.0 0.7 reshape.11.factor_ref
  0.7 1.2 %copy-done = bf16[512,1024]{1,0:T(8,128)(2,1)S(1)} copy-done((bf16[512,1024]{1,0:T(8,128)(2,1)S(1)}, bf16[512,1024]{1,0:T(8,128)(2,1)}, u32[]{:S(2)}) %copy-start) | copy-done | bytes 1048600
  1.9 0.7 copy-done.17
  2.6 1.7 %pack.1 = (bf16[272,256]{1,0:T(8,128)(2,1)S(1)}, bf16[272,256]{1,0:T(8,128)(2,1)S(1)}, bf16[272,256]{1,0:T(8,128)(2,1)S(1)}, bf16[272,256]{1,0:T(8,128)(2,1)S(1)...) custom-call(s32[1]{0:T(128)} %bitcast.3.home_ref, ...), custom_call_target="tpu_custom_call" | custom-call | flops 1024 | bytes 1024 | tf_op jit(solution)/shard_map/pack/pallas_call | solution.py:67
  4.3 3.1 %collective-permute-start = (bf16[272,256]{1,0:T(8,128)(2,1)S(1)}, bf16[272,256]{1,0:T(8,128)(2,1)S(1)}, u32[]{:S(2)}, u32[]{:S(2)}) collective-permute-start(bf16[272,256]{1,0:T(8,128)(2,1)S(1)} %get-tuple-element.48), channel_id=1, source_target_pairs={{0,4},{4,0},{8,12},{12,8},{1,5},{5,1},{9,13},{13,9},{2,6},{6,2},{1... | collective-permute-start | bytes 417800 | tf_op jit(solution)/shard_map/ppermute | solution.py:221
  7.4 2.6 %collective-permute-start.1 = (bf16[272,256]{1,0:T(8,128)(2,1)S(1)}, bf16[272,256]{1,0:T(8,128)(2,1)S(1)}, u32[]{:S(2)}, u32[]{:S(2)}) collective-permute-start(bf16[272,256]{1,0:T(8,128)(2,1)S(1)} %get-tuple-element.49), channel_id=1, source_target_pairs={{0,8},{4,12},{8,0},{12,4},{1,9},{5,13},{9,1},{13,5},{2,10},{6,14},... | collective-permute-start | bytes 417800 | tf_op jit(solution)/shard_map/ppermute | solution.py:221
  10.0 0.7 fusion
  10.7 2.1 %collective-permute-done.refs_1_.refs_5_ = bf16[272,256]{1,0:T(8,128)(2,1)S(1)} collective-permute-done((bf16[272,256]{1,0:T(8,128)(2,1)S(1)}, bf16[272,256]{1,0:T(8,128)(2,1)S(1)}, u32[]{:S(2)}, u32[]{:S(2)}) %collective-permute-start) | collective-permute-done | bytes 139296 | tf_op jit(solution)/shard_map/ppermute | solution.py:221
  12.8 8.0 %collective-permute-done.1.refs_2_.refs_6_ = bf16[272,256]{1,0:T(8,128)(2,1)S(1)} collective-permute-done((bf16[272,256]{1,0:T(8,128)(2,1)S(1)}, bf16[272,256]{1,0:T(8,128)(2,1)S(1)}, u32[]{:S(2)}, u32[]{:S(2)}) %collective-permute-start.1) | collective-permute-done | bytes 139296 | tf_op jit(solution)/shard_map/ppermute | solution.py:221
  20.9 1.4 %standardize.4 = (bf16[1024,256]{1,0:T(8,128)(2,1)S(1)}, bf16[256,1024]{1,0:T(8,128)(2,1)S(1)}, f32[8,128]{1,0:T(8,128)}) custom-call(f32[1,256]{1,0:T(1,128)S(1)} %get-tuple-element.83.mean_ref, bf16[272,256]{1,0:T(8,128)(2,1)S(1)} %get-tuple-element.47.refs_0_.refs_4_, bf16[272,256]{1,0:T(8,128)(2,1)S(1)} %collective-permute-done.refs_1_.refs_5_, ...), custom_call_target="tpu_custom_call" | custom-call | flops 1024 | bytes 1024 | tf_op jit(solution)/shard_map/standardize/pallas_call | solution.py:136
  22.2 1.5 %collective-permute-start.8 = (bf16[1024,256]{1,0:T(8,128)(2,1)S(1)}, bf16[1024,256]{1,0:T(8,128)(2,1)S(1)}, u32[]{:S(2)}, u32[]{:S(2)}) collective-permute-start(bf16[1024,256]{1,0:T(8,128)(2,1)S(1)} %get-tuple-element.81.refs_4_), channel_id=1, source_target_pairs={{0,2},{1,3},{2,0},{3,1},{4,6},{5,7},{6,4},{7,5},{8,10},{9,11},{10,... | collective-permute-start | bytes 1572872 | tf_op jit(solution)/shard_map/ppermute | solution.py:224
  23.7 2.1 %collective-permute-start.4 = (bf16[256,256]{1,0:T(8,128)(2,1)S(1)}, bf16[256,256]{1,0:T(8,128)(2,1)S(1)}, u32[]{:S(2)}, u32[]{:S(2)}) collective-permute-start(bf16[256,256]{1,0:T(8,128)(2,1)S(1)} %get-tuple-element.54), channel_id=1, source_target_pairs={{0,4},{4,0},{8,12},{12,8},{1,5},{5,1},{9,13},{13,9},{2,6},{6,2},{1... | collective-permute-start | bytes 393224 | tf_op jit(solution)/shard_map/ppermute | solution.py:221
  25.9 1.0 collective-permute-start.5
  26.9 1.5 %collective-permute-start.6 = (bf16[256,256]{1,0:T(8,128)(2,1)S(1)}, bf16[256,256]{1,0:T(8,128)(2,1)S(1)}, u32[]{:S(2)}, u32[]{:S(2)}) collective-permute-start(bf16[256,256]{1,0:T(8,128)(2,1)S(1)} %get-tuple-element.58), channel_id=1, source_target_pairs={{0,12},{4,8},{8,4},{12,0},{1,13},{5,9},{9,5},{13,1},{2,14},{6,10},... | collective-permute-start | bytes 393224 | tf_op jit(solution)/shard_map/ppermute | solution.py:221
  28.4 5.1 %collective-permute-done.8.refs_12_ = bf16[1024,256]{1,0:T(8,128)(2,1)S(1)} collective-permute-done((bf16[1024,256]{1,0:T(8,128)(2,1)S(1)}, bf16[1024,256]{1,0:T(8,128)(2,1)S(1)}, u32[]{:S(2)}, u32[]{:S(2)}) %collective-permute-start.8) | collective-permute-done | bytes 524320 | tf_op jit(solution)/shard_map/ppermute | solution.py:224
  33.5 0.8 copy-done.1
  34.3 4.5 %collective-permute-done.5.refs_2_ = bf16[256,256]{1,0:T(8,128)(2,1)S(1)} collective-permute-done((bf16[256,256]{1,0:T(8,128)(2,1)S(1)}, bf16[256,256]{1,0:T(8,128)(2,1)S(1)}, u32[]{:S(2)}, u32[]{:S(2)}) %collective-permute-start.5) | collective-permute-done | bytes 131104 | tf_op jit(solution)/shard_map/ppermute | solution.py:221
  38.8 1.4 %standardize.5 = (bf16[1024,256]{1,0:T(8,128)(2,1)S(1)}, bf16[256,1024]{1,0:T(8,128)(2,1)S(1)}, f32[8,128]{1,0:T(8,128)}) custom-call(f32[1,256]{1,0:T(1,128)S(1)} %get-tuple-element.84.mean_ref, bf16[256,256]{1,0:T(8,128)(2,1)S(1)} %get-tuple-element.52.refs_0_, bf16[256,256]{1,0:T(8,128)(2,1)S(1)} %collective-permute-done.4.refs_1_, ...), custom_call_target="tpu_custom_call" | custom-call | flops 1024 | bytes 1024 | tf_op jit(solution)/shard_map/standardize/pallas_call | solution.py:136
  40.2 0.5 collective-permute-start.14
  40.7 0.8 copy-done.5
  41.5 2.7 %collective-permute-start.10 = (bf16[256,256]{1,0:T(8,128)(2,1)S(1)}, bf16[256,256]{1,0:T(8,128)(2,1)S(1)}, u32[]{:S(2)}, u32[]{:S(2)}) collective-permute-start(bf16[256,256]{1,0:T(8,128)(2,1)S(1)} %get-tuple-element.62), channel_id=1, source_target_pairs={{0,4},{4,0},{8,12},{12,8},{1,5},{5,1},{9,13},{13,9},{2,6},{6,2},{1... | collective-permute-start | bytes 393224 | tf_op jit(solution)/shard_map/ppermute | solution.py:221
  44.2 1.0 collective-permute-start.11
  45.2 1.5 %collective-permute-start.12 = (bf16[256,256]{1,0:T(8,128)(2,1)S(1)}, bf16[256,256]{1,0:T(8,128)(2,1)S(1)}, u32[]{:S(2)}, u32[]{:S(2)}) collective-permute-start(bf16[256,256]{1,0:T(8,128)(2,1)S(1)} %get-tuple-element.66), channel_id=1, source_target_pairs={{0,12},{4,8},{8,4},{12,0},{1,13},{5,9},{9,5},{13,1},{2,14},{6,10},... | collective-permute-start | bytes 393224 | tf_op jit(solution)/shard_map/ppermute | solution.py:221
  46.7 6.1 %collective-permute-done.14.refs_14_ = bf16[1024,256]{1,0:T(8,128)(2,1)S(1)} collective-permute-done((bf16[1024,256]{1,0:T(8,128)(2,1)S(1)}, bf16[1024,256]{1,0:T(8,128)(2,1)S(1)}, u32[]{:S(2)}, u32[]{:S(2)}) %collective-permute-start.14) | collective-permute-done | bytes 524320 | tf_op jit(solution)/shard_map/ppermute | solution.py:224
  52.9 0.8 copy-done.9
  53.7 3.4 %collective-permute-done.11.refs_2_ = bf16[256,256]{1,0:T(8,128)(2,1)S(1)} collective-permute-done((bf16[256,256]{1,0:T(8,128)(2,1)S(1)}, bf16[256,256]{1,0:T(8,128)(2,1)S(1)}, u32[]{:S(2)}, u32[]{:S(2)}) %collective-permute-start.11) | collective-permute-done | bytes 131104 | tf_op jit(solution)/shard_map/ppermute | solution.py:221
  57.1 1.4 %standardize.6 = (bf16[1024,256]{1,0:T(8,128)(2,1)S(1)}, bf16[256,1024]{1,0:T(8,128)(2,1)S(1)}, f32[8,128]{1,0:T(8,128)}) custom-call(f32[1,256]{1,0:T(1,128)S(1)} %get-tuple-element.85.mean_ref, bf16[256,256]{1,0:T(8,128)(2,1)S(1)} %get-tuple-element.60.refs_0_, bf16[256,256]{1,0:T(8,128)(2,1)S(1)} %collective-permute-done.10.refs_1_, ...), custom_call_target="tpu_custom_call" | custom-call | flops 1024 | bytes 1024 | tf_op jit(solution)/shard_map/standardize/pallas_call | solution.py:136
  58.5 1.5 %collective-permute-start.20 = (bf16[1024,256]{1,0:T(8,128)(2,1)S(1)}, bf16[1024,256]{1,0:T(8,128)(2,1)}, u32[]{:S(2)}, u32[]{:S(2)}) collective-permute-start(bf16[1024,256]{1,0:T(8,128)(2,1)S(1)} %get-tuple-element.67.refs_8_), channel_id=1, source_target_pairs={{0,2},{1,3},{2,0},{3,1},{4,6},{5,7},{6,4},{7,5},{8,10},{9,11},{10,... | collective-permute-start | bytes 1572872 | tf_op jit(solution)/shard_map/ppermute | solution.py:224
  60.0 2.7 %collective-permute-start.16 = (bf16[256,256]{1,0:T(8,128)(2,1)S(1)}, bf16[256,256]{1,0:T(8,128)(2,1)S(1)}, u32[]{:S(2)}, u32[]{:S(2)}) collective-permute-start(bf16[256,256]{1,0:T(8,128)(2,1)S(1)} %get-tuple-element.70), channel_id=1, source_target_pairs={{0,4},{4,0},{8,12},{12,8},{1,5},{5,1},{9,13},{13,9},{2,6},{6,2},{1... | collective-permute-start | bytes 393224 | tf_op jit(solution)/shard_map/ppermute | solution.py:221
  62.6 1.0 collective-permute-start.17
  63.7 1.5 %collective-permute-start.18 = (bf16[256,256]{1,0:T(8,128)(2,1)S(1)}, bf16[256,256]{1,0:T(8,128)(2,1)S(1)}, u32[]{:S(2)}, u32[]{:S(2)}) collective-permute-start(bf16[256,256]{1,0:T(8,128)(2,1)S(1)} %get-tuple-element.74), channel_id=1, source_target_pairs={{0,12},{4,8},{8,4},{12,0},{1,13},{5,9},{9,5},{13,1},{2,14},{6,10},... | collective-permute-start | bytes 393224 | tf_op jit(solution)/shard_map/ppermute | solution.py:221
  65.2 0.8 copy-done.15
  66.0 2.5 %collective-permute-done.16.refs_1_ = bf16[256,256]{1,0:T(8,128)(2,1)S(1)} collective-permute-done((bf16[256,256]{1,0:T(8,128)(2,1)S(1)}, bf16[256,256]{1,0:T(8,128)(2,1)S(1)}, u32[]{:S(2)}, u32[]{:S(2)}) %collective-permute-start.16) | collective-permute-done | bytes 131104 | tf_op jit(solution)/shard_map/ppermute | solution.py:221
  68.5 7.0 %collective-permute-done.17.refs_2_ = bf16[256,256]{1,0:T(8,128)(2,1)S(1)} collective-permute-done((bf16[256,256]{1,0:T(8,128)(2,1)S(1)}, bf16[256,256]{1,0:T(8,128)(2,1)S(1)}, u32[]{:S(2)}, u32[]{:S(2)}) %collective-permute-start.17) | collective-permute-done | bytes 131104 | tf_op jit(solution)/shard_map/ppermute | solution.py:221
  75.5 1.6 %standardize.7 = (bf16[1024,256]{1,0:T(8,128)(2,1)}, bf16[256,1024]{1,0:T(8,128)(2,1)S(1)}, f32[8,128]{1,0:T(8,128)S(1)}) custom-call(f32[1,256]{1,0:T(1,128)S(1)} %get-tuple-element.86.mean_ref, bf16[256,256]{1,0:T(8,128)(2,1)S(1)} %get-tuple-element.68.refs_0_, bf16[256,256]{1,0:T(8,128)(2,1)S(1)} %collective-permute-done.16.refs_1_, ...), custom_call_target="tpu_custom_call" | custom-call | flops 1024 | bytes 1024 | tf_op jit(solution)/shard_map/standardize/pallas_call | solution.py:136
  78.4 1.0 collective-permute-done.22.refs_11_
  79.4 1.0 copy-done.2
  80.4 1.0 copy-done.4
  81.5 1.0 copy-done.6
  82.5 1.0 copy-done.8
  83.6 1.0 copy-done.10
  84.6 1.0 copy-done.12
  85.6 1.0 copy-done.14
  86.7 1.0 copy-done.16
  87.7 12.4 %gram.3.refs_6_ = bf16[1,1024,4096]{2,1,0:T(8,128)(2,1)} custom-call(s32[12]{0:T(128)S(1)} %stack.75.place_ref, f32[8,128]{1,0:T(8,128)S(1)} %get-tuple-element.75.count_ref, bf16[256,1024]{1,0:T(8,128)(2,1)S(1)} %get-tuple-element.76.refs_0_, bf16[256,1024]{1,0:T(8,128)(2,1)S(1)} %get-tuple-element.77.refs_1_, ...), custom_call_target="tpu_custom_call" | custom-call | flops 1024 | bytes 1024 | tf_op jit(solution)/shard_map/gram/pallas_call | solution.py:182
  100.1 4.0 %gram.4.refs_6_ = bf16[1,1024,4096]{2,1,0:T(8,128)(2,1)} custom-call(s32[2]{0:T(128)S(1)} %pad_add_fusion.1.place_ref, f32[8,128]{1,0:T(8,128)S(1)} %get-tuple-element.75.count_ref, bf16[256,1024]{1,0:T(8,128)(2,1)S(1)} %get-tuple-element.76.refs_0_, bf16[256,1024]{1,0:T(8,128)(2,1)S(1)} %get-tuple-element.77.refs_1_, ...), custom_call_target="tpu_custom_call", output_to_operand_aliasing={{}: (8, {})} | custom-call | flops 1024 | bytes 1024 | tf_op jit(solution)/shard_map/gram/pallas_call | solution.py:182
  104.3 1.9 %collective-permute-done.23.refs_5_ = bf16[1024,256]{1,0:T(8,128)(2,1)S(1)} collective-permute-done((bf16[1024,256]{1,0:T(8,128)(2,1)}, bf16[1024,256]{1,0:T(8,128)(2,1)S(1)}, u32[]{:S(2)}, u32[]{:S(2)}) %collective-permute-start.23) | collective-permute-done | bytes 524320 | tf_op jit(solution)/shard_map/ppermute | solution.py:227
  106.3 3.9 %gram.5 = bf16[1,1024,4096]{2,1,0:T(8,128)(2,1)} custom-call(s32[2]{0:T(128)S(1)} %pad_add_fusion.place_ref, f32[8,128]{1,0:T(8,128)S(1)} %get-tuple-element.75.count_ref, bf16[256,1024]{1,0:T(8,128)(2,1)S(1)} %get-tuple-element.76.refs_0_, bf16[256,1024]{1,0:T(8,128)(2,1)S(1)} %get-tuple-element.77.refs_1_, ...), custom_call_target="tpu_custom_call", output_to_operand_aliasing={{}: (8, {})} | custom-call | flops 1024 | bytes 1024 | tf_op jit(solution)/shard_map/gram/pallas_call | solution.py:182
  (49 shorter events, 1.5 us)
Async XLA Ops:
  0.7 1.2 %copy-start = (bf16[512,1024]{1,0:T(8,128)(2,1)S(1)}, bf16[512,1024]{1,0:T(8,128)(2,1)}, u32[]{:S(2)}) copy-start(bf16[512,1024]{1,0:T(8,128)(2,1)} %expr_ref.1) | copy-start | bytes 3145732
  1.9 0.7 copy-start.17
  4.3 8.6 %collective-permute-start = (bf16[272,256]{1,0:T(8,128)(2,1)S(1)}, bf16[272,256]{1,0:T(8,128)(2,1)S(1)}, u32[]{:S(2)}, u32[]{:S(2)}) collective-permute-start(bf16[272,256]{1,0:T(8,128)(2,1)S(1)} %get-tuple-element.48), channel_id=1, source_target_pairs={{0,4},{4,0},{8,12},{12,8},{1,5},{5,1},{9,13},{13,9},{2,6},{6,2},{1... | collective-permute-start | bytes 417800 | tf_op jit(solution)/shard_map/ppermute | solution.py:221
  7.4 13.5 %collective-permute-start.1 = (bf16[272,256]{1,0:T(8,128)(2,1)S(1)}, bf16[272,256]{1,0:T(8,128)(2,1)S(1)}, u32[]{:S(2)}, u32[]{:S(2)}) collective-permute-start(bf16[272,256]{1,0:T(8,128)(2,1)S(1)} %get-tuple-element.49), channel_id=1, source_target_pairs={{0,8},{4,12},{8,0},{12,4},{1,9},{5,13},{9,1},{13,5},{2,10},{6,14},... | collective-permute-start | bytes 417800 | tf_op jit(solution)/shard_map/ppermute | solution.py:221
  10.0 10.9 %collective-permute-start.2 = (bf16[272,256]{1,0:T(8,128)(2,1)S(1)}, bf16[272,256]{1,0:T(8,128)(2,1)S(1)}, u32[]{:S(2)}, u32[]{:S(2)}) collective-permute-start(bf16[272,256]{1,0:T(8,128)(2,1)S(1)} %get-tuple-element.50), channel_id=1, source_target_pairs={{0,12},{4,8},{8,4},{12,0},{1,13},{5,9},{9,5},{13,1},{2,14},{6,10},... | collective-permute-start | bytes 417800 | tf_op jit(solution)/shard_map/ppermute | solution.py:221
  22.2 11.2 %collective-permute-start.8 = (bf16[1024,256]{1,0:T(8,128)(2,1)S(1)}, bf16[1024,256]{1,0:T(8,128)(2,1)S(1)}, u32[]{:S(2)}, u32[]{:S(2)}) collective-permute-start(bf16[1024,256]{1,0:T(8,128)(2,1)S(1)} %get-tuple-element.81.refs_4_), channel_id=1, source_target_pairs={{0,2},{1,3},{2,0},{3,1},{4,6},{5,7},{6,4},{7,5},{8,10},{9,11},{10,... | collective-permute-start | bytes 1572872 | tf_op jit(solution)/shard_map/ppermute | solution.py:224
  23.7 9.7 %collective-permute-start.3 = (bf16[1024,256]{1,0:T(8,128)(2,1)S(1)}, bf16[1024,256]{1,0:T(8,128)(2,1)S(1)}, u32[]{:S(2)}, u32[]{:S(2)}) collective-permute-start(bf16[1024,256]{1,0:T(8,128)(2,1)S(1)} %get-tuple-element.81.refs_4_), channel_id=1, source_target_pairs={{0,1},{1,0},{2,3},{3,2},{4,5},{5,4},{6,7},{7,6},{8,9},{9,8},{10,11... | collective-permute-start | bytes 1572872 | tf_op jit(solution)/shard_map/ppermute | solution.py:227
  23.7 10.5 %collective-permute-start.4 = (bf16[256,256]{1,0:T(8,128)(2,1)S(1)}, bf16[256,256]{1,0:T(8,128)(2,1)S(1)}, u32[]{:S(2)}, u32[]{:S(2)}) collective-permute-start(bf16[256,256]{1,0:T(8,128)(2,1)S(1)} %get-tuple-element.54), channel_id=1, source_target_pairs={{0,4},{4,0},{8,12},{12,8},{1,5},{5,1},{9,13},{13,9},{2,6},{6,2},{1... | collective-permute-start | bytes 393224 | tf_op jit(solution)/shard_map/ppermute | solution.py:221
  25.9 12.9 %collective-permute-start.5 = (bf16[256,256]{1,0:T(8,128)(2,1)S(1)}, bf16[256,256]{1,0:T(8,128)(2,1)S(1)}, u32[]{:S(2)}, u32[]{:S(2)}) collective-permute-start(bf16[256,256]{1,0:T(8,128)(2,1)S(1)} %get-tuple-element.56), channel_id=1, source_target_pairs={{0,8},{4,12},{8,0},{12,4},{1,9},{5,13},{9,1},{13,5},{2,10},{6,14},... | collective-permute-start | bytes 393224 | tf_op jit(solution)/shard_map/ppermute | solution.py:221
  26.9 11.9 %collective-permute-start.6 = (bf16[256,256]{1,0:T(8,128)(2,1)S(1)}, bf16[256,256]{1,0:T(8,128)(2,1)S(1)}, u32[]{:S(2)}, u32[]{:S(2)}) collective-permute-start(bf16[256,256]{1,0:T(8,128)(2,1)S(1)} %get-tuple-element.58), channel_id=1, source_target_pairs={{0,12},{4,8},{8,4},{12,0},{1,13},{5,9},{9,5},{13,1},{2,14},{6,10},... | collective-permute-start | bytes 393224 | tf_op jit(solution)/shard_map/ppermute | solution.py:221
  33.5 11.8 %collective-permute-start.9 = (bf16[1024,256]{1,0:T(8,128)(2,1)S(1)}, bf16[1024,256]{1,0:T(8,128)(2,1)S(1)}, u32[]{:S(2)}, u32[]{:S(2)}) collective-permute-start(bf16[1024,256]{1,0:T(8,128)(2,1)S(1)} %collective-permute-done.8.refs_12_), channel_id=1, source_target_pairs={{0,1},{1,0},{2,3},{3,2},{4,5},{5,4},{6,7},{7,6},{8,9},{9,8},{10,11... | collective-permute-start | bytes 1572872 | tf_op jit(solution)/shard_map/ppermute | solution.py:227
  33.5 0.8 copy-start.1
  40.2 12.7 %collective-permute-start.14 = (bf16[1024,256]{1,0:T(8,128)(2,1)S(1)}, bf16[1024,256]{1,0:T(8,128)(2,1)S(1)}, u32[]{:S(2)}, u32[]{:S(2)}) collective-permute-start(bf16[1024,256]{1,0:T(8,128)(2,1)S(1)} %get-tuple-element.59.refs_6_), channel_id=1, source_target_pairs={{0,2},{1,3},{2,0},{3,1},{4,6},{5,7},{6,4},{7,5},{8,10},{9,11},{10,... | collective-permute-start | bytes 1572872 | tf_op jit(solution)/shard_map/ppermute | solution.py:224
  40.7 12.2 %collective-permute-start.7 = (bf16[1024,256]{1,0:T(8,128)(2,1)S(1)}, bf16[1024,256]{1,0:T(8,128)(2,1)S(1)}, u32[]{:S(2)}, u32[]{:S(2)}) collective-permute-start(bf16[1024,256]{1,0:T(8,128)(2,1)S(1)} %get-tuple-element.59.refs_6_), channel_id=1, source_target_pairs={{0,1},{1,0},{2,3},{3,2},{4,5},{5,4},{6,7},{7,6},{8,9},{9,8},{10,11... | collective-permute-start | bytes 1572872 | tf_op jit(solution)/shard_map/ppermute | solution.py:227
  40.7 0.8 copy-start.5
  41.5 12.2 %collective-permute-start.10 = (bf16[256,256]{1,0:T(8,128)(2,1)S(1)}, bf16[256,256]{1,0:T(8,128)(2,1)S(1)}, u32[]{:S(2)}, u32[]{:S(2)}) collective-permute-start(bf16[256,256]{1,0:T(8,128)(2,1)S(1)} %get-tuple-element.62), channel_id=1, source_target_pairs={{0,4},{4,0},{8,12},{12,8},{1,5},{5,1},{9,13},{13,9},{2,6},{6,2},{1... | collective-permute-start | bytes 393224 | tf_op jit(solution)/shard_map/ppermute | solution.py:221
  44.2 12.9 %collective-permute-start.11 = (bf16[256,256]{1,0:T(8,128)(2,1)S(1)}, bf16[256,256]{1,0:T(8,128)(2,1)S(1)}, u32[]{:S(2)}, u32[]{:S(2)}) collective-permute-start(bf16[256,256]{1,0:T(8,128)(2,1)S(1)} %get-tuple-element.64), channel_id=1, source_target_pairs={{0,8},{4,12},{8,0},{12,4},{1,9},{5,13},{9,1},{13,5},{2,10},{6,14},... | collective-permute-start | bytes 393224 | tf_op jit(solution)/shard_map/ppermute | solution.py:221
  45.2 31.9 %copy-start.3 = (bf16[1024,256]{1,0:T(8,128)(2,1)}, bf16[1024,256]{1,0:T(8,128)(2,1)S(1)}, u32[]{:S(2)}) copy-start(bf16[1024,256]{1,0:T(8,128)(2,1)S(1)} %collective-permute-done.9.refs_13_) | copy-start | bytes 1572868
  45.2 11.9 %collective-permute-start.12 = (bf16[256,256]{1,0:T(8,128)(2,1)S(1)}, bf16[256,256]{1,0:T(8,128)(2,1)S(1)}, u32[]{:S(2)}, u32[]{:S(2)}) collective-permute-start(bf16[256,256]{1,0:T(8,128)(2,1)S(1)} %get-tuple-element.66), channel_id=1, source_target_pairs={{0,12},{4,8},{8,4},{12,0},{1,13},{5,9},{9,5},{13,1},{2,14},{6,10},... | collective-permute-start | bytes 393224 | tf_op jit(solution)/shard_map/ppermute | solution.py:221
  52.9 22.7 %copy-start.7 = (bf16[1024,256]{1,0:T(8,128)(2,1)}, bf16[1024,256]{1,0:T(8,128)(2,1)S(1)}, u32[]{:S(2)}) copy-start(bf16[1024,256]{1,0:T(8,128)(2,1)S(1)} %collective-permute-done.14.refs_14_) | copy-start | bytes 1572868
  52.9 10.8 %collective-permute-start.15 = (bf16[1024,256]{1,0:T(8,128)(2,1)S(1)}, bf16[1024,256]{1,0:T(8,128)(2,1)S(1)}, u32[]{:S(2)}, u32[]{:S(2)}) collective-permute-start(bf16[1024,256]{1,0:T(8,128)(2,1)S(1)} %collective-permute-done.14.refs_14_), channel_id=1, source_target_pairs={{0,1},{1,0},{2,3},{3,2},{4,5},{5,4},{6,7},{7,6},{8,9},{9,8},{10,11... | collective-permute-start | bytes 1572872 | tf_op jit(solution)/shard_map/ppermute | solution.py:227
  52.9 0.8 copy-start.9
  58.5 18.7 %copy-start.13 = (bf16[1024,256]{1,0:T(8,128)(2,1)}, bf16[1024,256]{1,0:T(8,128)(2,1)S(1)}, u32[]{:S(2)}) copy-start(bf16[1024,256]{1,0:T(8,128)(2,1)S(1)} %get-tuple-element.67.refs_8_) | copy-start | bytes 1572868
  58.5 6.7 %collective-permute-start.13 = (bf16[1024,256]{1,0:T(8,128)(2,1)S(1)}, bf16[1024,256]{1,0:T(8,128)(2,1)S(1)}, u32[]{:S(2)}, u32[]{:S(2)}) collective-permute-start(bf16[1024,256]{1,0:T(8,128)(2,1)S(1)} %get-tuple-element.67.refs_8_), channel_id=1, source_target_pairs={{0,1},{1,0},{2,3},{3,2},{4,5},{5,4},{6,7},{7,6},{8,9},{9,8},{10,11... | collective-permute-start | bytes 1572872 | tf_op jit(solution)/shard_map/ppermute | solution.py:227
  58.5 18.7 %collective-permute-start.20 = (bf16[1024,256]{1,0:T(8,128)(2,1)S(1)}, bf16[1024,256]{1,0:T(8,128)(2,1)}, u32[]{:S(2)}, u32[]{:S(2)}) collective-permute-start(bf16[1024,256]{1,0:T(8,128)(2,1)S(1)} %get-tuple-element.67.refs_8_), channel_id=1, source_target_pairs={{0,2},{1,3},{2,0},{3,1},{4,6},{5,7},{6,4},{7,5},{8,10},{9,11},{10,... | collective-permute-start | bytes 1572872 | tf_op jit(solution)/shard_map/ppermute | solution.py:224
  60.0 8.5 %collective-permute-start.16 = (bf16[256,256]{1,0:T(8,128)(2,1)S(1)}, bf16[256,256]{1,0:T(8,128)(2,1)S(1)}, u32[]{:S(2)}, u32[]{:S(2)}) collective-permute-start(bf16[256,256]{1,0:T(8,128)(2,1)S(1)} %get-tuple-element.70), channel_id=1, source_target_pairs={{0,4},{4,0},{8,12},{12,8},{1,5},{5,1},{9,13},{13,9},{2,6},{6,2},{1... | collective-permute-start | bytes 393224 | tf_op jit(solution)/shard_map/ppermute | solution.py:221
  62.6 12.9 %collective-permute-start.17 = (bf16[256,256]{1,0:T(8,128)(2,1)S(1)}, bf16[256,256]{1,0:T(8,128)(2,1)S(1)}, u32[]{:S(2)}, u32[]{:S(2)}) collective-permute-start(bf16[256,256]{1,0:T(8,128)(2,1)S(1)} %get-tuple-element.72), channel_id=1, source_target_pairs={{0,8},{4,12},{8,0},{12,4},{1,9},{5,13},{9,1},{13,5},{2,10},{6,14},... | collective-permute-start | bytes 393224 | tf_op jit(solution)/shard_map/ppermute | solution.py:221
  63.7 13.5 %copy-start.11 = (bf16[1024,256]{1,0:T(8,128)(2,1)}, bf16[1024,256]{1,0:T(8,128)(2,1)S(1)}, u32[]{:S(2)}) copy-start(bf16[1024,256]{1,0:T(8,128)(2,1)S(1)} %collective-permute-done.15.refs_15_) | copy-start | bytes 1572868
  63.7 11.9 %collective-permute-start.18 = (bf16[256,256]{1,0:T(8,128)(2,1)S(1)}, bf16[256,256]{1,0:T(8,128)(2,1)S(1)}, u32[]{:S(2)}, u32[]{:S(2)}) collective-permute-start(bf16[256,256]{1,0:T(8,128)(2,1)S(1)} %get-tuple-element.74), channel_id=1, source_target_pairs={{0,12},{4,8},{8,4},{12,0},{1,13},{5,9},{9,5},{13,1},{2,14},{6,10},... | collective-permute-start | bytes 393224 | tf_op jit(solution)/shard_map/ppermute | solution.py:221
  65.2 0.8 copy-start.15
  77.1 2.3 %collective-permute-start.22 = (bf16[1024,256]{1,0:T(8,128)(2,1)}, bf16[1024,256]{1,0:T(8,128)(2,1)}, u32[]{:S(2)}, u32[]{:S(2)}) collective-permute-start(bf16[1024,256]{1,0:T(8,128)(2,1)} %get-tuple-element.80.refs_10_), channel_id=1, source_target_pairs={{0,1},{1,0},{2,3},{3,2},{4,5},{5,4},{6,7},{7,6},{8,9},{9,8},{10,11... | collective-permute-start | bytes 1572872 | tf_op jit(solution)/shard_map/ppermute | solution.py:227
  77.2 22.9 %collective-permute-start.21 = (bf16[1024,256]{1,0:T(8,128)(2,1)}, bf16[1024,256]{1,0:T(8,128)(2,1)}, u32[]{:S(2)}, u32[]{:S(2)}) collective-permute-start(bf16[1024,256]{1,0:T(8,128)(2,1)} %collective-permute-done.20.refs_4_), channel_id=1, source_target_pairs={{0,1},{1,0},{2,3},{3,2},{4,5},{5,4},{6,7},{7,6},{8,9},{9,8},{10,11... | collective-permute-start | bytes 1572872 | tf_op jit(solution)/shard_map/ppermute | solution.py:227
  77.7 26.5 %collective-permute-start.19 = (bf16[1024,256]{1,0:T(8,128)(2,1)}, bf16[1024,256]{1,0:T(8,128)(2,1)}, u32[]{:S(2)}, u32[]{:S(2)}) collective-permute-start(bf16[1024,256]{1,0:T(8,128)(2,1)} %get-tuple-element.80.refs_10_), channel_id=1, source_target_pairs={{0,2},{1,3},{2,0},{3,1},{4,6},{5,7},{6,4},{7,5},{8,10},{9,11},{10,... | collective-permute-start | bytes 1572872 | tf_op jit(solution)/shard_map/ppermute | solution.py:224
  79.4 1.0 copy-start.2
  80.4 1.0 copy-start.4
  81.5 1.0 copy-start.6
  82.5 1.0 copy-start.8
  83.6 1.0 copy-start.10
  84.6 1.0 copy-start.12
  85.6 1.0 copy-start.14
  86.7 1.0 copy-start.16
  104.1 2.1 %collective-permute-start.23 = (bf16[1024,256]{1,0:T(8,128)(2,1)}, bf16[1024,256]{1,0:T(8,128)(2,1)S(1)}, u32[]{:S(2)}, u32[]{:S(2)}) collective-permute-start(bf16[1024,256]{1,0:T(8,128)(2,1)} %collective-permute-done.19.refs_4_), channel_id=1, source_target_pairs={{0,1},{1,0},{2,3},{3,2},{4,5},{5,4},{6,7},{7,6},{8,9},{9,8},{10,11... | collective-permute-start | bytes 1572872 | tf_op jit(solution)/shard_map/ppermute | solution.py:227

commit v3 on v2

--- a/solution.py
+++ b/solution.py
@@ -10,10 +10,12 @@
 dispersion = 100.0
 epsilon = 1e-05
 TILE = 16
-VMEM = 24 * 1024 * 1024
+VMEM = 16 * 1024 * 1024
 
 brief = pl.CostEstimate(flops=1024, bytes_accessed=1024, transcendentals=0)
+lengthy = pl.CostEstimate(flops=2 * 10**10, bytes_accessed=1024, transcendentals=0)
 whole = pl.BlockSpec(memory_space=pltpu.VMEM)
+anywhere = pl.BlockSpec(memory_space=pl.ANY)
 
 
 def pack_kernel(types, cap, widths, home_ref, type_ref, factor_ref, expr_ref, *outs):
@@ -76,12 +78,12 @@
     return [flat[k * types : (k + 1) * types] for k in range(len(widths))]
 
 
-def standardize_kernel(types, cap, lead, separate, mean_ref, *refs):
+def standardize_kernel(types, cap, lead, separate, chunk, mean_ref, *refs):
     blocks = refs[:types]
     tails = refs[types : 2 * types] if separate else blocks
     base = 0 if separate else cap
     refs = refs[2 * types :] if separate else refs[types:]
-    scaled_ref, turned_ref, count_ref, work = refs
+    scaled_ref, all_ref, turned_ref, count_ref, work, turned, sems = refs[-7:]
     mean = mean_ref[...]
     width = mean.shape[1]
     piece = min(lead, cap)
@@ -120,11 +122,20 @@
         scaled = work[j * cap : (j + 1) * cap, :] * scale
         scaled_ref[j * cap : (j + 1) * cap, :] = scaled.astype(jnp.bfloat16)
         work[j * cap : (j + 1) * cap, :] = scaled
-    turned_ref[...] = jnp.transpose(work[...]).astype(jnp.bfloat16)
+    slots = types * cap
+    rows = pl.ds(chunk * slots, slots)
+    scaled_copy = pltpu.make_async_copy(scaled_ref, all_ref.at[rows, :], sems.at[0])
+    scaled_copy.start()
+    turned[...] = jnp.transpose(work[...]).astype(jnp.bfloat16)
+    rows = pl.ds(chunk * width, width)
+    turned_copy = pltpu.make_async_copy(turned, turned_ref.at[rows, :], sems.at[1])
+    turned_copy.start()
+    scaled_copy.wait()
+    turned_copy.wait()
     count_ref[...] = jnp.broadcast_to(count, count_ref.shape)
 
 
-def standardize(types, cap, lead, mean, blocks, first):
+def standardize(types, cap, lead, mean, chunk, chunks, blocks, first, before):
     width = mean.shape[1]
     separate = first is not blocks
     slots = types * cap
@@ -133,65 +144,94 @@
     if separate:
         specs += [pl.BlockSpec((TILE, lead), lambda i: (cap // TILE, 0))] * types
         args += list(first)
+    aliases = {}
+    if before is not None:
+        aliases = {len(args): 1, len(args) + 1: 2}
+        specs += [anywhere] * 2
+        args += list(before)
     return pl.pallas_call(
-        functools.partial(standardize_kernel, types, cap, lead, separate),
+        functools.partial(standardize_kernel, types, cap, lead, separate, chunk),
         grid=(1,),
         out_shape=[
             jax.ShapeDtypeStruct((slots, width), jnp.bfloat16),
-            jax.ShapeDtypeStruct((width, slots), jnp.bfloat16),
+            jax.ShapeDtypeStruct((chunks * slots, width), jnp.bfloat16),
+            jax.ShapeDtypeStruct((chunks * width, slots), jnp.bfloat16),
             jax.ShapeDtypeStruct((8, 128), jnp.float32),
         ],
         in_specs=specs,
-        out_specs=[whole] * 3,
-        scratch_shapes=[pltpu.VMEM((slots, width), jnp.float32)],
+        out_specs=[whole, anywhere, anywhere, whole],
+        scratch_shapes=[
+            pltpu.VMEM((slots, width), jnp.float32),
+            pltpu.VMEM((width, slots), jnp.bfloat16),
+            pltpu.SemaphoreType.DMA((2,)),
+        ],
+        input_output_aliases=aliases,
         compiler_params=pltpu.CompilerParams(vmem_limit_bytes=VMEM),
-        cost_estimate=brief,
+        cost_estimate=lengthy,
         name="standardize",
     )(*args)
 
 
-def gram_kernel(parts, panels, aliased, place_ref, count_ref, *refs):
-    pieces = refs[:parts]
-    right = refs[parts : parts + panels]
-    out_ref, left = refs[parts + panels + (1 if aliased else 0) :]
+def gram_kernel(spots, arrays, place_ref, count_ref, left_ref, *refs):
+    sources = refs[:arrays]
+    out_ref, left, panel, tile, left_sem, panel_sem, tile_sem = refs[-7:]
+    slots, width = panel.shape[1:]
+    panels = len(spots)
     inverse = 1.0 / count_ref[0:1, 0:1]
-    step = pl.program_id(0)
-
-    @pl.when(step == 0)
-    def _():
-        start = 0
-        for piece in pieces:
-            left[start : start + piece.shape[0], :] = piece[...]
-            start += piece.shape[0]
-
+
+    def fetch(j):
+        source, row = spots[j]
+        block = sources[source].at[pl.ds(row, slots), :]
+        return pltpu.make_async_copy(block, panel.at[j % 2], panel_sem.at[j % 2])
+
+    def store(j):
+        column = pl.multiple_of(place_ref[j] * width, width)
+        return pltpu.make_async_copy(
+            tile.at[j % 2], out_ref.at[0, :, pl.ds(column, width)], tile_sem.at[j % 2]
+        )
+
+    fetch(0).start()
+    left_copy = pltpu.make_async_copy(left_ref, left, left_sem)
+    left_copy.start()
+    left_copy.wait()
     for j in range(panels):
-
-        @pl.when(step == j)
-        def _(j=j):
-            product = jnp.dot(left[...], right[j][...], preferred_element_type=jnp.float32)
-            out_ref[0] = (product * inverse).astype(jnp.bfloat16)
-
-
-def gram(shape, places, count, left, right, before):
-    rows = shape[1]
-    slots, width = right[0].shape
-    aliased = before is not None
-    args = [places, count, *left, *right] + ([before] if aliased else [])
-    specs = [whole] * (1 + len(left) + len(right))
-    specs += [pl.BlockSpec(memory_space=pl.ANY)] if aliased else []
+        if j + 1 < panels:
+            fetch(j + 1).start()
+        fetch(j).wait()
+        if j >= 2:
+            store(j - 2).wait()
+        product = jnp.dot(left[...], panel[j % 2], preferred_element_type=jnp.float32)
+        tile[j % 2] = (product * inverse).astype(jnp.bfloat16)
+        store(j).start()
+    for j in range(max(panels - 2, 0), panels):
+        store(j).wait()
+
+
+def gram(shape, places, count, left, right, before, cost):
+    rows, slots = left.shape
+    width = right[0].shape[1]
+    spots = [
+        (i, row) for i, panels in enumerate(right) for row in range(0, panels.shape[0], slots)
+    ]
+    args = [jnp.stack(places).astype(jnp.int32), count, left, *right]
+    args += [] if before is None else [before]
+    specs = [pl.BlockSpec(memory_space=pltpu.SMEM), whole] + [anywhere] * (len(args) - 2)
     return pl.pallas_call(
-        functools.partial(gram_kernel, len(left), len(right), aliased),
-        grid_spec=pltpu.PrefetchScalarGridSpec(
-            num_scalar_prefetch=1,
-            grid=(len(right),),
-            in_specs=specs,
-            out_specs=pl.BlockSpec((1, rows, width), lambda i, place: (0, 0, place[i])),
-            scratch_shapes=[pltpu.VMEM((rows, slots), jnp.bfloat16)],
-        ),
+        functools.partial(gram_kernel, spots, len(right)),
+        in_specs=specs,
+        out_specs=anywhere,
         out_shape=jax.ShapeDtypeStruct(shape, jnp.bfloat16),
-        input_output_aliases={len(args) - 1: 0} if aliased else {},
+        scratch_shapes=[
+            pltpu.VMEM((rows, slots), jnp.bfloat16),
+            pltpu.VMEM((2, slots, width), jnp.bfloat16),
+            pltpu.VMEM((2, rows, width), jnp.bfloat16),
+            pltpu.SemaphoreType.DMA,
+            pltpu.SemaphoreType.DMA((2,)),
+            pltpu.SemaphoreType.DMA((2,)),
+        ],
+        input_output_aliases={} if before is None else {len(args) - 1: 0},
         compiler_params=pltpu.CompilerParams(vmem_limit_bytes=VMEM),
-        cost_estimate=brief,
+        cost_estimate=cost,
         name="gram",
     )(*args)
 
@@ -223,64 +263,52 @@
     def across(panel_, by):
         return lax.ppermute(panel_, "blk", [(b, (b + by * cores) % blocks) for b in range(blocks)])
 
-    def sibling(panel_):
-        return lax.ppermute(panel_, "blk", [(b, b ^ 1) for b in range(blocks)])
+    def side(name, panel_, *waits):
+        with jax.named_scope(name):
+            return lax.ppermute(after(panel_, *waits), "blk", [(b, b ^ 1) for b in range(blocks)])
 
     mean = gene_mean.reshape(1, panel)
-    order = sorted(range(1, types), key=lambda j: (j == types - 1, -j))
-    flights, first = [], None
-    left, own, near, far, far_near = [], [], [], [], []
+    order = sorted(range(1, types), key=lambda j: (j == 1, j))
+    left, own, far, before = None, None, [], None
+    first = None
     for k in range(chunks):
         arrived = [packed[k][0]] + [None] * (types - 1)
         for j in order:
-            waits = flights[-window:][:1] if len(flights) >= window else []
-            if j == order[-1] and k >= 2:
-                waits = waits + far[k - 2]
-            arrived[j] = swap(after(packed[k][j], *waits) if waits else packed[k][j], j)
-            flights.append(arrived[j])
-        if k >= 2:
-            far_near.append([sibling(got) for got in far[k - 2]])
-        done = near[-1:] + (far_near[-1] if k >= 2 else [])
-        if done:
-            arrived[0] = after(arrived[0], *done)
+            block = packed[k][j]
+            if k:
+                block = after(block, before[j])
+            with jax.named_scope(f"cells_{j}_chunk_{k}"):
+                arrived[j] = swap(block, j)
+        before = list(arrived)
+        waits = far[k - 2] if k >= 2 else []
+        if waits:
+            arrived[0] = after(arrived[0], *waits)
         first = first or arrived
-        scaled, turned, count = standardize(
-            types, cap, width, mean[:, k * width : (k + 1) * width], arrived, first
+        piece = mean[:, k * width : (k + 1) * width]
+        scaled, own, left, count = standardize(
+            types, cap, width, piece, k, chunks, arrived, first, (own, left) if k else None
         )
-        left.append(turned)
-        own.append(scaled)
-        far.append([across(scaled, d) for d in range(1, chips)])
-        near.append(sibling(scaled))
+        with jax.named_scope(f"far_{k}"):
+            far.append([across(scaled, d) for d in range(1, chips)])
 
     column = lambda source, k: source * chunks + k
     distant = [(me + blocks - d * cores) % blocks for d in range(1, chips)]
     shape = (1, panel, panel * blocks)
 
-    def far_panels(k):
-        panels, places = [], []
-        for source, got, other in zip(distant, far[k], far_near[k]):
-            panels += [got, other]
-            places += [column(source, k), column(source ^ 1, k)]
-        return panels, places
-
-    panels, places = [], []
-    for k in range(chunks):
-        panels += [own[k], near[k]]
-        places += [column(me, k), column(me ^ 1, k)]
-    for k in range(chunks - 2):
-        more, at = far_panels(k)
-        panels += more
-        places += at
-    late = max(chunks - 2, 0)
-    panels[0] = after(panels[0], *far[late])
-    far_near.append([sibling(got) for got in far[late]])
-    out = gram(shape, jnp.stack(places).astype(jnp.int32), count, left, panels, None)
-    for k in range(late, chunks):
-        if k > late:
-            far_near.append([sibling(after(got, out)) for got in far[k]])
-        panels, places = far_panels(k)
-        out = gram(shape, jnp.stack(places).astype(jnp.int32), count, left, panels, out)
-    return out
+    last = chunks - 1
+    there = sum(far[:last], [])
+    near = side("near", own)
+    far_near = [side(f"far_near_{i}", p, own, *there) for i, p in enumerate(there)]
+    places = [column(me, k) for k in range(chunks)]
+    out = gram(shape, places, count, left, [own], None, lengthy)
+    places = [column(me ^ 1, k) for k in range(chunks)]
+    places += [column(source, k) for k in range(last) for source in distant]
+    places += [column(source ^ 1, k) for k in range(last) for source in distant]
+    out = gram(shape, places, count, left, [near, *there, *far_near], out, brief)
+    far_near = [side(f"far_near_last_{i}", p, out) for i, p in enumerate(far[last])]
+    places = [column(source, last) for source in distant]
+    places += [column(source ^ 1, last) for source in distant]
+    return gram(shape, places, count, left, [*far[last], *far_near], out, brief)
 
 
 def solution(mesh):

time: 111 us -> 97 us (0.87)
  the two profiles are of different devices: /device:TPU:0 before, /device:TPU:11 now
where the time goes in v3:
time: 97 us; the launch traced here: 96.7 us
  Pallas kernels  37.5 us (39%)
  starting transfers between devices  28.5 us (29%)
  waiting for transfers between devices  25.9 us (27%)
  local copies, waits for them, and re-layouts  4.2 us (4%)
    pallas_call x3, Pallas kernels, gram(): pl.pallas_call(functools.partial(gram_kernel, spots, len(right)), in_spec...  27.4 us
    ppermute x12, waiting for transfers between devices, swap(): return lax.ppermute(block, 'cells', [(s, s ^ by) for s in range(types)])  21.7 us
    ppermute x12, starting transfers between devices, swap(): return lax.ppermute(block, 'cells', [(s, s ^ by) for s in range(types)])  17.9 us
    ppermute x5, starting transfers between devices, side(): lax.ppermute(after(panel_, *waits), 'blk', [(b, b ^ 1) for b in range(blo...  9.57 us
    pallas_call x4, Pallas kernels, standardize(): pl.pallas_call(functools.partial(standardize_kernel, types, cap, lead, se...  8.44 us
    unnamed x6, local copies, waits for them, and re-layouts  2.7 us
    ppermute x4, waiting for transfers between devices, across(): lax.ppermute(panel_, 'blk', [(b, (b + by * cores) % blocks) for b in rang...  2.24 us
    ppermute x5, waiting for transfers between devices, side(): lax.ppermute(after(panel_, *waits), 'blk', [(b, b ^ 1) for b in range(blo...  2.03 us
  transfers between devices with their start and end apart: 21, of which 9 were waited for; matrix products, arithmetic and copies ran while one was open for 1% of the time, Pallas kernels for 32%

profile of v3, /device:TPU:11, one launch (start us, length us, event | category | flops | bytes accessed | tf_op | source)
XLA Modules:
  0.0 96.7 jit_solution(16157050930717043601)
XLA Ops:
  0.0 0.7 reshape.11.factor_ref
  0.7 1.2 %copy-done = bf16[512,1024]{1,0:T(8,128)(2,1)S(1)} copy-done((bf16[512,1024]{1,0:T(8,128)(2,1)S(1)}, bf16[512,1024]{1,0:T(8,128)(2,1)}, u32[]{:S(2)}) %copy-start) | copy-done | bytes 1048600
  1.9 0.7 copy-done.1
  2.6 1.7 %pack.1 = (bf16[272,256]{1,0:T(8,128)(2,1)S(1)}, bf16[272,256]{1,0:T(8,128)(2,1)S(1)}, bf16[272,256]{1,0:T(8,128)(2,1)S(1)}, bf16[272,256]{1,0:T(8,128)(2,1)S(1)...) custom-call(s32[1]{0:T(128)} %bitcast.3.home_ref, ...), custom_call_target="tpu_custom_call" | custom-call | flops 1024 | bytes 1024 | tf_op jit(solution)/shard_map/pack/pallas_call | solution.py:69
  4.3 0.2 collective-permute-start
  4.5 2.3 %collective-permute-start.2 = (bf16[272,256]{1,0:T(8,128)(2,1)S(1)}, bf16[272,256]{1,0:T(8,128)(2,1)S(1)}, u32[]{:S(2)}, u32[]{:S(2)}) collective-permute-start(bf16[272,256]{1,0:T(8,128)(2,1)S(1)} %get-tuple-element.55), channel_id=1, source_target_pairs={{0,8},{4,12},{8,0},{12,4},{1,9},{5,13},{9,1},{13,5},{2,10},{6,14},... | collective-permute-start | bytes 417800 | tf_op jit(solution)/shard_map/cells_2_chunk_0/ppermute | solution.py:261
  6.8 0.2 collective-permute-start.4
  7.0 0.7 fusion
  7.7 1.2 %collective-permute-done.refs_1_.refs_5_ = bf16[272,256]{1,0:T(8,128)(2,1)S(1)} collective-permute-done((bf16[272,256]{1,0:T(8,128)(2,1)S(1)}, bf16[272,256]{1,0:T(8,128)(2,1)S(1)}, u32[]{:S(2)}, u32[]{:S(2)}) %collective-permute-start) | collective-permute-done | bytes 139296 | tf_op jit(solution)/shard_map/cells_1_chunk_0/ppermute | solution.py:261
  8.9 0.2 collective-permute-start.1
  9.1 3.8 %collective-permute-done.2.refs_2_.refs_6_ = bf16[272,256]{1,0:T(8,128)(2,1)S(1)} collective-permute-done((bf16[272,256]{1,0:T(8,128)(2,1)S(1)}, bf16[272,256]{1,0:T(8,128)(2,1)S(1)}, u32[]{:S(2)}, u32[]{:S(2)}) %collective-permute-start.2) | collective-permute-done | bytes 139296 | tf_op jit(solution)/shard_map/cells_2_chunk_0/ppermute | solution.py:261
  12.9 0.1 collective-permute-start.3
  13.0 5.9 %collective-permute-done.4.refs_3_.refs_7_ = bf16[272,256]{1,0:T(8,128)(2,1)S(1)} collective-permute-done((bf16[272,256]{1,0:T(8,128)(2,1)S(1)}, bf16[272,256]{1,0:T(8,128)(2,1)S(1)}, u32[]{:S(2)}, u32[]{:S(2)}) %collective-permute-start.4) | collective-permute-done | bytes 139296 | tf_op jit(solution)/shard_map/cells_3_chunk_0/ppermute | solution.py:261
  18.9 5.7 %collective-permute-start.5 = (bf16[256,256]{1,0:T(8,128)(2,1)S(1)}, bf16[256,256]{1,0:T(8,128)(2,1)S(1)}, u32[]{:S(2)}, u32[]{:S(2)}) collective-permute-start(bf16[256,256]{1,0:T(8,128)(2,1)S(1)} %get-tuple-element.59), channel_id=1, source_target_pairs={{0,12},{4,8},{8,4},{12,0},{1,13},{5,9},{9,5},{13,1},{2,14},{6,10},... | collective-permute-start | bytes 393224 | tf_op jit(solution)/shard_map/cells_3_chunk_1/ppermute | solution.py:261
  24.5 2.2 %standardize.4 = (bf16[1024,256]{1,0:T(8,128)(2,1)S(1)}, bf16[4096,256]{1,0:T(8,128)(2,1)}, bf16[1024,1024]{1,0:T(8,128)(2,1)S(1)}, f32[8,128]{1,0:T(8,128)}) custom-call(f32[1,256]{1,0:T(1,128)S(1)} %get-tuple-element.94.mean_ref, bf16[272,256]{1,0:T(8,128)(2,1)S(1)} %get-tuple-element.60.refs_0_.refs_4_, ...), custom_call_target="tpu_custom_call" | custom-call | flops 20000000000 | bytes 1024 | tf_op jit(solution)/shard_map/standardize/pallas_call | solution.py:152
  26.8 0.3 collective-permute-start.13
  27.1 0.0 collective-permute-done.1.refs_1_
  27.1 2.5 %collective-permute-start.9 = (bf16[256,256]{1,0:T(8,128)(2,1)S(1)}, bf16[256,256]{1,0:T(8,128)(2,1)S(1)}, u32[]{:S(2)}, u32[]{:S(2)}) collective-permute-start(bf16[256,256]{1,0:T(8,128)(2,1)S(1)} %get-tuple-element.71), channel_id=1, source_target_pairs={{0,8},{4,12},{8,0},{12,4},{1,9},{5,13},{9,1},{13,5},{2,10},{6,14},... | collective-permute-start | bytes 393224 | tf_op jit(solution)/shard_map/cells_2_chunk_2/ppermute | solution.py:261
  29.7 0.1 collective-permute-done.5.refs_3_
  29.7 1.4 %collective-permute-start.11 = (bf16[256,256]{1,0:T(8,128)(2,1)S(1)}, bf16[256,256]{1,0:T(8,128)(2,1)S(1)}, u32[]{:S(2)}, u32[]{:S(2)}) collective-permute-start(bf16[256,256]{1,0:T(8,128)(2,1)S(1)} %get-tuple-element.75), channel_id=1, source_target_pairs={{0,12},{4,8},{8,4},{12,0},{1,13},{5,9},{9,5},{13,1},{2,14},{6,10},... | collective-permute-start | bytes 393224 | tf_op jit(solution)/shard_map/cells_3_chunk_2/ppermute | solution.py:261
  31.1 2.2 %standardize.5 = (bf16[1024,256]{1,0:T(8,128)(2,1)S(1)}, bf16[4096,256]{1,0:T(8,128)(2,1)}, bf16[1024,1024]{1,0:T(8,128)(2,1)S(1)}, f32[8,128]{1,0:T(8,128)}) custom-call(f32[1,256]{1,0:T(1,128)S(1)} %get-tuple-element.95.mean_ref, bf16[256,256]{1,0:T(8,128)(2,1)S(1)} %get-tuple-element.50.refs_0_, ...), custom_call_target="tpu_custom_call", output_to_operand_aliasing={{1}: (9, {}), {2}: (10, {})} | custom-call | flops 20000000000 | bytes 1024 | tf_op jit(solution)/shard_map/standardize/pallas_call | solution.py:152
  33.3 0.3 collective-permute-start.6
  33.6 0.0 collective-permute-done.7.refs_1_
  33.6 0.6 collective-permute-start.8
  34.2 1.5 %collective-permute-done.9.refs_2_ = bf16[256,256]{1,0:T(8,128)(2,1)S(1)} collective-permute-done((bf16[256,256]{1,0:T(8,128)(2,1)S(1)}, bf16[256,256]{1,0:T(8,128)(2,1)S(1)}, u32[]{:S(2)}, u32[]{:S(2)}) %collective-permute-start.9) | collective-permute-done | bytes 131104 | tf_op jit(solution)/shard_map/cells_2_chunk_2/ppermute | solution.py:261
  35.7 3.2 %collective-permute-start.10 = (bf16[256,256]{1,0:T(8,128)(2,1)S(1)}, bf16[256,256]{1,0:T(8,128)(2,1)S(1)}, u32[]{:S(2)}, u32[]{:S(2)}) collective-permute-start(bf16[256,256]{1,0:T(8,128)(2,1)S(1)} %get-tuple-element.72), channel_id=1, source_target_pairs={{0,8},{4,12},{8,0},{12,4},{1,9},{5,13},{9,1},{13,5},{2,10},{6,14},... | collective-permute-start | bytes 393224 | tf_op jit(solution)/shard_map/cells_2_chunk_3/ppermute | solution.py:261
  38.9 5.8 %collective-permute-done.11.refs_3_ = bf16[256,256]{1,0:T(8,128)(2,1)S(1)} collective-permute-done((bf16[256,256]{1,0:T(8,128)(2,1)S(1)}, bf16[256,256]{1,0:T(8,128)(2,1)S(1)}, u32[]{:S(2)}, u32[]{:S(2)}) %collective-permute-start.11) | collective-permute-done | bytes 131104 | tf_op jit(solution)/shard_map/cells_3_chunk_2/ppermute | solution.py:261
  44.7 1.6 %collective-permute-start.12 = (bf16[256,256]{1,0:T(8,128)(2,1)S(1)}, bf16[256,256]{1,0:T(8,128)(2,1)S(1)}, u32[]{:S(2)}, u32[]{:S(2)}) collective-permute-start(bf16[256,256]{1,0:T(8,128)(2,1)S(1)} %get-tuple-element.76), channel_id=1, source_target_pairs={{0,12},{4,8},{8,4},{12,0},{1,13},{5,9},{9,5},{13,1},{2,14},{6,10},... | collective-permute-start | bytes 393224 | tf_op jit(solution)/shard_map/cells_3_chunk_3/ppermute | solution.py:261
  46.3 2.4 %standardize.6 = (bf16[1024,256]{1,0:T(8,128)(2,1)}, bf16[4096,256]{1,0:T(8,128)(2,1)}, bf16[1024,1024]{1,0:T(8,128)(2,1)S(1)}, f32[8,128]{1,0:T(8,128)}) custom-call(f32[1,256]{1,0:T(1,128)S(1)} %get-tuple-element.93.mean_ref, bf16[256,256]{1,0:T(8,128)(2,1)S(1)} %get-tuple-element.79.refs_0_, ...), custom_call_target="tpu_custom_call", output_to_operand_aliasing={{1}: (9, {}), {2}: (10, {})} | custom-call | flops 20000000000 | bytes 1024 | tf_op jit(solution)/shard_map/standardize/pallas_call | solution.py:152
  48.7 0.1 collective-permute-start.16
  48.8 0.0 collective-permute-done.6.refs_2_
  48.9 3.4 %collective-permute-done.12.refs_3_ = bf16[256,256]{1,0:T(8,128)(2,1)S(1)} collective-permute-done((bf16[256,256]{1,0:T(8,128)(2,1)S(1)}, bf16[256,256]{1,0:T(8,128)(2,1)S(1)}, u32[]{:S(2)}, u32[]{:S(2)}) %collective-permute-start.12) | collective-permute-done | bytes 131104 | tf_op jit(solution)/shard_map/cells_3_chunk_3/ppermute | solution.py:261
  52.2 1.6 %standardize.7 = (bf16[1024,256]{1,0:T(8,128)(2,1)S(1)}, bf16[4096,256]{1,0:T(8,128)(2,1)}, bf16[1024,1024]{1,0:T(8,128)(2,1)S(1)}, f32[8,128]{1,0:T(8,128)S(1)}) custom-call(f32[1,256]{1,0:T(1,128)S(1)} %get-tuple-element.96.mean_ref, bf16[256,256]{1,0:T(8,128)(2,1)S(1)} %get-tuple-element.64.refs_0_, ...), custom_call_target="tpu_custom_call", output_to_operand_aliasing={{1}: (9, {}), {2}: (10, {})} | custom-call | flops 20000000000 | bytes 1024 | tf_op jit(solution)/shard_map/standardize/pallas_call | solution.py:152
  53.9 0.8 copy-done.2
  54.6 2.9 %collective-permute-start.15 = (bf16[4096,256]{1,0:T(8,128)(2,1)}, bf16[4096,256]{1,0:T(8,128)(2,1)}, u32[]{:S(2)}, u32[]{:S(2)}) collective-permute-start(bf16[4096,256]{1,0:T(8,128)(2,1)} %get-tuple-element.87.refs_0_), channel_id=1, source_target_pairs={{0,1},{1,0},{2,3},{3,2},{4,5},{5,4},{6,7},{7,6},{8,9},{9,8},{10,11... | collective-permute-start | bytes 6291464 | tf_op jit(solution)/shard_map/near/ppermute | solution.py:268
  57.5 0.1 stack.70.place_ref
  57.6 0.1 pad_add_fusion.1.place_ref
  57.7 0.3 collective-permute-start.14
  58.0 2.2 %collective-permute-done.16.refs_3_ = bf16[1024,256]{1,0:T(8,128)(2,1)} collective-permute-done((bf16[1024,256]{1,0:T(8,128)(2,1)}, bf16[1024,256]{1,0:T(8,128)(2,1)}, u32[]{:S(2)}, u32[]{:S(2)}) %collective-permute-start.16) | collective-permute-done | bytes 524320 | tf_op jit(solution)/shard_map/far_2/ppermute | solution.py:264
  60.2 6.1 %collective-permute-start.17 = (bf16[1024,256]{1,0:T(8,128)(2,1)S(1)}, bf16[1024,256]{1,0:T(8,128)(2,1)S(1)}, u32[]{:S(2)}, u32[]{:S(2)}) collective-permute-start(bf16[1024,256]{1,0:T(8,128)(2,1)S(1)} %collective-permute-done.13.refs_1_), channel_id=1, source_target_pairs={{0,1},{1,0},{2,3},{3,2},{4,5},{5,4},{6,7},{7,6},{8,9},{9,8},{10,11... | collective-permute-start | bytes 1572872 | tf_op jit(solution)/shard_map/far_near_0/ppermute | solution.py:268
  66.3 0.0 collective-permute-start.18
  66.3 0.5 collective-permute-start.19
  66.8 7.4 %gram.3.refs_7_ = bf16[1,1024,4096]{2,1,0:T(8,128)(2,1)} custom-call(s32[4]{0:T(128)S(1)} %pad_add_fusion.1.place_ref, f32[8,128]{1,0:T(8,128)S(1)} %get-tuple-element.84.count_ref, bf16[1024,1024]{1,0:T(8,128)(2,1)S(1)} %get-tuple-element.85.left_ref, bf16[4096,256]{1,0:T(8,128)(2,1)} %get-tuple-element.87.refs_0_), custom_call_target="tpu_custom_call" | custom-call | flops 20000000000 | bytes 1024 | tf_op jit(solution)/shard_map/gram/pallas_call | solution.py:219
  74.2 15.2 %gram.4.refs_2_ = bf16[1,1024,4096]{2,1,0:T(8,128)(2,1)} custom-call(s32[10]{0:T(128)S(1)} %stack.70.place_ref, f32[8,128]{1,0:T(8,128)S(1)} %get-tuple-element.84.count_ref, bf16[1024,1024]{1,0:T(8,128)(2,1)S(1)} %get-tuple-element.85.left_ref, bf16[4096,256]{1,0:T(8,128)(2,1)} %collective-permute-done.15.refs_0_, ...), custom_call_target="tpu_custom_call", output_to_operand_aliasing={{}: (10, {})} | custom-call | flops 1024 | bytes 1024 | tf_op jit(solution)/shard_map/gram/pallas_call | solution.py:219
  89.4 0.1 collective-permute-start.20
  89.5 0.1 pad_add_fusion.place_ref
  89.6 2.0 %collective-permute-done.20.refs_1_ = bf16[1024,256]{1,0:T(8,128)(2,1)S(1)} collective-permute-done((bf16[1024,256]{1,0:T(8,128)(2,1)}, bf16[1024,256]{1,0:T(8,128)(2,1)S(1)}, u32[]{:S(2)}, u32[]{:S(2)}) %collective-permute-start.20) | collective-permute-done | bytes 524320 | tf_op jit(solution)/shard_map/far_near_last_0/ppermute | solution.py:268
  91.6 4.9 %gram.5 = bf16[1,1024,4096]{2,1,0:T(8,128)(2,1)} custom-call(s32[2]{0:T(128)S(1)} %pad_add_fusion.place_ref, f32[8,128]{1,0:T(8,128)S(1)} %get-tuple-element.84.count_ref, bf16[1024,1024]{1,0:T(8,128)(2,1)S(1)} %get-tuple-element.85.left_ref, bf16[1024,256]{1,0:T(8,128)(2,1)} %collective-permute-done.14.refs_0_, ...), custom_call_target="tpu_custom_call", output_to_operand_aliasing={{}: (5, {})} | custom-call | flops 1024 | bytes 1024 | tf_op jit(solution)/shard_map/gram/pallas_call | solution.py:219
  (13 shorter events, 0.0 us)
Async XLA Ops:
  0.7 1.2 %copy-start = (bf16[512,1024]{1,0:T(8,128)(2,1)S(1)}, bf16[512,1024]{1,0:T(8,128)(2,1)}, u32[]{:S(2)}) copy-start(bf16[512,1024]{1,0:T(8,128)(2,1)} %expr_ref.1) | copy-start | bytes 3145732
  1.9 0.7 copy-start.1
  4.3 4.6 %collective-permute-start = (bf16[272,256]{1,0:T(8,128)(2,1)S(1)}, bf16[272,256]{1,0:T(8,128)(2,1)S(1)}, u32[]{:S(2)}, u32[]{:S(2)}) collective-permute-start(bf16[272,256]{1,0:T(8,128)(2,1)S(1)} %get-tuple-element.52), channel_id=1, source_target_pairs={{0,4},{4,0},{8,12},{12,8},{1,5},{5,1},{9,13},{13,9},{2,6},{6,2},{1... | collective-permute-start | bytes 417800 | tf_op jit(solution)/shard_map/cells_1_chunk_0/ppermute | solution.py:261
  4.5 8.4 %collective-permute-start.2 = (bf16[272,256]{1,0:T(8,128)(2,1)S(1)}, bf16[272,256]{1,0:T(8,128)(2,1)S(1)}, u32[]{:S(2)}, u32[]{:S(2)}) collective-permute-start(bf16[272,256]{1,0:T(8,128)(2,1)S(1)} %get-tuple-element.55), channel_id=1, source_target_pairs={{0,8},{4,12},{8,0},{12,4},{1,9},{5,13},{9,1},{13,5},{2,10},{6,14},... | collective-permute-start | bytes 417800 | tf_op jit(solution)/shard_map/cells_2_chunk_0/ppermute | solution.py:261
  6.8 12.0 %collective-permute-start.4 = (bf16[272,256]{1,0:T(8,128)(2,1)S(1)}, bf16[272,256]{1,0:T(8,128)(2,1)S(1)}, u32[]{:S(2)}, u32[]{:S(2)}) collective-permute-start(bf16[272,256]{1,0:T(8,128)(2,1)S(1)} %get-tuple-element.58), channel_id=1, source_target_pairs={{0,12},{4,8},{8,4},{12,0},{1,13},{5,9},{9,5},{13,1},{2,14},{6,10},... | collective-permute-start | bytes 417800 | tf_op jit(solution)/shard_map/cells_3_chunk_0/ppermute | solution.py:261
  8.9 18.2 %collective-permute-start.1 = (bf16[256,256]{1,0:T(8,128)(2,1)S(1)}, bf16[256,256]{1,0:T(8,128)(2,1)S(1)}, u32[]{:S(2)}, u32[]{:S(2)}) collective-permute-start(bf16[256,256]{1,0:T(8,128)(2,1)S(1)} %get-tuple-element.53), channel_id=1, source_target_pairs={{0,4},{4,0},{8,12},{12,8},{1,5},{5,1},{9,13},{13,9},{2,6},{6,2},{1... | collective-permute-start | bytes 393224 | tf_op jit(solution)/shard_map/cells_1_chunk_1/ppermute | solution.py:261
  12.9 14.2 %collective-permute-start.3 = (bf16[256,256]{1,0:T(8,128)(2,1)S(1)}, bf16[256,256]{1,0:T(8,128)(2,1)S(1)}, u32[]{:S(2)}, u32[]{:S(2)}) collective-permute-start(bf16[256,256]{1,0:T(8,128)(2,1)S(1)} %get-tuple-element.56), channel_id=1, source_target_pairs={{0,8},{4,12},{8,0},{12,4},{1,9},{5,13},{9,1},{13,5},{2,10},{6,14},... | collective-permute-start | bytes 393224 | tf_op jit(solution)/shard_map/cells_2_chunk_1/ppermute | solution.py:261
  18.9 10.9 %collective-permute-start.5 = (bf16[256,256]{1,0:T(8,128)(2,1)S(1)}, bf16[256,256]{1,0:T(8,128)(2,1)S(1)}, u32[]{:S(2)}, u32[]{:S(2)}) collective-permute-start(bf16[256,256]{1,0:T(8,128)(2,1)S(1)} %get-tuple-element.59), channel_id=1, source_target_pairs={{0,12},{4,8},{8,4},{12,0},{1,13},{5,9},{9,5},{13,1},{2,14},{6,10},... | collective-permute-start | bytes 393224 | tf_op jit(solution)/shard_map/cells_3_chunk_1/ppermute | solution.py:261
  26.8 19.6 %collective-permute-start.13 = (bf16[1024,256]{1,0:T(8,128)(2,1)S(1)}, bf16[1024,256]{1,0:T(8,128)(2,1)S(1)}, u32[]{:S(2)}, u32[]{:S(2)}) collective-permute-start(bf16[1024,256]{1,0:T(8,128)(2,1)S(1)} %get-tuple-element.78), channel_id=1, source_target_pairs={{0,2},{1,3},{2,0},{3,1},{4,6},{5,7},{6,4},{7,5},{8,10},{9,11},{10,... | collective-permute-start | bytes 1572872 | tf_op jit(solution)/shard_map/far_0/ppermute | solution.py:264
  27.1 6.5 %collective-permute-start.7 = (bf16[256,256]{1,0:T(8,128)(2,1)S(1)}, bf16[256,256]{1,0:T(8,128)(2,1)S(1)}, u32[]{:S(2)}, u32[]{:S(2)}) collective-permute-start(bf16[256,256]{1,0:T(8,128)(2,1)S(1)} %get-tuple-element.67), channel_id=1, source_target_pairs={{0,4},{4,0},{8,12},{12,8},{1,5},{5,1},{9,13},{13,9},{2,6},{6,2},{1... | collective-permute-start | bytes 393224 | tf_op jit(solution)/shard_map/cells_1_chunk_2/ppermute | solution.py:261
  27.1 8.6 %collective-permute-start.9 = (bf16[256,256]{1,0:T(8,128)(2,1)S(1)}, bf16[256,256]{1,0:T(8,128)(2,1)S(1)}, u32[]{:S(2)}, u32[]{:S(2)}) collective-permute-start(bf16[256,256]{1,0:T(8,128)(2,1)S(1)} %get-tuple-element.71), channel_id=1, source_target_pairs={{0,8},{4,12},{8,0},{12,4},{1,9},{5,13},{9,1},{13,5},{2,10},{6,14},... | collective-permute-start | bytes 393224 | tf_op jit(solution)/shard_map/cells_2_chunk_2/ppermute | solution.py:261
  29.7 15.0 %collective-permute-start.11 = (bf16[256,256]{1,0:T(8,128)(2,1)S(1)}, bf16[256,256]{1,0:T(8,128)(2,1)S(1)}, u32[]{:S(2)}, u32[]{:S(2)}) collective-permute-start(bf16[256,256]{1,0:T(8,128)(2,1)S(1)} %get-tuple-element.75), channel_id=1, source_target_pairs={{0,12},{4,8},{8,4},{12,0},{1,13},{5,9},{9,5},{13,1},{2,14},{6,10},... | collective-permute-start | bytes 393224 | tf_op jit(solution)/shard_map/cells_3_chunk_2/ppermute | solution.py:261
  33.3 15.5 %collective-permute-start.6 = (bf16[1024,256]{1,0:T(8,128)(2,1)S(1)}, bf16[1024,256]{1,0:T(8,128)(2,1)S(1)}, u32[]{:S(2)}, u32[]{:S(2)}) collective-permute-start(bf16[1024,256]{1,0:T(8,128)(2,1)S(1)} %get-tuple-element.63), channel_id=1, source_target_pairs={{0,2},{1,3},{2,0},{3,1},{4,6},{5,7},{6,4},{7,5},{8,10},{9,11},{10,... | collective-permute-start | bytes 1572872 | tf_op jit(solution)/shard_map/far_1/ppermute | solution.py:264
  33.6 15.2 %collective-permute-start.8 = (bf16[256,256]{1,0:T(8,128)(2,1)S(1)}, bf16[256,256]{1,0:T(8,128)(2,1)S(1)}, u32[]{:S(2)}, u32[]{:S(2)}) collective-permute-start(bf16[256,256]{1,0:T(8,128)(2,1)S(1)} %get-tuple-element.68), channel_id=1, source_target_pairs={{0,4},{4,0},{8,12},{12,8},{1,5},{5,1},{9,13},{13,9},{2,6},{6,2},{1... | collective-permute-start | bytes 393224 | tf_op jit(solution)/shard_map/cells_1_chunk_3/ppermute | solution.py:261
  35.7 13.2 %collective-permute-start.10 = (bf16[256,256]{1,0:T(8,128)(2,1)S(1)}, bf16[256,256]{1,0:T(8,128)(2,1)S(1)}, u32[]{:S(2)}, u32[]{:S(2)}) collective-permute-start(bf16[256,256]{1,0:T(8,128)(2,1)S(1)} %get-tuple-element.72), channel_id=1, source_target_pairs={{0,8},{4,12},{8,0},{12,4},{1,9},{5,13},{9,1},{13,5},{2,10},{6,14},... | collective-permute-start | bytes 393224 | tf_op jit(solution)/shard_map/cells_2_chunk_3/ppermute | solution.py:261
  44.7 7.5 %collective-permute-start.12 = (bf16[256,256]{1,0:T(8,128)(2,1)S(1)}, bf16[256,256]{1,0:T(8,128)(2,1)S(1)}, u32[]{:S(2)}, u32[]{:S(2)}) collective-permute-start(bf16[256,256]{1,0:T(8,128)(2,1)S(1)} %get-tuple-element.76), channel_id=1, source_target_pairs={{0,12},{4,8},{8,4},{12,0},{1,13},{5,9},{9,5},{13,1},{2,14},{6,10},... | collective-permute-start | bytes 393224 | tf_op jit(solution)/shard_map/cells_3_chunk_3/ppermute | solution.py:261
  48.7 11.5 %collective-permute-start.16 = (bf16[1024,256]{1,0:T(8,128)(2,1)}, bf16[1024,256]{1,0:T(8,128)(2,1)}, u32[]{:S(2)}, u32[]{:S(2)}) collective-permute-start(bf16[1024,256]{1,0:T(8,128)(2,1)} %get-tuple-element.88), channel_id=1, source_target_pairs={{0,2},{1,3},{2,0},{3,1},{4,6},{5,7},{6,4},{7,5},{8,10},{9,11},{10,... | collective-permute-start | bytes 1572872 | tf_op jit(solution)/shard_map/far_2/ppermute | solution.py:264
  53.8 0.8 copy-start.2
  54.6 19.6 %collective-permute-start.15 = (bf16[4096,256]{1,0:T(8,128)(2,1)}, bf16[4096,256]{1,0:T(8,128)(2,1)}, u32[]{:S(2)}, u32[]{:S(2)}) collective-permute-start(bf16[4096,256]{1,0:T(8,128)(2,1)} %get-tuple-element.87.refs_0_), channel_id=1, source_target_pairs={{0,1},{1,0},{2,3},{3,2},{4,5},{5,4},{6,7},{7,6},{8,9},{9,8},{10,11... | collective-permute-start | bytes 6291464 | tf_op jit(solution)/shard_map/near/ppermute | solution.py:268
  57.7 31.7 %collective-permute-start.14 = (bf16[1024,256]{1,0:T(8,128)(2,1)}, bf16[1024,256]{1,0:T(8,128)(2,1)}, u32[]{:S(2)}, u32[]{:S(2)}) collective-permute-start(bf16[1024,256]{1,0:T(8,128)(2,1)} %copy-done.2), channel_id=1, source_target_pairs={{0,2},{1,3},{2,0},{3,1},{4,6},{5,7},{6,4},{7,5},{8,10},{9,11},{10,... | collective-permute-start | bytes 1572872 | tf_op jit(solution)/shard_map/far_3/ppermute | solution.py:264
  60.2 14.0 %collective-permute-start.17 = (bf16[1024,256]{1,0:T(8,128)(2,1)S(1)}, bf16[1024,256]{1,0:T(8,128)(2,1)S(1)}, u32[]{:S(2)}, u32[]{:S(2)}) collective-permute-start(bf16[1024,256]{1,0:T(8,128)(2,1)S(1)} %collective-permute-done.13.refs_1_), channel_id=1, source_target_pairs={{0,1},{1,0},{2,3},{3,2},{4,5},{5,4},{6,7},{7,6},{8,9},{9,8},{10,11... | collective-permute-start | bytes 1572872 | tf_op jit(solution)/shard_map/far_near_0/ppermute | solution.py:268
  66.3 7.9 %collective-permute-start.18 = (bf16[1024,256]{1,0:T(8,128)(2,1)S(1)}, bf16[1024,256]{1,0:T(8,128)(2,1)S(1)}, u32[]{:S(2)}, u32[]{:S(2)}) collective-permute-start(bf16[1024,256]{1,0:T(8,128)(2,1)S(1)} %collective-permute-done.6.refs_2_), channel_id=1, source_target_pairs={{0,1},{1,0},{2,3},{3,2},{4,5},{5,4},{6,7},{7,6},{8,9},{9,8},{10,11... | collective-permute-start | bytes 1572872 | tf_op jit(solution)/shard_map/far_near_1/ppermute | solution.py:268
  66.3 7.9 %collective-permute-start.19 = (bf16[1024,256]{1,0:T(8,128)(2,1)}, bf16[1024,256]{1,0:T(8,128)(2,1)S(1)}, u32[]{:S(2)}, u32[]{:S(2)}) collective-permute-start(bf16[1024,256]{1,0:T(8,128)(2,1)} %collective-permute-done.16.refs_3_), channel_id=1, source_target_pairs={{0,1},{1,0},{2,3},{3,2},{4,5},{5,4},{6,7},{7,6},{8,9},{9,8},{10,11... | collective-permute-start | bytes 1572872 | tf_op jit(solution)/shard_map/far_near_2/ppermute | solution.py:268
  89.4 2.2 %collective-permute-start.20 = (bf16[1024,256]{1,0:T(8,128)(2,1)}, bf16[1024,256]{1,0:T(8,128)(2,1)S(1)}, u32[]{:S(2)}, u32[]{:S(2)}) collective-permute-start(bf16[1024,256]{1,0:T(8,128)(2,1)} %collective-permute-done.14.refs_0_), channel_id=1, source_target_pairs={{0,1},{1,0},{2,3},{3,2},{4,5},{5,4},{6,7},{7,6},{8,9},{9,8},{10,11... | collective-permute-start | bytes 1572872 | tf_op jit(solution)/shard_map/far_near_last_0/ppermute | solution.py:268

commit v4 on v3

--- a/solution.py
+++ b/solution.py
@@ -172,61 +172,84 @@
     )(*args)
 
 
-def gram_kernel(spots, arrays, place_ref, count_ref, left_ref, *refs):
+def gram_kernel(groups, arrays, strip, place_ref, count_ref, left_ref, *refs):
     sources = refs[:arrays]
-    out_ref, left, panel, tile, left_sem, panel_sem, tile_sem = refs[-7:]
-    slots, width = panel.shape[1:]
-    panels = len(spots)
+    out_ref, panel, tile, panel_sem, tile_sem = refs[-5:]
+    rows, slots = left_ref.shape
     inverse = 1.0 / count_ref[0:1, 0:1]
 
-    def fetch(j):
-        source, row = spots[j]
-        block = sources[source].at[pl.ds(row, slots), :]
-        return pltpu.make_async_copy(block, panel.at[j % 2], panel_sem.at[j % 2])
-
-    def store(j):
-        column = pl.multiple_of(place_ref[j] * width, width)
-        return pltpu.make_async_copy(
-            tile.at[j % 2], out_ref.at[0, :, pl.ds(column, width)], tile_sem.at[j % 2]
-        )
-
-    fetch(0).start()
-    left_copy = pltpu.make_async_copy(left_ref, left, left_sem)
-    left_copy.start()
-    left_copy.wait()
-    for j in range(panels):
-        if j + 1 < panels:
-            fetch(j + 1).start()
-        fetch(j).wait()
-        if j >= 2:
-            store(j - 2).wait()
-        product = jnp.dot(left[...], panel[j % 2], preferred_element_type=jnp.float32)
-        tile[j % 2] = (product * inverse).astype(jnp.bfloat16)
-        store(j).start()
-    for j in range(max(panels - 2, 0), panels):
-        store(j).wait()
-
-
-def gram(shape, places, count, left, right, before, cost):
+    def fetch(g):
+        copies, column = [], 0
+        for source, row, width in groups[g]:
+            copies.append(
+                pltpu.make_async_copy(
+                    sources[source].at[pl.ds(row, slots), :],
+                    panel.at[g % 2, :, pl.ds(column, width)],
+                    panel_sem.at[g % 2, len(copies)],
+                )
+            )
+            column += width
+        return copies, column
+
+    for copy in fetch(0)[0]:
+        copy.start()
+    stores = []
+    for g in range(len(groups)):
+        if g + 1 < len(groups):
+            for copy in fetch(g + 1)[0]:
+                copy.start()
+        copies, columns = fetch(g)
+        for copy in copies:
+            copy.wait()
+        place = pl.multiple_of(place_ref[g] * 128, 128)
+        for row in range(0, rows, strip):
+            slot = len(stores) % 2
+            if len(stores) >= 2:
+                stores[-2].wait()
+            product = jnp.dot(
+                left_ref[row : row + strip, :],
+                panel[g % 2, :, 0:columns],
+                preferred_element_type=jnp.float32,
+            )
+            tile[slot, :, 0:columns] = (product * inverse).astype(jnp.bfloat16)
+            stores.append(
+                pltpu.make_async_copy(
+                    tile.at[slot, :, pl.ds(0, columns)],
+                    out_ref.at[0, pl.ds(row, strip), pl.ds(place, columns)],
+                    tile_sem.at[slot],
+                )
+            )
+            stores[-1].start()
+    for store in stores[-2:]:
+        store.wait()
+
+
+def gram(shape, count, left, groups, before, cost):
     rows, slots = left.shape
-    width = right[0].shape[1]
-    spots = [
-        (i, row) for i, panels in enumerate(right) for row in range(0, panels.shape[0], slots)
-    ]
-    args = [jnp.stack(places).astype(jnp.int32), count, left, *right]
+    strip = min(rows, 256)
+    places = jnp.stack([place for place, _ in groups]) // 128
+    arrays, layout = [], []
+    for _, panels in groups:
+        layout.append([])
+        for array, index in panels:
+            if not any(array is other for other in arrays):
+                arrays.append(array)
+            source = [array is other for other in arrays].index(True)
+            layout[-1].append((source, index * slots, array.shape[1]))
+    most = max(len(panels) for panels in layout)
+    widest = max(sum(width for _, _, width in panels) for panels in layout)
+    args = [places.astype(jnp.int32), count, left, *arrays]
     args += [] if before is None else [before]
-    specs = [pl.BlockSpec(memory_space=pltpu.SMEM), whole] + [anywhere] * (len(args) - 2)
+    specs = [pl.BlockSpec(memory_space=pltpu.SMEM), whole, whole] + [anywhere] * (len(args) - 3)
     return pl.pallas_call(
-        functools.partial(gram_kernel, spots, len(right)),
+        functools.partial(gram_kernel, layout, len(arrays), strip),
         in_specs=specs,
         out_specs=anywhere,
         out_shape=jax.ShapeDtypeStruct(shape, jnp.bfloat16),
         scratch_shapes=[
-            pltpu.VMEM((rows, slots), jnp.bfloat16),
-            pltpu.VMEM((2, slots, width), jnp.bfloat16),
-            pltpu.VMEM((2, rows, width), jnp.bfloat16),
-            pltpu.SemaphoreType.DMA,
-            pltpu.SemaphoreType.DMA((2,)),
+            pltpu.VMEM((2, slots, widest), jnp.bfloat16),
+            pltpu.VMEM((2, strip, widest), jnp.bfloat16),
+            pltpu.SemaphoreType.DMA((2, most)),
             pltpu.SemaphoreType.DMA((2,)),
         ],
         input_output_aliases={} if before is None else {len(args) - 1: 0},
@@ -291,24 +314,27 @@
         with jax.named_scope(f"far_{k}"):
             far.append([across(scaled, d) for d in range(1, chips)])
 
-    column = lambda source, k: source * chunks + k
     distant = [(me + blocks - d * cores) % blocks for d in range(1, chips)]
     shape = (1, panel, panel * blocks)
 
     last = chunks - 1
-    there = sum(far[:last], [])
     near = side("near", own)
-    far_near = [side(f"far_near_{i}", p, own, *there) for i, p in enumerate(there)]
-    places = [column(me, k) for k in range(chunks)]
-    out = gram(shape, places, count, left, [own], None, lengthy)
-    places = [column(me ^ 1, k) for k in range(chunks)]
-    places += [column(source, k) for k in range(last) for source in distant]
-    places += [column(source ^ 1, k) for k in range(last) for source in distant]
-    out = gram(shape, places, count, left, [near, *there, *far_near], out, brief)
-    far_near = [side(f"far_near_last_{i}", p, out) for i, p in enumerate(far[last])]
-    places = [column(source, last) for source in distant]
-    places += [column(source ^ 1, last) for source in distant]
-    return gram(shape, places, count, left, [*far[last], *far_near], out, brief)
+    far_near = [
+        [side(f"far_near_{k}", p, own, *far[last - 1]) for p in far[k]] for k in range(last)
+    ]
+    groups = [(me * panel, [(own, k) for k in range(chunks)])]
+    out = gram(shape, count, left, groups, None, lengthy)
+    groups = [((me ^ 1) * panel, [(near, k) for k in range(chunks)])]
+    for d, source in enumerate(distant):
+        groups.append((source * panel, [(far[k][d], 0) for k in range(last)]))
+        groups.append(((source ^ 1) * panel, [(far_near[k][d], 0) for k in range(last)]))
+    out = gram(shape, count, left, groups, out, brief)
+    far_near = [side(f"far_near_{last}", p, out) for p in far[last]]
+    edge = last * width
+    groups = [(source * panel + edge, [(p, 0)]) for source, p in zip(distant, far[last])]
+    out = gram(shape, count, left, groups, out, brief)
+    groups = [((source ^ 1) * panel + edge, [(p, 0)]) for source, p in zip(distant, far_near)]
+    return gram(shape, count, left, groups, out, brief)
 
 
 def solution(mesh):

time: 97 us -> 91.3 us (0.941)
  Pallas kernels: 37.5 us -> 33.8 us
  waiting for transfers between devices: 25.9 us -> 24 us
    pallas_call x3 -> x4, Pallas kernels: 27.4 us -> 23.7 us  [gram(): pl.pallas_call(functools.partial(gram_kernel, layout, len(arrays), strip)...]
    ppermute x5, waiting for transfers between devices: 2.03 us -> 0.01 us  [side(): lax.ppermute(after(panel_, *waits), 'blk', [(b, b ^ 1) for b in range(blo...]
  transfers between devices with their start and end apart: 21 -> 21, of which waited for: 9 -> 8; matrix products, arithmetic and copies ran while one was open for 1% -> 1% of each run, Pallas kernels for 32% -> 32%
where the time goes in v4:
time: 91.3 us; the launch traced here: 91 us
  Pallas kernels  33.8 us (37%)
  starting transfers between devices  28.6 us (31%)
  waiting for transfers between devices  24 us (26%)
  local copies, waits for them, and re-layouts  4.11 us (5%)
    pallas_call x4, Pallas kernels, gram(): pl.pallas_call(functools.partial(gram_kernel, layout, len(arrays), strip)...  23.7 us
    ppermute x12, waiting for transfers between devices, swap(): return lax.ppermute(block, 'cells', [(s, s ^ by) for s in range(types)])  21.7 us
    ppermute x12, starting transfers between devices, swap(): return lax.ppermute(block, 'cells', [(s, s ^ by) for s in range(types)])  17.9 us
    ppermute x5, starting transfers between devices, side(): lax.ppermute(after(panel_, *waits), 'blk', [(b, b ^ 1) for b in range(blo...  9.64 us
    pallas_call x4, Pallas kernels, standardize(): pl.pallas_call(functools.partial(standardize_kernel, types, cap, lead, se...  8.44 us
    unnamed x6, local copies, waits for them, and re-layouts  2.7 us
    ppermute x4, waiting for transfers between devices, across(): lax.ppermute(panel_, 'blk', [(b, (b + by * cores) % blocks) for b in rang...  2.32 us
  transfers between devices with their start and end apart: 21, of which 8 were waited for; matrix products, arithmetic and copies ran while one was open for 1% of the time, Pallas kernels for 32%

profile of v4, /device:TPU:11, one launch (start us, length us, event | category | flops | bytes accessed | tf_op | source)
XLA Modules:
  0.0 91.0 jit_solution(18068304868500918062)
XLA Ops:
  0.0 0.7 reshape.23.factor_ref
  0.7 1.2 %copy-done = bf16[512,1024]{1,0:T(8,128)(2,1)S(1)} copy-done((bf16[512,1024]{1,0:T(8,128)(2,1)S(1)}, bf16[512,1024]{1,0:T(8,128)(2,1)}, u32[]{:S(2)}) %copy-start) | copy-done | bytes 1048600
  1.9 0.7 copy-done.1
  2.6 1.7 %pack.1 = (bf16[272,256]{1,0:T(8,128)(2,1)S(1)}, bf16[272,256]{1,0:T(8,128)(2,1)S(1)}, bf16[272,256]{1,0:T(8,128)(2,1)S(1)}, bf16[272,256]{1,0:T(8,128)(2,1)S(1)...) custom-call(s32[1]{0:T(128)} %bitcast.2.home_ref, ...), custom_call_target="tpu_custom_call" | custom-call | flops 1024 | bytes 1024 | tf_op jit(solution)/shard_map/pack/pallas_call | solution.py:69
  4.3 0.2 collective-permute-start
  4.5 2.3 %collective-permute-start.2 = (bf16[272,256]{1,0:T(8,128)(2,1)S(1)}, bf16[272,256]{1,0:T(8,128)(2,1)S(1)}, u32[]{:S(2)}, u32[]{:S(2)}) collective-permute-start(bf16[272,256]{1,0:T(8,128)(2,1)S(1)} %get-tuple-element.55), channel_id=1, source_target_pairs={{0,8},{4,12},{8,0},{12,4},{1,9},{5,13},{9,1},{13,5},{2,10},{6,14},... | collective-permute-start | bytes 417800 | tf_op jit(solution)/shard_map/cells_2_chunk_0/ppermute | solution.py:284
  6.8 0.2 collective-permute-start.4
  7.0 0.7 fusion
  7.7 1.2 %collective-permute-done.refs_1_.refs_5_ = bf16[272,256]{1,0:T(8,128)(2,1)S(1)} collective-permute-done((bf16[272,256]{1,0:T(8,128)(2,1)S(1)}, bf16[272,256]{1,0:T(8,128)(2,1)S(1)}, u32[]{:S(2)}, u32[]{:S(2)}) %collective-permute-start) | collective-permute-done | bytes 139296 | tf_op jit(solution)/shard_map/cells_1_chunk_0/ppermute | solution.py:284
  8.9 0.2 collective-permute-start.1
  9.1 3.8 %collective-permute-done.2.refs_2_.refs_6_ = bf16[272,256]{1,0:T(8,128)(2,1)S(1)} collective-permute-done((bf16[272,256]{1,0:T(8,128)(2,1)S(1)}, bf16[272,256]{1,0:T(8,128)(2,1)S(1)}, u32[]{:S(2)}, u32[]{:S(2)}) %collective-permute-start.2) | collective-permute-done | bytes 139296 | tf_op jit(solution)/shard_map/cells_2_chunk_0/ppermute | solution.py:284
  12.9 0.1 collective-permute-start.3
  13.0 5.9 %collective-permute-done.4.refs_3_.refs_7_ = bf16[272,256]{1,0:T(8,128)(2,1)S(1)} collective-permute-done((bf16[272,256]{1,0:T(8,128)(2,1)S(1)}, bf16[272,256]{1,0:T(8,128)(2,1)S(1)}, u32[]{:S(2)}, u32[]{:S(2)}) %collective-permute-start.4) | collective-permute-done | bytes 139296 | tf_op jit(solution)/shard_map/cells_3_chunk_0/ppermute | solution.py:284
  18.9 5.7 %collective-permute-start.5 = (bf16[256,256]{1,0:T(8,128)(2,1)S(1)}, bf16[256,256]{1,0:T(8,128)(2,1)S(1)}, u32[]{:S(2)}, u32[]{:S(2)}) collective-permute-start(bf16[256,256]{1,0:T(8,128)(2,1)S(1)} %get-tuple-element.59), channel_id=1, source_target_pairs={{0,12},{4,8},{8,4},{12,0},{1,13},{5,9},{9,5},{13,1},{2,14},{6,10},... | collective-permute-start | bytes 393224 | tf_op jit(solution)/shard_map/cells_3_chunk_1/ppermute | solution.py:284
  24.6 2.2 %standardize.4 = (bf16[1024,256]{1,0:T(8,128)(2,1)S(1)}, bf16[4096,256]{1,0:T(8,128)(2,1)}, bf16[1024,1024]{1,0:T(8,128)(2,1)S(1)}, f32[8,128]{1,0:T(8,128)}) custom-call(f32[1,256]{1,0:T(1,128)S(1)} %get-tuple-element.94.mean_ref, bf16[272,256]{1,0:T(8,128)(2,1)S(1)} %get-tuple-element.60.refs_0_.refs_4_, ...), custom_call_target="tpu_custom_call" | custom-call | flops 20000000000 | bytes 1024 | tf_op jit(solution)/shard_map/standardize/pallas_call | solution.py:152
  26.8 0.3 collective-permute-start.13
  27.1 2.5 %collective-permute-start.9 = (bf16[256,256]{1,0:T(8,128)(2,1)S(1)}, bf16[256,256]{1,0:T(8,128)(2,1)S(1)}, u32[]{:S(2)}, u32[]{:S(2)}) collective-permute-start(bf16[256,256]{1,0:T(8,128)(2,1)S(1)} %get-tuple-element.71), channel_id=1, source_target_pairs={{0,8},{4,12},{8,0},{12,4},{1,9},{5,13},{9,1},{13,5},{2,10},{6,14},... | collective-permute-start | bytes 393224 | tf_op jit(solution)/shard_map/cells_2_chunk_2/ppermute | solution.py:284
  29.7 0.1 collective-permute-done.5.refs_3_
  29.8 1.4 %collective-permute-start.11 = (bf16[256,256]{1,0:T(8,128)(2,1)S(1)}, bf16[256,256]{1,0:T(8,128)(2,1)S(1)}, u32[]{:S(2)}, u32[]{:S(2)}) collective-permute-start(bf16[256,256]{1,0:T(8,128)(2,1)S(1)} %get-tuple-element.75), channel_id=1, source_target_pairs={{0,12},{4,8},{8,4},{12,0},{1,13},{5,9},{9,5},{13,1},{2,14},{6,10},... | collective-permute-start | bytes 393224 | tf_op jit(solution)/shard_map/cells_3_chunk_2/ppermute | solution.py:284
  31.1 2.2 %standardize.5 = (bf16[1024,256]{1,0:T(8,128)(2,1)S(1)}, bf16[4096,256]{1,0:T(8,128)(2,1)}, bf16[1024,1024]{1,0:T(8,128)(2,1)S(1)}, f32[8,128]{1,0:T(8,128)}) custom-call(f32[1,256]{1,0:T(1,128)S(1)} %get-tuple-element.95.mean_ref, bf16[256,256]{1,0:T(8,128)(2,1)S(1)} %get-tuple-element.50.refs_0_, ...), custom_call_target="tpu_custom_call", output_to_operand_aliasing={{1}: (9, {}), {2}: (10, {})} | custom-call | flops 20000000000 | bytes 1024 | tf_op jit(solution)/shard_map/standardize/pallas_call | solution.py:152
  33.3 0.3 collective-permute-start.6
  33.7 0.6 collective-permute-start.8
  34.2 1.5 %collective-permute-done.9.refs_2_ = bf16[256,256]{1,0:T(8,128)(2,1)S(1)} collective-permute-done((bf16[256,256]{1,0:T(8,128)(2,1)S(1)}, bf16[256,256]{1,0:T(8,128)(2,1)S(1)}, u32[]{:S(2)}, u32[]{:S(2)}) %collective-permute-start.9) | collective-permute-done | bytes 131104 | tf_op jit(solution)/shard_map/cells_2_chunk_2/ppermute | solution.py:284
  35.7 3.2 %collective-permute-start.10 = (bf16[256,256]{1,0:T(8,128)(2,1)S(1)}, bf16[256,256]{1,0:T(8,128)(2,1)S(1)}, u32[]{:S(2)}, u32[]{:S(2)}) collective-permute-start(bf16[256,256]{1,0:T(8,128)(2,1)S(1)} %get-tuple-element.72), channel_id=1, source_target_pairs={{0,8},{4,12},{8,0},{12,4},{1,9},{5,13},{9,1},{13,5},{2,10},{6,14},... | collective-permute-start | bytes 393224 | tf_op jit(solution)/shard_map/cells_2_chunk_3/ppermute | solution.py:284
  38.9 5.8 %collective-permute-done.11.refs_3_ = bf16[256,256]{1,0:T(8,128)(2,1)S(1)} collective-permute-done((bf16[256,256]{1,0:T(8,128)(2,1)S(1)}, bf16[256,256]{1,0:T(8,128)(2,1)S(1)}, u32[]{:S(2)}, u32[]{:S(2)}) %collective-permute-start.11) | collective-permute-done | bytes 131104 | tf_op jit(solution)/shard_map/cells_3_chunk_2/ppermute | solution.py:284
  44.7 1.6 %collective-permute-start.12 = (bf16[256,256]{1,0:T(8,128)(2,1)S(1)}, bf16[256,256]{1,0:T(8,128)(2,1)S(1)}, u32[]{:S(2)}, u32[]{:S(2)}) collective-permute-start(bf16[256,256]{1,0:T(8,128)(2,1)S(1)} %get-tuple-element.76), channel_id=1, source_target_pairs={{0,12},{4,8},{8,4},{12,0},{1,13},{5,9},{9,5},{13,1},{2,14},{6,10},... | collective-permute-start | bytes 393224 | tf_op jit(solution)/shard_map/cells_3_chunk_3/ppermute | solution.py:284
  46.3 0.0 collective-permute-done.13.refs_1_
  46.3 2.4 %standardize.6 = (bf16[1024,256]{1,0:T(8,128)(2,1)}, bf16[4096,256]{1,0:T(8,128)(2,1)}, bf16[1024,1024]{1,0:T(8,128)(2,1)S(1)}, f32[8,128]{1,0:T(8,128)}) custom-call(f32[1,256]{1,0:T(1,128)S(1)} %get-tuple-element.93.mean_ref, bf16[256,256]{1,0:T(8,128)(2,1)S(1)} %get-tuple-element.79.refs_0_, ...), custom_call_target="tpu_custom_call", output_to_operand_aliasing={{1}: (9, {}), {2}: (10, {})} | custom-call | flops 20000000000 | bytes 1024 | tf_op jit(solution)/shard_map/standardize/pallas_call | solution.py:152
  48.8 0.1 collective-permute-start.16
  48.8 0.0 collective-permute-done.6.refs_2_
  48.8 0.0 collective-permute-done.8.refs_1_
  48.9 3.4 %collective-permute-done.12.refs_3_ = bf16[256,256]{1,0:T(8,128)(2,1)S(1)} collective-permute-done((bf16[256,256]{1,0:T(8,128)(2,1)S(1)}, bf16[256,256]{1,0:T(8,128)(2,1)S(1)}, u32[]{:S(2)}, u32[]{:S(2)}) %collective-permute-start.12) | collective-permute-done | bytes 131104 | tf_op jit(solution)/shard_map/cells_3_chunk_3/ppermute | solution.py:284
  52.2 1.6 %standardize.7 = (bf16[1024,256]{1,0:T(8,128)(2,1)S(1)}, bf16[4096,256]{1,0:T(8,128)(2,1)}, bf16[1024,1024]{1,0:T(8,128)(2,1)S(1)}, f32[8,128]{1,0:T(8,128)S(1)}) custom-call(f32[1,256]{1,0:T(1,128)S(1)} %get-tuple-element.96.mean_ref, bf16[256,256]{1,0:T(8,128)(2,1)S(1)} %get-tuple-element.64.refs_0_, ...), custom_call_target="tpu_custom_call", output_to_operand_aliasing={{1}: (9, {}), {2}: (10, {})} | custom-call | flops 20000000000 | bytes 1024 | tf_op jit(solution)/shard_map/standardize/pallas_call | solution.py:152
  53.9 0.8 copy-done.2
  54.7 2.9 %collective-permute-start.15 = (bf16[4096,256]{1,0:T(8,128)(2,1)}, bf16[4096,256]{1,0:T(8,128)(2,1)}, u32[]{:S(2)}, u32[]{:S(2)}) collective-permute-start(bf16[4096,256]{1,0:T(8,128)(2,1)} %get-tuple-element.87.refs_0_), channel_id=1, source_target_pairs={{0,1},{1,0},{2,3},{3,2},{4,5},{5,4},{6,7},{7,6},{8,9},{9,8},{10,11... | collective-permute-start | bytes 6291464 | tf_op jit(solution)/shard_map/near/ppermute | solution.py:291
  57.5 0.1 and_select_fusion.place_ref
  57.6 0.3 collective-permute-start.14
  57.9 2.3 %collective-permute-done.16.refs_3_ = bf16[1024,256]{1,0:T(8,128)(2,1)} collective-permute-done((bf16[1024,256]{1,0:T(8,128)(2,1)}, bf16[1024,256]{1,0:T(8,128)(2,1)}, u32[]{:S(2)}, u32[]{:S(2)}) %collective-permute-start.16) | collective-permute-done | bytes 524320 | tf_op jit(solution)/shard_map/far_2/ppermute | solution.py:287
  60.2 6.2 %collective-permute-start.17 = (bf16[1024,256]{1,0:T(8,128)(2,1)S(1)}, bf16[1024,256]{1,0:T(8,128)(2,1)S(1)}, u32[]{:S(2)}, u32[]{:S(2)}) collective-permute-start(bf16[1024,256]{1,0:T(8,128)(2,1)S(1)} %collective-permute-done.13.refs_1_), channel_id=1, source_target_pairs={{0,1},{1,0},{2,3},{3,2},{4,5},{5,4},{6,7},{7,6},{8,9},{9,8},{10,11... | collective-permute-start | bytes 1572872 | tf_op jit(solution)/shard_map/far_near_0/ppermute | solution.py:291
  66.4 0.0 collective-permute-start.18
  66.4 0.5 collective-permute-start.19
  66.9 5.3 %gram.4.refs_7_ = bf16[1,1024,4096]{2,1,0:T(8,128)(2,1)} custom-call(s32[1]{0:T(128)S(6)} %select_n.26.place_ref, f32[8,128]{1,0:T(8,128)S(1)} %get-tuple-element.84.count_ref, bf16[1024,1024]{1,0:T(8,128)(2,1)S(1)} %get-tuple-element.85.left_ref, bf16[4096,256]{1,0:T(8,128)(2,1)} %get-tuple-element.87.refs_0_), custom_call_target="tpu_custom_call" | custom-call | flops 20000000000 | bytes 1024 | tf_op jit(solution)/shard_map/gram/pallas_call | solution.py:244
  72.3 0.0 collective-permute-done.17.refs_4_
  72.3 0.0 collective-permute-done.15.refs_0_
  72.3 12.0 %gram.5.refs_1_ = bf16[1,1024,4096]{2,1,0:T(8,128)(2,1)} custom-call(s32[3]{0:T(128)S(1)} %and_select_fusion.place_ref, f32[8,128]{1,0:T(8,128)S(1)} %get-tuple-element.84.count_ref, bf16[1024,1024]{1,0:T(8,128)(2,1)S(1)} %get-tuple-element.85.left_ref, bf16[4096,256]{1,0:T(8,128)(2,1)} %collective-permute-done.15.refs_0_, ...), custom_call_target="tpu_custom_call", output_to_operand_aliasing={{}: (10, {})} | custom-call | flops 1024 | bytes 1024 | tf_op jit(solution)/shard_map/gram/pallas_call | solution.py:244
  84.3 0.1 collective-permute-start.20
  84.4 3.7 %gram.6.refs_1_ = bf16[1,1024,4096]{2,1,0:T(8,128)(2,1)} custom-call(s32[1]{0:T(128)S(6)} %select_n.27.place_ref, f32[8,128]{1,0:T(8,128)S(1)} %get-tuple-element.84.count_ref, bf16[1024,1024]{1,0:T(8,128)(2,1)S(1)} %get-tuple-element.85.left_ref, bf16[1024,256]{1,0:T(8,128)(2,1)} %collective-permute-done.14.refs_0_, ...), custom_call_target="tpu_custom_call", output_to_operand_aliasing={{}: (4, {})} | custom-call | flops 1024 | bytes 1024 | tf_op jit(solution)/shard_map/gram/pallas_call | solution.py:244
  88.1 2.7 %gram.7 = bf16[1,1024,4096]{2,1,0:T(8,128)(2,1)} custom-call(s32[1]{0:T(128)S(6)} %select_n.24.place_ref, f32[8,128]{1,0:T(8,128)S(1)} %get-tuple-element.84.count_ref, bf16[1024,1024]{1,0:T(8,128)(2,1)S(1)} %get-tuple-element.85.left_ref, bf16[1024,256]{1,0:T(8,128)(2,1)S(1)} %collective-permute-done.20.refs_0_, ...), custom_call_target="tpu_custom_call", output_to_operand_aliasing={{}: (4, {})} | custom-call | flops 1024 | bytes 1024 | tf_op jit(solution)/shard_map/gram/pallas_call | solution.py:244
  (12 shorter events, 0.0 us)
Async XLA Ops:
  0.7 1.2 %copy-start = (bf16[512,1024]{1,0:T(8,128)(2,1)S(1)}, bf16[512,1024]{1,0:T(8,128)(2,1)}, u32[]{:S(2)}) copy-start(bf16[512,1024]{1,0:T(8,128)(2,1)} %expr_ref.1) | copy-start | bytes 3145732
  1.9 0.7 copy-start.1
  4.3 4.6 %collective-permute-start = (bf16[272,256]{1,0:T(8,128)(2,1)S(1)}, bf16[272,256]{1,0:T(8,128)(2,1)S(1)}, u32[]{:S(2)}, u32[]{:S(2)}) collective-permute-start(bf16[272,256]{1,0:T(8,128)(2,1)S(1)} %get-tuple-element.52), channel_id=1, source_target_pairs={{0,4},{4,0},{8,12},{12,8},{1,5},{5,1},{9,13},{13,9},{2,6},{6,2},{1... | collective-permute-start | bytes 417800 | tf_op jit(solution)/shard_map/cells_1_chunk_0/ppermute | solution.py:284
  4.5 8.4 %collective-permute-start.2 = (bf16[272,256]{1,0:T(8,128)(2,1)S(1)}, bf16[272,256]{1,0:T(8,128)(2,1)S(1)}, u32[]{:S(2)}, u32[]{:S(2)}) collective-permute-start(bf16[272,256]{1,0:T(8,128)(2,1)S(1)} %get-tuple-element.55), channel_id=1, source_target_pairs={{0,8},{4,12},{8,0},{12,4},{1,9},{5,13},{9,1},{13,5},{2,10},{6,14},... | collective-permute-start | bytes 417800 | tf_op jit(solution)/shard_map/cells_2_chunk_0/ppermute | solution.py:284
  6.8 12.0 %collective-permute-start.4 = (bf16[272,256]{1,0:T(8,128)(2,1)S(1)}, bf16[272,256]{1,0:T(8,128)(2,1)S(1)}, u32[]{:S(2)}, u32[]{:S(2)}) collective-permute-start(bf16[272,256]{1,0:T(8,128)(2,1)S(1)} %get-tuple-element.58), channel_id=1, source_target_pairs={{0,12},{4,8},{8,4},{12,0},{1,13},{5,9},{9,5},{13,1},{2,14},{6,10},... | collective-permute-start | bytes 417800 | tf_op jit(solution)/shard_map/cells_3_chunk_0/ppermute | solution.py:284
  8.9 18.2 %collective-permute-start.1 = (bf16[256,256]{1,0:T(8,128)(2,1)S(1)}, bf16[256,256]{1,0:T(8,128)(2,1)S(1)}, u32[]{:S(2)}, u32[]{:S(2)}) collective-permute-start(bf16[256,256]{1,0:T(8,128)(2,1)S(1)} %get-tuple-element.53), channel_id=1, source_target_pairs={{0,4},{4,0},{8,12},{12,8},{1,5},{5,1},{9,13},{13,9},{2,6},{6,2},{1... | collective-permute-start | bytes 393224 | tf_op jit(solution)/shard_map/cells_1_chunk_1/ppermute | solution.py:284
  12.9 14.2 %collective-permute-start.3 = (bf16[256,256]{1,0:T(8,128)(2,1)S(1)}, bf16[256,256]{1,0:T(8,128)(2,1)S(1)}, u32[]{:S(2)}, u32[]{:S(2)}) collective-permute-start(bf16[256,256]{1,0:T(8,128)(2,1)S(1)} %get-tuple-element.56), channel_id=1, source_target_pairs={{0,8},{4,12},{8,0},{12,4},{1,9},{5,13},{9,1},{13,5},{2,10},{6,14},... | collective-permute-start | bytes 393224 | tf_op jit(solution)/shard_map/cells_2_chunk_1/ppermute | solution.py:284
  18.9 10.9 %collective-permute-start.5 = (bf16[256,256]{1,0:T(8,128)(2,1)S(1)}, bf16[256,256]{1,0:T(8,128)(2,1)S(1)}, u32[]{:S(2)}, u32[]{:S(2)}) collective-permute-start(bf16[256,256]{1,0:T(8,128)(2,1)S(1)} %get-tuple-element.59), channel_id=1, source_target_pairs={{0,12},{4,8},{8,4},{12,0},{1,13},{5,9},{9,5},{13,1},{2,14},{6,10},... | collective-permute-start | bytes 393224 | tf_op jit(solution)/shard_map/cells_3_chunk_1/ppermute | solution.py:284
  26.8 19.6 %collective-permute-start.13 = (bf16[1024,256]{1,0:T(8,128)(2,1)S(1)}, bf16[1024,256]{1,0:T(8,128)(2,1)S(1)}, u32[]{:S(2)}, u32[]{:S(2)}) collective-permute-start(bf16[1024,256]{1,0:T(8,128)(2,1)S(1)} %get-tuple-element.78), channel_id=1, source_target_pairs={{0,2},{1,3},{2,0},{3,1},{4,6},{5,7},{6,4},{7,5},{8,10},{9,11},{10,... | collective-permute-start | bytes 1572872 | tf_op jit(solution)/shard_map/far_0/ppermute | solution.py:287
  27.1 6.5 %collective-permute-start.7 = (bf16[256,256]{1,0:T(8,128)(2,1)S(1)}, bf16[256,256]{1,0:T(8,128)(2,1)S(1)}, u32[]{:S(2)}, u32[]{:S(2)}) collective-permute-start(bf16[256,256]{1,0:T(8,128)(2,1)S(1)} %get-tuple-element.67), channel_id=1, source_target_pairs={{0,4},{4,0},{8,12},{12,8},{1,5},{5,1},{9,13},{13,9},{2,6},{6,2},{1... | collective-permute-start | bytes 393224 | tf_op jit(solution)/shard_map/cells_1_chunk_2/ppermute | solution.py:284
  27.1 8.6 %collective-permute-start.9 = (bf16[256,256]{1,0:T(8,128)(2,1)S(1)}, bf16[256,256]{1,0:T(8,128)(2,1)S(1)}, u32[]{:S(2)}, u32[]{:S(2)}) collective-permute-start(bf16[256,256]{1,0:T(8,128)(2,1)S(1)} %get-tuple-element.71), channel_id=1, source_target_pairs={{0,8},{4,12},{8,0},{12,4},{1,9},{5,13},{9,1},{13,5},{2,10},{6,14},... | collective-permute-start | bytes 393224 | tf_op jit(solution)/shard_map/cells_2_chunk_2/ppermute | solution.py:284
  29.8 15.0 %collective-permute-start.11 = (bf16[256,256]{1,0:T(8,128)(2,1)S(1)}, bf16[256,256]{1,0:T(8,128)(2,1)S(1)}, u32[]{:S(2)}, u32[]{:S(2)}) collective-permute-start(bf16[256,256]{1,0:T(8,128)(2,1)S(1)} %get-tuple-element.75), channel_id=1, source_target_pairs={{0,12},{4,8},{8,4},{12,0},{1,13},{5,9},{9,5},{13,1},{2,14},{6,10},... | collective-permute-start | bytes 393224 | tf_op jit(solution)/shard_map/cells_3_chunk_2/ppermute | solution.py:284
  33.3 15.5 %collective-permute-start.6 = (bf16[1024,256]{1,0:T(8,128)(2,1)S(1)}, bf16[1024,256]{1,0:T(8,128)(2,1)S(1)}, u32[]{:S(2)}, u32[]{:S(2)}) collective-permute-start(bf16[1024,256]{1,0:T(8,128)(2,1)S(1)} %get-tuple-element.63), channel_id=1, source_target_pairs={{0,2},{1,3},{2,0},{3,1},{4,6},{5,7},{6,4},{7,5},{8,10},{9,11},{10,... | collective-permute-start | bytes 1572872 | tf_op jit(solution)/shard_map/far_1/ppermute | solution.py:287
  33.7 15.2 %collective-permute-start.8 = (bf16[256,256]{1,0:T(8,128)(2,1)S(1)}, bf16[256,256]{1,0:T(8,128)(2,1)S(1)}, u32[]{:S(2)}, u32[]{:S(2)}) collective-permute-start(bf16[256,256]{1,0:T(8,128)(2,1)S(1)} %get-tuple-element.68), channel_id=1, source_target_pairs={{0,4},{4,0},{8,12},{12,8},{1,5},{5,1},{9,13},{13,9},{2,6},{6,2},{1... | collective-permute-start | bytes 393224 | tf_op jit(solution)/shard_map/cells_1_chunk_3/ppermute | solution.py:284
  35.7 13.2 %collective-permute-start.10 = (bf16[256,256]{1,0:T(8,128)(2,1)S(1)}, bf16[256,256]{1,0:T(8,128)(2,1)S(1)}, u32[]{:S(2)}, u32[]{:S(2)}) collective-permute-start(bf16[256,256]{1,0:T(8,128)(2,1)S(1)} %get-tuple-element.72), channel_id=1, source_target_pairs={{0,8},{4,12},{8,0},{12,4},{1,9},{5,13},{9,1},{13,5},{2,10},{6,14},... | collective-permute-start | bytes 393224 | tf_op jit(solution)/shard_map/cells_2_chunk_3/ppermute | solution.py:284
  44.7 7.5 %collective-permute-start.12 = (bf16[256,256]{1,0:T(8,128)(2,1)S(1)}, bf16[256,256]{1,0:T(8,128)(2,1)S(1)}, u32[]{:S(2)}, u32[]{:S(2)}) collective-permute-start(bf16[256,256]{1,0:T(8,128)(2,1)S(1)} %get-tuple-element.76), channel_id=1, source_target_pairs={{0,12},{4,8},{8,4},{12,0},{1,13},{5,9},{9,5},{13,1},{2,14},{6,10},... | collective-permute-start | bytes 393224 | tf_op jit(solution)/shard_map/cells_3_chunk_3/ppermute | solution.py:284
  48.8 11.5 %collective-permute-start.16 = (bf16[1024,256]{1,0:T(8,128)(2,1)}, bf16[1024,256]{1,0:T(8,128)(2,1)}, u32[]{:S(2)}, u32[]{:S(2)}) collective-permute-start(bf16[1024,256]{1,0:T(8,128)(2,1)} %get-tuple-element.88), channel_id=1, source_target_pairs={{0,2},{1,3},{2,0},{3,1},{4,6},{5,7},{6,4},{7,5},{8,10},{9,11},{10,... | collective-permute-start | bytes 1572872 | tf_op jit(solution)/shard_map/far_2/ppermute | solution.py:287
  53.9 0.8 copy-start.2
  54.7 17.6 %collective-permute-start.15 = (bf16[4096,256]{1,0:T(8,128)(2,1)}, bf16[4096,256]{1,0:T(8,128)(2,1)}, u32[]{:S(2)}, u32[]{:S(2)}) collective-permute-start(bf16[4096,256]{1,0:T(8,128)(2,1)} %get-tuple-element.87.refs_0_), channel_id=1, source_target_pairs={{0,1},{1,0},{2,3},{3,2},{4,5},{5,4},{6,7},{7,6},{8,9},{9,8},{10,11... | collective-permute-start | bytes 6291464 | tf_op jit(solution)/shard_map/near/ppermute | solution.py:291
  57.6 26.7 %collective-permute-start.14 = (bf16[1024,256]{1,0:T(8,128)(2,1)}, bf16[1024,256]{1,0:T(8,128)(2,1)}, u32[]{:S(2)}, u32[]{:S(2)}) collective-permute-start(bf16[1024,256]{1,0:T(8,128)(2,1)} %copy-done.2), channel_id=1, source_target_pairs={{0,2},{1,3},{2,0},{3,1},{4,6},{5,7},{6,4},{7,5},{8,10},{9,11},{10,... | collective-permute-start | bytes 1572872 | tf_op jit(solution)/shard_map/far_3/ppermute | solution.py:287
  60.2 12.0 %collective-permute-start.17 = (bf16[1024,256]{1,0:T(8,128)(2,1)S(1)}, bf16[1024,256]{1,0:T(8,128)(2,1)S(1)}, u32[]{:S(2)}, u32[]{:S(2)}) collective-permute-start(bf16[1024,256]{1,0:T(8,128)(2,1)S(1)} %collective-permute-done.13.refs_1_), channel_id=1, source_target_pairs={{0,1},{1,0},{2,3},{3,2},{4,5},{5,4},{6,7},{7,6},{8,9},{9,8},{10,11... | collective-permute-start | bytes 1572872 | tf_op jit(solution)/shard_map/far_near_0/ppermute | solution.py:291
  66.4 5.9 %collective-permute-start.18 = (bf16[1024,256]{1,0:T(8,128)(2,1)S(1)}, bf16[1024,256]{1,0:T(8,128)(2,1)S(1)}, u32[]{:S(2)}, u32[]{:S(2)}) collective-permute-start(bf16[1024,256]{1,0:T(8,128)(2,1)S(1)} %collective-permute-done.6.refs_2_), channel_id=1, source_target_pairs={{0,1},{1,0},{2,3},{3,2},{4,5},{5,4},{6,7},{7,6},{8,9},{9,8},{10,11... | collective-permute-start | bytes 1572872 | tf_op jit(solution)/shard_map/far_near_1/ppermute | solution.py:291
  66.4 5.9 %collective-permute-start.19 = (bf16[1024,256]{1,0:T(8,128)(2,1)}, bf16[1024,256]{1,0:T(8,128)(2,1)S(1)}, u32[]{:S(2)}, u32[]{:S(2)}) collective-permute-start(bf16[1024,256]{1,0:T(8,128)(2,1)} %collective-permute-done.16.refs_3_), channel_id=1, source_target_pairs={{0,1},{1,0},{2,3},{3,2},{4,5},{5,4},{6,7},{7,6},{8,9},{9,8},{10,11... | collective-permute-start | bytes 1572872 | tf_op jit(solution)/shard_map/far_near_2/ppermute | solution.py:291
  84.3 3.8 %collective-permute-start.20 = (bf16[1024,256]{1,0:T(8,128)(2,1)}, bf16[1024,256]{1,0:T(8,128)(2,1)S(1)}, u32[]{:S(2)}, u32[]{:S(2)}) collective-permute-start(bf16[1024,256]{1,0:T(8,128)(2,1)} %collective-permute-done.14.refs_0_), channel_id=1, source_target_pairs={{0,1},{1,0},{2,3},{3,2},{4,5},{5,4},{6,7},{7,6},{8,9},{9,8},{10,11... | collective-permute-start | bytes 1572872 | tf_op jit(solution)/shard_map/far_near_3/ppermute | solution.py:291

commit v5 on v4

--- a/solution.py
+++ b/solution.py
@@ -21,7 +21,7 @@
 def pack_kernel(types, cap, widths, home_ref, type_ref, factor_ref, expr_ref, *outs):
     rows = expr_ref.shape[0]
     home = home_ref[0]
-    kind = type_ref[...]
+    kind = type_ref[...].reshape(1, rows)
     rel = jnp.bitwise_xor(kind, home)
     lines = max(types, 8)
     hot = lax.broadcasted_iota(jnp.int32, (lines, rows), 0) == rel
@@ -35,9 +35,8 @@
     running = jnp.dot(hot_f.astype(jnp.bfloat16), upper, preferred_element_type=jnp.float32)
     rank = jnp.sum(hot_f * running, axis=0, keepdims=True) - 1.0
     slot = rel * cap + rank.astype(jnp.int32)
-    factor = jnp.broadcast_to(factor_ref[...].astype(jnp.float32), (TILE, rows)).astype(
-        jnp.bfloat16
-    )
+    factor = factor_ref[...].astype(jnp.float32).reshape(1, rows)
+    factor = jnp.broadcast_to(factor, (TILE, rows)).astype(jnp.bfloat16)
     values = expr_ref[...]
     for j in range(types):
         place = jnp.where(
@@ -74,7 +73,7 @@
         compiler_params=pltpu.CompilerParams(vmem_limit_bytes=VMEM),
         cost_estimate=brief,
         name="pack",
-    )(home, cell_type.reshape(1, rows), size_factor.reshape(1, rows), expression)
+    )(home, cell_type, size_factor, expression)
     return [flat[k * types : (k + 1) * types] for k in range(len(widths))]
 
 
@@ -83,7 +82,7 @@
     tails = refs[types : 2 * types] if separate else blocks
     base = 0 if separate else cap
     refs = refs[2 * types :] if separate else refs[types:]
-    scaled_ref, all_ref, turned_ref, count_ref, work, turned, sems = refs[-7:]
+    scaled_ref, turned_ref, count_ref, all_ref, work, turned, sems = refs[-7:]
     mean = mean_ref[...]
     width = mean.shape[1]
     piece = min(lead, cap)
@@ -124,18 +123,18 @@
         work[j * cap : (j + 1) * cap, :] = scaled
     slots = types * cap
     rows = pl.ds(chunk * slots, slots)
-    scaled_copy = pltpu.make_async_copy(scaled_ref, all_ref.at[rows, :], sems.at[0])
-    scaled_copy.start()
+    copies = [pltpu.make_async_copy(scaled_ref, all_ref.at[rows, :], sems.at[0])]
+    copies[0].start()
     turned[...] = jnp.transpose(work[...]).astype(jnp.bfloat16)
     rows = pl.ds(chunk * width, width)
-    turned_copy = pltpu.make_async_copy(turned, turned_ref.at[rows, :], sems.at[1])
-    turned_copy.start()
-    scaled_copy.wait()
-    turned_copy.wait()
+    copies.append(pltpu.make_async_copy(turned, turned_ref.at[rows, :], sems.at[1]))
+    copies[-1].start()
+    for copy in copies:
+        copy.wait()
     count_ref[...] = jnp.broadcast_to(count, count_ref.shape)
 
 
-def standardize(types, cap, lead, mean, chunk, chunks, blocks, first, before):
+def standardize(types, cap, lead, mean, chunk, chunks, blocks, first, left, own):
     width = mean.shape[1]
     separate = first is not blocks
     slots = types * cap
@@ -144,22 +143,24 @@
     if separate:
         specs += [pl.BlockSpec((TILE, lead), lambda i: (cap // TILE, 0))] * types
         args += list(first)
+    shapes = [
+        jax.ShapeDtypeStruct((slots, width), jnp.bfloat16),
+        jax.ShapeDtypeStruct((chunks * width, slots), jnp.bfloat16),
+        jax.ShapeDtypeStruct((8, 128), jnp.float32),
+        jax.ShapeDtypeStruct((chunks * slots, width), jnp.bfloat16),
+    ]
     aliases = {}
-    if before is not None:
-        aliases = {len(args): 1, len(args) + 1: 2}
-        specs += [anywhere] * 2
-        args += list(before)
+    for value, output in ((left, 1), (own, 3)):
+        if value is not None:
+            aliases[len(args)] = output
+            specs.append(anywhere)
+            args.append(value)
     return pl.pallas_call(
         functools.partial(standardize_kernel, types, cap, lead, separate, chunk),
         grid=(1,),
-        out_shape=[
-            jax.ShapeDtypeStruct((slots, width), jnp.bfloat16),
-            jax.ShapeDtypeStruct((chunks * slots, width), jnp.bfloat16),
-            jax.ShapeDtypeStruct((chunks * width, slots), jnp.bfloat16),
-            jax.ShapeDtypeStruct((8, 128), jnp.float32),
-        ],
+        out_shape=shapes,
         in_specs=specs,
-        out_specs=[whole, anywhere, anywhere, whole],
+        out_specs=[whole, anywhere, whole, anywhere],
         scratch_shapes=[
             pltpu.VMEM((slots, width), jnp.float32),
             pltpu.VMEM((width, slots), jnp.bfloat16),
@@ -172,10 +173,10 @@
     )(*args)
 
 
-def gram_kernel(groups, arrays, strip, place_ref, count_ref, left_ref, *refs):
+def gram_kernel(groups, spans, arrays, strip, place_ref, count_ref, left_ref, *refs):
     sources = refs[:arrays]
     out_ref, panel, tile, panel_sem, tile_sem = refs[-5:]
-    rows, slots = left_ref.shape
+    slots = left_ref.shape[1]
     inverse = 1.0 / count_ref[0:1, 0:1]
 
     def fetch(g):
@@ -202,7 +203,7 @@
         for copy in copies:
             copy.wait()
         place = pl.multiple_of(place_ref[g] * 128, 128)
-        for row in range(0, rows, strip):
+        for row in range(*spans[g], strip):
             slot = len(stores) % 2
             if len(stores) >= 2:
                 stores[-2].wait()
@@ -227,9 +228,10 @@
 def gram(shape, count, left, groups, before, cost):
     rows, slots = left.shape
     strip = min(rows, 256)
-    places = jnp.stack([place for place, _ in groups]) // 128
+    spans = [span for span, _, _ in groups]
+    places = jnp.stack([place for _, place, _ in groups]) // 128
     arrays, layout = [], []
-    for _, panels in groups:
+    for _, _, panels in groups:
         layout.append([])
         for array, index in panels:
             if not any(array is other for other in arrays):
@@ -242,7 +244,7 @@
     args += [] if before is None else [before]
     specs = [pl.BlockSpec(memory_space=pltpu.SMEM), whole, whole] + [anywhere] * (len(args) - 3)
     return pl.pallas_call(
-        functools.partial(gram_kernel, layout, len(arrays), strip),
+        functools.partial(gram_kernel, layout, spans, len(arrays), strip),
         in_specs=specs,
         out_specs=anywhere,
         out_shape=jax.ShapeDtypeStruct(shape, jnp.bfloat16),
@@ -292,48 +294,79 @@
 
     mean = gene_mean.reshape(1, panel)
     order = sorted(range(1, types), key=lambda j: (j == 1, j))
-    left, own, far, before = None, None, [], None
-    first = None
+    distant = [(me + blocks - d * cores) % blocks for d in range(1, chips)]
+    shape = (1, panel, panel * blocks)
+    early, last = 2, chunks - 1
+    upper, lower, every = (0, early * width), (early * width, panel), (0, panel)
+    left, own, out, far, before = None, None, None, [], None
     for k in range(chunks):
         arrived = [packed[k][0]] + [None] * (types - 1)
         for j in order:
             block = packed[k][j]
             if k:
-                block = after(block, before[j])
+                block = after(block, before[j], *([out] if k == early + 1 and j != 1 else []))
             with jax.named_scope(f"cells_{j}_chunk_{k}"):
                 arrived[j] = swap(block, j)
         before = list(arrived)
         waits = far[k - 2] if k >= 2 else []
+        if k == early:
+            groups = [
+                (upper, me * panel, [(own, i) for i in range(early)]),
+            ]
+            groups += [
+                (upper, source * panel, [(p, 0)]) for source, p in zip(distant, far[0])
+            ]
+            out = gram(shape, count, left, groups, None, brief)
+            waits = waits + [out]
         if waits:
             arrived[0] = after(arrived[0], *waits)
-        first = first or arrived
+        if k == 0:
+            first = arrived
         piece = mean[:, k * width : (k + 1) * width]
-        scaled, own, left, count = standardize(
-            types, cap, width, piece, k, chunks, arrived, first, (own, left) if k else None
+        scaled, left, count, own = standardize(
+            types, cap, width, piece, k, chunks, arrived, first, left, own
         )
         with jax.named_scope(f"far_{k}"):
             far.append([across(scaled, d) for d in range(1, chips)])
 
-    distant = [(me + blocks - d * cores) % blocks for d in range(1, chips)]
-    shape = (1, panel, panel * blocks)
-
-    last = chunks - 1
     near = side("near", own)
     far_near = [
-        [side(f"far_near_{k}", p, own, *far[last - 1]) for p in far[k]] for k in range(last)
-    ]
-    groups = [(me * panel, [(own, k) for k in range(chunks)])]
-    out = gram(shape, count, left, groups, None, lengthy)
-    groups = [((me ^ 1) * panel, [(near, k) for k in range(chunks)])]
+        [side(f"far_near_{k}", p, own, *far[last - 1]) for p in far[k]]
+        for k in range(max(last - 1, 1))
+    ]
+    edge = early * width
+    groups = []
+    if out is not None:
+        rest = [(own, i) for i in range(early, chunks)]
+        groups.append((upper, me * panel + edge, rest))
+        groups.append((lower, me * panel, [(own, i) for i in range(chunks)]))
+    else:
+        groups.append((every, me * panel, [(own, i) for i in range(chunks)]))
+    out = gram(shape, count, left, groups, out, lengthy)
+    begun = lower if chunks > early else every
+    groups = [
+        (every, (me ^ 1) * panel, [(near, i) for i in range(chunks)]),
+    ]
     for d, source in enumerate(distant):
-        groups.append((source * panel, [(far[k][d], 0) for k in range(last)]))
-        groups.append(((source ^ 1) * panel, [(far_near[k][d], 0) for k in range(last)]))
+        groups.append((begun, source * panel, [(far[0][d], 0)]))
+        if last > 1:
+            panels = [(far[k][d], 0) for k in range(1, last)]
+            groups.append((every, source * panel + width, panels))
+        panels = [(got[d], 0) for got in far_near]
+        groups.append((every, (source ^ 1) * panel, panels))
     out = gram(shape, count, left, groups, out, brief)
-    far_near = [side(f"far_near_{last}", p, out) for p in far[last]]
+    start = len(far_near)
+    far_near = [
+        [side(f"far_near_{k}", p, out) for p in far[k]] for k in range(start, chunks)
+    ]
     edge = last * width
-    groups = [(source * panel + edge, [(p, 0)]) for source, p in zip(distant, far[last])]
+    groups = [(every, source * panel + edge, [(p, 0)]) for source, p in zip(distant, far[last])]
     out = gram(shape, count, left, groups, out, brief)
-    groups = [((source ^ 1) * panel + edge, [(p, 0)]) for source, p in zip(distant, far_near)]
+    edge = start * width
+    groups = [
+        (every, (source ^ 1) * panel + edge, [(got[d], 0) for got in far_near])
+        for d, source in enumerate(distant)
+    ]
     return gram(shape, count, left, groups, out, brief)
 
 

time: 91.3 us -> 95.4 us (1.045)
  the two profiles are of different devices: /device:TPU:11 before, /device:TPU:0 now
where the time goes in v5:
time: 95.4 us; the launch traced here: 95.1 us
  starting transfers between devices  35.1 us (37%)
  Pallas kernels  33.3 us (35%)
  waiting for transfers between devices  18.2 us (19%)
  local copies, waits for them, and re-layouts  7.88 us (8%)
    ppermute x12, starting transfers between devices, swap(): return lax.ppermute(block, 'cells', [(s, s ^ by) for s in range(types)])  28.7 us
    pallas_call x5, Pallas kernels, gram(): pl.pallas_call(functools.partial(gram_kernel, layout, spans, len(arrays),...  25 us
    ppermute x12, waiting for transfers between devices, swap(): return lax.ppermute(block, 'cells', [(s, s ^ by) for s in range(types)])  12.7 us
    unnamed x34, local copies, waits for them, and re-layouts  7.15 us
    pallas_call x4, Pallas kernels, standardize(): pl.pallas_call(functools.partial(standardize_kernel, types, cap, lead, se...  6.05 us
    ppermute x4, waiting for transfers between devices, across(): lax.ppermute(panel_, 'blk', [(b, (b + by * cores) % blocks) for b in rang...  5.55 us
    ppermute x4, starting transfers between devices, across(): lax.ppermute(panel_, 'blk', [(b, (b + by * cores) % blocks) for b in rang...  5.28 us
    pallas_call x1, Pallas kernels, pack(): pl.pallas_call(functools.partial(pack_kernel, types, cap, widths), out_sh...  2.22 us
  transfers between devices with their start and end apart: 21, of which 5 were waited for; matrix products, arithmetic and copies ran while one was open for 1% of the time, Pallas kernels for 28%

profile of v5, /device:TPU:0, one launch (start us, length us, event | category | flops | bytes accessed | tf_op | source)
XLA Modules:
  0.0 95.1 jit_solution(3845682608849714418)
XLA Ops:
  0.0 1.2 %copy-done = bf16[512,1024]{1,0:T(8,128)(2,1)S(1)} copy-done((bf16[512,1024]{1,0:T(8,128)(2,1)S(1)}, bf16[512,1024]{1,0:T(8,128)(2,1)}, u32[]{:S(2)}) %copy-start) | copy-done | bytes 1048600
  1.2 0.7 copy-done.1
  1.9 0.7 copy-done.2
  2.6 2.2 %pack.1 = (bf16[272,256]{1,0:T(8,128)(2,1)S(1)}, bf16[272,256]{1,0:T(8,128)(2,1)S(1)}, bf16[272,256]{1,0:T(8,128)(2,1)S(1)}, bf16[272,256]{1,0:T(8,128)(2,1)S(1)...) custom-call(s32[1]{0:T(128)} %bitcast.2.home_ref, ...), custom_call_target="tpu_custom_call" | custom-call | flops 1024 | bytes 1024 | tf_op jit(solution)/shard_map/pack/pallas_call | solution.py:68
  4.8 0.6 copy-done.3
  5.5 0.6 copy-done.5
  6.1 0.6 copy-done.7
  6.7 0.6 copy-done.9
  7.4 0.7 copy-done.11
  8.0 0.7 copy-done.13
  8.7 0.6 copy-done.15
  9.4 3.0 %collective-permute-start = (bf16[272,256]{1,0:T(8,128)(2,1)S(1)}, bf16[272,256]{1,0:T(8,128)(2,1)S(1)}, u32[]{:S(2)}, u32[]{:S(2)}) collective-permute-start(bf16[272,256]{1,0:T(8,128)(2,1)S(1)} %get-tuple-element.53), channel_id=1, source_target_pairs={{0,4},{4,0},{8,12},{12,8},{1,5},{5,1},{9,13},{13,9},{2,6},{6,2},{1... | collective-permute-start | bytes 417800 | tf_op jit(solution)/shard_map/cells_1_chunk_0/ppermute | solution.py:286
  12.4 2.6 %collective-permute-start.2 = (bf16[272,256]{1,0:T(8,128)(2,1)S(1)}, bf16[272,256]{1,0:T(8,128)(2,1)S(1)}, u32[]{:S(2)}, u32[]{:S(2)}) collective-permute-start(bf16[272,256]{1,0:T(8,128)(2,1)S(1)} %get-tuple-element.56), channel_id=1, source_target_pairs={{0,8},{4,12},{8,0},{12,4},{1,9},{5,13},{9,1},{13,5},{2,10},{6,14},... | collective-permute-start | bytes 417800 | tf_op jit(solution)/shard_map/cells_2_chunk_0/ppermute | solution.py:286
  15.0 0.7 fusion
  15.7 0.1 and_select_fusion.2.place_ref
  15.8 2.0 %collective-permute-done.refs_1_.refs_5_ = bf16[272,256]{1,0:T(8,128)(2,1)S(1)} collective-permute-done((bf16[272,256]{1,0:T(8,128)(2,1)S(1)}, bf16[272,256]{1,0:T(8,128)(2,1)S(1)}, u32[]{:S(2)}, u32[]{:S(2)}) %collective-permute-start) | collective-permute-done | bytes 139296 | tf_op jit(solution)/shard_map/cells_1_chunk_0/ppermute | solution.py:286
  17.8 0.6 collective-permute-start.1
  18.5 7.4 %collective-permute-done.2.refs_2_.refs_6_ = bf16[272,256]{1,0:T(8,128)(2,1)S(1)} collective-permute-done((bf16[272,256]{1,0:T(8,128)(2,1)S(1)}, bf16[272,256]{1,0:T(8,128)(2,1)S(1)}, u32[]{:S(2)}, u32[]{:S(2)}) %collective-permute-start.2) | collective-permute-done | bytes 139296 | tf_op jit(solution)/shard_map/cells_2_chunk_0/ppermute | solution.py:286
  25.9 0.0 collective-permute-start.3
  25.9 2.8 %collective-permute-start.5 = (bf16[256,256]{1,0:T(8,128)(2,1)}, bf16[256,256]{1,0:T(8,128)(2,1)S(1)}, u32[]{:S(2)}, u32[]{:S(2)}) collective-permute-start(bf16[256,256]{1,0:T(8,128)(2,1)} %get-tuple-element.60), channel_id=1, source_target_pairs={{0,12},{4,8},{8,4},{12,0},{1,13},{5,9},{9,5},{13,1},{2,14},{6,10},... | collective-permute-start | bytes 393224 | tf_op jit(solution)/shard_map/cells_3_chunk_1/ppermute | solution.py:286
  28.7 1.9 %standardize.4 = (bf16[1024,256]{1,0:T(8,128)(2,1)S(1)}, bf16[1024,1024]{1,0:T(8,128)(2,1)S(1)}, f32[8,128]{1,0:T(8,128)}, bf16[4096,256]{1,0:T(8,128)(2,1)S(1)}) custom-call(f32[1,256]{1,0:T(1,128)S(1)} %get-tuple-element.96.mean_ref, bf16[272,256]{1,0:T(8,128)(2,1)S(1)} %get-tuple-element.61.refs_0_.refs_4_, ...), custom_call_target="tpu_custom_call" | custom-call | flops 20000000000 | bytes 1024 | tf_op jit(solution)/shard_map/standardize/pallas_call | solution.py:158
  30.7 1.6 %collective-permute-start.10 = (bf16[1024,256]{1,0:T(8,128)(2,1)S(1)}, bf16[1024,256]{1,0:T(8,128)(2,1)S(1)}, u32[]{:S(2)}, u32[]{:S(2)}) collective-permute-start(bf16[1024,256]{1,0:T(8,128)(2,1)S(1)} %get-tuple-element.76), channel_id=1, source_target_pairs={{0,2},{1,3},{2,0},{3,1},{4,6},{5,7},{6,4},{7,5},{8,10},{9,11},{10,... | collective-permute-start | bytes 1572872 | tf_op jit(solution)/shard_map/far_0/ppermute | solution.py:289
  32.3 7.7 %collective-permute-start.7 = (bf16[256,256]{1,0:T(8,128)(2,1)S(1)}, bf16[256,256]{1,0:T(8,128)(2,1)S(1)}, u32[]{:S(2)}, u32[]{:S(2)}) collective-permute-start(bf16[256,256]{1,0:T(8,128)(2,1)S(1)} %copy-done.14), channel_id=1, source_target_pairs={{0,4},{4,0},{8,12},{12,8},{1,5},{5,1},{9,13},{13,9},{2,6},{6,2},{1... | collective-permute-start | bytes 393224 | tf_op jit(solution)/shard_map/cells_1_chunk_2/ppermute | solution.py:286
  40.0 0.1 collective-permute-start.9
  40.1 2.3 %collective-permute-start.12 = (bf16[256,256]{1,0:T(8,128)(2,1)S(1)}, bf16[256,256]{1,0:T(8,128)(2,1)S(1)}, u32[]{:S(2)}, u32[]{:S(2)}) collective-permute-start(bf16[256,256]{1,0:T(8,128)(2,1)S(1)} %copy-done.12), channel_id=1, source_target_pairs={{0,12},{4,8},{8,4},{12,0},{1,13},{5,9},{9,5},{13,1},{2,14},{6,10},... | collective-permute-start | bytes 393224 | tf_op jit(solution)/shard_map/cells_3_chunk_2/ppermute | solution.py:286
  42.4 1.2 %standardize.5 = (bf16[1024,256]{1,0:T(8,128)(2,1)S(1)}, bf16[1024,1024]{1,0:T(8,128)(2,1)S(1)}, f32[8,128]{1,0:T(8,128)S(1)}, bf16[4096,256]{1,0:T(8,128)(2,1)S(1)}) custom-call(f32[1,256]{1,0:T(1,128)S(1)} %get-tuple-element.97.mean_ref, bf16[256,256]{1,0:T(8,128)(2,1)S(1)} %copy-done.16, ...), custom_call_target="tpu_custom_call", output_to_operand_aliasing={{1}: (9, {}), {3}: (10, {})} | custom-call | flops 20000000000 | bytes 1024 | tf_op jit(solution)/shard_map/standardize/pallas_call | solution.py:158
  43.6 0.6 collective-permute-start.6
  44.2 2.1 %collective-permute-done.7.refs_1_ = bf16[256,256]{1,0:T(8,128)(2,1)S(1)} collective-permute-done((bf16[256,256]{1,0:T(8,128)(2,1)S(1)}, bf16[256,256]{1,0:T(8,128)(2,1)S(1)}, u32[]{:S(2)}, u32[]{:S(2)}) %collective-permute-start.7) | collective-permute-done | bytes 131104 | tf_op jit(solution)/shard_map/cells_1_chunk_2/ppermute | solution.py:286
  46.3 2.2 %collective-permute-start.8 = (bf16[256,256]{1,0:T(8,128)(2,1)S(1)}, bf16[256,256]{1,0:T(8,128)(2,1)S(1)}, u32[]{:S(2)}, u32[]{:S(2)}) collective-permute-start(bf16[256,256]{1,0:T(8,128)(2,1)S(1)} %copy-done.6), channel_id=1, source_target_pairs={{0,4},{4,0},{8,12},{12,8},{1,5},{5,1},{9,13},{13,9},{2,6},{6,2},{1... | collective-permute-start | bytes 393224 | tf_op jit(solution)/shard_map/cells_1_chunk_3/ppermute | solution.py:286
  48.5 3.4 %gram.5.refs_1_ = bf16[1,1024,4096]{2,1,0:T(8,128)(2,1)} custom-call(s32[2]{0:T(128)S(1)} %and_select_fusion.2.place_ref, f32[8,128]{1,0:T(8,128)S(1)} %get-tuple-element.73.count_ref, bf16[1024,1024]{1,0:T(8,128)(2,1)S(1)} %get-tuple-element.74.left_ref.refs_8_, bf16[4096,256]{1,0:T(8,128)(2,1)S(1)} %get-tuple-element.75.refs_0_.refs_9_, ...), custom_call_target="tpu_custom_call" | custom-call | flops 1024 | bytes 1024 | tf_op jit(solution)/shard_map/gram/pallas_call | solution.py:246
  51.9 4.9 %collective-permute-start.11 = (bf16[256,256]{1,0:T(8,128)(2,1)S(1)}, bf16[256,256]{1,0:T(8,128)(2,1)S(1)}, u32[]{:S(2)}, u32[]{:S(2)}) collective-permute-start(bf16[256,256]{1,0:T(8,128)(2,1)S(1)} %copy-done.4), channel_id=1, source_target_pairs={{0,8},{4,12},{8,0},{12,4},{1,9},{5,13},{9,1},{13,5},{2,10},{6,14},... | collective-permute-start | bytes 393224 | tf_op jit(solution)/shard_map/cells_2_chunk_3/ppermute | solution.py:286
  56.8 2.4 %collective-permute-start.13 = (bf16[256,256]{1,0:T(8,128)(2,1)S(1)}, bf16[256,256]{1,0:T(8,128)(2,1)S(1)}, u32[]{:S(2)}, u32[]{:S(2)}) collective-permute-start(bf16[256,256]{1,0:T(8,128)(2,1)S(1)} %get-tuple-element.81), channel_id=1, source_target_pairs={{0,12},{4,8},{8,4},{12,0},{1,13},{5,9},{9,5},{13,1},{2,14},{6,10},... | collective-permute-start | bytes 393224 | tf_op jit(solution)/shard_map/cells_3_chunk_3/ppermute | solution.py:286
  59.2 1.8 %standardize.6 = (bf16[1024,256]{1,0:T(8,128)(2,1)S(1)}, bf16[1024,1024]{1,0:T(8,128)(2,1)S(1)}, f32[8,128]{1,0:T(8,128)}, bf16[4096,256]{1,0:T(8,128)(2,1)S(1)}) custom-call(f32[1,256]{1,0:T(1,128)S(1)} %get-tuple-element.95.mean_ref, bf16[256,256]{1,0:T(8,128)(2,1)S(1)} %copy-done.8, ...), custom_call_target="tpu_custom_call", output_to_operand_aliasing={{1}: (9, {}), {3}: (10, {})} | custom-call | flops 20000000000 | bytes 1024 | tf_op jit(solution)/shard_map/standardize/pallas_call | solution.py:158
  60.9 1.6 %collective-permute-start.14 = (bf16[1024,256]{1,0:T(8,128)(2,1)S(1)}, bf16[1024,256]{1,0:T(8,128)(2,1)S(1)}, u32[]{:S(2)}, u32[]{:S(2)}) collective-permute-start(bf16[1024,256]{1,0:T(8,128)(2,1)S(1)} %get-tuple-element.88), channel_id=1, source_target_pairs={{0,2},{1,3},{2,0},{3,1},{4,6},{5,7},{6,4},{7,5},{8,10},{9,11},{10,... | collective-permute-start | bytes 1572872 | tf_op jit(solution)/shard_map/far_2/ppermute | solution.py:289
  62.5 1.1 %collective-permute-done.13.refs_3_ = bf16[256,256]{1,0:T(8,128)(2,1)S(1)} collective-permute-done((bf16[256,256]{1,0:T(8,128)(2,1)S(1)}, bf16[256,256]{1,0:T(8,128)(2,1)S(1)}, u32[]{:S(2)}, u32[]{:S(2)}) %collective-permute-start.13) | collective-permute-done | bytes 131104 | tf_op jit(solution)/shard_map/cells_3_chunk_3/ppermute | solution.py:286
  63.6 1.2 %standardize.7 = (bf16[1024,256]{1,0:T(8,128)(2,1)S(1)}, bf16[1024,1024]{1,0:T(8,128)(2,1)S(1)}, f32[8,128]{1,0:T(8,128)S(1)}, bf16[4096,256]{1,0:T(8,128)(2,1)S(1)}) custom-call(f32[1,256]{1,0:T(1,128)S(1)} %get-tuple-element.98.mean_ref, bf16[256,256]{1,0:T(8,128)(2,1)S(1)} %get-tuple-element.65.refs_0_, ...), custom_call_target="tpu_custom_call", output_to_operand_aliasing={{1}: (9, {}), {3}: (10, {})} | custom-call | flops 20000000000 | bytes 1024 | tf_op jit(solution)/shard_map/standardize/pallas_call | solution.py:158
  64.8 0.1 collective-permute-start.15
  64.9 0.1 and_select_fusion.place_ref
  65.0 0.1 and_select_fusion.1.place_ref
  65.1 1.5 %collective-permute-start.19 = (bf16[1024,256]{1,0:T(8,128)(2,1)S(1)}, bf16[1024,256]{1,0:T(8,128)(2,1)S(1)}, u32[]{:S(2)}, u32[]{:S(2)}) collective-permute-start(bf16[1024,256]{1,0:T(8,128)(2,1)S(1)} %get-tuple-element.93), channel_id=1, source_target_pairs={{0,2},{1,3},{2,0},{3,1},{4,6},{5,7},{6,4},{7,5},{8,10},{9,11},{10,... | collective-permute-start | bytes 1572872 | tf_op jit(solution)/shard_map/far_3/ppermute | solution.py:289
  66.6 5.5 %collective-permute-done.14.refs_3_ = bf16[1024,256]{1,0:T(8,128)(2,1)S(1)} collective-permute-done((bf16[1024,256]{1,0:T(8,128)(2,1)S(1)}, bf16[1024,256]{1,0:T(8,128)(2,1)S(1)}, u32[]{:S(2)}, u32[]{:S(2)}) %collective-permute-start.14) | collective-permute-done | bytes 524320 | tf_op jit(solution)/shard_map/far_2/ppermute | solution.py:289
  72.2 0.5 collective-permute-start.17
  72.7 4.4 %gram.6.refs_6_ = bf16[1,1024,4096]{2,1,0:T(8,128)(2,1)} custom-call(s32[2]{0:T(128)S(1)} %and_select_fusion.place_ref, f32[8,128]{1,0:T(8,128)S(1)} %get-tuple-element.86.count_ref, bf16[1024,1024]{1,0:T(8,128)(2,1)S(1)} %get-tuple-element.87.left_ref, bf16[4096,256]{1,0:T(8,128)(2,1)S(1)} %get-tuple-element.89.refs_0_, ...), custom_call_target="tpu_custom_call", output_to_operand_aliasing={{}: (4, {})} | custom-call | flops 20000000000 | bytes 1024 | tf_op jit(solution)/shard_map/gram/pallas_call | solution.py:246
  77.1 10.5 %gram.7.refs_1_ = bf16[1,1024,4096]{2,1,0:T(8,128)(2,1)} custom-call(s32[4]{0:T(128)S(1)} %and_select_fusion.1.place_ref, f32[8,128]{1,0:T(8,128)S(1)} %get-tuple-element.86.count_ref, bf16[1024,1024]{1,0:T(8,128)(2,1)S(1)} %get-tuple-element.87.left_ref, bf16[4096,256]{1,0:T(8,128)(2,1)S(1)} %collective-permute-done.15.refs_0_, ...), custom_call_target="tpu_custom_call", output_to_operand_aliasing={{}: (9, {})} | custom-call | flops 1024 | bytes 1024 | tf_op jit(solution)/shard_map/gram/pallas_call | solution.py:246
  87.7 0.1 collective-permute-start.18
  87.8 0.5 collective-permute-start.20
  88.3 2.7 %gram.8.refs_2_ = bf16[1,1024,4096]{2,1,0:T(8,128)(2,1)} custom-call(s32[1]{0:T(128)S(6)} %select_n.33.place_ref, f32[8,128]{1,0:T(8,128)S(1)} %get-tuple-element.86.count_ref, bf16[1024,1024]{1,0:T(8,128)(2,1)S(1)} %get-tuple-element.87.left_ref, bf16[1024,256]{1,0:T(8,128)(2,1)S(1)} %collective-permute-done.19.refs_0_, ...), custom_call_target="tpu_custom_call", output_to_operand_aliasing={{}: (4, {})} | custom-call | flops 1024 | bytes 1024 | tf_op jit(solution)/shard_map/gram/pallas_call | solution.py:246
  91.0 4.0 %gram.9 = bf16[1,1024,4096]{2,1,0:T(8,128)(2,1)} custom-call(s32[1]{0:T(128)S(6)} %select_n.29.place_ref, f32[8,128]{1,0:T(8,128)S(1)} %get-tuple-element.86.count_ref, bf16[1024,1024]{1,0:T(8,128)(2,1)S(1)} %get-tuple-element.87.left_ref, bf16[1024,256]{1,0:T(8,128)(2,1)} %collective-permute-done.18.refs_0_, ...), custom_call_target="tpu_custom_call", output_to_operand_aliasing={{}: (5, {})} | custom-call | flops 1024 | bytes 1024 | tf_op jit(solution)/shard_map/gram/pallas_call | solution.py:246
  (42 shorter events, 0.1 us)
Async XLA Ops:
  0.0 1.2 %copy-start = (bf16[512,1024]{1,0:T(8,128)(2,1)S(1)}, bf16[512,1024]{1,0:T(8,128)(2,1)}, u32[]{:S(2)}) copy-start(bf16[512,1024]{1,0:T(8,128)(2,1)} %expr_ref.1) | copy-start | bytes 3145732
  1.2 0.7 copy-start.1
  1.9 0.7 copy-start.2
  4.8 0.6 copy-start.3
  5.5 0.6 copy-start.5
  6.1 0.6 copy-start.7
  6.7 0.6 copy-start.9
  7.4 0.7 copy-start.11
  8.0 0.7 copy-start.13
  8.7 0.6 copy-start.15
  9.4 8.5 %collective-permute-start = (bf16[272,256]{1,0:T(8,128)(2,1)S(1)}, bf16[272,256]{1,0:T(8,128)(2,1)S(1)}, u32[]{:S(2)}, u32[]{:S(2)}) collective-permute-start(bf16[272,256]{1,0:T(8,128)(2,1)S(1)} %get-tuple-element.53), channel_id=1, source_target_pairs={{0,4},{4,0},{8,12},{12,8},{1,5},{5,1},{9,13},{13,9},{2,6},{6,2},{1... | collective-permute-start | bytes 417800 | tf_op jit(solution)/shard_map/cells_1_chunk_0/ppermute | solution.py:286
  12.4 13.5 %collective-permute-start.2 = (bf16[272,256]{1,0:T(8,128)(2,1)S(1)}, bf16[272,256]{1,0:T(8,128)(2,1)S(1)}, u32[]{:S(2)}, u32[]{:S(2)}) collective-permute-start(bf16[272,256]{1,0:T(8,128)(2,1)S(1)} %get-tuple-element.56), channel_id=1, source_target_pairs={{0,8},{4,12},{8,0},{12,4},{1,9},{5,13},{9,1},{13,5},{2,10},{6,14},... | collective-permute-start | bytes 417800 | tf_op jit(solution)/shard_map/cells_2_chunk_0/ppermute | solution.py:286
  15.0 10.9 %collective-permute-start.4 = (bf16[272,256]{1,0:T(8,128)(2,1)S(1)}, bf16[272,256]{1,0:T(8,128)(2,1)S(1)}, u32[]{:S(2)}, u32[]{:S(2)}) collective-permute-start(bf16[272,256]{1,0:T(8,128)(2,1)S(1)} %get-tuple-element.59), channel_id=1, source_target_pairs={{0,12},{4,8},{8,4},{12,0},{1,13},{5,9},{9,5},{13,1},{2,14},{6,10},... | collective-permute-start | bytes 417800 | tf_op jit(solution)/shard_map/cells_3_chunk_0/ppermute | solution.py:286
  17.8 14.4 %collective-permute-start.1 = (bf16[256,256]{1,0:T(8,128)(2,1)}, bf16[256,256]{1,0:T(8,128)(2,1)S(1)}, u32[]{:S(2)}, u32[]{:S(2)}) collective-permute-start(bf16[256,256]{1,0:T(8,128)(2,1)} %get-tuple-element.54), channel_id=1, source_target_pairs={{0,4},{4,0},{8,12},{12,8},{1,5},{5,1},{9,13},{13,9},{2,6},{6,2},{1... | collective-permute-start | bytes 393224 | tf_op jit(solution)/shard_map/cells_1_chunk_1/ppermute | solution.py:286
  25.9 14.1 %collective-permute-start.3 = (bf16[256,256]{1,0:T(8,128)(2,1)}, bf16[256,256]{1,0:T(8,128)(2,1)S(1)}, u32[]{:S(2)}, u32[]{:S(2)}) collective-permute-start(bf16[256,256]{1,0:T(8,128)(2,1)} %get-tuple-element.57), channel_id=1, source_target_pairs={{0,8},{4,12},{8,0},{12,4},{1,9},{5,13},{9,1},{13,5},{2,10},{6,14},... | collective-permute-start | bytes 393224 | tf_op jit(solution)/shard_map/cells_2_chunk_1/ppermute | solution.py:286
  25.9 14.2 %collective-permute-start.5 = (bf16[256,256]{1,0:T(8,128)(2,1)}, bf16[256,256]{1,0:T(8,128)(2,1)S(1)}, u32[]{:S(2)}, u32[]{:S(2)}) collective-permute-start(bf16[256,256]{1,0:T(8,128)(2,1)} %get-tuple-element.60), channel_id=1, source_target_pairs={{0,12},{4,8},{8,4},{12,0},{1,13},{5,9},{9,5},{13,1},{2,14},{6,10},... | collective-permute-start | bytes 393224 | tf_op jit(solution)/shard_map/cells_3_chunk_1/ppermute | solution.py:286
  28.7 3.5 %copy-start.14 = (bf16[256,256]{1,0:T(8,128)(2,1)S(1)}, bf16[256,256]{1,0:T(8,128)(2,1)}, u32[]{:S(2)}) copy-start(bf16[256,256]{1,0:T(8,128)(2,1)} %copy-done.13) | copy-start | bytes 393220
  28.7 11.3 %copy-start.10 = (bf16[256,256]{1,0:T(8,128)(2,1)S(1)}, bf16[256,256]{1,0:T(8,128)(2,1)}, u32[]{:S(2)}) copy-start(bf16[256,256]{1,0:T(8,128)(2,1)} %copy-done.9) | copy-start | bytes 393220
  28.7 11.4 %copy-start.12 = (bf16[256,256]{1,0:T(8,128)(2,1)S(1)}, bf16[256,256]{1,0:T(8,128)(2,1)}, u32[]{:S(2)}) copy-start(bf16[256,256]{1,0:T(8,128)(2,1)} %copy-done.11) | copy-start | bytes 393220
  28.7 13.7 %copy-start.16 = (bf16[256,256]{1,0:T(8,128)(2,1)S(1)}, bf16[256,256]{1,0:T(8,128)(2,1)}, u32[]{:S(2)}) copy-start(bf16[256,256]{1,0:T(8,128)(2,1)} %copy-done.15) | copy-start | bytes 393220
  30.7 17.8 %collective-permute-start.10 = (bf16[1024,256]{1,0:T(8,128)(2,1)S(1)}, bf16[1024,256]{1,0:T(8,128)(2,1)S(1)}, u32[]{:S(2)}, u32[]{:S(2)}) collective-permute-start(bf16[1024,256]{1,0:T(8,128)(2,1)S(1)} %get-tuple-element.76), channel_id=1, source_target_pairs={{0,2},{1,3},{2,0},{3,1},{4,6},{5,7},{6,4},{7,5},{8,10},{9,11},{10,... | collective-permute-start | bytes 1572872 | tf_op jit(solution)/shard_map/far_0/ppermute | solution.py:289
  32.3 14.1 %collective-permute-start.7 = (bf16[256,256]{1,0:T(8,128)(2,1)S(1)}, bf16[256,256]{1,0:T(8,128)(2,1)S(1)}, u32[]{:S(2)}, u32[]{:S(2)}) collective-permute-start(bf16[256,256]{1,0:T(8,128)(2,1)S(1)} %copy-done.14), channel_id=1, source_target_pairs={{0,4},{4,0},{8,12},{12,8},{1,5},{5,1},{9,13},{13,9},{2,6},{6,2},{1... | collective-permute-start | bytes 393224 | tf_op jit(solution)/shard_map/cells_1_chunk_2/ppermute | solution.py:286
  40.0 11.9 %collective-permute-start.9 = (bf16[256,256]{1,0:T(8,128)(2,1)S(1)}, bf16[256,256]{1,0:T(8,128)(2,1)S(1)}, u32[]{:S(2)}, u32[]{:S(2)}) collective-permute-start(bf16[256,256]{1,0:T(8,128)(2,1)S(1)} %copy-done.10), channel_id=1, source_target_pairs={{0,8},{4,12},{8,0},{12,4},{1,9},{5,13},{9,1},{13,5},{2,10},{6,14},... | collective-permute-start | bytes 393224 | tf_op jit(solution)/shard_map/cells_2_chunk_2/ppermute | solution.py:286
  40.1 11.8 %collective-permute-start.12 = (bf16[256,256]{1,0:T(8,128)(2,1)S(1)}, bf16[256,256]{1,0:T(8,128)(2,1)S(1)}, u32[]{:S(2)}, u32[]{:S(2)}) collective-permute-start(bf16[256,256]{1,0:T(8,128)(2,1)S(1)} %copy-done.12), channel_id=1, source_target_pairs={{0,12},{4,8},{8,4},{12,0},{1,13},{5,9},{9,5},{13,1},{2,14},{6,10},... | collective-permute-start | bytes 393224 | tf_op jit(solution)/shard_map/cells_3_chunk_2/ppermute | solution.py:286
  42.4 3.9 %copy-start.6 = (bf16[256,256]{1,0:T(8,128)(2,1)S(1)}, bf16[256,256]{1,0:T(8,128)(2,1)}, u32[]{:S(2)}) copy-start(bf16[256,256]{1,0:T(8,128)(2,1)} %copy-done.5) | copy-start | bytes 393220
  43.6 18.9 %collective-permute-start.6 = (bf16[1024,256]{1,0:T(8,128)(2,1)S(1)}, bf16[1024,256]{1,0:T(8,128)(2,1)S(1)}, u32[]{:S(2)}, u32[]{:S(2)}) collective-permute-start(bf16[1024,256]{1,0:T(8,128)(2,1)S(1)} %get-tuple-element.64), channel_id=1, source_target_pairs={{0,2},{1,3},{2,0},{3,1},{4,6},{5,7},{6,4},{7,5},{8,10},{9,11},{10,... | collective-permute-start | bytes 1572872 | tf_op jit(solution)/shard_map/far_1/ppermute | solution.py:289
  46.3 16.2 %collective-permute-start.8 = (bf16[256,256]{1,0:T(8,128)(2,1)S(1)}, bf16[256,256]{1,0:T(8,128)(2,1)S(1)}, u32[]{:S(2)}, u32[]{:S(2)}) collective-permute-start(bf16[256,256]{1,0:T(8,128)(2,1)S(1)} %copy-done.6), channel_id=1, source_target_pairs={{0,4},{4,0},{8,12},{12,8},{1,5},{5,1},{9,13},{13,9},{2,6},{6,2},{1... | collective-permute-start | bytes 393224 | tf_op jit(solution)/shard_map/cells_1_chunk_3/ppermute | solution.py:286
  48.5 3.4 %copy-start.4 = (bf16[256,256]{1,0:T(8,128)(2,1)S(1)}, bf16[256,256]{1,0:T(8,128)(2,1)}, u32[]{:S(2)}) copy-start(bf16[256,256]{1,0:T(8,128)(2,1)} %copy-done.3) | copy-start | bytes 393220
  48.5 10.7 %copy-start.8 = (bf16[256,256]{1,0:T(8,128)(2,1)S(1)}, bf16[256,256]{1,0:T(8,128)(2,1)}, u32[]{:S(2)}) copy-start(bf16[256,256]{1,0:T(8,128)(2,1)} %copy-done.7) | copy-start | bytes 393220
  51.9 10.6 %collective-permute-start.11 = (bf16[256,256]{1,0:T(8,128)(2,1)S(1)}, bf16[256,256]{1,0:T(8,128)(2,1)S(1)}, u32[]{:S(2)}, u32[]{:S(2)}) collective-permute-start(bf16[256,256]{1,0:T(8,128)(2,1)S(1)} %copy-done.4), channel_id=1, source_target_pairs={{0,8},{4,12},{8,0},{12,4},{1,9},{5,13},{9,1},{13,5},{2,10},{6,14},... | collective-permute-start | bytes 393224 | tf_op jit(solution)/shard_map/cells_2_chunk_3/ppermute | solution.py:286
  56.8 6.8 %collective-permute-start.13 = (bf16[256,256]{1,0:T(8,128)(2,1)S(1)}, bf16[256,256]{1,0:T(8,128)(2,1)S(1)}, u32[]{:S(2)}, u32[]{:S(2)}) collective-permute-start(bf16[256,256]{1,0:T(8,128)(2,1)S(1)} %get-tuple-element.81), channel_id=1, source_target_pairs={{0,12},{4,8},{8,4},{12,0},{1,13},{5,9},{9,5},{13,1},{2,14},{6,10},... | collective-permute-start | bytes 393224 | tf_op jit(solution)/shard_map/cells_3_chunk_3/ppermute | solution.py:286
  60.9 11.2 %collective-permute-start.14 = (bf16[1024,256]{1,0:T(8,128)(2,1)S(1)}, bf16[1024,256]{1,0:T(8,128)(2,1)S(1)}, u32[]{:S(2)}, u32[]{:S(2)}) collective-permute-start(bf16[1024,256]{1,0:T(8,128)(2,1)S(1)} %get-tuple-element.88), channel_id=1, source_target_pairs={{0,2},{1,3},{2,0},{3,1},{4,6},{5,7},{6,4},{7,5},{8,10},{9,11},{10,... | collective-permute-start | bytes 1572872 | tf_op jit(solution)/shard_map/far_2/ppermute | solution.py:289
  64.8 12.3 %collective-permute-start.15 = (bf16[4096,256]{1,0:T(8,128)(2,1)S(1)}, bf16[4096,256]{1,0:T(8,128)(2,1)S(1)}, u32[]{:S(2)}, u32[]{:S(2)}) collective-permute-start(bf16[4096,256]{1,0:T(8,128)(2,1)S(1)} %get-tuple-element.89.refs_0_), channel_id=1, source_target_pairs={{0,1},{1,0},{2,3},{3,2},{4,5},{5,4},{6,7},{7,6},{8,9},{9,8},{10,11... | collective-permute-start | bytes 6291464 | tf_op jit(solution)/shard_map/near/ppermute | solution.py:293
  65.1 22.6 %collective-permute-start.19 = (bf16[1024,256]{1,0:T(8,128)(2,1)S(1)}, bf16[1024,256]{1,0:T(8,128)(2,1)S(1)}, u32[]{:S(2)}, u32[]{:S(2)}) collective-permute-start(bf16[1024,256]{1,0:T(8,128)(2,1)S(1)} %get-tuple-element.93), channel_id=1, source_target_pairs={{0,2},{1,3},{2,0},{3,1},{4,6},{5,7},{6,4},{7,5},{8,10},{9,11},{10,... | collective-permute-start | bytes 1572872 | tf_op jit(solution)/shard_map/far_3/ppermute | solution.py:289
  72.1 5.0 %collective-permute-start.16 = (bf16[1024,256]{1,0:T(8,128)(2,1)S(1)}, bf16[1024,256]{1,0:T(8,128)(2,1)S(1)}, u32[]{:S(2)}, u32[]{:S(2)}) collective-permute-start(bf16[1024,256]{1,0:T(8,128)(2,1)S(1)} %collective-permute-done.10.refs_1_), channel_id=1, source_target_pairs={{0,1},{1,0},{2,3},{3,2},{4,5},{5,4},{6,7},{7,6},{8,9},{9,8},{10,11... | collective-permute-start | bytes 1572872 | tf_op jit(solution)/shard_map/far_near_0/ppermute | solution.py:293
  72.2 5.0 %collective-permute-start.17 = (bf16[1024,256]{1,0:T(8,128)(2,1)S(1)}, bf16[1024,256]{1,0:T(8,128)(2,1)S(1)}, u32[]{:S(2)}, u32[]{:S(2)}) collective-permute-start(bf16[1024,256]{1,0:T(8,128)(2,1)S(1)} %collective-permute-done.6.refs_2_), channel_id=1, source_target_pairs={{0,1},{1,0},{2,3},{3,2},{4,5},{5,4},{6,7},{7,6},{8,9},{9,8},{10,11... | collective-permute-start | bytes 1572872 | tf_op jit(solution)/shard_map/far_near_1/ppermute | solution.py:293
  87.7 3.3 %collective-permute-start.18 = (bf16[1024,256]{1,0:T(8,128)(2,1)S(1)}, bf16[1024,256]{1,0:T(8,128)(2,1)}, u32[]{:S(2)}, u32[]{:S(2)}) collective-permute-start(bf16[1024,256]{1,0:T(8,128)(2,1)S(1)} %collective-permute-done.14.refs_3_), channel_id=1, source_target_pairs={{0,1},{1,0},{2,3},{3,2},{4,5},{5,4},{6,7},{7,6},{8,9},{9,8},{10,11... | collective-permute-start | bytes 1572872 | tf_op jit(solution)/shard_map/far_near_2/ppermute | solution.py:293
  87.8 3.2 %collective-permute-start.20 = (bf16[1024,256]{1,0:T(8,128)(2,1)S(1)}, bf16[1024,256]{1,0:T(8,128)(2,1)}, u32[]{:S(2)}, u32[]{:S(2)}) collective-permute-start(bf16[1024,256]{1,0:T(8,128)(2,1)S(1)} %collective-permute-done.19.refs_0_), channel_id=1, source_target_pairs={{0,1},{1,0},{2,3},{3,2},{4,5},{5,4},{6,7},{7,6},{8,9},{9,8},{10,11... | collective-permute-start | bytes 1572872 | tf_op jit(solution)/shard_map/far_near_3/ppermute | solution.py:293

commit v6 on v3

v6 whole, which is shorter than its diff:
```python
import functools

import jax
import jax.numpy as jnp
from jax import lax
from jax.experimental import pallas as pl
from jax.experimental.pallas import tpu as pltpu
from jax.sharding import PartitionSpec as P

dispersion = 100.0
epsilon = 1e-05
TILE = 16
VMEM = 16 * 1024 * 1024

brief = pl.CostEstimate(flops=1024, bytes_accessed=1024, transcendentals=0)
lengthy = pl.CostEstimate(flops=2 * 10**10, bytes_accessed=1024, transcendentals=0)
whole = pl.BlockSpec(memory_space=pltpu.VMEM)
anywhere = pl.BlockSpec(memory_space=pl.ANY)


def pack_kernel(types, cap, widths, type_ref, factor_ref, expr_ref, *outs):
    rows = expr_ref.shape[0]
    home = lax.axis_index("cells")
    kind = type_ref[...].reshape(1, rows)
    rel = jnp.bitwise_xor(kind, home)
    lines = max(types, 8)
    hot = lax.broadcasted_iota(jnp.int32, (lines, rows), 0) == rel
    hot_f = jnp.where(hot, 1.0, 0.0)
    upper = jnp.where(
        lax.broadcasted_iota(jnp.int32, (rows, rows), 0)
        <= lax.broadcasted_iota(jnp.int32, (rows, rows), 1),
        1.0,
        0.0,
    ).astype(jnp.bfloat16)
    running = jnp.dot(hot_f.astype(jnp.bfloat16), upper, preferred_element_type=jnp.float32)
    rank = jnp.sum(hot_f * running, axis=0, keepdims=True) - 1.0
    slot = rel * cap + rank.astype(jnp.int32)
    factor = factor_ref[...].astype(jnp.float32).reshape(1, rows)
    factor = jnp.broadcast_to(factor, (TILE, rows)).astype(jnp.bfloat16)
    values = expr_ref[...]
    for j in range(types):
        place = jnp.where(
            lax.broadcasted_iota(jnp.int32, (cap, rows), 0) + j * cap == slot, 1.0, 0.0
        ).astype(jnp.bfloat16)
        block = jnp.dot(place, values, preferred_element_type=jnp.float32).astype(jnp.bfloat16)
        start = 0
        for k, width in enumerate(widths):
            outs[k * types + j][0:cap, :] = block[:, start : start + width]
            start += width
        line = lax.dot_general(
            factor, place, (((1,), (1,)), ((), ())), preferred_element_type=jnp.float32
        )
        row = lax.broadcasted_iota(jnp.int32, (TILE, 1), 0)
        width = widths[0]
        tail = jnp.zeros((TILE, min(width, cap)), jnp.float32)
        for i in range(pl.cdiv(cap, width)):
            tail = jnp.where(row == i, line[:, i * width : min((i + 1) * width, cap)], tail)
        outs[j][cap : cap + TILE, 0 : min(width, cap)] = tail.astype(jnp.bfloat16)


def pack(types, cap, widths, cell_type, size_factor, expression):
    rows = expression.shape[0]
    shapes = [
        jax.ShapeDtypeStruct((cap + (TILE if k == 0 else 0), width), jnp.bfloat16)
        for k, width in enumerate(widths)
        for _ in range(types)
    ]
    flat = pl.pallas_call(
        functools.partial(pack_kernel, types, cap, widths),
        out_shape=shapes,
        in_specs=[whole] * 3,
        out_specs=[whole] * len(shapes),
        compiler_params=pltpu.CompilerParams(vmem_limit_bytes=VMEM),
        cost_estimate=brief,
        name="pack",
    )(cell_type, size_factor, expression)
    return [flat[k * types : (k + 1) * types] for k in range(len(widths))]


def standardize_kernel(types, cap, lead, separate, chunk, mean_ref, *refs):
    blocks = refs[:types]
    tails = refs[types : 2 * types] if separate else blocks
    base = 0 if separate else cap
    refs = refs[2 * types :] if separate else refs[types:]
    scaled_ref, turned_ref, count_ref, all_ref, work, turned, sems = refs[-7:]
    width = work.shape[1]
    mean = mean_ref[:, chunk * width : (chunk + 1) * width]
    piece = min(lead, cap)
    total = jnp.zeros((1, width), jnp.float32)
    count = jnp.zeros((1, 1), jnp.float32)
    alive = []
    for j in range(types):
        column = jnp.zeros((cap, 1), jnp.float32)
        for i in range(pl.cdiv(cap, lead)):
            line = tails[j][base : base + TILE, 0:piece].astype(jnp.float32)[i : i + 1, :]
            diagonal = (
                lax.broadcasted_iota(jnp.int32, (cap, piece), 0)
                == lax.broadcasted_iota(jnp.int32, (cap, piece), 1) + i * lead
            )
            column += jnp.sum(jnp.where(diagonal, line, 0.0), axis=1, keepdims=True)
        live = column > 0.0
        alive.append(live)
        count += jnp.sum(jnp.where(live, 1.0, 0.0), axis=0, keepdims=True)
        expected = jnp.where(live, column * mean, 1.0)
        values = blocks[j][0:cap, :].astype(jnp.float32)
        residual = jnp.where(
            live,
            (values - expected) * lax.rsqrt(expected + expected * expected * (1.0 / dispersion)),
            0.0,
        )
        work[j * cap : (j + 1) * cap, :] = residual
        total += jnp.sum(residual, axis=0, keepdims=True)
    center = total / count
    square = jnp.zeros((1, width), jnp.float32)
    for j in range(types):
        centered = jnp.where(alive[j], work[j * cap : (j + 1) * cap, :] - center, 0.0)
        work[j * cap : (j + 1) * cap, :] = centered
        square += jnp.sum(centered * centered, axis=0, keepdims=True)
    scale = lax.rsqrt(square / count + epsilon)
    for j in range(types):
        scaled = work[j * cap : (j + 1) * cap, :] * scale
        scaled_ref[j * cap : (j + 1) * cap, :] = scaled.astype(jnp.bfloat16)
        work[j * cap : (j + 1) * cap, :] = scaled
    slots = types * cap
    rows = pl.ds(chunk * slots, slots)
    copies = [pltpu.make_async_copy(scaled_ref, all_ref.at[rows, :], sems.at[0])]
    copies[0].start()
    turned[...] = jnp.transpose(work[...]).astype(jnp.bfloat16)
    rows = pl.ds(chunk * width, width)
    copies.append(pltpu.make_async_copy(turned, turned_ref.at[rows, :], sems.at[1]))
    copies[-1].start()
    for copy in copies:
        copy.wait()
    count_ref[...] = jnp.broadcast_to(count, count_ref.shape)


def standardize(types, cap, lead, width, mean, chunk, blocks, first, left, own):
    chunks = mean.shape[1] // width
    separate = first is not blocks
    slots = types * cap
    specs = [whole] * (1 + types)
    args = [mean, *blocks]
    if separate:
        specs += [pl.BlockSpec((TILE, lead), lambda i: (cap // TILE, 0))] * types
        args += list(first)
    shapes = [
        jax.ShapeDtypeStruct((slots, width), jnp.bfloat16),
        jax.ShapeDtypeStruct((chunks * width, slots), jnp.bfloat16),
        jax.ShapeDtypeStruct((8, 128), jnp.float32),
        jax.ShapeDtypeStruct((chunks * slots, width), jnp.bfloat16),
    ]
    aliases = {}
    for value, output in ((left, 1), (own, 3)):
        if value is not None:
            aliases[len(args)] = output
            specs.append(anywhere)
            args.append(value)
    return pl.pallas_call(
        functools.partial(standardize_kernel, types, cap, lead, separate, chunk),
        grid=(1,),
        out_shape=shapes,
        in_specs=specs,
        out_specs=[whole, anywhere, whole, anywhere],
        scratch_shapes=[
            pltpu.VMEM((slots, width), jnp.float32),
            pltpu.VMEM((width, slots), jnp.bfloat16),
            pltpu.SemaphoreType.DMA((2,)),
        ],
        input_output_aliases=aliases,
        compiler_params=pltpu.CompilerParams(vmem_limit_bytes=VMEM),
        cost_estimate=lengthy,
        name="standardize",
    )(*args)


def gram_kernel(blocks, cores, items, count_ref, left_ref, *refs):
    out_ref, tile, sems = refs[-3:]
    rows, slots = left_ref.shape
    width = tile.shape[2]
    inverse = 1.0 / count_ref[0:1, 0:1]
    me = lax.axis_index("blk")
    stores = []
    for source, index, chip, flip, chunk in items:
        slot = len(stores) % 2
        if len(stores) >= 2:
            stores[-2].wait()
        product = jnp.dot(
            left_ref[...],
            refs[source][index * slots : (index + 1) * slots, :],
            preferred_element_type=jnp.float32,
        )
        tile[slot] = (product * inverse).astype(jnp.bfloat16)
        owner = lax.rem(me + (blocks - chip * cores), blocks)
        owner = jnp.bitwise_xor(owner, flip)
        column = pl.multiple_of(owner * rows + chunk * width, 128)
        stores.append(
            pltpu.make_async_copy(
                tile.at[slot], out_ref.at[0, :, pl.ds(column, width)], sems.at[slot]
            )
        )
        stores[-1].start()
    for store in stores[-2:]:
        store.wait()


def gram(blocks, cores, count, left, panels, before, cost):
    rows, slots = left.shape
    arrays, items = [], []
    for array, index, *owner in panels:
        if not any(array is other for other in arrays):
            arrays.append(array)
        items.append(([array is other for other in arrays].index(True), index, *owner))
    width = arrays[0].shape[1]
    args = [count, left, *arrays]
    specs = [whole] * len(args)
    if before is not None:
        args.append(before)
        specs.append(anywhere)
    return pl.pallas_call(
        functools.partial(gram_kernel, blocks, cores, items),
        in_specs=specs,
        out_specs=anywhere,
        out_shape=jax.ShapeDtypeStruct((1, rows, rows * blocks), jnp.bfloat16),
        scratch_shapes=[
            pltpu.VMEM((2, rows, width), jnp.bfloat16),
            pltpu.SemaphoreType.DMA((2,)),
        ],
        input_output_aliases={} if before is None else {len(args) - 1: 0},
        compiler_params=pltpu.CompilerParams(vmem_limit_bytes=VMEM),
        cost_estimate=cost,
        name="gram",
    )(*args)


def after(value, *others):
    return lax.optimization_barrier((value, *others))[0]


def shards(expression, cell_type, size_factor, gene_mean):
    types = lax.axis_size("cells")
    blocks = lax.axis_size("blk")
    shard_rows, panel = expression.shape
    cap = 2 * shard_rows // types
    assert types & (types - 1) == 0
    width = 256
    widths = [width] * (panel // width)
    chunks = len(widths)
    cores = 2
    chips = blocks // cores
    window = 3

    packed = pack(types, cap, widths, cell_type, size_factor, expression)

    def swap(block, by):
        return lax.ppermute(block, "cells", [(s, s ^ by) for s in range(types)])

    def across(panel_, by):
        return lax.ppermute(panel_, "blk", [(b, (b + by * cores) % blocks) for b in range(blocks)])

    def side(name, panel_, *waits):
        with jax.named_scope(name):
            return lax.ppermute(after(panel_, *waits), "blk", [(b, b ^ 1) for b in range(blocks)])

    mean = gene_mean.reshape(1, panel)
    order = sorted(range(1, types), key=lambda j: (j == 1, j))
    left, own, far, before = None, None, [], None
    for k in range(chunks):
        arrived = [packed[k][0]] + [None] * (types - 1)
        for j in order:
            block = packed[k][j]
            if k:
                block = after(block, before[j])
            with jax.named_scope(f"cells_{j}_chunk_{k}"):
                arrived[j] = swap(block, j)
        before = list(arrived)
        if k >= 2:
            arrived[0] = after(arrived[0], *far[k - 2])
        if k == 0:
            first = arrived
        scaled, left, count, own = standardize(
            types, cap, width, width, mean, k, arrived, first, left, own
        )
        with jax.named_scope(f"far_{k}"):
            far.append([across(scaled, d) for d in range(1, chips)])

    multiply = functools.partial(gram, blocks, cores, count, left)
    last = chunks - 1
    near = side("near", own)
    far_near = [
        [side(f"far_near_{k}", p, own, *far[last - 1]) for p in far[k]] for k in range(last)
    ]
    out = multiply([(own, k, 0, 0, k) for k in range(chunks)], None, lengthy)
    panels = [(near, k, 0, 1, k) for k in range(chunks)]
    for flip, group in ((0, far), (1, far_near)):
        panels += [(p, 0, d, flip, k) for k in range(last) for d, p in enumerate(group[k], 1)]
    out = multiply(panels, out, brief)
    far_near = [side(f"far_near_{last}", p, out) for p in far[last]]
    out = multiply([(p, 0, d, 0, last) for d, p in enumerate(far[last], 1)], out, brief)
    return multiply([(p, 0, d, 1, last) for d, p in enumerate(far_near, 1)], out, brief)


def solution(mesh):
    placed = (
        P(("parts", "cells"), "blk"),
        P(("parts", "cells")),
        P(("parts", "cells")),
        P(("parts", "blk")),
    )
    return jax.shard_map(
        shards,
        mesh=mesh,
        in_specs=placed,
        out_specs=P(("parts", "cells"), "blk", None),
        check_vma=False,
    )
```

time: 97 us -> 88.7 us (0.914)
  the two profiles are of different devices: /device:TPU:11 before, /device:TPU:13 now
where the time goes in v6:
time: 88.7 us; the launch traced here: 88.5 us
  starting transfers between devices  40.7 us (46%)
  Pallas kernels  29.4 us (33%)
  waiting for transfers between devices  14.7 us (17%)
  local copies, waits for them, and re-layouts  3.27 us (4%)
    pallas_call x4, Pallas kernels, gram(): pl.pallas_call(functools.partial(gram_kernel, blocks, cores, items), in_s...  21.1 us
    ppermute x12, starting transfers between devices, swap(): return lax.ppermute(block, 'cells', [(s, s ^ by) for s in range(types)])  20.7 us
    ppermute x4, starting transfers between devices, across(): lax.ppermute(panel_, 'blk', [(b, (b + by * cores) % blocks) for b in rang...  11.4 us
    ppermute x12, waiting for transfers between devices, swap(): return lax.ppermute(block, 'cells', [(s, s ^ by) for s in range(types)])  11 us
    ppermute x5, starting transfers between devices, side(): lax.ppermute(after(panel_, *waits), 'blk', [(b, b ^ 1) for b in range(blo...  8.64 us
    pallas_call x4, Pallas kernels, standardize(): pl.pallas_call(functools.partial(standardize_kernel, types, cap, lead, se...  6.63 us
    ppermute x4, waiting for transfers between devices, across(): lax.ppermute(panel_, 'blk', [(b, (b + by * cores) % blocks) for b in rang...  3.4 us
    unnamed x8, local copies, waits for them, and re-layouts  3.27 us
  transfers between devices with their start and end apart: 21, of which 8 were waited for; matrix products, arithmetic and copies ran while one was open for 0% of the time, Pallas kernels for 30%

profile of v6, /device:TPU:13, one launch (start us, length us, event | category | flops | bytes accessed | tf_op | source)
XLA Modules:
  0.0 88.5 jit_solution(4560586551140329991)
XLA Ops:
  0.0 1.2 %copy-done = bf16[512,1024]{1,0:T(8,128)(2,1)S(1)} copy-done((bf16[512,1024]{1,0:T(8,128)(2,1)S(1)}, bf16[512,1024]{1,0:T(8,128)(2,1)}, u32[]{:S(2)}) %copy-start) | copy-done | bytes 1048600
  1.2 0.7 copy-done.1
  1.9 0.7 copy-done.2
  2.6 1.7 %pack.1 = (bf16[272,256]{1,0:T(8,128)(2,1)S(1)}, bf16[272,256]{1,0:T(8,128)(2,1)S(1)}, bf16[272,256]{1,0:T(8,128)(2,1)S(1)}, bf16[272,256]{1,0:T(8,128)(2,1)S(1)...) custom-call(s32[512]{0:T(512)S(1)} %copy-done.1, ...), custom_call_target="tpu_custom_call" | custom-call | flops 1024 | bytes 1024 | tf_op jit(solution)/shard_map/pack/pallas_call | solution.py:68
  4.3 0.2 collective-permute-start
  4.5 2.3 %collective-permute-start.2 = (bf16[272,256]{1,0:T(8,128)(2,1)S(1)}, bf16[272,256]{1,0:T(8,128)(2,1)S(1)}, u32[]{:S(2)}, u32[]{:S(2)}) collective-permute-start(bf16[272,256]{1,0:T(8,128)(2,1)S(1)} %get-tuple-element.55), channel_id=1, source_target_pairs={{0,8},{4,12},{8,0},{12,4},{1,9},{5,13},{9,1},{13,5},{2,10},{6,14},... | collective-permute-start | bytes 417800 | tf_op jit(solution)/shard_map/cells_2_chunk_0/ppermute | solution.py:255
  6.8 0.2 collective-permute-start.4
  7.0 1.9 %collective-permute-done.refs_1_.refs_5_ = bf16[272,256]{1,0:T(8,128)(2,1)S(1)} collective-permute-done((bf16[272,256]{1,0:T(8,128)(2,1)S(1)}, bf16[272,256]{1,0:T(8,128)(2,1)S(1)}, u32[]{:S(2)}, u32[]{:S(2)}) %collective-permute-start) | collective-permute-done | bytes 139296 | tf_op jit(solution)/shard_map/cells_1_chunk_0/ppermute | solution.py:255
  8.9 0.2 collective-permute-start.1
  9.1 3.8 %collective-permute-done.2.refs_2_.refs_6_ = bf16[272,256]{1,0:T(8,128)(2,1)S(1)} collective-permute-done((bf16[272,256]{1,0:T(8,128)(2,1)S(1)}, bf16[272,256]{1,0:T(8,128)(2,1)S(1)}, u32[]{:S(2)}, u32[]{:S(2)}) %collective-permute-start.2) | collective-permute-done | bytes 139296 | tf_op jit(solution)/shard_map/cells_2_chunk_0/ppermute | solution.py:255
  12.9 4.7 %collective-permute-start.3 = (bf16[256,256]{1,0:T(8,128)(2,1)S(1)}, bf16[256,256]{1,0:T(8,128)(2,1)S(1)}, u32[]{:S(2)}, u32[]{:S(2)}) collective-permute-start(bf16[256,256]{1,0:T(8,128)(2,1)S(1)} %get-tuple-element.56), channel_id=1, source_target_pairs={{0,8},{4,12},{8,0},{12,4},{1,9},{5,13},{9,1},{13,5},{2,10},{6,14},... | collective-permute-start | bytes 393224 | tf_op jit(solution)/shard_map/cells_2_chunk_1/ppermute | solution.py:255
  17.6 1.2 %collective-permute-done.4.refs_3_.refs_7_ = bf16[272,256]{1,0:T(8,128)(2,1)S(1)} collective-permute-done((bf16[272,256]{1,0:T(8,128)(2,1)S(1)}, bf16[272,256]{1,0:T(8,128)(2,1)S(1)}, u32[]{:S(2)}, u32[]{:S(2)}) %collective-permute-start.4) | collective-permute-done | bytes 139296 | tf_op jit(solution)/shard_map/cells_3_chunk_0/ppermute | solution.py:255
  18.8 5.8 %collective-permute-start.5 = (bf16[256,256]{1,0:T(8,128)(2,1)S(1)}, bf16[256,256]{1,0:T(8,128)(2,1)S(1)}, u32[]{:S(2)}, u32[]{:S(2)}) collective-permute-start(bf16[256,256]{1,0:T(8,128)(2,1)S(1)} %get-tuple-element.59), channel_id=1, source_target_pairs={{0,12},{4,8},{8,4},{12,0},{1,13},{5,9},{9,5},{13,1},{2,14},{6,10},... | collective-permute-start | bytes 393224 | tf_op jit(solution)/shard_map/cells_3_chunk_1/ppermute | solution.py:255
  24.6 0.7 copy-done.3
  25.2 1.8 %standardize.4 = (bf16[1024,256]{1,0:T(8,128)(2,1)S(1)}, bf16[1024,1024]{1,0:T(8,128)(2,1)S(1)}, f32[8,128]{1,0:T(8,128)}, bf16[4096,256]{1,0:T(8,128)(2,1)S(1)}) custom-call(f32[1,1024]{1,0:T(1,128)S(1)} %bitcast.1, bf16[272,256]{1,0:T(8,128)(2,1)S(1)} %get-tuple-element.60.refs_0_.refs_4_, bf16[272,256]{1,0:T(8,128)(2,1)S(1)} %collective-permute-done.refs_1_.refs_5_, ...), custom_call_target="tpu_custom_call" | custom-call | flops 20000000000 | bytes 1024 | tf_op jit(solution)/shard_map/standardize/pallas_call | solution.py:158
  27.0 1.3 %collective-permute-start.13 = (bf16[1024,256]{1,0:T(8,128)(2,1)S(1)}, bf16[1024,256]{1,0:T(8,128)(2,1)S(1)}, u32[]{:S(2)}, u32[]{:S(2)}) collective-permute-start(bf16[1024,256]{1,0:T(8,128)(2,1)S(1)} %get-tuple-element.78), channel_id=1, source_target_pairs={{0,2},{1,3},{2,0},{3,1},{4,6},{5,7},{6,4},{7,5},{8,10},{9,11},{10,... | collective-permute-start | bytes 1572872 | tf_op jit(solution)/shard_map/far_0/ppermute | solution.py:258
  28.3 1.4 %collective-permute-start.9 = (bf16[256,256]{1,0:T(8,128)(2,1)S(1)}, bf16[256,256]{1,0:T(8,128)(2,1)S(1)}, u32[]{:S(2)}, u32[]{:S(2)}) collective-permute-start(bf16[256,256]{1,0:T(8,128)(2,1)S(1)} %get-tuple-element.71), channel_id=1, source_target_pairs={{0,8},{4,12},{8,0},{12,4},{1,9},{5,13},{9,1},{13,5},{2,10},{6,14},... | collective-permute-start | bytes 393224 | tf_op jit(solution)/shard_map/cells_2_chunk_2/ppermute | solution.py:255
  29.7 0.1 collective-permute-done.5.refs_3_
  29.7 1.4 %collective-permute-start.11 = (bf16[256,256]{1,0:T(8,128)(2,1)S(1)}, bf16[256,256]{1,0:T(8,128)(2,1)S(1)}, u32[]{:S(2)}, u32[]{:S(2)}) collective-permute-start(bf16[256,256]{1,0:T(8,128)(2,1)S(1)} %get-tuple-element.75), channel_id=1, source_target_pairs={{0,12},{4,8},{8,4},{12,0},{1,13},{5,9},{9,5},{13,1},{2,14},{6,10},... | collective-permute-start | bytes 393224 | tf_op jit(solution)/shard_map/cells_3_chunk_2/ppermute | solution.py:255
  31.1 1.8 %standardize.5 = (bf16[1024,256]{1,0:T(8,128)(2,1)S(1)}, bf16[1024,1024]{1,0:T(8,128)(2,1)S(1)}, f32[8,128]{1,0:T(8,128)}, bf16[4096,256]{1,0:T(8,128)(2,1)S(1)}) custom-call(f32[1,1024]{1,0:T(1,128)S(1)} %bitcast.2, bf16[256,256]{1,0:T(8,128)(2,1)S(1)} %get-tuple-element.50.refs_0_, ...), custom_call_target="tpu_custom_call", output_to_operand_aliasing={{1}: (9, {}), {3}: (10, {})} | custom-call | flops 20000000000 | bytes 1024 | tf_op jit(solution)/shard_map/standardize/pallas_call | solution.py:158
  32.9 1.3 %collective-permute-start.6 = (bf16[1024,256]{1,0:T(8,128)(2,1)S(1)}, bf16[1024,256]{1,0:T(8,128)(2,1)S(1)}, u32[]{:S(2)}, u32[]{:S(2)}) collective-permute-start(bf16[1024,256]{1,0:T(8,128)(2,1)S(1)} %get-tuple-element.63), channel_id=1, source_target_pairs={{0,2},{1,3},{2,0},{3,1},{4,6},{5,7},{6,4},{7,5},{8,10},{9,11},{10,... | collective-permute-start | bytes 1572872 | tf_op jit(solution)/shard_map/far_1/ppermute | solution.py:258
  34.2 0.0 collective-permute-done.7.refs_1_
  34.2 0.0 collective-permute-start.8
  34.2 1.2 %collective-permute-done.9.refs_2_ = bf16[256,256]{1,0:T(8,128)(2,1)S(1)} collective-permute-done((bf16[256,256]{1,0:T(8,128)(2,1)S(1)}, bf16[256,256]{1,0:T(8,128)(2,1)S(1)}, u32[]{:S(2)}, u32[]{:S(2)}) %collective-permute-start.9) | collective-permute-done | bytes 131104 | tf_op jit(solution)/shard_map/cells_2_chunk_2/ppermute | solution.py:255
  35.4 2.8 %collective-permute-start.10 = (bf16[256,256]{1,0:T(8,128)(2,1)S(1)}, bf16[256,256]{1,0:T(8,128)(2,1)S(1)}, u32[]{:S(2)}, u32[]{:S(2)}) collective-permute-start(bf16[256,256]{1,0:T(8,128)(2,1)S(1)} %get-tuple-element.72), channel_id=1, source_target_pairs={{0,8},{4,12},{8,0},{12,4},{1,9},{5,13},{9,1},{13,5},{2,10},{6,14},... | collective-permute-start | bytes 393224 | tf_op jit(solution)/shard_map/cells_2_chunk_3/ppermute | solution.py:255
  38.3 0.0 collective-permute-done.11.refs_3_
  38.3 1.8 %collective-permute-start.12 = (bf16[256,256]{1,0:T(8,128)(2,1)S(1)}, bf16[256,256]{1,0:T(8,128)(2,1)S(1)}, u32[]{:S(2)}, u32[]{:S(2)}) collective-permute-start(bf16[256,256]{1,0:T(8,128)(2,1)S(1)} %get-tuple-element.76), channel_id=1, source_target_pairs={{0,12},{4,8},{8,4},{12,0},{1,13},{5,9},{9,5},{13,1},{2,14},{6,10},... | collective-permute-start | bytes 393224 | tf_op jit(solution)/shard_map/cells_3_chunk_3/ppermute | solution.py:255
  40.0 1.8 %standardize.6 = (bf16[1024,256]{1,0:T(8,128)(2,1)S(1)}, bf16[1024,1024]{1,0:T(8,128)(2,1)S(1)}, f32[8,128]{1,0:T(8,128)}, bf16[4096,256]{1,0:T(8,128)(2,1)S(1)}) custom-call(f32[1,1024]{1,0:T(1,128)S(1)} %bitcast.3, bf16[256,256]{1,0:T(8,128)(2,1)S(1)} %get-tuple-element.79.refs_0_, ...), custom_call_target="tpu_custom_call", output_to_operand_aliasing={{1}: (9, {}), {3}: (10, {})} | custom-call | flops 20000000000 | bytes 1024 | tf_op jit(solution)/shard_map/standardize/pallas_call | solution.py:158
  41.8 7.6 %collective-permute-start.16 = (bf16[1024,256]{1,0:T(8,128)(2,1)S(1)}, bf16[1024,256]{1,0:T(8,128)(2,1)S(1)}, u32[]{:S(2)}, u32[]{:S(2)}) collective-permute-start(bf16[1024,256]{1,0:T(8,128)(2,1)S(1)} %get-tuple-element.88), channel_id=1, source_target_pairs={{0,2},{1,3},{2,0},{3,1},{4,6},{5,7},{6,4},{7,5},{8,10},{9,11},{10,... | collective-permute-start | bytes 1572872 | tf_op jit(solution)/shard_map/far_2/ppermute | solution.py:258
  49.4 0.0 collective-permute-done.6.refs_2_
  49.4 0.0 collective-permute-done.8.refs_1_
  49.4 0.0 collective-permute-done.10.refs_2_
  49.4 2.8 %collective-permute-done.12.refs_3_ = bf16[256,256]{1,0:T(8,128)(2,1)S(1)} collective-permute-done((bf16[256,256]{1,0:T(8,128)(2,1)S(1)}, bf16[256,256]{1,0:T(8,128)(2,1)S(1)}, u32[]{:S(2)}, u32[]{:S(2)}) %collective-permute-start.12) | collective-permute-done | bytes 131104 | tf_op jit(solution)/shard_map/cells_3_chunk_3/ppermute | solution.py:255
  52.2 1.4 %standardize.7 = (bf16[1024,256]{1,0:T(8,128)(2,1)S(1)}, bf16[1024,1024]{1,0:T(8,128)(2,1)S(1)}, f32[8,128]{1,0:T(8,128)S(1)}, bf16[4096,256]{1,0:T(8,128)(2,1)S(1)}) custom-call(f32[1,1024]{1,0:T(1,128)S(1)} %bitcast.4, bf16[256,256]{1,0:T(8,128)(2,1)S(1)} %get-tuple-element.64.refs_0_, ...), custom_call_target="tpu_custom_call", output_to_operand_aliasing={{1}: (9, {}), {3}: (10, {})} | custom-call | flops 20000000000 | bytes 1024 | tf_op jit(solution)/shard_map/standardize/pallas_call | solution.py:158
  53.5 3.0 %collective-permute-start.15 = (bf16[4096,256]{1,0:T(8,128)(2,1)S(1)}, bf16[4096,256]{1,0:T(8,128)(2,1)S(1)}, u32[]{:S(2)}, u32[]{:S(2)}) collective-permute-start(bf16[4096,256]{1,0:T(8,128)(2,1)S(1)} %get-tuple-element.87.refs_0_), channel_id=1, source_target_pairs={{0,1},{1,0},{2,3},{3,2},{4,5},{5,4},{6,7},{7,6},{8,9},{9,8},{10,11... | collective-permute-start | bytes 6291464 | tf_op jit(solution)/shard_map/near/ppermute | solution.py:262
  56.6 1.2 %collective-permute-start.14 = (bf16[1024,256]{1,0:T(8,128)(2,1)S(1)}, bf16[1024,256]{1,0:T(8,128)(2,1)S(1)}, u32[]{:S(2)}, u32[]{:S(2)}) collective-permute-start(bf16[1024,256]{1,0:T(8,128)(2,1)S(1)} %get-tuple-element.86), channel_id=1, source_target_pairs={{0,2},{1,3},{2,0},{3,1},{4,6},{5,7},{6,4},{7,5},{8,10},{9,11},{10,... | collective-permute-start | bytes 1572872 | tf_op jit(solution)/shard_map/far_3/ppermute | solution.py:258
  57.8 3.4 %collective-permute-done.16.refs_3_ = bf16[1024,256]{1,0:T(8,128)(2,1)S(1)} collective-permute-done((bf16[1024,256]{1,0:T(8,128)(2,1)S(1)}, bf16[1024,256]{1,0:T(8,128)(2,1)S(1)}, u32[]{:S(2)}, u32[]{:S(2)}) %collective-permute-start.16) | collective-permute-done | bytes 524320 | tf_op jit(solution)/shard_map/far_2/ppermute | solution.py:258
  61.2 5.0 %collective-permute-start.17 = (bf16[1024,256]{1,0:T(8,128)(2,1)S(1)}, bf16[1024,256]{1,0:T(8,128)(2,1)S(1)}, u32[]{:S(2)}, u32[]{:S(2)}) collective-permute-start(bf16[1024,256]{1,0:T(8,128)(2,1)S(1)} %collective-permute-done.13.refs_1_), channel_id=1, source_target_pairs={{0,1},{1,0},{2,3},{3,2},{4,5},{5,4},{6,7},{7,6},{8,9},{9,8},{10,11... | collective-permute-start | bytes 1572872 | tf_op jit(solution)/shard_map/far_near_0/ppermute | solution.py:262
  66.2 0.0 collective-permute-start.18
  66.2 0.5 collective-permute-start.19
  66.7 5.3 %gram.4.refs_7_ = bf16[1,1024,4096]{2,1,0:T(8,128)(2,1)} custom-call(f32[8,128]{1,0:T(8,128)S(1)} %get-tuple-element.84.count_ref, bf16[1024,1024]{1,0:T(8,128)(2,1)S(1)} %get-tuple-element.85.left_ref, bf16[4096,256]{1,0:T(8,128)(2,1)S(1)} %get-tuple-element.87.refs_0_), custom_call_target="tpu_custom_call" | custom-call | flops 20000000000 | bytes 1024 | tf_op jit(solution)/shard_map/gram/pallas_call | solution.py:219
  72.0 0.0 collective-permute-done.17.refs_4_
  72.1 0.0 collective-permute-done.19.refs_6_
  72.1 12.7 %gram.5.refs_1_ = bf16[1,1024,4096]{2,1,0:T(8,128)(2,1)} custom-call(f32[8,128]{1,0:T(8,128)S(1)} %get-tuple-element.84.count_ref, bf16[1024,1024]{1,0:T(8,128)(2,1)S(1)} %get-tuple-element.85.left_ref, bf16[4096,256]{1,0:T(8,128)(2,1)S(1)} %collective-permute-done.15.refs_0_, ...), custom_call_target="tpu_custom_call", output_to_operand_aliasing={{}: (9, {})} | custom-call | flops 1024 | bytes 1024 | tf_op jit(solution)/shard_map/gram/pallas_call | solution.py:219
  84.8 0.1 collective-permute-start.20
  84.9 1.5 %gram.6.refs_1_ = bf16[1,1024,4096]{2,1,0:T(8,128)(2,1)} custom-call(f32[8,128]{1,0:T(8,128)S(1)} %get-tuple-element.84.count_ref, bf16[1024,1024]{1,0:T(8,128)(2,1)S(1)} %get-tuple-element.85.left_ref, bf16[1024,256]{1,0:T(8,128)(2,1)S(1)} %collective-permute-done.14.refs_0_, bf16[1,1024,4096]{2,1,0:T(8,128)(2,1)} %gram.5.refs_1_), custom_call_target="tpu_custom_call", output_to_operand_aliasing={{}: (3, {})} | custom-call | flops 1024 | bytes 1024 | tf_op jit(solution)/shard_map/gram/pallas_call | solution.py:219
  86.4 0.4 collective-permute-done.20.refs_0_
  86.8 1.5 %gram.7 = bf16[1,1024,4096]{2,1,0:T(8,128)(2,1)} custom-call(f32[8,128]{1,0:T(8,128)S(1)} %get-tuple-element.84.count_ref, bf16[1024,1024]{1,0:T(8,128)(2,1)S(1)} %get-tuple-element.85.left_ref, bf16[1024,256]{1,0:T(8,128)(2,1)S(1)} %collective-permute-done.20.refs_0_, bf16[1,1024,4096]{2,1,0:T(8,128)(2,1)} %gram.6.refs_1_), custom_call_target="tpu_custom_call", output_to_operand_aliasing={{}: (3, {})} | custom-call | flops 1024 | bytes 1024 | tf_op jit(solution)/shard_map/gram/pallas_call | solution.py:219
  (11 shorter events, 0.0 us)
Async XLA Ops:
  0.0 1.2 %copy-start = (bf16[512,1024]{1,0:T(8,128)(2,1)S(1)}, bf16[512,1024]{1,0:T(8,128)(2,1)}, u32[]{:S(2)}) copy-start(bf16[512,1024]{1,0:T(8,128)(2,1)} %expr_ref.1) | copy-start | bytes 3145732
  1.2 0.7 copy-start.1
  1.9 0.7 copy-start.2
  4.3 4.6 %collective-permute-start = (bf16[272,256]{1,0:T(8,128)(2,1)S(1)}, bf16[272,256]{1,0:T(8,128)(2,1)S(1)}, u32[]{:S(2)}, u32[]{:S(2)}) collective-permute-start(bf16[272,256]{1,0:T(8,128)(2,1)S(1)} %get-tuple-element.52), channel_id=1, source_target_pairs={{0,4},{4,0},{8,12},{12,8},{1,5},{5,1},{9,13},{13,9},{2,6},{6,2},{1... | collective-permute-start | bytes 417800 | tf_op jit(solution)/shard_map/cells_1_chunk_0/ppermute | solution.py:255
  4.5 8.3 %collective-permute-start.2 = (bf16[272,256]{1,0:T(8,128)(2,1)S(1)}, bf16[272,256]{1,0:T(8,128)(2,1)S(1)}, u32[]{:S(2)}, u32[]{:S(2)}) collective-permute-start(bf16[272,256]{1,0:T(8,128)(2,1)S(1)} %get-tuple-element.55), channel_id=1, source_target_pairs={{0,8},{4,12},{8,0},{12,4},{1,9},{5,13},{9,1},{13,5},{2,10},{6,14},... | collective-permute-start | bytes 417800 | tf_op jit(solution)/shard_map/cells_2_chunk_0/ppermute | solution.py:255
  6.8 11.9 %collective-permute-start.4 = (bf16[272,256]{1,0:T(8,128)(2,1)S(1)}, bf16[272,256]{1,0:T(8,128)(2,1)S(1)}, u32[]{:S(2)}, u32[]{:S(2)}) collective-permute-start(bf16[272,256]{1,0:T(8,128)(2,1)S(1)} %get-tuple-element.58), channel_id=1, source_target_pairs={{0,12},{4,8},{8,4},{12,0},{1,13},{5,9},{9,5},{13,1},{2,14},{6,10},... | collective-permute-start | bytes 417800 | tf_op jit(solution)/shard_map/cells_3_chunk_0/ppermute | solution.py:255
  8.9 19.4 %collective-permute-start.1 = (bf16[256,256]{1,0:T(8,128)(2,1)S(1)}, bf16[256,256]{1,0:T(8,128)(2,1)S(1)}, u32[]{:S(2)}, u32[]{:S(2)}) collective-permute-start(bf16[256,256]{1,0:T(8,128)(2,1)S(1)} %get-tuple-element.53), channel_id=1, source_target_pairs={{0,4},{4,0},{8,12},{12,8},{1,5},{5,1},{9,13},{13,9},{2,6},{6,2},{1... | collective-permute-start | bytes 393224 | tf_op jit(solution)/shard_map/cells_1_chunk_1/ppermute | solution.py:255
  12.9 15.4 %collective-permute-start.3 = (bf16[256,256]{1,0:T(8,128)(2,1)S(1)}, bf16[256,256]{1,0:T(8,128)(2,1)S(1)}, u32[]{:S(2)}, u32[]{:S(2)}) collective-permute-start(bf16[256,256]{1,0:T(8,128)(2,1)S(1)} %get-tuple-element.56), channel_id=1, source_target_pairs={{0,8},{4,12},{8,0},{12,4},{1,9},{5,13},{9,1},{13,5},{2,10},{6,14},... | collective-permute-start | bytes 393224 | tf_op jit(solution)/shard_map/cells_2_chunk_1/ppermute | solution.py:255
  18.8 10.9 %collective-permute-start.5 = (bf16[256,256]{1,0:T(8,128)(2,1)S(1)}, bf16[256,256]{1,0:T(8,128)(2,1)S(1)}, u32[]{:S(2)}, u32[]{:S(2)}) collective-permute-start(bf16[256,256]{1,0:T(8,128)(2,1)S(1)} %get-tuple-element.59), channel_id=1, source_target_pairs={{0,12},{4,8},{8,4},{12,0},{1,13},{5,9},{9,5},{13,1},{2,14},{6,10},... | collective-permute-start | bytes 393224 | tf_op jit(solution)/shard_map/cells_3_chunk_1/ppermute | solution.py:255
  24.6 0.7 copy-start.3
  27.0 13.0 %collective-permute-start.13 = (bf16[1024,256]{1,0:T(8,128)(2,1)S(1)}, bf16[1024,256]{1,0:T(8,128)(2,1)S(1)}, u32[]{:S(2)}, u32[]{:S(2)}) collective-permute-start(bf16[1024,256]{1,0:T(8,128)(2,1)S(1)} %get-tuple-element.78), channel_id=1, source_target_pairs={{0,2},{1,3},{2,0},{3,1},{4,6},{5,7},{6,4},{7,5},{8,10},{9,11},{10,... | collective-permute-start | bytes 1572872 | tf_op jit(solution)/shard_map/far_0/ppermute | solution.py:258
  28.3 5.9 %collective-permute-start.7 = (bf16[256,256]{1,0:T(8,128)(2,1)S(1)}, bf16[256,256]{1,0:T(8,128)(2,1)S(1)}, u32[]{:S(2)}, u32[]{:S(2)}) collective-permute-start(bf16[256,256]{1,0:T(8,128)(2,1)S(1)} %get-tuple-element.67), channel_id=1, source_target_pairs={{0,4},{4,0},{8,12},{12,8},{1,5},{5,1},{9,13},{13,9},{2,6},{6,2},{1... | collective-permute-start | bytes 393224 | tf_op jit(solution)/shard_map/cells_1_chunk_2/ppermute | solution.py:255
  28.3 7.1 %collective-permute-start.9 = (bf16[256,256]{1,0:T(8,128)(2,1)S(1)}, bf16[256,256]{1,0:T(8,128)(2,1)S(1)}, u32[]{:S(2)}, u32[]{:S(2)}) collective-permute-start(bf16[256,256]{1,0:T(8,128)(2,1)S(1)} %get-tuple-element.71), channel_id=1, source_target_pairs={{0,8},{4,12},{8,0},{12,4},{1,9},{5,13},{9,1},{13,5},{2,10},{6,14},... | collective-permute-start | bytes 393224 | tf_op jit(solution)/shard_map/cells_2_chunk_2/ppermute | solution.py:255
  29.7 8.5 %collective-permute-start.11 = (bf16[256,256]{1,0:T(8,128)(2,1)S(1)}, bf16[256,256]{1,0:T(8,128)(2,1)S(1)}, u32[]{:S(2)}, u32[]{:S(2)}) collective-permute-start(bf16[256,256]{1,0:T(8,128)(2,1)S(1)} %get-tuple-element.75), channel_id=1, source_target_pairs={{0,12},{4,8},{8,4},{12,0},{1,13},{5,9},{9,5},{13,1},{2,14},{6,10},... | collective-permute-start | bytes 393224 | tf_op jit(solution)/shard_map/cells_3_chunk_2/ppermute | solution.py:255
  32.9 16.5 %collective-permute-start.6 = (bf16[1024,256]{1,0:T(8,128)(2,1)S(1)}, bf16[1024,256]{1,0:T(8,128)(2,1)S(1)}, u32[]{:S(2)}, u32[]{:S(2)}) collective-permute-start(bf16[1024,256]{1,0:T(8,128)(2,1)S(1)} %get-tuple-element.63), channel_id=1, source_target_pairs={{0,2},{1,3},{2,0},{3,1},{4,6},{5,7},{6,4},{7,5},{8,10},{9,11},{10,... | collective-permute-start | bytes 1572872 | tf_op jit(solution)/shard_map/far_1/ppermute | solution.py:258
  34.2 15.2 %collective-permute-start.8 = (bf16[256,256]{1,0:T(8,128)(2,1)S(1)}, bf16[256,256]{1,0:T(8,128)(2,1)S(1)}, u32[]{:S(2)}, u32[]{:S(2)}) collective-permute-start(bf16[256,256]{1,0:T(8,128)(2,1)S(1)} %get-tuple-element.68), channel_id=1, source_target_pairs={{0,4},{4,0},{8,12},{12,8},{1,5},{5,1},{9,13},{13,9},{2,6},{6,2},{1... | collective-permute-start | bytes 393224 | tf_op jit(solution)/shard_map/cells_1_chunk_3/ppermute | solution.py:255
  35.4 14.0 %collective-permute-start.10 = (bf16[256,256]{1,0:T(8,128)(2,1)S(1)}, bf16[256,256]{1,0:T(8,128)(2,1)S(1)}, u32[]{:S(2)}, u32[]{:S(2)}) collective-permute-start(bf16[256,256]{1,0:T(8,128)(2,1)S(1)} %get-tuple-element.72), channel_id=1, source_target_pairs={{0,8},{4,12},{8,0},{12,4},{1,9},{5,13},{9,1},{13,5},{2,10},{6,14},... | collective-permute-start | bytes 393224 | tf_op jit(solution)/shard_map/cells_2_chunk_3/ppermute | solution.py:255
  38.3 13.9 %collective-permute-start.12 = (bf16[256,256]{1,0:T(8,128)(2,1)S(1)}, bf16[256,256]{1,0:T(8,128)(2,1)S(1)}, u32[]{:S(2)}, u32[]{:S(2)}) collective-permute-start(bf16[256,256]{1,0:T(8,128)(2,1)S(1)} %get-tuple-element.76), channel_id=1, source_target_pairs={{0,12},{4,8},{8,4},{12,0},{1,13},{5,9},{9,5},{13,1},{2,14},{6,10},... | collective-permute-start | bytes 393224 | tf_op jit(solution)/shard_map/cells_3_chunk_3/ppermute | solution.py:255
  41.8 19.4 %collective-permute-start.16 = (bf16[1024,256]{1,0:T(8,128)(2,1)S(1)}, bf16[1024,256]{1,0:T(8,128)(2,1)S(1)}, u32[]{:S(2)}, u32[]{:S(2)}) collective-permute-start(bf16[1024,256]{1,0:T(8,128)(2,1)S(1)} %get-tuple-element.88), channel_id=1, source_target_pairs={{0,2},{1,3},{2,0},{3,1},{4,6},{5,7},{6,4},{7,5},{8,10},{9,11},{10,... | collective-permute-start | bytes 1572872 | tf_op jit(solution)/shard_map/far_2/ppermute | solution.py:258
  53.5 18.5 %collective-permute-start.15 = (bf16[4096,256]{1,0:T(8,128)(2,1)S(1)}, bf16[4096,256]{1,0:T(8,128)(2,1)S(1)}, u32[]{:S(2)}, u32[]{:S(2)}) collective-permute-start(bf16[4096,256]{1,0:T(8,128)(2,1)S(1)} %get-tuple-element.87.refs_0_), channel_id=1, source_target_pairs={{0,1},{1,0},{2,3},{3,2},{4,5},{5,4},{6,7},{7,6},{8,9},{9,8},{10,11... | collective-permute-start | bytes 6291464 | tf_op jit(solution)/shard_map/near/ppermute | solution.py:262
  56.6 28.2 %collective-permute-start.14 = (bf16[1024,256]{1,0:T(8,128)(2,1)S(1)}, bf16[1024,256]{1,0:T(8,128)(2,1)S(1)}, u32[]{:S(2)}, u32[]{:S(2)}) collective-permute-start(bf16[1024,256]{1,0:T(8,128)(2,1)S(1)} %get-tuple-element.86), channel_id=1, source_target_pairs={{0,2},{1,3},{2,0},{3,1},{4,6},{5,7},{6,4},{7,5},{8,10},{9,11},{10,... | collective-permute-start | bytes 1572872 | tf_op jit(solution)/shard_map/far_3/ppermute | solution.py:258
  61.2 10.9 %collective-permute-start.17 = (bf16[1024,256]{1,0:T(8,128)(2,1)S(1)}, bf16[1024,256]{1,0:T(8,128)(2,1)S(1)}, u32[]{:S(2)}, u32[]{:S(2)}) collective-permute-start(bf16[1024,256]{1,0:T(8,128)(2,1)S(1)} %collective-permute-done.13.refs_1_), channel_id=1, source_target_pairs={{0,1},{1,0},{2,3},{3,2},{4,5},{5,4},{6,7},{7,6},{8,9},{9,8},{10,11... | collective-permute-start | bytes 1572872 | tf_op jit(solution)/shard_map/far_near_0/ppermute | solution.py:262
  66.2 5.8 %collective-permute-start.18 = (bf16[1024,256]{1,0:T(8,128)(2,1)S(1)}, bf16[1024,256]{1,0:T(8,128)(2,1)S(1)}, u32[]{:S(2)}, u32[]{:S(2)}) collective-permute-start(bf16[1024,256]{1,0:T(8,128)(2,1)S(1)} %collective-permute-done.6.refs_2_), channel_id=1, source_target_pairs={{0,1},{1,0},{2,3},{3,2},{4,5},{5,4},{6,7},{7,6},{8,9},{9,8},{10,11... | collective-permute-start | bytes 1572872 | tf_op jit(solution)/shard_map/far_near_1/ppermute | solution.py:262
  66.2 5.9 %collective-permute-start.19 = (bf16[1024,256]{1,0:T(8,128)(2,1)S(1)}, bf16[1024,256]{1,0:T(8,128)(2,1)S(1)}, u32[]{:S(2)}, u32[]{:S(2)}) collective-permute-start(bf16[1024,256]{1,0:T(8,128)(2,1)S(1)} %collective-permute-done.16.refs_3_), channel_id=1, source_target_pairs={{0,1},{1,0},{2,3},{3,2},{4,5},{5,4},{6,7},{7,6},{8,9},{9,8},{10,11... | collective-permute-start | bytes 1572872 | tf_op jit(solution)/shard_map/far_near_2/ppermute | solution.py:262
  84.8 2.0 %collective-permute-start.20 = (bf16[1024,256]{1,0:T(8,128)(2,1)S(1)}, bf16[1024,256]{1,0:T(8,128)(2,1)S(1)}, u32[]{:S(2)}, u32[]{:S(2)}) collective-permute-start(bf16[1024,256]{1,0:T(8,128)(2,1)S(1)} %collective-permute-done.14.refs_0_), channel_id=1, source_target_pairs={{0,1},{1,0},{2,3},{3,2},{4,5},{5,4},{6,7},{7,6},{8,9},{9,8},{10,11... | collective-permute-start | bytes 1572872 | tf_op jit(solution)/shard_map/far_near_3/ppermute | solution.py:262

commit v7 on v6

--- a/solution.py
+++ b/solution.py
@@ -122,12 +122,11 @@
         scaled_ref[j * cap : (j + 1) * cap, :] = scaled.astype(jnp.bfloat16)
         work[j * cap : (j + 1) * cap, :] = scaled
     slots = types * cap
-    rows = pl.ds(chunk * slots, slots)
-    copies = [pltpu.make_async_copy(scaled_ref, all_ref.at[rows, :], sems.at[0])]
+    columns = pl.ds(chunk * width, width)
+    copies = [pltpu.make_async_copy(scaled_ref, all_ref.at[:, columns], sems.at[0])]
     copies[0].start()
     turned[...] = jnp.transpose(work[...]).astype(jnp.bfloat16)
-    rows = pl.ds(chunk * width, width)
-    copies.append(pltpu.make_async_copy(turned, turned_ref.at[rows, :], sems.at[1]))
+    copies.append(pltpu.make_async_copy(turned, turned_ref.at[columns, :], sems.at[1]))
     copies[-1].start()
     for copy in copies:
         copy.wait()
@@ -147,7 +146,7 @@
         jax.ShapeDtypeStruct((slots, width), jnp.bfloat16),
         jax.ShapeDtypeStruct((chunks * width, slots), jnp.bfloat16),
         jax.ShapeDtypeStruct((8, 128), jnp.float32),
-        jax.ShapeDtypeStruct((chunks * slots, width), jnp.bfloat16),
+        jax.ShapeDtypeStruct((slots, chunks * width), jnp.bfloat16),
     ]
     aliases = {}
     for value, output in ((left, 1), (own, 3)):
@@ -173,56 +172,83 @@
     )(*args)
 
 
-def gram_kernel(blocks, cores, items, count_ref, left_ref, *refs):
-    out_ref, tile, sems = refs[-3:]
+def gram_kernel(blocks, cores, strip, groups, arrays, count_ref, left_ref, *refs):
+    sources = refs[:arrays]
+    out_ref, joined, tile, join_sems, sems = refs[-5:]
     rows, slots = left_ref.shape
-    width = tile.shape[2]
     inverse = 1.0 / count_ref[0:1, 0:1]
     me = lax.axis_index("blk")
-    stores = []
-    for source, index, chip, flip, chunk in items:
-        slot = len(stores) % 2
-        if len(stores) >= 2:
-            stores[-2].wait()
-        product = jnp.dot(
-            left_ref[...],
-            refs[source][index * slots : (index + 1) * slots, :],
-            preferred_element_type=jnp.float32,
-        )
-        tile[slot] = (product * inverse).astype(jnp.bfloat16)
+
+    joins, column = [], 0
+    for panels, _ in groups:
+        joins.append([])
+        if len(panels) > 1:
+            for index in panels:
+                width = sources[index].shape[1]
+                spot = joined.at[:, pl.ds(column, width)]
+                joins[-1].append((column, sources[index], spot))
+                column += width
+    sent = 0
+    for parts in joins:
+        for _, source, spot in parts:
+            pltpu.make_async_copy(source, spot, join_sems.at[sent]).start()
+            sent += 1
+    stores, sent = [], 0
+    for (panels, (chip, flip, first)), parts in zip(groups, joins):
+        for _, source, spot in parts:
+            pltpu.make_async_copy(source, spot, join_sems.at[sent]).wait()
+            sent += 1
+        width = sum(sources[index].shape[1] for index in panels)
         owner = lax.rem(me + (blocks - chip * cores), blocks)
         owner = jnp.bitwise_xor(owner, flip)
-        column = pl.multiple_of(owner * rows + chunk * width, 128)
-        stores.append(
-            pltpu.make_async_copy(
-                tile.at[slot], out_ref.at[0, :, pl.ds(column, width)], sems.at[slot]
+        column = pl.multiple_of(owner * rows + first, 128)
+        for row in range(0, rows, strip):
+            slot = len(stores) % 2
+            if len(stores) >= 2:
+                stores[-2].wait()
+            if parts:
+                right = joined[:, parts[0][0] : parts[0][0] + width]
+            else:
+                right = sources[panels[0]][...]
+            product = jnp.dot(
+                left_ref[row : row + strip, :], right, preferred_element_type=jnp.float32
             )
-        )
-        stores[-1].start()
+            tile[slot, :, 0:width] = (product * inverse).astype(jnp.bfloat16)
+            stores.append(
+                pltpu.make_async_copy(
+                    tile.at[slot, :, pl.ds(0, width)],
+                    out_ref.at[0, pl.ds(row, strip), pl.ds(column, width)],
+                    sems.at[slot],
+                )
+            )
+            stores[-1].start()
     for store in stores[-2:]:
         store.wait()
 
 
-def gram(blocks, cores, count, left, panels, before, cost):
+def gram(blocks, cores, count, left, groups, before, cost):
     rows, slots = left.shape
-    arrays, items = [], []
-    for array, index, *owner in panels:
-        if not any(array is other for other in arrays):
-            arrays.append(array)
-        items.append(([array is other for other in arrays].index(True), index, *owner))
-    width = arrays[0].shape[1]
+    arrays, layout = [], []
+    for panels, place in groups:
+        layout.append((list(range(len(arrays), len(arrays) + len(panels))), place))
+        arrays += panels
+    joined = [array for panels, _ in groups if len(panels) > 1 for array in panels]
+    widest = max(sum(array.shape[1] for array in panels) for panels, _ in groups)
+    strip = min(rows, 256)
     args = [count, left, *arrays]
     specs = [whole] * len(args)
     if before is not None:
         args.append(before)
         specs.append(anywhere)
     return pl.pallas_call(
-        functools.partial(gram_kernel, blocks, cores, items),
+        functools.partial(gram_kernel, blocks, cores, strip, layout, len(arrays)),
         in_specs=specs,
         out_specs=anywhere,
         out_shape=jax.ShapeDtypeStruct((1, rows, rows * blocks), jnp.bfloat16),
         scratch_shapes=[
-            pltpu.VMEM((2, rows, width), jnp.bfloat16),
+            pltpu.VMEM((slots, max(sum(array.shape[1] for array in joined), 128)), jnp.bfloat16),
+            pltpu.VMEM((2, strip, widest), jnp.bfloat16),
+            pltpu.SemaphoreType.DMA((max(len(joined), 1),)),
             pltpu.SemaphoreType.DMA((2,)),
         ],
         input_output_aliases={} if before is None else {len(args) - 1: 0},
@@ -289,14 +315,16 @@
     far_near = [
         [side(f"far_near_{k}", p, own, *far[last - 1]) for p in far[k]] for k in range(last)
     ]
-    out = multiply([(own, k, 0, 0, k) for k in range(chunks)], None, lengthy)
-    panels = [(near, k, 0, 1, k) for k in range(chunks)]
+    out = multiply([([own], (0, 0, 0))], None, lengthy)
+    groups = [([near], (0, 1, 0))]
     for flip, group in ((0, far), (1, far_near)):
-        panels += [(p, 0, d, flip, k) for k in range(last) for d, p in enumerate(group[k], 1)]
-    out = multiply(panels, out, brief)
+        for d in range(1, chips):
+            groups.append(([group[k][d - 1] for k in range(last)], (d, flip, 0)))
+    out = multiply(groups, out, brief)
     far_near = [side(f"far_near_{last}", p, out) for p in far[last]]
-    out = multiply([(p, 0, d, 0, last) for d, p in enumerate(far[last], 1)], out, brief)
-    return multiply([(p, 0, d, 1, last) for d, p in enumerate(far_near, 1)], out, brief)
+    edge = last * width
+    out = multiply([([p], (d, 0, edge)) for d, p in enumerate(far[last], 1)], out, brief)
+    return multiply([([p], (d, 1, edge)) for d, p in enumerate(far_near, 1)], out, brief)
 
 
 def solution(mesh):

time: 88.7 us -> 86.6 us (0.976)
  the two profiles are of different devices: /device:TPU:13 before, /device:TPU:9 now
where the time goes in v7:
time: 86.6 us; the launch traced here: 86.3 us
  starting transfers between devices  40.2 us (46%)
  Pallas kernels  27.4 us (32%)
  waiting for transfers between devices  15.1 us (17%)
  local copies, waits for them, and re-layouts  3.27 us (4%)
    ppermute x12, starting transfers between devices, swap(): return lax.ppermute(block, 'cells', [(s, s ^ by) for s in range(types)])  20.7 us
    pallas_call x4, Pallas kernels, gram(): pl.pallas_call(functools.partial(gram_kernel, blocks, cores, strip, layou...  19.1 us
    ppermute x12, waiting for transfers between devices, swap(): return lax.ppermute(block, 'cells', [(s, s ^ by) for s in range(types)])  11.6 us
    ppermute x4, starting transfers between devices, across(): lax.ppermute(panel_, 'blk', [(b, (b + by * cores) % blocks) for b in rang...  11.4 us
    ppermute x5, starting transfers between devices, side(): lax.ppermute(after(panel_, *waits), 'blk', [(b, b ^ 1) for b in range(blo...  8.19 us
    pallas_call x4, Pallas kernels, standardize(): pl.pallas_call(functools.partial(standardize_kernel, types, cap, lead, se...  6.6 us
    ppermute x4, waiting for transfers between devices, across(): lax.ppermute(panel_, 'blk', [(b, (b + by * cores) % blocks) for b in rang...  3.49 us
    unnamed x8, local copies, waits for them, and re-layouts  3.27 us
  transfers between devices with their start and end apart: 21, of which 7 were waited for; matrix products, arithmetic and copies ran while one was open for 0% of the time, Pallas kernels for 27%

profile of v7, /device:TPU:9, one launch (start us, length us, event | category | flops | bytes accessed | tf_op | source)
XLA Modules:
  0.0 86.3 jit_solution(4635167588434354219)
XLA Ops:
  0.0 1.2 %copy-done = bf16[512,1024]{1,0:T(8,128)(2,1)S(1)} copy-done((bf16[512,1024]{1,0:T(8,128)(2,1)S(1)}, bf16[512,1024]{1,0:T(8,128)(2,1)}, u32[]{:S(2)}) %copy-start) | copy-done | bytes 1048600
  1.2 0.7 copy-done.1
  1.9 0.7 copy-done.2
  2.6 1.7 %pack.1 = (bf16[272,256]{1,0:T(8,128)(2,1)S(1)}, bf16[272,256]{1,0:T(8,128)(2,1)S(1)}, bf16[272,256]{1,0:T(8,128)(2,1)S(1)}, bf16[272,256]{1,0:T(8,128)(2,1)S(1)...) custom-call(s32[512]{0:T(512)S(1)} %copy-done.1, ...), custom_call_target="tpu_custom_call" | custom-call | flops 1024 | bytes 1024 | tf_op jit(solution)/shard_map/pack/pallas_call | solution.py:68
  4.3 0.1 collective-permute-start
  4.4 2.5 %collective-permute-start.2 = (bf16[272,256]{1,0:T(8,128)(2,1)S(1)}, bf16[272,256]{1,0:T(8,128)(2,1)S(1)}, u32[]{:S(2)}, u32[]{:S(2)}) collective-permute-start(bf16[272,256]{1,0:T(8,128)(2,1)S(1)} %get-tuple-element.55), channel_id=1, source_target_pairs={{0,8},{4,12},{8,0},{12,4},{1,9},{5,13},{9,1},{13,5},{2,10},{6,14},... | collective-permute-start | bytes 417800 | tf_op jit(solution)/shard_map/cells_2_chunk_0/ppermute | solution.py:281
  6.9 0.2 collective-permute-start.4
  7.0 1.9 %collective-permute-done.refs_1_.refs_5_ = bf16[272,256]{1,0:T(8,128)(2,1)S(1)} collective-permute-done((bf16[272,256]{1,0:T(8,128)(2,1)S(1)}, bf16[272,256]{1,0:T(8,128)(2,1)S(1)}, u32[]{:S(2)}, u32[]{:S(2)}) %collective-permute-start) | collective-permute-done | bytes 139296 | tf_op jit(solution)/shard_map/cells_1_chunk_0/ppermute | solution.py:281
  8.9 0.3 collective-permute-start.1
  9.2 3.7 %collective-permute-done.2.refs_2_.refs_6_ = bf16[272,256]{1,0:T(8,128)(2,1)S(1)} collective-permute-done((bf16[272,256]{1,0:T(8,128)(2,1)S(1)}, bf16[272,256]{1,0:T(8,128)(2,1)S(1)}, u32[]{:S(2)}, u32[]{:S(2)}) %collective-permute-start.2) | collective-permute-done | bytes 139296 | tf_op jit(solution)/shard_map/cells_2_chunk_0/ppermute | solution.py:281
  12.9 4.7 %collective-permute-start.3 = (bf16[256,256]{1,0:T(8,128)(2,1)S(1)}, bf16[256,256]{1,0:T(8,128)(2,1)S(1)}, u32[]{:S(2)}, u32[]{:S(2)}) collective-permute-start(bf16[256,256]{1,0:T(8,128)(2,1)S(1)} %get-tuple-element.56), channel_id=1, source_target_pairs={{0,8},{4,12},{8,0},{12,4},{1,9},{5,13},{9,1},{13,5},{2,10},{6,14},... | collective-permute-start | bytes 393224 | tf_op jit(solution)/shard_map/cells_2_chunk_1/ppermute | solution.py:281
  17.6 1.2 %collective-permute-done.4.refs_3_.refs_7_ = bf16[272,256]{1,0:T(8,128)(2,1)S(1)} collective-permute-done((bf16[272,256]{1,0:T(8,128)(2,1)S(1)}, bf16[272,256]{1,0:T(8,128)(2,1)S(1)}, u32[]{:S(2)}, u32[]{:S(2)}) %collective-permute-start.4) | collective-permute-done | bytes 139296 | tf_op jit(solution)/shard_map/cells_3_chunk_0/ppermute | solution.py:281
  18.8 5.8 %collective-permute-start.5 = (bf16[256,256]{1,0:T(8,128)(2,1)S(1)}, bf16[256,256]{1,0:T(8,128)(2,1)S(1)}, u32[]{:S(2)}, u32[]{:S(2)}) collective-permute-start(bf16[256,256]{1,0:T(8,128)(2,1)S(1)} %get-tuple-element.59), channel_id=1, source_target_pairs={{0,12},{4,8},{8,4},{12,0},{1,13},{5,9},{9,5},{13,1},{2,14},{6,10},... | collective-permute-start | bytes 393224 | tf_op jit(solution)/shard_map/cells_3_chunk_1/ppermute | solution.py:281
  24.6 0.7 copy-done.3
  25.3 1.8 %standardize.4 = (bf16[1024,256]{1,0:T(8,128)(2,1)S(1)}, bf16[1024,1024]{1,0:T(8,128)(2,1)S(1)}, f32[8,128]{1,0:T(8,128)}, bf16[1024,1024]{1,0:T(8,128)(2,1)S(1)}) custom-call(f32[1,1024]{1,0:T(1,128)S(1)} %bitcast.1, bf16[272,256]{1,0:T(8,128)(2,1)S(1)} %get-tuple-element.60.refs_0_.refs_4_, bf16[272,256]{1,0:T(8,128)(2,1)S(1)} %collective-permute-done.refs_1_.refs_5_, ...), custom_call_target="tpu_custom_call" | custom-call | flops 20000000000 | bytes 1024 | tf_op jit(solution)/shard_map/standardize/pallas_call | solution.py:157
  27.1 1.2 %collective-permute-start.13 = (bf16[1024,256]{1,0:T(8,128)(2,1)S(1)}, bf16[1024,256]{1,0:T(8,128)(2,1)S(1)}, u32[]{:S(2)}, u32[]{:S(2)}) collective-permute-start(bf16[1024,256]{1,0:T(8,128)(2,1)S(1)} %get-tuple-element.78), channel_id=1, source_target_pairs={{0,2},{1,3},{2,0},{3,1},{4,6},{5,7},{6,4},{7,5},{8,10},{9,11},{10,... | collective-permute-start | bytes 1572872 | tf_op jit(solution)/shard_map/far_0/ppermute | solution.py:284
  28.3 0.0 collective-permute-done.1.refs_1_
  28.3 0.0 collective-permute-start.7
  28.3 1.4 %collective-permute-start.9 = (bf16[256,256]{1,0:T(8,128)(2,1)S(1)}, bf16[256,256]{1,0:T(8,128)(2,1)S(1)}, u32[]{:S(2)}, u32[]{:S(2)}) collective-permute-start(bf16[256,256]{1,0:T(8,128)(2,1)S(1)} %get-tuple-element.71), channel_id=1, source_target_pairs={{0,8},{4,12},{8,0},{12,4},{1,9},{5,13},{9,1},{13,5},{2,10},{6,14},... | collective-permute-start | bytes 393224 | tf_op jit(solution)/shard_map/cells_2_chunk_2/ppermute | solution.py:281
  29.7 0.1 collective-permute-done.5.refs_3_
  29.8 1.4 %collective-permute-start.11 = (bf16[256,256]{1,0:T(8,128)(2,1)S(1)}, bf16[256,256]{1,0:T(8,128)(2,1)S(1)}, u32[]{:S(2)}, u32[]{:S(2)}) collective-permute-start(bf16[256,256]{1,0:T(8,128)(2,1)S(1)} %get-tuple-element.75), channel_id=1, source_target_pairs={{0,12},{4,8},{8,4},{12,0},{1,13},{5,9},{9,5},{13,1},{2,14},{6,10},... | collective-permute-start | bytes 393224 | tf_op jit(solution)/shard_map/cells_3_chunk_2/ppermute | solution.py:281
  31.1 1.8 %standardize.5 = (bf16[1024,256]{1,0:T(8,128)(2,1)S(1)}, bf16[1024,1024]{1,0:T(8,128)(2,1)S(1)}, f32[8,128]{1,0:T(8,128)}, bf16[1024,1024]{1,0:T(8,128)(2,1)S(1)}) custom-call(f32[1,1024]{1,0:T(1,128)S(1)} %bitcast.2, bf16[256,256]{1,0:T(8,128)(2,1)S(1)} %get-tuple-element.50.refs_0_, ...), custom_call_target="tpu_custom_call", output_to_operand_aliasing={{1}: (9, {}), {3}: (10, {})} | custom-call | flops 20000000000 | bytes 1024 | tf_op jit(solution)/shard_map/standardize/pallas_call | solution.py:157
  32.9 1.3 %collective-permute-start.6 = (bf16[1024,256]{1,0:T(8,128)(2,1)S(1)}, bf16[1024,256]{1,0:T(8,128)(2,1)S(1)}, u32[]{:S(2)}, u32[]{:S(2)}) collective-permute-start(bf16[1024,256]{1,0:T(8,128)(2,1)S(1)} %get-tuple-element.63), channel_id=1, source_target_pairs={{0,2},{1,3},{2,0},{3,1},{4,6},{5,7},{6,4},{7,5},{8,10},{9,11},{10,... | collective-permute-start | bytes 1572872 | tf_op jit(solution)/shard_map/far_1/ppermute | solution.py:284
  34.2 1.2 %collective-permute-done.9.refs_2_ = bf16[256,256]{1,0:T(8,128)(2,1)S(1)} collective-permute-done((bf16[256,256]{1,0:T(8,128)(2,1)S(1)}, bf16[256,256]{1,0:T(8,128)(2,1)S(1)}, u32[]{:S(2)}, u32[]{:S(2)}) %collective-permute-start.9) | collective-permute-done | bytes 131104 | tf_op jit(solution)/shard_map/cells_2_chunk_2/ppermute | solution.py:281
  35.4 2.8 %collective-permute-start.10 = (bf16[256,256]{1,0:T(8,128)(2,1)S(1)}, bf16[256,256]{1,0:T(8,128)(2,1)S(1)}, u32[]{:S(2)}, u32[]{:S(2)}) collective-permute-start(bf16[256,256]{1,0:T(8,128)(2,1)S(1)} %get-tuple-element.72), channel_id=1, source_target_pairs={{0,8},{4,12},{8,0},{12,4},{1,9},{5,13},{9,1},{13,5},{2,10},{6,14},... | collective-permute-start | bytes 393224 | tf_op jit(solution)/shard_map/cells_2_chunk_3/ppermute | solution.py:281
  38.3 1.6 %collective-permute-start.12 = (bf16[256,256]{1,0:T(8,128)(2,1)S(1)}, bf16[256,256]{1,0:T(8,128)(2,1)S(1)}, u32[]{:S(2)}, u32[]{:S(2)}) collective-permute-start(bf16[256,256]{1,0:T(8,128)(2,1)S(1)} %get-tuple-element.76), channel_id=1, source_target_pairs={{0,12},{4,8},{8,4},{12,0},{1,13},{5,9},{9,5},{13,1},{2,14},{6,10},... | collective-permute-start | bytes 393224 | tf_op jit(solution)/shard_map/cells_3_chunk_3/ppermute | solution.py:281
  39.9 1.8 %standardize.6 = (bf16[1024,256]{1,0:T(8,128)(2,1)S(1)}, bf16[1024,1024]{1,0:T(8,128)(2,1)S(1)}, f32[8,128]{1,0:T(8,128)}, bf16[1024,1024]{1,0:T(8,128)(2,1)S(1)}) custom-call(f32[1,1024]{1,0:T(1,128)S(1)} %bitcast.3, bf16[256,256]{1,0:T(8,128)(2,1)S(1)} %get-tuple-element.79.refs_0_, ...), custom_call_target="tpu_custom_call", output_to_operand_aliasing={{1}: (9, {}), {3}: (10, {})} | custom-call | flops 20000000000 | bytes 1024 | tf_op jit(solution)/shard_map/standardize/pallas_call | solution.py:157
  41.7 7.7 %collective-permute-start.16 = (bf16[1024,256]{1,0:T(8,128)(2,1)S(1)}, bf16[1024,256]{1,0:T(8,128)(2,1)S(1)}, u32[]{:S(2)}, u32[]{:S(2)}) collective-permute-start(bf16[1024,256]{1,0:T(8,128)(2,1)S(1)} %get-tuple-element.88), channel_id=1, source_target_pairs={{0,2},{1,3},{2,0},{3,1},{4,6},{5,7},{6,4},{7,5},{8,10},{9,11},{10,... | collective-permute-start | bytes 1572872 | tf_op jit(solution)/shard_map/far_2/ppermute | solution.py:284
  49.4 0.0 collective-permute-done.6.refs_2_
  49.4 0.0 collective-permute-done.8.refs_1_
  49.4 0.0 collective-permute-done.10.refs_2_
  49.4 3.5 %collective-permute-done.12.refs_3_ = bf16[256,256]{1,0:T(8,128)(2,1)S(1)} collective-permute-done((bf16[256,256]{1,0:T(8,128)(2,1)S(1)}, bf16[256,256]{1,0:T(8,128)(2,1)S(1)}, u32[]{:S(2)}, u32[]{:S(2)}) %collective-permute-start.12) | collective-permute-done | bytes 131104 | tf_op jit(solution)/shard_map/cells_3_chunk_3/ppermute | solution.py:281
  52.9 1.2 %standardize.7 = (bf16[1024,256]{1,0:T(8,128)(2,1)S(1)}, bf16[1024,1024]{1,0:T(8,128)(2,1)S(1)}, f32[8,128]{1,0:T(8,128)S(1)}, bf16[1024,1024]{1,0:T(8,128)(2,1)S(1)}) custom-call(f32[1,1024]{1,0:T(1,128)S(1)} %bitcast.4, bf16[256,256]{1,0:T(8,128)(2,1)S(1)} %get-tuple-element.64.refs_0_, ...), custom_call_target="tpu_custom_call", output_to_operand_aliasing={{1}: (9, {}), {3}: (10, {})} | custom-call | flops 20000000000 | bytes 1024 | tf_op jit(solution)/shard_map/standardize/pallas_call | solution.py:157
  54.1 2.4 %collective-permute-start.15 = (bf16[1024,1024]{1,0:T(8,128)(2,1)S(1)}, bf16[1024,1024]{1,0:T(8,128)(2,1)S(1)}, u32[]{:S(2)}, u32[]{:S(2)}) collective-permute-start(bf16[1024,1024]{1,0:T(8,128)(2,1)S(1)} %get-tuple-element.87.refs_0_), channel_id=1, source_target_pairs={{0,1},{1,0},{2,3},{3,2},{4,5},{5,4},{6,7},{7,6},{8,9},{9,8},{10,11... | collective-permute-start | bytes 6291464 | tf_op jit(solution)/shard_map/near/ppermute | solution.py:288
  56.4 1.2 %collective-permute-start.14 = (bf16[1024,256]{1,0:T(8,128)(2,1)S(1)}, bf16[1024,256]{1,0:T(8,128)(2,1)S(1)}, u32[]{:S(2)}, u32[]{:S(2)}) collective-permute-start(bf16[1024,256]{1,0:T(8,128)(2,1)S(1)} %get-tuple-element.86), channel_id=1, source_target_pairs={{0,2},{1,3},{2,0},{3,1},{4,6},{5,7},{6,4},{7,5},{8,10},{9,11},{10,... | collective-permute-start | bytes 1572872 | tf_op jit(solution)/shard_map/far_3/ppermute | solution.py:284
  57.6 3.5 %collective-permute-done.16.refs_3_ = bf16[1024,256]{1,0:T(8,128)(2,1)S(1)} collective-permute-done((bf16[1024,256]{1,0:T(8,128)(2,1)S(1)}, bf16[1024,256]{1,0:T(8,128)(2,1)S(1)}, u32[]{:S(2)}, u32[]{:S(2)}) %collective-permute-start.16) | collective-permute-done | bytes 524320 | tf_op jit(solution)/shard_map/far_2/ppermute | solution.py:284
  61.1 5.2 %collective-permute-start.17 = (bf16[1024,256]{1,0:T(8,128)(2,1)S(1)}, bf16[1024,256]{1,0:T(8,128)(2,1)S(1)}, u32[]{:S(2)}, u32[]{:S(2)}) collective-permute-start(bf16[1024,256]{1,0:T(8,128)(2,1)S(1)} %collective-permute-done.13.refs_1_), channel_id=1, source_target_pairs={{0,1},{1,0},{2,3},{3,2},{4,5},{5,4},{6,7},{7,6},{8,9},{9,8},{10,11... | collective-permute-start | bytes 1572872 | tf_op jit(solution)/shard_map/far_near_0/ppermute | solution.py:288
  66.4 0.0 collective-permute-start.18
  66.4 0.5 collective-permute-start.19
  66.9 3.8 %gram.4.refs_7_ = bf16[1,1024,4096]{2,1,0:T(8,128)(2,1)} custom-call(f32[8,128]{1,0:T(8,128)S(1)} %get-tuple-element.84.count_ref, bf16[1024,1024]{1,0:T(8,128)(2,1)S(1)} %get-tuple-element.85.left_ref, bf16[1024,1024]{1,0:T(8,128)(2,1)S(1)} %get-tuple-element.87.refs_0_), custom_call_target="tpu_custom_call" | custom-call | flops 20000000000 | bytes 1024 | tf_op jit(solution)/shard_map/gram/pallas_call | solution.py:243
  70.7 0.0 collective-permute-done.17.refs_4_
  70.7 0.0 collective-permute-done.18.refs_5_
  70.7 10.1 %gram.5.refs_1_ = bf16[1,1024,4096]{2,1,0:T(8,128)(2,1)} custom-call(f32[8,128]{1,0:T(8,128)S(1)} %get-tuple-element.84.count_ref, bf16[1024,1024]{1,0:T(8,128)(2,1)S(1)} %get-tuple-element.85.left_ref, bf16[1024,1024]{1,0:T(8,128)(2,1)S(1)} %collective-permute-done.15.refs_0_, ...), custom_call_target="tpu_custom_call", output_to_operand_aliasing={{}: (9, {})} | custom-call | flops 1024 | bytes 1024 | tf_op jit(solution)/shard_map/gram/pallas_call | solution.py:243
  80.8 0.0 collective-permute-done.14.refs_0_
  80.8 0.1 collective-permute-start.20
  80.9 2.6 %gram.6.refs_1_ = bf16[1,1024,4096]{2,1,0:T(8,128)(2,1)} custom-call(f32[8,128]{1,0:T(8,128)S(1)} %get-tuple-element.84.count_ref, bf16[1024,1024]{1,0:T(8,128)(2,1)S(1)} %get-tuple-element.85.left_ref, bf16[1024,256]{1,0:T(8,128)(2,1)S(1)} %collective-permute-done.14.refs_0_, bf16[1,1024,4096]{2,1,0:T(8,128)(2,1)} %gram.5.refs_1_), custom_call_target="tpu_custom_call", output_to_operand_aliasing={{}: (3, {})} | custom-call | flops 1024 | bytes 1024 | tf_op jit(solution)/shard_map/gram/pallas_call | solution.py:243
  83.5 0.0 collective-permute-done.20.refs_0_
  83.5 2.6 %gram.7 = bf16[1,1024,4096]{2,1,0:T(8,128)(2,1)} custom-call(f32[8,128]{1,0:T(8,128)S(1)} %get-tuple-element.84.count_ref, bf16[1024,1024]{1,0:T(8,128)(2,1)S(1)} %get-tuple-element.85.left_ref, bf16[1024,256]{1,0:T(8,128)(2,1)S(1)} %collective-permute-done.20.refs_0_, bf16[1,1024,4096]{2,1,0:T(8,128)(2,1)} %gram.6.refs_1_), custom_call_target="tpu_custom_call", output_to_operand_aliasing={{}: (3, {})} | custom-call | flops 1024 | bytes 1024 | tf_op jit(solution)/shard_map/gram/pallas_call | solution.py:243
  (11 shorter events, 0.0 us)
Async XLA Ops:
  0.0 1.2 %copy-start = (bf16[512,1024]{1,0:T(8,128)(2,1)S(1)}, bf16[512,1024]{1,0:T(8,128)(2,1)}, u32[]{:S(2)}) copy-start(bf16[512,1024]{1,0:T(8,128)(2,1)} %expr_ref.1) | copy-start | bytes 3145732
  1.2 0.7 copy-start.1
  1.9 0.7 copy-start.2
  4.3 4.6 %collective-permute-start = (bf16[272,256]{1,0:T(8,128)(2,1)S(1)}, bf16[272,256]{1,0:T(8,128)(2,1)S(1)}, u32[]{:S(2)}, u32[]{:S(2)}) collective-permute-start(bf16[272,256]{1,0:T(8,128)(2,1)S(1)} %get-tuple-element.52), channel_id=1, source_target_pairs={{0,4},{4,0},{8,12},{12,8},{1,5},{5,1},{9,13},{13,9},{2,6},{6,2},{1... | collective-permute-start | bytes 417800 | tf_op jit(solution)/shard_map/cells_1_chunk_0/ppermute | solution.py:281
  4.4 8.5 %collective-permute-start.2 = (bf16[272,256]{1,0:T(8,128)(2,1)S(1)}, bf16[272,256]{1,0:T(8,128)(2,1)S(1)}, u32[]{:S(2)}, u32[]{:S(2)}) collective-permute-start(bf16[272,256]{1,0:T(8,128)(2,1)S(1)} %get-tuple-element.55), channel_id=1, source_target_pairs={{0,8},{4,12},{8,0},{12,4},{1,9},{5,13},{9,1},{13,5},{2,10},{6,14},... | collective-permute-start | bytes 417800 | tf_op jit(solution)/shard_map/cells_2_chunk_0/ppermute | solution.py:281
  6.9 12.0 %collective-permute-start.4 = (bf16[272,256]{1,0:T(8,128)(2,1)S(1)}, bf16[272,256]{1,0:T(8,128)(2,1)S(1)}, u32[]{:S(2)}, u32[]{:S(2)}) collective-permute-start(bf16[272,256]{1,0:T(8,128)(2,1)S(1)} %get-tuple-element.58), channel_id=1, source_target_pairs={{0,12},{4,8},{8,4},{12,0},{1,13},{5,9},{9,5},{13,1},{2,14},{6,10},... | collective-permute-start | bytes 417800 | tf_op jit(solution)/shard_map/cells_3_chunk_0/ppermute | solution.py:281
  8.9 19.4 %collective-permute-start.1 = (bf16[256,256]{1,0:T(8,128)(2,1)S(1)}, bf16[256,256]{1,0:T(8,128)(2,1)S(1)}, u32[]{:S(2)}, u32[]{:S(2)}) collective-permute-start(bf16[256,256]{1,0:T(8,128)(2,1)S(1)} %get-tuple-element.53), channel_id=1, source_target_pairs={{0,4},{4,0},{8,12},{12,8},{1,5},{5,1},{9,13},{13,9},{2,6},{6,2},{1... | collective-permute-start | bytes 393224 | tf_op jit(solution)/shard_map/cells_1_chunk_1/ppermute | solution.py:281
  12.9 15.4 %collective-permute-start.3 = (bf16[256,256]{1,0:T(8,128)(2,1)S(1)}, bf16[256,256]{1,0:T(8,128)(2,1)S(1)}, u32[]{:S(2)}, u32[]{:S(2)}) collective-permute-start(bf16[256,256]{1,0:T(8,128)(2,1)S(1)} %get-tuple-element.56), channel_id=1, source_target_pairs={{0,8},{4,12},{8,0},{12,4},{1,9},{5,13},{9,1},{13,5},{2,10},{6,14},... | collective-permute-start | bytes 393224 | tf_op jit(solution)/shard_map/cells_2_chunk_1/ppermute | solution.py:281
  18.8 10.9 %collective-permute-start.5 = (bf16[256,256]{1,0:T(8,128)(2,1)S(1)}, bf16[256,256]{1,0:T(8,128)(2,1)S(1)}, u32[]{:S(2)}, u32[]{:S(2)}) collective-permute-start(bf16[256,256]{1,0:T(8,128)(2,1)S(1)} %get-tuple-element.59), channel_id=1, source_target_pairs={{0,12},{4,8},{8,4},{12,0},{1,13},{5,9},{9,5},{13,1},{2,14},{6,10},... | collective-permute-start | bytes 393224 | tf_op jit(solution)/shard_map/cells_3_chunk_1/ppermute | solution.py:281
  24.6 0.7 copy-start.3
  27.1 12.8 %collective-permute-start.13 = (bf16[1024,256]{1,0:T(8,128)(2,1)S(1)}, bf16[1024,256]{1,0:T(8,128)(2,1)S(1)}, u32[]{:S(2)}, u32[]{:S(2)}) collective-permute-start(bf16[1024,256]{1,0:T(8,128)(2,1)S(1)} %get-tuple-element.78), channel_id=1, source_target_pairs={{0,2},{1,3},{2,0},{3,1},{4,6},{5,7},{6,4},{7,5},{8,10},{9,11},{10,... | collective-permute-start | bytes 1572872 | tf_op jit(solution)/shard_map/far_0/ppermute | solution.py:284
  28.3 5.9 %collective-permute-start.7 = (bf16[256,256]{1,0:T(8,128)(2,1)S(1)}, bf16[256,256]{1,0:T(8,128)(2,1)S(1)}, u32[]{:S(2)}, u32[]{:S(2)}) collective-permute-start(bf16[256,256]{1,0:T(8,128)(2,1)S(1)} %get-tuple-element.67), channel_id=1, source_target_pairs={{0,4},{4,0},{8,12},{12,8},{1,5},{5,1},{9,13},{13,9},{2,6},{6,2},{1... | collective-permute-start | bytes 393224 | tf_op jit(solution)/shard_map/cells_1_chunk_2/ppermute | solution.py:281
  28.3 7.1 %collective-permute-start.9 = (bf16[256,256]{1,0:T(8,128)(2,1)S(1)}, bf16[256,256]{1,0:T(8,128)(2,1)S(1)}, u32[]{:S(2)}, u32[]{:S(2)}) collective-permute-start(bf16[256,256]{1,0:T(8,128)(2,1)S(1)} %get-tuple-element.71), channel_id=1, source_target_pairs={{0,8},{4,12},{8,0},{12,4},{1,9},{5,13},{9,1},{13,5},{2,10},{6,14},... | collective-permute-start | bytes 393224 | tf_op jit(solution)/shard_map/cells_2_chunk_2/ppermute | solution.py:281
  29.8 8.5 %collective-permute-start.11 = (bf16[256,256]{1,0:T(8,128)(2,1)S(1)}, bf16[256,256]{1,0:T(8,128)(2,1)S(1)}, u32[]{:S(2)}, u32[]{:S(2)}) collective-permute-start(bf16[256,256]{1,0:T(8,128)(2,1)S(1)} %get-tuple-element.75), channel_id=1, source_target_pairs={{0,12},{4,8},{8,4},{12,0},{1,13},{5,9},{9,5},{13,1},{2,14},{6,10},... | collective-permute-start | bytes 393224 | tf_op jit(solution)/shard_map/cells_3_chunk_2/ppermute | solution.py:281
  32.9 16.5 %collective-permute-start.6 = (bf16[1024,256]{1,0:T(8,128)(2,1)S(1)}, bf16[1024,256]{1,0:T(8,128)(2,1)S(1)}, u32[]{:S(2)}, u32[]{:S(2)}) collective-permute-start(bf16[1024,256]{1,0:T(8,128)(2,1)S(1)} %get-tuple-element.63), channel_id=1, source_target_pairs={{0,2},{1,3},{2,0},{3,1},{4,6},{5,7},{6,4},{7,5},{8,10},{9,11},{10,... | collective-permute-start | bytes 1572872 | tf_op jit(solution)/shard_map/far_1/ppermute | solution.py:284
  34.2 15.2 %collective-permute-start.8 = (bf16[256,256]{1,0:T(8,128)(2,1)S(1)}, bf16[256,256]{1,0:T(8,128)(2,1)S(1)}, u32[]{:S(2)}, u32[]{:S(2)}) collective-permute-start(bf16[256,256]{1,0:T(8,128)(2,1)S(1)} %get-tuple-element.68), channel_id=1, source_target_pairs={{0,4},{4,0},{8,12},{12,8},{1,5},{5,1},{9,13},{13,9},{2,6},{6,2},{1... | collective-permute-start | bytes 393224 | tf_op jit(solution)/shard_map/cells_1_chunk_3/ppermute | solution.py:281
  35.4 14.0 %collective-permute-start.10 = (bf16[256,256]{1,0:T(8,128)(2,1)S(1)}, bf16[256,256]{1,0:T(8,128)(2,1)S(1)}, u32[]{:S(2)}, u32[]{:S(2)}) collective-permute-start(bf16[256,256]{1,0:T(8,128)(2,1)S(1)} %get-tuple-element.72), channel_id=1, source_target_pairs={{0,8},{4,12},{8,0},{12,4},{1,9},{5,13},{9,1},{13,5},{2,10},{6,14},... | collective-permute-start | bytes 393224 | tf_op jit(solution)/shard_map/cells_2_chunk_3/ppermute | solution.py:281
  38.3 14.6 %collective-permute-start.12 = (bf16[256,256]{1,0:T(8,128)(2,1)S(1)}, bf16[256,256]{1,0:T(8,128)(2,1)S(1)}, u32[]{:S(2)}, u32[]{:S(2)}) collective-permute-start(bf16[256,256]{1,0:T(8,128)(2,1)S(1)} %get-tuple-element.76), channel_id=1, source_target_pairs={{0,12},{4,8},{8,4},{12,0},{1,13},{5,9},{9,5},{13,1},{2,14},{6,10},... | collective-permute-start | bytes 393224 | tf_op jit(solution)/shard_map/cells_3_chunk_3/ppermute | solution.py:281
  41.7 19.4 %collective-permute-start.16 = (bf16[1024,256]{1,0:T(8,128)(2,1)S(1)}, bf16[1024,256]{1,0:T(8,128)(2,1)S(1)}, u32[]{:S(2)}, u32[]{:S(2)}) collective-permute-start(bf16[1024,256]{1,0:T(8,128)(2,1)S(1)} %get-tuple-element.88), channel_id=1, source_target_pairs={{0,2},{1,3},{2,0},{3,1},{4,6},{5,7},{6,4},{7,5},{8,10},{9,11},{10,... | collective-permute-start | bytes 1572872 | tf_op jit(solution)/shard_map/far_2/ppermute | solution.py:284
  54.1 16.6 %collective-permute-start.15 = (bf16[1024,1024]{1,0:T(8,128)(2,1)S(1)}, bf16[1024,1024]{1,0:T(8,128)(2,1)S(1)}, u32[]{:S(2)}, u32[]{:S(2)}) collective-permute-start(bf16[1024,1024]{1,0:T(8,128)(2,1)S(1)} %get-tuple-element.87.refs_0_), channel_id=1, source_target_pairs={{0,1},{1,0},{2,3},{3,2},{4,5},{5,4},{6,7},{7,6},{8,9},{9,8},{10,11... | collective-permute-start | bytes 6291464 | tf_op jit(solution)/shard_map/near/ppermute | solution.py:288
  56.4 24.4 %collective-permute-start.14 = (bf16[1024,256]{1,0:T(8,128)(2,1)S(1)}, bf16[1024,256]{1,0:T(8,128)(2,1)S(1)}, u32[]{:S(2)}, u32[]{:S(2)}) collective-permute-start(bf16[1024,256]{1,0:T(8,128)(2,1)S(1)} %get-tuple-element.86), channel_id=1, source_target_pairs={{0,2},{1,3},{2,0},{3,1},{4,6},{5,7},{6,4},{7,5},{8,10},{9,11},{10,... | collective-permute-start | bytes 1572872 | tf_op jit(solution)/shard_map/far_3/ppermute | solution.py:284
  61.1 9.5 %collective-permute-start.17 = (bf16[1024,256]{1,0:T(8,128)(2,1)S(1)}, bf16[1024,256]{1,0:T(8,128)(2,1)S(1)}, u32[]{:S(2)}, u32[]{:S(2)}) collective-permute-start(bf16[1024,256]{1,0:T(8,128)(2,1)S(1)} %collective-permute-done.13.refs_1_), channel_id=1, source_target_pairs={{0,1},{1,0},{2,3},{3,2},{4,5},{5,4},{6,7},{7,6},{8,9},{9,8},{10,11... | collective-permute-start | bytes 1572872 | tf_op jit(solution)/shard_map/far_near_0/ppermute | solution.py:288
  66.4 4.3 %collective-permute-start.18 = (bf16[1024,256]{1,0:T(8,128)(2,1)S(1)}, bf16[1024,256]{1,0:T(8,128)(2,1)S(1)}, u32[]{:S(2)}, u32[]{:S(2)}) collective-permute-start(bf16[1024,256]{1,0:T(8,128)(2,1)S(1)} %collective-permute-done.6.refs_2_), channel_id=1, source_target_pairs={{0,1},{1,0},{2,3},{3,2},{4,5},{5,4},{6,7},{7,6},{8,9},{9,8},{10,11... | collective-permute-start | bytes 1572872 | tf_op jit(solution)/shard_map/far_near_1/ppermute | solution.py:288
  66.4 4.3 %collective-permute-start.19 = (bf16[1024,256]{1,0:T(8,128)(2,1)S(1)}, bf16[1024,256]{1,0:T(8,128)(2,1)S(1)}, u32[]{:S(2)}, u32[]{:S(2)}) collective-permute-start(bf16[1024,256]{1,0:T(8,128)(2,1)S(1)} %collective-permute-done.16.refs_3_), channel_id=1, source_target_pairs={{0,1},{1,0},{2,3},{3,2},{4,5},{5,4},{6,7},{7,6},{8,9},{9,8},{10,11... | collective-permute-start | bytes 1572872 | tf_op jit(solution)/shard_map/far_near_2/ppermute | solution.py:288
  80.8 2.7 %collective-permute-start.20 = (bf16[1024,256]{1,0:T(8,128)(2,1)S(1)}, bf16[1024,256]{1,0:T(8,128)(2,1)S(1)}, u32[]{:S(2)}, u32[]{:S(2)}) collective-permute-start(bf16[1024,256]{1,0:T(8,128)(2,1)S(1)} %collective-permute-done.14.refs_0_), channel_id=1, source_target_pairs={{0,1},{1,0},{2,3},{3,2},{4,5},{5,4},{6,7},{7,6},{8,9},{9,8},{10,11... | collective-permute-start | bytes 1572872 | tf_op jit(solution)/shard_map/far_near_3/ppermute | solution.py:288

commit v8 on v7

--- a/solution.py
+++ b/solution.py
@@ -234,7 +234,7 @@
         arrays += panels
     joined = [array for panels, _ in groups if len(panels) > 1 for array in panels]
     widest = max(sum(array.shape[1] for array in panels) for panels, _ in groups)
-    strip = min(rows, 256)
+    strip = min(rows, 256 if widest > 512 else 1024)
     args = [count, left, *arrays]
     specs = [whole] * len(args)
     if before is not None:
@@ -311,20 +311,22 @@
 
     multiply = functools.partial(gram, blocks, cores, count, left)
     last = chunks - 1
+    late = max(last - 1, 1)
     near = side("near", own)
-    far_near = [
-        [side(f"far_near_{k}", p, own, *far[last - 1]) for p in far[k]] for k in range(last)
-    ]
-    out = multiply([([own], (0, 0, 0))], None, lengthy)
+    far_near = [[side(f"far_near_{k}", p, own) for p in far[k]] for k in range(late)]
+    out = multiply([([own], (0, 0, 0))], None, brief)
+    groups = [([far[k][d - 1] for k in range(last)], (d, 0, 0)) for d in range(1, chips)]
+    out = multiply(groups, out, lengthy)
     groups = [([near], (0, 1, 0))]
-    for flip, group in ((0, far), (1, far_near)):
-        for d in range(1, chips):
-            groups.append(([group[k][d - 1] for k in range(last)], (d, flip, 0)))
+    for d in range(1, chips):
+        groups.append(([far_near[k][d - 1] for k in range(late)], (d, 1, 0)))
     out = multiply(groups, out, brief)
-    far_near = [side(f"far_near_{last}", p, out) for p in far[last]]
+    far_near = [[side(f"far_near_{k}", p, out) for p in far[k]] for k in range(late, chunks)]
     edge = last * width
     out = multiply([([p], (d, 0, edge)) for d, p in enumerate(far[last], 1)], out, brief)
-    return multiply([([p], (d, 1, edge)) for d, p in enumerate(far_near, 1)], out, brief)
+    edge = late * width
+    groups = [([p[d - 1] for p in far_near], (d, 1, edge)) for d in range(1, chips)]
+    return multiply(groups, out, brief)
 
 
 def solution(mesh):

time: 86.6 us -> 81.5 us (0.941)
  the two profiles are of different devices: /device:TPU:9 before, /device:TPU:0 now
where the time goes in v8:
time: 81.5 us; the launch traced here: 81.2 us
  starting transfers between devices  30.2 us (37%)
  Pallas kernels  26.1 us (32%)
  waiting for transfers between devices  21.3 us (26%)
  local copies, waits for them, and re-layouts  3.27 us (4%)
    ppermute x12, starting transfers between devices, swap(): return lax.ppermute(block, 'cells', [(s, s ^ by) for s in range(types)])  25.6 us
    pallas_call x5, Pallas kernels, gram(): pl.pallas_call(functools.partial(gram_kernel, blocks, cores, strip, layou...  17.6 us
    ppermute x12, waiting for transfers between devices, swap(): return lax.ppermute(block, 'cells', [(s, s ^ by) for s in range(types)])  17.4 us
    pallas_call x4, Pallas kernels, standardize(): pl.pallas_call(functools.partial(standardize_kernel, types, cap, lead, se...  6.78 us
    ppermute x4, starting transfers between devices, across(): lax.ppermute(panel_, 'blk', [(b, (b + by * cores) % blocks) for b in rang...  3.44 us
    unnamed x8, local copies, waits for them, and re-layouts  3.27 us
    ppermute x4, waiting for transfers between devices, across(): lax.ppermute(panel_, 'blk', [(b, (b + by * cores) % blocks) for b in rang...  3.26 us
    pallas_call x1, Pallas kernels, pack(): pl.pallas_call(functools.partial(pack_kernel, types, cap, widths), out_sh...  1.71 us
  transfers between devices with their start and end apart: 21, of which 8 were waited for; matrix products, arithmetic and copies ran while one was open for 0% of the time, Pallas kernels for 27%

profile of v8, /device:TPU:0, one launch (start us, length us, event | category | flops | bytes accessed | tf_op | source)
XLA Modules:
  0.0 81.2 jit_solution(10252710301602733785)
XLA Ops:
  0.0 1.2 %copy-done = bf16[512,1024]{1,0:T(8,128)(2,1)S(1)} copy-done((bf16[512,1024]{1,0:T(8,128)(2,1)S(1)}, bf16[512,1024]{1,0:T(8,128)(2,1)}, u32[]{:S(2)}) %copy-start) | copy-done | bytes 1048600
  1.2 0.7 copy-done.1
  1.9 0.7 copy-done.2
  2.6 1.7 %pack.1 = (bf16[272,256]{1,0:T(8,128)(2,1)S(1)}, bf16[272,256]{1,0:T(8,128)(2,1)S(1)}, bf16[272,256]{1,0:T(8,128)(2,1)S(1)}, bf16[272,256]{1,0:T(8,128)(2,1)S(1)...) custom-call(s32[512]{0:T(512)S(1)} %copy-done.1, ...), custom_call_target="tpu_custom_call" | custom-call | flops 1024 | bytes 1024 | tf_op jit(solution)/shard_map/pack/pallas_call | solution.py:68
  4.3 5.1 %collective-permute-start.4 = (bf16[272,256]{1,0:T(8,128)(2,1)S(1)}, bf16[272,256]{1,0:T(8,128)(2,1)S(1)}, u32[]{:S(2)}, u32[]{:S(2)}) collective-permute-start(bf16[272,256]{1,0:T(8,128)(2,1)S(1)} %get-tuple-element.58), channel_id=1, source_target_pairs={{0,12},{4,8},{8,4},{12,0},{1,13},{5,9},{9,5},{13,1},{2,14},{6,10},... | collective-permute-start | bytes 417800 | tf_op jit(solution)/shard_map/cells_3_chunk_0/ppermute | solution.py:281
  9.4 0.0 collective-permute-start.2
  9.4 0.6 collective-permute-start
  10.1 4.0 %collective-permute-done.4.refs_3_.refs_7_ = bf16[272,256]{1,0:T(8,128)(2,1)S(1)} collective-permute-done((bf16[272,256]{1,0:T(8,128)(2,1)S(1)}, bf16[272,256]{1,0:T(8,128)(2,1)S(1)}, u32[]{:S(2)}, u32[]{:S(2)}) %collective-permute-start.4) | collective-permute-done | bytes 139296 | tf_op jit(solution)/shard_map/cells_3_chunk_0/ppermute | solution.py:281
  14.0 3.8 %collective-permute-start.5 = (bf16[256,256]{1,0:T(8,128)(2,1)S(1)}, bf16[256,256]{1,0:T(8,128)(2,1)S(1)}, u32[]{:S(2)}, u32[]{:S(2)}) collective-permute-start(bf16[256,256]{1,0:T(8,128)(2,1)S(1)} %get-tuple-element.59), channel_id=1, source_target_pairs={{0,12},{4,8},{8,4},{12,0},{1,13},{5,9},{9,5},{13,1},{2,14},{6,10},... | collective-permute-start | bytes 393224 | tf_op jit(solution)/shard_map/cells_3_chunk_1/ppermute | solution.py:281
  17.9 8.5 %collective-permute-done.2.refs_2_.refs_6_ = bf16[272,256]{1,0:T(8,128)(2,1)S(1)} collective-permute-done((bf16[272,256]{1,0:T(8,128)(2,1)S(1)}, bf16[272,256]{1,0:T(8,128)(2,1)S(1)}, u32[]{:S(2)}, u32[]{:S(2)}) %collective-permute-start.2) | collective-permute-done | bytes 139296 | tf_op jit(solution)/shard_map/cells_2_chunk_0/ppermute | solution.py:281
  26.4 0.0 collective-permute-done.refs_1_.refs_5_
  26.4 1.8 %collective-permute-start.1 = (bf16[256,256]{1,0:T(8,128)(2,1)S(1)}, bf16[256,256]{1,0:T(8,128)(2,1)S(1)}, u32[]{:S(2)}, u32[]{:S(2)}) collective-permute-start(bf16[256,256]{1,0:T(8,128)(2,1)S(1)} %get-tuple-element.53), channel_id=1, source_target_pairs={{0,4},{4,0},{8,12},{12,8},{1,5},{5,1},{9,13},{13,9},{2,6},{6,2},{1... | collective-permute-start | bytes 393224 | tf_op jit(solution)/shard_map/cells_1_chunk_1/ppermute | solution.py:281
  28.2 0.7 copy-done.3
  28.9 2.0 %standardize.4 = (bf16[1024,256]{1,0:T(8,128)(2,1)S(1)}, bf16[1024,1024]{1,0:T(8,128)(2,1)S(1)}, f32[8,128]{1,0:T(8,128)}, bf16[1024,1024]{1,0:T(8,128)(2,1)S(1)}) custom-call(f32[1,1024]{1,0:T(1,128)S(1)} %bitcast.1, bf16[272,256]{1,0:T(8,128)(2,1)S(1)} %get-tuple-element.60.refs_0_.refs_4_, bf16[272,256]{1,0:T(8,128)(2,1)S(1)} %collective-permute-done.refs_1_.refs_5_, ...), custom_call_target="tpu_custom_call" | custom-call | flops 20000000000 | bytes 1024 | tf_op jit(solution)/shard_map/standardize/pallas_call | solution.py:157
  30.9 1.6 %collective-permute-start.13 = (bf16[1024,256]{1,0:T(8,128)(2,1)S(1)}, bf16[1024,256]{1,0:T(8,128)(2,1)S(1)}, u32[]{:S(2)}, u32[]{:S(2)}) collective-permute-start(bf16[1024,256]{1,0:T(8,128)(2,1)S(1)} %get-tuple-element.78), channel_id=1, source_target_pairs={{0,2},{1,3},{2,0},{3,1},{4,6},{5,7},{6,4},{7,5},{8,10},{9,11},{10,... | collective-permute-start | bytes 1572872 | tf_op jit(solution)/shard_map/far_0/ppermute | solution.py:284
  32.5 0.0 collective-permute-done.5.refs_3_
  32.5 2.5 %collective-permute-start.11 = (bf16[256,256]{1,0:T(8,128)(2,1)S(1)}, bf16[256,256]{1,0:T(8,128)(2,1)S(1)}, u32[]{:S(2)}, u32[]{:S(2)}) collective-permute-start(bf16[256,256]{1,0:T(8,128)(2,1)S(1)} %get-tuple-element.75), channel_id=1, source_target_pairs={{0,12},{4,8},{8,4},{12,0},{1,13},{5,9},{9,5},{13,1},{2,14},{6,10},... | collective-permute-start | bytes 393224 | tf_op jit(solution)/shard_map/cells_3_chunk_2/ppermute | solution.py:281
  35.0 1.5 %collective-permute-done.3.refs_2_ = bf16[256,256]{1,0:T(8,128)(2,1)S(1)} collective-permute-done((bf16[256,256]{1,0:T(8,128)(2,1)S(1)}, bf16[256,256]{1,0:T(8,128)(2,1)S(1)}, u32[]{:S(2)}, u32[]{:S(2)}) %collective-permute-start.3) | collective-permute-done | bytes 131104 | tf_op jit(solution)/shard_map/cells_2_chunk_1/ppermute | solution.py:281
  36.5 2.9 %collective-permute-start.7 = (bf16[256,256]{1,0:T(8,128)(2,1)S(1)}, bf16[256,256]{1,0:T(8,128)(2,1)S(1)}, u32[]{:S(2)}, u32[]{:S(2)}) collective-permute-start(bf16[256,256]{1,0:T(8,128)(2,1)S(1)} %get-tuple-element.67), channel_id=1, source_target_pairs={{0,4},{4,0},{8,12},{12,8},{1,5},{5,1},{9,13},{13,9},{2,6},{6,2},{1... | collective-permute-start | bytes 393224 | tf_op jit(solution)/shard_map/cells_1_chunk_2/ppermute | solution.py:281
  39.5 1.8 %standardize.5 = (bf16[1024,256]{1,0:T(8,128)(2,1)S(1)}, bf16[1024,1024]{1,0:T(8,128)(2,1)S(1)}, f32[8,128]{1,0:T(8,128)}, bf16[1024,1024]{1,0:T(8,128)(2,1)S(1)}) custom-call(f32[1,1024]{1,0:T(1,128)S(1)} %bitcast.2, bf16[256,256]{1,0:T(8,128)(2,1)S(1)} %get-tuple-element.50.refs_0_, ...), custom_call_target="tpu_custom_call", output_to_operand_aliasing={{1}: (9, {}), {3}: (10, {})} | custom-call | flops 20000000000 | bytes 1024 | tf_op jit(solution)/shard_map/standardize/pallas_call | solution.py:157
  41.3 0.2 collective-permute-start.6
  41.4 0.0 collective-permute-done.11.refs_3_
  41.4 2.9 %collective-permute-start.12 = (bf16[256,256]{1,0:T(8,128)(2,1)S(1)}, bf16[256,256]{1,0:T(8,128)(2,1)S(1)}, u32[]{:S(2)}, u32[]{:S(2)}) collective-permute-start(bf16[256,256]{1,0:T(8,128)(2,1)S(1)} %get-tuple-element.76), channel_id=1, source_target_pairs={{0,12},{4,8},{8,4},{12,0},{1,13},{5,9},{9,5},{13,1},{2,14},{6,10},... | collective-permute-start | bytes 393224 | tf_op jit(solution)/shard_map/cells_3_chunk_3/ppermute | solution.py:281
  44.3 2.0 %collective-permute-done.9.refs_2_ = bf16[256,256]{1,0:T(8,128)(2,1)S(1)} collective-permute-done((bf16[256,256]{1,0:T(8,128)(2,1)S(1)}, bf16[256,256]{1,0:T(8,128)(2,1)S(1)}, u32[]{:S(2)}, u32[]{:S(2)}) %collective-permute-start.9) | collective-permute-done | bytes 131104 | tf_op jit(solution)/shard_map/cells_2_chunk_2/ppermute | solution.py:281
  46.3 0.0 collective-permute-start.10
  46.4 0.0 collective-permute-done.7.refs_1_
  46.4 5.8 %collective-permute-start.8 = (bf16[256,256]{1,0:T(8,128)(2,1)S(1)}, bf16[256,256]{1,0:T(8,128)(2,1)S(1)}, u32[]{:S(2)}, u32[]{:S(2)}) collective-permute-start(bf16[256,256]{1,0:T(8,128)(2,1)S(1)} %get-tuple-element.68), channel_id=1, source_target_pairs={{0,4},{4,0},{8,12},{12,8},{1,5},{5,1},{9,13},{13,9},{2,6},{6,2},{1... | collective-permute-start | bytes 393224 | tf_op jit(solution)/shard_map/cells_1_chunk_3/ppermute | solution.py:281
  52.1 0.0 collective-permute-done.13.refs_0_
  52.1 1.8 %standardize.6 = (bf16[1024,256]{1,0:T(8,128)(2,1)S(1)}, bf16[1024,1024]{1,0:T(8,128)(2,1)S(1)}, f32[8,128]{1,0:T(8,128)}, bf16[1024,1024]{1,0:T(8,128)(2,1)S(1)}) custom-call(f32[1,1024]{1,0:T(1,128)S(1)} %bitcast.3, bf16[256,256]{1,0:T(8,128)(2,1)S(1)} %get-tuple-element.79.refs_0_, ...), custom_call_target="tpu_custom_call", output_to_operand_aliasing={{1}: (9, {}), {3}: (10, {})} | custom-call | flops 20000000000 | bytes 1024 | tf_op jit(solution)/shard_map/standardize/pallas_call | solution.py:157
  54.0 0.1 collective-permute-start.14
  54.0 0.0 collective-permute-done.6.refs_1_
  54.1 1.0 %collective-permute-done.10.refs_2_ = bf16[256,256]{1,0:T(8,128)(2,1)S(1)} collective-permute-done((bf16[256,256]{1,0:T(8,128)(2,1)S(1)}, bf16[256,256]{1,0:T(8,128)(2,1)S(1)}, u32[]{:S(2)}, u32[]{:S(2)}) %collective-permute-start.10) | collective-permute-done | bytes 131104 | tf_op jit(solution)/shard_map/cells_2_chunk_3/ppermute | solution.py:281
  55.1 0.4 collective-permute-done.8.refs_1_
  55.4 1.2 %standardize.7 = (bf16[1024,256]{1,0:T(8,128)(2,1)S(1)}, bf16[1024,1024]{1,0:T(8,128)(2,1)S(1)}, f32[8,128]{1,0:T(8,128)S(1)}, bf16[1024,1024]{1,0:T(8,128)(2,1)S(1)}) custom-call(f32[1,1024]{1,0:T(1,128)S(1)} %bitcast.4, bf16[256,256]{1,0:T(8,128)(2,1)S(1)} %get-tuple-element.64.refs_0_, ...), custom_call_target="tpu_custom_call", output_to_operand_aliasing={{1}: (9, {}), {3}: (10, {})} | custom-call | flops 20000000000 | bytes 1024 | tf_op jit(solution)/shard_map/standardize/pallas_call | solution.py:157
  56.6 0.1 collective-permute-start.15
  56.7 0.5 collective-permute-start.17
  57.2 0.1 collective-permute-start.16
  57.3 1.6 %collective-permute-start.19 = (bf16[1024,256]{1,0:T(8,128)(2,1)S(1)}, bf16[1024,256]{1,0:T(8,128)(2,1)S(1)}, u32[]{:S(2)}, u32[]{:S(2)}) collective-permute-start(bf16[1024,256]{1,0:T(8,128)(2,1)S(1)} %get-tuple-element.91), channel_id=1, source_target_pairs={{0,2},{1,3},{2,0},{3,1},{4,6},{5,7},{6,4},{7,5},{8,10},{9,11},{10,... | collective-permute-start | bytes 1572872 | tf_op jit(solution)/shard_map/far_3/ppermute | solution.py:284
  58.9 3.8 %gram.5.refs_3_ = bf16[1,1024,4096]{2,1,0:T(8,128)(2,1)} custom-call(f32[8,128]{1,0:T(8,128)S(1)} %get-tuple-element.84.count_ref, bf16[1024,1024]{1,0:T(8,128)(2,1)S(1)} %get-tuple-element.85.left_ref, bf16[1024,1024]{1,0:T(8,128)(2,1)S(1)} %get-tuple-element.87.refs_0_), custom_call_target="tpu_custom_call" | custom-call | flops 1024 | bytes 1024 | tf_op jit(solution)/shard_map/gram/pallas_call | solution.py:243
  62.7 3.3 %collective-permute-done.14.refs_2_ = bf16[1024,256]{1,0:T(8,128)(2,1)S(1)} collective-permute-done((bf16[1024,256]{1,0:T(8,128)(2,1)S(1)}, bf16[1024,256]{1,0:T(8,128)(2,1)S(1)}, u32[]{:S(2)}, u32[]{:S(2)}) %collective-permute-start.14) | collective-permute-done | bytes 524320 | tf_op jit(solution)/shard_map/far_2/ppermute | solution.py:284
  66.0 3.8 %gram.6.refs_3_ = bf16[1,1024,4096]{2,1,0:T(8,128)(2,1)} custom-call(f32[8,128]{1,0:T(8,128)S(1)} %get-tuple-element.84.count_ref, bf16[1024,1024]{1,0:T(8,128)(2,1)S(1)} %get-tuple-element.85.left_ref, bf16[1024,256]{1,0:T(8,128)(2,1)S(1)} %collective-permute-done.13.refs_0_, ...), custom_call_target="tpu_custom_call", output_to_operand_aliasing={{}: (5, {})} | custom-call | flops 20000000000 | bytes 1024 | tf_op jit(solution)/shard_map/gram/pallas_call | solution.py:243
  69.8 0.0 collective-permute-done.16.refs_1_
  69.8 6.1 %gram.7.refs_1_ = bf16[1,1024,4096]{2,1,0:T(8,128)(2,1)} custom-call(f32[8,128]{1,0:T(8,128)S(1)} %get-tuple-element.84.count_ref, bf16[1024,1024]{1,0:T(8,128)(2,1)S(1)} %get-tuple-element.85.left_ref, bf16[1024,1024]{1,0:T(8,128)(2,1)S(1)} %collective-permute-done.15.refs_0_, ...), custom_call_target="tpu_custom_call", output_to_operand_aliasing={{}: (5, {})} | custom-call | flops 1024 | bytes 1024 | tf_op jit(solution)/shard_map/gram/pallas_call | solution.py:243
  76.0 0.1 collective-permute-start.20
  76.1 0.5 collective-permute-start.18
  76.6 1.5 %gram.8.refs_2_ = bf16[1,1024,4096]{2,1,0:T(8,128)(2,1)} custom-call(f32[8,128]{1,0:T(8,128)S(1)} %get-tuple-element.84.count_ref, bf16[1024,1024]{1,0:T(8,128)(2,1)S(1)} %get-tuple-element.85.left_ref, bf16[1024,256]{1,0:T(8,128)(2,1)S(1)} %collective-permute-done.19.refs_0_, bf16[1,1024,4096]{2,1,0:T(8,128)(2,1)} %gram.7.refs_1_), custom_call_target="tpu_custom_call", output_to_operand_aliasing={{}: (3, {})} | custom-call | flops 1024 | bytes 1024 | tf_op jit(solution)/shard_map/gram/pallas_call | solution.py:243
  78.1 0.6 collective-permute-done.18.refs_0_
  78.7 2.4 %gram.9 = bf16[1,1024,4096]{2,1,0:T(8,128)(2,1)} custom-call(f32[8,128]{1,0:T(8,128)S(1)} %get-tuple-element.84.count_ref, bf16[1024,1024]{1,0:T(8,128)(2,1)S(1)} %get-tuple-element.85.left_ref, bf16[1024,256]{1,0:T(8,128)(2,1)S(1)} %collective-permute-done.18.refs_0_, ...), custom_call_target="tpu_custom_call", output_to_operand_aliasing={{}: (4, {})} | custom-call | flops 1024 | bytes 1024 | tf_op jit(solution)/shard_map/gram/pallas_call | solution.py:243
  (12 shorter events, 0.0 us)
Async XLA Ops:
  0.0 1.2 %copy-start = (bf16[512,1024]{1,0:T(8,128)(2,1)S(1)}, bf16[512,1024]{1,0:T(8,128)(2,1)}, u32[]{:S(2)}) copy-start(bf16[512,1024]{1,0:T(8,128)(2,1)} %expr_ref.1) | copy-start | bytes 3145732
  1.2 0.7 copy-start.1
  1.9 0.7 copy-start.2
  4.3 9.7 %collective-permute-start.4 = (bf16[272,256]{1,0:T(8,128)(2,1)S(1)}, bf16[272,256]{1,0:T(8,128)(2,1)S(1)}, u32[]{:S(2)}, u32[]{:S(2)}) collective-permute-start(bf16[272,256]{1,0:T(8,128)(2,1)S(1)} %get-tuple-element.58), channel_id=1, source_target_pairs={{0,12},{4,8},{8,4},{12,0},{1,13},{5,9},{9,5},{13,1},{2,14},{6,10},... | collective-permute-start | bytes 417800 | tf_op jit(solution)/shard_map/cells_3_chunk_0/ppermute | solution.py:281
  9.4 17.0 %collective-permute-start.2 = (bf16[272,256]{1,0:T(8,128)(2,1)S(1)}, bf16[272,256]{1,0:T(8,128)(2,1)S(1)}, u32[]{:S(2)}, u32[]{:S(2)}) collective-permute-start(bf16[272,256]{1,0:T(8,128)(2,1)S(1)} %get-tuple-element.55), channel_id=1, source_target_pairs={{0,8},{4,12},{8,0},{12,4},{1,9},{5,13},{9,1},{13,5},{2,10},{6,14},... | collective-permute-start | bytes 417800 | tf_op jit(solution)/shard_map/cells_2_chunk_0/ppermute | solution.py:281
  9.4 17.0 %collective-permute-start = (bf16[272,256]{1,0:T(8,128)(2,1)S(1)}, bf16[272,256]{1,0:T(8,128)(2,1)S(1)}, u32[]{:S(2)}, u32[]{:S(2)}) collective-permute-start(bf16[272,256]{1,0:T(8,128)(2,1)S(1)} %get-tuple-element.52), channel_id=1, source_target_pairs={{0,4},{4,0},{8,12},{12,8},{1,5},{5,1},{9,13},{13,9},{2,6},{6,2},{1... | collective-permute-start | bytes 417800 | tf_op jit(solution)/shard_map/cells_1_chunk_0/ppermute | solution.py:281
  14.0 18.4 %collective-permute-start.5 = (bf16[256,256]{1,0:T(8,128)(2,1)S(1)}, bf16[256,256]{1,0:T(8,128)(2,1)S(1)}, u32[]{:S(2)}, u32[]{:S(2)}) collective-permute-start(bf16[256,256]{1,0:T(8,128)(2,1)S(1)} %get-tuple-element.59), channel_id=1, source_target_pairs={{0,12},{4,8},{8,4},{12,0},{1,13},{5,9},{9,5},{13,1},{2,14},{6,10},... | collective-permute-start | bytes 393224 | tf_op jit(solution)/shard_map/cells_3_chunk_1/ppermute | solution.py:281
  26.4 10.1 %collective-permute-start.3 = (bf16[256,256]{1,0:T(8,128)(2,1)S(1)}, bf16[256,256]{1,0:T(8,128)(2,1)S(1)}, u32[]{:S(2)}, u32[]{:S(2)}) collective-permute-start(bf16[256,256]{1,0:T(8,128)(2,1)S(1)} %get-tuple-element.56), channel_id=1, source_target_pairs={{0,8},{4,12},{8,0},{12,4},{1,9},{5,13},{9,1},{13,5},{2,10},{6,14},... | collective-permute-start | bytes 393224 | tf_op jit(solution)/shard_map/cells_2_chunk_1/ppermute | solution.py:281
  26.4 10.1 %collective-permute-start.1 = (bf16[256,256]{1,0:T(8,128)(2,1)S(1)}, bf16[256,256]{1,0:T(8,128)(2,1)S(1)}, u32[]{:S(2)}, u32[]{:S(2)}) collective-permute-start(bf16[256,256]{1,0:T(8,128)(2,1)S(1)} %get-tuple-element.53), channel_id=1, source_target_pairs={{0,4},{4,0},{8,12},{12,8},{1,5},{5,1},{9,13},{13,9},{2,6},{6,2},{1... | collective-permute-start | bytes 393224 | tf_op jit(solution)/shard_map/cells_1_chunk_1/ppermute | solution.py:281
  28.2 0.7 copy-start.3
  30.9 21.3 %collective-permute-start.13 = (bf16[1024,256]{1,0:T(8,128)(2,1)S(1)}, bf16[1024,256]{1,0:T(8,128)(2,1)S(1)}, u32[]{:S(2)}, u32[]{:S(2)}) collective-permute-start(bf16[1024,256]{1,0:T(8,128)(2,1)S(1)} %get-tuple-element.78), channel_id=1, source_target_pairs={{0,2},{1,3},{2,0},{3,1},{4,6},{5,7},{6,4},{7,5},{8,10},{9,11},{10,... | collective-permute-start | bytes 1572872 | tf_op jit(solution)/shard_map/far_0/ppermute | solution.py:284
  32.5 9.0 %collective-permute-start.11 = (bf16[256,256]{1,0:T(8,128)(2,1)S(1)}, bf16[256,256]{1,0:T(8,128)(2,1)S(1)}, u32[]{:S(2)}, u32[]{:S(2)}) collective-permute-start(bf16[256,256]{1,0:T(8,128)(2,1)S(1)} %get-tuple-element.75), channel_id=1, source_target_pairs={{0,12},{4,8},{8,4},{12,0},{1,13},{5,9},{9,5},{13,1},{2,14},{6,10},... | collective-permute-start | bytes 393224 | tf_op jit(solution)/shard_map/cells_3_chunk_2/ppermute | solution.py:281
  36.5 9.8 %collective-permute-start.9 = (bf16[256,256]{1,0:T(8,128)(2,1)S(1)}, bf16[256,256]{1,0:T(8,128)(2,1)S(1)}, u32[]{:S(2)}, u32[]{:S(2)}) collective-permute-start(bf16[256,256]{1,0:T(8,128)(2,1)S(1)} %get-tuple-element.71), channel_id=1, source_target_pairs={{0,8},{4,12},{8,0},{12,4},{1,9},{5,13},{9,1},{13,5},{2,10},{6,14},... | collective-permute-start | bytes 393224 | tf_op jit(solution)/shard_map/cells_2_chunk_2/ppermute | solution.py:281
  36.5 9.8 %collective-permute-start.7 = (bf16[256,256]{1,0:T(8,128)(2,1)S(1)}, bf16[256,256]{1,0:T(8,128)(2,1)S(1)}, u32[]{:S(2)}, u32[]{:S(2)}) collective-permute-start(bf16[256,256]{1,0:T(8,128)(2,1)S(1)} %get-tuple-element.67), channel_id=1, source_target_pairs={{0,4},{4,0},{8,12},{12,8},{1,5},{5,1},{9,13},{13,9},{2,6},{6,2},{1... | collective-permute-start | bytes 393224 | tf_op jit(solution)/shard_map/cells_1_chunk_2/ppermute | solution.py:281
  41.3 12.8 %collective-permute-start.6 = (bf16[1024,256]{1,0:T(8,128)(2,1)S(1)}, bf16[1024,256]{1,0:T(8,128)(2,1)S(1)}, u32[]{:S(2)}, u32[]{:S(2)}) collective-permute-start(bf16[1024,256]{1,0:T(8,128)(2,1)S(1)} %get-tuple-element.63), channel_id=1, source_target_pairs={{0,2},{1,3},{2,0},{3,1},{4,6},{5,7},{6,4},{7,5},{8,10},{9,11},{10,... | collective-permute-start | bytes 1572872 | tf_op jit(solution)/shard_map/far_1/ppermute | solution.py:284
  41.4 12.6 %collective-permute-start.12 = (bf16[256,256]{1,0:T(8,128)(2,1)S(1)}, bf16[256,256]{1,0:T(8,128)(2,1)S(1)}, u32[]{:S(2)}, u32[]{:S(2)}) collective-permute-start(bf16[256,256]{1,0:T(8,128)(2,1)S(1)} %get-tuple-element.76), channel_id=1, source_target_pairs={{0,12},{4,8},{8,4},{12,0},{1,13},{5,9},{9,5},{13,1},{2,14},{6,10},... | collective-permute-start | bytes 393224 | tf_op jit(solution)/shard_map/cells_3_chunk_3/ppermute | solution.py:281
  46.3 8.7 %collective-permute-start.10 = (bf16[256,256]{1,0:T(8,128)(2,1)S(1)}, bf16[256,256]{1,0:T(8,128)(2,1)S(1)}, u32[]{:S(2)}, u32[]{:S(2)}) collective-permute-start(bf16[256,256]{1,0:T(8,128)(2,1)S(1)} %get-tuple-element.72), channel_id=1, source_target_pairs={{0,8},{4,12},{8,0},{12,4},{1,9},{5,13},{9,1},{13,5},{2,10},{6,14},... | collective-permute-start | bytes 393224 | tf_op jit(solution)/shard_map/cells_2_chunk_3/ppermute | solution.py:281
  46.4 9.1 %collective-permute-start.8 = (bf16[256,256]{1,0:T(8,128)(2,1)S(1)}, bf16[256,256]{1,0:T(8,128)(2,1)S(1)}, u32[]{:S(2)}, u32[]{:S(2)}) collective-permute-start(bf16[256,256]{1,0:T(8,128)(2,1)S(1)} %get-tuple-element.68), channel_id=1, source_target_pairs={{0,4},{4,0},{8,12},{12,8},{1,5},{5,1},{9,13},{13,9},{2,6},{6,2},{1... | collective-permute-start | bytes 393224 | tf_op jit(solution)/shard_map/cells_1_chunk_3/ppermute | solution.py:281
  54.0 12.0 %collective-permute-start.14 = (bf16[1024,256]{1,0:T(8,128)(2,1)S(1)}, bf16[1024,256]{1,0:T(8,128)(2,1)S(1)}, u32[]{:S(2)}, u32[]{:S(2)}) collective-permute-start(bf16[1024,256]{1,0:T(8,128)(2,1)S(1)} %get-tuple-element.86), channel_id=1, source_target_pairs={{0,2},{1,3},{2,0},{3,1},{4,6},{5,7},{6,4},{7,5},{8,10},{9,11},{10,... | collective-permute-start | bytes 1572872 | tf_op jit(solution)/shard_map/far_2/ppermute | solution.py:284
  56.6 13.2 %collective-permute-start.15 = (bf16[1024,1024]{1,0:T(8,128)(2,1)S(1)}, bf16[1024,1024]{1,0:T(8,128)(2,1)S(1)}, u32[]{:S(2)}, u32[]{:S(2)}) collective-permute-start(bf16[1024,1024]{1,0:T(8,128)(2,1)S(1)} %get-tuple-element.87.refs_0_), channel_id=1, source_target_pairs={{0,1},{1,0},{2,3},{3,2},{4,5},{5,4},{6,7},{7,6},{8,9},{9,8},{10,11... | collective-permute-start | bytes 6291464 | tf_op jit(solution)/shard_map/near/ppermute | solution.py:288
  56.7 13.1 %collective-permute-start.17 = (bf16[1024,256]{1,0:T(8,128)(2,1)S(1)}, bf16[1024,256]{1,0:T(8,128)(2,1)S(1)}, u32[]{:S(2)}, u32[]{:S(2)}) collective-permute-start(bf16[1024,256]{1,0:T(8,128)(2,1)S(1)} %collective-permute-done.6.refs_1_), channel_id=1, source_target_pairs={{0,1},{1,0},{2,3},{3,2},{4,5},{5,4},{6,7},{7,6},{8,9},{9,8},{10,11... | collective-permute-start | bytes 1572872 | tf_op jit(solution)/shard_map/far_near_1/ppermute | solution.py:288
  57.2 12.6 %collective-permute-start.16 = (bf16[1024,256]{1,0:T(8,128)(2,1)S(1)}, bf16[1024,256]{1,0:T(8,128)(2,1)S(1)}, u32[]{:S(2)}, u32[]{:S(2)}) collective-permute-start(bf16[1024,256]{1,0:T(8,128)(2,1)S(1)} %collective-permute-done.13.refs_0_), channel_id=1, source_target_pairs={{0,1},{1,0},{2,3},{3,2},{4,5},{5,4},{6,7},{7,6},{8,9},{9,8},{10,11... | collective-permute-start | bytes 1572872 | tf_op jit(solution)/shard_map/far_near_0/ppermute | solution.py:288
  57.3 18.7 %collective-permute-start.19 = (bf16[1024,256]{1,0:T(8,128)(2,1)S(1)}, bf16[1024,256]{1,0:T(8,128)(2,1)S(1)}, u32[]{:S(2)}, u32[]{:S(2)}) collective-permute-start(bf16[1024,256]{1,0:T(8,128)(2,1)S(1)} %get-tuple-element.91), channel_id=1, source_target_pairs={{0,2},{1,3},{2,0},{3,1},{4,6},{5,7},{6,4},{7,5},{8,10},{9,11},{10,... | collective-permute-start | bytes 1572872 | tf_op jit(solution)/shard_map/far_3/ppermute | solution.py:284
  76.0 2.1 %collective-permute-start.20 = (bf16[1024,256]{1,0:T(8,128)(2,1)S(1)}, bf16[1024,256]{1,0:T(8,128)(2,1)S(1)}, u32[]{:S(2)}, u32[]{:S(2)}) collective-permute-start(bf16[1024,256]{1,0:T(8,128)(2,1)S(1)} %collective-permute-done.19.refs_0_), channel_id=1, source_target_pairs={{0,1},{1,0},{2,3},{3,2},{4,5},{5,4},{6,7},{7,6},{8,9},{9,8},{10,11... | collective-permute-start | bytes 1572872 | tf_op jit(solution)/shard_map/far_near_3/ppermute | solution.py:288
  76.1 2.6 %collective-permute-start.18 = (bf16[1024,256]{1,0:T(8,128)(2,1)S(1)}, bf16[1024,256]{1,0:T(8,128)(2,1)S(1)}, u32[]{:S(2)}, u32[]{:S(2)}) collective-permute-start(bf16[1024,256]{1,0:T(8,128)(2,1)S(1)} %collective-permute-done.14.refs_2_), channel_id=1, source_target_pairs={{0,1},{1,0},{2,3},{3,2},{4,5},{5,4},{6,7},{7,6},{8,9},{9,8},{10,11... | collective-permute-start | bytes 1572872 | tf_op jit(solution)/shard_map/far_near_2/ppermute | solution.py:288

commit v9 on v8

--- a/solution.py
+++ b/solution.py
@@ -234,7 +234,7 @@
         arrays += panels
     joined = [array for panels, _ in groups if len(panels) > 1 for array in panels]
     widest = max(sum(array.shape[1] for array in panels) for panels, _ in groups)
-    strip = min(rows, 256 if widest > 512 else 1024)
+    strip = min(rows, 512 if widest > 512 else 1024)
     args = [count, left, *arrays]
     specs = [whole] * len(args)
     if before is not None:
@@ -288,16 +288,16 @@
             return lax.ppermute(after(panel_, *waits), "blk", [(b, b ^ 1) for b in range(blocks)])
 
     mean = gene_mean.reshape(1, panel)
-    order = sorted(range(1, types), key=lambda j: (j == 1, j))
+    order = sorted(range(1, types), key=lambda j: (j == 2, j == 1, -j))
     left, own, far, before = None, None, [], None
     for k in range(chunks):
-        arrived = [packed[k][0]] + [None] * (types - 1)
+        arrived = [packed[k][0]]
         for j in order:
             block = packed[k][j]
             if k:
-                block = after(block, before[j])
+                block = after(block, before[len(arrived)])
             with jax.named_scope(f"cells_{j}_chunk_{k}"):
-                arrived[j] = swap(block, j)
+                arrived.append(swap(block, j))
         before = list(arrived)
         if k >= 2:
             arrived[0] = after(arrived[0], *far[k - 2])

time: 81.5 us -> 81.1 us (level)
  the two profiles are of different devices: /device:TPU:0 before, /device:TPU:13 now
where the time goes in v9:
time: 81.1 us; the launch traced here: 80.9 us
  starting transfers between devices  28.2 us (35%)
  waiting for transfers between devices  25.6 us (32%)
  Pallas kernels  23.6 us (29%)
  local copies, waits for them, and re-layouts  3.27 us (4%)
    ppermute x12, waiting for transfers between devices, swap(): return lax.ppermute(block, 'cells', [(s, s ^ by) for s in range(types)])  20.4 us
    ppermute x12, starting transfers between devices, swap(): return lax.ppermute(block, 'cells', [(s, s ^ by) for s in range(types)])  17.6 us
    pallas_call x5, Pallas kernels, gram(): pl.pallas_call(functools.partial(gram_kernel, blocks, cores, strip, layou...  15.1 us
    pallas_call x4, Pallas kernels, standardize(): pl.pallas_call(functools.partial(standardize_kernel, types, cap, lead, se...  6.78 us
    ppermute x5, starting transfers between devices, side(): lax.ppermute(after(panel_, *waits), 'blk', [(b, b ^ 1) for b in range(blo...  5.96 us
    ppermute x4, starting transfers between devices, across(): lax.ppermute(panel_, 'blk', [(b, (b + by * cores) % blocks) for b in rang...  4.63 us
    ppermute x4, waiting for transfers between devices, across(): lax.ppermute(panel_, 'blk', [(b, (b + by * cores) % blocks) for b in rang...  4.43 us
    unnamed x8, local copies, waits for them, and re-layouts  3.27 us
  transfers between devices with their start and end apart: 21, of which 9 were waited for; matrix products, arithmetic and copies ran while one was open for 0% of the time, Pallas kernels for 24%

profile of v9, /device:TPU:13, one launch (start us, length us, event | category | flops | bytes accessed | tf_op | source)
XLA Modules:
  0.0 80.9 jit_solution(10124015691607869254)
XLA Ops:
  0.0 1.2 %copy-done = bf16[512,1024]{1,0:T(8,128)(2,1)S(1)} copy-done((bf16[512,1024]{1,0:T(8,128)(2,1)S(1)}, bf16[512,1024]{1,0:T(8,128)(2,1)}, u32[]{:S(2)}) %copy-start) | copy-done | bytes 1048600
  1.2 0.7 copy-done.1
  1.9 0.7 copy-done.2
  2.6 1.7 %pack.1 = (bf16[272,256]{1,0:T(8,128)(2,1)S(1)}, bf16[272,256]{1,0:T(8,128)(2,1)S(1)}, bf16[272,256]{1,0:T(8,128)(2,1)S(1)}, bf16[272,256]{1,0:T(8,128)(2,1)S(1)...) custom-call(s32[512]{0:T(512)S(1)} %copy-done.1, ...), custom_call_target="tpu_custom_call" | custom-call | flops 1024 | bytes 1024 | tf_op jit(solution)/shard_map/pack/pallas_call | solution.py:68
  4.3 2.4 %collective-permute-start.4 = (bf16[272,256]{1,0:T(8,128)(2,1)S(1)}, bf16[272,256]{1,0:T(8,128)(2,1)S(1)}, u32[]{:S(2)}, u32[]{:S(2)}) collective-permute-start(bf16[272,256]{1,0:T(8,128)(2,1)S(1)} %get-tuple-element.58), channel_id=1, source_target_pairs={{0,8},{4,12},{8,0},{12,4},{1,9},{5,13},{9,1},{13,5},{2,10},{6,14},... | collective-permute-start | bytes 417800 | tf_op jit(solution)/shard_map/cells_2_chunk_0/ppermute | solution.py:281
  6.7 0.2 collective-permute-start.2
  6.8 0.2 collective-permute-start
  7.0 6.4 %collective-permute-done.4.refs_3_.refs_7_ = bf16[272,256]{1,0:T(8,128)(2,1)S(1)} collective-permute-done((bf16[272,256]{1,0:T(8,128)(2,1)S(1)}, bf16[272,256]{1,0:T(8,128)(2,1)S(1)}, u32[]{:S(2)}, u32[]{:S(2)}) %collective-permute-start.4) | collective-permute-done | bytes 139296 | tf_op jit(solution)/shard_map/cells_2_chunk_0/ppermute | solution.py:281
  13.5 3.6 %collective-permute-start.5 = (bf16[256,256]{1,0:T(8,128)(2,1)S(1)}, bf16[256,256]{1,0:T(8,128)(2,1)S(1)}, u32[]{:S(2)}, u32[]{:S(2)}) collective-permute-start(bf16[256,256]{1,0:T(8,128)(2,1)S(1)} %get-tuple-element.59), channel_id=1, source_target_pairs={{0,8},{4,12},{8,0},{12,4},{1,9},{5,13},{9,1},{13,5},{2,10},{6,14},... | collective-permute-start | bytes 393224 | tf_op jit(solution)/shard_map/cells_2_chunk_1/ppermute | solution.py:281
  17.1 5.5 %collective-permute-done.refs_1_.refs_5_ = bf16[272,256]{1,0:T(8,128)(2,1)S(1)} collective-permute-done((bf16[272,256]{1,0:T(8,128)(2,1)S(1)}, bf16[272,256]{1,0:T(8,128)(2,1)S(1)}, u32[]{:S(2)}, u32[]{:S(2)}) %collective-permute-start) | collective-permute-done | bytes 139296 | tf_op jit(solution)/shard_map/cells_3_chunk_0/ppermute | solution.py:281
  22.6 2.7 %collective-permute-start.1 = (bf16[256,256]{1,0:T(8,128)(2,1)S(1)}, bf16[256,256]{1,0:T(8,128)(2,1)S(1)}, u32[]{:S(2)}, u32[]{:S(2)}) collective-permute-start(bf16[256,256]{1,0:T(8,128)(2,1)S(1)} %get-tuple-element.53), channel_id=1, source_target_pairs={{0,12},{4,8},{8,4},{12,0},{1,13},{5,9},{9,5},{13,1},{2,14},{6,10},... | collective-permute-start | bytes 393224 | tf_op jit(solution)/shard_map/cells_3_chunk_1/ppermute | solution.py:281
  25.3 0.7 copy-done.3
  26.0 2.0 %standardize.4 = (bf16[1024,256]{1,0:T(8,128)(2,1)S(1)}, bf16[1024,1024]{1,0:T(8,128)(2,1)S(1)}, f32[8,128]{1,0:T(8,128)}, bf16[1024,1024]{1,0:T(8,128)(2,1)S(1)}) custom-call(f32[1,1024]{1,0:T(1,128)S(1)} %bitcast.1, bf16[272,256]{1,0:T(8,128)(2,1)S(1)} %get-tuple-element.60.refs_0_.refs_4_, bf16[272,256]{1,0:T(8,128)(2,1)S(1)} %collective-permute-done.refs_1_.refs_5_, ...), custom_call_target="tpu_custom_call" | custom-call | flops 20000000000 | bytes 1024 | tf_op jit(solution)/shard_map/standardize/pallas_call | solution.py:157
  28.0 1.3 %collective-permute-start.13 = (bf16[1024,256]{1,0:T(8,128)(2,1)S(1)}, bf16[1024,256]{1,0:T(8,128)(2,1)S(1)}, u32[]{:S(2)}, u32[]{:S(2)}) collective-permute-start(bf16[1024,256]{1,0:T(8,128)(2,1)S(1)} %get-tuple-element.78), channel_id=1, source_target_pairs={{0,2},{1,3},{2,0},{3,1},{4,6},{5,7},{6,4},{7,5},{8,10},{9,11},{10,... | collective-permute-start | bytes 1572872 | tf_op jit(solution)/shard_map/far_0/ppermute | solution.py:284
  29.3 0.0 collective-permute-done.5.refs_3_
  29.3 1.2 %collective-permute-start.11 = (bf16[256,256]{1,0:T(8,128)(2,1)S(1)}, bf16[256,256]{1,0:T(8,128)(2,1)S(1)}, u32[]{:S(2)}, u32[]{:S(2)}) collective-permute-start(bf16[256,256]{1,0:T(8,128)(2,1)S(1)} %get-tuple-element.75), channel_id=1, source_target_pairs={{0,8},{4,12},{8,0},{12,4},{1,9},{5,13},{9,1},{13,5},{2,10},{6,14},... | collective-permute-start | bytes 393224 | tf_op jit(solution)/shard_map/cells_2_chunk_2/ppermute | solution.py:281
  30.4 0.0 collective-permute-done.3.refs_2_
  30.4 0.0 collective-permute-start.9
  30.5 1.5 %collective-permute-start.7 = (bf16[256,256]{1,0:T(8,128)(2,1)S(1)}, bf16[256,256]{1,0:T(8,128)(2,1)S(1)}, u32[]{:S(2)}, u32[]{:S(2)}) collective-permute-start(bf16[256,256]{1,0:T(8,128)(2,1)S(1)} %get-tuple-element.67), channel_id=1, source_target_pairs={{0,12},{4,8},{8,4},{12,0},{1,13},{5,9},{9,5},{13,1},{2,14},{6,10},... | collective-permute-start | bytes 393224 | tf_op jit(solution)/shard_map/cells_3_chunk_2/ppermute | solution.py:281
  31.9 1.8 %standardize.5 = (bf16[1024,256]{1,0:T(8,128)(2,1)S(1)}, bf16[1024,1024]{1,0:T(8,128)(2,1)S(1)}, f32[8,128]{1,0:T(8,128)}, bf16[1024,1024]{1,0:T(8,128)(2,1)S(1)}) custom-call(f32[1,1024]{1,0:T(1,128)S(1)} %bitcast.2, bf16[256,256]{1,0:T(8,128)(2,1)S(1)} %get-tuple-element.50.refs_0_, ...), custom_call_target="tpu_custom_call", output_to_operand_aliasing={{1}: (9, {}), {3}: (10, {})} | custom-call | flops 20000000000 | bytes 1024 | tf_op jit(solution)/shard_map/standardize/pallas_call | solution.py:157
  33.7 0.9 %collective-permute-start.6 = (bf16[1024,256]{1,0:T(8,128)(2,1)S(1)}, bf16[1024,256]{1,0:T(8,128)(2,1)S(1)}, u32[]{:S(2)}, u32[]{:S(2)}) collective-permute-start(bf16[1024,256]{1,0:T(8,128)(2,1)S(1)} %get-tuple-element.63), channel_id=1, source_target_pairs={{0,2},{1,3},{2,0},{3,1},{4,6},{5,7},{6,4},{7,5},{8,10},{9,11},{10,... | collective-permute-start | bytes 1572872 | tf_op jit(solution)/shard_map/far_1/ppermute | solution.py:284
  34.6 2.8 %collective-permute-done.11.refs_3_ = bf16[256,256]{1,0:T(8,128)(2,1)S(1)} collective-permute-done((bf16[256,256]{1,0:T(8,128)(2,1)S(1)}, bf16[256,256]{1,0:T(8,128)(2,1)S(1)}, u32[]{:S(2)}, u32[]{:S(2)}) %collective-permute-start.11) | collective-permute-done | bytes 131104 | tf_op jit(solution)/shard_map/cells_2_chunk_2/ppermute | solution.py:281
  37.4 3.6 %collective-permute-start.12 = (bf16[256,256]{1,0:T(8,128)(2,1)S(1)}, bf16[256,256]{1,0:T(8,128)(2,1)S(1)}, u32[]{:S(2)}, u32[]{:S(2)}) collective-permute-start(bf16[256,256]{1,0:T(8,128)(2,1)S(1)} %get-tuple-element.76), channel_id=1, source_target_pairs={{0,8},{4,12},{8,0},{12,4},{1,9},{5,13},{9,1},{13,5},{2,10},{6,14},... | collective-permute-start | bytes 393224 | tf_op jit(solution)/shard_map/cells_2_chunk_3/ppermute | solution.py:281
  41.0 0.0 collective-permute-done.9.refs_2_
  41.0 0.0 collective-permute-start.10
  41.0 3.1 %collective-permute-done.7.refs_1_ = bf16[256,256]{1,0:T(8,128)(2,1)S(1)} collective-permute-done((bf16[256,256]{1,0:T(8,128)(2,1)S(1)}, bf16[256,256]{1,0:T(8,128)(2,1)S(1)}, u32[]{:S(2)}, u32[]{:S(2)}) %collective-permute-start.7) | collective-permute-done | bytes 131104 | tf_op jit(solution)/shard_map/cells_3_chunk_2/ppermute | solution.py:281
  44.1 2.3 %collective-permute-start.8 = (bf16[256,256]{1,0:T(8,128)(2,1)S(1)}, bf16[256,256]{1,0:T(8,128)(2,1)S(1)}, u32[]{:S(2)}, u32[]{:S(2)}) collective-permute-start(bf16[256,256]{1,0:T(8,128)(2,1)S(1)} %get-tuple-element.68), channel_id=1, source_target_pairs={{0,12},{4,8},{8,4},{12,0},{1,13},{5,9},{9,5},{13,1},{2,14},{6,10},... | collective-permute-start | bytes 393224 | tf_op jit(solution)/shard_map/cells_3_chunk_3/ppermute | solution.py:281
  46.4 0.0 collective-permute-done.13.refs_0_
  46.4 1.8 %standardize.6 = (bf16[1024,256]{1,0:T(8,128)(2,1)S(1)}, bf16[1024,1024]{1,0:T(8,128)(2,1)S(1)}, f32[8,128]{1,0:T(8,128)}, bf16[1024,1024]{1,0:T(8,128)(2,1)S(1)}) custom-call(f32[1,1024]{1,0:T(1,128)S(1)} %bitcast.3, bf16[256,256]{1,0:T(8,128)(2,1)S(1)} %get-tuple-element.79.refs_0_, ...), custom_call_target="tpu_custom_call", output_to_operand_aliasing={{1}: (9, {}), {3}: (10, {})} | custom-call | flops 20000000000 | bytes 1024 | tf_op jit(solution)/shard_map/standardize/pallas_call | solution.py:157
  48.2 1.4 %collective-permute-start.14 = (bf16[1024,256]{1,0:T(8,128)(2,1)S(1)}, bf16[1024,256]{1,0:T(8,128)(2,1)S(1)}, u32[]{:S(2)}, u32[]{:S(2)}) collective-permute-start(bf16[1024,256]{1,0:T(8,128)(2,1)S(1)} %get-tuple-element.86), channel_id=1, source_target_pairs={{0,2},{1,3},{2,0},{3,1},{4,6},{5,7},{6,4},{7,5},{8,10},{9,11},{10,... | collective-permute-start | bytes 1572872 | tf_op jit(solution)/shard_map/far_2/ppermute | solution.py:284
  49.7 0.7 collective-permute-done.6.refs_1_
  50.4 0.0 collective-permute-done.12.refs_3_
  50.4 2.5 %collective-permute-done.8.refs_1_ = bf16[256,256]{1,0:T(8,128)(2,1)S(1)} collective-permute-done((bf16[256,256]{1,0:T(8,128)(2,1)S(1)}, bf16[256,256]{1,0:T(8,128)(2,1)S(1)}, u32[]{:S(2)}, u32[]{:S(2)}) %collective-permute-start.8) | collective-permute-done | bytes 131104 | tf_op jit(solution)/shard_map/cells_3_chunk_3/ppermute | solution.py:281
  53.0 1.2 %standardize.7 = (bf16[1024,256]{1,0:T(8,128)(2,1)S(1)}, bf16[1024,1024]{1,0:T(8,128)(2,1)S(1)}, f32[8,128]{1,0:T(8,128)S(1)}, bf16[1024,1024]{1,0:T(8,128)(2,1)S(1)}) custom-call(f32[1,1024]{1,0:T(1,128)S(1)} %bitcast.4, bf16[256,256]{1,0:T(8,128)(2,1)S(1)} %get-tuple-element.64.refs_0_, ...), custom_call_target="tpu_custom_call", output_to_operand_aliasing={{1}: (9, {}), {3}: (10, {})} | custom-call | flops 20000000000 | bytes 1024 | tf_op jit(solution)/shard_map/standardize/pallas_call | solution.py:157
  54.2 2.9 %collective-permute-start.15 = (bf16[1024,1024]{1,0:T(8,128)(2,1)S(1)}, bf16[1024,1024]{1,0:T(8,128)(2,1)S(1)}, u32[]{:S(2)}, u32[]{:S(2)}) collective-permute-start(bf16[1024,1024]{1,0:T(8,128)(2,1)S(1)} %get-tuple-element.87.refs_0_), channel_id=1, source_target_pairs={{0,1},{1,0},{2,3},{3,2},{4,5},{5,4},{6,7},{7,6},{8,9},{9,8},{10,11... | collective-permute-start | bytes 6291464 | tf_op jit(solution)/shard_map/near/ppermute | solution.py:288
  57.1 0.1 collective-permute-start.17
  57.2 0.4 collective-permute-start.16
  57.6 1.0 %collective-permute-start.19 = (bf16[1024,256]{1,0:T(8,128)(2,1)S(1)}, bf16[1024,256]{1,0:T(8,128)(2,1)S(1)}, u32[]{:S(2)}, u32[]{:S(2)}) collective-permute-start(bf16[1024,256]{1,0:T(8,128)(2,1)S(1)} %get-tuple-element.91), channel_id=1, source_target_pairs={{0,2},{1,3},{2,0},{3,1},{4,6},{5,7},{6,4},{7,5},{8,10},{9,11},{10,... | collective-permute-start | bytes 1572872 | tf_op jit(solution)/shard_map/far_3/ppermute | solution.py:284
  58.6 3.4 %gram.5.refs_3_ = bf16[1,1024,4096]{2,1,0:T(8,128)(2,1)} custom-call(f32[8,128]{1,0:T(8,128)S(1)} %get-tuple-element.84.count_ref, bf16[1024,1024]{1,0:T(8,128)(2,1)S(1)} %get-tuple-element.85.left_ref, bf16[1024,1024]{1,0:T(8,128)(2,1)S(1)} %get-tuple-element.87.refs_0_), custom_call_target="tpu_custom_call" | custom-call | flops 1024 | bytes 1024 | tf_op jit(solution)/shard_map/gram/pallas_call | solution.py:243
  62.0 0.3 collective-permute-done.14.refs_2_
  62.3 2.9 %gram.6.refs_3_ = bf16[1,1024,4096]{2,1,0:T(8,128)(2,1)} custom-call(f32[8,128]{1,0:T(8,128)S(1)} %get-tuple-element.84.count_ref, bf16[1024,1024]{1,0:T(8,128)(2,1)S(1)} %get-tuple-element.85.left_ref, bf16[1024,256]{1,0:T(8,128)(2,1)S(1)} %collective-permute-done.13.refs_0_, ...), custom_call_target="tpu_custom_call", output_to_operand_aliasing={{}: (5, {})} | custom-call | flops 20000000000 | bytes 1024 | tf_op jit(solution)/shard_map/gram/pallas_call | solution.py:243
  65.3 5.0 %gram.7.refs_1_ = bf16[1,1024,4096]{2,1,0:T(8,128)(2,1)} custom-call(f32[8,128]{1,0:T(8,128)S(1)} %get-tuple-element.84.count_ref, bf16[1024,1024]{1,0:T(8,128)(2,1)S(1)} %get-tuple-element.85.left_ref, bf16[1024,1024]{1,0:T(8,128)(2,1)S(1)} %collective-permute-done.15.refs_0_, ...), custom_call_target="tpu_custom_call", output_to_operand_aliasing={{}: (5, {})} | custom-call | flops 1024 | bytes 1024 | tf_op jit(solution)/shard_map/gram/pallas_call | solution.py:243
  70.2 3.3 %collective-permute-done.19.refs_0_ = bf16[1024,256]{1,0:T(8,128)(2,1)S(1)} collective-permute-done((bf16[1024,256]{1,0:T(8,128)(2,1)S(1)}, bf16[1024,256]{1,0:T(8,128)(2,1)S(1)}, u32[]{:S(2)}, u32[]{:S(2)}) %collective-permute-start.19) | collective-permute-done | bytes 524320 | tf_op jit(solution)/shard_map/far_3/ppermute | solution.py:284
  73.6 2.5 %collective-permute-start.20 = (bf16[1024,256]{1,0:T(8,128)(2,1)S(1)}, bf16[1024,256]{1,0:T(8,128)(2,1)S(1)}, u32[]{:S(2)}, u32[]{:S(2)}) collective-permute-start(bf16[1024,256]{1,0:T(8,128)(2,1)S(1)} %collective-permute-done.19.refs_0_), channel_id=1, source_target_pairs={{0,1},{1,0},{2,3},{3,2},{4,5},{5,4},{6,7},{7,6},{8,9},{9,8},{10,11... | collective-permute-start | bytes 1572872 | tf_op jit(solution)/shard_map/far_near_3/ppermute | solution.py:288
  76.1 0.0 collective-permute-start.18
  76.1 1.5 %gram.8.refs_2_ = bf16[1,1024,4096]{2,1,0:T(8,128)(2,1)} custom-call(f32[8,128]{1,0:T(8,128)S(1)} %get-tuple-element.84.count_ref, bf16[1024,1024]{1,0:T(8,128)(2,1)S(1)} %get-tuple-element.85.left_ref, bf16[1024,256]{1,0:T(8,128)(2,1)S(1)} %collective-permute-done.19.refs_0_, bf16[1,1024,4096]{2,1,0:T(8,128)(2,1)} %gram.7.refs_1_), custom_call_target="tpu_custom_call", output_to_operand_aliasing={{}: (3, {})} | custom-call | flops 1024 | bytes 1024 | tf_op jit(solution)/shard_map/gram/pallas_call | solution.py:243
  77.7 0.7 collective-permute-done.18.refs_0_
  78.4 2.4 %gram.9 = bf16[1,1024,4096]{2,1,0:T(8,128)(2,1)} custom-call(f32[8,128]{1,0:T(8,128)S(1)} %get-tuple-element.84.count_ref, bf16[1024,1024]{1,0:T(8,128)(2,1)S(1)} %get-tuple-element.85.left_ref, bf16[1024,256]{1,0:T(8,128)(2,1)S(1)} %collective-permute-done.18.refs_0_, ...), custom_call_target="tpu_custom_call", output_to_operand_aliasing={{}: (4, {})} | custom-call | flops 1024 | bytes 1024 | tf_op jit(solution)/shard_map/gram/pallas_call | solution.py:243
  (12 shorter events, 0.0 us)
Async XLA Ops:
  0.0 1.2 %copy-start = (bf16[512,1024]{1,0:T(8,128)(2,1)S(1)}, bf16[512,1024]{1,0:T(8,128)(2,1)}, u32[]{:S(2)}) copy-start(bf16[512,1024]{1,0:T(8,128)(2,1)} %expr_ref.1) | copy-start | bytes 3145732
  1.2 0.7 copy-start.1
  1.9 0.7 copy-start.2
  4.3 9.2 %collective-permute-start.4 = (bf16[272,256]{1,0:T(8,128)(2,1)S(1)}, bf16[272,256]{1,0:T(8,128)(2,1)S(1)}, u32[]{:S(2)}, u32[]{:S(2)}) collective-permute-start(bf16[272,256]{1,0:T(8,128)(2,1)S(1)} %get-tuple-element.58), channel_id=1, source_target_pairs={{0,8},{4,12},{8,0},{12,4},{1,9},{5,13},{9,1},{13,5},{2,10},{6,14},... | collective-permute-start | bytes 417800 | tf_op jit(solution)/shard_map/cells_2_chunk_0/ppermute | solution.py:281
  6.7 10.4 %collective-permute-start.2 = (bf16[272,256]{1,0:T(8,128)(2,1)S(1)}, bf16[272,256]{1,0:T(8,128)(2,1)S(1)}, u32[]{:S(2)}, u32[]{:S(2)}) collective-permute-start(bf16[272,256]{1,0:T(8,128)(2,1)S(1)} %get-tuple-element.55), channel_id=1, source_target_pairs={{0,4},{4,0},{8,12},{12,8},{1,5},{5,1},{9,13},{13,9},{2,6},{6,2},{1... | collective-permute-start | bytes 417800 | tf_op jit(solution)/shard_map/cells_1_chunk_0/ppermute | solution.py:281
  6.8 15.8 %collective-permute-start = (bf16[272,256]{1,0:T(8,128)(2,1)S(1)}, bf16[272,256]{1,0:T(8,128)(2,1)S(1)}, u32[]{:S(2)}, u32[]{:S(2)}) collective-permute-start(bf16[272,256]{1,0:T(8,128)(2,1)S(1)} %get-tuple-element.52), channel_id=1, source_target_pairs={{0,12},{4,8},{8,4},{12,0},{1,13},{5,9},{9,5},{13,1},{2,14},{6,10},... | collective-permute-start | bytes 417800 | tf_op jit(solution)/shard_map/cells_3_chunk_0/ppermute | solution.py:281
  13.5 15.8 %collective-permute-start.5 = (bf16[256,256]{1,0:T(8,128)(2,1)S(1)}, bf16[256,256]{1,0:T(8,128)(2,1)S(1)}, u32[]{:S(2)}, u32[]{:S(2)}) collective-permute-start(bf16[256,256]{1,0:T(8,128)(2,1)S(1)} %get-tuple-element.59), channel_id=1, source_target_pairs={{0,8},{4,12},{8,0},{12,4},{1,9},{5,13},{9,1},{13,5},{2,10},{6,14},... | collective-permute-start | bytes 393224 | tf_op jit(solution)/shard_map/cells_2_chunk_1/ppermute | solution.py:281
  17.1 13.4 %collective-permute-start.3 = (bf16[256,256]{1,0:T(8,128)(2,1)S(1)}, bf16[256,256]{1,0:T(8,128)(2,1)S(1)}, u32[]{:S(2)}, u32[]{:S(2)}) collective-permute-start(bf16[256,256]{1,0:T(8,128)(2,1)S(1)} %get-tuple-element.56), channel_id=1, source_target_pairs={{0,4},{4,0},{8,12},{12,8},{1,5},{5,1},{9,13},{13,9},{2,6},{6,2},{1... | collective-permute-start | bytes 393224 | tf_op jit(solution)/shard_map/cells_1_chunk_1/ppermute | solution.py:281
  22.6 7.8 %collective-permute-start.1 = (bf16[256,256]{1,0:T(8,128)(2,1)S(1)}, bf16[256,256]{1,0:T(8,128)(2,1)S(1)}, u32[]{:S(2)}, u32[]{:S(2)}) collective-permute-start(bf16[256,256]{1,0:T(8,128)(2,1)S(1)} %get-tuple-element.53), channel_id=1, source_target_pairs={{0,12},{4,8},{8,4},{12,0},{1,13},{5,9},{9,5},{13,1},{2,14},{6,10},... | collective-permute-start | bytes 393224 | tf_op jit(solution)/shard_map/cells_3_chunk_1/ppermute | solution.py:281
  25.3 0.7 copy-start.3
  28.0 18.4 %collective-permute-start.13 = (bf16[1024,256]{1,0:T(8,128)(2,1)S(1)}, bf16[1024,256]{1,0:T(8,128)(2,1)S(1)}, u32[]{:S(2)}, u32[]{:S(2)}) collective-permute-start(bf16[1024,256]{1,0:T(8,128)(2,1)S(1)} %get-tuple-element.78), channel_id=1, source_target_pairs={{0,2},{1,3},{2,0},{3,1},{4,6},{5,7},{6,4},{7,5},{8,10},{9,11},{10,... | collective-permute-start | bytes 1572872 | tf_op jit(solution)/shard_map/far_0/ppermute | solution.py:284
  29.3 8.1 %collective-permute-start.11 = (bf16[256,256]{1,0:T(8,128)(2,1)S(1)}, bf16[256,256]{1,0:T(8,128)(2,1)S(1)}, u32[]{:S(2)}, u32[]{:S(2)}) collective-permute-start(bf16[256,256]{1,0:T(8,128)(2,1)S(1)} %get-tuple-element.75), channel_id=1, source_target_pairs={{0,8},{4,12},{8,0},{12,4},{1,9},{5,13},{9,1},{13,5},{2,10},{6,14},... | collective-permute-start | bytes 393224 | tf_op jit(solution)/shard_map/cells_2_chunk_2/ppermute | solution.py:281
  30.4 10.5 %collective-permute-start.9 = (bf16[256,256]{1,0:T(8,128)(2,1)S(1)}, bf16[256,256]{1,0:T(8,128)(2,1)S(1)}, u32[]{:S(2)}, u32[]{:S(2)}) collective-permute-start(bf16[256,256]{1,0:T(8,128)(2,1)S(1)} %get-tuple-element.71), channel_id=1, source_target_pairs={{0,4},{4,0},{8,12},{12,8},{1,5},{5,1},{9,13},{13,9},{2,6},{6,2},{1... | collective-permute-start | bytes 393224 | tf_op jit(solution)/shard_map/cells_1_chunk_2/ppermute | solution.py:281
  30.5 13.6 %collective-permute-start.7 = (bf16[256,256]{1,0:T(8,128)(2,1)S(1)}, bf16[256,256]{1,0:T(8,128)(2,1)S(1)}, u32[]{:S(2)}, u32[]{:S(2)}) collective-permute-start(bf16[256,256]{1,0:T(8,128)(2,1)S(1)} %get-tuple-element.67), channel_id=1, source_target_pairs={{0,12},{4,8},{8,4},{12,0},{1,13},{5,9},{9,5},{13,1},{2,14},{6,10},... | collective-permute-start | bytes 393224 | tf_op jit(solution)/shard_map/cells_3_chunk_2/ppermute | solution.py:281
  33.7 16.7 %collective-permute-start.6 = (bf16[1024,256]{1,0:T(8,128)(2,1)S(1)}, bf16[1024,256]{1,0:T(8,128)(2,1)S(1)}, u32[]{:S(2)}, u32[]{:S(2)}) collective-permute-start(bf16[1024,256]{1,0:T(8,128)(2,1)S(1)} %get-tuple-element.63), channel_id=1, source_target_pairs={{0,2},{1,3},{2,0},{3,1},{4,6},{5,7},{6,4},{7,5},{8,10},{9,11},{10,... | collective-permute-start | bytes 1572872 | tf_op jit(solution)/shard_map/far_1/ppermute | solution.py:284
  37.4 13.1 %collective-permute-start.12 = (bf16[256,256]{1,0:T(8,128)(2,1)S(1)}, bf16[256,256]{1,0:T(8,128)(2,1)S(1)}, u32[]{:S(2)}, u32[]{:S(2)}) collective-permute-start(bf16[256,256]{1,0:T(8,128)(2,1)S(1)} %get-tuple-element.76), channel_id=1, source_target_pairs={{0,8},{4,12},{8,0},{12,4},{1,9},{5,13},{9,1},{13,5},{2,10},{6,14},... | collective-permute-start | bytes 393224 | tf_op jit(solution)/shard_map/cells_2_chunk_3/ppermute | solution.py:281
  41.0 9.5 %collective-permute-start.10 = (bf16[256,256]{1,0:T(8,128)(2,1)S(1)}, bf16[256,256]{1,0:T(8,128)(2,1)S(1)}, u32[]{:S(2)}, u32[]{:S(2)}) collective-permute-start(bf16[256,256]{1,0:T(8,128)(2,1)S(1)} %get-tuple-element.72), channel_id=1, source_target_pairs={{0,4},{4,0},{8,12},{12,8},{1,5},{5,1},{9,13},{13,9},{2,6},{6,2},{1... | collective-permute-start | bytes 393224 | tf_op jit(solution)/shard_map/cells_1_chunk_3/ppermute | solution.py:281
  44.1 8.9 %collective-permute-start.8 = (bf16[256,256]{1,0:T(8,128)(2,1)S(1)}, bf16[256,256]{1,0:T(8,128)(2,1)S(1)}, u32[]{:S(2)}, u32[]{:S(2)}) collective-permute-start(bf16[256,256]{1,0:T(8,128)(2,1)S(1)} %get-tuple-element.68), channel_id=1, source_target_pairs={{0,12},{4,8},{8,4},{12,0},{1,13},{5,9},{9,5},{13,1},{2,14},{6,10},... | collective-permute-start | bytes 393224 | tf_op jit(solution)/shard_map/cells_3_chunk_3/ppermute | solution.py:281
  48.2 14.1 %collective-permute-start.14 = (bf16[1024,256]{1,0:T(8,128)(2,1)S(1)}, bf16[1024,256]{1,0:T(8,128)(2,1)S(1)}, u32[]{:S(2)}, u32[]{:S(2)}) collective-permute-start(bf16[1024,256]{1,0:T(8,128)(2,1)S(1)} %get-tuple-element.86), channel_id=1, source_target_pairs={{0,2},{1,3},{2,0},{3,1},{4,6},{5,7},{6,4},{7,5},{8,10},{9,11},{10,... | collective-permute-start | bytes 1572872 | tf_op jit(solution)/shard_map/far_2/ppermute | solution.py:284
  54.2 11.1 %collective-permute-start.15 = (bf16[1024,1024]{1,0:T(8,128)(2,1)S(1)}, bf16[1024,1024]{1,0:T(8,128)(2,1)S(1)}, u32[]{:S(2)}, u32[]{:S(2)}) collective-permute-start(bf16[1024,1024]{1,0:T(8,128)(2,1)S(1)} %get-tuple-element.87.refs_0_), channel_id=1, source_target_pairs={{0,1},{1,0},{2,3},{3,2},{4,5},{5,4},{6,7},{7,6},{8,9},{9,8},{10,11... | collective-permute-start | bytes 6291464 | tf_op jit(solution)/shard_map/near/ppermute | solution.py:288
  57.1 8.1 %collective-permute-start.17 = (bf16[1024,256]{1,0:T(8,128)(2,1)S(1)}, bf16[1024,256]{1,0:T(8,128)(2,1)S(1)}, u32[]{:S(2)}, u32[]{:S(2)}) collective-permute-start(bf16[1024,256]{1,0:T(8,128)(2,1)S(1)} %collective-permute-done.6.refs_1_), channel_id=1, source_target_pairs={{0,1},{1,0},{2,3},{3,2},{4,5},{5,4},{6,7},{7,6},{8,9},{9,8},{10,11... | collective-permute-start | bytes 1572872 | tf_op jit(solution)/shard_map/far_near_1/ppermute | solution.py:288
  57.2 8.1 %collective-permute-start.16 = (bf16[1024,256]{1,0:T(8,128)(2,1)S(1)}, bf16[1024,256]{1,0:T(8,128)(2,1)S(1)}, u32[]{:S(2)}, u32[]{:S(2)}) collective-permute-start(bf16[1024,256]{1,0:T(8,128)(2,1)S(1)} %collective-permute-done.13.refs_0_), channel_id=1, source_target_pairs={{0,1},{1,0},{2,3},{3,2},{4,5},{5,4},{6,7},{7,6},{8,9},{9,8},{10,11... | collective-permute-start | bytes 1572872 | tf_op jit(solution)/shard_map/far_near_0/ppermute | solution.py:288
  57.6 16.0 %collective-permute-start.19 = (bf16[1024,256]{1,0:T(8,128)(2,1)S(1)}, bf16[1024,256]{1,0:T(8,128)(2,1)S(1)}, u32[]{:S(2)}, u32[]{:S(2)}) collective-permute-start(bf16[1024,256]{1,0:T(8,128)(2,1)S(1)} %get-tuple-element.91), channel_id=1, source_target_pairs={{0,2},{1,3},{2,0},{3,1},{4,6},{5,7},{6,4},{7,5},{8,10},{9,11},{10,... | collective-permute-start | bytes 1572872 | tf_op jit(solution)/shard_map/far_3/ppermute | solution.py:284
  73.6 4.1 %collective-permute-start.20 = (bf16[1024,256]{1,0:T(8,128)(2,1)S(1)}, bf16[1024,256]{1,0:T(8,128)(2,1)S(1)}, u32[]{:S(2)}, u32[]{:S(2)}) collective-permute-start(bf16[1024,256]{1,0:T(8,128)(2,1)S(1)} %collective-permute-done.19.refs_0_), channel_id=1, source_target_pairs={{0,1},{1,0},{2,3},{3,2},{4,5},{5,4},{6,7},{7,6},{8,9},{9,8},{10,11... | collective-permute-start | bytes 1572872 | tf_op jit(solution)/shard_map/far_near_3/ppermute | solution.py:288
  76.1 2.3 %collective-permute-start.18 = (bf16[1024,256]{1,0:T(8,128)(2,1)S(1)}, bf16[1024,256]{1,0:T(8,128)(2,1)S(1)}, u32[]{:S(2)}, u32[]{:S(2)}) collective-permute-start(bf16[1024,256]{1,0:T(8,128)(2,1)S(1)} %collective-permute-done.14.refs_2_), channel_id=1, source_target_pairs={{0,1},{1,0},{2,3},{3,2},{4,5},{5,4},{6,7},{7,6},{8,9},{9,8},{10,11... | collective-permute-start | bytes 1572872 | tf_op jit(solution)/shard_map/far_near_2/ppermute | solution.py:288

commit v10 on v9

--- a/solution.py
+++ b/solution.py
@@ -295,10 +295,11 @@
         for j in order:
             block = packed[k][j]
             if k:
-                block = after(block, before[len(arrived)])
+                block = after(block, before[len(arrived)], *(crossing if k == 1 and j > 1 else []))
             with jax.named_scope(f"cells_{j}_chunk_{k}"):
                 arrived.append(swap(block, j))
         before = list(arrived)
+        crossing = [got for got, j in zip(arrived[1:], order) if j > 1]
         if k >= 2:
             arrived[0] = after(arrived[0], *far[k - 2])
         if k == 0:

time: 81.1 us -> 84.2 us (1.038)
  the two profiles are of different devices: /device:TPU:13 before, /device:TPU:0 now
where the time goes in v10:
time: 84.2 us; the launch traced here: 84 us
  starting transfers between devices  28.6 us (34%)
  waiting for transfers between devices  28.2 us (33%)
  Pallas kernels  23.6 us (28%)
  local copies, waits for them, and re-layouts  3.27 us (4%)
    ppermute x12, starting transfers between devices, swap(): return lax.ppermute(block, 'cells', [(s, s ^ by) for s in range(types)])  21.8 us
    pallas_call x5, Pallas kernels, gram(): pl.pallas_call(functools.partial(gram_kernel, blocks, cores, strip, layou...  15.1 us
    ppermute x12, waiting for transfers between devices, swap(): return lax.ppermute(block, 'cells', [(s, s ^ by) for s in range(types)])  14.3 us
    ppermute x4, waiting for transfers between devices, across(): lax.ppermute(panel_, 'blk', [(b, (b + by * cores) % blocks) for b in rang...  13.4 us
    pallas_call x4, Pallas kernels, standardize(): pl.pallas_call(functools.partial(standardize_kernel, types, cap, lead, se...  6.79 us
    ppermute x4, starting transfers between devices, across(): lax.ppermute(panel_, 'blk', [(b, (b + by * cores) % blocks) for b in rang...  5.68 us
    unnamed x10, local copies, waits for them, and re-layouts  3.27 us
    pallas_call x1, Pallas kernels, pack(): pl.pallas_call(functools.partial(pack_kernel, types, cap, widths), out_sh...  1.71 us
  transfers between devices with their start and end apart: 21, of which 7 were waited for; matrix products, arithmetic and copies ran while one was open for 0% of the time, Pallas kernels for 23%

profile of v10, /device:TPU:0, one launch (start us, length us, event | category | flops | bytes accessed | tf_op | source)
XLA Modules:
  0.0 84.0 jit_solution(3374148300799645211)
XLA Ops:
  0.0 1.2 %copy-done = bf16[512,1024]{1,0:T(8,128)(2,1)S(1)} copy-done((bf16[512,1024]{1,0:T(8,128)(2,1)S(1)}, bf16[512,1024]{1,0:T(8,128)(2,1)}, u32[]{:S(2)}) %copy-start) | copy-done | bytes 1048600
  1.2 0.7 copy-done.1
  1.9 0.7 copy-done.2
  2.6 1.7 %pack.1 = (bf16[272,256]{1,0:T(8,128)(2,1)S(1)}, bf16[272,256]{1,0:T(8,128)(2,1)S(1)}, bf16[272,256]{1,0:T(8,128)(2,1)S(1)}, bf16[272,256]{1,0:T(8,128)(2,1)S(1)...) custom-call(s32[512]{0:T(512)S(1)} %copy-done.1, ...), custom_call_target="tpu_custom_call" | custom-call | flops 1024 | bytes 1024 | tf_op jit(solution)/shard_map/pack/pallas_call | solution.py:68
  4.3 5.1 %collective-permute-start = (bf16[272,256]{1,0:T(8,128)(2,1)S(1)}, bf16[272,256]{1,0:T(8,128)(2,1)S(1)}, u32[]{:S(2)}, u32[]{:S(2)}) collective-permute-start(bf16[272,256]{1,0:T(8,128)(2,1)S(1)} %get-tuple-element.52), channel_id=1, source_target_pairs={{0,12},{4,8},{8,4},{12,0},{1,13},{5,9},{9,5},{13,1},{2,14},{6,10},... | collective-permute-start | bytes 417800 | tf_op jit(solution)/shard_map/cells_3_chunk_0/ppermute | solution.py:281
  9.4 0.6 collective-permute-start.3
  10.1 4.0 %collective-permute-done.refs_1_.refs_5_ = bf16[272,256]{1,0:T(8,128)(2,1)S(1)} collective-permute-done((bf16[272,256]{1,0:T(8,128)(2,1)S(1)}, bf16[272,256]{1,0:T(8,128)(2,1)S(1)}, u32[]{:S(2)}, u32[]{:S(2)}) %collective-permute-start) | collective-permute-done | bytes 139296 | tf_op jit(solution)/shard_map/cells_3_chunk_0/ppermute | solution.py:281
  14.0 7.2 %collective-permute-done.1.refs_3_.refs_7_ = bf16[272,256]{1,0:T(8,128)(2,1)S(1)} collective-permute-done((bf16[272,256]{1,0:T(8,128)(2,1)S(1)}, bf16[272,256]{1,0:T(8,128)(2,1)S(1)}, u32[]{:S(2)}, u32[]{:S(2)}) %collective-permute-start.1) | collective-permute-done | bytes 139296 | tf_op jit(solution)/shard_map/cells_2_chunk_0/ppermute | solution.py:281
  21.2 0.0 collective-permute-start.5
  21.2 2.5 %collective-permute-start.2 = (bf16[256,256]{1,0:T(8,128)(2,1)S(1)}, bf16[256,256]{1,0:T(8,128)(2,1)S(1)}, u32[]{:S(2)}, u32[]{:S(2)}) collective-permute-start(bf16[256,256]{1,0:T(8,128)(2,1)S(1)} %get-tuple-element.54), channel_id=1, source_target_pairs={{0,12},{4,8},{8,4},{12,0},{1,13},{5,9},{9,5},{13,1},{2,14},{6,10},... | collective-permute-start | bytes 393224 | tf_op jit(solution)/shard_map/cells_3_chunk_1/ppermute | solution.py:281
  23.7 0.0 collective-permute-done.3.refs_2_.refs_6_
  23.7 1.0 %collective-permute-start.4 = (bf16[256,256]{1,0:T(8,128)(2,1)S(1)}, bf16[256,256]{1,0:T(8,128)(2,1)S(1)}, u32[]{:S(2)}, u32[]{:S(2)}) collective-permute-start(bf16[256,256]{1,0:T(8,128)(2,1)S(1)} %get-tuple-element.57), channel_id=1, source_target_pairs={{0,4},{4,0},{8,12},{12,8},{1,5},{5,1},{9,13},{13,9},{2,6},{6,2},{1... | collective-permute-start | bytes 393224 | tf_op jit(solution)/shard_map/cells_1_chunk_1/ppermute | solution.py:281
  24.7 0.7 copy-done.3
  25.4 2.0 %standardize.4 = (bf16[1024,256]{1,0:T(8,128)(2,1)S(1)}, bf16[1024,1024]{1,0:T(8,128)(2,1)S(1)}, f32[8,128]{1,0:T(8,128)}, bf16[1024,1024]{1,0:T(8,128)(2,1)S(1)}) custom-call(f32[1,1024]{1,0:T(1,128)S(1)} %bitcast.1, bf16[272,256]{1,0:T(8,128)(2,1)S(1)} %get-tuple-element.60.refs_0_.refs_4_, bf16[272,256]{1,0:T(8,128)(2,1)S(1)} %collective-permute-done.refs_1_.refs_5_, ...), custom_call_target="tpu_custom_call" | custom-call | flops 20000000000 | bytes 1024 | tf_op jit(solution)/shard_map/standardize/pallas_call | solution.py:157
  27.4 1.6 %collective-permute-start.13 = (bf16[1024,256]{1,0:T(8,128)(2,1)S(1)}, bf16[1024,256]{1,0:T(8,128)(2,1)S(1)}, u32[]{:S(2)}, u32[]{:S(2)}) collective-permute-start(bf16[1024,256]{1,0:T(8,128)(2,1)S(1)} %get-tuple-element.78), channel_id=1, source_target_pairs={{0,2},{1,3},{2,0},{3,1},{4,6},{5,7},{6,4},{7,5},{8,10},{9,11},{10,... | collective-permute-start | bytes 1572872 | tf_op jit(solution)/shard_map/far_0/ppermute | solution.py:284
  28.9 3.1 %collective-permute-done.5.refs_3_ = bf16[256,256]{1,0:T(8,128)(2,1)S(1)} collective-permute-done((bf16[256,256]{1,0:T(8,128)(2,1)S(1)}, bf16[256,256]{1,0:T(8,128)(2,1)S(1)}, u32[]{:S(2)}, u32[]{:S(2)}) %collective-permute-start.5) | collective-permute-done | bytes 131104 | tf_op jit(solution)/shard_map/cells_2_chunk_1/ppermute | solution.py:281
  32.0 0.0 collective-permute-start.11
  32.0 0.0 collective-permute-done.2.refs_1_
  32.0 1.6 %collective-permute-start.7 = (bf16[256,256]{1,0:T(8,128)(2,1)S(1)}, bf16[256,256]{1,0:T(8,128)(2,1)S(1)}, u32[]{:S(2)}, u32[]{:S(2)}) collective-permute-start(bf16[256,256]{1,0:T(8,128)(2,1)S(1)} %get-tuple-element.67), channel_id=1, source_target_pairs={{0,12},{4,8},{8,4},{12,0},{1,13},{5,9},{9,5},{13,1},{2,14},{6,10},... | collective-permute-start | bytes 393224 | tf_op jit(solution)/shard_map/cells_3_chunk_2/ppermute | solution.py:281
  33.6 0.0 collective-permute-done.4.refs_2_
  33.6 7.4 %collective-permute-start.9 = (bf16[256,256]{1,0:T(8,128)(2,1)S(1)}, bf16[256,256]{1,0:T(8,128)(2,1)S(1)}, u32[]{:S(2)}, u32[]{:S(2)}) collective-permute-start(bf16[256,256]{1,0:T(8,128)(2,1)S(1)} %get-tuple-element.71), channel_id=1, source_target_pairs={{0,4},{4,0},{8,12},{12,8},{1,5},{5,1},{9,13},{13,9},{2,6},{6,2},{1... | collective-permute-start | bytes 393224 | tf_op jit(solution)/shard_map/cells_1_chunk_2/ppermute | solution.py:281
  41.0 1.8 %standardize.5 = (bf16[1024,256]{1,0:T(8,128)(2,1)S(1)}, bf16[1024,1024]{1,0:T(8,128)(2,1)S(1)}, f32[8,128]{1,0:T(8,128)}, bf16[1024,1024]{1,0:T(8,128)(2,1)S(1)}) custom-call(f32[1,1024]{1,0:T(1,128)S(1)} %bitcast.2, bf16[256,256]{1,0:T(8,128)(2,1)S(1)} %get-tuple-element.50.refs_0_, ...), custom_call_target="tpu_custom_call", output_to_operand_aliasing={{1}: (9, {}), {3}: (10, {})} | custom-call | flops 20000000000 | bytes 1024 | tf_op jit(solution)/shard_map/standardize/pallas_call | solution.py:157
  42.8 1.5 %collective-permute-start.6 = (bf16[1024,256]{1,0:T(8,128)(2,1)S(1)}, bf16[1024,256]{1,0:T(8,128)(2,1)S(1)}, u32[]{:S(2)}, u32[]{:S(2)}) collective-permute-start(bf16[1024,256]{1,0:T(8,128)(2,1)S(1)} %get-tuple-element.63), channel_id=1, source_target_pairs={{0,2},{1,3},{2,0},{3,1},{4,6},{5,7},{6,4},{7,5},{8,10},{9,11},{10,... | collective-permute-start | bytes 1572872 | tf_op jit(solution)/shard_map/far_1/ppermute | solution.py:284
  44.4 1.5 %collective-permute-start.12 = (bf16[256,256]{1,0:T(8,128)(2,1)S(1)}, bf16[256,256]{1,0:T(8,128)(2,1)S(1)}, u32[]{:S(2)}, u32[]{:S(2)}) collective-permute-start(bf16[256,256]{1,0:T(8,128)(2,1)S(1)} %get-tuple-element.76), channel_id=1, source_target_pairs={{0,8},{4,12},{8,0},{12,4},{1,9},{5,13},{9,1},{13,5},{2,10},{6,14},... | collective-permute-start | bytes 393224 | tf_op jit(solution)/shard_map/cells_2_chunk_3/ppermute | solution.py:281
  45.8 0.0 collective-permute-done.7.refs_1_
  45.8 1.5 %collective-permute-start.8 = (bf16[256,256]{1,0:T(8,128)(2,1)S(1)}, bf16[256,256]{1,0:T(8,128)(2,1)S(1)}, u32[]{:S(2)}, u32[]{:S(2)}) collective-permute-start(bf16[256,256]{1,0:T(8,128)(2,1)S(1)} %get-tuple-element.68), channel_id=1, source_target_pairs={{0,12},{4,8},{8,4},{12,0},{1,13},{5,9},{9,5},{13,1},{2,14},{6,10},... | collective-permute-start | bytes 393224 | tf_op jit(solution)/shard_map/cells_3_chunk_3/ppermute | solution.py:281
  47.4 0.6 collective-permute-start.10
  47.9 1.8 %standardize.6 = (bf16[1024,256]{1,0:T(8,128)(2,1)S(1)}, bf16[1024,1024]{1,0:T(8,128)(2,1)S(1)}, f32[8,128]{1,0:T(8,128)}, bf16[1024,1024]{1,0:T(8,128)(2,1)S(1)}) custom-call(f32[1,1024]{1,0:T(1,128)S(1)} %bitcast.3, bf16[256,256]{1,0:T(8,128)(2,1)S(1)} %get-tuple-element.79.refs_0_, ...), custom_call_target="tpu_custom_call", output_to_operand_aliasing={{1}: (9, {}), {3}: (10, {})} | custom-call | flops 20000000000 | bytes 1024 | tf_op jit(solution)/shard_map/standardize/pallas_call | solution.py:157
  49.7 1.1 %collective-permute-start.14 = (bf16[1024,256]{1,0:T(8,128)(2,1)S(1)}, bf16[1024,256]{1,0:T(8,128)(2,1)S(1)}, u32[]{:S(2)}, u32[]{:S(2)}) collective-permute-start(bf16[1024,256]{1,0:T(8,128)(2,1)S(1)} %get-tuple-element.86), channel_id=1, source_target_pairs={{0,2},{1,3},{2,0},{3,1},{4,6},{5,7},{6,4},{7,5},{8,10},{9,11},{10,... | collective-permute-start | bytes 1572872 | tf_op jit(solution)/shard_map/far_2/ppermute | solution.py:284
  50.9 6.9 %collective-permute-done.6.refs_1_ = bf16[1024,256]{1,0:T(8,128)(2,1)S(1)} collective-permute-done((bf16[1024,256]{1,0:T(8,128)(2,1)S(1)}, bf16[1024,256]{1,0:T(8,128)(2,1)S(1)}, u32[]{:S(2)}, u32[]{:S(2)}) %collective-permute-start.6) | collective-permute-done | bytes 524320 | tf_op jit(solution)/shard_map/far_1/ppermute | solution.py:284
  57.7 0.0 collective-permute-done.10.refs_2_
  57.8 1.2 %standardize.7 = (bf16[1024,256]{1,0:T(8,128)(2,1)S(1)}, bf16[1024,1024]{1,0:T(8,128)(2,1)S(1)}, f32[8,128]{1,0:T(8,128)S(1)}, bf16[1024,1024]{1,0:T(8,128)(2,1)S(1)}) custom-call(f32[1,1024]{1,0:T(1,128)S(1)} %bitcast.4, bf16[256,256]{1,0:T(8,128)(2,1)S(1)} %get-tuple-element.64.refs_0_, ...), custom_call_target="tpu_custom_call", output_to_operand_aliasing={{1}: (9, {}), {3}: (10, {})} | custom-call | flops 20000000000 | bytes 1024 | tf_op jit(solution)/shard_map/standardize/pallas_call | solution.py:157
  59.0 0.1 collective-permute-start.15
  59.1 0.5 collective-permute-start.17
  59.5 0.1 collective-permute-start.16
  59.6 1.5 %collective-permute-start.19 = (bf16[1024,256]{1,0:T(8,128)(2,1)S(1)}, bf16[1024,256]{1,0:T(8,128)(2,1)S(1)}, u32[]{:S(2)}, u32[]{:S(2)}) collective-permute-start(bf16[1024,256]{1,0:T(8,128)(2,1)S(1)} %get-tuple-element.91), channel_id=1, source_target_pairs={{0,2},{1,3},{2,0},{3,1},{4,6},{5,7},{6,4},{7,5},{8,10},{9,11},{10,... | collective-permute-start | bytes 1572872 | tf_op jit(solution)/shard_map/far_3/ppermute | solution.py:284
  61.1 3.4 %gram.5.refs_3_ = bf16[1,1024,4096]{2,1,0:T(8,128)(2,1)} custom-call(f32[8,128]{1,0:T(8,128)S(1)} %get-tuple-element.84.count_ref, bf16[1024,1024]{1,0:T(8,128)(2,1)S(1)} %get-tuple-element.85.left_ref, bf16[1024,1024]{1,0:T(8,128)(2,1)S(1)} %get-tuple-element.87.refs_0_), custom_call_target="tpu_custom_call" | custom-call | flops 1024 | bytes 1024 | tf_op jit(solution)/shard_map/gram/pallas_call | solution.py:243
  64.5 4.5 %collective-permute-done.14.refs_2_ = bf16[1024,256]{1,0:T(8,128)(2,1)S(1)} collective-permute-done((bf16[1024,256]{1,0:T(8,128)(2,1)S(1)}, bf16[1024,256]{1,0:T(8,128)(2,1)S(1)}, u32[]{:S(2)}, u32[]{:S(2)}) %collective-permute-start.14) | collective-permute-done | bytes 524320 | tf_op jit(solution)/shard_map/far_2/ppermute | solution.py:284
  69.0 2.9 %gram.6.refs_3_ = bf16[1,1024,4096]{2,1,0:T(8,128)(2,1)} custom-call(f32[8,128]{1,0:T(8,128)S(1)} %get-tuple-element.84.count_ref, bf16[1024,1024]{1,0:T(8,128)(2,1)S(1)} %get-tuple-element.85.left_ref, bf16[1024,256]{1,0:T(8,128)(2,1)S(1)} %collective-permute-done.13.refs_0_, ...), custom_call_target="tpu_custom_call", output_to_operand_aliasing={{}: (5, {})} | custom-call | flops 20000000000 | bytes 1024 | tf_op jit(solution)/shard_map/gram/pallas_call | solution.py:243
  71.9 0.0 collective-permute-done.17.refs_2_
  71.9 0.0 collective-permute-done.15.refs_0_
  71.9 5.0 %gram.7.refs_1_ = bf16[1,1024,4096]{2,1,0:T(8,128)(2,1)} custom-call(f32[8,128]{1,0:T(8,128)S(1)} %get-tuple-element.84.count_ref, bf16[1024,1024]{1,0:T(8,128)(2,1)S(1)} %get-tuple-element.85.left_ref, bf16[1024,1024]{1,0:T(8,128)(2,1)S(1)} %collective-permute-done.15.refs_0_, ...), custom_call_target="tpu_custom_call", output_to_operand_aliasing={{}: (5, {})} | custom-call | flops 1024 | bytes 1024 | tf_op jit(solution)/shard_map/gram/pallas_call | solution.py:243
  76.9 2.0 %collective-permute-done.19.refs_0_ = bf16[1024,256]{1,0:T(8,128)(2,1)S(1)} collective-permute-done((bf16[1024,256]{1,0:T(8,128)(2,1)S(1)}, bf16[1024,256]{1,0:T(8,128)(2,1)S(1)}, u32[]{:S(2)}, u32[]{:S(2)}) %collective-permute-start.19) | collective-permute-done | bytes 524320 | tf_op jit(solution)/shard_map/far_3/ppermute | solution.py:284
  78.8 0.0 collective-permute-start.20
  78.8 0.5 collective-permute-start.18
  79.4 1.5 %gram.8.refs_2_ = bf16[1,1024,4096]{2,1,0:T(8,128)(2,1)} custom-call(f32[8,128]{1,0:T(8,128)S(1)} %get-tuple-element.84.count_ref, bf16[1024,1024]{1,0:T(8,128)(2,1)S(1)} %get-tuple-element.85.left_ref, bf16[1024,256]{1,0:T(8,128)(2,1)S(1)} %collective-permute-done.19.refs_0_, bf16[1,1024,4096]{2,1,0:T(8,128)(2,1)} %gram.7.refs_1_), custom_call_target="tpu_custom_call", output_to_operand_aliasing={{}: (3, {})} | custom-call | flops 1024 | bytes 1024 | tf_op jit(solution)/shard_map/gram/pallas_call | solution.py:243
  80.9 0.6 collective-permute-done.18.refs_0_
  81.5 2.3 %gram.9 = bf16[1,1024,4096]{2,1,0:T(8,128)(2,1)} custom-call(f32[8,128]{1,0:T(8,128)S(1)} %get-tuple-element.84.count_ref, bf16[1024,1024]{1,0:T(8,128)(2,1)S(1)} %get-tuple-element.85.left_ref, bf16[1024,256]{1,0:T(8,128)(2,1)S(1)} %collective-permute-done.18.refs_0_, ...), custom_call_target="tpu_custom_call", output_to_operand_aliasing={{}: (4, {})} | custom-call | flops 1024 | bytes 1024 | tf_op jit(solution)/shard_map/gram/pallas_call | solution.py:243
  (14 shorter events, 0.0 us)
Async XLA Ops:
  0.0 1.2 %copy-start = (bf16[512,1024]{1,0:T(8,128)(2,1)S(1)}, bf16[512,1024]{1,0:T(8,128)(2,1)}, u32[]{:S(2)}) copy-start(bf16[512,1024]{1,0:T(8,128)(2,1)} %expr_ref.1) | copy-start | bytes 3145732
  1.2 0.7 copy-start.1
  1.9 0.7 copy-start.2
  4.3 9.7 %collective-permute-start = (bf16[272,256]{1,0:T(8,128)(2,1)S(1)}, bf16[272,256]{1,0:T(8,128)(2,1)S(1)}, u32[]{:S(2)}, u32[]{:S(2)}) collective-permute-start(bf16[272,256]{1,0:T(8,128)(2,1)S(1)} %get-tuple-element.52), channel_id=1, source_target_pairs={{0,12},{4,8},{8,4},{12,0},{1,13},{5,9},{9,5},{13,1},{2,14},{6,10},... | collective-permute-start | bytes 417800 | tf_op jit(solution)/shard_map/cells_3_chunk_0/ppermute | solution.py:281
  9.4 11.8 %collective-permute-start.1 = (bf16[272,256]{1,0:T(8,128)(2,1)S(1)}, bf16[272,256]{1,0:T(8,128)(2,1)S(1)}, u32[]{:S(2)}, u32[]{:S(2)}) collective-permute-start(bf16[272,256]{1,0:T(8,128)(2,1)S(1)} %get-tuple-element.53), channel_id=1, source_target_pairs={{0,8},{4,12},{8,0},{12,4},{1,9},{5,13},{9,1},{13,5},{2,10},{6,14},... | collective-permute-start | bytes 417800 | tf_op jit(solution)/shard_map/cells_2_chunk_0/ppermute | solution.py:281
  9.4 14.3 %collective-permute-start.3 = (bf16[272,256]{1,0:T(8,128)(2,1)S(1)}, bf16[272,256]{1,0:T(8,128)(2,1)S(1)}, u32[]{:S(2)}, u32[]{:S(2)}) collective-permute-start(bf16[272,256]{1,0:T(8,128)(2,1)S(1)} %get-tuple-element.56), channel_id=1, source_target_pairs={{0,4},{4,0},{8,12},{12,8},{1,5},{5,1},{9,13},{13,9},{2,6},{6,2},{1... | collective-permute-start | bytes 417800 | tf_op jit(solution)/shard_map/cells_1_chunk_0/ppermute | solution.py:281
  21.2 10.8 %collective-permute-start.5 = (bf16[256,256]{1,0:T(8,128)(2,1)S(1)}, bf16[256,256]{1,0:T(8,128)(2,1)S(1)}, u32[]{:S(2)}, u32[]{:S(2)}) collective-permute-start(bf16[256,256]{1,0:T(8,128)(2,1)S(1)} %get-tuple-element.59), channel_id=1, source_target_pairs={{0,8},{4,12},{8,0},{12,4},{1,9},{5,13},{9,1},{13,5},{2,10},{6,14},... | collective-permute-start | bytes 393224 | tf_op jit(solution)/shard_map/cells_2_chunk_1/ppermute | solution.py:281
  21.2 10.8 %collective-permute-start.2 = (bf16[256,256]{1,0:T(8,128)(2,1)S(1)}, bf16[256,256]{1,0:T(8,128)(2,1)S(1)}, u32[]{:S(2)}, u32[]{:S(2)}) collective-permute-start(bf16[256,256]{1,0:T(8,128)(2,1)S(1)} %get-tuple-element.54), channel_id=1, source_target_pairs={{0,12},{4,8},{8,4},{12,0},{1,13},{5,9},{9,5},{13,1},{2,14},{6,10},... | collective-permute-start | bytes 393224 | tf_op jit(solution)/shard_map/cells_3_chunk_1/ppermute | solution.py:281
  23.7 9.9 %collective-permute-start.4 = (bf16[256,256]{1,0:T(8,128)(2,1)S(1)}, bf16[256,256]{1,0:T(8,128)(2,1)S(1)}, u32[]{:S(2)}, u32[]{:S(2)}) collective-permute-start(bf16[256,256]{1,0:T(8,128)(2,1)S(1)} %get-tuple-element.57), channel_id=1, source_target_pairs={{0,4},{4,0},{8,12},{12,8},{1,5},{5,1},{9,13},{13,9},{2,6},{6,2},{1... | collective-permute-start | bytes 393224 | tf_op jit(solution)/shard_map/cells_1_chunk_1/ppermute | solution.py:281
  24.7 0.7 copy-start.3
  27.4 20.6 %collective-permute-start.13 = (bf16[1024,256]{1,0:T(8,128)(2,1)S(1)}, bf16[1024,256]{1,0:T(8,128)(2,1)S(1)}, u32[]{:S(2)}, u32[]{:S(2)}) collective-permute-start(bf16[1024,256]{1,0:T(8,128)(2,1)S(1)} %get-tuple-element.78), channel_id=1, source_target_pairs={{0,2},{1,3},{2,0},{3,1},{4,6},{5,7},{6,4},{7,5},{8,10},{9,11},{10,... | collective-permute-start | bytes 1572872 | tf_op jit(solution)/shard_map/far_0/ppermute | solution.py:284
  32.0 12.3 %collective-permute-start.11 = (bf16[256,256]{1,0:T(8,128)(2,1)S(1)}, bf16[256,256]{1,0:T(8,128)(2,1)S(1)}, u32[]{:S(2)}, u32[]{:S(2)}) collective-permute-start(bf16[256,256]{1,0:T(8,128)(2,1)S(1)} %get-tuple-element.75), channel_id=1, source_target_pairs={{0,8},{4,12},{8,0},{12,4},{1,9},{5,13},{9,1},{13,5},{2,10},{6,14},... | collective-permute-start | bytes 393224 | tf_op jit(solution)/shard_map/cells_2_chunk_2/ppermute | solution.py:281
  32.0 13.8 %collective-permute-start.7 = (bf16[256,256]{1,0:T(8,128)(2,1)S(1)}, bf16[256,256]{1,0:T(8,128)(2,1)S(1)}, u32[]{:S(2)}, u32[]{:S(2)}) collective-permute-start(bf16[256,256]{1,0:T(8,128)(2,1)S(1)} %get-tuple-element.67), channel_id=1, source_target_pairs={{0,12},{4,8},{8,4},{12,0},{1,13},{5,9},{9,5},{13,1},{2,14},{6,10},... | collective-permute-start | bytes 393224 | tf_op jit(solution)/shard_map/cells_3_chunk_2/ppermute | solution.py:281
  33.6 13.8 %collective-permute-start.9 = (bf16[256,256]{1,0:T(8,128)(2,1)S(1)}, bf16[256,256]{1,0:T(8,128)(2,1)S(1)}, u32[]{:S(2)}, u32[]{:S(2)}) collective-permute-start(bf16[256,256]{1,0:T(8,128)(2,1)S(1)} %get-tuple-element.71), channel_id=1, source_target_pairs={{0,4},{4,0},{8,12},{12,8},{1,5},{5,1},{9,13},{13,9},{2,6},{6,2},{1... | collective-permute-start | bytes 393224 | tf_op jit(solution)/shard_map/cells_1_chunk_2/ppermute | solution.py:281
  41.0 6.9 %copy-start.4 = (f32[1024]{0:T(1024)S(1)}, f32[1024]{0:T(1024)}, u32[]{:S(2)}) copy-start(f32[1024]{0:T(1024)} %param.7) | copy-start | bytes 12292
  42.8 14.9 %collective-permute-start.6 = (bf16[1024,256]{1,0:T(8,128)(2,1)S(1)}, bf16[1024,256]{1,0:T(8,128)(2,1)S(1)}, u32[]{:S(2)}, u32[]{:S(2)}) collective-permute-start(bf16[1024,256]{1,0:T(8,128)(2,1)S(1)} %get-tuple-element.63), channel_id=1, source_target_pairs={{0,2},{1,3},{2,0},{3,1},{4,6},{5,7},{6,4},{7,5},{8,10},{9,11},{10,... | collective-permute-start | bytes 1572872 | tf_op jit(solution)/shard_map/far_1/ppermute | solution.py:284
  44.4 13.4 %collective-permute-start.12 = (bf16[256,256]{1,0:T(8,128)(2,1)S(1)}, bf16[256,256]{1,0:T(8,128)(2,1)S(1)}, u32[]{:S(2)}, u32[]{:S(2)}) collective-permute-start(bf16[256,256]{1,0:T(8,128)(2,1)S(1)} %get-tuple-element.76), channel_id=1, source_target_pairs={{0,8},{4,12},{8,0},{12,4},{1,9},{5,13},{9,1},{13,5},{2,10},{6,14},... | collective-permute-start | bytes 393224 | tf_op jit(solution)/shard_map/cells_2_chunk_3/ppermute | solution.py:281
  45.8 11.9 %collective-permute-start.8 = (bf16[256,256]{1,0:T(8,128)(2,1)S(1)}, bf16[256,256]{1,0:T(8,128)(2,1)S(1)}, u32[]{:S(2)}, u32[]{:S(2)}) collective-permute-start(bf16[256,256]{1,0:T(8,128)(2,1)S(1)} %get-tuple-element.68), channel_id=1, source_target_pairs={{0,12},{4,8},{8,4},{12,0},{1,13},{5,9},{9,5},{13,1},{2,14},{6,10},... | collective-permute-start | bytes 393224 | tf_op jit(solution)/shard_map/cells_3_chunk_3/ppermute | solution.py:281
  47.4 10.4 %collective-permute-start.10 = (bf16[256,256]{1,0:T(8,128)(2,1)S(1)}, bf16[256,256]{1,0:T(8,128)(2,1)S(1)}, u32[]{:S(2)}, u32[]{:S(2)}) collective-permute-start(bf16[256,256]{1,0:T(8,128)(2,1)S(1)} %get-tuple-element.72), channel_id=1, source_target_pairs={{0,4},{4,0},{8,12},{12,8},{1,5},{5,1},{9,13},{13,9},{2,6},{6,2},{1... | collective-permute-start | bytes 393224 | tf_op jit(solution)/shard_map/cells_1_chunk_3/ppermute | solution.py:281
  49.7 19.2 %collective-permute-start.14 = (bf16[1024,256]{1,0:T(8,128)(2,1)S(1)}, bf16[1024,256]{1,0:T(8,128)(2,1)S(1)}, u32[]{:S(2)}, u32[]{:S(2)}) collective-permute-start(bf16[1024,256]{1,0:T(8,128)(2,1)S(1)} %get-tuple-element.86), channel_id=1, source_target_pairs={{0,2},{1,3},{2,0},{3,1},{4,6},{5,7},{6,4},{7,5},{8,10},{9,11},{10,... | collective-permute-start | bytes 1572872 | tf_op jit(solution)/shard_map/far_2/ppermute | solution.py:284
  59.0 12.9 %collective-permute-start.15 = (bf16[1024,1024]{1,0:T(8,128)(2,1)S(1)}, bf16[1024,1024]{1,0:T(8,128)(2,1)S(1)}, u32[]{:S(2)}, u32[]{:S(2)}) collective-permute-start(bf16[1024,1024]{1,0:T(8,128)(2,1)S(1)} %get-tuple-element.87.refs_0_), channel_id=1, source_target_pairs={{0,1},{1,0},{2,3},{3,2},{4,5},{5,4},{6,7},{7,6},{8,9},{9,8},{10,11... | collective-permute-start | bytes 6291464 | tf_op jit(solution)/shard_map/near/ppermute | solution.py:288
  59.1 12.8 %collective-permute-start.17 = (bf16[1024,256]{1,0:T(8,128)(2,1)S(1)}, bf16[1024,256]{1,0:T(8,128)(2,1)S(1)}, u32[]{:S(2)}, u32[]{:S(2)}) collective-permute-start(bf16[1024,256]{1,0:T(8,128)(2,1)S(1)} %collective-permute-done.6.refs_1_), channel_id=1, source_target_pairs={{0,1},{1,0},{2,3},{3,2},{4,5},{5,4},{6,7},{7,6},{8,9},{9,8},{10,11... | collective-permute-start | bytes 1572872 | tf_op jit(solution)/shard_map/far_near_1/ppermute | solution.py:288
  59.5 12.3 %collective-permute-start.16 = (bf16[1024,256]{1,0:T(8,128)(2,1)S(1)}, bf16[1024,256]{1,0:T(8,128)(2,1)S(1)}, u32[]{:S(2)}, u32[]{:S(2)}) collective-permute-start(bf16[1024,256]{1,0:T(8,128)(2,1)S(1)} %collective-permute-done.13.refs_0_), channel_id=1, source_target_pairs={{0,1},{1,0},{2,3},{3,2},{4,5},{5,4},{6,7},{7,6},{8,9},{9,8},{10,11... | collective-permute-start | bytes 1572872 | tf_op jit(solution)/shard_map/far_near_0/ppermute | solution.py:288
  59.6 19.2 %collective-permute-start.19 = (bf16[1024,256]{1,0:T(8,128)(2,1)S(1)}, bf16[1024,256]{1,0:T(8,128)(2,1)S(1)}, u32[]{:S(2)}, u32[]{:S(2)}) collective-permute-start(bf16[1024,256]{1,0:T(8,128)(2,1)S(1)} %get-tuple-element.91), channel_id=1, source_target_pairs={{0,2},{1,3},{2,0},{3,1},{4,6},{5,7},{6,4},{7,5},{8,10},{9,11},{10,... | collective-permute-start | bytes 1572872 | tf_op jit(solution)/shard_map/far_3/ppermute | solution.py:284
  78.8 2.1 %collective-permute-start.20 = (bf16[1024,256]{1,0:T(8,128)(2,1)S(1)}, bf16[1024,256]{1,0:T(8,128)(2,1)S(1)}, u32[]{:S(2)}, u32[]{:S(2)}) collective-permute-start(bf16[1024,256]{1,0:T(8,128)(2,1)S(1)} %collective-permute-done.19.refs_0_), channel_id=1, source_target_pairs={{0,1},{1,0},{2,3},{3,2},{4,5},{5,4},{6,7},{7,6},{8,9},{9,8},{10,11... | collective-permute-start | bytes 1572872 | tf_op jit(solution)/shard_map/far_near_3/ppermute | solution.py:288
  78.8 2.7 %collective-permute-start.18 = (bf16[1024,256]{1,0:T(8,128)(2,1)S(1)}, bf16[1024,256]{1,0:T(8,128)(2,1)S(1)}, u32[]{:S(2)}, u32[]{:S(2)}) collective-permute-start(bf16[1024,256]{1,0:T(8,128)(2,1)S(1)} %collective-permute-done.14.refs_2_), channel_id=1, source_target_pairs={{0,1},{1,0},{2,3},{3,2},{4,5},{5,4},{6,7},{7,6},{8,9},{9,8},{10,11... | collective-permute-start | bytes 1572872 | tf_op jit(solution)/shard_map/far_near_2/ppermute | solution.py:288

commit v11 on v9

--- a/solution.py
+++ b/solution.py
@@ -77,14 +77,26 @@
     return [flat[k * types : (k + 1) * types] for k in range(len(widths))]
 
 
-def standardize_kernel(types, cap, lead, separate, chunk, mean_ref, *refs):
+def standardize_kernel(types, cap, lead, separate, start, gathered, mean_ref, *refs):
     blocks = refs[:types]
     tails = refs[types : 2 * types] if separate else blocks
     base = 0 if separate else cap
     refs = refs[2 * types :] if separate else refs[types:]
-    scaled_ref, turned_ref, count_ref, all_ref, work, turned, sems = refs[-7:]
+    work, turned, sems = refs[-3:]
+    if gathered:
+        scaled_ref, turned_ref, count_ref, all_ref, *joined_refs = refs[-7 - gathered[0] : -3]
+    else:
+        scaled_ref, turned_ref, count_ref, all_ref = refs[-7:-3]
+        joined_refs = []
+    copies = []
+    if gathered:
+        sources = refs[: len(gathered[1])]
+        for source, (joined, column) in zip(sources, gathered[1]):
+            spot = joined_refs[joined].at[:, pl.ds(column, source.shape[1])]
+            copies.append(pltpu.make_async_copy(source, spot, sems.at[2 + len(copies)]))
+            copies[-1].start()
     width = work.shape[1]
-    mean = mean_ref[:, chunk * width : (chunk + 1) * width]
+    mean = mean_ref[:, start : start + width]
     piece = min(lead, cap)
     total = jnp.zeros((1, width), jnp.float32)
     count = jnp.zeros((1, 1), jnp.float32)
@@ -122,9 +134,9 @@
         scaled_ref[j * cap : (j + 1) * cap, :] = scaled.astype(jnp.bfloat16)
         work[j * cap : (j + 1) * cap, :] = scaled
     slots = types * cap
-    columns = pl.ds(chunk * width, width)
-    copies = [pltpu.make_async_copy(scaled_ref, all_ref.at[:, columns], sems.at[0])]
-    copies[0].start()
+    columns = pl.ds(start, width)
+    copies.append(pltpu.make_async_copy(scaled_ref, all_ref.at[:, columns], sems.at[0]))
+    copies[-1].start()
     turned[...] = jnp.transpose(work[...]).astype(jnp.bfloat16)
     copies.append(pltpu.make_async_copy(turned, turned_ref.at[columns, :], sems.at[1]))
     copies[-1].start()
@@ -133,8 +145,9 @@
     count_ref[...] = jnp.broadcast_to(count, count_ref.shape)
 
 
-def standardize(types, cap, lead, width, mean, chunk, blocks, first, left, own):
-    chunks = mean.shape[1] // width
+def standardize(types, cap, mean, start, blocks, first, left, own, gather):
+    lead, width = first[0].shape[1], blocks[0].shape[1]
+    panel = mean.shape[1]
     separate = first is not blocks
     slots = types * cap
     specs = [whole] * (1 + types)
@@ -142,12 +155,15 @@
     if separate:
         specs += [pl.BlockSpec((TILE, lead), lambda i: (cap // TILE, 0))] * types
         args += list(first)
-    shapes = [
-        jax.ShapeDtypeStruct((slots, width), jnp.bfloat16),
-        jax.ShapeDtypeStruct((chunks * width, slots), jnp.bfloat16),
-        jax.ShapeDtypeStruct((8, 128), jnp.float32),
-        jax.ShapeDtypeStruct((slots, chunks * width), jnp.bfloat16),
-    ]
+    gathered, shapes = [], []
+    for i, panels in enumerate(gather):
+        column = 0
+        for array in panels:
+            gathered.append((i, column))
+            column += array.shape[1]
+            specs.append(whole)
+            args.append(array)
+        shapes.append(jax.ShapeDtypeStruct((slots, column), jnp.bfloat16))
     aliases = {}
     for value, output in ((left, 1), (own, 3)):
         if value is not None:
@@ -155,15 +171,29 @@
             specs.append(anywhere)
             args.append(value)
     return pl.pallas_call(
-        functools.partial(standardize_kernel, types, cap, lead, separate, chunk),
+        functools.partial(
+            standardize_kernel,
+            types,
+            cap,
+            lead,
+            separate,
+            start,
+            (len(gather), gathered) if gathered else None,
+        ),
         grid=(1,),
-        out_shape=shapes,
+        out_shape=[
+            jax.ShapeDtypeStruct((slots, width), jnp.bfloat16),
+            jax.ShapeDtypeStruct((panel, slots), jnp.bfloat16),
+            jax.ShapeDtypeStruct((8, 128), jnp.float32),
+            jax.ShapeDtypeStruct((slots, panel), jnp.bfloat16),
+            *shapes,
+        ],
         in_specs=specs,
-        out_specs=[whole, anywhere, whole, anywhere],
+        out_specs=[whole, anywhere, whole, anywhere] + [whole] * len(shapes),
         scratch_shapes=[
             pltpu.VMEM((slots, width), jnp.float32),
             pltpu.VMEM((width, slots), jnp.bfloat16),
-            pltpu.SemaphoreType.DMA((2,)),
+            pltpu.SemaphoreType.DMA((2 + len(gathered),)),
         ],
         input_output_aliases=aliases,
         compiler_params=pltpu.CompilerParams(vmem_limit_bytes=VMEM),
@@ -268,9 +298,9 @@
     shard_rows, panel = expression.shape
     cap = 2 * shard_rows // types
     assert types & (types - 1) == 0
-    width = 256
-    widths = [width] * (panel // width)
+    widths = [128] + [256] * (panel // 256 - 1) + [128]
     chunks = len(widths)
+    starts = [sum(widths[:k]) for k in range(chunks)]
     cores = 2
     chips = blocks // cores
     window = 3
@@ -288,7 +318,7 @@
             return lax.ppermute(after(panel_, *waits), "blk", [(b, b ^ 1) for b in range(blocks)])
 
     mean = gene_mean.reshape(1, panel)
-    order = sorted(range(1, types), key=lambda j: (j == 2, j == 1, -j))
+    order = sorted(range(1, types), key=lambda j: (j == 3, j == 1, j))
     left, own, far, before = None, None, [], None
     for k in range(chunks):
         arrived = [packed[k][0]]
@@ -303,30 +333,30 @@
             arrived[0] = after(arrived[0], *far[k - 2])
         if k == 0:
             first = arrived
-        scaled, left, count, own = standardize(
-            types, cap, width, width, mean, k, arrived, first, left, own
+        gather = []
+        if k == chunks - 1:
+            gather = [[got[d] for got in far[: k - 1]] for d in range(chips - 1)]
+        scaled, left, count, own, *joined = standardize(
+            types, cap, mean, starts[k], arrived, first, left, own, gather
         )
         with jax.named_scope(f"far_{k}"):
             far.append([across(scaled, d) for d in range(1, chips)])
 
     multiply = functools.partial(gram, blocks, cores, count, left)
     last = chunks - 1
-    late = max(last - 1, 1)
     near = side("near", own)
-    far_near = [[side(f"far_near_{k}", p, own) for p in far[k]] for k in range(late)]
+    joined_near = [side("far_near", p) for p in joined]
     out = multiply([([own], (0, 0, 0))], None, brief)
-    groups = [([far[k][d - 1] for k in range(last)], (d, 0, 0)) for d in range(1, chips)]
+    second = [side(f"far_near_{last - 1}", p, own) for p in far[last - 1]]
+    groups = [([p, far[last - 1][i]], (i + 1, 0, 0)) for i, p in enumerate(joined)]
     out = multiply(groups, out, lengthy)
     groups = [([near], (0, 1, 0))]
-    for d in range(1, chips):
-        groups.append(([far_near[k][d - 1] for k in range(late)], (d, 1, 0)))
+    groups += [([p, second[i]], (i + 1, 1, 0)) for i, p in enumerate(joined_near)]
     out = multiply(groups, out, brief)
-    far_near = [[side(f"far_near_{k}", p, out) for p in far[k]] for k in range(late, chunks)]
-    edge = last * width
+    final = [side(f"far_near_{last}", p, out) for p in far[last]]
+    edge = starts[last]
     out = multiply([([p], (d, 0, edge)) for d, p in enumerate(far[last], 1)], out, brief)
-    edge = late * width
-    groups = [([p[d - 1] for p in far_near], (d, 1, edge)) for d in range(1, chips)]
-    return multiply(groups, out, brief)
+    return multiply([([p], (d, 1, edge)) for d, p in enumerate(final, 1)], out, brief)
 
 
 def solution(mesh):

time: 81.1 us -> 82.7 us (1.020)
  the two profiles are of different devices: /device:TPU:13 before, /device:TPU:15 now
where the time goes in v11:
time: 82.7 us; the launch traced here: 82.5 us
  starting transfers between devices  36.8 us (44%)
  Pallas kernels  25.5 us (31%)
  waiting for transfers between devices  16.6 us (20%)
  local copies, waits for them, and re-layouts  3.27 us (4%)
    ppermute x15, starting transfers between devices, swap(): return lax.ppermute(block, 'cells', [(s, s ^ by) for s in range(types)])  24 us
    pallas_call x5, Pallas kernels, gram(): pl.pallas_call(functools.partial(gram_kernel, blocks, cores, strip, layou...  15.9 us
    ppermute x15, waiting for transfers between devices, swap(): return lax.ppermute(block, 'cells', [(s, s ^ by) for s in range(types)])  14.8 us
    ppermute x4, starting transfers between devices, side(): lax.ppermute(after(panel_, *waits), 'blk', [(b, b ^ 1) for b in range(blo...  11.7 us
    pallas_call x5, Pallas kernels, standardize(): pl.pallas_call(functools.partial(standardize_kernel, types, cap, lead, se...  7.9 us
    unnamed x8, local copies, waits for them, and re-layouts  3.27 us
    ppermute x5, waiting for transfers between devices, across(): lax.ppermute(panel_, 'blk', [(b, (b + by * cores) % blocks) for b in rang...  1.78 us
    pallas_call x1, Pallas kernels, pack(): pl.pallas_call(functools.partial(pack_kernel, types, cap, widths), out_sh...  1.7 us
  transfers between devices with their start and end apart: 24, of which 11 were waited for; matrix products, arithmetic and copies ran while one was open for 0% of the time, Pallas kernels for 27%

profile of v11, /device:TPU:15, one launch (start us, length us, event | category | flops | bytes accessed | tf_op | source)
XLA Modules:
  0.0 82.5 jit_solution(14398000064799332431)
XLA Ops:
  0.0 1.2 %copy-done = bf16[512,1024]{1,0:T(8,128)(2,1)S(1)} copy-done((bf16[512,1024]{1,0:T(8,128)(2,1)S(1)}, bf16[512,1024]{1,0:T(8,128)(2,1)}, u32[]{:S(2)}) %copy-start) | copy-done | bytes 1048600
  1.2 0.7 copy-done.1
  1.9 0.7 copy-done.2
  2.6 1.7 %pack.1 = (bf16[272,128]{1,0:T(8,128)(2,1)S(1)}, bf16[272,128]{1,0:T(8,128)(2,1)S(1)}, bf16[272,128]{1,0:T(8,128)(2,1)S(1)}, bf16[272,128]{1,0:T(8,128)(2,1)S(1)...) custom-call(s32[512]{0:T(512)S(1)} %copy-done.1, ...), custom_call_target="tpu_custom_call" | custom-call | flops 1024 | bytes 1024 | tf_op jit(solution)/shard_map/pack/pallas_call | solution.py:68
  4.3 2.4 %collective-permute-start = (bf16[272,128]{1,0:T(8,128)(2,1)S(1)}, bf16[272,128]{1,0:T(8,128)(2,1)S(1)}, u32[]{:S(2)}, u32[]{:S(2)}) collective-permute-start(bf16[272,128]{1,0:T(8,128)(2,1)S(1)} %get-tuple-element.62), channel_id=1, source_target_pairs={{0,8},{4,12},{8,0},{12,4},{1,9},{5,13},{9,1},{13,5},{2,10},{6,14},... | collective-permute-start | bytes 208904 | tf_op jit(solution)/shard_map/cells_2_chunk_0/ppermute | solution.py:311
  6.7 0.2 collective-permute-start.1
  6.8 0.2 collective-permute-start.2
  7.0 2.2 %collective-permute-done.refs_1_.refs_5_ = bf16[272,128]{1,0:T(8,128)(2,1)S(1)} collective-permute-done((bf16[272,128]{1,0:T(8,128)(2,1)S(1)}, bf16[272,128]{1,0:T(8,128)(2,1)S(1)}, u32[]{:S(2)}, u32[]{:S(2)}) %collective-permute-start) | collective-permute-done | bytes 69664 | tf_op jit(solution)/shard_map/cells_2_chunk_0/ppermute | solution.py:311
  9.3 3.5 %collective-permute-start.4 = (bf16[256,256]{1,0:T(8,128)(2,1)S(1)}, bf16[256,256]{1,0:T(8,128)(2,1)S(1)}, u32[]{:S(2)}, u32[]{:S(2)}) collective-permute-start(bf16[256,256]{1,0:T(8,128)(2,1)S(1)} %get-tuple-element.69), channel_id=1, source_target_pairs={{0,8},{4,12},{8,0},{12,4},{1,9},{5,13},{9,1},{13,5},{2,10},{6,14},... | collective-permute-start | bytes 393224 | tf_op jit(solution)/shard_map/cells_2_chunk_1/ppermute | solution.py:311
  12.7 0.0 collective-permute-done.1.refs_2_.refs_6_
  12.7 0.0 collective-permute-start.6
  12.8 1.1 %collective-permute-done.2.refs_3_.refs_7_ = bf16[272,128]{1,0:T(8,128)(2,1)S(1)} collective-permute-done((bf16[272,128]{1,0:T(8,128)(2,1)S(1)}, bf16[272,128]{1,0:T(8,128)(2,1)S(1)}, u32[]{:S(2)}, u32[]{:S(2)}) %collective-permute-start.2) | collective-permute-done | bytes 69664 | tf_op jit(solution)/shard_map/cells_3_chunk_0/ppermute | solution.py:311
  13.9 2.4 %collective-permute-start.8 = (bf16[256,256]{1,0:T(8,128)(2,1)S(1)}, bf16[256,256]{1,0:T(8,128)(2,1)S(1)}, u32[]{:S(2)}, u32[]{:S(2)}) collective-permute-start(bf16[256,256]{1,0:T(8,128)(2,1)S(1)} %get-tuple-element.77), channel_id=1, source_target_pairs={{0,12},{4,8},{8,4},{12,0},{1,13},{5,9},{9,5},{13,1},{2,14},{6,10},... | collective-permute-start | bytes 393224 | tf_op jit(solution)/shard_map/cells_3_chunk_1/ppermute | solution.py:311
  16.2 0.7 copy-done.3
  16.9 1.4 %standardize.5 = (bf16[1024,128]{1,0:T(8,128)(2,1)S(1)}, bf16[1024,1024]{1,0:T(8,128)(2,1)S(1)}, f32[8,128]{1,0:T(8,128)}, bf16[1024,1024]{1,0:T(8,128)(2,1)S(1)}) custom-call(f32[1,1024]{1,0:T(1,128)S(1)} %bitcast.1, bf16[272,128]{1,0:T(8,128)(2,1)S(1)} %get-tuple-element.61.refs_0_.refs_4_, bf16[272,128]{1,0:T(8,128)(2,1)S(1)} %collective-permute-done.refs_1_.refs_5_, ...), custom_call_target="tpu_custom_call" | custom-call | flops 20000000000 | bytes 1024 | tf_op jit(solution)/shard_map/standardize/pallas_call | solution.py:173
  18.3 0.3 collective-permute-start.3
  18.6 0.4 collective-permute-done.4.refs_1_
  19.1 3.1 %collective-permute-start.5 = (bf16[256,256]{1,0:T(8,128)(2,1)S(1)}, bf16[256,256]{1,0:T(8,128)(2,1)S(1)}, u32[]{:S(2)}, u32[]{:S(2)}) collective-permute-start(bf16[256,256]{1,0:T(8,128)(2,1)S(1)} %get-tuple-element.70), channel_id=1, source_target_pairs={{0,8},{4,12},{8,0},{12,4},{1,9},{5,13},{9,1},{13,5},{2,10},{6,14},... | collective-permute-start | bytes 393224 | tf_op jit(solution)/shard_map/cells_2_chunk_2/ppermute | solution.py:311
  22.2 3.7 %collective-permute-done.8.refs_3_ = bf16[256,256]{1,0:T(8,128)(2,1)S(1)} collective-permute-done((bf16[256,256]{1,0:T(8,128)(2,1)S(1)}, bf16[256,256]{1,0:T(8,128)(2,1)S(1)}, u32[]{:S(2)}, u32[]{:S(2)}) %collective-permute-start.8) | collective-permute-done | bytes 131104 | tf_op jit(solution)/shard_map/cells_3_chunk_1/ppermute | solution.py:311
  25.8 2.5 %collective-permute-start.9 = (bf16[256,256]{1,0:T(8,128)(2,1)S(1)}, bf16[256,256]{1,0:T(8,128)(2,1)S(1)}, u32[]{:S(2)}, u32[]{:S(2)}) collective-permute-start(bf16[256,256]{1,0:T(8,128)(2,1)S(1)} %get-tuple-element.78), channel_id=1, source_target_pairs={{0,12},{4,8},{8,4},{12,0},{1,13},{5,9},{9,5},{13,1},{2,14},{6,10},... | collective-permute-start | bytes 393224 | tf_op jit(solution)/shard_map/cells_3_chunk_2/ppermute | solution.py:311
  28.3 1.9 %standardize.6 = (bf16[1024,256]{1,0:T(8,128)(2,1)S(1)}, bf16[1024,1024]{1,0:T(8,128)(2,1)S(1)}, f32[8,128]{1,0:T(8,128)}, bf16[1024,1024]{1,0:T(8,128)(2,1)S(1)}) custom-call(f32[1,1024]{1,0:T(1,128)S(1)} %bitcast.2, bf16[256,256]{1,0:T(8,128)(2,1)S(1)} %get-tuple-element.79.refs_0_, ...), custom_call_target="tpu_custom_call", output_to_operand_aliasing={{1}: (9, {}), {3}: (10, {})} | custom-call | flops 20000000000 | bytes 1024 | tf_op jit(solution)/shard_map/standardize/pallas_call | solution.py:173
  30.2 0.1 collective-permute-start.17
  30.3 0.1 collective-permute-done.5.refs_1_
  30.3 3.1 %collective-permute-start.11 = (bf16[256,256]{1,0:T(8,128)(2,1)S(1)}, bf16[256,256]{1,0:T(8,128)(2,1)S(1)}, u32[]{:S(2)}, u32[]{:S(2)}) collective-permute-start(bf16[256,256]{1,0:T(8,128)(2,1)S(1)} %get-tuple-element.88), channel_id=1, source_target_pairs={{0,8},{4,12},{8,0},{12,4},{1,9},{5,13},{9,1},{13,5},{2,10},{6,14},... | collective-permute-start | bytes 393224 | tf_op jit(solution)/shard_map/cells_2_chunk_3/ppermute | solution.py:311
  33.4 0.0 collective-permute-done.7.refs_2_
  33.4 2.5 %collective-permute-done.9.refs_3_ = bf16[256,256]{1,0:T(8,128)(2,1)S(1)} collective-permute-done((bf16[256,256]{1,0:T(8,128)(2,1)S(1)}, bf16[256,256]{1,0:T(8,128)(2,1)S(1)}, u32[]{:S(2)}, u32[]{:S(2)}) %collective-permute-start.9) | collective-permute-done | bytes 131104 | tf_op jit(solution)/shard_map/cells_3_chunk_2/ppermute | solution.py:311
  35.9 2.2 %collective-permute-start.15 = (bf16[256,256]{1,0:T(8,128)(2,1)S(1)}, bf16[256,256]{1,0:T(8,128)(2,1)S(1)}, u32[]{:S(2)}, u32[]{:S(2)}) collective-permute-start(bf16[256,256]{1,0:T(8,128)(2,1)S(1)} %get-tuple-element.96), channel_id=1, source_target_pairs={{0,12},{4,8},{8,4},{12,0},{1,13},{5,9},{9,5},{13,1},{2,14},{6,10},... | collective-permute-start | bytes 393224 | tf_op jit(solution)/shard_map/cells_3_chunk_3/ppermute | solution.py:311
  38.1 1.9 %standardize.7 = (bf16[1024,256]{1,0:T(8,128)(2,1)S(1)}, bf16[1024,1024]{1,0:T(8,128)(2,1)S(1)}, f32[8,128]{1,0:T(8,128)}, bf16[1024,1024]{1,0:T(8,128)(2,1)S(1)}) custom-call(f32[1,1024]{1,0:T(1,128)S(1)} %bitcast.3, bf16[256,256]{1,0:T(8,128)(2,1)S(1)} %get-tuple-element.66.refs_0_, ...), custom_call_target="tpu_custom_call", output_to_operand_aliasing={{1}: (9, {}), {3}: (10, {})} | custom-call | flops 20000000000 | bytes 1024 | tf_op jit(solution)/shard_map/standardize/pallas_call | solution.py:173
  40.0 0.3 collective-permute-start.10
  40.3 1.2 %collective-permute-done.11.refs_1_ = bf16[256,256]{1,0:T(8,128)(2,1)S(1)} collective-permute-done((bf16[256,256]{1,0:T(8,128)(2,1)S(1)}, bf16[256,256]{1,0:T(8,128)(2,1)S(1)}, u32[]{:S(2)}, u32[]{:S(2)}) %collective-permute-start.11) | collective-permute-done | bytes 131104 | tf_op jit(solution)/shard_map/cells_2_chunk_3/ppermute | solution.py:311
  41.5 3.1 %collective-permute-start.12 = (bf16[256,128]{1,0:T(8,128)(2,1)S(1)}, bf16[256,128]{1,0:T(8,128)(2,1)S(1)}, u32[]{:S(2)}, u32[]{:S(2)}) collective-permute-start(bf16[256,128]{1,0:T(8,128)(2,1)S(1)} %get-tuple-element.89), channel_id=1, source_target_pairs={{0,8},{4,12},{8,0},{12,4},{1,9},{5,13},{9,1},{13,5},{2,10},{6,14},... | collective-permute-start | bytes 196616 | tf_op jit(solution)/shard_map/cells_2_chunk_4/ppermute | solution.py:311
  44.6 2.5 %collective-permute-done.15.refs_3_ = bf16[256,256]{1,0:T(8,128)(2,1)S(1)} collective-permute-done((bf16[256,256]{1,0:T(8,128)(2,1)S(1)}, bf16[256,256]{1,0:T(8,128)(2,1)S(1)}, u32[]{:S(2)}, u32[]{:S(2)}) %collective-permute-start.15) | collective-permute-done | bytes 131104 | tf_op jit(solution)/shard_map/cells_3_chunk_3/ppermute | solution.py:311
  47.2 1.5 %collective-permute-start.16 = (bf16[256,128]{1,0:T(8,128)(2,1)S(1)}, bf16[256,128]{1,0:T(8,128)(2,1)S(1)}, u32[]{:S(2)}, u32[]{:S(2)}) collective-permute-start(bf16[256,128]{1,0:T(8,128)(2,1)S(1)} %get-tuple-element.97), channel_id=1, source_target_pairs={{0,12},{4,8},{8,4},{12,0},{1,13},{5,9},{9,5},{13,1},{2,14},{6,10},... | collective-permute-start | bytes 196616 | tf_op jit(solution)/shard_map/cells_3_chunk_4/ppermute | solution.py:311
  48.7 1.9 %standardize.8 = (bf16[1024,256]{1,0:T(8,128)(2,1)S(1)}, bf16[1024,1024]{1,0:T(8,128)(2,1)S(1)}, f32[8,128]{1,0:T(8,128)}, bf16[1024,1024]{1,0:T(8,128)(2,1)S(1)}) custom-call(f32[1,1024]{1,0:T(1,128)S(1)} %bitcast.4, bf16[256,256]{1,0:T(8,128)(2,1)S(1)} %get-tuple-element.100.refs_0_, ...), custom_call_target="tpu_custom_call", output_to_operand_aliasing={{1}: (9, {}), {3}: (10, {})} | custom-call | flops 20000000000 | bytes 1024 | tf_op jit(solution)/shard_map/standardize/pallas_call | solution.py:173
  50.5 0.3 collective-permute-start.21
  50.9 1.0 %collective-permute-done.16.refs_3_ = bf16[256,128]{1,0:T(8,128)(2,1)S(1)} collective-permute-done((bf16[256,128]{1,0:T(8,128)(2,1)S(1)}, bf16[256,128]{1,0:T(8,128)(2,1)S(1)}, u32[]{:S(2)}, u32[]{:S(2)}) %collective-permute-start.16) | collective-permute-done | bytes 65568 | tf_op jit(solution)/shard_map/cells_3_chunk_4/ppermute | solution.py:311
  51.9 0.9 %standardize.9 = (bf16[1024,128]{1,0:T(8,128)(2,1)S(1)}, bf16[1024,1024]{1,0:T(8,128)(2,1)S(1)}, f32[8,128]{1,0:T(8,128)S(1)}, bf16[1024,1024]{1,0:T(8,128)(2,1)S(1)}, bf16[1024,640]{1,0:T(8,128)(2,1)S(1)}) custom-call(f32[1,1024]{1,0:T(1,128)S(1)} %bitcast.5, ...), custom_call_target="tpu_custom_call", output_to_operand_aliasing={{1}: (12, {}), {3}: (13, {})} | custom-call | flops 20000000000 | bytes 1024 | tf_op jit(solution)/shard_map/standardize/pallas_call | solution.py:173
  52.8 6.0 %collective-permute-start.19 = (bf16[1024,1024]{1,0:T(8,128)(2,1)S(1)}, bf16[1024,1024]{1,0:T(8,128)(2,1)S(1)}, u32[]{:S(2)}, u32[]{:S(2)}) collective-permute-start(bf16[1024,1024]{1,0:T(8,128)(2,1)S(1)} %get-tuple-element.108.refs_0_), channel_id=1, source_target_pairs={{0,1},{1,0},{2,3},{3,2},{4,5},{5,4},{6,7},{7,6},{8,9},{9,8},{10,11... | collective-permute-start | bytes 6291464 | tf_op jit(solution)/shard_map/near/ppermute | solution.py:318
  58.9 0.1 collective-permute-start.20
  58.9 3.4 %gram.5.refs_2_ = bf16[1,1024,4096]{2,1,0:T(8,128)(2,1)} custom-call(f32[8,128]{1,0:T(8,128)S(1)} %get-tuple-element.105.count_ref, bf16[1024,1024]{1,0:T(8,128)(2,1)S(1)} %get-tuple-element.106.left_ref, bf16[1024,1024]{1,0:T(8,128)(2,1)S(1)} %get-tuple-element.108.refs_0_), custom_call_target="tpu_custom_call" | custom-call | flops 1024 | bytes 1024 | tf_op jit(solution)/shard_map/gram/pallas_call | solution.py:273
  62.3 1.8 %collective-permute-done.21.refs_1_ = bf16[1024,256]{1,0:T(8,128)(2,1)S(1)} collective-permute-done((bf16[1024,256]{1,0:T(8,128)(2,1)S(1)}, bf16[1024,256]{1,0:T(8,128)(2,1)S(1)}, u32[]{:S(2)}, u32[]{:S(2)}) %collective-permute-start.21) | collective-permute-done | bytes 524320 | tf_op jit(solution)/shard_map/far_3/ppermute | solution.py:314
  64.1 5.5 %collective-permute-start.22 = (bf16[1024,256]{1,0:T(8,128)(2,1)S(1)}, bf16[1024,256]{1,0:T(8,128)(2,1)S(1)}, u32[]{:S(2)}, u32[]{:S(2)}) collective-permute-start(bf16[1024,256]{1,0:T(8,128)(2,1)S(1)} %collective-permute-done.21.refs_1_), channel_id=1, source_target_pairs={{0,1},{1,0},{2,3},{3,2},{4,5},{5,4},{6,7},{7,6},{8,9},{9,8},{10,11... | collective-permute-start | bytes 1572872 | tf_op jit(solution)/shard_map/far_near_3/ppermute | solution.py:318
  69.6 3.5 %gram.6.refs_3_ = bf16[1,1024,4096]{2,1,0:T(8,128)(2,1)} custom-call(f32[8,128]{1,0:T(8,128)S(1)} %get-tuple-element.105.count_ref, bf16[1024,1024]{1,0:T(8,128)(2,1)S(1)} %get-tuple-element.106.left_ref, bf16[1024,640]{1,0:T(8,128)(2,1)S(1)} %get-tuple-element.109.refs_0_, ...), custom_call_target="tpu_custom_call", output_to_operand_aliasing={{}: (4, {})} | custom-call | flops 20000000000 | bytes 1024 | tf_op jit(solution)/shard_map/gram/pallas_call | solution.py:273
  73.1 6.2 %gram.7.refs_1_ = bf16[1,1024,4096]{2,1,0:T(8,128)(2,1)} custom-call(f32[8,128]{1,0:T(8,128)S(1)} %get-tuple-element.105.count_ref, bf16[1024,1024]{1,0:T(8,128)(2,1)S(1)} %get-tuple-element.106.left_ref, bf16[1024,1024]{1,0:T(8,128)(2,1)S(1)} %collective-permute-done.19.refs_0_, ...), custom_call_target="tpu_custom_call", output_to_operand_aliasing={{}: (5, {})} | custom-call | flops 1024 | bytes 1024 | tf_op jit(solution)/shard_map/gram/pallas_call | solution.py:273
  79.3 0.1 collective-permute-start.23
  79.4 1.4 %gram.8.refs_1_ = bf16[1,1024,4096]{2,1,0:T(8,128)(2,1)} custom-call(f32[8,128]{1,0:T(8,128)S(1)} %get-tuple-element.105.count_ref, bf16[1024,1024]{1,0:T(8,128)(2,1)S(1)} %get-tuple-element.106.left_ref, bf16[1024,128]{1,0:T(8,128)(2,1)S(1)} %collective-permute-done.18.refs_0_, bf16[1,1024,4096]{2,1,0:T(8,128)(2,1)} %gram.7.refs_1_), custom_call_target="tpu_custom_call", output_to_operand_aliasing={{}: (3, {})} | custom-call | flops 1024 | bytes 1024 | tf_op jit(solution)/shard_map/gram/pallas_call | solution.py:273
  80.8 0.1 collective-permute-done.23.refs_0_
  80.9 1.4 %gram.9 = bf16[1,1024,4096]{2,1,0:T(8,128)(2,1)} custom-call(f32[8,128]{1,0:T(8,128)S(1)} %get-tuple-element.105.count_ref, bf16[1024,1024]{1,0:T(8,128)(2,1)S(1)} %get-tuple-element.106.left_ref, bf16[1024,128]{1,0:T(8,128)(2,1)S(1)} %collective-permute-done.23.refs_0_, bf16[1,1024,4096]{2,1,0:T(8,128)(2,1)} %gram.8.refs_1_), custom_call_target="tpu_custom_call", output_to_operand_aliasing={{}: (3, {})} | custom-call | flops 1024 | bytes 1024 | tf_op jit(solution)/shard_map/gram/pallas_call | solution.py:273
  (19 shorter events, 0.0 us)
Async XLA Ops:
  0.0 1.2 %copy-start = (bf16[512,1024]{1,0:T(8,128)(2,1)S(1)}, bf16[512,1024]{1,0:T(8,128)(2,1)}, u32[]{:S(2)}) copy-start(bf16[512,1024]{1,0:T(8,128)(2,1)} %expr_ref.1) | copy-start | bytes 3145732
  1.2 0.7 copy-start.1
  1.9 0.7 copy-start.2
  4.3 5.0 %collective-permute-start = (bf16[272,128]{1,0:T(8,128)(2,1)S(1)}, bf16[272,128]{1,0:T(8,128)(2,1)S(1)}, u32[]{:S(2)}, u32[]{:S(2)}) collective-permute-start(bf16[272,128]{1,0:T(8,128)(2,1)S(1)} %get-tuple-element.62), channel_id=1, source_target_pairs={{0,8},{4,12},{8,0},{12,4},{1,9},{5,13},{9,1},{13,5},{2,10},{6,14},... | collective-permute-start | bytes 208904 | tf_op jit(solution)/shard_map/cells_2_chunk_0/ppermute | solution.py:311
  6.7 6.1 %collective-permute-start.1 = (bf16[272,128]{1,0:T(8,128)(2,1)S(1)}, bf16[272,128]{1,0:T(8,128)(2,1)S(1)}, u32[]{:S(2)}, u32[]{:S(2)}) collective-permute-start(bf16[272,128]{1,0:T(8,128)(2,1)S(1)} %get-tuple-element.63), channel_id=1, source_target_pairs={{0,4},{4,0},{8,12},{12,8},{1,5},{5,1},{9,13},{13,9},{2,6},{6,2},{1... | collective-permute-start | bytes 208904 | tf_op jit(solution)/shard_map/cells_1_chunk_0/ppermute | solution.py:311
  6.8 7.0 %collective-permute-start.2 = (bf16[272,128]{1,0:T(8,128)(2,1)S(1)}, bf16[272,128]{1,0:T(8,128)(2,1)S(1)}, u32[]{:S(2)}, u32[]{:S(2)}) collective-permute-start(bf16[272,128]{1,0:T(8,128)(2,1)S(1)} %get-tuple-element.64), channel_id=1, source_target_pairs={{0,12},{4,8},{8,4},{12,0},{1,13},{5,9},{9,5},{13,1},{2,14},{6,10},... | collective-permute-start | bytes 208904 | tf_op jit(solution)/shard_map/cells_3_chunk_0/ppermute | solution.py:311
  9.3 9.8 %collective-permute-start.4 = (bf16[256,256]{1,0:T(8,128)(2,1)S(1)}, bf16[256,256]{1,0:T(8,128)(2,1)S(1)}, u32[]{:S(2)}, u32[]{:S(2)}) collective-permute-start(bf16[256,256]{1,0:T(8,128)(2,1)S(1)} %get-tuple-element.69), channel_id=1, source_target_pairs={{0,8},{4,12},{8,0},{12,4},{1,9},{5,13},{9,1},{13,5},{2,10},{6,14},... | collective-permute-start | bytes 393224 | tf_op jit(solution)/shard_map/cells_2_chunk_1/ppermute | solution.py:311
  12.7 9.4 %collective-permute-start.6 = (bf16[256,256]{1,0:T(8,128)(2,1)S(1)}, bf16[256,256]{1,0:T(8,128)(2,1)S(1)}, u32[]{:S(2)}, u32[]{:S(2)}) collective-permute-start(bf16[256,256]{1,0:T(8,128)(2,1)S(1)} %get-tuple-element.73), channel_id=1, source_target_pairs={{0,4},{4,0},{8,12},{12,8},{1,5},{5,1},{9,13},{13,9},{2,6},{6,2},{1... | collective-permute-start | bytes 393224 | tf_op jit(solution)/shard_map/cells_1_chunk_1/ppermute | solution.py:311
  13.9 11.9 %collective-permute-start.8 = (bf16[256,256]{1,0:T(8,128)(2,1)S(1)}, bf16[256,256]{1,0:T(8,128)(2,1)S(1)}, u32[]{:S(2)}, u32[]{:S(2)}) collective-permute-start(bf16[256,256]{1,0:T(8,128)(2,1)S(1)} %get-tuple-element.77), channel_id=1, source_target_pairs={{0,12},{4,8},{8,4},{12,0},{1,13},{5,9},{9,5},{13,1},{2,14},{6,10},... | collective-permute-start | bytes 393224 | tf_op jit(solution)/shard_map/cells_3_chunk_1/ppermute | solution.py:311
  16.2 0.7 copy-start.3
  18.3 11.9 %collective-permute-start.3 = (bf16[1024,128]{1,0:T(8,128)(2,1)S(1)}, bf16[1024,128]{1,0:T(8,128)(2,1)S(1)}, u32[]{:S(2)}, u32[]{:S(2)}) collective-permute-start(bf16[1024,128]{1,0:T(8,128)(2,1)S(1)} %get-tuple-element.65), channel_id=1, source_target_pairs={{0,2},{1,3},{2,0},{3,1},{4,6},{5,7},{6,4},{7,5},{8,10},{9,11},{10,... | collective-permute-start | bytes 786440 | tf_op jit(solution)/shard_map/far_0/ppermute | solution.py:314
  19.1 11.2 %collective-permute-start.5 = (bf16[256,256]{1,0:T(8,128)(2,1)S(1)}, bf16[256,256]{1,0:T(8,128)(2,1)S(1)}, u32[]{:S(2)}, u32[]{:S(2)}) collective-permute-start(bf16[256,256]{1,0:T(8,128)(2,1)S(1)} %get-tuple-element.70), channel_id=1, source_target_pairs={{0,8},{4,12},{8,0},{12,4},{1,9},{5,13},{9,1},{13,5},{2,10},{6,14},... | collective-permute-start | bytes 393224 | tf_op jit(solution)/shard_map/cells_2_chunk_2/ppermute | solution.py:311
  22.2 11.2 %collective-permute-start.7 = (bf16[256,256]{1,0:T(8,128)(2,1)S(1)}, bf16[256,256]{1,0:T(8,128)(2,1)S(1)}, u32[]{:S(2)}, u32[]{:S(2)}) collective-permute-start(bf16[256,256]{1,0:T(8,128)(2,1)S(1)} %get-tuple-element.74), channel_id=1, source_target_pairs={{0,4},{4,0},{8,12},{12,8},{1,5},{5,1},{9,13},{13,9},{2,6},{6,2},{1... | collective-permute-start | bytes 393224 | tf_op jit(solution)/shard_map/cells_1_chunk_2/ppermute | solution.py:311
  25.8 10.1 %collective-permute-start.9 = (bf16[256,256]{1,0:T(8,128)(2,1)S(1)}, bf16[256,256]{1,0:T(8,128)(2,1)S(1)}, u32[]{:S(2)}, u32[]{:S(2)}) collective-permute-start(bf16[256,256]{1,0:T(8,128)(2,1)S(1)} %get-tuple-element.78), channel_id=1, source_target_pairs={{0,12},{4,8},{8,4},{12,0},{1,13},{5,9},{9,5},{13,1},{2,14},{6,10},... | collective-permute-start | bytes 393224 | tf_op jit(solution)/shard_map/cells_3_chunk_2/ppermute | solution.py:311
  30.2 18.5 %collective-permute-start.17 = (bf16[1024,256]{1,0:T(8,128)(2,1)S(1)}, bf16[1024,256]{1,0:T(8,128)(2,1)S(1)}, u32[]{:S(2)}, u32[]{:S(2)}) collective-permute-start(bf16[1024,256]{1,0:T(8,128)(2,1)S(1)} %get-tuple-element.98), channel_id=1, source_target_pairs={{0,2},{1,3},{2,0},{3,1},{4,6},{5,7},{6,4},{7,5},{8,10},{9,11},{10,... | collective-permute-start | bytes 1572872 | tf_op jit(solution)/shard_map/far_1/ppermute | solution.py:314
  30.3 11.2 %collective-permute-start.11 = (bf16[256,256]{1,0:T(8,128)(2,1)S(1)}, bf16[256,256]{1,0:T(8,128)(2,1)S(1)}, u32[]{:S(2)}, u32[]{:S(2)}) collective-permute-start(bf16[256,256]{1,0:T(8,128)(2,1)S(1)} %get-tuple-element.88), channel_id=1, source_target_pairs={{0,8},{4,12},{8,0},{12,4},{1,9},{5,13},{9,1},{13,5},{2,10},{6,14},... | collective-permute-start | bytes 393224 | tf_op jit(solution)/shard_map/cells_2_chunk_3/ppermute | solution.py:311
  33.4 11.2 %collective-permute-start.13 = (bf16[256,256]{1,0:T(8,128)(2,1)S(1)}, bf16[256,256]{1,0:T(8,128)(2,1)S(1)}, u32[]{:S(2)}, u32[]{:S(2)}) collective-permute-start(bf16[256,256]{1,0:T(8,128)(2,1)S(1)} %get-tuple-element.92), channel_id=1, source_target_pairs={{0,4},{4,0},{8,12},{12,8},{1,5},{5,1},{9,13},{13,9},{2,6},{6,2},{1... | collective-permute-start | bytes 393224 | tf_op jit(solution)/shard_map/cells_1_chunk_3/ppermute | solution.py:311
  35.9 11.2 %collective-permute-start.15 = (bf16[256,256]{1,0:T(8,128)(2,1)S(1)}, bf16[256,256]{1,0:T(8,128)(2,1)S(1)}, u32[]{:S(2)}, u32[]{:S(2)}) collective-permute-start(bf16[256,256]{1,0:T(8,128)(2,1)S(1)} %get-tuple-element.96), channel_id=1, source_target_pairs={{0,12},{4,8},{8,4},{12,0},{1,13},{5,9},{9,5},{13,1},{2,14},{6,10},... | collective-permute-start | bytes 393224 | tf_op jit(solution)/shard_map/cells_3_chunk_3/ppermute | solution.py:311
  40.0 10.9 %collective-permute-start.10 = (bf16[1024,256]{1,0:T(8,128)(2,1)S(1)}, bf16[1024,256]{1,0:T(8,128)(2,1)S(1)}, u32[]{:S(2)}, u32[]{:S(2)}) collective-permute-start(bf16[1024,256]{1,0:T(8,128)(2,1)S(1)} %get-tuple-element.84), channel_id=1, source_target_pairs={{0,2},{1,3},{2,0},{3,1},{4,6},{5,7},{6,4},{7,5},{8,10},{9,11},{10,... | collective-permute-start | bytes 1572872 | tf_op jit(solution)/shard_map/far_2/ppermute | solution.py:314
  41.5 9.3 %collective-permute-start.12 = (bf16[256,128]{1,0:T(8,128)(2,1)S(1)}, bf16[256,128]{1,0:T(8,128)(2,1)S(1)}, u32[]{:S(2)}, u32[]{:S(2)}) collective-permute-start(bf16[256,128]{1,0:T(8,128)(2,1)S(1)} %get-tuple-element.89), channel_id=1, source_target_pairs={{0,8},{4,12},{8,0},{12,4},{1,9},{5,13},{9,1},{13,5},{2,10},{6,14},... | collective-permute-start | bytes 196616 | tf_op jit(solution)/shard_map/cells_2_chunk_4/ppermute | solution.py:311
  44.6 6.2 %collective-permute-start.14 = (bf16[256,128]{1,0:T(8,128)(2,1)S(1)}, bf16[256,128]{1,0:T(8,128)(2,1)S(1)}, u32[]{:S(2)}, u32[]{:S(2)}) collective-permute-start(bf16[256,128]{1,0:T(8,128)(2,1)S(1)} %get-tuple-element.93), channel_id=1, source_target_pairs={{0,4},{4,0},{8,12},{12,8},{1,5},{5,1},{9,13},{13,9},{2,6},{6,2},{1... | collective-permute-start | bytes 196616 | tf_op jit(solution)/shard_map/cells_1_chunk_4/ppermute | solution.py:311
  47.2 4.7 %collective-permute-start.16 = (bf16[256,128]{1,0:T(8,128)(2,1)S(1)}, bf16[256,128]{1,0:T(8,128)(2,1)S(1)}, u32[]{:S(2)}, u32[]{:S(2)}) collective-permute-start(bf16[256,128]{1,0:T(8,128)(2,1)S(1)} %get-tuple-element.97), channel_id=1, source_target_pairs={{0,12},{4,8},{8,4},{12,0},{1,13},{5,9},{9,5},{13,1},{2,14},{6,10},... | collective-permute-start | bytes 196616 | tf_op jit(solution)/shard_map/cells_3_chunk_4/ppermute | solution.py:311
  50.5 13.6 %collective-permute-start.21 = (bf16[1024,256]{1,0:T(8,128)(2,1)S(1)}, bf16[1024,256]{1,0:T(8,128)(2,1)S(1)}, u32[]{:S(2)}, u32[]{:S(2)}) collective-permute-start(bf16[1024,256]{1,0:T(8,128)(2,1)S(1)} %get-tuple-element.110), channel_id=1, source_target_pairs={{0,2},{1,3},{2,0},{3,1},{4,6},{5,7},{6,4},{7,5},{8,10},{9,11},{10,... | collective-permute-start | bytes 1572872 | tf_op jit(solution)/shard_map/far_3/ppermute | solution.py:314
  52.8 20.3 %collective-permute-start.19 = (bf16[1024,1024]{1,0:T(8,128)(2,1)S(1)}, bf16[1024,1024]{1,0:T(8,128)(2,1)S(1)}, u32[]{:S(2)}, u32[]{:S(2)}) collective-permute-start(bf16[1024,1024]{1,0:T(8,128)(2,1)S(1)} %get-tuple-element.108.refs_0_), channel_id=1, source_target_pairs={{0,1},{1,0},{2,3},{3,2},{4,5},{5,4},{6,7},{7,6},{8,9},{9,8},{10,11... | collective-permute-start | bytes 6291464 | tf_op jit(solution)/shard_map/near/ppermute | solution.py:318
  58.9 14.2 %collective-permute-start.20 = (bf16[1024,640]{1,0:T(8,128)(2,1)S(1)}, bf16[1024,640]{1,0:T(8,128)(2,1)S(1)}, u32[]{:S(2)}, u32[]{:S(2)}) collective-permute-start(bf16[1024,640]{1,0:T(8,128)(2,1)S(1)} %get-tuple-element.109.refs_0_), channel_id=1, source_target_pairs={{0,1},{1,0},{2,3},{3,2},{4,5},{5,4},{6,7},{7,6},{8,9},{9,8},{10,11... | collective-permute-start | bytes 3932168 | tf_op jit(solution)/shard_map/far_near/ppermute | solution.py:318
  58.9 20.3 %collective-permute-start.18 = (bf16[1024,128]{1,0:T(8,128)(2,1)S(1)}, bf16[1024,128]{1,0:T(8,128)(2,1)S(1)}, u32[]{:S(2)}, u32[]{:S(2)}) collective-permute-start(bf16[1024,128]{1,0:T(8,128)(2,1)S(1)} %get-tuple-element.107), channel_id=1, source_target_pairs={{0,2},{1,3},{2,0},{3,1},{4,6},{5,7},{6,4},{7,5},{8,10},{9,11},{10,... | collective-permute-start | bytes 786440 | tf_op jit(solution)/shard_map/far_4/ppermute | solution.py:314
  64.1 9.0 %collective-permute-start.22 = (bf16[1024,256]{1,0:T(8,128)(2,1)S(1)}, bf16[1024,256]{1,0:T(8,128)(2,1)S(1)}, u32[]{:S(2)}, u32[]{:S(2)}) collective-permute-start(bf16[1024,256]{1,0:T(8,128)(2,1)S(1)} %collective-permute-done.21.refs_1_), channel_id=1, source_target_pairs={{0,1},{1,0},{2,3},{3,2},{4,5},{5,4},{6,7},{7,6},{8,9},{9,8},{10,11... | collective-permute-start | bytes 1572872 | tf_op jit(solution)/shard_map/far_near_3/ppermute | solution.py:318
  79.3 1.6 %collective-permute-start.23 = (bf16[1024,128]{1,0:T(8,128)(2,1)S(1)}, bf16[1024,128]{1,0:T(8,128)(2,1)S(1)}, u32[]{:S(2)}, u32[]{:S(2)}) collective-permute-start(bf16[1024,128]{1,0:T(8,128)(2,1)S(1)} %collective-permute-done.18.refs_0_), channel_id=1, source_target_pairs={{0,1},{1,0},{2,3},{3,2},{4,5},{5,4},{6,7},{7,6},{8,9},{9,8},{10,11... | collective-permute-start | bytes 786440 | tf_op jit(solution)/shard_map/far_near_4/ppermute | solution.py:318

commit v12 on v11

--- a/solution.py
+++ b/solution.py
@@ -298,7 +298,7 @@
     shard_rows, panel = expression.shape
     cap = 2 * shard_rows // types
     assert types & (types - 1) == 0
-    widths = [128] + [256] * (panel // 256 - 1) + [128]
+    widths = [256] * (panel // 256)
     chunks = len(widths)
     starts = [sum(widths[:k]) for k in range(chunks)]
     cores = 2
@@ -334,7 +334,7 @@
         if k == 0:
             first = arrived
         gather = []
-        if k == chunks - 1:
+        if k == chunks - 1 and k > 1:
             gather = [[got[d] for got in far[: k - 1]] for d in range(chips - 1)]
         scaled, left, count, own, *joined = standardize(
             types, cap, mean, starts[k], arrived, first, left, own, gather
@@ -345,13 +345,14 @@
     multiply = functools.partial(gram, blocks, cores, count, left)
     last = chunks - 1
     near = side("near", own)
-    joined_near = [side("far_near", p) for p in joined]
+    joined_near = [[side("far_near", p)] for p in joined] or [[]] * (chips - 1)
+    joined = [[p] for p in joined] or [[]] * (chips - 1)
     out = multiply([([own], (0, 0, 0))], None, brief)
     second = [side(f"far_near_{last - 1}", p, own) for p in far[last - 1]]
-    groups = [([p, far[last - 1][i]], (i + 1, 0, 0)) for i, p in enumerate(joined)]
+    groups = [([*p, far[last - 1][i]], (i + 1, 0, 0)) for i, p in enumerate(joined)]
     out = multiply(groups, out, lengthy)
     groups = [([near], (0, 1, 0))]
-    groups += [([p, second[i]], (i + 1, 1, 0)) for i, p in enumerate(joined_near)]
+    groups += [([*p, second[i]], (i + 1, 1, 0)) for i, p in enumerate(joined_near)]
     out = multiply(groups, out, brief)
     final = [side(f"far_near_{last}", p, out) for p in far[last]]
     edge = starts[last]

time: 82.7 us -> 78.4 us (0.948)
  the two profiles are of different devices: /device:TPU:15 before, /device:TPU:0 now
where the time goes in v12:
time: 78.4 us; the launch traced here: 76.9 us
  starting transfers between devices  25.5 us (33%)
  waiting for transfers between devices  24.1 us (31%)
  Pallas kernels  23.8 us (30%)
  local copies, waits for them, and re-layouts  3.27 us (4%)
    ppermute x12, starting transfers between devices, swap(): return lax.ppermute(block, 'cells', [(s, s ^ by) for s in range(types)])  21.3 us
    ppermute x12, waiting for transfers between devices, swap(): return lax.ppermute(block, 'cells', [(s, s ^ by) for s in range(types)])  19.2 us
    pallas_call x5, Pallas kernels, gram(): pl.pallas_call(functools.partial(gram_kernel, blocks, cores, strip, layou...  15.4 us
    pallas_call x4, Pallas kernels, standardize(): pl.pallas_call(functools.partial(standardize_kernel, types, cap, lead, se...  6.7 us
    ppermute x4, waiting for transfers between devices, across(): lax.ppermute(panel_, 'blk', [(b, (b + by * cores) % blocks) for b in rang...  4.48 us
    ppermute x4, starting transfers between devices, across(): lax.ppermute(panel_, 'blk', [(b, (b + by * cores) % blocks) for b in rang...  3.55 us
    unnamed x8, local copies, waits for them, and re-layouts  3.27 us
    pallas_call x1, Pallas kernels, pack(): pl.pallas_call(functools.partial(pack_kernel, types, cap, widths), out_sh...  1.71 us
  transfers between devices with their start and end apart: 20, of which 10 were waited for; matrix products, arithmetic and copies ran while one was open for 0% of the time, Pallas kernels for 27%

profile of v12, /device:TPU:0, one launch (start us, length us, event | category | flops | bytes accessed | tf_op | source)
XLA Modules:
  0.0 76.9 jit_solution(7791575818315408971)
XLA Ops:
  0.0 1.2 %copy-done = bf16[512,1024]{1,0:T(8,128)(2,1)S(1)} copy-done((bf16[512,1024]{1,0:T(8,128)(2,1)S(1)}, bf16[512,1024]{1,0:T(8,128)(2,1)}, u32[]{:S(2)}) %copy-start) | copy-done | bytes 1048600
  1.2 0.7 copy-done.1
  1.9 0.7 copy-done.2
  2.6 1.7 %pack.1 = (bf16[272,256]{1,0:T(8,128)(2,1)S(1)}, bf16[272,256]{1,0:T(8,128)(2,1)S(1)}, bf16[272,256]{1,0:T(8,128)(2,1)S(1)}, bf16[272,256]{1,0:T(8,128)(2,1)S(1)...) custom-call(s32[512]{0:T(512)S(1)} %copy-done.1, ...), custom_call_target="tpu_custom_call" | custom-call | flops 1024 | bytes 1024 | tf_op jit(solution)/shard_map/pack/pallas_call | solution.py:68
  4.3 5.1 %collective-permute-start.4 = (bf16[272,256]{1,0:T(8,128)(2,1)S(1)}, bf16[272,256]{1,0:T(8,128)(2,1)S(1)}, u32[]{:S(2)}, u32[]{:S(2)}) collective-permute-start(bf16[272,256]{1,0:T(8,128)(2,1)S(1)} %get-tuple-element.57), channel_id=1, source_target_pairs={{0,12},{4,8},{8,4},{12,0},{1,13},{5,9},{9,5},{13,1},{2,14},{6,10},... | collective-permute-start | bytes 417800 | tf_op jit(solution)/shard_map/cells_3_chunk_0/ppermute | solution.py:311
  9.4 0.0 collective-permute-start.2
  9.4 0.6 collective-permute-start
  10.1 3.9 %collective-permute-done.4.refs_3_.refs_7_ = bf16[272,256]{1,0:T(8,128)(2,1)S(1)} collective-permute-done((bf16[272,256]{1,0:T(8,128)(2,1)S(1)}, bf16[272,256]{1,0:T(8,128)(2,1)S(1)}, u32[]{:S(2)}, u32[]{:S(2)}) %collective-permute-start.4) | collective-permute-done | bytes 139296 | tf_op jit(solution)/shard_map/cells_3_chunk_0/ppermute | solution.py:311
  14.0 3.8 %collective-permute-start.5 = (bf16[256,256]{1,0:T(8,128)(2,1)S(1)}, bf16[256,256]{1,0:T(8,128)(2,1)S(1)}, u32[]{:S(2)}, u32[]{:S(2)}) collective-permute-start(bf16[256,256]{1,0:T(8,128)(2,1)S(1)} %get-tuple-element.58), channel_id=1, source_target_pairs={{0,12},{4,8},{8,4},{12,0},{1,13},{5,9},{9,5},{13,1},{2,14},{6,10},... | collective-permute-start | bytes 393224 | tf_op jit(solution)/shard_map/cells_3_chunk_1/ppermute | solution.py:311
  17.8 0.0 collective-permute-done.2.refs_2_.refs_6_
  17.8 1.2 %collective-permute-start.3 = (bf16[256,256]{1,0:T(8,128)(2,1)S(1)}, bf16[256,256]{1,0:T(8,128)(2,1)S(1)}, u32[]{:S(2)}, u32[]{:S(2)}) collective-permute-start(bf16[256,256]{1,0:T(8,128)(2,1)S(1)} %get-tuple-element.55), channel_id=1, source_target_pairs={{0,4},{4,0},{8,12},{12,8},{1,5},{5,1},{9,13},{13,9},{2,6},{6,2},{1... | collective-permute-start | bytes 393224 | tf_op jit(solution)/shard_map/cells_1_chunk_1/ppermute | solution.py:311
  19.0 7.5 %collective-permute-done.refs_1_.refs_5_ = bf16[272,256]{1,0:T(8,128)(2,1)S(1)} collective-permute-done((bf16[272,256]{1,0:T(8,128)(2,1)S(1)}, bf16[272,256]{1,0:T(8,128)(2,1)S(1)}, u32[]{:S(2)}, u32[]{:S(2)}) %collective-permute-start) | collective-permute-done | bytes 139296 | tf_op jit(solution)/shard_map/cells_2_chunk_0/ppermute | solution.py:311
  26.4 0.0 collective-permute-start.1
  26.4 0.7 copy-done.3
  27.1 1.8 %standardize.4 = (bf16[1024,256]{1,0:T(8,128)(2,1)S(1)}, bf16[1024,1024]{1,0:T(8,128)(2,1)S(1)}, f32[8,128]{1,0:T(8,128)}, bf16[1024,1024]{1,0:T(8,128)(2,1)S(1)}) custom-call(f32[1,1024]{1,0:T(1,128)S(1)} %bitcast.1, bf16[272,256]{1,0:T(8,128)(2,1)S(1)} %get-tuple-element.59.refs_0_.refs_4_, bf16[272,256]{1,0:T(8,128)(2,1)S(1)} %collective-permute-done.refs_1_.refs_5_, ...), custom_call_target="tpu_custom_call" | custom-call | flops 20000000000 | bytes 1024 | tf_op jit(solution)/shard_map/standardize/pallas_call | solution.py:173
  28.9 1.6 %collective-permute-start.13 = (bf16[1024,256]{1,0:T(8,128)(2,1)S(1)}, bf16[1024,256]{1,0:T(8,128)(2,1)S(1)}, u32[]{:S(2)}, u32[]{:S(2)}) collective-permute-start(bf16[1024,256]{1,0:T(8,128)(2,1)S(1)} %get-tuple-element.76), channel_id=1, source_target_pairs={{0,2},{1,3},{2,0},{3,1},{4,6},{5,7},{6,4},{7,5},{8,10},{9,11},{10,... | collective-permute-start | bytes 1572872 | tf_op jit(solution)/shard_map/far_0/ppermute | solution.py:314
  30.5 0.0 collective-permute-done.5.refs_3_
  30.5 1.0 %collective-permute-start.11 = (bf16[256,256]{1,0:T(8,128)(2,1)S(1)}, bf16[256,256]{1,0:T(8,128)(2,1)S(1)}, u32[]{:S(2)}, u32[]{:S(2)}) collective-permute-start(bf16[256,256]{1,0:T(8,128)(2,1)S(1)} %get-tuple-element.74), channel_id=1, source_target_pairs={{0,12},{4,8},{8,4},{12,0},{1,13},{5,9},{9,5},{13,1},{2,14},{6,10},... | collective-permute-start | bytes 393224 | tf_op jit(solution)/shard_map/cells_3_chunk_2/ppermute | solution.py:311
  31.5 0.0 collective-permute-done.3.refs_2_
  31.5 2.5 %collective-permute-start.9 = (bf16[256,256]{1,0:T(8,128)(2,1)S(1)}, bf16[256,256]{1,0:T(8,128)(2,1)S(1)}, u32[]{:S(2)}, u32[]{:S(2)}) collective-permute-start(bf16[256,256]{1,0:T(8,128)(2,1)S(1)} %get-tuple-element.70), channel_id=1, source_target_pairs={{0,4},{4,0},{8,12},{12,8},{1,5},{5,1},{9,13},{13,9},{2,6},{6,2},{1... | collective-permute-start | bytes 393224 | tf_op jit(solution)/shard_map/cells_1_chunk_2/ppermute | solution.py:311
  34.0 1.2 %collective-permute-done.1.refs_1_ = bf16[256,256]{1,0:T(8,128)(2,1)S(1)} collective-permute-done((bf16[256,256]{1,0:T(8,128)(2,1)S(1)}, bf16[256,256]{1,0:T(8,128)(2,1)S(1)}, u32[]{:S(2)}, u32[]{:S(2)}) %collective-permute-start.1) | collective-permute-done | bytes 131104 | tf_op jit(solution)/shard_map/cells_2_chunk_1/ppermute | solution.py:311
  35.2 0.0 collective-permute-start.7
  35.2 1.8 %standardize.5 = (bf16[1024,256]{1,0:T(8,128)(2,1)S(1)}, bf16[1024,1024]{1,0:T(8,128)(2,1)S(1)}, f32[8,128]{1,0:T(8,128)}, bf16[1024,1024]{1,0:T(8,128)(2,1)S(1)}) custom-call(f32[1,1024]{1,0:T(1,128)S(1)} %bitcast.2, bf16[256,256]{1,0:T(8,128)(2,1)S(1)} %get-tuple-element.49.refs_0_, ...), custom_call_target="tpu_custom_call", output_to_operand_aliasing={{1}: (9, {}), {3}: (10, {})} | custom-call | flops 20000000000 | bytes 1024 | tf_op jit(solution)/shard_map/standardize/pallas_call | solution.py:173
  37.0 1.3 %collective-permute-start.6 = (bf16[1024,256]{1,0:T(8,128)(2,1)S(1)}, bf16[1024,256]{1,0:T(8,128)(2,1)S(1)}, u32[]{:S(2)}, u32[]{:S(2)}) collective-permute-start(bf16[1024,256]{1,0:T(8,128)(2,1)S(1)} %get-tuple-element.62), channel_id=1, source_target_pairs={{0,2},{1,3},{2,0},{3,1},{4,6},{5,7},{6,4},{7,5},{8,10},{9,11},{10,... | collective-permute-start | bytes 1572872 | tf_op jit(solution)/shard_map/far_1/ppermute | solution.py:314
  38.2 0.2 collective-permute-done.11.refs_3_
  38.4 5.0 %collective-permute-start.12 = (bf16[256,256]{1,0:T(8,128)(2,1)S(1)}, bf16[256,256]{1,0:T(8,128)(2,1)S(1)}, u32[]{:S(2)}, u32[]{:S(2)}) collective-permute-start(bf16[256,256]{1,0:T(8,128)(2,1)S(1)} %get-tuple-element.75), channel_id=1, source_target_pairs={{0,12},{4,8},{8,4},{12,0},{1,13},{5,9},{9,5},{13,1},{2,14},{6,10},... | collective-permute-start | bytes 393224 | tf_op jit(solution)/shard_map/cells_3_chunk_3/ppermute | solution.py:311
  43.4 0.0 collective-permute-done.9.refs_2_
  43.4 2.1 %collective-permute-start.10 = (bf16[256,256]{1,0:T(8,128)(2,1)S(1)}, bf16[256,256]{1,0:T(8,128)(2,1)S(1)}, u32[]{:S(2)}, u32[]{:S(2)}) collective-permute-start(bf16[256,256]{1,0:T(8,128)(2,1)S(1)} %get-tuple-element.71), channel_id=1, source_target_pairs={{0,4},{4,0},{8,12},{12,8},{1,5},{5,1},{9,13},{13,9},{2,6},{6,2},{1... | collective-permute-start | bytes 393224 | tf_op jit(solution)/shard_map/cells_1_chunk_3/ppermute | solution.py:311
  45.5 3.7 %collective-permute-done.7.refs_1_ = bf16[256,256]{1,0:T(8,128)(2,1)S(1)} collective-permute-done((bf16[256,256]{1,0:T(8,128)(2,1)S(1)}, bf16[256,256]{1,0:T(8,128)(2,1)S(1)}, u32[]{:S(2)}, u32[]{:S(2)}) %collective-permute-start.7) | collective-permute-done | bytes 131104 | tf_op jit(solution)/shard_map/cells_2_chunk_2/ppermute | solution.py:311
  49.2 1.8 %standardize.6 = (bf16[1024,256]{1,0:T(8,128)(2,1)S(1)}, bf16[1024,1024]{1,0:T(8,128)(2,1)S(1)}, f32[8,128]{1,0:T(8,128)}, bf16[1024,1024]{1,0:T(8,128)(2,1)S(1)}) custom-call(f32[1,1024]{1,0:T(1,128)S(1)} %bitcast.3, bf16[256,256]{1,0:T(8,128)(2,1)S(1)} %get-tuple-element.78.refs_0_, ...), custom_call_target="tpu_custom_call", output_to_operand_aliasing={{1}: (9, {}), {3}: (10, {})} | custom-call | flops 20000000000 | bytes 1024 | tf_op jit(solution)/shard_map/standardize/pallas_call | solution.py:173
  51.0 0.1 collective-permute-start.17
  51.1 1.9 %collective-permute-done.6.refs_9_ = bf16[1024,256]{1,0:T(8,128)(2,1)S(1)} collective-permute-done((bf16[1024,256]{1,0:T(8,128)(2,1)S(1)}, bf16[1024,256]{1,0:T(8,128)(2,1)S(1)}, u32[]{:S(2)}, u32[]{:S(2)}) %collective-permute-start.6) | collective-permute-done | bytes 524320 | tf_op jit(solution)/shard_map/far_1/ppermute | solution.py:314
  53.0 0.0 collective-permute-done.12.refs_3_
  53.0 2.8 %collective-permute-done.8.refs_1_ = bf16[256,256]{1,0:T(8,128)(2,1)S(1)} collective-permute-done((bf16[256,256]{1,0:T(8,128)(2,1)S(1)}, bf16[256,256]{1,0:T(8,128)(2,1)S(1)}, u32[]{:S(2)}, u32[]{:S(2)}) %collective-permute-start.8) | collective-permute-done | bytes 131104 | tf_op jit(solution)/shard_map/cells_2_chunk_3/ppermute | solution.py:311
  55.8 1.3 %standardize.7 = (bf16[1024,256]{1,0:T(8,128)(2,1)S(1)}, bf16[1024,1024]{1,0:T(8,128)(2,1)S(1)}, f32[8,128]{1,0:T(8,128)S(1)}, bf16[1024,1024]{1,0:T(8,128)(2,1)S(1)}, bf16[1024,512]{1,0:T(8,128)(2,1)S(1)}) custom-call(f32[1,1024]{1,0:T(1,128)S(1)} %bitcast.4, ...), custom_call_target="tpu_custom_call", output_to_operand_aliasing={{1}: (11, {}), {3}: (12, {})} | custom-call | flops 20000000000 | bytes 1024 | tf_op jit(solution)/shard_map/standardize/pallas_call | solution.py:173
  57.2 0.1 collective-permute-start.15
  57.2 0.5 collective-permute-start.16
  57.7 0.6 collective-permute-start.14
  58.4 3.4 %gram.5.refs_2_ = bf16[1,1024,4096]{2,1,0:T(8,128)(2,1)} custom-call(f32[8,128]{1,0:T(8,128)S(1)} %get-tuple-element.83.count_ref, bf16[1024,1024]{1,0:T(8,128)(2,1)S(1)} %get-tuple-element.84.left_ref, bf16[1024,1024]{1,0:T(8,128)(2,1)S(1)} %get-tuple-element.86.refs_0_), custom_call_target="tpu_custom_call" | custom-call | flops 1024 | bytes 1024 | tf_op jit(solution)/shard_map/gram/pallas_call | solution.py:273
  61.7 1.9 %collective-permute-done.17.refs_1_ = bf16[1024,256]{1,0:T(8,128)(2,1)S(1)} collective-permute-done((bf16[1024,256]{1,0:T(8,128)(2,1)S(1)}, bf16[1024,256]{1,0:T(8,128)(2,1)S(1)}, u32[]{:S(2)}, u32[]{:S(2)}) %collective-permute-start.17) | collective-permute-done | bytes 524320 | tf_op jit(solution)/shard_map/far_2/ppermute | solution.py:314
  63.6 0.0 collective-permute-start.18
  63.6 2.9 %gram.6.refs_3_ = bf16[1,1024,4096]{2,1,0:T(8,128)(2,1)} custom-call(f32[8,128]{1,0:T(8,128)S(1)} %get-tuple-element.83.count_ref, bf16[1024,1024]{1,0:T(8,128)(2,1)S(1)} %get-tuple-element.84.left_ref, bf16[1024,512]{1,0:T(8,128)(2,1)S(1)} %get-tuple-element.87.refs_0_, ...), custom_call_target="tpu_custom_call", output_to_operand_aliasing={{}: (4, {})} | custom-call | flops 20000000000 | bytes 1024 | tf_op jit(solution)/shard_map/gram/pallas_call | solution.py:273
  66.5 0.0 collective-permute-done.16.refs_1_
  66.6 6.1 %gram.7.refs_1_ = bf16[1,1024,4096]{2,1,0:T(8,128)(2,1)} custom-call(f32[8,128]{1,0:T(8,128)S(1)} %get-tuple-element.83.count_ref, bf16[1024,1024]{1,0:T(8,128)(2,1)S(1)} %get-tuple-element.84.left_ref, bf16[1024,1024]{1,0:T(8,128)(2,1)S(1)} %collective-permute-done.15.refs_0_, ...), custom_call_target="tpu_custom_call", output_to_operand_aliasing={{}: (5, {})} | custom-call | flops 1024 | bytes 1024 | tf_op jit(solution)/shard_map/gram/pallas_call | solution.py:273
  72.6 0.7 collective-permute-done.14.refs_0_
  73.3 1.5 %gram.8.refs_1_ = bf16[1,1024,4096]{2,1,0:T(8,128)(2,1)} custom-call(f32[8,128]{1,0:T(8,128)S(1)} %get-tuple-element.83.count_ref, bf16[1024,1024]{1,0:T(8,128)(2,1)S(1)} %get-tuple-element.84.left_ref, bf16[1024,256]{1,0:T(8,128)(2,1)S(1)} %collective-permute-done.14.refs_0_, bf16[1,1024,4096]{2,1,0:T(8,128)(2,1)} %gram.7.refs_1_), custom_call_target="tpu_custom_call", output_to_operand_aliasing={{}: (3, {})} | custom-call | flops 1024 | bytes 1024 | tf_op jit(solution)/shard_map/gram/pallas_call | solution.py:273
  74.8 0.4 collective-permute-done.19.refs_0_
  75.2 1.5 %gram.9 = bf16[1,1024,4096]{2,1,0:T(8,128)(2,1)} custom-call(f32[8,128]{1,0:T(8,128)S(1)} %get-tuple-element.83.count_ref, bf16[1024,1024]{1,0:T(8,128)(2,1)S(1)} %get-tuple-element.84.left_ref, bf16[1024,256]{1,0:T(8,128)(2,1)S(1)} %collective-permute-done.19.refs_0_, bf16[1,1024,4096]{2,1,0:T(8,128)(2,1)} %gram.8.refs_1_), custom_call_target="tpu_custom_call", output_to_operand_aliasing={{}: (3, {})} | custom-call | flops 1024 | bytes 1024 | tf_op jit(solution)/shard_map/gram/pallas_call | solution.py:273
  (10 shorter events, 0.0 us)
Async XLA Ops:
  0.0 1.2 %copy-start = (bf16[512,1024]{1,0:T(8,128)(2,1)S(1)}, bf16[512,1024]{1,0:T(8,128)(2,1)}, u32[]{:S(2)}) copy-start(bf16[512,1024]{1,0:T(8,128)(2,1)} %expr_ref.1) | copy-start | bytes 3145732
  1.2 0.7 copy-start.1
  1.9 0.7 copy-start.2
  4.3 9.7 %collective-permute-start.4 = (bf16[272,256]{1,0:T(8,128)(2,1)S(1)}, bf16[272,256]{1,0:T(8,128)(2,1)S(1)}, u32[]{:S(2)}, u32[]{:S(2)}) collective-permute-start(bf16[272,256]{1,0:T(8,128)(2,1)S(1)} %get-tuple-element.57), channel_id=1, source_target_pairs={{0,12},{4,8},{8,4},{12,0},{1,13},{5,9},{9,5},{13,1},{2,14},{6,10},... | collective-permute-start | bytes 417800 | tf_op jit(solution)/shard_map/cells_3_chunk_0/ppermute | solution.py:311
  9.4 8.4 %collective-permute-start.2 = (bf16[272,256]{1,0:T(8,128)(2,1)S(1)}, bf16[272,256]{1,0:T(8,128)(2,1)S(1)}, u32[]{:S(2)}, u32[]{:S(2)}) collective-permute-start(bf16[272,256]{1,0:T(8,128)(2,1)S(1)} %get-tuple-element.54), channel_id=1, source_target_pairs={{0,4},{4,0},{8,12},{12,8},{1,5},{5,1},{9,13},{13,9},{2,6},{6,2},{1... | collective-permute-start | bytes 417800 | tf_op jit(solution)/shard_map/cells_1_chunk_0/ppermute | solution.py:311
  9.4 17.0 %collective-permute-start = (bf16[272,256]{1,0:T(8,128)(2,1)S(1)}, bf16[272,256]{1,0:T(8,128)(2,1)S(1)}, u32[]{:S(2)}, u32[]{:S(2)}) collective-permute-start(bf16[272,256]{1,0:T(8,128)(2,1)S(1)} %get-tuple-element.51), channel_id=1, source_target_pairs={{0,8},{4,12},{8,0},{12,4},{1,9},{5,13},{9,1},{13,5},{2,10},{6,14},... | collective-permute-start | bytes 417800 | tf_op jit(solution)/shard_map/cells_2_chunk_0/ppermute | solution.py:311
  14.0 16.5 %collective-permute-start.5 = (bf16[256,256]{1,0:T(8,128)(2,1)S(1)}, bf16[256,256]{1,0:T(8,128)(2,1)S(1)}, u32[]{:S(2)}, u32[]{:S(2)}) collective-permute-start(bf16[256,256]{1,0:T(8,128)(2,1)S(1)} %get-tuple-element.58), channel_id=1, source_target_pairs={{0,12},{4,8},{8,4},{12,0},{1,13},{5,9},{9,5},{13,1},{2,14},{6,10},... | collective-permute-start | bytes 393224 | tf_op jit(solution)/shard_map/cells_3_chunk_1/ppermute | solution.py:311
  17.8 13.7 %collective-permute-start.3 = (bf16[256,256]{1,0:T(8,128)(2,1)S(1)}, bf16[256,256]{1,0:T(8,128)(2,1)S(1)}, u32[]{:S(2)}, u32[]{:S(2)}) collective-permute-start(bf16[256,256]{1,0:T(8,128)(2,1)S(1)} %get-tuple-element.55), channel_id=1, source_target_pairs={{0,4},{4,0},{8,12},{12,8},{1,5},{5,1},{9,13},{13,9},{2,6},{6,2},{1... | collective-permute-start | bytes 393224 | tf_op jit(solution)/shard_map/cells_1_chunk_1/ppermute | solution.py:311
  26.4 8.7 %collective-permute-start.1 = (bf16[256,256]{1,0:T(8,128)(2,1)S(1)}, bf16[256,256]{1,0:T(8,128)(2,1)S(1)}, u32[]{:S(2)}, u32[]{:S(2)}) collective-permute-start(bf16[256,256]{1,0:T(8,128)(2,1)S(1)} %get-tuple-element.52), channel_id=1, source_target_pairs={{0,8},{4,12},{8,0},{12,4},{1,9},{5,13},{9,1},{13,5},{2,10},{6,14},... | collective-permute-start | bytes 393224 | tf_op jit(solution)/shard_map/cells_2_chunk_1/ppermute | solution.py:311
  26.4 0.7 copy-start.3
  28.9 20.3 %collective-permute-start.13 = (bf16[1024,256]{1,0:T(8,128)(2,1)S(1)}, bf16[1024,256]{1,0:T(8,128)(2,1)S(1)}, u32[]{:S(2)}, u32[]{:S(2)}) collective-permute-start(bf16[1024,256]{1,0:T(8,128)(2,1)S(1)} %get-tuple-element.76), channel_id=1, source_target_pairs={{0,2},{1,3},{2,0},{3,1},{4,6},{5,7},{6,4},{7,5},{8,10},{9,11},{10,... | collective-permute-start | bytes 1572872 | tf_op jit(solution)/shard_map/far_0/ppermute | solution.py:314
  30.5 8.0 %collective-permute-start.11 = (bf16[256,256]{1,0:T(8,128)(2,1)S(1)}, bf16[256,256]{1,0:T(8,128)(2,1)S(1)}, u32[]{:S(2)}, u32[]{:S(2)}) collective-permute-start(bf16[256,256]{1,0:T(8,128)(2,1)S(1)} %get-tuple-element.74), channel_id=1, source_target_pairs={{0,12},{4,8},{8,4},{12,0},{1,13},{5,9},{9,5},{13,1},{2,14},{6,10},... | collective-permute-start | bytes 393224 | tf_op jit(solution)/shard_map/cells_3_chunk_2/ppermute | solution.py:311
  31.5 12.0 %collective-permute-start.9 = (bf16[256,256]{1,0:T(8,128)(2,1)S(1)}, bf16[256,256]{1,0:T(8,128)(2,1)S(1)}, u32[]{:S(2)}, u32[]{:S(2)}) collective-permute-start(bf16[256,256]{1,0:T(8,128)(2,1)S(1)} %get-tuple-element.70), channel_id=1, source_target_pairs={{0,4},{4,0},{8,12},{12,8},{1,5},{5,1},{9,13},{13,9},{2,6},{6,2},{1... | collective-permute-start | bytes 393224 | tf_op jit(solution)/shard_map/cells_1_chunk_2/ppermute | solution.py:311
  35.2 14.0 %collective-permute-start.7 = (bf16[256,256]{1,0:T(8,128)(2,1)S(1)}, bf16[256,256]{1,0:T(8,128)(2,1)S(1)}, u32[]{:S(2)}, u32[]{:S(2)}) collective-permute-start(bf16[256,256]{1,0:T(8,128)(2,1)S(1)} %get-tuple-element.66), channel_id=1, source_target_pairs={{0,8},{4,12},{8,0},{12,4},{1,9},{5,13},{9,1},{13,5},{2,10},{6,14},... | collective-permute-start | bytes 393224 | tf_op jit(solution)/shard_map/cells_2_chunk_2/ppermute | solution.py:311
  37.0 16.1 %collective-permute-start.6 = (bf16[1024,256]{1,0:T(8,128)(2,1)S(1)}, bf16[1024,256]{1,0:T(8,128)(2,1)S(1)}, u32[]{:S(2)}, u32[]{:S(2)}) collective-permute-start(bf16[1024,256]{1,0:T(8,128)(2,1)S(1)} %get-tuple-element.62), channel_id=1, source_target_pairs={{0,2},{1,3},{2,0},{3,1},{4,6},{5,7},{6,4},{7,5},{8,10},{9,11},{10,... | collective-permute-start | bytes 1572872 | tf_op jit(solution)/shard_map/far_1/ppermute | solution.py:314
  38.4 14.6 %collective-permute-start.12 = (bf16[256,256]{1,0:T(8,128)(2,1)S(1)}, bf16[256,256]{1,0:T(8,128)(2,1)S(1)}, u32[]{:S(2)}, u32[]{:S(2)}) collective-permute-start(bf16[256,256]{1,0:T(8,128)(2,1)S(1)} %get-tuple-element.75), channel_id=1, source_target_pairs={{0,12},{4,8},{8,4},{12,0},{1,13},{5,9},{9,5},{13,1},{2,14},{6,10},... | collective-permute-start | bytes 393224 | tf_op jit(solution)/shard_map/cells_3_chunk_3/ppermute | solution.py:311
  43.4 9.6 %collective-permute-start.10 = (bf16[256,256]{1,0:T(8,128)(2,1)S(1)}, bf16[256,256]{1,0:T(8,128)(2,1)S(1)}, u32[]{:S(2)}, u32[]{:S(2)}) collective-permute-start(bf16[256,256]{1,0:T(8,128)(2,1)S(1)} %get-tuple-element.71), channel_id=1, source_target_pairs={{0,4},{4,0},{8,12},{12,8},{1,5},{5,1},{9,13},{13,9},{2,6},{6,2},{1... | collective-permute-start | bytes 393224 | tf_op jit(solution)/shard_map/cells_1_chunk_3/ppermute | solution.py:311
  49.2 6.6 %collective-permute-start.8 = (bf16[256,256]{1,0:T(8,128)(2,1)S(1)}, bf16[256,256]{1,0:T(8,128)(2,1)S(1)}, u32[]{:S(2)}, u32[]{:S(2)}) collective-permute-start(bf16[256,256]{1,0:T(8,128)(2,1)S(1)} %get-tuple-element.67), channel_id=1, source_target_pairs={{0,8},{4,12},{8,0},{12,4},{1,9},{5,13},{9,1},{13,5},{2,10},{6,14},... | collective-permute-start | bytes 393224 | tf_op jit(solution)/shard_map/cells_2_chunk_3/ppermute | solution.py:311
  51.0 12.6 %collective-permute-start.17 = (bf16[1024,256]{1,0:T(8,128)(2,1)S(1)}, bf16[1024,256]{1,0:T(8,128)(2,1)S(1)}, u32[]{:S(2)}, u32[]{:S(2)}) collective-permute-start(bf16[1024,256]{1,0:T(8,128)(2,1)S(1)} %get-tuple-element.88), channel_id=1, source_target_pairs={{0,2},{1,3},{2,0},{3,1},{4,6},{5,7},{6,4},{7,5},{8,10},{9,11},{10,... | collective-permute-start | bytes 1572872 | tf_op jit(solution)/shard_map/far_2/ppermute | solution.py:314
  57.2 9.4 %collective-permute-start.15 = (bf16[1024,1024]{1,0:T(8,128)(2,1)S(1)}, bf16[1024,1024]{1,0:T(8,128)(2,1)S(1)}, u32[]{:S(2)}, u32[]{:S(2)}) collective-permute-start(bf16[1024,1024]{1,0:T(8,128)(2,1)S(1)} %get-tuple-element.86.refs_0_), channel_id=1, source_target_pairs={{0,1},{1,0},{2,3},{3,2},{4,5},{5,4},{6,7},{7,6},{8,9},{9,8},{10,11... | collective-permute-start | bytes 6291464 | tf_op jit(solution)/shard_map/near/ppermute | solution.py:318
  57.2 9.3 %collective-permute-start.16 = (bf16[1024,512]{1,0:T(8,128)(2,1)S(1)}, bf16[1024,512]{1,0:T(8,128)(2,1)S(1)}, u32[]{:S(2)}, u32[]{:S(2)}) collective-permute-start(bf16[1024,512]{1,0:T(8,128)(2,1)S(1)} %get-tuple-element.87.refs_0_), channel_id=1, source_target_pairs={{0,1},{1,0},{2,3},{3,2},{4,5},{5,4},{6,7},{7,6},{8,9},{9,8},{10,11... | collective-permute-start | bytes 3145736 | tf_op jit(solution)/shard_map/far_near/ppermute | solution.py:318
  57.7 15.6 %collective-permute-start.14 = (bf16[1024,256]{1,0:T(8,128)(2,1)S(1)}, bf16[1024,256]{1,0:T(8,128)(2,1)S(1)}, u32[]{:S(2)}, u32[]{:S(2)}) collective-permute-start(bf16[1024,256]{1,0:T(8,128)(2,1)S(1)} %get-tuple-element.85), channel_id=1, source_target_pairs={{0,2},{1,3},{2,0},{3,1},{4,6},{5,7},{6,4},{7,5},{8,10},{9,11},{10,... | collective-permute-start | bytes 1572872 | tf_op jit(solution)/shard_map/far_3/ppermute | solution.py:314
  63.6 2.9 %collective-permute-start.18 = (bf16[1024,256]{1,0:T(8,128)(2,1)S(1)}, bf16[1024,256]{1,0:T(8,128)(2,1)S(1)}, u32[]{:S(2)}, u32[]{:S(2)}) collective-permute-start(bf16[1024,256]{1,0:T(8,128)(2,1)S(1)} %collective-permute-done.17.refs_1_), channel_id=1, source_target_pairs={{0,1},{1,0},{2,3},{3,2},{4,5},{5,4},{6,7},{7,6},{8,9},{9,8},{10,11... | collective-permute-start | bytes 1572872 | tf_op jit(solution)/shard_map/far_near_2/ppermute | solution.py:318
  73.3 1.9 %collective-permute-start.19 = (bf16[1024,256]{1,0:T(8,128)(2,1)S(1)}, bf16[1024,256]{1,0:T(8,128)(2,1)S(1)}, u32[]{:S(2)}, u32[]{:S(2)}) collective-permute-start(bf16[1024,256]{1,0:T(8,128)(2,1)S(1)} %collective-permute-done.14.refs_0_), channel_id=1, source_target_pairs={{0,1},{1,0},{2,3},{3,2},{4,5},{5,4},{6,7},{7,6},{8,9},{9,8},{10,11... | collective-permute-start | bytes 1572872 | tf_op jit(solution)/shard_map/far_near_3/ppermute | solution.py:318

commit v13 on v12

--- a/solution.py
+++ b/solution.py
@@ -339,25 +339,29 @@
         scaled, left, count, own, *joined = standardize(
             types, cap, mean, starts[k], arrived, first, left, own, gather
         )
-        with jax.named_scope(f"far_{k}"):
-            far.append([across(scaled, d) for d in range(1, chips)])
+        if k < chunks - 1:
+            with jax.named_scope(f"far_{k}"):
+                far.append([across(scaled, d) for d in range(1, chips)])
 
     multiply = functools.partial(gram, blocks, cores, count, left)
     last = chunks - 1
     near = side("near", own)
     joined_near = [[side("far_near", p)] for p in joined] or [[]] * (chips - 1)
     joined = [[p] for p in joined] or [[]] * (chips - 1)
-    out = multiply([([own], (0, 0, 0))], None, brief)
+    groups = [([own], (0, 0, 0))] + [(p, (d, 0, 0)) for d, p in enumerate(joined, 1) if p]
+    out = multiply(groups, None, brief)
+    final = [across(after(scaled, out), d) for d in range(1, chips)]
     second = [side(f"far_near_{last - 1}", p, own) for p in far[last - 1]]
-    groups = [([*p, far[last - 1][i]], (i + 1, 0, 0)) for i, p in enumerate(joined)]
+    edge = starts[last - 1]
+    groups = [([p], (d, 0, edge)) for d, p in enumerate(far[last - 1], 1)]
     out = multiply(groups, out, lengthy)
     groups = [([near], (0, 1, 0))]
     groups += [([*p, second[i]], (i + 1, 1, 0)) for i, p in enumerate(joined_near)]
     out = multiply(groups, out, brief)
-    final = [side(f"far_near_{last}", p, out) for p in far[last]]
+    final_near = [side(f"far_near_{last}", p, out) for p in final]
     edge = starts[last]
-    out = multiply([([p], (d, 0, edge)) for d, p in enumerate(far[last], 1)], out, brief)
-    return multiply([([p], (d, 1, edge)) for d, p in enumerate(final, 1)], out, brief)
+    out = multiply([([p], (d, 0, edge)) for d, p in enumerate(final, 1)], out, brief)
+    return multiply([([p], (d, 1, edge)) for d, p in enumerate(final_near, 1)], out, brief)
 
 
 def solution(mesh):

time: 78.4 us -> 80.4 us (1.026); the launches traced: 76.9 us -> 80.2 us
  waiting for transfers between devices: 24.1 us -> 27.2 us
    ppermute x4, waiting for transfers between devices: 4.48 us -> 6.73 us  [across(): lax.ppermute(panel_, 'blk', [(b, (b + by * cores) % blocks) for b in rang...]
    ppermute x4, waiting for transfers between devices: 0.37 us -> 1.25 us  [side(): lax.ppermute(after(panel_, *waits), 'blk', [(b, b ^ 1) for b in range(blo...]
    unnamed x8 -> x10, local copies, waits for them, and re-layouts: 3.27 us -> 3.27 us
  transfers between devices with their start and end apart: 20 -> 20, of which waited for: 10 -> 10; matrix products, arithmetic and copies ran while one was open for 0% -> 0% of each run, Pallas kernels for 27% -> 26%
where the time goes in v13:
time: 80.4 us; the launch traced here: 80.2 us
  waiting for transfers between devices  27.2 us (34%)
  starting transfers between devices  25.5 us (32%)
  Pallas kernels  23.9 us (30%)
  local copies, waits for them, and re-layouts  3.27 us (4%)
    ppermute x12, starting transfers between devices, swap(): return lax.ppermute(block, 'cells', [(s, s ^ by) for s in range(types)])  21.3 us
    ppermute x12, waiting for transfers between devices, swap(): return lax.ppermute(block, 'cells', [(s, s ^ by) for s in range(types)])  19.3 us
    pallas_call x5, Pallas kernels, gram(): pl.pallas_call(functools.partial(gram_kernel, blocks, cores, strip, layou...  15.5 us
    ppermute x4, waiting for transfers between devices, across(): lax.ppermute(panel_, 'blk', [(b, (b + by * cores) % blocks) for b in rang...  6.73 us
    pallas_call x4, Pallas kernels, standardize(): pl.pallas_call(functools.partial(standardize_kernel, types, cap, lead, se...  6.71 us
    ppermute x4, starting transfers between devices, across(): lax.ppermute(panel_, 'blk', [(b, (b + by * cores) % blocks) for b in rang...  3.5 us
    unnamed x10, local copies, waits for them, and re-layouts  3.27 us
    pallas_call x1, Pallas kernels, pack(): pl.pallas_call(functools.partial(pack_kernel, types, cap, widths), out_sh...  1.71 us
  transfers between devices with their start and end apart: 20, of which 10 were waited for; matrix products, arithmetic and copies ran while one was open for 0% of the time, Pallas kernels for 26%

profile of v13, /device:TPU:0, one launch (start us, length us, event | category | flops | bytes accessed | tf_op | source)
XLA Modules:
  0.0 80.2 jit_solution(9628406779594237885)
XLA Ops:
  0.0 1.2 %copy-done = bf16[512,1024]{1,0:T(8,128)(2,1)S(1)} copy-done((bf16[512,1024]{1,0:T(8,128)(2,1)S(1)}, bf16[512,1024]{1,0:T(8,128)(2,1)}, u32[]{:S(2)}) %copy-start) | copy-done | bytes 1048600
  1.2 0.7 copy-done.1
  1.9 0.7 copy-done.2
  2.6 1.7 %pack.1 = (bf16[272,256]{1,0:T(8,128)(2,1)S(1)}, bf16[272,256]{1,0:T(8,128)(2,1)S(1)}, bf16[272,256]{1,0:T(8,128)(2,1)S(1)}, bf16[272,256]{1,0:T(8,128)(2,1)S(1)...) custom-call(s32[512]{0:T(512)S(1)} %copy-done.1, ...), custom_call_target="tpu_custom_call" | custom-call | flops 1024 | bytes 1024 | tf_op jit(solution)/shard_map/pack/pallas_call | solution.py:68
  4.3 5.1 %collective-permute-start.4 = (bf16[272,256]{1,0:T(8,128)(2,1)S(1)}, bf16[272,256]{1,0:T(8,128)(2,1)S(1)}, u32[]{:S(2)}, u32[]{:S(2)}) collective-permute-start(bf16[272,256]{1,0:T(8,128)(2,1)S(1)} %get-tuple-element.58), channel_id=1, source_target_pairs={{0,12},{4,8},{8,4},{12,0},{1,13},{5,9},{9,5},{13,1},{2,14},{6,10},... | collective-permute-start | bytes 417800 | tf_op jit(solution)/shard_map/cells_3_chunk_0/ppermute | solution.py:311
  9.4 0.0 collective-permute-start.2
  9.4 0.6 collective-permute-start
  10.1 3.9 %collective-permute-done.4.refs_3_.refs_7_ = bf16[272,256]{1,0:T(8,128)(2,1)S(1)} collective-permute-done((bf16[272,256]{1,0:T(8,128)(2,1)S(1)}, bf16[272,256]{1,0:T(8,128)(2,1)S(1)}, u32[]{:S(2)}, u32[]{:S(2)}) %collective-permute-start.4) | collective-permute-done | bytes 139296 | tf_op jit(solution)/shard_map/cells_3_chunk_0/ppermute | solution.py:311
  14.0 3.8 %collective-permute-start.5 = (bf16[256,256]{1,0:T(8,128)(2,1)S(1)}, bf16[256,256]{1,0:T(8,128)(2,1)S(1)}, u32[]{:S(2)}, u32[]{:S(2)}) collective-permute-start(bf16[256,256]{1,0:T(8,128)(2,1)S(1)} %get-tuple-element.59), channel_id=1, source_target_pairs={{0,12},{4,8},{8,4},{12,0},{1,13},{5,9},{9,5},{13,1},{2,14},{6,10},... | collective-permute-start | bytes 393224 | tf_op jit(solution)/shard_map/cells_3_chunk_1/ppermute | solution.py:311
  17.8 1.2 %collective-permute-start.3 = (bf16[256,256]{1,0:T(8,128)(2,1)S(1)}, bf16[256,256]{1,0:T(8,128)(2,1)S(1)}, u32[]{:S(2)}, u32[]{:S(2)}) collective-permute-start(bf16[256,256]{1,0:T(8,128)(2,1)S(1)} %get-tuple-element.56), channel_id=1, source_target_pairs={{0,4},{4,0},{8,12},{12,8},{1,5},{5,1},{9,13},{13,9},{2,6},{6,2},{1... | collective-permute-start | bytes 393224 | tf_op jit(solution)/shard_map/cells_1_chunk_1/ppermute | solution.py:311
  19.0 7.5 %collective-permute-done.refs_1_.refs_5_ = bf16[272,256]{1,0:T(8,128)(2,1)S(1)} collective-permute-done((bf16[272,256]{1,0:T(8,128)(2,1)S(1)}, bf16[272,256]{1,0:T(8,128)(2,1)S(1)}, u32[]{:S(2)}, u32[]{:S(2)}) %collective-permute-start) | collective-permute-done | bytes 139296 | tf_op jit(solution)/shard_map/cells_2_chunk_0/ppermute | solution.py:311
  26.4 0.0 collective-permute-start.1
  26.4 0.7 copy-done.3
  27.1 1.8 %standardize.4 = (bf16[1024,256]{1,0:T(8,128)(2,1)S(1)}, bf16[1024,1024]{1,0:T(8,128)(2,1)S(1)}, f32[8,128]{1,0:T(8,128)}, bf16[1024,1024]{1,0:T(8,128)(2,1)S(1)}) custom-call(f32[1,1024]{1,0:T(1,128)S(1)} %bitcast.1, bf16[272,256]{1,0:T(8,128)(2,1)S(1)} %get-tuple-element.60.refs_0_.refs_4_, bf16[272,256]{1,0:T(8,128)(2,1)S(1)} %collective-permute-done.refs_1_.refs_5_, ...), custom_call_target="tpu_custom_call" | custom-call | flops 20000000000 | bytes 1024 | tf_op jit(solution)/shard_map/standardize/pallas_call | solution.py:173
  28.9 1.6 %collective-permute-start.13 = (bf16[1024,256]{1,0:T(8,128)(2,1)S(1)}, bf16[1024,256]{1,0:T(8,128)(2,1)S(1)}, u32[]{:S(2)}, u32[]{:S(2)}) collective-permute-start(bf16[1024,256]{1,0:T(8,128)(2,1)S(1)} %get-tuple-element.77), channel_id=1, source_target_pairs={{0,2},{1,3},{2,0},{3,1},{4,6},{5,7},{6,4},{7,5},{8,10},{9,11},{10,... | collective-permute-start | bytes 1572872 | tf_op jit(solution)/shard_map/far_0/ppermute | solution.py:314
  30.5 0.0 collective-permute-done.5.refs_3_
  30.5 1.0 %collective-permute-start.11 = (bf16[256,256]{1,0:T(8,128)(2,1)S(1)}, bf16[256,256]{1,0:T(8,128)(2,1)S(1)}, u32[]{:S(2)}, u32[]{:S(2)}) collective-permute-start(bf16[256,256]{1,0:T(8,128)(2,1)S(1)} %get-tuple-element.75), channel_id=1, source_target_pairs={{0,12},{4,8},{8,4},{12,0},{1,13},{5,9},{9,5},{13,1},{2,14},{6,10},... | collective-permute-start | bytes 393224 | tf_op jit(solution)/shard_map/cells_3_chunk_2/ppermute | solution.py:311
  31.5 0.0 collective-permute-done.3.refs_2_
  31.5 2.5 %collective-permute-start.9 = (bf16[256,256]{1,0:T(8,128)(2,1)S(1)}, bf16[256,256]{1,0:T(8,128)(2,1)S(1)}, u32[]{:S(2)}, u32[]{:S(2)}) collective-permute-start(bf16[256,256]{1,0:T(8,128)(2,1)S(1)} %get-tuple-element.71), channel_id=1, source_target_pairs={{0,4},{4,0},{8,12},{12,8},{1,5},{5,1},{9,13},{13,9},{2,6},{6,2},{1... | collective-permute-start | bytes 393224 | tf_op jit(solution)/shard_map/cells_1_chunk_2/ppermute | solution.py:311
  34.0 1.2 %collective-permute-done.1.refs_1_ = bf16[256,256]{1,0:T(8,128)(2,1)S(1)} collective-permute-done((bf16[256,256]{1,0:T(8,128)(2,1)S(1)}, bf16[256,256]{1,0:T(8,128)(2,1)S(1)}, u32[]{:S(2)}, u32[]{:S(2)}) %collective-permute-start.1) | collective-permute-done | bytes 131104 | tf_op jit(solution)/shard_map/cells_2_chunk_1/ppermute | solution.py:311
  35.2 1.8 %standardize.5 = (bf16[1024,256]{1,0:T(8,128)(2,1)S(1)}, bf16[1024,1024]{1,0:T(8,128)(2,1)S(1)}, f32[8,128]{1,0:T(8,128)}, bf16[1024,1024]{1,0:T(8,128)(2,1)S(1)}) custom-call(f32[1,1024]{1,0:T(1,128)S(1)} %bitcast.2, bf16[256,256]{1,0:T(8,128)(2,1)S(1)} %get-tuple-element.50.refs_0_, ...), custom_call_target="tpu_custom_call", output_to_operand_aliasing={{1}: (9, {}), {3}: (10, {})} | custom-call | flops 20000000000 | bytes 1024 | tf_op jit(solution)/shard_map/standardize/pallas_call | solution.py:173
  37.0 1.3 %collective-permute-start.6 = (bf16[1024,256]{1,0:T(8,128)(2,1)S(1)}, bf16[1024,256]{1,0:T(8,128)(2,1)S(1)}, u32[]{:S(2)}, u32[]{:S(2)}) collective-permute-start(bf16[1024,256]{1,0:T(8,128)(2,1)S(1)} %get-tuple-element.63), channel_id=1, source_target_pairs={{0,2},{1,3},{2,0},{3,1},{4,6},{5,7},{6,4},{7,5},{8,10},{9,11},{10,... | collective-permute-start | bytes 1572872 | tf_op jit(solution)/shard_map/far_1/ppermute | solution.py:314
  38.2 0.2 collective-permute-done.11.refs_3_
  38.4 5.0 %collective-permute-start.12 = (bf16[256,256]{1,0:T(8,128)(2,1)S(1)}, bf16[256,256]{1,0:T(8,128)(2,1)S(1)}, u32[]{:S(2)}, u32[]{:S(2)}) collective-permute-start(bf16[256,256]{1,0:T(8,128)(2,1)S(1)} %get-tuple-element.76), channel_id=1, source_target_pairs={{0,12},{4,8},{8,4},{12,0},{1,13},{5,9},{9,5},{13,1},{2,14},{6,10},... | collective-permute-start | bytes 393224 | tf_op jit(solution)/shard_map/cells_3_chunk_3/ppermute | solution.py:311
  43.4 0.0 collective-permute-done.9.refs_2_
  43.4 2.1 %collective-permute-start.10 = (bf16[256,256]{1,0:T(8,128)(2,1)S(1)}, bf16[256,256]{1,0:T(8,128)(2,1)S(1)}, u32[]{:S(2)}, u32[]{:S(2)}) collective-permute-start(bf16[256,256]{1,0:T(8,128)(2,1)S(1)} %get-tuple-element.72), channel_id=1, source_target_pairs={{0,4},{4,0},{8,12},{12,8},{1,5},{5,1},{9,13},{13,9},{2,6},{6,2},{1... | collective-permute-start | bytes 393224 | tf_op jit(solution)/shard_map/cells_1_chunk_3/ppermute | solution.py:311
  45.5 3.7 %collective-permute-done.7.refs_1_ = bf16[256,256]{1,0:T(8,128)(2,1)S(1)} collective-permute-done((bf16[256,256]{1,0:T(8,128)(2,1)S(1)}, bf16[256,256]{1,0:T(8,128)(2,1)S(1)}, u32[]{:S(2)}, u32[]{:S(2)}) %collective-permute-start.7) | collective-permute-done | bytes 131104 | tf_op jit(solution)/shard_map/cells_2_chunk_2/ppermute | solution.py:311
  49.2 0.0 collective-permute-start.8
  49.2 0.0 collective-permute-done.13.refs_8_
  49.2 1.8 %standardize.6 = (bf16[1024,256]{1,0:T(8,128)(2,1)S(1)}, bf16[1024,1024]{1,0:T(8,128)(2,1)S(1)}, f32[8,128]{1,0:T(8,128)}, bf16[1024,1024]{1,0:T(8,128)(2,1)S(1)}) custom-call(f32[1,1024]{1,0:T(1,128)S(1)} %bitcast.3, bf16[256,256]{1,0:T(8,128)(2,1)S(1)} %get-tuple-element.79.refs_0_, ...), custom_call_target="tpu_custom_call", output_to_operand_aliasing={{1}: (9, {}), {3}: (10, {})} | custom-call | flops 20000000000 | bytes 1024 | tf_op jit(solution)/shard_map/standardize/pallas_call | solution.py:173
  51.0 0.1 collective-permute-start.17
  51.1 1.9 %collective-permute-done.6.refs_9_ = bf16[1024,256]{1,0:T(8,128)(2,1)S(1)} collective-permute-done((bf16[1024,256]{1,0:T(8,128)(2,1)S(1)}, bf16[1024,256]{1,0:T(8,128)(2,1)S(1)}, u32[]{:S(2)}, u32[]{:S(2)}) %collective-permute-start.6) | collective-permute-done | bytes 524320 | tf_op jit(solution)/shard_map/far_1/ppermute | solution.py:314
  53.0 2.8 %collective-permute-done.8.refs_1_ = bf16[256,256]{1,0:T(8,128)(2,1)S(1)} collective-permute-done((bf16[256,256]{1,0:T(8,128)(2,1)S(1)}, bf16[256,256]{1,0:T(8,128)(2,1)S(1)}, u32[]{:S(2)}, u32[]{:S(2)}) %collective-permute-start.8) | collective-permute-done | bytes 131104 | tf_op jit(solution)/shard_map/cells_2_chunk_3/ppermute | solution.py:311
  55.9 1.3 %standardize.7 = (bf16[1024,256]{1,0:T(8,128)(2,1)S(1)}, bf16[1024,1024]{1,0:T(8,128)(2,1)S(1)}, f32[8,128]{1,0:T(8,128)S(1)}, bf16[1024,1024]{1,0:T(8,128)(2,1)S(1)}, bf16[1024,512]{1,0:T(8,128)(2,1)S(1)}) custom-call(f32[1,1024]{1,0:T(1,128)S(1)} %bitcast.4, ...), custom_call_target="tpu_custom_call", output_to_operand_aliasing={{1}: (11, {}), {3}: (12, {})} | custom-call | flops 20000000000 | bytes 1024 | tf_op jit(solution)/shard_map/standardize/pallas_call | solution.py:173
  57.2 0.1 collective-permute-start.15
  57.3 4.9 %gram.5.refs_1_ = bf16[1,1024,4096]{2,1,0:T(8,128)(2,1)} custom-call(f32[8,128]{1,0:T(8,128)S(1)} %get-tuple-element.84.count_ref, bf16[1024,1024]{1,0:T(8,128)(2,1)S(1)} %get-tuple-element.85.left_ref, bf16[1024,1024]{1,0:T(8,128)(2,1)S(1)} %get-tuple-element.87.refs_0_, bf16[1024,512]{1,0:T(8,128)(2,1)S(1)} %get-tuple-element.88.refs_1_), custom_call_target="tpu_custom_call" | custom-call | flops 1024 | bytes 1024 | tf_op jit(solution)/shard_map/gram/pallas_call | solution.py:273
  62.1 0.6 collective-permute-start.16
  62.7 0.6 collective-permute-start.14
  63.3 0.0 collective-permute-done.17.refs_0_
  63.3 1.5 %gram.6.refs_3_ = bf16[1,1024,4096]{2,1,0:T(8,128)(2,1)} custom-call(f32[8,128]{1,0:T(8,128)S(1)} %get-tuple-element.84.count_ref, bf16[1024,1024]{1,0:T(8,128)(2,1)S(1)} %get-tuple-element.85.left_ref, bf16[1024,256]{1,0:T(8,128)(2,1)S(1)} %collective-permute-done.17.refs_0_, bf16[1,1024,4096]{2,1,0:T(8,128)(2,1)} %gram.5.refs_1_), custom_call_target="tpu_custom_call", output_to_operand_aliasing={{}: (3, {})} | custom-call | flops 20000000000 | bytes 1024 | tf_op jit(solution)/shard_map/gram/pallas_call | solution.py:273
  64.9 0.9 %collective-permute-done.18.refs_2_ = bf16[1024,256]{1,0:T(8,128)(2,1)S(1)} collective-permute-done((bf16[1024,256]{1,0:T(8,128)(2,1)S(1)}, bf16[1024,256]{1,0:T(8,128)(2,1)S(1)}, u32[]{:S(2)}, u32[]{:S(2)}) %collective-permute-start.18) | collective-permute-done | bytes 524320 | tf_op jit(solution)/shard_map/far_near_2/ppermute | solution.py:318
  65.7 0.0 collective-permute-done.16.refs_1_
  65.7 0.0 collective-permute-done.15.refs_0_
  65.7 6.1 %gram.7.refs_1_ = bf16[1,1024,4096]{2,1,0:T(8,128)(2,1)} custom-call(f32[8,128]{1,0:T(8,128)S(1)} %get-tuple-element.84.count_ref, bf16[1024,1024]{1,0:T(8,128)(2,1)S(1)} %get-tuple-element.85.left_ref, bf16[1024,1024]{1,0:T(8,128)(2,1)S(1)} %collective-permute-done.15.refs_0_, ...), custom_call_target="tpu_custom_call", output_to_operand_aliasing={{}: (5, {})} | custom-call | flops 1024 | bytes 1024 | tf_op jit(solution)/shard_map/gram/pallas_call | solution.py:273
  71.8 4.8 %collective-permute-done.14.refs_0_ = bf16[1024,256]{1,0:T(8,128)(2,1)S(1)} collective-permute-done((bf16[1024,256]{1,0:T(8,128)(2,1)S(1)}, bf16[1024,256]{1,0:T(8,128)(2,1)S(1)}, u32[]{:S(2)}, u32[]{:S(2)}) %collective-permute-start.14) | collective-permute-done | bytes 524320 | tf_op jit(solution)/shard_map/ppermute | solution.py:314
  76.6 1.5 %gram.8.refs_1_ = bf16[1,1024,4096]{2,1,0:T(8,128)(2,1)} custom-call(f32[8,128]{1,0:T(8,128)S(1)} %get-tuple-element.84.count_ref, bf16[1024,1024]{1,0:T(8,128)(2,1)S(1)} %get-tuple-element.85.left_ref, bf16[1024,256]{1,0:T(8,128)(2,1)S(1)} %collective-permute-done.14.refs_0_, bf16[1,1024,4096]{2,1,0:T(8,128)(2,1)} %gram.7.refs_1_), custom_call_target="tpu_custom_call", output_to_operand_aliasing={{}: (3, {})} | custom-call | flops 1024 | bytes 1024 | tf_op jit(solution)/shard_map/gram/pallas_call | solution.py:273
  78.2 0.4 collective-permute-done.19.refs_0_
  78.5 1.5 %gram.9 = bf16[1,1024,4096]{2,1,0:T(8,128)(2,1)} custom-call(f32[8,128]{1,0:T(8,128)S(1)} %get-tuple-element.84.count_ref, bf16[1024,1024]{1,0:T(8,128)(2,1)S(1)} %get-tuple-element.85.left_ref, bf16[1024,256]{1,0:T(8,128)(2,1)S(1)} %collective-permute-done.19.refs_0_, bf16[1,1024,4096]{2,1,0:T(8,128)(2,1)} %gram.8.refs_1_), custom_call_target="tpu_custom_call", output_to_operand_aliasing={{}: (3, {})} | custom-call | flops 1024 | bytes 1024 | tf_op jit(solution)/shard_map/gram/pallas_call | solution.py:273
  (12 shorter events, 0.0 us)
Async XLA Ops:
  0.0 1.2 %copy-start = (bf16[512,1024]{1,0:T(8,128)(2,1)S(1)}, bf16[512,1024]{1,0:T(8,128)(2,1)}, u32[]{:S(2)}) copy-start(bf16[512,1024]{1,0:T(8,128)(2,1)} %expr_ref.1) | copy-start | bytes 3145732
  1.2 0.7 copy-start.1
  1.9 0.7 copy-start.2
  4.3 9.7 %collective-permute-start.4 = (bf16[272,256]{1,0:T(8,128)(2,1)S(1)}, bf16[272,256]{1,0:T(8,128)(2,1)S(1)}, u32[]{:S(2)}, u32[]{:S(2)}) collective-permute-start(bf16[272,256]{1,0:T(8,128)(2,1)S(1)} %get-tuple-element.58), channel_id=1, source_target_pairs={{0,12},{4,8},{8,4},{12,0},{1,13},{5,9},{9,5},{13,1},{2,14},{6,10},... | collective-permute-start | bytes 417800 | tf_op jit(solution)/shard_map/cells_3_chunk_0/ppermute | solution.py:311
  9.4 8.4 %collective-permute-start.2 = (bf16[272,256]{1,0:T(8,128)(2,1)S(1)}, bf16[272,256]{1,0:T(8,128)(2,1)S(1)}, u32[]{:S(2)}, u32[]{:S(2)}) collective-permute-start(bf16[272,256]{1,0:T(8,128)(2,1)S(1)} %get-tuple-element.55), channel_id=1, source_target_pairs={{0,4},{4,0},{8,12},{12,8},{1,5},{5,1},{9,13},{13,9},{2,6},{6,2},{1... | collective-permute-start | bytes 417800 | tf_op jit(solution)/shard_map/cells_1_chunk_0/ppermute | solution.py:311
  9.4 17.0 %collective-permute-start = (bf16[272,256]{1,0:T(8,128)(2,1)S(1)}, bf16[272,256]{1,0:T(8,128)(2,1)S(1)}, u32[]{:S(2)}, u32[]{:S(2)}) collective-permute-start(bf16[272,256]{1,0:T(8,128)(2,1)S(1)} %get-tuple-element.52), channel_id=1, source_target_pairs={{0,8},{4,12},{8,0},{12,4},{1,9},{5,13},{9,1},{13,5},{2,10},{6,14},... | collective-permute-start | bytes 417800 | tf_op jit(solution)/shard_map/cells_2_chunk_0/ppermute | solution.py:311
  14.0 16.5 %collective-permute-start.5 = (bf16[256,256]{1,0:T(8,128)(2,1)S(1)}, bf16[256,256]{1,0:T(8,128)(2,1)S(1)}, u32[]{:S(2)}, u32[]{:S(2)}) collective-permute-start(bf16[256,256]{1,0:T(8,128)(2,1)S(1)} %get-tuple-element.59), channel_id=1, source_target_pairs={{0,12},{4,8},{8,4},{12,0},{1,13},{5,9},{9,5},{13,1},{2,14},{6,10},... | collective-permute-start | bytes 393224 | tf_op jit(solution)/shard_map/cells_3_chunk_1/ppermute | solution.py:311
  17.8 13.7 %collective-permute-start.3 = (bf16[256,256]{1,0:T(8,128)(2,1)S(1)}, bf16[256,256]{1,0:T(8,128)(2,1)S(1)}, u32[]{:S(2)}, u32[]{:S(2)}) collective-permute-start(bf16[256,256]{1,0:T(8,128)(2,1)S(1)} %get-tuple-element.56), channel_id=1, source_target_pairs={{0,4},{4,0},{8,12},{12,8},{1,5},{5,1},{9,13},{13,9},{2,6},{6,2},{1... | collective-permute-start | bytes 393224 | tf_op jit(solution)/shard_map/cells_1_chunk_1/ppermute | solution.py:311
  26.4 8.7 %collective-permute-start.1 = (bf16[256,256]{1,0:T(8,128)(2,1)S(1)}, bf16[256,256]{1,0:T(8,128)(2,1)S(1)}, u32[]{:S(2)}, u32[]{:S(2)}) collective-permute-start(bf16[256,256]{1,0:T(8,128)(2,1)S(1)} %get-tuple-element.53), channel_id=1, source_target_pairs={{0,8},{4,12},{8,0},{12,4},{1,9},{5,13},{9,1},{13,5},{2,10},{6,14},... | collective-permute-start | bytes 393224 | tf_op jit(solution)/shard_map/cells_2_chunk_1/ppermute | solution.py:311
  26.4 0.7 copy-start.3
  28.9 20.3 %collective-permute-start.13 = (bf16[1024,256]{1,0:T(8,128)(2,1)S(1)}, bf16[1024,256]{1,0:T(8,128)(2,1)S(1)}, u32[]{:S(2)}, u32[]{:S(2)}) collective-permute-start(bf16[1024,256]{1,0:T(8,128)(2,1)S(1)} %get-tuple-element.77), channel_id=1, source_target_pairs={{0,2},{1,3},{2,0},{3,1},{4,6},{5,7},{6,4},{7,5},{8,10},{9,11},{10,... | collective-permute-start | bytes 1572872 | tf_op jit(solution)/shard_map/far_0/ppermute | solution.py:314
  30.5 8.0 %collective-permute-start.11 = (bf16[256,256]{1,0:T(8,128)(2,1)S(1)}, bf16[256,256]{1,0:T(8,128)(2,1)S(1)}, u32[]{:S(2)}, u32[]{:S(2)}) collective-permute-start(bf16[256,256]{1,0:T(8,128)(2,1)S(1)} %get-tuple-element.75), channel_id=1, source_target_pairs={{0,12},{4,8},{8,4},{12,0},{1,13},{5,9},{9,5},{13,1},{2,14},{6,10},... | collective-permute-start | bytes 393224 | tf_op jit(solution)/shard_map/cells_3_chunk_2/ppermute | solution.py:311
  31.5 12.0 %collective-permute-start.9 = (bf16[256,256]{1,0:T(8,128)(2,1)S(1)}, bf16[256,256]{1,0:T(8,128)(2,1)S(1)}, u32[]{:S(2)}, u32[]{:S(2)}) collective-permute-start(bf16[256,256]{1,0:T(8,128)(2,1)S(1)} %get-tuple-element.71), channel_id=1, source_target_pairs={{0,4},{4,0},{8,12},{12,8},{1,5},{5,1},{9,13},{13,9},{2,6},{6,2},{1... | collective-permute-start | bytes 393224 | tf_op jit(solution)/shard_map/cells_1_chunk_2/ppermute | solution.py:311
  35.2 14.0 %collective-permute-start.7 = (bf16[256,256]{1,0:T(8,128)(2,1)S(1)}, bf16[256,256]{1,0:T(8,128)(2,1)S(1)}, u32[]{:S(2)}, u32[]{:S(2)}) collective-permute-start(bf16[256,256]{1,0:T(8,128)(2,1)S(1)} %get-tuple-element.67), channel_id=1, source_target_pairs={{0,8},{4,12},{8,0},{12,4},{1,9},{5,13},{9,1},{13,5},{2,10},{6,14},... | collective-permute-start | bytes 393224 | tf_op jit(solution)/shard_map/cells_2_chunk_2/ppermute | solution.py:311
  35.2 14.0 %copy-start.4 = (f32[1024]{0:T(1024)S(1)}, f32[1024]{0:T(1024)}, u32[]{:S(2)}) copy-start(f32[1024]{0:T(1024)} %param.7) | copy-start | bytes 12292
  37.0 16.1 %collective-permute-start.6 = (bf16[1024,256]{1,0:T(8,128)(2,1)S(1)}, bf16[1024,256]{1,0:T(8,128)(2,1)S(1)}, u32[]{:S(2)}, u32[]{:S(2)}) collective-permute-start(bf16[1024,256]{1,0:T(8,128)(2,1)S(1)} %get-tuple-element.63), channel_id=1, source_target_pairs={{0,2},{1,3},{2,0},{3,1},{4,6},{5,7},{6,4},{7,5},{8,10},{9,11},{10,... | collective-permute-start | bytes 1572872 | tf_op jit(solution)/shard_map/far_1/ppermute | solution.py:314
  38.4 14.6 %collective-permute-start.12 = (bf16[256,256]{1,0:T(8,128)(2,1)S(1)}, bf16[256,256]{1,0:T(8,128)(2,1)S(1)}, u32[]{:S(2)}, u32[]{:S(2)}) collective-permute-start(bf16[256,256]{1,0:T(8,128)(2,1)S(1)} %get-tuple-element.76), channel_id=1, source_target_pairs={{0,12},{4,8},{8,4},{12,0},{1,13},{5,9},{9,5},{13,1},{2,14},{6,10},... | collective-permute-start | bytes 393224 | tf_op jit(solution)/shard_map/cells_3_chunk_3/ppermute | solution.py:311
  43.4 9.6 %collective-permute-start.10 = (bf16[256,256]{1,0:T(8,128)(2,1)S(1)}, bf16[256,256]{1,0:T(8,128)(2,1)S(1)}, u32[]{:S(2)}, u32[]{:S(2)}) collective-permute-start(bf16[256,256]{1,0:T(8,128)(2,1)S(1)} %get-tuple-element.72), channel_id=1, source_target_pairs={{0,4},{4,0},{8,12},{12,8},{1,5},{5,1},{9,13},{13,9},{2,6},{6,2},{1... | collective-permute-start | bytes 393224 | tf_op jit(solution)/shard_map/cells_1_chunk_3/ppermute | solution.py:311
  49.2 6.7 %collective-permute-start.8 = (bf16[256,256]{1,0:T(8,128)(2,1)S(1)}, bf16[256,256]{1,0:T(8,128)(2,1)S(1)}, u32[]{:S(2)}, u32[]{:S(2)}) collective-permute-start(bf16[256,256]{1,0:T(8,128)(2,1)S(1)} %get-tuple-element.68), channel_id=1, source_target_pairs={{0,8},{4,12},{8,0},{12,4},{1,9},{5,13},{9,1},{13,5},{2,10},{6,14},... | collective-permute-start | bytes 393224 | tf_op jit(solution)/shard_map/cells_2_chunk_3/ppermute | solution.py:311
  51.0 12.3 %collective-permute-start.17 = (bf16[1024,256]{1,0:T(8,128)(2,1)S(1)}, bf16[1024,256]{1,0:T(8,128)(2,1)S(1)}, u32[]{:S(2)}, u32[]{:S(2)}) collective-permute-start(bf16[1024,256]{1,0:T(8,128)(2,1)S(1)} %get-tuple-element.90), channel_id=1, source_target_pairs={{0,2},{1,3},{2,0},{3,1},{4,6},{5,7},{6,4},{7,5},{8,10},{9,11},{10,... | collective-permute-start | bytes 1572872 | tf_op jit(solution)/shard_map/far_2/ppermute | solution.py:314
  57.2 8.5 %collective-permute-start.15 = (bf16[1024,1024]{1,0:T(8,128)(2,1)S(1)}, bf16[1024,1024]{1,0:T(8,128)(2,1)S(1)}, u32[]{:S(2)}, u32[]{:S(2)}) collective-permute-start(bf16[1024,1024]{1,0:T(8,128)(2,1)S(1)} %get-tuple-element.87.refs_0_), channel_id=1, source_target_pairs={{0,1},{1,0},{2,3},{3,2},{4,5},{5,4},{6,7},{7,6},{8,9},{9,8},{10,11... | collective-permute-start | bytes 6291464 | tf_op jit(solution)/shard_map/near/ppermute | solution.py:318
  62.1 3.6 %collective-permute-start.16 = (bf16[1024,512]{1,0:T(8,128)(2,1)S(1)}, bf16[1024,512]{1,0:T(8,128)(2,1)S(1)}, u32[]{:S(2)}, u32[]{:S(2)}) collective-permute-start(bf16[1024,512]{1,0:T(8,128)(2,1)S(1)} %get-tuple-element.88.refs_1_), channel_id=1, source_target_pairs={{0,1},{1,0},{2,3},{3,2},{4,5},{5,4},{6,7},{7,6},{8,9},{9,8},{10,11... | collective-permute-start | bytes 3145736 | tf_op jit(solution)/shard_map/far_near/ppermute | solution.py:318
  62.7 13.9 %collective-permute-start.14 = (bf16[1024,256]{1,0:T(8,128)(2,1)S(1)}, bf16[1024,256]{1,0:T(8,128)(2,1)S(1)}, u32[]{:S(2)}, u32[]{:S(2)}) collective-permute-start(bf16[1024,256]{1,0:T(8,128)(2,1)S(1)} %get-tuple-element.89), channel_id=1, source_target_pairs={{0,2},{1,3},{2,0},{3,1},{4,6},{5,7},{6,4},{7,5},{8,10},{9,11},{10,... | collective-permute-start | bytes 1572872 | tf_op jit(solution)/shard_map/ppermute | solution.py:314
  63.3 2.4 %collective-permute-start.18 = (bf16[1024,256]{1,0:T(8,128)(2,1)S(1)}, bf16[1024,256]{1,0:T(8,128)(2,1)S(1)}, u32[]{:S(2)}, u32[]{:S(2)}) collective-permute-start(bf16[1024,256]{1,0:T(8,128)(2,1)S(1)} %collective-permute-done.17.refs_0_), channel_id=1, source_target_pairs={{0,1},{1,0},{2,3},{3,2},{4,5},{5,4},{6,7},{7,6},{8,9},{9,8},{10,11... | collective-permute-start | bytes 1572872 | tf_op jit(solution)/shard_map/far_near_2/ppermute | solution.py:318
  76.6 1.9 %collective-permute-start.19 = (bf16[1024,256]{1,0:T(8,128)(2,1)S(1)}, bf16[1024,256]{1,0:T(8,128)(2,1)S(1)}, u32[]{:S(2)}, u32[]{:S(2)}) collective-permute-start(bf16[1024,256]{1,0:T(8,128)(2,1)S(1)} %collective-permute-done.14.refs_0_), channel_id=1, source_target_pairs={{0,1},{1,0},{2,3},{3,2},{4,5},{5,4},{6,7},{7,6},{8,9},{9,8},{10,11... | collective-permute-start | bytes 1572872 | tf_op jit(solution)/shard_map/far_near_3/ppermute | solution.py:318

commit v14 on v13

--- a/solution.py
+++ b/solution.py
@@ -18,10 +18,10 @@
 anywhere = pl.BlockSpec(memory_space=pl.ANY)
 
 
-def pack_kernel(types, cap, widths, type_ref, factor_ref, expr_ref, *outs):
+def pack_kernel(types, cap, widths, small_ref, expr_ref, *outs):
     rows = expr_ref.shape[0]
     home = lax.axis_index("cells")
-    kind = type_ref[...].reshape(1, rows)
+    kind = small_ref[0:1, 0:rows].astype(jnp.int32)
     rel = jnp.bitwise_xor(kind, home)
     lines = max(types, 8)
     hot = lax.broadcasted_iota(jnp.int32, (lines, rows), 0) == rel
@@ -35,8 +35,7 @@
     running = jnp.dot(hot_f.astype(jnp.bfloat16), upper, preferred_element_type=jnp.float32)
     rank = jnp.sum(hot_f * running, axis=0, keepdims=True) - 1.0
     slot = rel * cap + rank.astype(jnp.int32)
-    factor = factor_ref[...].astype(jnp.float32).reshape(1, rows)
-    factor = jnp.broadcast_to(factor, (TILE, rows)).astype(jnp.bfloat16)
+    factor = jnp.broadcast_to(small_ref[1:2, 0:rows], (TILE, rows)).astype(jnp.bfloat16)
     values = expr_ref[...]
     for j in range(types):
         place = jnp.where(
@@ -58,7 +57,7 @@
         outs[j][cap : cap + TILE, 0 : min(width, cap)] = tail.astype(jnp.bfloat16)
 
 
-def pack(types, cap, widths, cell_type, size_factor, expression):
+def pack(types, cap, widths, small, expression):
     rows = expression.shape[0]
     shapes = [
         jax.ShapeDtypeStruct((cap + (TILE if k == 0 else 0), width), jnp.bfloat16)
@@ -68,16 +67,16 @@
     flat = pl.pallas_call(
         functools.partial(pack_kernel, types, cap, widths),
         out_shape=shapes,
-        in_specs=[whole] * 3,
+        in_specs=[whole] * 2,
         out_specs=[whole] * len(shapes),
         compiler_params=pltpu.CompilerParams(vmem_limit_bytes=VMEM),
         cost_estimate=brief,
         name="pack",
-    )(cell_type, size_factor, expression)
+    )(small, expression)
     return [flat[k * types : (k + 1) * types] for k in range(len(widths))]
 
 
-def standardize_kernel(types, cap, lead, separate, start, gathered, mean_ref, *refs):
+def standardize_kernel(types, cap, lead, separate, start, gathered, small_ref, *refs):
     blocks = refs[:types]
     tails = refs[types : 2 * types] if separate else blocks
     base = 0 if separate else cap
@@ -96,7 +95,7 @@
             copies.append(pltpu.make_async_copy(source, spot, sems.at[2 + len(copies)]))
             copies[-1].start()
     width = work.shape[1]
-    mean = mean_ref[:, start : start + width]
+    mean = small_ref[2:3, start : start + width]
     piece = min(lead, cap)
     total = jnp.zeros((1, width), jnp.float32)
     count = jnp.zeros((1, 1), jnp.float32)
@@ -145,13 +144,12 @@
     count_ref[...] = jnp.broadcast_to(count, count_ref.shape)
 
 
-def standardize(types, cap, mean, start, blocks, first, left, own, gather):
+def standardize(types, cap, panel, small, start, blocks, first, left, own, gather):
     lead, width = first[0].shape[1], blocks[0].shape[1]
-    panel = mean.shape[1]
     separate = first is not blocks
     slots = types * cap
     specs = [whole] * (1 + types)
-    args = [mean, *blocks]
+    args = [small, *blocks]
     if separate:
         specs += [pl.BlockSpec((TILE, lead), lambda i: (cap // TILE, 0))] * types
         args += list(first)
@@ -305,7 +303,10 @@
     chips = blocks // cores
     window = 3
 
-    packed = pack(types, cap, widths, cell_type, size_factor, expression)
+    small = [row.astype(jnp.float32) for row in (cell_type, size_factor, gene_mean)]
+    size = max(shard_rows, panel)
+    small = jnp.stack([jnp.pad(row, (0, size - row.shape[0])) for row in small])
+    packed = pack(types, cap, widths, small, expression)
 
     def swap(block, by):
         return lax.ppermute(block, "cells", [(s, s ^ by) for s in range(types)])
@@ -317,7 +318,6 @@
         with jax.named_scope(name):
             return lax.ppermute(after(panel_, *waits), "blk", [(b, b ^ 1) for b in range(blocks)])
 
-    mean = gene_mean.reshape(1, panel)
     order = sorted(range(1, types), key=lambda j: (j == 3, j == 1, j))
     left, own, far, before = None, None, [], None
     for k in range(chunks):
@@ -337,11 +337,10 @@
         if k == chunks - 1 and k > 1:
             gather = [[got[d] for got in far[: k - 1]] for d in range(chips - 1)]
         scaled, left, count, own, *joined = standardize(
-            types, cap, mean, starts[k], arrived, first, left, own, gather
+            types, cap, panel, small, starts[k], arrived, first, left, own, gather
         )
-        if k < chunks - 1:
-            with jax.named_scope(f"far_{k}"):
-                far.append([across(scaled, d) for d in range(1, chips)])
+        with jax.named_scope(f"far_{k}"):
+            far.append([across(scaled, d) for d in range(1, chips)])
 
     multiply = functools.partial(gram, blocks, cores, count, left)
     last = chunks - 1
@@ -350,7 +349,7 @@
     joined = [[p] for p in joined] or [[]] * (chips - 1)
     groups = [([own], (0, 0, 0))] + [(p, (d, 0, 0)) for d, p in enumerate(joined, 1) if p]
     out = multiply(groups, None, brief)
-    final = [across(after(scaled, out), d) for d in range(1, chips)]
+    final = far[last]
     second = [side(f"far_near_{last - 1}", p, own) for p in far[last - 1]]
     edge = starts[last - 1]
     groups = [([p], (d, 0, edge)) for d, p in enumerate(far[last - 1], 1)]

time: 80.4 us -> 78.5 us (0.976); the launches traced: 80.2 us -> 76.9 us
  waiting for transfers between devices: 27.2 us -> 23.4 us
  other arithmetic: 0 us -> 2.07 us
  local copies, waits for them, and re-layouts: 3.27 us -> 1.22 us
    ppermute x4, waiting for transfers between devices: 6.73 us -> 1.95 us  [across(): lax.ppermute(panel_, 'blk', [(b, (b + by * cores) % blocks) for b in rang...]
    ppermute x4, starting transfers between devices: 3.5 us -> 5.78 us  [across(): lax.ppermute(panel_, 'blk', [(b, (b + by * cores) % blocks) for b in rang...]
    unnamed x10 -> x2, local copies, waits for them, and re-layouts: 3.27 us -> 1.22 us
    ppermute x12, starting transfers between devices: 21.3 us -> 19.6 us  [swap(): return lax.ppermute(block, 'cells', [(s, s ^ by) for s in range(types)])]
    ppermute x12, waiting for transfers between devices: 19.3 us -> 20.7 us  [swap(): return lax.ppermute(block, 'cells', [(s, s ^ by) for s in range(types)])]
    another operation x0 -> x2, other arithmetic: none -> 1.38 us  [shards(): small = jnp.stack([jnp.pad(row, (0, size - row.shape[0])) for row in small])]
  transfers between devices with their start and end apart: 20 -> 20, of which waited for: 10 -> 9; matrix products, arithmetic and copies ran while one was open for 0% -> 0% of each run, Pallas kernels for 26% -> 27%
where the time goes in v14:
time: 78.5 us; the launch traced here: 76.9 us
  starting transfers between devices  26 us (33%)
  Pallas kernels  23.9 us (30%)
  waiting for transfers between devices  23.4 us (30%)
  other arithmetic  2.07 us (3%)
  local copies, waits for them, and re-layouts  1.22 us (2%)
    ppermute x12, waiting for transfers between devices, swap(): return lax.ppermute(block, 'cells', [(s, s ^ by) for s in range(types)])  20.7 us
    ppermute x12, starting transfers between devices, swap(): return lax.ppermute(block, 'cells', [(s, s ^ by) for s in range(types)])  19.6 us
    pallas_call x5, Pallas kernels, gram(): pl.pallas_call(functools.partial(gram_kernel, blocks, cores, strip, layou...  15.5 us
    pallas_call x4, Pallas kernels, standardize(): pl.pallas_call(functools.partial(standardize_kernel, types, cap, lead, se...  6.71 us
    ppermute x4, starting transfers between devices, across(): lax.ppermute(panel_, 'blk', [(b, (b + by * cores) % blocks) for b in rang...  5.78 us
    ppermute x4, waiting for transfers between devices, across(): lax.ppermute(panel_, 'blk', [(b, (b + by * cores) % blocks) for b in rang...  1.95 us
    pallas_call x1, Pallas kernels, pack(): pl.pallas_call(functools.partial(pack_kernel, types, cap, widths), out_sh...  1.7 us
  transfers between devices with their start and end apart: 20, of which 9 were waited for; matrix products, arithmetic and copies ran while one was open for 0% of the time, Pallas kernels for 27%

profile of v14, /device:TPU:0, one launch (start us, length us, event | category | flops | bytes accessed | tf_op | source)
XLA Modules:
  0.0 76.9 jit_solution(1258853301999280747)
XLA Ops:
  0.0 0.7 convert_element_type.7
  0.7 0.7 pad_convert_fusion
  1.4 0.7 pad_maximum_fusion.small_ref
  2.1 0.0 copy-start
  2.1 1.2 %copy-done = bf16[512,1024]{1,0:T(8,128)(2,1)S(1)} copy-done((bf16[512,1024]{1,0:T(8,128)(2,1)S(1)}, bf16[512,1024]{1,0:T(8,128)(2,1)}, u32[]{:S(2)}) %copy-start) | copy-done | bytes 1048600
  3.3 1.7 %pack.1 = (bf16[272,256]{1,0:T(8,128)(2,1)S(1)}, bf16[272,256]{1,0:T(8,128)(2,1)S(1)}, bf16[272,256]{1,0:T(8,128)(2,1)S(1)}, bf16[272,256]{1,0:T(8,128)(2,1)S(1)...) custom-call(f32[3,1024]{1,0:T(4,128)S(1)} %pad_maximum_fusion.small_, ...), custom_call_target="tpu_custom_call" | custom-call | flops 1024 | bytes 1024 | tf_op jit(solution)/shard_map/pack/pallas_call | solution.py:67
  5.0 5.1 %collective-permute-start.4 = (bf16[272,256]{1,0:T(8,128)(2,1)S(1)}, bf16[272,256]{1,0:T(8,128)(2,1)S(1)}, u32[]{:S(2)}, u32[]{:S(2)}) collective-permute-start(bf16[272,256]{1,0:T(8,128)(2,1)S(1)} %get-tuple-element.57), channel_id=1, source_target_pairs={{0,12},{4,8},{8,4},{12,0},{1,13},{5,9},{9,5},{13,1},{2,14},{6,10},... | collective-permute-start | bytes 417800 | tf_op jit(solution)/shard_map/cells_3_chunk_0/ppermute | solution.py:312
  10.1 0.0 collective-permute-start.2
  10.1 0.6 collective-permute-start
  10.8 3.9 %collective-permute-done.4.refs_3_.refs_7_ = bf16[272,256]{1,0:T(8,128)(2,1)S(1)} collective-permute-done((bf16[272,256]{1,0:T(8,128)(2,1)S(1)}, bf16[272,256]{1,0:T(8,128)(2,1)S(1)}, u32[]{:S(2)}, u32[]{:S(2)}) %collective-permute-start.4) | collective-permute-done | bytes 139296 | tf_op jit(solution)/shard_map/cells_3_chunk_0/ppermute | solution.py:312
  14.7 3.8 %collective-permute-start.5 = (bf16[256,256]{1,0:T(8,128)(2,1)S(1)}, bf16[256,256]{1,0:T(8,128)(2,1)S(1)}, u32[]{:S(2)}, u32[]{:S(2)}) collective-permute-start(bf16[256,256]{1,0:T(8,128)(2,1)S(1)} %get-tuple-element.58), channel_id=1, source_target_pairs={{0,12},{4,8},{8,4},{12,0},{1,13},{5,9},{9,5},{13,1},{2,14},{6,10},... | collective-permute-start | bytes 393224 | tf_op jit(solution)/shard_map/cells_3_chunk_1/ppermute | solution.py:312
  18.5 0.0 collective-permute-done.2.refs_2_.refs_6_
  18.5 1.2 %collective-permute-start.3 = (bf16[256,256]{1,0:T(8,128)(2,1)S(1)}, bf16[256,256]{1,0:T(8,128)(2,1)S(1)}, u32[]{:S(2)}, u32[]{:S(2)}) collective-permute-start(bf16[256,256]{1,0:T(8,128)(2,1)S(1)} %get-tuple-element.55), channel_id=1, source_target_pairs={{0,4},{4,0},{8,12},{12,8},{1,5},{5,1},{9,13},{13,9},{2,6},{6,2},{1... | collective-permute-start | bytes 393224 | tf_op jit(solution)/shard_map/cells_1_chunk_1/ppermute | solution.py:312
  19.7 7.4 %collective-permute-done.refs_1_.refs_5_ = bf16[272,256]{1,0:T(8,128)(2,1)S(1)} collective-permute-done((bf16[272,256]{1,0:T(8,128)(2,1)S(1)}, bf16[272,256]{1,0:T(8,128)(2,1)S(1)}, u32[]{:S(2)}, u32[]{:S(2)}) %collective-permute-start) | collective-permute-done | bytes 139296 | tf_op jit(solution)/shard_map/cells_2_chunk_0/ppermute | solution.py:312
  27.1 0.0 collective-permute-start.1
  27.1 1.8 %standardize.4 = (bf16[1024,256]{1,0:T(8,128)(2,1)S(1)}, bf16[1024,1024]{1,0:T(8,128)(2,1)S(1)}, f32[8,128]{1,0:T(8,128)}, bf16[1024,1024]{1,0:T(8,128)(2,1)S(1)}) custom-call(f32[3,1024]{1,0:T(4,128)S(1)} %pad_maximum_fusion.small_ref, bf16[272,256]{1,0:T(8,128)(2,1)S(1)} %get-tuple-element.59.refs_0_.refs_4_, ...), custom_call_target="tpu_custom_call" | custom-call | flops 20000000000 | bytes 1024 | tf_op jit(solution)/shard_map/standardize/pallas_call | solution.py:171
  28.9 1.6 %collective-permute-start.13 = (bf16[1024,256]{1,0:T(8,128)(2,1)S(1)}, bf16[1024,256]{1,0:T(8,128)(2,1)S(1)}, u32[]{:S(2)}, u32[]{:S(2)}) collective-permute-start(bf16[1024,256]{1,0:T(8,128)(2,1)S(1)} %get-tuple-element.76), channel_id=1, source_target_pairs={{0,2},{1,3},{2,0},{3,1},{4,6},{5,7},{6,4},{7,5},{8,10},{9,11},{10,... | collective-permute-start | bytes 1572872 | tf_op jit(solution)/shard_map/far_0/ppermute | solution.py:315
  30.5 0.0 collective-permute-done.5.refs_3_
  30.5 1.0 %collective-permute-start.11 = (bf16[256,256]{1,0:T(8,128)(2,1)S(1)}, bf16[256,256]{1,0:T(8,128)(2,1)S(1)}, u32[]{:S(2)}, u32[]{:S(2)}) collective-permute-start(bf16[256,256]{1,0:T(8,128)(2,1)S(1)} %get-tuple-element.74), channel_id=1, source_target_pairs={{0,12},{4,8},{8,4},{12,0},{1,13},{5,9},{9,5},{13,1},{2,14},{6,10},... | collective-permute-start | bytes 393224 | tf_op jit(solution)/shard_map/cells_3_chunk_2/ppermute | solution.py:312
  31.5 0.0 collective-permute-done.3.refs_2_
  31.5 3.3 %collective-permute-start.9 = (bf16[256,256]{1,0:T(8,128)(2,1)S(1)}, bf16[256,256]{1,0:T(8,128)(2,1)S(1)}, u32[]{:S(2)}, u32[]{:S(2)}) collective-permute-start(bf16[256,256]{1,0:T(8,128)(2,1)S(1)} %get-tuple-element.70), channel_id=1, source_target_pairs={{0,4},{4,0},{8,12},{12,8},{1,5},{5,1},{9,13},{13,9},{2,6},{6,2},{1... | collective-permute-start | bytes 393224 | tf_op jit(solution)/shard_map/cells_1_chunk_2/ppermute | solution.py:312
  34.8 0.9 %collective-permute-done.1.refs_1_ = bf16[256,256]{1,0:T(8,128)(2,1)S(1)} collective-permute-done((bf16[256,256]{1,0:T(8,128)(2,1)S(1)}, bf16[256,256]{1,0:T(8,128)(2,1)S(1)}, u32[]{:S(2)}, u32[]{:S(2)}) %collective-permute-start.1) | collective-permute-done | bytes 131104 | tf_op jit(solution)/shard_map/cells_2_chunk_1/ppermute | solution.py:312
  35.7 0.0 collective-permute-start.7
  35.7 1.8 %standardize.5 = (bf16[1024,256]{1,0:T(8,128)(2,1)S(1)}, bf16[1024,1024]{1,0:T(8,128)(2,1)S(1)}, f32[8,128]{1,0:T(8,128)}, bf16[1024,1024]{1,0:T(8,128)(2,1)S(1)}) custom-call(f32[3,1024]{1,0:T(4,128)S(1)} %pad_maximum_fusion.small_ref, bf16[256,256]{1,0:T(8,128)(2,1)S(1)} %get-tuple-element.49.refs_0_, ...), custom_call_target="tpu_custom_call", output_to_operand_aliasing={{1}: (9, {}), {3}: (10, {})} | custom-call | flops 20000000000 | bytes 1024 | tf_op jit(solution)/shard_map/standardize/pallas_call | solution.py:171
  37.5 2.8 %collective-permute-start.6 = (bf16[1024,256]{1,0:T(8,128)(2,1)S(1)}, bf16[1024,256]{1,0:T(8,128)(2,1)S(1)}, u32[]{:S(2)}, u32[]{:S(2)}) collective-permute-start(bf16[1024,256]{1,0:T(8,128)(2,1)S(1)} %get-tuple-element.62), channel_id=1, source_target_pairs={{0,2},{1,3},{2,0},{3,1},{4,6},{5,7},{6,4},{7,5},{8,10},{9,11},{10,... | collective-permute-start | bytes 1572872 | tf_op jit(solution)/shard_map/far_1/ppermute | solution.py:315
  40.3 0.0 collective-permute-done.11.refs_3_
  40.3 3.8 %collective-permute-start.12 = (bf16[256,256]{1,0:T(8,128)(2,1)S(1)}, bf16[256,256]{1,0:T(8,128)(2,1)S(1)}, u32[]{:S(2)}, u32[]{:S(2)}) collective-permute-start(bf16[256,256]{1,0:T(8,128)(2,1)S(1)} %get-tuple-element.75), channel_id=1, source_target_pairs={{0,12},{4,8},{8,4},{12,0},{1,13},{5,9},{9,5},{13,1},{2,14},{6,10},... | collective-permute-start | bytes 393224 | tf_op jit(solution)/shard_map/cells_3_chunk_3/ppermute | solution.py:312
  44.2 0.0 collective-permute-done.9.refs_2_
  44.2 0.6 collective-permute-start.10
  44.8 5.1 %collective-permute-done.7.refs_1_ = bf16[256,256]{1,0:T(8,128)(2,1)S(1)} collective-permute-done((bf16[256,256]{1,0:T(8,128)(2,1)S(1)}, bf16[256,256]{1,0:T(8,128)(2,1)S(1)}, u32[]{:S(2)}, u32[]{:S(2)}) %collective-permute-start.7) | collective-permute-done | bytes 131104 | tf_op jit(solution)/shard_map/cells_2_chunk_2/ppermute | solution.py:312
  49.9 0.0 collective-permute-start.8
  49.9 1.8 %standardize.6 = (bf16[1024,256]{1,0:T(8,128)(2,1)S(1)}, bf16[1024,1024]{1,0:T(8,128)(2,1)S(1)}, f32[8,128]{1,0:T(8,128)}, bf16[1024,1024]{1,0:T(8,128)(2,1)S(1)}) custom-call(f32[3,1024]{1,0:T(4,128)S(1)} %pad_maximum_fusion.small_ref, bf16[256,256]{1,0:T(8,128)(2,1)S(1)} %get-tuple-element.78.refs_0_, ...), custom_call_target="tpu_custom_call", output_to_operand_aliasing={{1}: (9, {}), {3}: (10, {})} | custom-call | flops 20000000000 | bytes 1024 | tf_op jit(solution)/shard_map/standardize/pallas_call | solution.py:171
  51.7 0.1 collective-permute-start.17
  51.8 0.6 collective-permute-done.6.refs_9_
  52.4 3.4 %collective-permute-done.8.refs_1_ = bf16[256,256]{1,0:T(8,128)(2,1)S(1)} collective-permute-done((bf16[256,256]{1,0:T(8,128)(2,1)S(1)}, bf16[256,256]{1,0:T(8,128)(2,1)S(1)}, u32[]{:S(2)}, u32[]{:S(2)}) %collective-permute-start.8) | collective-permute-done | bytes 131104 | tf_op jit(solution)/shard_map/cells_2_chunk_3/ppermute | solution.py:312
  55.8 1.3 %standardize.7 = (bf16[1024,256]{1,0:T(8,128)(2,1)S(1)}, bf16[1024,1024]{1,0:T(8,128)(2,1)S(1)}, f32[8,128]{1,0:T(8,128)S(1)}, bf16[1024,1024]{1,0:T(8,128)(2,1)S(1)}, bf16[1024,512]{1,0:T(8,128)(2,1)S(1)}) custom-call(f32[3,1024]{1,0:T(4,128)S(1)} %pad_maximum_fusion.small_ref, ...), custom_call_target="tpu_custom_call", output_to_operand_aliasing={{1}: (11, {}), {3}: (12, {})} | custom-call | flops 20000000000 | bytes 1024 | tf_op jit(solution)/shard_map/standardize/pallas_call | solution.py:171
  57.1 0.1 collective-permute-start.15
  57.2 0.5 collective-permute-start.16
  57.7 1.3 %collective-permute-start.14 = (bf16[1024,256]{1,0:T(8,128)(2,1)S(1)}, bf16[1024,256]{1,0:T(8,128)(2,1)S(1)}, u32[]{:S(2)}, u32[]{:S(2)}) collective-permute-start(bf16[1024,256]{1,0:T(8,128)(2,1)S(1)} %get-tuple-element.85), channel_id=1, source_target_pairs={{0,2},{1,3},{2,0},{3,1},{4,6},{5,7},{6,4},{7,5},{8,10},{9,11},{10,... | collective-permute-start | bytes 1572872 | tf_op jit(solution)/shard_map/far_3/ppermute | solution.py:315
  59.0 4.8 %gram.5.refs_1_ = bf16[1,1024,4096]{2,1,0:T(8,128)(2,1)} custom-call(f32[8,128]{1,0:T(8,128)S(1)} %get-tuple-element.83.count_ref, bf16[1024,1024]{1,0:T(8,128)(2,1)S(1)} %get-tuple-element.84.left_ref, bf16[1024,1024]{1,0:T(8,128)(2,1)S(1)} %get-tuple-element.86.refs_0_, bf16[1024,512]{1,0:T(8,128)(2,1)S(1)} %get-tuple-element.87.refs_1_), custom_call_target="tpu_custom_call" | custom-call | flops 1024 | bytes 1024 | tf_op jit(solution)/shard_map/gram/pallas_call | solution.py:271
  63.9 0.1 collective-permute-start.18
  64.0 1.5 %gram.6.refs_3_ = bf16[1,1024,4096]{2,1,0:T(8,128)(2,1)} custom-call(f32[8,128]{1,0:T(8,128)S(1)} %get-tuple-element.83.count_ref, bf16[1024,1024]{1,0:T(8,128)(2,1)S(1)} %get-tuple-element.84.left_ref, bf16[1024,256]{1,0:T(8,128)(2,1)S(1)} %collective-permute-done.17.refs_0_, bf16[1,1024,4096]{2,1,0:T(8,128)(2,1)} %gram.5.refs_1_), custom_call_target="tpu_custom_call", output_to_operand_aliasing={{}: (3, {})} | custom-call | flops 20000000000 | bytes 1024 | tf_op jit(solution)/shard_map/gram/pallas_call | solution.py:271
  65.5 0.3 collective-permute-done.18.refs_2_
  65.9 6.1 %gram.7.refs_1_ = bf16[1,1024,4096]{2,1,0:T(8,128)(2,1)} custom-call(f32[8,128]{1,0:T(8,128)S(1)} %get-tuple-element.83.count_ref, bf16[1024,1024]{1,0:T(8,128)(2,1)S(1)} %get-tuple-element.84.left_ref, bf16[1024,1024]{1,0:T(8,128)(2,1)S(1)} %collective-permute-done.15.refs_0_, ...), custom_call_target="tpu_custom_call", output_to_operand_aliasing={{}: (5, {})} | custom-call | flops 1024 | bytes 1024 | tf_op jit(solution)/shard_map/gram/pallas_call | solution.py:271
  72.0 1.4 %collective-permute-done.14.refs_0_ = bf16[1024,256]{1,0:T(8,128)(2,1)S(1)} collective-permute-done((bf16[1024,256]{1,0:T(8,128)(2,1)S(1)}, bf16[1024,256]{1,0:T(8,128)(2,1)S(1)}, u32[]{:S(2)}, u32[]{:S(2)}) %collective-permute-start.14) | collective-permute-done | bytes 524320 | tf_op jit(solution)/shard_map/far_3/ppermute | solution.py:315
  73.3 1.5 %gram.8.refs_1_ = bf16[1,1024,4096]{2,1,0:T(8,128)(2,1)} custom-call(f32[8,128]{1,0:T(8,128)S(1)} %get-tuple-element.83.count_ref, bf16[1024,1024]{1,0:T(8,128)(2,1)S(1)} %get-tuple-element.84.left_ref, bf16[1024,256]{1,0:T(8,128)(2,1)S(1)} %collective-permute-done.14.refs_0_, bf16[1,1024,4096]{2,1,0:T(8,128)(2,1)} %gram.7.refs_1_), custom_call_target="tpu_custom_call", output_to_operand_aliasing={{}: (3, {})} | custom-call | flops 1024 | bytes 1024 | tf_op jit(solution)/shard_map/gram/pallas_call | solution.py:271
  74.9 0.4 collective-permute-done.19.refs_0_
  75.2 1.5 %gram.9 = bf16[1,1024,4096]{2,1,0:T(8,128)(2,1)} custom-call(f32[8,128]{1,0:T(8,128)S(1)} %get-tuple-element.83.count_ref, bf16[1024,1024]{1,0:T(8,128)(2,1)S(1)} %get-tuple-element.84.left_ref, bf16[1024,256]{1,0:T(8,128)(2,1)S(1)} %collective-permute-done.19.refs_0_, bf16[1,1024,4096]{2,1,0:T(8,128)(2,1)} %gram.8.refs_1_), custom_call_target="tpu_custom_call", output_to_operand_aliasing={{}: (3, {})} | custom-call | flops 1024 | bytes 1024 | tf_op jit(solution)/shard_map/gram/pallas_call | solution.py:271
  (8 shorter events, 0.0 us)
Async XLA Ops:
  2.1 1.2 %copy-start = (bf16[512,1024]{1,0:T(8,128)(2,1)S(1)}, bf16[512,1024]{1,0:T(8,128)(2,1)}, u32[]{:S(2)}) copy-start(bf16[512,1024]{1,0:T(8,128)(2,1)} %expr_ref.1) | copy-start | bytes 3145732
  5.0 9.7 %collective-permute-start.4 = (bf16[272,256]{1,0:T(8,128)(2,1)S(1)}, bf16[272,256]{1,0:T(8,128)(2,1)S(1)}, u32[]{:S(2)}, u32[]{:S(2)}) collective-permute-start(bf16[272,256]{1,0:T(8,128)(2,1)S(1)} %get-tuple-element.57), channel_id=1, source_target_pairs={{0,12},{4,8},{8,4},{12,0},{1,13},{5,9},{9,5},{13,1},{2,14},{6,10},... | collective-permute-start | bytes 417800 | tf_op jit(solution)/shard_map/cells_3_chunk_0/ppermute | solution.py:312
  10.1 8.4 %collective-permute-start.2 = (bf16[272,256]{1,0:T(8,128)(2,1)S(1)}, bf16[272,256]{1,0:T(8,128)(2,1)S(1)}, u32[]{:S(2)}, u32[]{:S(2)}) collective-permute-start(bf16[272,256]{1,0:T(8,128)(2,1)S(1)} %get-tuple-element.54), channel_id=1, source_target_pairs={{0,4},{4,0},{8,12},{12,8},{1,5},{5,1},{9,13},{13,9},{2,6},{6,2},{1... | collective-permute-start | bytes 417800 | tf_op jit(solution)/shard_map/cells_1_chunk_0/ppermute | solution.py:312
  10.1 17.0 %collective-permute-start = (bf16[272,256]{1,0:T(8,128)(2,1)S(1)}, bf16[272,256]{1,0:T(8,128)(2,1)S(1)}, u32[]{:S(2)}, u32[]{:S(2)}) collective-permute-start(bf16[272,256]{1,0:T(8,128)(2,1)S(1)} %get-tuple-element.51), channel_id=1, source_target_pairs={{0,8},{4,12},{8,0},{12,4},{1,9},{5,13},{9,1},{13,5},{2,10},{6,14},... | collective-permute-start | bytes 417800 | tf_op jit(solution)/shard_map/cells_2_chunk_0/ppermute | solution.py:312
  14.7 15.8 %collective-permute-start.5 = (bf16[256,256]{1,0:T(8,128)(2,1)S(1)}, bf16[256,256]{1,0:T(8,128)(2,1)S(1)}, u32[]{:S(2)}, u32[]{:S(2)}) collective-permute-start(bf16[256,256]{1,0:T(8,128)(2,1)S(1)} %get-tuple-element.58), channel_id=1, source_target_pairs={{0,12},{4,8},{8,4},{12,0},{1,13},{5,9},{9,5},{13,1},{2,14},{6,10},... | collective-permute-start | bytes 393224 | tf_op jit(solution)/shard_map/cells_3_chunk_1/ppermute | solution.py:312
  18.5 13.0 %collective-permute-start.3 = (bf16[256,256]{1,0:T(8,128)(2,1)S(1)}, bf16[256,256]{1,0:T(8,128)(2,1)S(1)}, u32[]{:S(2)}, u32[]{:S(2)}) collective-permute-start(bf16[256,256]{1,0:T(8,128)(2,1)S(1)} %get-tuple-element.55), channel_id=1, source_target_pairs={{0,4},{4,0},{8,12},{12,8},{1,5},{5,1},{9,13},{13,9},{2,6},{6,2},{1... | collective-permute-start | bytes 393224 | tf_op jit(solution)/shard_map/cells_1_chunk_1/ppermute | solution.py:312
  27.1 8.6 %collective-permute-start.1 = (bf16[256,256]{1,0:T(8,128)(2,1)S(1)}, bf16[256,256]{1,0:T(8,128)(2,1)S(1)}, u32[]{:S(2)}, u32[]{:S(2)}) collective-permute-start(bf16[256,256]{1,0:T(8,128)(2,1)S(1)} %get-tuple-element.52), channel_id=1, source_target_pairs={{0,8},{4,12},{8,0},{12,4},{1,9},{5,13},{9,1},{13,5},{2,10},{6,14},... | collective-permute-start | bytes 393224 | tf_op jit(solution)/shard_map/cells_2_chunk_1/ppermute | solution.py:312
  28.9 21.0 %collective-permute-start.13 = (bf16[1024,256]{1,0:T(8,128)(2,1)S(1)}, bf16[1024,256]{1,0:T(8,128)(2,1)S(1)}, u32[]{:S(2)}, u32[]{:S(2)}) collective-permute-start(bf16[1024,256]{1,0:T(8,128)(2,1)S(1)} %get-tuple-element.76), channel_id=1, source_target_pairs={{0,2},{1,3},{2,0},{3,1},{4,6},{5,7},{6,4},{7,5},{8,10},{9,11},{10,... | collective-permute-start | bytes 1572872 | tf_op jit(solution)/shard_map/far_0/ppermute | solution.py:315
  30.5 9.8 %collective-permute-start.11 = (bf16[256,256]{1,0:T(8,128)(2,1)S(1)}, bf16[256,256]{1,0:T(8,128)(2,1)S(1)}, u32[]{:S(2)}, u32[]{:S(2)}) collective-permute-start(bf16[256,256]{1,0:T(8,128)(2,1)S(1)} %get-tuple-element.74), channel_id=1, source_target_pairs={{0,12},{4,8},{8,4},{12,0},{1,13},{5,9},{9,5},{13,1},{2,14},{6,10},... | collective-permute-start | bytes 393224 | tf_op jit(solution)/shard_map/cells_3_chunk_2/ppermute | solution.py:312
  31.5 12.6 %collective-permute-start.9 = (bf16[256,256]{1,0:T(8,128)(2,1)S(1)}, bf16[256,256]{1,0:T(8,128)(2,1)S(1)}, u32[]{:S(2)}, u32[]{:S(2)}) collective-permute-start(bf16[256,256]{1,0:T(8,128)(2,1)S(1)} %get-tuple-element.70), channel_id=1, source_target_pairs={{0,4},{4,0},{8,12},{12,8},{1,5},{5,1},{9,13},{13,9},{2,6},{6,2},{1... | collective-permute-start | bytes 393224 | tf_op jit(solution)/shard_map/cells_1_chunk_2/ppermute | solution.py:312
  35.7 14.2 %collective-permute-start.7 = (bf16[256,256]{1,0:T(8,128)(2,1)S(1)}, bf16[256,256]{1,0:T(8,128)(2,1)S(1)}, u32[]{:S(2)}, u32[]{:S(2)}) collective-permute-start(bf16[256,256]{1,0:T(8,128)(2,1)S(1)} %get-tuple-element.66), channel_id=1, source_target_pairs={{0,8},{4,12},{8,0},{12,4},{1,9},{5,13},{9,1},{13,5},{2,10},{6,14},... | collective-permute-start | bytes 393224 | tf_op jit(solution)/shard_map/cells_2_chunk_2/ppermute | solution.py:312
  37.5 14.9 %collective-permute-start.6 = (bf16[1024,256]{1,0:T(8,128)(2,1)S(1)}, bf16[1024,256]{1,0:T(8,128)(2,1)S(1)}, u32[]{:S(2)}, u32[]{:S(2)}) collective-permute-start(bf16[1024,256]{1,0:T(8,128)(2,1)S(1)} %get-tuple-element.62), channel_id=1, source_target_pairs={{0,2},{1,3},{2,0},{3,1},{4,6},{5,7},{6,4},{7,5},{8,10},{9,11},{10,... | collective-permute-start | bytes 1572872 | tf_op jit(solution)/shard_map/far_1/ppermute | solution.py:315
  40.3 12.1 %collective-permute-start.12 = (bf16[256,256]{1,0:T(8,128)(2,1)S(1)}, bf16[256,256]{1,0:T(8,128)(2,1)S(1)}, u32[]{:S(2)}, u32[]{:S(2)}) collective-permute-start(bf16[256,256]{1,0:T(8,128)(2,1)S(1)} %get-tuple-element.75), channel_id=1, source_target_pairs={{0,12},{4,8},{8,4},{12,0},{1,13},{5,9},{9,5},{13,1},{2,14},{6,10},... | collective-permute-start | bytes 393224 | tf_op jit(solution)/shard_map/cells_3_chunk_3/ppermute | solution.py:312
  44.2 8.3 %collective-permute-start.10 = (bf16[256,256]{1,0:T(8,128)(2,1)S(1)}, bf16[256,256]{1,0:T(8,128)(2,1)S(1)}, u32[]{:S(2)}, u32[]{:S(2)}) collective-permute-start(bf16[256,256]{1,0:T(8,128)(2,1)S(1)} %get-tuple-element.71), channel_id=1, source_target_pairs={{0,4},{4,0},{8,12},{12,8},{1,5},{5,1},{9,13},{13,9},{2,6},{6,2},{1... | collective-permute-start | bytes 393224 | tf_op jit(solution)/shard_map/cells_1_chunk_3/ppermute | solution.py:312
  49.9 5.9 %collective-permute-start.8 = (bf16[256,256]{1,0:T(8,128)(2,1)S(1)}, bf16[256,256]{1,0:T(8,128)(2,1)S(1)}, u32[]{:S(2)}, u32[]{:S(2)}) collective-permute-start(bf16[256,256]{1,0:T(8,128)(2,1)S(1)} %get-tuple-element.67), channel_id=1, source_target_pairs={{0,8},{4,12},{8,0},{12,4},{1,9},{5,13},{9,1},{13,5},{2,10},{6,14},... | collective-permute-start | bytes 393224 | tf_op jit(solution)/shard_map/cells_2_chunk_3/ppermute | solution.py:312
  51.7 12.2 %collective-permute-start.17 = (bf16[1024,256]{1,0:T(8,128)(2,1)S(1)}, bf16[1024,256]{1,0:T(8,128)(2,1)S(1)}, u32[]{:S(2)}, u32[]{:S(2)}) collective-permute-start(bf16[1024,256]{1,0:T(8,128)(2,1)S(1)} %get-tuple-element.88), channel_id=1, source_target_pairs={{0,2},{1,3},{2,0},{3,1},{4,6},{5,7},{6,4},{7,5},{8,10},{9,11},{10,... | collective-permute-start | bytes 1572872 | tf_op jit(solution)/shard_map/far_2/ppermute | solution.py:315
  57.1 8.8 %collective-permute-start.15 = (bf16[1024,1024]{1,0:T(8,128)(2,1)S(1)}, bf16[1024,1024]{1,0:T(8,128)(2,1)S(1)}, u32[]{:S(2)}, u32[]{:S(2)}) collective-permute-start(bf16[1024,1024]{1,0:T(8,128)(2,1)S(1)} %get-tuple-element.86.refs_0_), channel_id=1, source_target_pairs={{0,1},{1,0},{2,3},{3,2},{4,5},{5,4},{6,7},{7,6},{8,9},{9,8},{10,11... | collective-permute-start | bytes 6291464 | tf_op jit(solution)/shard_map/near/ppermute | solution.py:319
  57.2 8.7 %collective-permute-start.16 = (bf16[1024,512]{1,0:T(8,128)(2,1)S(1)}, bf16[1024,512]{1,0:T(8,128)(2,1)S(1)}, u32[]{:S(2)}, u32[]{:S(2)}) collective-permute-start(bf16[1024,512]{1,0:T(8,128)(2,1)S(1)} %get-tuple-element.87.refs_1_), channel_id=1, source_target_pairs={{0,1},{1,0},{2,3},{3,2},{4,5},{5,4},{6,7},{7,6},{8,9},{9,8},{10,11... | collective-permute-start | bytes 3145736 | tf_op jit(solution)/shard_map/far_near/ppermute | solution.py:319
  57.7 15.6 %collective-permute-start.14 = (bf16[1024,256]{1,0:T(8,128)(2,1)S(1)}, bf16[1024,256]{1,0:T(8,128)(2,1)S(1)}, u32[]{:S(2)}, u32[]{:S(2)}) collective-permute-start(bf16[1024,256]{1,0:T(8,128)(2,1)S(1)} %get-tuple-element.85), channel_id=1, source_target_pairs={{0,2},{1,3},{2,0},{3,1},{4,6},{5,7},{6,4},{7,5},{8,10},{9,11},{10,... | collective-permute-start | bytes 1572872 | tf_op jit(solution)/shard_map/far_3/ppermute | solution.py:315
  63.9 2.0 %collective-permute-start.18 = (bf16[1024,256]{1,0:T(8,128)(2,1)S(1)}, bf16[1024,256]{1,0:T(8,128)(2,1)S(1)}, u32[]{:S(2)}, u32[]{:S(2)}) collective-permute-start(bf16[1024,256]{1,0:T(8,128)(2,1)S(1)} %collective-permute-done.17.refs_0_), channel_id=1, source_target_pairs={{0,1},{1,0},{2,3},{3,2},{4,5},{5,4},{6,7},{7,6},{8,9},{9,8},{10,11... | collective-permute-start | bytes 1572872 | tf_op jit(solution)/shard_map/far_near_2/ppermute | solution.py:319
  73.3 1.9 %collective-permute-start.19 = (bf16[1024,256]{1,0:T(8,128)(2,1)S(1)}, bf16[1024,256]{1,0:T(8,128)(2,1)S(1)}, u32[]{:S(2)}, u32[]{:S(2)}) collective-permute-start(bf16[1024,256]{1,0:T(8,128)(2,1)S(1)} %collective-permute-done.14.refs_0_), channel_id=1, source_target_pairs={{0,1},{1,0},{2,3},{3,2},{4,5},{5,4},{6,7},{7,6},{8,9},{9,8},{10,11... | collective-permute-start | bytes 1572872 | tf_op jit(solution)/shard_map/far_near_3/ppermute | solution.py:319

commit v15 on v13

--- a/solution.py
+++ b/solution.py
@@ -96,7 +96,7 @@
             copies.append(pltpu.make_async_copy(source, spot, sems.at[2 + len(copies)]))
             copies[-1].start()
     width = work.shape[1]
-    mean = mean_ref[:, start : start + width]
+    mean = mean_ref[0:1, start : start + width]
     piece = min(lead, cap)
     total = jnp.zeros((1, width), jnp.float32)
     count = jnp.zeros((1, 1), jnp.float32)
@@ -317,7 +317,8 @@
         with jax.named_scope(name):
             return lax.ppermute(after(panel_, *waits), "blk", [(b, b ^ 1) for b in range(blocks)])
 
-    mean = gene_mean.reshape(1, panel)
+    mean = jnp.broadcast_to(after(gene_mean, packed[0][0]), (8, panel))
+
     order = sorted(range(1, types), key=lambda j: (j == 3, j == 1, j))
     left, own, far, before = None, None, [], None
     for k in range(chunks):
@@ -348,12 +349,10 @@
     near = side("near", own)
     joined_near = [[side("far_near", p)] for p in joined] or [[]] * (chips - 1)
     joined = [[p] for p in joined] or [[]] * (chips - 1)
-    groups = [([own], (0, 0, 0))] + [(p, (d, 0, 0)) for d, p in enumerate(joined, 1) if p]
-    out = multiply(groups, None, brief)
+    out = multiply([([own], (0, 0, 0))], None, brief)
     final = [across(after(scaled, out), d) for d in range(1, chips)]
     second = [side(f"far_near_{last - 1}", p, own) for p in far[last - 1]]
-    edge = starts[last - 1]
-    groups = [([p], (d, 0, edge)) for d, p in enumerate(far[last - 1], 1)]
+    groups = [([*p, far[last - 1][i]], (i + 1, 0, 0)) for i, p in enumerate(joined)]
     out = multiply(groups, out, lengthy)
     groups = [([near], (0, 1, 0))]
     groups += [([*p, second[i]], (i + 1, 1, 0)) for i, p in enumerate(joined_near)]

time: 80.4 us -> 78.9 us (0.981)
  waiting for transfers between devices: 27.2 us -> 25.8 us
    ppermute x4, waiting for transfers between devices: 1.25 us -> 0.37 us  [side(): lax.ppermute(after(panel_, *waits), 'blk', [(b, b ^ 1) for b in range(blo...]
    unnamed x10 -> x6, local copies, waits for them, and re-layouts: 3.27 us -> 2.58 us
  transfers between devices with their start and end apart: 20 -> 20, of which waited for: 10 -> 10; matrix products, arithmetic and copies ran while one was open for 0% -> 1% of each run, Pallas kernels for 26% -> 26%
where the time goes in v15:
time: 78.9 us; the launch traced here: 78.7 us
  waiting for transfers between devices  25.8 us (33%)
  starting transfers between devices  25.5 us (32%)
  Pallas kernels  23.8 us (30%)
  local copies, waits for them, and re-layouts  3.27 us (4%)
    ppermute x12, starting transfers between devices, swap(): return lax.ppermute(block, 'cells', [(s, s ^ by) for s in range(types)])  21.3 us
    ppermute x12, waiting for transfers between devices, swap(): return lax.ppermute(block, 'cells', [(s, s ^ by) for s in range(types)])  19.2 us
    pallas_call x5, Pallas kernels, gram(): pl.pallas_call(functools.partial(gram_kernel, blocks, cores, strip, layou...  15.4 us
    pallas_call x4, Pallas kernels, standardize(): pl.pallas_call(functools.partial(standardize_kernel, types, cap, lead, se...  6.71 us
    ppermute x4, waiting for transfers between devices, across(): lax.ppermute(panel_, 'blk', [(b, (b + by * cores) % blocks) for b in rang...  6.21 us
    ppermute x4, starting transfers between devices, across(): lax.ppermute(panel_, 'blk', [(b, (b + by * cores) % blocks) for b in rang...  3.55 us
    unnamed x6, local copies, waits for them, and re-layouts  2.58 us
    pallas_call x1, Pallas kernels, pack(): pl.pallas_call(functools.partial(pack_kernel, types, cap, widths), out_sh...  1.71 us
  transfers between devices with their start and end apart: 20, of which 10 were waited for; matrix products, arithmetic and copies ran while one was open for 1% of the time, Pallas kernels for 26%

profile of v15, /device:TPU:0, one launch (start us, length us, event | category | flops | bytes accessed | tf_op | source)
XLA Modules:
  0.0 78.7 jit_solution(8705321731623699011)
XLA Ops:
  0.0 1.2 %copy-done = bf16[512,1024]{1,0:T(8,128)(2,1)S(1)} copy-done((bf16[512,1024]{1,0:T(8,128)(2,1)S(1)}, bf16[512,1024]{1,0:T(8,128)(2,1)}, u32[]{:S(2)}) %copy-start) | copy-done | bytes 1048600
  1.2 0.7 copy-done.1
  1.9 0.7 copy-done.2
  2.6 1.7 %pack.1 = (bf16[272,256]{1,0:T(8,128)(2,1)S(1)}, bf16[272,256]{1,0:T(8,128)(2,1)S(1)}, bf16[272,256]{1,0:T(8,128)(2,1)S(1)}, bf16[272,256]{1,0:T(8,128)(2,1)S(1)...) custom-call(s32[512]{0:T(512)S(1)} %copy-done.1, ...), custom_call_target="tpu_custom_call" | custom-call | flops 1024 | bytes 1024 | tf_op jit(solution)/shard_map/pack/pallas_call | solution.py:68
  4.3 5.1 %collective-permute-start.4 = (bf16[272,256]{1,0:T(8,128)(2,1)S(1)}, bf16[272,256]{1,0:T(8,128)(2,1)S(1)}, u32[]{:S(2)}, u32[]{:S(2)}) collective-permute-start(bf16[272,256]{1,0:T(8,128)(2,1)S(1)} %get-tuple-element.61), channel_id=1, source_target_pairs={{0,12},{4,8},{8,4},{12,0},{1,13},{5,9},{9,5},{13,1},{2,14},{6,10},... | collective-permute-start | bytes 417800 | tf_op jit(solution)/shard_map/cells_3_chunk_0/ppermute | solution.py:311
  9.4 0.0 collective-permute-start.2
  9.4 0.6 collective-permute-start
  10.1 3.9 %collective-permute-done.4.refs_3_.refs_7_ = bf16[272,256]{1,0:T(8,128)(2,1)S(1)} collective-permute-done((bf16[272,256]{1,0:T(8,128)(2,1)S(1)}, bf16[272,256]{1,0:T(8,128)(2,1)S(1)}, u32[]{:S(2)}, u32[]{:S(2)}) %collective-permute-start.4) | collective-permute-done | bytes 139296 | tf_op jit(solution)/shard_map/cells_3_chunk_0/ppermute | solution.py:311
  14.0 3.8 %collective-permute-start.5 = (bf16[256,256]{1,0:T(8,128)(2,1)S(1)}, bf16[256,256]{1,0:T(8,128)(2,1)S(1)}, u32[]{:S(2)}, u32[]{:S(2)}) collective-permute-start(bf16[256,256]{1,0:T(8,128)(2,1)S(1)} %get-tuple-element.62), channel_id=1, source_target_pairs={{0,12},{4,8},{8,4},{12,0},{1,13},{5,9},{9,5},{13,1},{2,14},{6,10},... | collective-permute-start | bytes 393224 | tf_op jit(solution)/shard_map/cells_3_chunk_1/ppermute | solution.py:311
  17.8 1.2 %collective-permute-start.3 = (bf16[256,256]{1,0:T(8,128)(2,1)S(1)}, bf16[256,256]{1,0:T(8,128)(2,1)S(1)}, u32[]{:S(2)}, u32[]{:S(2)}) collective-permute-start(bf16[256,256]{1,0:T(8,128)(2,1)S(1)} %get-tuple-element.59), channel_id=1, source_target_pairs={{0,4},{4,0},{8,12},{12,8},{1,5},{5,1},{9,13},{13,9},{2,6},{6,2},{1... | collective-permute-start | bytes 393224 | tf_op jit(solution)/shard_map/cells_1_chunk_1/ppermute | solution.py:311
  19.0 7.5 %collective-permute-done.refs_1_.refs_5_ = bf16[272,256]{1,0:T(8,128)(2,1)S(1)} collective-permute-done((bf16[272,256]{1,0:T(8,128)(2,1)S(1)}, bf16[272,256]{1,0:T(8,128)(2,1)S(1)}, u32[]{:S(2)}, u32[]{:S(2)}) %collective-permute-start) | collective-permute-done | bytes 139296 | tf_op jit(solution)/shard_map/cells_2_chunk_0/ppermute | solution.py:311
  26.4 0.0 collective-permute-start.1
  26.4 0.7 broadcast_in_dim.3.mean_ref
  27.1 1.8 %standardize.4 = (bf16[1024,256]{1,0:T(8,128)(2,1)S(1)}, bf16[1024,1024]{1,0:T(8,128)(2,1)S(1)}, f32[8,128]{1,0:T(8,128)}, bf16[1024,1024]{1,0:T(8,128)(2,1)S(1)}) custom-call(f32[8,1024]{1,0:T(8,128)S(1)} %broadcast_in_dim.3.mean_ref, bf16[272,256]{1,0:T(8,128)(2,1)S(1)} %get-tuple-element.50.refs_0_.refs_4_, ...), custom_call_target="tpu_custom_call" | custom-call | flops 20000000000 | bytes 1024 | tf_op jit(solution)/shard_map/standardize/pallas_call | solution.py:173
  28.9 1.6 %collective-permute-start.13 = (bf16[1024,256]{1,0:T(8,128)(2,1)S(1)}, bf16[1024,256]{1,0:T(8,128)(2,1)S(1)}, u32[]{:S(2)}, u32[]{:S(2)}) collective-permute-start(bf16[1024,256]{1,0:T(8,128)(2,1)S(1)} %get-tuple-element.79), channel_id=1, source_target_pairs={{0,2},{1,3},{2,0},{3,1},{4,6},{5,7},{6,4},{7,5},{8,10},{9,11},{10,... | collective-permute-start | bytes 1572872 | tf_op jit(solution)/shard_map/far_0/ppermute | solution.py:314
  30.5 0.0 collective-permute-done.5.refs_3_
  30.5 1.0 %collective-permute-start.11 = (bf16[256,256]{1,0:T(8,128)(2,1)S(1)}, bf16[256,256]{1,0:T(8,128)(2,1)S(1)}, u32[]{:S(2)}, u32[]{:S(2)}) collective-permute-start(bf16[256,256]{1,0:T(8,128)(2,1)S(1)} %get-tuple-element.77), channel_id=1, source_target_pairs={{0,12},{4,8},{8,4},{12,0},{1,13},{5,9},{9,5},{13,1},{2,14},{6,10},... | collective-permute-start | bytes 393224 | tf_op jit(solution)/shard_map/cells_3_chunk_2/ppermute | solution.py:311
  31.5 0.0 collective-permute-done.3.refs_2_
  31.5 2.5 %collective-permute-start.9 = (bf16[256,256]{1,0:T(8,128)(2,1)S(1)}, bf16[256,256]{1,0:T(8,128)(2,1)S(1)}, u32[]{:S(2)}, u32[]{:S(2)}) collective-permute-start(bf16[256,256]{1,0:T(8,128)(2,1)S(1)} %get-tuple-element.73), channel_id=1, source_target_pairs={{0,4},{4,0},{8,12},{12,8},{1,5},{5,1},{9,13},{13,9},{2,6},{6,2},{1... | collective-permute-start | bytes 393224 | tf_op jit(solution)/shard_map/cells_1_chunk_2/ppermute | solution.py:311
  34.0 1.2 %collective-permute-done.1.refs_1_ = bf16[256,256]{1,0:T(8,128)(2,1)S(1)} collective-permute-done((bf16[256,256]{1,0:T(8,128)(2,1)S(1)}, bf16[256,256]{1,0:T(8,128)(2,1)S(1)}, u32[]{:S(2)}, u32[]{:S(2)}) %collective-permute-start.1) | collective-permute-done | bytes 131104 | tf_op jit(solution)/shard_map/cells_2_chunk_1/ppermute | solution.py:311
  35.2 0.0 collective-permute-start.7
  35.2 1.8 %standardize.5 = (bf16[1024,256]{1,0:T(8,128)(2,1)S(1)}, bf16[1024,1024]{1,0:T(8,128)(2,1)S(1)}, f32[8,128]{1,0:T(8,128)}, bf16[1024,1024]{1,0:T(8,128)(2,1)S(1)}) custom-call(f32[8,1024]{1,0:T(8,128)S(1)} %broadcast_in_dim.3.mean_ref, bf16[256,256]{1,0:T(8,128)(2,1)S(1)} %get-tuple-element.53.refs_0_, ...), custom_call_target="tpu_custom_call", output_to_operand_aliasing={{1}: (9, {}), {3}: (10, {})} | custom-call | flops 20000000000 | bytes 1024 | tf_op jit(solution)/shard_map/standardize/pallas_call | solution.py:173
  37.0 1.3 %collective-permute-start.6 = (bf16[1024,256]{1,0:T(8,128)(2,1)S(1)}, bf16[1024,256]{1,0:T(8,128)(2,1)S(1)}, u32[]{:S(2)}, u32[]{:S(2)}) collective-permute-start(bf16[1024,256]{1,0:T(8,128)(2,1)S(1)} %get-tuple-element.65), channel_id=1, source_target_pairs={{0,2},{1,3},{2,0},{3,1},{4,6},{5,7},{6,4},{7,5},{8,10},{9,11},{10,... | collective-permute-start | bytes 1572872 | tf_op jit(solution)/shard_map/far_1/ppermute | solution.py:314
  38.2 0.2 collective-permute-done.11.refs_3_
  38.4 5.0 %collective-permute-start.12 = (bf16[256,256]{1,0:T(8,128)(2,1)S(1)}, bf16[256,256]{1,0:T(8,128)(2,1)S(1)}, u32[]{:S(2)}, u32[]{:S(2)}) collective-permute-start(bf16[256,256]{1,0:T(8,128)(2,1)S(1)} %get-tuple-element.78), channel_id=1, source_target_pairs={{0,12},{4,8},{8,4},{12,0},{1,13},{5,9},{9,5},{13,1},{2,14},{6,10},... | collective-permute-start | bytes 393224 | tf_op jit(solution)/shard_map/cells_3_chunk_3/ppermute | solution.py:311
  43.4 0.0 collective-permute-done.9.refs_2_
  43.4 2.1 %collective-permute-start.10 = (bf16[256,256]{1,0:T(8,128)(2,1)S(1)}, bf16[256,256]{1,0:T(8,128)(2,1)S(1)}, u32[]{:S(2)}, u32[]{:S(2)}) collective-permute-start(bf16[256,256]{1,0:T(8,128)(2,1)S(1)} %get-tuple-element.74), channel_id=1, source_target_pairs={{0,4},{4,0},{8,12},{12,8},{1,5},{5,1},{9,13},{13,9},{2,6},{6,2},{1... | collective-permute-start | bytes 393224 | tf_op jit(solution)/shard_map/cells_1_chunk_3/ppermute | solution.py:311
  45.5 3.7 %collective-permute-done.7.refs_1_ = bf16[256,256]{1,0:T(8,128)(2,1)S(1)} collective-permute-done((bf16[256,256]{1,0:T(8,128)(2,1)S(1)}, bf16[256,256]{1,0:T(8,128)(2,1)S(1)}, u32[]{:S(2)}, u32[]{:S(2)}) %collective-permute-start.7) | collective-permute-done | bytes 131104 | tf_op jit(solution)/shard_map/cells_2_chunk_2/ppermute | solution.py:311
  49.2 0.0 collective-permute-start.8
  49.2 1.8 %standardize.6 = (bf16[1024,256]{1,0:T(8,128)(2,1)S(1)}, bf16[1024,1024]{1,0:T(8,128)(2,1)S(1)}, f32[8,128]{1,0:T(8,128)}, bf16[1024,1024]{1,0:T(8,128)(2,1)S(1)}) custom-call(f32[8,1024]{1,0:T(8,128)S(1)} %broadcast_in_dim.3.mean_ref, bf16[256,256]{1,0:T(8,128)(2,1)S(1)} %get-tuple-element.81.refs_0_, ...), custom_call_target="tpu_custom_call", output_to_operand_aliasing={{1}: (9, {}), {3}: (10, {})} | custom-call | flops 20000000000 | bytes 1024 | tf_op jit(solution)/shard_map/standardize/pallas_call | solution.py:173
  51.0 0.1 collective-permute-start.17
  51.1 1.9 %collective-permute-done.6.refs_9_ = bf16[1024,256]{1,0:T(8,128)(2,1)S(1)} collective-permute-done((bf16[1024,256]{1,0:T(8,128)(2,1)S(1)}, bf16[1024,256]{1,0:T(8,128)(2,1)S(1)}, u32[]{:S(2)}, u32[]{:S(2)}) %collective-permute-start.6) | collective-permute-done | bytes 524320 | tf_op jit(solution)/shard_map/far_1/ppermute | solution.py:314
  53.0 2.8 %collective-permute-done.8.refs_1_ = bf16[256,256]{1,0:T(8,128)(2,1)S(1)} collective-permute-done((bf16[256,256]{1,0:T(8,128)(2,1)S(1)}, bf16[256,256]{1,0:T(8,128)(2,1)S(1)}, u32[]{:S(2)}, u32[]{:S(2)}) %collective-permute-start.8) | collective-permute-done | bytes 131104 | tf_op jit(solution)/shard_map/cells_2_chunk_3/ppermute | solution.py:311
  55.8 1.3 %standardize.7 = (bf16[1024,256]{1,0:T(8,128)(2,1)S(1)}, bf16[1024,1024]{1,0:T(8,128)(2,1)S(1)}, f32[8,128]{1,0:T(8,128)S(1)}, bf16[1024,1024]{1,0:T(8,128)(2,1)S(1)}, bf16[1024,512]{1,0:T(8,128)(2,1)S(1)}) custom-call(f32[8,1024]{1,0:T(8,128)S(1)} %broadcast_in_dim.3.mean_ref, ...), custom_call_target="tpu_custom_call", output_to_operand_aliasing={{1}: (11, {}), {3}: (12, {})} | custom-call | flops 20000000000 | bytes 1024 | tf_op jit(solution)/shard_map/standardize/pallas_call | solution.py:173
  57.2 0.1 collective-permute-start.15
  57.2 3.4 %gram.5.refs_2_ = bf16[1,1024,4096]{2,1,0:T(8,128)(2,1)} custom-call(f32[8,128]{1,0:T(8,128)S(1)} %get-tuple-element.86.count_ref, bf16[1024,1024]{1,0:T(8,128)(2,1)S(1)} %get-tuple-element.87.left_ref, bf16[1024,1024]{1,0:T(8,128)(2,1)S(1)} %get-tuple-element.89.refs_0_), custom_call_target="tpu_custom_call" | custom-call | flops 1024 | bytes 1024 | tf_op jit(solution)/shard_map/gram/pallas_call | solution.py:273
  60.6 0.6 collective-permute-start.16
  61.2 0.6 collective-permute-start.14
  61.8 0.3 collective-permute-done.17.refs_1_
  62.1 0.0 collective-permute-start.18
  62.1 2.9 %gram.6.refs_3_ = bf16[1,1024,4096]{2,1,0:T(8,128)(2,1)} custom-call(f32[8,128]{1,0:T(8,128)S(1)} %get-tuple-element.86.count_ref, bf16[1024,1024]{1,0:T(8,128)(2,1)S(1)} %get-tuple-element.87.left_ref, bf16[1024,512]{1,0:T(8,128)(2,1)S(1)} %get-tuple-element.91.refs_0_, ...), custom_call_target="tpu_custom_call", output_to_operand_aliasing={{}: (4, {})} | custom-call | flops 20000000000 | bytes 1024 | tf_op jit(solution)/shard_map/gram/pallas_call | solution.py:273
  64.9 0.0 collective-permute-done.18.refs_2_
  65.0 0.0 collective-permute-done.16.refs_1_
  65.0 6.1 %gram.7.refs_1_ = bf16[1,1024,4096]{2,1,0:T(8,128)(2,1)} custom-call(f32[8,128]{1,0:T(8,128)S(1)} %get-tuple-element.86.count_ref, bf16[1024,1024]{1,0:T(8,128)(2,1)S(1)} %get-tuple-element.87.left_ref, bf16[1024,1024]{1,0:T(8,128)(2,1)S(1)} %collective-permute-done.15.refs_0_, ...), custom_call_target="tpu_custom_call", output_to_operand_aliasing={{}: (5, {})} | custom-call | flops 1024 | bytes 1024 | tf_op jit(solution)/shard_map/gram/pallas_call | solution.py:273
  71.1 4.0 %collective-permute-done.14.refs_0_ = bf16[1024,256]{1,0:T(8,128)(2,1)S(1)} collective-permute-done((bf16[1024,256]{1,0:T(8,128)(2,1)S(1)}, bf16[1024,256]{1,0:T(8,128)(2,1)S(1)}, u32[]{:S(2)}, u32[]{:S(2)}) %collective-permute-start.14) | collective-permute-done | bytes 524320 | tf_op jit(solution)/shard_map/ppermute | solution.py:314
  75.1 1.5 %gram.8.refs_1_ = bf16[1,1024,4096]{2,1,0:T(8,128)(2,1)} custom-call(f32[8,128]{1,0:T(8,128)S(1)} %get-tuple-element.86.count_ref, bf16[1024,1024]{1,0:T(8,128)(2,1)S(1)} %get-tuple-element.87.left_ref, bf16[1024,256]{1,0:T(8,128)(2,1)S(1)} %collective-permute-done.14.refs_0_, bf16[1,1024,4096]{2,1,0:T(8,128)(2,1)} %gram.7.refs_1_), custom_call_target="tpu_custom_call", output_to_operand_aliasing={{}: (3, {})} | custom-call | flops 1024 | bytes 1024 | tf_op jit(solution)/shard_map/gram/pallas_call | solution.py:273
  76.6 0.4 collective-permute-done.19.refs_0_
  77.0 1.5 %gram.9 = bf16[1,1024,4096]{2,1,0:T(8,128)(2,1)} custom-call(f32[8,128]{1,0:T(8,128)S(1)} %get-tuple-element.86.count_ref, bf16[1024,1024]{1,0:T(8,128)(2,1)S(1)} %get-tuple-element.87.left_ref, bf16[1024,256]{1,0:T(8,128)(2,1)S(1)} %collective-permute-done.19.refs_0_, bf16[1,1024,4096]{2,1,0:T(8,128)(2,1)} %gram.8.refs_1_), custom_call_target="tpu_custom_call", output_to_operand_aliasing={{}: (3, {})} | custom-call | flops 1024 | bytes 1024 | tf_op jit(solution)/shard_map/gram/pallas_call | solution.py:273
  (9 shorter events, 0.0 us)
Async XLA Ops:
  0.0 1.2 %copy-start = (bf16[512,1024]{1,0:T(8,128)(2,1)S(1)}, bf16[512,1024]{1,0:T(8,128)(2,1)}, u32[]{:S(2)}) copy-start(bf16[512,1024]{1,0:T(8,128)(2,1)} %expr_ref.1) | copy-start | bytes 3145732
  1.2 0.7 copy-start.1
  1.9 0.7 copy-start.2
  4.3 9.7 %collective-permute-start.4 = (bf16[272,256]{1,0:T(8,128)(2,1)S(1)}, bf16[272,256]{1,0:T(8,128)(2,1)S(1)}, u32[]{:S(2)}, u32[]{:S(2)}) collective-permute-start(bf16[272,256]{1,0:T(8,128)(2,1)S(1)} %get-tuple-element.61), channel_id=1, source_target_pairs={{0,12},{4,8},{8,4},{12,0},{1,13},{5,9},{9,5},{13,1},{2,14},{6,10},... | collective-permute-start | bytes 417800 | tf_op jit(solution)/shard_map/cells_3_chunk_0/ppermute | solution.py:311
  9.4 8.4 %collective-permute-start.2 = (bf16[272,256]{1,0:T(8,128)(2,1)S(1)}, bf16[272,256]{1,0:T(8,128)(2,1)S(1)}, u32[]{:S(2)}, u32[]{:S(2)}) collective-permute-start(bf16[272,256]{1,0:T(8,128)(2,1)S(1)} %get-tuple-element.58), channel_id=1, source_target_pairs={{0,4},{4,0},{8,12},{12,8},{1,5},{5,1},{9,13},{13,9},{2,6},{6,2},{1... | collective-permute-start | bytes 417800 | tf_op jit(solution)/shard_map/cells_1_chunk_0/ppermute | solution.py:311
  9.4 17.0 %collective-permute-start = (bf16[272,256]{1,0:T(8,128)(2,1)S(1)}, bf16[272,256]{1,0:T(8,128)(2,1)S(1)}, u32[]{:S(2)}, u32[]{:S(2)}) collective-permute-start(bf16[272,256]{1,0:T(8,128)(2,1)S(1)} %get-tuple-element.55), channel_id=1, source_target_pairs={{0,8},{4,12},{8,0},{12,4},{1,9},{5,13},{9,1},{13,5},{2,10},{6,14},... | collective-permute-start | bytes 417800 | tf_op jit(solution)/shard_map/cells_2_chunk_0/ppermute | solution.py:311
  14.0 16.5 %collective-permute-start.5 = (bf16[256,256]{1,0:T(8,128)(2,1)S(1)}, bf16[256,256]{1,0:T(8,128)(2,1)S(1)}, u32[]{:S(2)}, u32[]{:S(2)}) collective-permute-start(bf16[256,256]{1,0:T(8,128)(2,1)S(1)} %get-tuple-element.62), channel_id=1, source_target_pairs={{0,12},{4,8},{8,4},{12,0},{1,13},{5,9},{9,5},{13,1},{2,14},{6,10},... | collective-permute-start | bytes 393224 | tf_op jit(solution)/shard_map/cells_3_chunk_1/ppermute | solution.py:311
  17.8 13.7 %collective-permute-start.3 = (bf16[256,256]{1,0:T(8,128)(2,1)S(1)}, bf16[256,256]{1,0:T(8,128)(2,1)S(1)}, u32[]{:S(2)}, u32[]{:S(2)}) collective-permute-start(bf16[256,256]{1,0:T(8,128)(2,1)S(1)} %get-tuple-element.59), channel_id=1, source_target_pairs={{0,4},{4,0},{8,12},{12,8},{1,5},{5,1},{9,13},{13,9},{2,6},{6,2},{1... | collective-permute-start | bytes 393224 | tf_op jit(solution)/shard_map/cells_1_chunk_1/ppermute | solution.py:311
  26.4 8.7 %collective-permute-start.1 = (bf16[256,256]{1,0:T(8,128)(2,1)S(1)}, bf16[256,256]{1,0:T(8,128)(2,1)S(1)}, u32[]{:S(2)}, u32[]{:S(2)}) collective-permute-start(bf16[256,256]{1,0:T(8,128)(2,1)S(1)} %get-tuple-element.56), channel_id=1, source_target_pairs={{0,8},{4,12},{8,0},{12,4},{1,9},{5,13},{9,1},{13,5},{2,10},{6,14},... | collective-permute-start | bytes 393224 | tf_op jit(solution)/shard_map/cells_2_chunk_1/ppermute | solution.py:311
  28.9 20.3 %collective-permute-start.13 = (bf16[1024,256]{1,0:T(8,128)(2,1)S(1)}, bf16[1024,256]{1,0:T(8,128)(2,1)S(1)}, u32[]{:S(2)}, u32[]{:S(2)}) collective-permute-start(bf16[1024,256]{1,0:T(8,128)(2,1)S(1)} %get-tuple-element.79), channel_id=1, source_target_pairs={{0,2},{1,3},{2,0},{3,1},{4,6},{5,7},{6,4},{7,5},{8,10},{9,11},{10,... | collective-permute-start | bytes 1572872 | tf_op jit(solution)/shard_map/far_0/ppermute | solution.py:314
  30.5 8.0 %collective-permute-start.11 = (bf16[256,256]{1,0:T(8,128)(2,1)S(1)}, bf16[256,256]{1,0:T(8,128)(2,1)S(1)}, u32[]{:S(2)}, u32[]{:S(2)}) collective-permute-start(bf16[256,256]{1,0:T(8,128)(2,1)S(1)} %get-tuple-element.77), channel_id=1, source_target_pairs={{0,12},{4,8},{8,4},{12,0},{1,13},{5,9},{9,5},{13,1},{2,14},{6,10},... | collective-permute-start | bytes 393224 | tf_op jit(solution)/shard_map/cells_3_chunk_2/ppermute | solution.py:311
  31.5 11.9 %collective-permute-start.9 = (bf16[256,256]{1,0:T(8,128)(2,1)S(1)}, bf16[256,256]{1,0:T(8,128)(2,1)S(1)}, u32[]{:S(2)}, u32[]{:S(2)}) collective-permute-start(bf16[256,256]{1,0:T(8,128)(2,1)S(1)} %get-tuple-element.73), channel_id=1, source_target_pairs={{0,4},{4,0},{8,12},{12,8},{1,5},{5,1},{9,13},{13,9},{2,6},{6,2},{1... | collective-permute-start | bytes 393224 | tf_op jit(solution)/shard_map/cells_1_chunk_2/ppermute | solution.py:311
  35.2 14.0 %collective-permute-start.7 = (bf16[256,256]{1,0:T(8,128)(2,1)S(1)}, bf16[256,256]{1,0:T(8,128)(2,1)S(1)}, u32[]{:S(2)}, u32[]{:S(2)}) collective-permute-start(bf16[256,256]{1,0:T(8,128)(2,1)S(1)} %get-tuple-element.69), channel_id=1, source_target_pairs={{0,8},{4,12},{8,0},{12,4},{1,9},{5,13},{9,1},{13,5},{2,10},{6,14},... | collective-permute-start | bytes 393224 | tf_op jit(solution)/shard_map/cells_2_chunk_2/ppermute | solution.py:311
  37.0 16.1 %collective-permute-start.6 = (bf16[1024,256]{1,0:T(8,128)(2,1)S(1)}, bf16[1024,256]{1,0:T(8,128)(2,1)S(1)}, u32[]{:S(2)}, u32[]{:S(2)}) collective-permute-start(bf16[1024,256]{1,0:T(8,128)(2,1)S(1)} %get-tuple-element.65), channel_id=1, source_target_pairs={{0,2},{1,3},{2,0},{3,1},{4,6},{5,7},{6,4},{7,5},{8,10},{9,11},{10,... | collective-permute-start | bytes 1572872 | tf_op jit(solution)/shard_map/far_1/ppermute | solution.py:314
  38.4 14.6 %collective-permute-start.12 = (bf16[256,256]{1,0:T(8,128)(2,1)S(1)}, bf16[256,256]{1,0:T(8,128)(2,1)S(1)}, u32[]{:S(2)}, u32[]{:S(2)}) collective-permute-start(bf16[256,256]{1,0:T(8,128)(2,1)S(1)} %get-tuple-element.78), channel_id=1, source_target_pairs={{0,12},{4,8},{8,4},{12,0},{1,13},{5,9},{9,5},{13,1},{2,14},{6,10},... | collective-permute-start | bytes 393224 | tf_op jit(solution)/shard_map/cells_3_chunk_3/ppermute | solution.py:311
  43.4 9.6 %collective-permute-start.10 = (bf16[256,256]{1,0:T(8,128)(2,1)S(1)}, bf16[256,256]{1,0:T(8,128)(2,1)S(1)}, u32[]{:S(2)}, u32[]{:S(2)}) collective-permute-start(bf16[256,256]{1,0:T(8,128)(2,1)S(1)} %get-tuple-element.74), channel_id=1, source_target_pairs={{0,4},{4,0},{8,12},{12,8},{1,5},{5,1},{9,13},{13,9},{2,6},{6,2},{1... | collective-permute-start | bytes 393224 | tf_op jit(solution)/shard_map/cells_1_chunk_3/ppermute | solution.py:311
  49.2 6.6 %collective-permute-start.8 = (bf16[256,256]{1,0:T(8,128)(2,1)S(1)}, bf16[256,256]{1,0:T(8,128)(2,1)S(1)}, u32[]{:S(2)}, u32[]{:S(2)}) collective-permute-start(bf16[256,256]{1,0:T(8,128)(2,1)S(1)} %get-tuple-element.70), channel_id=1, source_target_pairs={{0,8},{4,12},{8,0},{12,4},{1,9},{5,13},{9,1},{13,5},{2,10},{6,14},... | collective-permute-start | bytes 393224 | tf_op jit(solution)/shard_map/cells_2_chunk_3/ppermute | solution.py:311
  51.0 11.0 %collective-permute-start.17 = (bf16[1024,256]{1,0:T(8,128)(2,1)S(1)}, bf16[1024,256]{1,0:T(8,128)(2,1)S(1)}, u32[]{:S(2)}, u32[]{:S(2)}) collective-permute-start(bf16[1024,256]{1,0:T(8,128)(2,1)S(1)} %get-tuple-element.92), channel_id=1, source_target_pairs={{0,2},{1,3},{2,0},{3,1},{4,6},{5,7},{6,4},{7,5},{8,10},{9,11},{10,... | collective-permute-start | bytes 1572872 | tf_op jit(solution)/shard_map/far_2/ppermute | solution.py:314
  57.2 7.8 %collective-permute-start.15 = (bf16[1024,1024]{1,0:T(8,128)(2,1)S(1)}, bf16[1024,1024]{1,0:T(8,128)(2,1)S(1)}, u32[]{:S(2)}, u32[]{:S(2)}) collective-permute-start(bf16[1024,1024]{1,0:T(8,128)(2,1)S(1)} %get-tuple-element.89.refs_0_), channel_id=1, source_target_pairs={{0,1},{1,0},{2,3},{3,2},{4,5},{5,4},{6,7},{7,6},{8,9},{9,8},{10,11... | collective-permute-start | bytes 6291464 | tf_op jit(solution)/shard_map/near/ppermute | solution.py:318
  60.6 4.4 %collective-permute-start.16 = (bf16[1024,512]{1,0:T(8,128)(2,1)S(1)}, bf16[1024,512]{1,0:T(8,128)(2,1)S(1)}, u32[]{:S(2)}, u32[]{:S(2)}) collective-permute-start(bf16[1024,512]{1,0:T(8,128)(2,1)S(1)} %get-tuple-element.91.refs_0_), channel_id=1, source_target_pairs={{0,1},{1,0},{2,3},{3,2},{4,5},{5,4},{6,7},{7,6},{8,9},{9,8},{10,11... | collective-permute-start | bytes 3145736 | tf_op jit(solution)/shard_map/far_near/ppermute | solution.py:318
  61.2 13.9 %collective-permute-start.14 = (bf16[1024,256]{1,0:T(8,128)(2,1)S(1)}, bf16[1024,256]{1,0:T(8,128)(2,1)S(1)}, u32[]{:S(2)}, u32[]{:S(2)}) collective-permute-start(bf16[1024,256]{1,0:T(8,128)(2,1)S(1)} %get-tuple-element.90), channel_id=1, source_target_pairs={{0,2},{1,3},{2,0},{3,1},{4,6},{5,7},{6,4},{7,5},{8,10},{9,11},{10,... | collective-permute-start | bytes 1572872 | tf_op jit(solution)/shard_map/ppermute | solution.py:314
  62.1 2.9 %collective-permute-start.18 = (bf16[1024,256]{1,0:T(8,128)(2,1)S(1)}, bf16[1024,256]{1,0:T(8,128)(2,1)S(1)}, u32[]{:S(2)}, u32[]{:S(2)}) collective-permute-start(bf16[1024,256]{1,0:T(8,128)(2,1)S(1)} %collective-permute-done.17.refs_1_), channel_id=1, source_target_pairs={{0,1},{1,0},{2,3},{3,2},{4,5},{5,4},{6,7},{7,6},{8,9},{9,8},{10,11... | collective-permute-start | bytes 1572872 | tf_op jit(solution)/shard_map/far_near_2/ppermute | solution.py:318
  75.1 1.9 %collective-permute-start.19 = (bf16[1024,256]{1,0:T(8,128)(2,1)S(1)}, bf16[1024,256]{1,0:T(8,128)(2,1)S(1)}, u32[]{:S(2)}, u32[]{:S(2)}) collective-permute-start(bf16[1024,256]{1,0:T(8,128)(2,1)S(1)} %collective-permute-done.14.refs_0_), channel_id=1, source_target_pairs={{0,1},{1,0},{2,3},{3,2},{4,5},{5,4},{6,7},{7,6},{8,9},{9,8},{10,11... | collective-permute-start | bytes 1572872 | tf_op jit(solution)/shard_map/far_near_3/ppermute | solution.py:318

commit v16 on v15

--- a/solution.py
+++ b/solution.py
@@ -224,11 +224,11 @@
             pltpu.make_async_copy(source, spot, join_sems.at[sent]).start()
             sent += 1
     stores, sent = [], 0
-    for (panels, (chip, flip, first)), parts in zip(groups, joins):
+    for (panels, (chip, flip, first, *part)), parts in zip(groups, joins):
         for _, source, spot in parts:
             pltpu.make_async_copy(source, spot, join_sems.at[sent]).wait()
             sent += 1
-        width = sum(sources[index].shape[1] for index in panels)
+        width = part[0] if part else sum(sources[index].shape[1] for index in panels)
         owner = lax.rem(me + (blocks - chip * cores), blocks)
         owner = jnp.bitwise_xor(owner, flip)
         column = pl.multiple_of(owner * rows + first, 128)
@@ -239,7 +239,8 @@
             if parts:
                 right = joined[:, parts[0][0] : parts[0][0] + width]
             else:
-                right = sources[panels[0]][...]
+                skip = first if part else 0
+                right = sources[panels[0]][:, skip : skip + width]
             product = jnp.dot(
                 left_ref[row : row + strip, :], right, preferred_element_type=jnp.float32
             )
@@ -326,7 +327,7 @@
         for j in order:
             block = packed[k][j]
             if k:
-                block = after(block, before[len(arrived)])
+                block = after(block, before[len(arrived)], *([mean] if k == 1 else []))
             with jax.named_scope(f"cells_{j}_chunk_{k}"):
                 arrived.append(swap(block, j))
         before = list(arrived)
@@ -349,10 +350,12 @@
     near = side("near", own)
     joined_near = [[side("far_near", p)] for p in joined] or [[]] * (chips - 1)
     joined = [[p] for p in joined] or [[]] * (chips - 1)
-    out = multiply([([own], (0, 0, 0))], None, brief)
+    half = panel // 2
+    out = multiply([([own], (0, 0, 0, half))], None, brief)
     final = [across(after(scaled, out), d) for d in range(1, chips)]
     second = [side(f"far_near_{last - 1}", p, own) for p in far[last - 1]]
-    groups = [([*p, far[last - 1][i]], (i + 1, 0, 0)) for i, p in enumerate(joined)]
+    groups = [([own], (0, 0, half, half))]
+    groups += [([*p, far[last - 1][i]], (i + 1, 0, 0)) for i, p in enumerate(joined)]
     out = multiply(groups, out, lengthy)
     groups = [([near], (0, 1, 0))]
     groups += [([*p, second[i]], (i + 1, 1, 0)) for i, p in enumerate(joined_near)]

time: 78.9 us -> 79.1 us (level)
  the two profiles are of different devices: /device:TPU:0 before, /device:TPU:11 now
where the time goes in v16:
time: 79.1 us; the launch traced here: 78.9 us
  starting transfers between devices  27.6 us (35%)
  Pallas kernels  24.7 us (31%)
  waiting for transfers between devices  23 us (29%)
  local copies, waits for them, and re-layouts  3.27 us (4%)
    ppermute x12, waiting for transfers between devices, swap(): return lax.ppermute(block, 'cells', [(s, s ^ by) for s in range(types)])  22.7 us
    ppermute x12, starting transfers between devices, swap(): return lax.ppermute(block, 'cells', [(s, s ^ by) for s in range(types)])  16.8 us
    pallas_call x5, Pallas kernels, gram(): pl.pallas_call(functools.partial(gram_kernel, blocks, cores, strip, layou...  16.3 us
    ppermute x4, starting transfers between devices, side(): lax.ppermute(after(panel_, *waits), 'blk', [(b, b ^ 1) for b in range(blo...  9.61 us
    pallas_call x4, Pallas kernels, standardize(): pl.pallas_call(functools.partial(standardize_kernel, types, cap, lead, se...  6.7 us
    unnamed x6, local copies, waits for them, and re-layouts  2.58 us
    pallas_call x1, Pallas kernels, pack(): pl.pallas_call(functools.partial(pack_kernel, types, cap, widths), out_sh...  1.72 us
  transfers between devices with their start and end apart: 20, of which 9 were waited for; matrix products, arithmetic and copies ran while one was open for 1% of the time, Pallas kernels for 27%

profile of v16, /device:TPU:11, one launch (start us, length us, event | category | flops | bytes accessed | tf_op | source)
XLA Modules:
  0.0 78.9 jit_solution(3269607847931301254)
XLA Ops:
  0.0 1.2 %copy-done = bf16[512,1024]{1,0:T(8,128)(2,1)S(1)} copy-done((bf16[512,1024]{1,0:T(8,128)(2,1)S(1)}, bf16[512,1024]{1,0:T(8,128)(2,1)}, u32[]{:S(2)}) %copy-start) | copy-done | bytes 1048600
  1.2 0.7 copy-done.1
  1.9 0.7 copy-done.2
  2.6 1.7 %pack.1 = (bf16[272,256]{1,0:T(8,128)(2,1)S(1)}, bf16[272,256]{1,0:T(8,128)(2,1)S(1)}, bf16[272,256]{1,0:T(8,128)(2,1)S(1)}, bf16[272,256]{1,0:T(8,128)(2,1)S(1)...) custom-call(s32[512]{0:T(512)S(1)} %copy-done.1, ...), custom_call_target="tpu_custom_call" | custom-call | flops 1024 | bytes 1024 | tf_op jit(solution)/shard_map/pack/pallas_call | solution.py:68
  4.3 1.3 %collective-permute-start.4 = (bf16[272,256]{1,0:T(8,128)(2,1)S(1)}, bf16[272,256]{1,0:T(8,128)(2,1)S(1)}, u32[]{:S(2)}, u32[]{:S(2)}) collective-permute-start(bf16[272,256]{1,0:T(8,128)(2,1)S(1)} %get-tuple-element.61), channel_id=1, source_target_pairs={{0,12},{4,8},{8,4},{12,0},{1,13},{5,9},{9,5},{13,1},{2,14},{6,10},... | collective-permute-start | bytes 417800 | tf_op jit(solution)/shard_map/cells_3_chunk_0/ppermute | solution.py:312
  5.7 2.2 %collective-permute-start.2 = (bf16[272,256]{1,0:T(8,128)(2,1)S(1)}, bf16[272,256]{1,0:T(8,128)(2,1)S(1)}, u32[]{:S(2)}, u32[]{:S(2)}) collective-permute-start(bf16[272,256]{1,0:T(8,128)(2,1)S(1)} %get-tuple-element.58), channel_id=1, source_target_pairs={{0,4},{4,0},{8,12},{12,8},{1,5},{5,1},{9,13},{13,9},{2,6},{6,2},{1... | collective-permute-start | bytes 417800 | tf_op jit(solution)/shard_map/cells_1_chunk_0/ppermute | solution.py:312
  7.9 0.0 collective-permute-start
  7.9 4.2 %collective-permute-done.4.refs_3_.refs_7_ = bf16[272,256]{1,0:T(8,128)(2,1)S(1)} collective-permute-done((bf16[272,256]{1,0:T(8,128)(2,1)S(1)}, bf16[272,256]{1,0:T(8,128)(2,1)S(1)}, u32[]{:S(2)}, u32[]{:S(2)}) %collective-permute-start.4) | collective-permute-done | bytes 139296 | tf_op jit(solution)/shard_map/cells_3_chunk_0/ppermute | solution.py:312
  12.1 0.7 broadcast_in_dim.3.mean_ref
  12.8 0.0 collective-permute-start.5
  12.8 1.2 %collective-permute-done.2.refs_2_.refs_6_ = bf16[272,256]{1,0:T(8,128)(2,1)S(1)} collective-permute-done((bf16[272,256]{1,0:T(8,128)(2,1)S(1)}, bf16[272,256]{1,0:T(8,128)(2,1)S(1)}, u32[]{:S(2)}, u32[]{:S(2)}) %collective-permute-start.2) | collective-permute-done | bytes 139296 | tf_op jit(solution)/shard_map/cells_1_chunk_0/ppermute | solution.py:312
  14.0 1.5 %collective-permute-start.3 = (bf16[256,256]{1,0:T(8,128)(2,1)S(1)}, bf16[256,256]{1,0:T(8,128)(2,1)S(1)}, u32[]{:S(2)}, u32[]{:S(2)}) collective-permute-start(bf16[256,256]{1,0:T(8,128)(2,1)S(1)} %get-tuple-element.59), channel_id=1, source_target_pairs={{0,4},{4,0},{8,12},{12,8},{1,5},{5,1},{9,13},{13,9},{2,6},{6,2},{1... | collective-permute-start | bytes 393224 | tf_op jit(solution)/shard_map/cells_1_chunk_1/ppermute | solution.py:312
  15.5 0.4 collective-permute-done.refs_1_.refs_5_
  15.9 2.5 %collective-permute-start.1 = (bf16[256,256]{1,0:T(8,128)(2,1)S(1)}, bf16[256,256]{1,0:T(8,128)(2,1)S(1)}, u32[]{:S(2)}, u32[]{:S(2)}) collective-permute-start(bf16[256,256]{1,0:T(8,128)(2,1)S(1)} %get-tuple-element.56), channel_id=1, source_target_pairs={{0,8},{4,12},{8,0},{12,4},{1,9},{5,13},{9,1},{13,5},{2,10},{6,14},... | collective-permute-start | bytes 393224 | tf_op jit(solution)/shard_map/cells_2_chunk_1/ppermute | solution.py:312
  18.4 1.8 %standardize.4 = (bf16[1024,256]{1,0:T(8,128)(2,1)S(1)}, bf16[1024,1024]{1,0:T(8,128)(2,1)S(1)}, f32[8,128]{1,0:T(8,128)}, bf16[1024,1024]{1,0:T(8,128)(2,1)S(1)}) custom-call(f32[8,1024]{1,0:T(8,128)S(1)} %broadcast_in_dim.3.mean_ref, bf16[272,256]{1,0:T(8,128)(2,1)S(1)} %get-tuple-element.50.refs_0_.refs_4_, ...), custom_call_target="tpu_custom_call" | custom-call | flops 20000000000 | bytes 1024 | tf_op jit(solution)/shard_map/standardize/pallas_call | solution.py:173
  20.2 0.3 collective-permute-start.13
  20.5 4.6 %collective-permute-done.5.refs_3_ = bf16[256,256]{1,0:T(8,128)(2,1)S(1)} collective-permute-done((bf16[256,256]{1,0:T(8,128)(2,1)S(1)}, bf16[256,256]{1,0:T(8,128)(2,1)S(1)}, u32[]{:S(2)}, u32[]{:S(2)}) %collective-permute-start.5) | collective-permute-done | bytes 131104 | tf_op jit(solution)/shard_map/cells_3_chunk_1/ppermute | solution.py:312
  25.1 0.3 collective-permute-start.11
  25.4 4.4 %collective-permute-done.1.refs_1_ = bf16[256,256]{1,0:T(8,128)(2,1)S(1)} collective-permute-done((bf16[256,256]{1,0:T(8,128)(2,1)S(1)}, bf16[256,256]{1,0:T(8,128)(2,1)S(1)}, u32[]{:S(2)}, u32[]{:S(2)}) %collective-permute-start.1) | collective-permute-done | bytes 131104 | tf_op jit(solution)/shard_map/cells_2_chunk_1/ppermute | solution.py:312
  29.8 4.5 %collective-permute-start.7 = (bf16[256,256]{1,0:T(8,128)(2,1)S(1)}, bf16[256,256]{1,0:T(8,128)(2,1)S(1)}, u32[]{:S(2)}, u32[]{:S(2)}) collective-permute-start(bf16[256,256]{1,0:T(8,128)(2,1)S(1)} %get-tuple-element.69), channel_id=1, source_target_pairs={{0,8},{4,12},{8,0},{12,4},{1,9},{5,13},{9,1},{13,5},{2,10},{6,14},... | collective-permute-start | bytes 393224 | tf_op jit(solution)/shard_map/cells_2_chunk_2/ppermute | solution.py:312
  34.3 1.8 %standardize.5 = (bf16[1024,256]{1,0:T(8,128)(2,1)S(1)}, bf16[1024,1024]{1,0:T(8,128)(2,1)S(1)}, f32[8,128]{1,0:T(8,128)}, bf16[1024,1024]{1,0:T(8,128)(2,1)S(1)}) custom-call(f32[8,1024]{1,0:T(8,128)S(1)} %broadcast_in_dim.3.mean_ref, bf16[256,256]{1,0:T(8,128)(2,1)S(1)} %get-tuple-element.53.refs_0_, ...), custom_call_target="tpu_custom_call", output_to_operand_aliasing={{1}: (9, {}), {3}: (10, {})} | custom-call | flops 20000000000 | bytes 1024 | tf_op jit(solution)/shard_map/standardize/pallas_call | solution.py:173
  36.1 0.1 collective-permute-start.6
  36.2 0.0 collective-permute-done.11.refs_3_
  36.2 1.4 %collective-permute-start.12 = (bf16[256,256]{1,0:T(8,128)(2,1)S(1)}, bf16[256,256]{1,0:T(8,128)(2,1)S(1)}, u32[]{:S(2)}, u32[]{:S(2)}) collective-permute-start(bf16[256,256]{1,0:T(8,128)(2,1)S(1)} %get-tuple-element.78), channel_id=1, source_target_pairs={{0,12},{4,8},{8,4},{12,0},{1,13},{5,9},{9,5},{13,1},{2,14},{6,10},... | collective-permute-start | bytes 393224 | tf_op jit(solution)/shard_map/cells_3_chunk_3/ppermute | solution.py:312
  37.6 0.0 collective-permute-start.10
  37.6 3.5 %collective-permute-done.7.refs_1_ = bf16[256,256]{1,0:T(8,128)(2,1)S(1)} collective-permute-done((bf16[256,256]{1,0:T(8,128)(2,1)S(1)}, bf16[256,256]{1,0:T(8,128)(2,1)S(1)}, u32[]{:S(2)}, u32[]{:S(2)}) %collective-permute-start.7) | collective-permute-done | bytes 131104 | tf_op jit(solution)/shard_map/cells_2_chunk_2/ppermute | solution.py:312
  41.1 3.1 %collective-permute-start.8 = (bf16[256,256]{1,0:T(8,128)(2,1)S(1)}, bf16[256,256]{1,0:T(8,128)(2,1)S(1)}, u32[]{:S(2)}, u32[]{:S(2)}) collective-permute-start(bf16[256,256]{1,0:T(8,128)(2,1)S(1)} %get-tuple-element.70), channel_id=1, source_target_pairs={{0,8},{4,12},{8,0},{12,4},{1,9},{5,13},{9,1},{13,5},{2,10},{6,14},... | collective-permute-start | bytes 393224 | tf_op jit(solution)/shard_map/cells_2_chunk_3/ppermute | solution.py:312
  44.2 0.0 collective-permute-done.13.refs_8_
  44.2 1.8 %standardize.6 = (bf16[1024,256]{1,0:T(8,128)(2,1)S(1)}, bf16[1024,1024]{1,0:T(8,128)(2,1)S(1)}, f32[8,128]{1,0:T(8,128)}, bf16[1024,1024]{1,0:T(8,128)(2,1)S(1)}) custom-call(f32[8,1024]{1,0:T(8,128)S(1)} %broadcast_in_dim.3.mean_ref, bf16[256,256]{1,0:T(8,128)(2,1)S(1)} %get-tuple-element.81.refs_0_, ...), custom_call_target="tpu_custom_call", output_to_operand_aliasing={{1}: (9, {}), {3}: (10, {})} | custom-call | flops 20000000000 | bytes 1024 | tf_op jit(solution)/shard_map/standardize/pallas_call | solution.py:173
  46.0 0.1 collective-permute-start.17
  46.1 0.0 collective-permute-done.6.refs_9_
  46.1 1.1 %collective-permute-done.12.refs_3_ = bf16[256,256]{1,0:T(8,128)(2,1)S(1)} collective-permute-done((bf16[256,256]{1,0:T(8,128)(2,1)S(1)}, bf16[256,256]{1,0:T(8,128)(2,1)S(1)}, u32[]{:S(2)}, u32[]{:S(2)}) %collective-permute-start.12) | collective-permute-done | bytes 131104 | tf_op jit(solution)/shard_map/cells_3_chunk_3/ppermute | solution.py:312
  47.2 0.0 collective-permute-done.10.refs_2_
  47.2 3.2 %collective-permute-done.8.refs_1_ = bf16[256,256]{1,0:T(8,128)(2,1)S(1)} collective-permute-done((bf16[256,256]{1,0:T(8,128)(2,1)S(1)}, bf16[256,256]{1,0:T(8,128)(2,1)S(1)}, u32[]{:S(2)}, u32[]{:S(2)}) %collective-permute-start.8) | collective-permute-done | bytes 131104 | tf_op jit(solution)/shard_map/cells_2_chunk_3/ppermute | solution.py:312
  50.4 1.3 %standardize.7 = (bf16[1024,256]{1,0:T(8,128)(2,1)S(1)}, bf16[1024,1024]{1,0:T(8,128)(2,1)S(1)}, f32[8,128]{1,0:T(8,128)S(1)}, bf16[1024,1024]{1,0:T(8,128)(2,1)S(1)}, bf16[1024,512]{1,0:T(8,128)(2,1)S(1)}) custom-call(f32[8,1024]{1,0:T(8,128)S(1)} %broadcast_in_dim.3.mean_ref, ...), custom_call_target="tpu_custom_call", output_to_operand_aliasing={{1}: (11, {}), {3}: (12, {})} | custom-call | flops 20000000000 | bytes 1024 | tf_op jit(solution)/shard_map/standardize/pallas_call | solution.py:173
  51.8 2.2 %collective-permute-start.15 = (bf16[1024,1024]{1,0:T(8,128)(2,1)S(1)}, bf16[1024,1024]{1,0:T(8,128)(2,1)S(1)}, u32[]{:S(2)}, u32[]{:S(2)}) collective-permute-start(bf16[1024,1024]{1,0:T(8,128)(2,1)S(1)} %get-tuple-element.89.refs_0_), channel_id=1, source_target_pairs={{0,1},{1,0},{2,3},{3,2},{4,5},{5,4},{6,7},{7,6},{8,9},{9,8},{10,11... | collective-permute-start | bytes 6291464 | tf_op jit(solution)/shard_map/near/ppermute | solution.py:319
  54.0 2.1 %gram.5.refs_3_ = bf16[1,1024,4096]{2,1,0:T(8,128)(2,1)} custom-call(f32[8,128]{1,0:T(8,128)S(1)} %get-tuple-element.86.count_ref, bf16[1024,1024]{1,0:T(8,128)(2,1)S(1)} %get-tuple-element.87.left_ref, bf16[1024,1024]{1,0:T(8,128)(2,1)S(1)} %get-tuple-element.89.refs_0_), custom_call_target="tpu_custom_call" | custom-call | flops 1024 | bytes 1024 | tf_op jit(solution)/shard_map/gram/pallas_call | solution.py:274
  56.1 0.1 collective-permute-start.16
  56.2 0.7 collective-permute-start.14
  56.8 7.2 %collective-permute-start.18 = (bf16[1024,256]{1,0:T(8,128)(2,1)S(1)}, bf16[1024,256]{1,0:T(8,128)(2,1)S(1)}, u32[]{:S(2)}, u32[]{:S(2)}) collective-permute-start(bf16[1024,256]{1,0:T(8,128)(2,1)S(1)} %collective-permute-done.17.refs_2_), channel_id=1, source_target_pairs={{0,1},{1,0},{2,3},{3,2},{4,5},{5,4},{6,7},{7,6},{8,9},{9,8},{10,11... | collective-permute-start | bytes 1572872 | tf_op jit(solution)/shard_map/far_near_2/ppermute | solution.py:319
  64.1 5.0 %gram.6.refs_3_ = bf16[1,1024,4096]{2,1,0:T(8,128)(2,1)} custom-call(f32[8,128]{1,0:T(8,128)S(1)} %get-tuple-element.86.count_ref, bf16[1024,1024]{1,0:T(8,128)(2,1)S(1)} %get-tuple-element.87.left_ref, bf16[1024,1024]{1,0:T(8,128)(2,1)S(1)} %get-tuple-element.89.refs_0_, ...), custom_call_target="tpu_custom_call", output_to_operand_aliasing={{}: (5, {})} | custom-call | flops 20000000000 | bytes 1024 | tf_op jit(solution)/shard_map/gram/pallas_call | solution.py:274
  69.1 0.0 collective-permute-done.16.refs_1_
  69.1 0.0 collective-permute-done.15.refs_0_
  69.1 6.1 %gram.7.refs_1_ = bf16[1,1024,4096]{2,1,0:T(8,128)(2,1)} custom-call(f32[8,128]{1,0:T(8,128)S(1)} %get-tuple-element.86.count_ref, bf16[1024,1024]{1,0:T(8,128)(2,1)S(1)} %get-tuple-element.87.left_ref, bf16[1024,1024]{1,0:T(8,128)(2,1)S(1)} %collective-permute-done.15.refs_0_, ...), custom_call_target="tpu_custom_call", output_to_operand_aliasing={{}: (5, {})} | custom-call | flops 1024 | bytes 1024 | tf_op jit(solution)/shard_map/gram/pallas_call | solution.py:274
  75.2 0.1 collective-permute-start.19
  75.3 1.5 %gram.8.refs_1_ = bf16[1,1024,4096]{2,1,0:T(8,128)(2,1)} custom-call(f32[8,128]{1,0:T(8,128)S(1)} %get-tuple-element.86.count_ref, bf16[1024,1024]{1,0:T(8,128)(2,1)S(1)} %get-tuple-element.87.left_ref, bf16[1024,256]{1,0:T(8,128)(2,1)S(1)} %collective-permute-done.14.refs_0_, bf16[1,1024,4096]{2,1,0:T(8,128)(2,1)} %gram.7.refs_1_), custom_call_target="tpu_custom_call", output_to_operand_aliasing={{}: (3, {})} | custom-call | flops 1024 | bytes 1024 | tf_op jit(solution)/shard_map/gram/pallas_call | solution.py:274
  76.9 0.3 collective-permute-done.19.refs_0_
  77.2 1.5 %gram.9 = bf16[1,1024,4096]{2,1,0:T(8,128)(2,1)} custom-call(f32[8,128]{1,0:T(8,128)S(1)} %get-tuple-element.86.count_ref, bf16[1024,1024]{1,0:T(8,128)(2,1)S(1)} %get-tuple-element.87.left_ref, bf16[1024,256]{1,0:T(8,128)(2,1)S(1)} %collective-permute-done.19.refs_0_, bf16[1,1024,4096]{2,1,0:T(8,128)(2,1)} %gram.8.refs_1_), custom_call_target="tpu_custom_call", output_to_operand_aliasing={{}: (3, {})} | custom-call | flops 1024 | bytes 1024 | tf_op jit(solution)/shard_map/gram/pallas_call | solution.py:274
  (9 shorter events, 0.0 us)
Async XLA Ops:
  0.0 1.2 %copy-start = (bf16[512,1024]{1,0:T(8,128)(2,1)S(1)}, bf16[512,1024]{1,0:T(8,128)(2,1)}, u32[]{:S(2)}) copy-start(bf16[512,1024]{1,0:T(8,128)(2,1)} %expr_ref.1) | copy-start | bytes 3145732
  1.2 0.7 copy-start.1
  1.9 0.7 copy-start.2
  4.3 7.8 %collective-permute-start.4 = (bf16[272,256]{1,0:T(8,128)(2,1)S(1)}, bf16[272,256]{1,0:T(8,128)(2,1)S(1)}, u32[]{:S(2)}, u32[]{:S(2)}) collective-permute-start(bf16[272,256]{1,0:T(8,128)(2,1)S(1)} %get-tuple-element.61), channel_id=1, source_target_pairs={{0,12},{4,8},{8,4},{12,0},{1,13},{5,9},{9,5},{13,1},{2,14},{6,10},... | collective-permute-start | bytes 417800 | tf_op jit(solution)/shard_map/cells_3_chunk_0/ppermute | solution.py:312
  5.7 8.3 %collective-permute-start.2 = (bf16[272,256]{1,0:T(8,128)(2,1)S(1)}, bf16[272,256]{1,0:T(8,128)(2,1)S(1)}, u32[]{:S(2)}, u32[]{:S(2)}) collective-permute-start(bf16[272,256]{1,0:T(8,128)(2,1)S(1)} %get-tuple-element.58), channel_id=1, source_target_pairs={{0,4},{4,0},{8,12},{12,8},{1,5},{5,1},{9,13},{13,9},{2,6},{6,2},{1... | collective-permute-start | bytes 417800 | tf_op jit(solution)/shard_map/cells_1_chunk_0/ppermute | solution.py:312
  7.9 8.0 %collective-permute-start = (bf16[272,256]{1,0:T(8,128)(2,1)S(1)}, bf16[272,256]{1,0:T(8,128)(2,1)S(1)}, u32[]{:S(2)}, u32[]{:S(2)}) collective-permute-start(bf16[272,256]{1,0:T(8,128)(2,1)S(1)} %get-tuple-element.55), channel_id=1, source_target_pairs={{0,8},{4,12},{8,0},{12,4},{1,9},{5,13},{9,1},{13,5},{2,10},{6,14},... | collective-permute-start | bytes 417800 | tf_op jit(solution)/shard_map/cells_2_chunk_0/ppermute | solution.py:312
  12.8 12.3 %collective-permute-start.5 = (bf16[256,256]{1,0:T(8,128)(2,1)S(1)}, bf16[256,256]{1,0:T(8,128)(2,1)S(1)}, u32[]{:S(2)}, u32[]{:S(2)}) collective-permute-start(bf16[256,256]{1,0:T(8,128)(2,1)S(1)} %get-tuple-element.62), channel_id=1, source_target_pairs={{0,12},{4,8},{8,4},{12,0},{1,13},{5,9},{9,5},{13,1},{2,14},{6,10},... | collective-permute-start | bytes 393224 | tf_op jit(solution)/shard_map/cells_3_chunk_1/ppermute | solution.py:312
  14.0 11.4 %collective-permute-start.3 = (bf16[256,256]{1,0:T(8,128)(2,1)S(1)}, bf16[256,256]{1,0:T(8,128)(2,1)S(1)}, u32[]{:S(2)}, u32[]{:S(2)}) collective-permute-start(bf16[256,256]{1,0:T(8,128)(2,1)S(1)} %get-tuple-element.59), channel_id=1, source_target_pairs={{0,4},{4,0},{8,12},{12,8},{1,5},{5,1},{9,13},{13,9},{2,6},{6,2},{1... | collective-permute-start | bytes 393224 | tf_op jit(solution)/shard_map/cells_1_chunk_1/ppermute | solution.py:312
  15.9 13.9 %collective-permute-start.1 = (bf16[256,256]{1,0:T(8,128)(2,1)S(1)}, bf16[256,256]{1,0:T(8,128)(2,1)S(1)}, u32[]{:S(2)}, u32[]{:S(2)}) collective-permute-start(bf16[256,256]{1,0:T(8,128)(2,1)S(1)} %get-tuple-element.56), channel_id=1, source_target_pairs={{0,8},{4,12},{8,0},{12,4},{1,9},{5,13},{9,1},{13,5},{2,10},{6,14},... | collective-permute-start | bytes 393224 | tf_op jit(solution)/shard_map/cells_2_chunk_1/ppermute | solution.py:312
  20.2 24.0 %collective-permute-start.13 = (bf16[1024,256]{1,0:T(8,128)(2,1)S(1)}, bf16[1024,256]{1,0:T(8,128)(2,1)S(1)}, u32[]{:S(2)}, u32[]{:S(2)}) collective-permute-start(bf16[1024,256]{1,0:T(8,128)(2,1)S(1)} %get-tuple-element.79), channel_id=1, source_target_pairs={{0,2},{1,3},{2,0},{3,1},{4,6},{5,7},{6,4},{7,5},{8,10},{9,11},{10,... | collective-permute-start | bytes 1572872 | tf_op jit(solution)/shard_map/far_0/ppermute | solution.py:315
  25.1 11.0 %collective-permute-start.11 = (bf16[256,256]{1,0:T(8,128)(2,1)S(1)}, bf16[256,256]{1,0:T(8,128)(2,1)S(1)}, u32[]{:S(2)}, u32[]{:S(2)}) collective-permute-start(bf16[256,256]{1,0:T(8,128)(2,1)S(1)} %get-tuple-element.77), channel_id=1, source_target_pairs={{0,12},{4,8},{8,4},{12,0},{1,13},{5,9},{9,5},{13,1},{2,14},{6,10},... | collective-permute-start | bytes 393224 | tf_op jit(solution)/shard_map/cells_3_chunk_2/ppermute | solution.py:312
  25.4 12.2 %collective-permute-start.9 = (bf16[256,256]{1,0:T(8,128)(2,1)S(1)}, bf16[256,256]{1,0:T(8,128)(2,1)S(1)}, u32[]{:S(2)}, u32[]{:S(2)}) collective-permute-start(bf16[256,256]{1,0:T(8,128)(2,1)S(1)} %get-tuple-element.73), channel_id=1, source_target_pairs={{0,4},{4,0},{8,12},{12,8},{1,5},{5,1},{9,13},{13,9},{2,6},{6,2},{1... | collective-permute-start | bytes 393224 | tf_op jit(solution)/shard_map/cells_1_chunk_2/ppermute | solution.py:312
  29.8 11.3 %collective-permute-start.7 = (bf16[256,256]{1,0:T(8,128)(2,1)S(1)}, bf16[256,256]{1,0:T(8,128)(2,1)S(1)}, u32[]{:S(2)}, u32[]{:S(2)}) collective-permute-start(bf16[256,256]{1,0:T(8,128)(2,1)S(1)} %get-tuple-element.69), channel_id=1, source_target_pairs={{0,8},{4,12},{8,0},{12,4},{1,9},{5,13},{9,1},{13,5},{2,10},{6,14},... | collective-permute-start | bytes 393224 | tf_op jit(solution)/shard_map/cells_2_chunk_2/ppermute | solution.py:312
  36.1 10.0 %collective-permute-start.6 = (bf16[1024,256]{1,0:T(8,128)(2,1)S(1)}, bf16[1024,256]{1,0:T(8,128)(2,1)S(1)}, u32[]{:S(2)}, u32[]{:S(2)}) collective-permute-start(bf16[1024,256]{1,0:T(8,128)(2,1)S(1)} %get-tuple-element.65), channel_id=1, source_target_pairs={{0,2},{1,3},{2,0},{3,1},{4,6},{5,7},{6,4},{7,5},{8,10},{9,11},{10,... | collective-permute-start | bytes 1572872 | tf_op jit(solution)/shard_map/far_1/ppermute | solution.py:315
  36.2 11.1 %collective-permute-start.12 = (bf16[256,256]{1,0:T(8,128)(2,1)S(1)}, bf16[256,256]{1,0:T(8,128)(2,1)S(1)}, u32[]{:S(2)}, u32[]{:S(2)}) collective-permute-start(bf16[256,256]{1,0:T(8,128)(2,1)S(1)} %get-tuple-element.78), channel_id=1, source_target_pairs={{0,12},{4,8},{8,4},{12,0},{1,13},{5,9},{9,5},{13,1},{2,14},{6,10},... | collective-permute-start | bytes 393224 | tf_op jit(solution)/shard_map/cells_3_chunk_3/ppermute | solution.py:312
  37.6 9.6 %collective-permute-start.10 = (bf16[256,256]{1,0:T(8,128)(2,1)S(1)}, bf16[256,256]{1,0:T(8,128)(2,1)S(1)}, u32[]{:S(2)}, u32[]{:S(2)}) collective-permute-start(bf16[256,256]{1,0:T(8,128)(2,1)S(1)} %get-tuple-element.74), channel_id=1, source_target_pairs={{0,4},{4,0},{8,12},{12,8},{1,5},{5,1},{9,13},{13,9},{2,6},{6,2},{1... | collective-permute-start | bytes 393224 | tf_op jit(solution)/shard_map/cells_1_chunk_3/ppermute | solution.py:312
  41.1 9.4 %collective-permute-start.8 = (bf16[256,256]{1,0:T(8,128)(2,1)S(1)}, bf16[256,256]{1,0:T(8,128)(2,1)S(1)}, u32[]{:S(2)}, u32[]{:S(2)}) collective-permute-start(bf16[256,256]{1,0:T(8,128)(2,1)S(1)} %get-tuple-element.70), channel_id=1, source_target_pairs={{0,8},{4,12},{8,0},{12,4},{1,9},{5,13},{9,1},{13,5},{2,10},{6,14},... | collective-permute-start | bytes 393224 | tf_op jit(solution)/shard_map/cells_2_chunk_3/ppermute | solution.py:312
  46.0 10.9 %collective-permute-start.17 = (bf16[1024,256]{1,0:T(8,128)(2,1)S(1)}, bf16[1024,256]{1,0:T(8,128)(2,1)S(1)}, u32[]{:S(2)}, u32[]{:S(2)}) collective-permute-start(bf16[1024,256]{1,0:T(8,128)(2,1)S(1)} %get-tuple-element.92), channel_id=1, source_target_pairs={{0,2},{1,3},{2,0},{3,1},{4,6},{5,7},{6,4},{7,5},{8,10},{9,11},{10,... | collective-permute-start | bytes 1572872 | tf_op jit(solution)/shard_map/far_2/ppermute | solution.py:315
  51.8 17.4 %collective-permute-start.15 = (bf16[1024,1024]{1,0:T(8,128)(2,1)S(1)}, bf16[1024,1024]{1,0:T(8,128)(2,1)S(1)}, u32[]{:S(2)}, u32[]{:S(2)}) collective-permute-start(bf16[1024,1024]{1,0:T(8,128)(2,1)S(1)} %get-tuple-element.89.refs_0_), channel_id=1, source_target_pairs={{0,1},{1,0},{2,3},{3,2},{4,5},{5,4},{6,7},{7,6},{8,9},{9,8},{10,11... | collective-permute-start | bytes 6291464 | tf_op jit(solution)/shard_map/near/ppermute | solution.py:319
  56.1 13.0 %collective-permute-start.16 = (bf16[1024,512]{1,0:T(8,128)(2,1)S(1)}, bf16[1024,512]{1,0:T(8,128)(2,1)S(1)}, u32[]{:S(2)}, u32[]{:S(2)}) collective-permute-start(bf16[1024,512]{1,0:T(8,128)(2,1)S(1)} %get-tuple-element.91.refs_1_), channel_id=1, source_target_pairs={{0,1},{1,0},{2,3},{3,2},{4,5},{5,4},{6,7},{7,6},{8,9},{9,8},{10,11... | collective-permute-start | bytes 3145736 | tf_op jit(solution)/shard_map/far_near/ppermute | solution.py:319
  56.2 19.1 %collective-permute-start.14 = (bf16[1024,256]{1,0:T(8,128)(2,1)S(1)}, bf16[1024,256]{1,0:T(8,128)(2,1)S(1)}, u32[]{:S(2)}, u32[]{:S(2)}) collective-permute-start(bf16[1024,256]{1,0:T(8,128)(2,1)S(1)} %get-tuple-element.90), channel_id=1, source_target_pairs={{0,2},{1,3},{2,0},{3,1},{4,6},{5,7},{6,4},{7,5},{8,10},{9,11},{10,... | collective-permute-start | bytes 1572872 | tf_op jit(solution)/shard_map/ppermute | solution.py:315
  56.8 12.3 %collective-permute-start.18 = (bf16[1024,256]{1,0:T(8,128)(2,1)S(1)}, bf16[1024,256]{1,0:T(8,128)(2,1)S(1)}, u32[]{:S(2)}, u32[]{:S(2)}) collective-permute-start(bf16[1024,256]{1,0:T(8,128)(2,1)S(1)} %collective-permute-done.17.refs_2_), channel_id=1, source_target_pairs={{0,1},{1,0},{2,3},{3,2},{4,5},{5,4},{6,7},{7,6},{8,9},{9,8},{10,11... | collective-permute-start | bytes 1572872 | tf_op jit(solution)/shard_map/far_near_2/ppermute | solution.py:319
  75.2 2.0 %collective-permute-start.19 = (bf16[1024,256]{1,0:T(8,128)(2,1)S(1)}, bf16[1024,256]{1,0:T(8,128)(2,1)S(1)}, u32[]{:S(2)}, u32[]{:S(2)}) collective-permute-start(bf16[1024,256]{1,0:T(8,128)(2,1)S(1)} %collective-permute-done.14.refs_0_), channel_id=1, source_target_pairs={{0,1},{1,0},{2,3},{3,2},{4,5},{5,4},{6,7},{7,6},{8,9},{9,8},{10,11... | collective-permute-start | bytes 1572872 | tf_op jit(solution)/shard_map/far_near_3/ppermute | solution.py:319

commit v17 on v16

--- a/solution.py
+++ b/solution.py
@@ -229,10 +229,12 @@
             pltpu.make_async_copy(source, spot, join_sems.at[sent]).wait()
             sent += 1
         width = part[0] if part else sum(sources[index].shape[1] for index in panels)
+        low, high = part[1:] if part[1:] else (0, rows)
         owner = lax.rem(me + (blocks - chip * cores), blocks)
         owner = jnp.bitwise_xor(owner, flip)
         column = pl.multiple_of(owner * rows + first, 128)
-        for row in range(0, rows, strip):
+        for row in range(low, high, strip):
+            size = min(strip, high - row)
             slot = len(stores) % 2
             if len(stores) >= 2:
                 stores[-2].wait()
@@ -242,13 +244,13 @@
                 skip = first if part else 0
                 right = sources[panels[0]][:, skip : skip + width]
             product = jnp.dot(
-                left_ref[row : row + strip, :], right, preferred_element_type=jnp.float32
+                left_ref[row : row + size, :], right, preferred_element_type=jnp.float32
             )
-            tile[slot, :, 0:width] = (product * inverse).astype(jnp.bfloat16)
+            tile[slot, 0:size, 0:width] = (product * inverse).astype(jnp.bfloat16)
             stores.append(
                 pltpu.make_async_copy(
-                    tile.at[slot, :, pl.ds(0, width)],
-                    out_ref.at[0, pl.ds(row, strip), pl.ds(column, width)],
+                    tile.at[slot, pl.ds(0, size), pl.ds(0, width)],
+                    out_ref.at[0, pl.ds(row, size), pl.ds(column, width)],
                     sems.at[slot],
                 )
             )
@@ -321,7 +323,7 @@
     mean = jnp.broadcast_to(after(gene_mean, packed[0][0]), (8, panel))
 
     order = sorted(range(1, types), key=lambda j: (j == 3, j == 1, j))
-    left, own, far, before = None, None, [], None
+    left, own, out, far, before = None, None, None, [], None
     for k in range(chunks):
         arrived = [packed[k][0]]
         for j in order:
@@ -337,6 +339,9 @@
             first = arrived
         gather = []
         if k == chunks - 1 and k > 1:
+            groups = [([own], (0, 0, 0, starts[k], 0, starts[k]))]
+            out = gram(blocks, cores, count, left, groups, None, brief)
+            arrived[0] = after(arrived[0], out)
             gather = [[got[d] for got in far[: k - 1]] for d in range(chips - 1)]
         scaled, left, count, own, *joined = standardize(
             types, cap, mean, starts[k], arrived, first, left, own, gather
@@ -350,12 +355,18 @@
     near = side("near", own)
     joined_near = [[side("far_near", p)] for p in joined] or [[]] * (chips - 1)
     joined = [[p] for p in joined] or [[]] * (chips - 1)
-    half = panel // 2
-    out = multiply([([own], (0, 0, 0, half))], None, brief)
+    if out is None:
+        out = multiply([([own], (0, 0, 0))], None, brief)
+    else:
+        edge = starts[last]
+        groups = [
+            ([own], (0, 0, 0, panel, edge, panel)),
+            ([own], (0, 0, edge, panel - edge, 0, edge)),
+        ]
+        out = multiply(groups, out, brief)
     final = [across(after(scaled, out), d) for d in range(1, chips)]
     second = [side(f"far_near_{last - 1}", p, own) for p in far[last - 1]]
-    groups = [([own], (0, 0, half, half))]
-    groups += [([*p, far[last - 1][i]], (i + 1, 0, 0)) for i, p in enumerate(joined)]
+    groups = [([*p, far[last - 1][i]], (i + 1, 0, 0)) for i, p in enumerate(joined)]
     out = multiply(groups, out, lengthy)
     groups = [([near], (0, 1, 0))]
     groups += [([*p, second[i]], (i + 1, 1, 0)) for i, p in enumerate(joined_near)]

time: 79.1 us -> 77.4 us (0.979)
  the two profiles are of different devices: /device:TPU:11 before, /device:TPU:0 now
where the time goes in v17:
time: 77.4 us; the launch traced here: 77.2 us
  starting transfers between devices  25.5 us (33%)
  Pallas kernels  24.7 us (32%)
  waiting for transfers between devices  23.5 us (30%)
  local copies, waits for them, and re-layouts  3.27 us (4%)
    ppermute x12, waiting for transfers between devices, swap(): return lax.ppermute(block, 'cells', [(s, s ^ by) for s in range(types)])  19.5 us
    ppermute x12, starting transfers between devices, swap(): return lax.ppermute(block, 'cells', [(s, s ^ by) for s in range(types)])  19 us
    pallas_call x6, Pallas kernels, gram(): pl.pallas_call(functools.partial(gram_kernel, blocks, cores, strip, layou...  16.8 us
    pallas_call x4, Pallas kernels, standardize(): pl.pallas_call(functools.partial(standardize_kernel, types, cap, lead, se...  6.12 us
    ppermute x4, starting transfers between devices, across(): lax.ppermute(panel_, 'blk', [(b, (b + by * cores) % blocks) for b in rang...  5.78 us
    ppermute x4, waiting for transfers between devices, across(): lax.ppermute(panel_, 'blk', [(b, (b + by * cores) % blocks) for b in rang...  3.57 us
    unnamed x6, local copies, waits for them, and re-layouts  2.58 us
    pallas_call x1, Pallas kernels, pack(): pl.pallas_call(functools.partial(pack_kernel, types, cap, widths), out_sh...  1.71 us
  transfers between devices with their start and end apart: 20, of which 8 were waited for; matrix products, arithmetic and copies ran while one was open for 1% of the time, Pallas kernels for 28%

profile of v17, /device:TPU:0, one launch (start us, length us, event | category | flops | bytes accessed | tf_op | source)
XLA Modules:
  0.0 77.2 jit_solution(1089170298242731380)
XLA Ops:
  0.0 1.2 %copy-done = bf16[512,1024]{1,0:T(8,128)(2,1)S(1)} copy-done((bf16[512,1024]{1,0:T(8,128)(2,1)S(1)}, bf16[512,1024]{1,0:T(8,128)(2,1)}, u32[]{:S(2)}) %copy-start) | copy-done | bytes 1048600
  1.2 0.7 copy-done.1
  1.9 0.7 copy-done.2
  2.6 1.7 %pack.1 = (bf16[272,256]{1,0:T(8,128)(2,1)S(1)}, bf16[272,256]{1,0:T(8,128)(2,1)S(1)}, bf16[272,256]{1,0:T(8,128)(2,1)S(1)}, bf16[272,256]{1,0:T(8,128)(2,1)S(1)...) custom-call(s32[512]{0:T(512)S(1)} %copy-done.1, ...), custom_call_target="tpu_custom_call" | custom-call | flops 1024 | bytes 1024 | tf_op jit(solution)/shard_map/pack/pallas_call | solution.py:68
  4.3 5.1 %collective-permute-start.4 = (bf16[272,256]{1,0:T(8,128)(2,1)S(1)}, bf16[272,256]{1,0:T(8,128)(2,1)S(1)}, u32[]{:S(2)}, u32[]{:S(2)}) collective-permute-start(bf16[272,256]{1,0:T(8,128)(2,1)S(1)} %get-tuple-element.63), channel_id=1, source_target_pairs={{0,12},{4,8},{8,4},{12,0},{1,13},{5,9},{9,5},{13,1},{2,14},{6,10},... | collective-permute-start | bytes 417800 | tf_op jit(solution)/shard_map/cells_3_chunk_0/ppermute | solution.py:314
  9.4 0.6 collective-permute-start
  10.1 3.9 %collective-permute-done.4.refs_3_.refs_7_ = bf16[272,256]{1,0:T(8,128)(2,1)S(1)} collective-permute-done((bf16[272,256]{1,0:T(8,128)(2,1)S(1)}, bf16[272,256]{1,0:T(8,128)(2,1)S(1)}, u32[]{:S(2)}, u32[]{:S(2)}) %collective-permute-start.4) | collective-permute-done | bytes 139296 | tf_op jit(solution)/shard_map/cells_3_chunk_0/ppermute | solution.py:314
  14.0 0.7 broadcast_in_dim.3.mean_ref
  14.7 3.8 %collective-permute-start.5 = (bf16[256,256]{1,0:T(8,128)(2,1)S(1)}, bf16[256,256]{1,0:T(8,128)(2,1)S(1)}, u32[]{:S(2)}, u32[]{:S(2)}) collective-permute-start(bf16[256,256]{1,0:T(8,128)(2,1)S(1)} %get-tuple-element.64), channel_id=1, source_target_pairs={{0,12},{4,8},{8,4},{12,0},{1,13},{5,9},{9,5},{13,1},{2,14},{6,10},... | collective-permute-start | bytes 393224 | tf_op jit(solution)/shard_map/cells_3_chunk_1/ppermute | solution.py:314
  18.5 0.0 collective-permute-done.2.refs_2_.refs_6_
  18.5 0.7 collective-permute-start.3
  19.1 7.3 %collective-permute-done.refs_1_.refs_5_ = bf16[272,256]{1,0:T(8,128)(2,1)S(1)} collective-permute-done((bf16[272,256]{1,0:T(8,128)(2,1)S(1)}, bf16[272,256]{1,0:T(8,128)(2,1)S(1)}, u32[]{:S(2)}, u32[]{:S(2)}) %collective-permute-start) | collective-permute-done | bytes 139296 | tf_op jit(solution)/shard_map/cells_2_chunk_0/ppermute | solution.py:314
  26.4 0.0 collective-permute-start.1
  26.4 1.8 %standardize.4 = (bf16[1024,256]{1,0:T(8,128)(2,1)S(1)}, bf16[1024,1024]{1,0:T(8,128)(2,1)S(1)}, f32[8,128]{1,0:T(8,128)}, bf16[1024,1024]{1,0:T(8,128)(2,1)S(1)}) custom-call(f32[8,1024]{1,0:T(8,128)S(1)} %broadcast_in_dim.3.mean_ref, bf16[272,256]{1,0:T(8,128)(2,1)S(1)} %get-tuple-element.52.refs_0_.refs_4_, ...), custom_call_target="tpu_custom_call" | custom-call | flops 20000000000 | bytes 1024 | tf_op jit(solution)/shard_map/standardize/pallas_call | solution.py:173
  28.2 1.6 %collective-permute-start.7 = (bf16[1024,256]{1,0:T(8,128)(2,1)S(1)}, bf16[1024,256]{1,0:T(8,128)(2,1)S(1)}, u32[]{:S(2)}, u32[]{:S(2)}) collective-permute-start(bf16[1024,256]{1,0:T(8,128)(2,1)S(1)} %get-tuple-element.70), channel_id=1, source_target_pairs={{0,2},{1,3},{2,0},{3,1},{4,6},{5,7},{6,4},{7,5},{8,10},{9,11},{10,... | collective-permute-start | bytes 1572872 | tf_op jit(solution)/shard_map/far_0/ppermute | solution.py:317
  29.8 0.0 collective-permute-done.5.refs_3_
  29.8 1.0 %collective-permute-start.10 = (bf16[256,256]{1,0:T(8,128)(2,1)S(1)}, bf16[256,256]{1,0:T(8,128)(2,1)S(1)}, u32[]{:S(2)}, u32[]{:S(2)}) collective-permute-start(bf16[256,256]{1,0:T(8,128)(2,1)S(1)} %get-tuple-element.77), channel_id=1, source_target_pairs={{0,12},{4,8},{8,4},{12,0},{1,13},{5,9},{9,5},{13,1},{2,14},{6,10},... | collective-permute-start | bytes 393224 | tf_op jit(solution)/shard_map/cells_3_chunk_2/ppermute | solution.py:314
  30.8 0.0 collective-permute-done.3.refs_2_
  30.8 3.3 %collective-permute-start.9 = (bf16[256,256]{1,0:T(8,128)(2,1)S(1)}, bf16[256,256]{1,0:T(8,128)(2,1)S(1)}, u32[]{:S(2)}, u32[]{:S(2)}) collective-permute-start(bf16[256,256]{1,0:T(8,128)(2,1)S(1)} %get-tuple-element.75), channel_id=1, source_target_pairs={{0,4},{4,0},{8,12},{12,8},{1,5},{5,1},{9,13},{13,9},{2,6},{6,2},{1... | collective-permute-start | bytes 393224 | tf_op jit(solution)/shard_map/cells_1_chunk_2/ppermute | solution.py:314
  34.1 0.9 %collective-permute-done.1.refs_1_ = bf16[256,256]{1,0:T(8,128)(2,1)S(1)} collective-permute-done((bf16[256,256]{1,0:T(8,128)(2,1)S(1)}, bf16[256,256]{1,0:T(8,128)(2,1)S(1)}, u32[]{:S(2)}, u32[]{:S(2)}) %collective-permute-start.1) | collective-permute-done | bytes 131104 | tf_op jit(solution)/shard_map/cells_2_chunk_1/ppermute | solution.py:314
  35.0 0.0 collective-permute-start.8
  35.0 1.8 %standardize.5 = (bf16[1024,256]{1,0:T(8,128)(2,1)S(1)}, bf16[1024,1024]{1,0:T(8,128)(2,1)S(1)}, f32[8,128]{1,0:T(8,128)}, bf16[1024,1024]{1,0:T(8,128)(2,1)S(1)}) custom-call(f32[8,1024]{1,0:T(8,128)S(1)} %broadcast_in_dim.3.mean_ref, bf16[256,256]{1,0:T(8,128)(2,1)S(1)} %get-tuple-element.55.refs_0_, ...), custom_call_target="tpu_custom_call", output_to_operand_aliasing={{1}: (9, {}), {3}: (10, {})} | custom-call | flops 20000000000 | bytes 1024 | tf_op jit(solution)/shard_map/standardize/pallas_call | solution.py:173
  36.8 2.8 %collective-permute-start.6 = (bf16[1024,256]{1,0:T(8,128)(2,1)S(1)}, bf16[1024,256]{1,0:T(8,128)(2,1)S(1)}, u32[]{:S(2)}, u32[]{:S(2)}) collective-permute-start(bf16[1024,256]{1,0:T(8,128)(2,1)S(1)} %get-tuple-element.67), channel_id=1, source_target_pairs={{0,2},{1,3},{2,0},{3,1},{4,6},{5,7},{6,4},{7,5},{8,10},{9,11},{10,... | collective-permute-start | bytes 1572872 | tf_op jit(solution)/shard_map/far_1/ppermute | solution.py:317
  39.6 0.0 collective-permute-done.10.refs_3_
  39.6 3.8 %collective-permute-start.13 = (bf16[256,256]{1,0:T(8,128)(2,1)S(1)}, bf16[256,256]{1,0:T(8,128)(2,1)S(1)}, u32[]{:S(2)}, u32[]{:S(2)}) collective-permute-start(bf16[256,256]{1,0:T(8,128)(2,1)S(1)} %get-tuple-element.89), channel_id=1, source_target_pairs={{0,12},{4,8},{8,4},{12,0},{1,13},{5,9},{9,5},{13,1},{2,14},{6,10},... | collective-permute-start | bytes 393224 | tf_op jit(solution)/shard_map/cells_3_chunk_3/ppermute | solution.py:314
  43.4 0.6 collective-permute-start.12
  44.1 5.1 %collective-permute-done.8.refs_1_ = bf16[256,256]{1,0:T(8,128)(2,1)S(1)} collective-permute-done((bf16[256,256]{1,0:T(8,128)(2,1)S(1)}, bf16[256,256]{1,0:T(8,128)(2,1)S(1)}, u32[]{:S(2)}, u32[]{:S(2)}) %collective-permute-start.8) | collective-permute-done | bytes 131104 | tf_op jit(solution)/shard_map/cells_2_chunk_2/ppermute | solution.py:314
  49.2 0.0 collective-permute-start.11
  49.2 0.0 collective-permute-done.7.refs_8_
  49.2 1.2 %standardize.6 = (bf16[1024,256]{1,0:T(8,128)(2,1)S(1)}, bf16[1024,1024]{1,0:T(8,128)(2,1)S(1)}, f32[8,128]{1,0:T(8,128)S(1)}, bf16[1024,1024]{1,0:T(8,128)(2,1)S(1)}) custom-call(f32[8,1024]{1,0:T(8,128)S(1)} %broadcast_in_dim.3.mean_ref, bf16[256,256]{1,0:T(8,128)(2,1)S(1)} %get-tuple-element.71.refs_0_, ...), custom_call_target="tpu_custom_call", output_to_operand_aliasing={{1}: (9, {}), {3}: (10, {})} | custom-call | flops 20000000000 | bytes 1024 | tf_op jit(solution)/shard_map/standardize/pallas_call | solution.py:173
  50.4 0.1 collective-permute-start.17
  50.5 2.2 %gram.6.refs_2_ = bf16[1,1024,4096]{2,1,0:T(8,128)(2,1)} custom-call(f32[8,128]{1,0:T(8,128)S(1)} %get-tuple-element.80.count_ref, bf16[1024,1024]{1,0:T(8,128)(2,1)S(1)} %get-tuple-element.81.left_ref.refs_10_, bf16[1024,1024]{1,0:T(8,128)(2,1)S(1)} %get-tuple-element.82.refs_0_.refs_11_), custom_call_target="tpu_custom_call" | custom-call | flops 1024 | bytes 1024 | tf_op jit(solution)/shard_map/gram/pallas_call | solution.py:276
  52.8 0.0 collective-permute-done.12.refs_2_
  52.8 2.3 %collective-permute-done.11.refs_1_ = bf16[256,256]{1,0:T(8,128)(2,1)S(1)} collective-permute-done((bf16[256,256]{1,0:T(8,128)(2,1)S(1)}, bf16[256,256]{1,0:T(8,128)(2,1)S(1)}, u32[]{:S(2)}, u32[]{:S(2)}) %collective-permute-start.11) | collective-permute-done | bytes 131104 | tf_op jit(solution)/shard_map/cells_2_chunk_3/ppermute | solution.py:314
  55.1 1.3 %standardize.7 = (bf16[1024,256]{1,0:T(8,128)(2,1)S(1)}, bf16[1024,1024]{1,0:T(8,128)(2,1)S(1)}, f32[8,128]{1,0:T(8,128)S(1)}, bf16[1024,1024]{1,0:T(8,128)(2,1)S(1)}, bf16[1024,512]{1,0:T(8,128)(2,1)S(1)}) custom-call(f32[8,1024]{1,0:T(8,128)S(1)} %broadcast_in_dim.3.mean_ref, ...), custom_call_target="tpu_custom_call", output_to_operand_aliasing={{1}: (11, {}), {3}: (12, {})} | custom-call | flops 20000000000 | bytes 1024 | tf_op jit(solution)/shard_map/standardize/pallas_call | solution.py:173
  56.4 0.1 collective-permute-start.15
  56.5 2.6 %gram.7.refs_2_ = bf16[1,1024,4096]{2,1,0:T(8,128)(2,1)} custom-call(f32[8,128]{1,0:T(8,128)S(1)} %get-tuple-element.90.count_ref, bf16[1024,1024]{1,0:T(8,128)(2,1)S(1)} %get-tuple-element.91.left_ref, bf16[1024,1024]{1,0:T(8,128)(2,1)S(1)} %get-tuple-element.93.refs_0_.refs_1_, ...), custom_call_target="tpu_custom_call", output_to_operand_aliasing={{}: (4, {})} | custom-call | flops 1024 | bytes 1024 | tf_op jit(solution)/shard_map/gram/pallas_call | solution.py:276
  59.1 0.6 collective-permute-start.16
  59.7 1.4 %collective-permute-start.14 = (bf16[1024,256]{1,0:T(8,128)(2,1)S(1)}, bf16[1024,256]{1,0:T(8,128)(2,1)S(1)}, u32[]{:S(2)}, u32[]{:S(2)}) collective-permute-start(bf16[1024,256]{1,0:T(8,128)(2,1)S(1)} %get-tuple-element.94), channel_id=1, source_target_pairs={{0,2},{1,3},{2,0},{3,1},{4,6},{5,7},{6,4},{7,5},{8,10},{9,11},{10,... | collective-permute-start | bytes 1572872 | tf_op jit(solution)/shard_map/ppermute | solution.py:317
  61.0 0.3 collective-permute-done.17.refs_1_
  61.4 0.0 collective-permute-start.18
  61.4 2.9 %gram.8.refs_3_ = bf16[1,1024,4096]{2,1,0:T(8,128)(2,1)} custom-call(f32[8,128]{1,0:T(8,128)S(1)} %get-tuple-element.90.count_ref, bf16[1024,1024]{1,0:T(8,128)(2,1)S(1)} %get-tuple-element.91.left_ref, bf16[1024,512]{1,0:T(8,128)(2,1)S(1)} %get-tuple-element.95.refs_0_, ...), custom_call_target="tpu_custom_call", output_to_operand_aliasing={{}: (4, {})} | custom-call | flops 20000000000 | bytes 1024 | tf_op jit(solution)/shard_map/gram/pallas_call | solution.py:276
  64.3 0.0 collective-permute-done.16.refs_1_
  64.3 6.1 %gram.9.refs_1_ = bf16[1,1024,4096]{2,1,0:T(8,128)(2,1)} custom-call(f32[8,128]{1,0:T(8,128)S(1)} %get-tuple-element.90.count_ref, bf16[1024,1024]{1,0:T(8,128)(2,1)S(1)} %get-tuple-element.91.left_ref, bf16[1024,1024]{1,0:T(8,128)(2,1)S(1)} %collective-permute-done.15.refs_0_, ...), custom_call_target="tpu_custom_call", output_to_operand_aliasing={{}: (5, {})} | custom-call | flops 1024 | bytes 1024 | tf_op jit(solution)/shard_map/gram/pallas_call | solution.py:276
  70.4 3.2 %collective-permute-done.14.refs_0_ = bf16[1024,256]{1,0:T(8,128)(2,1)S(1)} collective-permute-done((bf16[1024,256]{1,0:T(8,128)(2,1)S(1)}, bf16[1024,256]{1,0:T(8,128)(2,1)S(1)}, u32[]{:S(2)}, u32[]{:S(2)}) %collective-permute-start.14) | collective-permute-done | bytes 524320 | tf_op jit(solution)/shard_map/ppermute | solution.py:317
  73.6 1.5 %gram.10.refs_1_ = bf16[1,1024,4096]{2,1,0:T(8,128)(2,1)} custom-call(f32[8,128]{1,0:T(8,128)S(1)} %get-tuple-element.90.count_ref, bf16[1024,1024]{1,0:T(8,128)(2,1)S(1)} %get-tuple-element.91.left_ref, bf16[1024,256]{1,0:T(8,128)(2,1)S(1)} %collective-permute-done.14.refs_0_, bf16[1,1024,4096]{2,1,0:T(8,128)(2,1)} %gram.9.refs_1_), custom_call_target="tpu_custom_call", output_to_operand_aliasing={{}: (3, {})} | custom-call | flops 1024 | bytes 1024 | tf_op jit(solution)/shard_map/gram/pallas_call | solution.py:276
  75.1 0.4 collective-permute-done.19.refs_0_
  75.5 1.5 %gram.11 = bf16[1,1024,4096]{2,1,0:T(8,128)(2,1)} custom-call(f32[8,128]{1,0:T(8,128)S(1)} %get-tuple-element.90.count_ref, bf16[1024,1024]{1,0:T(8,128)(2,1)S(1)} %get-tuple-element.91.left_ref, bf16[1024,256]{1,0:T(8,128)(2,1)S(1)} %collective-permute-done.19.refs_0_, bf16[1,1024,4096]{2,1,0:T(8,128)(2,1)} %gram.10.refs_1_), custom_call_target="tpu_custom_call", output_to_operand_aliasing={{}: (3, {})} | custom-call | flops 1024 | bytes 1024 | tf_op jit(solution)/shard_map/gram/pallas_call | solution.py:276
  (10 shorter events, 0.0 us)
Async XLA Ops:
  0.0 1.2 %copy-start = (bf16[512,1024]{1,0:T(8,128)(2,1)S(1)}, bf16[512,1024]{1,0:T(8,128)(2,1)}, u32[]{:S(2)}) copy-start(bf16[512,1024]{1,0:T(8,128)(2,1)} %expr_ref.1) | copy-start | bytes 3145732
  1.2 0.7 copy-start.1
  1.9 0.7 copy-start.2
  4.3 9.7 %collective-permute-start.4 = (bf16[272,256]{1,0:T(8,128)(2,1)S(1)}, bf16[272,256]{1,0:T(8,128)(2,1)S(1)}, u32[]{:S(2)}, u32[]{:S(2)}) collective-permute-start(bf16[272,256]{1,0:T(8,128)(2,1)S(1)} %get-tuple-element.63), channel_id=1, source_target_pairs={{0,12},{4,8},{8,4},{12,0},{1,13},{5,9},{9,5},{13,1},{2,14},{6,10},... | collective-permute-start | bytes 417800 | tf_op jit(solution)/shard_map/cells_3_chunk_0/ppermute | solution.py:314
  9.4 9.1 %collective-permute-start.2 = (bf16[272,256]{1,0:T(8,128)(2,1)S(1)}, bf16[272,256]{1,0:T(8,128)(2,1)S(1)}, u32[]{:S(2)}, u32[]{:S(2)}) collective-permute-start(bf16[272,256]{1,0:T(8,128)(2,1)S(1)} %get-tuple-element.60), channel_id=1, source_target_pairs={{0,4},{4,0},{8,12},{12,8},{1,5},{5,1},{9,13},{13,9},{2,6},{6,2},{1... | collective-permute-start | bytes 417800 | tf_op jit(solution)/shard_map/cells_1_chunk_0/ppermute | solution.py:314
  9.4 17.0 %collective-permute-start = (bf16[272,256]{1,0:T(8,128)(2,1)S(1)}, bf16[272,256]{1,0:T(8,128)(2,1)S(1)}, u32[]{:S(2)}, u32[]{:S(2)}) collective-permute-start(bf16[272,256]{1,0:T(8,128)(2,1)S(1)} %get-tuple-element.57), channel_id=1, source_target_pairs={{0,8},{4,12},{8,0},{12,4},{1,9},{5,13},{9,1},{13,5},{2,10},{6,14},... | collective-permute-start | bytes 417800 | tf_op jit(solution)/shard_map/cells_2_chunk_0/ppermute | solution.py:314
  14.7 15.1 %collective-permute-start.5 = (bf16[256,256]{1,0:T(8,128)(2,1)S(1)}, bf16[256,256]{1,0:T(8,128)(2,1)S(1)}, u32[]{:S(2)}, u32[]{:S(2)}) collective-permute-start(bf16[256,256]{1,0:T(8,128)(2,1)S(1)} %get-tuple-element.64), channel_id=1, source_target_pairs={{0,12},{4,8},{8,4},{12,0},{1,13},{5,9},{9,5},{13,1},{2,14},{6,10},... | collective-permute-start | bytes 393224 | tf_op jit(solution)/shard_map/cells_3_chunk_1/ppermute | solution.py:314
  18.5 12.3 %collective-permute-start.3 = (bf16[256,256]{1,0:T(8,128)(2,1)S(1)}, bf16[256,256]{1,0:T(8,128)(2,1)S(1)}, u32[]{:S(2)}, u32[]{:S(2)}) collective-permute-start(bf16[256,256]{1,0:T(8,128)(2,1)S(1)} %get-tuple-element.61), channel_id=1, source_target_pairs={{0,4},{4,0},{8,12},{12,8},{1,5},{5,1},{9,13},{13,9},{2,6},{6,2},{1... | collective-permute-start | bytes 393224 | tf_op jit(solution)/shard_map/cells_1_chunk_1/ppermute | solution.py:314
  26.4 8.6 %collective-permute-start.1 = (bf16[256,256]{1,0:T(8,128)(2,1)S(1)}, bf16[256,256]{1,0:T(8,128)(2,1)S(1)}, u32[]{:S(2)}, u32[]{:S(2)}) collective-permute-start(bf16[256,256]{1,0:T(8,128)(2,1)S(1)} %get-tuple-element.58), channel_id=1, source_target_pairs={{0,8},{4,12},{8,0},{12,4},{1,9},{5,13},{9,1},{13,5},{2,10},{6,14},... | collective-permute-start | bytes 393224 | tf_op jit(solution)/shard_map/cells_2_chunk_1/ppermute | solution.py:314
  28.2 21.0 %collective-permute-start.7 = (bf16[1024,256]{1,0:T(8,128)(2,1)S(1)}, bf16[1024,256]{1,0:T(8,128)(2,1)S(1)}, u32[]{:S(2)}, u32[]{:S(2)}) collective-permute-start(bf16[1024,256]{1,0:T(8,128)(2,1)S(1)} %get-tuple-element.70), channel_id=1, source_target_pairs={{0,2},{1,3},{2,0},{3,1},{4,6},{5,7},{6,4},{7,5},{8,10},{9,11},{10,... | collective-permute-start | bytes 1572872 | tf_op jit(solution)/shard_map/far_0/ppermute | solution.py:317
  29.8 9.8 %collective-permute-start.10 = (bf16[256,256]{1,0:T(8,128)(2,1)S(1)}, bf16[256,256]{1,0:T(8,128)(2,1)S(1)}, u32[]{:S(2)}, u32[]{:S(2)}) collective-permute-start(bf16[256,256]{1,0:T(8,128)(2,1)S(1)} %get-tuple-element.77), channel_id=1, source_target_pairs={{0,12},{4,8},{8,4},{12,0},{1,13},{5,9},{9,5},{13,1},{2,14},{6,10},... | collective-permute-start | bytes 393224 | tf_op jit(solution)/shard_map/cells_3_chunk_2/ppermute | solution.py:314
  30.8 12.6 %collective-permute-start.9 = (bf16[256,256]{1,0:T(8,128)(2,1)S(1)}, bf16[256,256]{1,0:T(8,128)(2,1)S(1)}, u32[]{:S(2)}, u32[]{:S(2)}) collective-permute-start(bf16[256,256]{1,0:T(8,128)(2,1)S(1)} %get-tuple-element.75), channel_id=1, source_target_pairs={{0,4},{4,0},{8,12},{12,8},{1,5},{5,1},{9,13},{13,9},{2,6},{6,2},{1... | collective-permute-start | bytes 393224 | tf_op jit(solution)/shard_map/cells_1_chunk_2/ppermute | solution.py:314
  35.0 14.2 %collective-permute-start.8 = (bf16[256,256]{1,0:T(8,128)(2,1)S(1)}, bf16[256,256]{1,0:T(8,128)(2,1)S(1)}, u32[]{:S(2)}, u32[]{:S(2)}) collective-permute-start(bf16[256,256]{1,0:T(8,128)(2,1)S(1)} %get-tuple-element.73), channel_id=1, source_target_pairs={{0,8},{4,12},{8,0},{12,4},{1,9},{5,13},{9,1},{13,5},{2,10},{6,14},... | collective-permute-start | bytes 393224 | tf_op jit(solution)/shard_map/cells_2_chunk_2/ppermute | solution.py:314
  36.8 15.9 %collective-permute-start.6 = (bf16[1024,256]{1,0:T(8,128)(2,1)S(1)}, bf16[1024,256]{1,0:T(8,128)(2,1)S(1)}, u32[]{:S(2)}, u32[]{:S(2)}) collective-permute-start(bf16[1024,256]{1,0:T(8,128)(2,1)S(1)} %get-tuple-element.67), channel_id=1, source_target_pairs={{0,2},{1,3},{2,0},{3,1},{4,6},{5,7},{6,4},{7,5},{8,10},{9,11},{10,... | collective-permute-start | bytes 1572872 | tf_op jit(solution)/shard_map/far_1/ppermute | solution.py:317
  39.6 13.1 %collective-permute-start.13 = (bf16[256,256]{1,0:T(8,128)(2,1)S(1)}, bf16[256,256]{1,0:T(8,128)(2,1)S(1)}, u32[]{:S(2)}, u32[]{:S(2)}) collective-permute-start(bf16[256,256]{1,0:T(8,128)(2,1)S(1)} %get-tuple-element.89), channel_id=1, source_target_pairs={{0,12},{4,8},{8,4},{12,0},{1,13},{5,9},{9,5},{13,1},{2,14},{6,10},... | collective-permute-start | bytes 393224 | tf_op jit(solution)/shard_map/cells_3_chunk_3/ppermute | solution.py:314
  43.4 9.3 %collective-permute-start.12 = (bf16[256,256]{1,0:T(8,128)(2,1)S(1)}, bf16[256,256]{1,0:T(8,128)(2,1)S(1)}, u32[]{:S(2)}, u32[]{:S(2)}) collective-permute-start(bf16[256,256]{1,0:T(8,128)(2,1)S(1)} %get-tuple-element.87), channel_id=1, source_target_pairs={{0,4},{4,0},{8,12},{12,8},{1,5},{5,1},{9,13},{13,9},{2,6},{6,2},{1... | collective-permute-start | bytes 393224 | tf_op jit(solution)/shard_map/cells_1_chunk_3/ppermute | solution.py:314
  49.2 5.9 %collective-permute-start.11 = (bf16[256,256]{1,0:T(8,128)(2,1)S(1)}, bf16[256,256]{1,0:T(8,128)(2,1)S(1)}, u32[]{:S(2)}, u32[]{:S(2)}) collective-permute-start(bf16[256,256]{1,0:T(8,128)(2,1)S(1)} %get-tuple-element.85), channel_id=1, source_target_pairs={{0,8},{4,12},{8,0},{12,4},{1,9},{5,13},{9,1},{13,5},{2,10},{6,14},... | collective-permute-start | bytes 393224 | tf_op jit(solution)/shard_map/cells_2_chunk_3/ppermute | solution.py:314
  50.4 10.9 %collective-permute-start.17 = (bf16[1024,256]{1,0:T(8,128)(2,1)S(1)}, bf16[1024,256]{1,0:T(8,128)(2,1)S(1)}, u32[]{:S(2)}, u32[]{:S(2)}) collective-permute-start(bf16[1024,256]{1,0:T(8,128)(2,1)S(1)} %get-tuple-element.96), channel_id=1, source_target_pairs={{0,2},{1,3},{2,0},{3,1},{4,6},{5,7},{6,4},{7,5},{8,10},{9,11},{10,... | collective-permute-start | bytes 1572872 | tf_op jit(solution)/shard_map/far_2/ppermute | solution.py:317
  56.4 7.9 %collective-permute-start.15 = (bf16[1024,1024]{1,0:T(8,128)(2,1)S(1)}, bf16[1024,1024]{1,0:T(8,128)(2,1)S(1)}, u32[]{:S(2)}, u32[]{:S(2)}) collective-permute-start(bf16[1024,1024]{1,0:T(8,128)(2,1)S(1)} %get-tuple-element.93.refs_0_.refs_1_), channel_id=1, source_target_pairs={{0,1},{1,0},{2,3},{3,2},{4,5},{5,4},{6,7},{7,6},{8,9},{9,8},{10,11... | collective-permute-start | bytes 6291464 | tf_op jit(solution)/shard_map/near/ppermute | solution.py:321
  59.1 5.1 %collective-permute-start.16 = (bf16[1024,512]{1,0:T(8,128)(2,1)S(1)}, bf16[1024,512]{1,0:T(8,128)(2,1)S(1)}, u32[]{:S(2)}, u32[]{:S(2)}) collective-permute-start(bf16[1024,512]{1,0:T(8,128)(2,1)S(1)} %get-tuple-element.95.refs_0_), channel_id=1, source_target_pairs={{0,1},{1,0},{2,3},{3,2},{4,5},{5,4},{6,7},{7,6},{8,9},{9,8},{10,11... | collective-permute-start | bytes 3145736 | tf_op jit(solution)/shard_map/far_near/ppermute | solution.py:321
  59.7 13.9 %collective-permute-start.14 = (bf16[1024,256]{1,0:T(8,128)(2,1)S(1)}, bf16[1024,256]{1,0:T(8,128)(2,1)S(1)}, u32[]{:S(2)}, u32[]{:S(2)}) collective-permute-start(bf16[1024,256]{1,0:T(8,128)(2,1)S(1)} %get-tuple-element.94), channel_id=1, source_target_pairs={{0,2},{1,3},{2,0},{3,1},{4,6},{5,7},{6,4},{7,5},{8,10},{9,11},{10,... | collective-permute-start | bytes 1572872 | tf_op jit(solution)/shard_map/ppermute | solution.py:317
  61.4 2.9 %collective-permute-start.18 = (bf16[1024,256]{1,0:T(8,128)(2,1)S(1)}, bf16[1024,256]{1,0:T(8,128)(2,1)S(1)}, u32[]{:S(2)}, u32[]{:S(2)}) collective-permute-start(bf16[1024,256]{1,0:T(8,128)(2,1)S(1)} %collective-permute-done.17.refs_1_), channel_id=1, source_target_pairs={{0,1},{1,0},{2,3},{3,2},{4,5},{5,4},{6,7},{7,6},{8,9},{9,8},{10,11... | collective-permute-start | bytes 1572872 | tf_op jit(solution)/shard_map/far_near_2/ppermute | solution.py:321
  73.6 1.9 %collective-permute-start.19 = (bf16[1024,256]{1,0:T(8,128)(2,1)S(1)}, bf16[1024,256]{1,0:T(8,128)(2,1)S(1)}, u32[]{:S(2)}, u32[]{:S(2)}) collective-permute-start(bf16[1024,256]{1,0:T(8,128)(2,1)S(1)} %collective-permute-done.14.refs_0_), channel_id=1, source_target_pairs={{0,1},{1,0},{2,3},{3,2},{4,5},{5,4},{6,7},{7,6},{8,9},{9,8},{10,11... | collective-permute-start | bytes 1572872 | tf_op jit(solution)/shard_map/far_near_3/ppermute | solution.py:321

commit v18 on v17

--- a/solution.py
+++ b/solution.py
@@ -77,17 +77,46 @@
     return [flat[k * types : (k + 1) * types] for k in range(len(widths))]
 
 
-def standardize_kernel(types, cap, lead, separate, start, gathered, mean_ref, *refs):
+def factor_column(cap, lead, tail_ref, base):
+    piece = min(lead, cap)
+    column = jnp.zeros((cap, 1), jnp.float32)
+    for i in range(pl.cdiv(cap, lead)):
+        line = tail_ref[base : base + TILE, 0:piece].astype(jnp.float32)[i : i + 1, :]
+        diagonal = (
+            lax.broadcasted_iota(jnp.int32, (cap, piece), 0)
+            == lax.broadcasted_iota(jnp.int32, (cap, piece), 1) + i * lead
+        )
+        column += jnp.sum(jnp.where(diagonal, line, 0.0), axis=1, keepdims=True)
+    return column
+
+
+def residuals(column, mean, levels):
+    live = column > 0.0
+    expected = jnp.where(live, column * mean, 1.0)
+    return jnp.where(
+        live,
+        (levels.astype(jnp.float32) - expected)
+        * lax.rsqrt(expected + expected * expected * (1.0 / dispersion)),
+        0.0,
+    )
+
+
+def thirds(value):
+    parts = []
+    for _ in range(3):
+        parts.append(value.astype(jnp.bfloat16).astype(jnp.float32))
+        value = value - parts[-1]
+    return parts
+
+
+def standardize_kernel(types, cap, lead, separate, start, gathered, late, mean_ref, *refs):
     blocks = refs[:types]
     tails = refs[types : 2 * types] if separate else blocks
     base = 0 if separate else cap
     refs = refs[2 * types :] if separate else refs[types:]
     work, turned, sems = refs[-3:]
-    if gathered:
-        scaled_ref, turned_ref, count_ref, all_ref, *joined_refs = refs[-7 - gathered[0] : -3]
-    else:
-        scaled_ref, turned_ref, count_ref, all_ref = refs[-7:-3]
-        joined_refs = []
+    more = (gathered[0] if gathered else 0) + (1 if late else 0)
+    scaled_ref, turned_ref, count_ref, all_ref, *joined_refs = refs[-7 - more : -3]
     copies = []
     if gathered:
         sources = refs[: len(gathered[1])]
@@ -97,29 +126,15 @@
             copies[-1].start()
     width = work.shape[1]
     mean = mean_ref[0:1, start : start + width]
-    piece = min(lead, cap)
     total = jnp.zeros((1, width), jnp.float32)
     count = jnp.zeros((1, 1), jnp.float32)
     alive = []
     for j in range(types):
-        column = jnp.zeros((cap, 1), jnp.float32)
-        for i in range(pl.cdiv(cap, lead)):
-            line = tails[j][base : base + TILE, 0:piece].astype(jnp.float32)[i : i + 1, :]
-            diagonal = (
-                lax.broadcasted_iota(jnp.int32, (cap, piece), 0)
-                == lax.broadcasted_iota(jnp.int32, (cap, piece), 1) + i * lead
-            )
-            column += jnp.sum(jnp.where(diagonal, line, 0.0), axis=1, keepdims=True)
+        column = factor_column(cap, lead, tails[j], base)
         live = column > 0.0
         alive.append(live)
         count += jnp.sum(jnp.where(live, 1.0, 0.0), axis=0, keepdims=True)
-        expected = jnp.where(live, column * mean, 1.0)
-        values = blocks[j][0:cap, :].astype(jnp.float32)
-        residual = jnp.where(
-            live,
-            (values - expected) * lax.rsqrt(expected + expected * expected * (1.0 / dispersion)),
-            0.0,
-        )
+        residual = residuals(column, mean, blocks[j][0:cap, :])
         work[j * cap : (j + 1) * cap, :] = residual
         total += jnp.sum(residual, axis=0, keepdims=True)
     center = total / count
@@ -134,6 +149,14 @@
         scaled_ref[j * cap : (j + 1) * cap, :] = scaled.astype(jnp.bfloat16)
         work[j * cap : (j + 1) * cap, :] = scaled
     slots = types * cap
+    if late:
+        sent_ref = joined_refs[-1]
+        sent_ref[0 : slots - cap, :] = scaled_ref[cap:slots, :]
+        row = lax.broadcasted_iota(jnp.int32, (TILE, 1), 0)
+        notes = jnp.zeros((TILE, width), jnp.float32)
+        for i, part in enumerate(thirds(center) + thirds(scale) + thirds(mean)):
+            notes = jnp.where(row == i, part, notes)
+        sent_ref[slots - cap : slots - cap + TILE, :] = notes.astype(jnp.bfloat16)
     columns = pl.ds(start, width)
     copies.append(pltpu.make_async_copy(scaled_ref, all_ref.at[:, columns], sems.at[0]))
     copies[-1].start()
@@ -145,7 +168,7 @@
     count_ref[...] = jnp.broadcast_to(count, count_ref.shape)
 
 
-def standardize(types, cap, mean, start, blocks, first, left, own, gather):
+def standardize(types, cap, mean, start, blocks, first, left, own, gather, late):
     lead, width = first[0].shape[1], blocks[0].shape[1]
     panel = mean.shape[1]
     separate = first is not blocks
@@ -164,6 +187,8 @@
             specs.append(whole)
             args.append(array)
         shapes.append(jax.ShapeDtypeStruct((slots, column), jnp.bfloat16))
+    if late:
+        shapes.append(jax.ShapeDtypeStruct((slots - cap + TILE, width), jnp.bfloat16))
     aliases = {}
     for value, output in ((left, 1), (own, 3)):
         if value is not None:
@@ -179,6 +204,7 @@
             separate,
             start,
             (len(gather), gathered) if gathered else None,
+            late,
         ),
         grid=(1,),
         out_shape=[
@@ -200,6 +226,33 @@
         cost_estimate=lengthy,
         name="standardize",
     )(*args)
+
+
+def finish_kernel(cap, lead, sent_ref, local_ref, tail_ref, out_ref):
+    rest = out_ref.shape[0] - cap
+    out_ref[cap : cap + rest, :] = sent_ref[0:rest, :]
+    notes = sent_ref[rest : rest + TILE, :].astype(jnp.float32)
+    center, scale, mean = [
+        notes[i : i + 1, :] + notes[i + 1 : i + 2, :] + notes[i + 2 : i + 3, :] for i in (0, 3, 6)
+    ]
+    column = factor_column(cap, lead, tail_ref, 0)
+    residual = residuals(column, mean, local_ref[0:cap, :])
+    centered = jnp.where(column > 0.0, residual - center, 0.0)
+    out_ref[0:cap, :] = (centered * scale).astype(jnp.bfloat16)
+
+
+def finish(types, cap, first, local, sent):
+    lead, width = first.shape[1], sent.shape[1]
+    return pl.pallas_call(
+        functools.partial(finish_kernel, cap, lead),
+        grid=(1,),
+        out_shape=jax.ShapeDtypeStruct((types * cap, width), jnp.bfloat16),
+        in_specs=[whole, whole, pl.BlockSpec((TILE, lead), lambda i: (cap // TILE, 0))],
+        out_specs=whole,
+        compiler_params=pltpu.CompilerParams(vmem_limit_bytes=VMEM),
+        cost_estimate=brief,
+        name="finish",
+    )(sent, local, first)
 
 
 def gram_kernel(blocks, cores, strip, groups, arrays, count_ref, left_ref, *refs):
@@ -333,6 +386,10 @@
             with jax.named_scope(f"cells_{j}_chunk_{k}"):
                 arrived.append(swap(block, j))
         before = list(arrived)
+        if k == 1:
+            with jax.named_scope("far_local"):
+                local = [across(packed[-1][0], d) for d in range(1, chips)]
+            arrived[0] = after(arrived[0], *local)
         if k >= 2:
             arrived[0] = after(arrived[0], *far[k - 2])
         if k == 0:
@@ -344,7 +401,7 @@
             arrived[0] = after(arrived[0], out)
             gather = [[got[d] for got in far[: k - 1]] for d in range(chips - 1)]
         scaled, left, count, own, *joined = standardize(
-            types, cap, mean, starts[k], arrived, first, left, own, gather
+            types, cap, mean, starts[k], arrived, first, left, own, gather, k == chunks - 1
         )
         if k < chunks - 1:
             with jax.named_scope(f"far_{k}"):
@@ -353,6 +410,7 @@
     multiply = functools.partial(gram, blocks, cores, count, left)
     last = chunks - 1
     near = side("near", own)
+    sent = joined.pop()
     joined_near = [[side("far_near", p)] for p in joined] or [[]] * (chips - 1)
     joined = [[p] for p in joined] or [[]] * (chips - 1)
     if out is None:
@@ -364,14 +422,18 @@
             ([own], (0, 0, edge, panel - edge, 0, edge)),
         ]
         out = multiply(groups, out, brief)
-    final = [across(after(scaled, out), d) for d in range(1, chips)]
+    final = [across(after(sent, out), d) for d in range(1, chips)]
     second = [side(f"far_near_{last - 1}", p, own) for p in far[last - 1]]
     groups = [([*p, far[last - 1][i]], (i + 1, 0, 0)) for i, p in enumerate(joined)]
     out = multiply(groups, out, lengthy)
     groups = [([near], (0, 1, 0))]
     groups += [([*p, second[i]], (i + 1, 1, 0)) for i, p in enumerate(joined_near)]
     out = multiply(groups, out, brief)
-    final_near = [side(f"far_near_{last}", p, out) for p in final]
+    final = [
+        finish(types, cap, packed[0][0], near_by, after(got, out))
+        for near_by, got in zip(local, final)
+    ]
+    final_near = [side(f"far_near_{last}", p) for p in final]
     edge = starts[last]
     out = multiply([([p], (d, 0, edge)) for d, p in enumerate(final, 1)], out, brief)
     return multiply([([p], (d, 1, edge)) for d, p in enumerate(final_near, 1)], out, brief)

time: 77.4 us -> 76.5 us (0.988)
  waiting for transfers between devices: 23.5 us -> 20 us
  starting transfers between devices: 25.5 us -> 27 us
  Pallas kernels: 24.7 us -> 25.7 us
    ppermute x12, waiting for transfers between devices: 19.5 us -> 14.7 us  [swap(): return lax.ppermute(block, 'cells', [(s, s ^ by) for s in range(types)])]
    ppermute x4 -> x5, waiting for transfers between devices: 3.57 us -> 4.86 us  [across(): lax.ppermute(panel_, 'blk', [(b, (b + by * cores) % blocks) for b in rang...]
    ppermute x4 -> x5, starting transfers between devices: 5.78 us -> 6.64 us  [across(): lax.ppermute(panel_, 'blk', [(b, (b + by * cores) % blocks) for b in rang...]
    pallas_call x4, Pallas kernels: 6.12 us -> 6.96 us  [standardize(): pl.pallas_call(functools.partial(standardize_kernel, types, cap, lead, se...]
  transfers between devices with their start and end apart: 20 -> 21, of which waited for: 8 -> 7; matrix products, arithmetic and copies ran while one was open for 1% -> 1% of each run, Pallas kernels for 28% -> 29%
where the time goes in v18:
time: 76.5 us; the launch traced here: 76.3 us
  starting transfers between devices  27 us (35%)
  Pallas kernels  25.7 us (34%)
  waiting for transfers between devices  20 us (26%)
  local copies, waits for them, and re-layouts  3.27 us (4%)
    ppermute x12, starting transfers between devices, swap(): return lax.ppermute(block, 'cells', [(s, s ^ by) for s in range(types)])  19.6 us
    pallas_call x6, Pallas kernels, gram(): pl.pallas_call(functools.partial(gram_kernel, blocks, cores, strip, layou...  16.9 us
    ppermute x12, waiting for transfers between devices, swap(): return lax.ppermute(block, 'cells', [(s, s ^ by) for s in range(types)])  14.7 us
    pallas_call x4, Pallas kernels, standardize(): pl.pallas_call(functools.partial(standardize_kernel, types, cap, lead, se...  6.96 us
    ppermute x5, starting transfers between devices, across(): lax.ppermute(panel_, 'blk', [(b, (b + by * cores) % blocks) for b in rang...  6.64 us
    ppermute x5, waiting for transfers between devices, across(): lax.ppermute(panel_, 'blk', [(b, (b + by * cores) % blocks) for b in rang...  4.86 us
    unnamed x6, local copies, waits for them, and re-layouts  2.58 us
    pallas_call x1, Pallas kernels, pack(): pl.pallas_call(functools.partial(pack_kernel, types, cap, widths), out_sh...  1.71 us
  transfers between devices with their start and end apart: 21, of which 7 were waited for; matrix products, arithmetic and copies ran while one was open for 1% of the time, Pallas kernels for 29%

profile of v18, /device:TPU:0, one launch (start us, length us, event | category | flops | bytes accessed | tf_op | source)
XLA Modules:
  0.0 76.3 jit_solution(6851508406888233442)
XLA Ops:
  0.0 1.2 %copy-done = bf16[512,1024]{1,0:T(8,128)(2,1)S(1)} copy-done((bf16[512,1024]{1,0:T(8,128)(2,1)S(1)}, bf16[512,1024]{1,0:T(8,128)(2,1)}, u32[]{:S(2)}) %copy-start) | copy-done | bytes 1048600
  1.2 0.7 copy-done.1
  1.9 0.7 copy-done.2
  2.6 1.7 %pack.1 = (bf16[272,256]{1,0:T(8,128)(2,1)S(1)}, bf16[272,256]{1,0:T(8,128)(2,1)S(1)}, bf16[272,256]{1,0:T(8,128)(2,1)S(1)}, bf16[272,256]{1,0:T(8,128)(2,1)S(1)...) custom-call(s32[512]{0:T(512)S(1)} %copy-done.1, ...), custom_call_target="tpu_custom_call" | custom-call | flops 1024 | bytes 1024 | tf_op jit(solution)/shard_map/pack/pallas_call | solution.py:68
  4.3 5.1 %collective-permute-start.5 = (bf16[272,256]{1,0:T(8,128)(2,1)S(1)}, bf16[272,256]{1,0:T(8,128)(2,1)S(1)}, u32[]{:S(2)}, u32[]{:S(2)}) collective-permute-start(bf16[272,256]{1,0:T(8,128)(2,1)S(1)} %get-tuple-element.65), channel_id=1, source_target_pairs={{0,12},{4,8},{8,4},{12,0},{1,13},{5,9},{9,5},{13,1},{2,14},{6,10},... | collective-permute-start | bytes 417800 | tf_op jit(solution)/shard_map/cells_3_chunk_0/ppermute | solution.py:367
  9.4 0.6 collective-permute-start.1
  10.1 1.6 %collective-permute-start = (bf16[256,256]{1,0:T(8,128)(2,1)S(1)}, bf16[256,256]{1,0:T(8,128)(2,1)S(1)}, u32[]{:S(2)}, u32[]{:S(2)}) collective-permute-start(bf16[256,256]{1,0:T(8,128)(2,1)S(1)} %get-tuple-element.85.refs_0_), channel_id=1, source_target_pairs={{0,2},{1,3},{2,0},{3,1},{4,6},{5,7},{6,4},{7,5},{8,10},{9,11},{10,... | collective-permute-start | bytes 393224 | tf_op jit(solution)/shard_map/far_local/ppermute | solution.py:370
  11.7 3.3 %collective-permute-done.local_ref = bf16[256,256]{1,0:T(8,128)(2,1)S(1)} collective-permute-done((bf16[256,256]{1,0:T(8,128)(2,1)S(1)}, bf16[256,256]{1,0:T(8,128)(2,1)S(1)}, u32[]{:S(2)}, u32[]{:S(2)}) %collective-permute-start) | collective-permute-done | bytes 131104 | tf_op jit(solution)/shard_map/far_local/ppermute | solution.py:370
  15.0 0.0 collective-permute-done.5.refs_3_.refs_7_
  15.0 0.7 broadcast_in_dim.3.mean_ref
  15.7 3.7 %collective-permute-start.6 = (bf16[256,256]{1,0:T(8,128)(2,1)S(1)}, bf16[256,256]{1,0:T(8,128)(2,1)S(1)}, u32[]{:S(2)}, u32[]{:S(2)}) collective-permute-start(bf16[256,256]{1,0:T(8,128)(2,1)S(1)} %get-tuple-element.66), channel_id=1, source_target_pairs={{0,12},{4,8},{8,4},{12,0},{1,13},{5,9},{9,5},{13,1},{2,14},{6,10},... | collective-permute-start | bytes 393224 | tf_op jit(solution)/shard_map/cells_3_chunk_1/ppermute | solution.py:367
  19.5 0.0 collective-permute-done.3.refs_2_.refs_6_
  19.5 0.0 collective-permute-start.4
  19.5 6.9 %collective-permute-done.1.refs_1_.refs_5_ = bf16[272,256]{1,0:T(8,128)(2,1)S(1)} collective-permute-done((bf16[272,256]{1,0:T(8,128)(2,1)S(1)}, bf16[272,256]{1,0:T(8,128)(2,1)S(1)}, u32[]{:S(2)}, u32[]{:S(2)}) %collective-permute-start.1) | collective-permute-done | bytes 139296 | tf_op jit(solution)/shard_map/cells_2_chunk_0/ppermute | solution.py:367
  26.4 1.8 %standardize.4 = (bf16[1024,256]{1,0:T(8,128)(2,1)S(1)}, bf16[1024,1024]{1,0:T(8,128)(2,1)S(1)}, f32[8,128]{1,0:T(8,128)}, bf16[1024,1024]{1,0:T(8,128)(2,1)S(1)}) custom-call(f32[8,1024]{1,0:T(8,128)S(1)} %broadcast_in_dim.3.mean_ref, bf16[272,256]{1,0:T(8,128)(2,1)S(1)} %get-tuple-element.53.refs_0_.refs_4_.tail_ref, ...), custom_call_target="tpu_custom_call" | custom-call | flops 20000000000 | bytes 1024 | tf_op jit(solution)/shard_map/standardize/pallas_call | solution.py:198
  28.2 1.6 %collective-permute-start.8 = (bf16[1024,256]{1,0:T(8,128)(2,1)S(1)}, bf16[1024,256]{1,0:T(8,128)(2,1)S(1)}, u32[]{:S(2)}, u32[]{:S(2)}) collective-permute-start(bf16[1024,256]{1,0:T(8,128)(2,1)S(1)} %get-tuple-element.72), channel_id=1, source_target_pairs={{0,2},{1,3},{2,0},{3,1},{4,6},{5,7},{6,4},{7,5},{8,10},{9,11},{10,... | collective-permute-start | bytes 1572872 | tf_op jit(solution)/shard_map/far_0/ppermute | solution.py:370
  29.8 1.5 %collective-permute-start.11 = (bf16[256,256]{1,0:T(8,128)(2,1)S(1)}, bf16[256,256]{1,0:T(8,128)(2,1)S(1)}, u32[]{:S(2)}, u32[]{:S(2)}) collective-permute-start(bf16[256,256]{1,0:T(8,128)(2,1)S(1)} %get-tuple-element.79), channel_id=1, source_target_pairs={{0,12},{4,8},{8,4},{12,0},{1,13},{5,9},{9,5},{13,1},{2,14},{6,10},... | collective-permute-start | bytes 393224 | tf_op jit(solution)/shard_map/cells_3_chunk_2/ppermute | solution.py:367
  31.3 0.0 collective-permute-done.4.refs_2_
  31.3 2.8 %collective-permute-start.10 = (bf16[256,256]{1,0:T(8,128)(2,1)S(1)}, bf16[256,256]{1,0:T(8,128)(2,1)S(1)}, u32[]{:S(2)}, u32[]{:S(2)}) collective-permute-start(bf16[256,256]{1,0:T(8,128)(2,1)S(1)} %get-tuple-element.77), channel_id=1, source_target_pairs={{0,4},{4,0},{8,12},{12,8},{1,5},{5,1},{9,13},{13,9},{2,6},{6,2},{1... | collective-permute-start | bytes 393224 | tf_op jit(solution)/shard_map/cells_1_chunk_2/ppermute | solution.py:367
  34.1 1.0 %collective-permute-done.2.refs_1_ = bf16[256,256]{1,0:T(8,128)(2,1)S(1)} collective-permute-done((bf16[256,256]{1,0:T(8,128)(2,1)S(1)}, bf16[256,256]{1,0:T(8,128)(2,1)S(1)}, u32[]{:S(2)}, u32[]{:S(2)}) %collective-permute-start.2) | collective-permute-done | bytes 131104 | tf_op jit(solution)/shard_map/cells_2_chunk_1/ppermute | solution.py:367
  35.2 0.0 collective-permute-start.9
  35.2 1.8 %standardize.5 = (bf16[1024,256]{1,0:T(8,128)(2,1)S(1)}, bf16[1024,1024]{1,0:T(8,128)(2,1)S(1)}, f32[8,128]{1,0:T(8,128)}, bf16[1024,1024]{1,0:T(8,128)(2,1)S(1)}) custom-call(f32[8,1024]{1,0:T(8,128)S(1)} %broadcast_in_dim.3.mean_ref, bf16[256,256]{1,0:T(8,128)(2,1)S(1)} %get-tuple-element.57.refs_0_, ...), custom_call_target="tpu_custom_call", output_to_operand_aliasing={{1}: (9, {}), {3}: (10, {})} | custom-call | flops 20000000000 | bytes 1024 | tf_op jit(solution)/shard_map/standardize/pallas_call | solution.py:198
  37.0 2.6 %collective-permute-start.7 = (bf16[1024,256]{1,0:T(8,128)(2,1)S(1)}, bf16[1024,256]{1,0:T(8,128)(2,1)S(1)}, u32[]{:S(2)}, u32[]{:S(2)}) collective-permute-start(bf16[1024,256]{1,0:T(8,128)(2,1)S(1)} %get-tuple-element.69), channel_id=1, source_target_pairs={{0,2},{1,3},{2,0},{3,1},{4,6},{5,7},{6,4},{7,5},{8,10},{9,11},{10,... | collective-permute-start | bytes 1572872 | tf_op jit(solution)/shard_map/far_1/ppermute | solution.py:370
  39.6 0.0 collective-permute-done.11.refs_3_
  39.6 3.8 %collective-permute-start.14 = (bf16[256,256]{1,0:T(8,128)(2,1)S(1)}, bf16[256,256]{1,0:T(8,128)(2,1)S(1)}, u32[]{:S(2)}, u32[]{:S(2)}) collective-permute-start(bf16[256,256]{1,0:T(8,128)(2,1)S(1)} %get-tuple-element.91), channel_id=1, source_target_pairs={{0,12},{4,8},{8,4},{12,0},{1,13},{5,9},{9,5},{13,1},{2,14},{6,10},... | collective-permute-start | bytes 393224 | tf_op jit(solution)/shard_map/cells_3_chunk_3/ppermute | solution.py:367
  43.4 0.0 collective-permute-done.10.refs_2_
  43.4 1.9 %collective-permute-start.13 = (bf16[256,256]{1,0:T(8,128)(2,1)S(1)}, bf16[256,256]{1,0:T(8,128)(2,1)S(1)}, u32[]{:S(2)}, u32[]{:S(2)}) collective-permute-start(bf16[256,256]{1,0:T(8,128)(2,1)S(1)} %get-tuple-element.89), channel_id=1, source_target_pairs={{0,4},{4,0},{8,12},{12,8},{1,5},{5,1},{9,13},{13,9},{2,6},{6,2},{1... | collective-permute-start | bytes 393224 | tf_op jit(solution)/shard_map/cells_1_chunk_3/ppermute | solution.py:367
  45.4 3.6 %collective-permute-done.9.refs_1_ = bf16[256,256]{1,0:T(8,128)(2,1)S(1)} collective-permute-done((bf16[256,256]{1,0:T(8,128)(2,1)S(1)}, bf16[256,256]{1,0:T(8,128)(2,1)S(1)}, u32[]{:S(2)}, u32[]{:S(2)}) %collective-permute-start.9) | collective-permute-done | bytes 131104 | tf_op jit(solution)/shard_map/cells_2_chunk_2/ppermute | solution.py:367
  49.0 1.2 %standardize.6 = (bf16[1024,256]{1,0:T(8,128)(2,1)S(1)}, bf16[1024,1024]{1,0:T(8,128)(2,1)S(1)}, f32[8,128]{1,0:T(8,128)S(1)}, bf16[1024,1024]{1,0:T(8,128)(2,1)S(1)}) custom-call(f32[8,1024]{1,0:T(8,128)S(1)} %broadcast_in_dim.3.mean_ref, bf16[256,256]{1,0:T(8,128)(2,1)S(1)} %get-tuple-element.73.refs_0_, ...), custom_call_target="tpu_custom_call", output_to_operand_aliasing={{1}: (9, {}), {3}: (10, {})} | custom-call | flops 20000000000 | bytes 1024 | tf_op jit(solution)/shard_map/standardize/pallas_call | solution.py:198
  50.2 0.1 collective-permute-start.18
  50.3 2.2 %gram.6.refs_2_ = bf16[1,1024,4096]{2,1,0:T(8,128)(2,1)} custom-call(f32[8,128]{1,0:T(8,128)S(1)} %get-tuple-element.82.count_ref, bf16[1024,1024]{1,0:T(8,128)(2,1)S(1)} %get-tuple-element.83.left_ref.refs_10_, bf16[1024,1024]{1,0:T(8,128)(2,1)S(1)} %get-tuple-element.84.refs_0_.refs_11_), custom_call_target="tpu_custom_call" | custom-call | flops 1024 | bytes 1024 | tf_op jit(solution)/shard_map/gram/pallas_call | solution.py:329
  52.5 0.0 collective-permute-done.7.refs_9_
  52.5 0.0 collective-permute-done.14.refs_3_
  52.5 3.1 %collective-permute-done.12.refs_1_ = bf16[256,256]{1,0:T(8,128)(2,1)S(1)} collective-permute-done((bf16[256,256]{1,0:T(8,128)(2,1)S(1)}, bf16[256,256]{1,0:T(8,128)(2,1)S(1)}, u32[]{:S(2)}, u32[]{:S(2)}) %collective-permute-start.12) | collective-permute-done | bytes 131104 | tf_op jit(solution)/shard_map/cells_2_chunk_3/ppermute | solution.py:367
  55.7 2.1 %standardize.7 = (bf16[1024,256]{1,0:T(8,128)(2,1)}, bf16[1024,1024]{1,0:T(8,128)(2,1)S(1)}, f32[8,128]{1,0:T(8,128)S(1)}, bf16[1024,1024]{1,0:T(8,128)(2,1)S(1)...) custom-call(f32[8,1024]{1,0:T(8,128)S(1)} %broadcast_in_dim.3.mean_r, ...), custom_call_target="tpu_custom_call", output_to_operand_aliasing={{1}: (11, {}), {3}: (12, {})} | custom-call | flops 20000000000 | bytes 1024 | tf_op jit(solution)/shard_map/standardize/pallas_call | solution.py:198
  57.8 0.1 collective-permute-start.16
  57.9 2.6 %gram.7.refs_2_ = bf16[1,1024,4096]{2,1,0:T(8,128)(2,1)} custom-call(f32[8,128]{1,0:T(8,128)S(1)} %get-tuple-element.92.count_ref, bf16[1024,1024]{1,0:T(8,128)(2,1)S(1)} %get-tuple-element.93.left_ref, bf16[1024,1024]{1,0:T(8,128)(2,1)S(1)} %get-tuple-element.95.refs_0_.refs_1_, ...), custom_call_target="tpu_custom_call", output_to_operand_aliasing={{}: (4, {})} | custom-call | flops 1024 | bytes 1024 | tf_op jit(solution)/shard_map/gram/pallas_call | solution.py:329
  60.5 0.6 collective-permute-start.17
  61.1 0.8 collective-permute-start.15
  61.9 0.0 collective-permute-done.18.refs_1_
  61.9 2.9 %gram.8.refs_3_ = bf16[1,1024,4096]{2,1,0:T(8,128)(2,1)} custom-call(f32[8,128]{1,0:T(8,128)S(1)} %get-tuple-element.92.count_ref, bf16[1024,1024]{1,0:T(8,128)(2,1)S(1)} %get-tuple-element.93.left_ref, bf16[1024,512]{1,0:T(8,128)(2,1)S(1)} %get-tuple-element.97.refs_0_, ...), custom_call_target="tpu_custom_call", output_to_operand_aliasing={{}: (4, {})} | custom-call | flops 20000000000 | bytes 1024 | tf_op jit(solution)/shard_map/gram/pallas_call | solution.py:329
  64.8 6.1 %gram.9.refs_1_ = bf16[1,1024,4096]{2,1,0:T(8,128)(2,1)} custom-call(f32[8,128]{1,0:T(8,128)S(1)} %get-tuple-element.92.count_ref, bf16[1024,1024]{1,0:T(8,128)(2,1)S(1)} %get-tuple-element.93.left_ref, bf16[1024,1024]{1,0:T(8,128)(2,1)S(1)} %collective-permute-done.16.refs_0_, ...), custom_call_target="tpu_custom_call", output_to_operand_aliasing={{}: (5, {})} | custom-call | flops 1024 | bytes 1024 | tf_op jit(solution)/shard_map/gram/pallas_call | solution.py:329
  70.9 1.5 %collective-permute-done.15.sent_ref = bf16[784,256]{1,0:T(8,128)(2,1)S(1)} collective-permute-done((bf16[784,256]{1,0:T(8,128)(2,1)S(1)}, bf16[784,256]{1,0:T(8,128)(2,1)S(1)}, u32[]{:S(2)}, u32[]{:S(2)}) %collective-permute-start.15) | collective-permute-done | bytes 401440 | tf_op jit(solution)/shard_map/ppermute | solution.py:370
  72.4 0.2 finish.1.refs_0_
  72.6 0.1 collective-permute-start.20
  72.7 1.5 %gram.10.refs_1_ = bf16[1,1024,4096]{2,1,0:T(8,128)(2,1)} custom-call(f32[8,128]{1,0:T(8,128)S(1)} %get-tuple-element.92.count_ref, bf16[1024,1024]{1,0:T(8,128)(2,1)S(1)} %get-tuple-element.93.left_ref, bf16[1024,256]{1,0:T(8,128)(2,1)S(1)} %finish.1.refs_0_, bf16[1,1024,4096]{2,1,0:T(8,128)(2,1)} %gram.9.refs_1_), custom_call_target="tpu_custom_call", output_to_operand_aliasing={{}: (3, {})} | custom-call | flops 1024 | bytes 1024 | tf_op jit(solution)/shard_map/gram/pallas_call | solution.py:329
  74.2 0.3 collective-permute-done.20.refs_0_
  74.6 1.5 %gram.11 = bf16[1,1024,4096]{2,1,0:T(8,128)(2,1)} custom-call(f32[8,128]{1,0:T(8,128)S(1)} %get-tuple-element.92.count_ref, bf16[1024,1024]{1,0:T(8,128)(2,1)S(1)} %get-tuple-element.93.left_ref, bf16[1024,256]{1,0:T(8,128)(2,1)S(1)} %collective-permute-done.20.refs_0_, bf16[1,1024,4096]{2,1,0:T(8,128)(2,1)} %gram.10.refs_1_), custom_call_target="tpu_custom_call", output_to_operand_aliasing={{}: (3, {})} | custom-call | flops 1024 | bytes 1024 | tf_op jit(solution)/shard_map/gram/pallas_call | solution.py:329
  (13 shorter events, 0.0 us)
Async XLA Ops:
  0.0 1.2 %copy-start = (bf16[512,1024]{1,0:T(8,128)(2,1)S(1)}, bf16[512,1024]{1,0:T(8,128)(2,1)}, u32[]{:S(2)}) copy-start(bf16[512,1024]{1,0:T(8,128)(2,1)} %expr_ref.1) | copy-start | bytes 3145732
  1.2 0.7 copy-start.1
  1.9 0.7 copy-start.2
  4.3 10.7 %collective-permute-start.5 = (bf16[272,256]{1,0:T(8,128)(2,1)S(1)}, bf16[272,256]{1,0:T(8,128)(2,1)S(1)}, u32[]{:S(2)}, u32[]{:S(2)}) collective-permute-start(bf16[272,256]{1,0:T(8,128)(2,1)S(1)} %get-tuple-element.65), channel_id=1, source_target_pairs={{0,12},{4,8},{8,4},{12,0},{1,13},{5,9},{9,5},{13,1},{2,14},{6,10},... | collective-permute-start | bytes 417800 | tf_op jit(solution)/shard_map/cells_3_chunk_0/ppermute | solution.py:367
  9.4 10.1 %collective-permute-start.3 = (bf16[272,256]{1,0:T(8,128)(2,1)S(1)}, bf16[272,256]{1,0:T(8,128)(2,1)S(1)}, u32[]{:S(2)}, u32[]{:S(2)}) collective-permute-start(bf16[272,256]{1,0:T(8,128)(2,1)S(1)} %get-tuple-element.62), channel_id=1, source_target_pairs={{0,4},{4,0},{8,12},{12,8},{1,5},{5,1},{9,13},{13,9},{2,6},{6,2},{1... | collective-permute-start | bytes 417800 | tf_op jit(solution)/shard_map/cells_1_chunk_0/ppermute | solution.py:367
  9.4 17.0 %collective-permute-start.1 = (bf16[272,256]{1,0:T(8,128)(2,1)S(1)}, bf16[272,256]{1,0:T(8,128)(2,1)S(1)}, u32[]{:S(2)}, u32[]{:S(2)}) collective-permute-start(bf16[272,256]{1,0:T(8,128)(2,1)S(1)} %get-tuple-element.59), channel_id=1, source_target_pairs={{0,8},{4,12},{8,0},{12,4},{1,9},{5,13},{9,1},{13,5},{2,10},{6,14},... | collective-permute-start | bytes 417800 | tf_op jit(solution)/shard_map/cells_2_chunk_0/ppermute | solution.py:367
  10.1 5.0 %collective-permute-start = (bf16[256,256]{1,0:T(8,128)(2,1)S(1)}, bf16[256,256]{1,0:T(8,128)(2,1)S(1)}, u32[]{:S(2)}, u32[]{:S(2)}) collective-permute-start(bf16[256,256]{1,0:T(8,128)(2,1)S(1)} %get-tuple-element.85.refs_0_), channel_id=1, source_target_pairs={{0,2},{1,3},{2,0},{3,1},{4,6},{5,7},{6,4},{7,5},{8,10},{9,11},{10,... | collective-permute-start | bytes 393224 | tf_op jit(solution)/shard_map/far_local/ppermute | solution.py:370
  15.7 14.1 %collective-permute-start.6 = (bf16[256,256]{1,0:T(8,128)(2,1)S(1)}, bf16[256,256]{1,0:T(8,128)(2,1)S(1)}, u32[]{:S(2)}, u32[]{:S(2)}) collective-permute-start(bf16[256,256]{1,0:T(8,128)(2,1)S(1)} %get-tuple-element.66), channel_id=1, source_target_pairs={{0,12},{4,8},{8,4},{12,0},{1,13},{5,9},{9,5},{13,1},{2,14},{6,10},... | collective-permute-start | bytes 393224 | tf_op jit(solution)/shard_map/cells_3_chunk_1/ppermute | solution.py:367
  19.5 11.8 %collective-permute-start.4 = (bf16[256,256]{1,0:T(8,128)(2,1)S(1)}, bf16[256,256]{1,0:T(8,128)(2,1)S(1)}, u32[]{:S(2)}, u32[]{:S(2)}) collective-permute-start(bf16[256,256]{1,0:T(8,128)(2,1)S(1)} %get-tuple-element.63), channel_id=1, source_target_pairs={{0,4},{4,0},{8,12},{12,8},{1,5},{5,1},{9,13},{13,9},{2,6},{6,2},{1... | collective-permute-start | bytes 393224 | tf_op jit(solution)/shard_map/cells_1_chunk_1/ppermute | solution.py:367
  26.4 8.8 %collective-permute-start.2 = (bf16[256,256]{1,0:T(8,128)(2,1)S(1)}, bf16[256,256]{1,0:T(8,128)(2,1)S(1)}, u32[]{:S(2)}, u32[]{:S(2)}) collective-permute-start(bf16[256,256]{1,0:T(8,128)(2,1)S(1)} %get-tuple-element.60), channel_id=1, source_target_pairs={{0,8},{4,12},{8,0},{12,4},{1,9},{5,13},{9,1},{13,5},{2,10},{6,14},... | collective-permute-start | bytes 393224 | tf_op jit(solution)/shard_map/cells_2_chunk_1/ppermute | solution.py:367
  28.2 20.8 %collective-permute-start.8 = (bf16[1024,256]{1,0:T(8,128)(2,1)S(1)}, bf16[1024,256]{1,0:T(8,128)(2,1)S(1)}, u32[]{:S(2)}, u32[]{:S(2)}) collective-permute-start(bf16[1024,256]{1,0:T(8,128)(2,1)S(1)} %get-tuple-element.72), channel_id=1, source_target_pairs={{0,2},{1,3},{2,0},{3,1},{4,6},{5,7},{6,4},{7,5},{8,10},{9,11},{10,... | collective-permute-start | bytes 1572872 | tf_op jit(solution)/shard_map/far_0/ppermute | solution.py:370
  29.8 9.8 %collective-permute-start.11 = (bf16[256,256]{1,0:T(8,128)(2,1)S(1)}, bf16[256,256]{1,0:T(8,128)(2,1)S(1)}, u32[]{:S(2)}, u32[]{:S(2)}) collective-permute-start(bf16[256,256]{1,0:T(8,128)(2,1)S(1)} %get-tuple-element.79), channel_id=1, source_target_pairs={{0,12},{4,8},{8,4},{12,0},{1,13},{5,9},{9,5},{13,1},{2,14},{6,10},... | collective-permute-start | bytes 393224 | tf_op jit(solution)/shard_map/cells_3_chunk_2/ppermute | solution.py:367
  31.3 12.1 %collective-permute-start.10 = (bf16[256,256]{1,0:T(8,128)(2,1)S(1)}, bf16[256,256]{1,0:T(8,128)(2,1)S(1)}, u32[]{:S(2)}, u32[]{:S(2)}) collective-permute-start(bf16[256,256]{1,0:T(8,128)(2,1)S(1)} %get-tuple-element.77), channel_id=1, source_target_pairs={{0,4},{4,0},{8,12},{12,8},{1,5},{5,1},{9,13},{13,9},{2,6},{6,2},{1... | collective-permute-start | bytes 393224 | tf_op jit(solution)/shard_map/cells_1_chunk_2/ppermute | solution.py:367
  35.2 13.8 %collective-permute-start.9 = (bf16[256,256]{1,0:T(8,128)(2,1)S(1)}, bf16[256,256]{1,0:T(8,128)(2,1)S(1)}, u32[]{:S(2)}, u32[]{:S(2)}) collective-permute-start(bf16[256,256]{1,0:T(8,128)(2,1)S(1)} %get-tuple-element.75), channel_id=1, source_target_pairs={{0,8},{4,12},{8,0},{12,4},{1,9},{5,13},{9,1},{13,5},{2,10},{6,14},... | collective-permute-start | bytes 393224 | tf_op jit(solution)/shard_map/cells_2_chunk_2/ppermute | solution.py:367
  37.0 15.5 %collective-permute-start.7 = (bf16[1024,256]{1,0:T(8,128)(2,1)S(1)}, bf16[1024,256]{1,0:T(8,128)(2,1)S(1)}, u32[]{:S(2)}, u32[]{:S(2)}) collective-permute-start(bf16[1024,256]{1,0:T(8,128)(2,1)S(1)} %get-tuple-element.69), channel_id=1, source_target_pairs={{0,2},{1,3},{2,0},{3,1},{4,6},{5,7},{6,4},{7,5},{8,10},{9,11},{10,... | collective-permute-start | bytes 1572872 | tf_op jit(solution)/shard_map/far_1/ppermute | solution.py:370
  39.6 12.9 %collective-permute-start.14 = (bf16[256,256]{1,0:T(8,128)(2,1)S(1)}, bf16[256,256]{1,0:T(8,128)(2,1)S(1)}, u32[]{:S(2)}, u32[]{:S(2)}) collective-permute-start(bf16[256,256]{1,0:T(8,128)(2,1)S(1)} %get-tuple-element.91), channel_id=1, source_target_pairs={{0,12},{4,8},{8,4},{12,0},{1,13},{5,9},{9,5},{13,1},{2,14},{6,10},... | collective-permute-start | bytes 393224 | tf_op jit(solution)/shard_map/cells_3_chunk_3/ppermute | solution.py:367
  43.4 9.1 %collective-permute-start.13 = (bf16[256,256]{1,0:T(8,128)(2,1)S(1)}, bf16[256,256]{1,0:T(8,128)(2,1)S(1)}, u32[]{:S(2)}, u32[]{:S(2)}) collective-permute-start(bf16[256,256]{1,0:T(8,128)(2,1)S(1)} %get-tuple-element.89), channel_id=1, source_target_pairs={{0,4},{4,0},{8,12},{12,8},{1,5},{5,1},{9,13},{13,9},{2,6},{6,2},{1... | collective-permute-start | bytes 393224 | tf_op jit(solution)/shard_map/cells_1_chunk_3/ppermute | solution.py:367
  49.0 6.7 %collective-permute-start.12 = (bf16[256,256]{1,0:T(8,128)(2,1)S(1)}, bf16[256,256]{1,0:T(8,128)(2,1)S(1)}, u32[]{:S(2)}, u32[]{:S(2)}) collective-permute-start(bf16[256,256]{1,0:T(8,128)(2,1)S(1)} %get-tuple-element.87), channel_id=1, source_target_pairs={{0,8},{4,12},{8,0},{12,4},{1,9},{5,13},{9,1},{13,5},{2,10},{6,14},... | collective-permute-start | bytes 393224 | tf_op jit(solution)/shard_map/cells_2_chunk_3/ppermute | solution.py:367
  50.2 11.7 %collective-permute-start.18 = (bf16[1024,256]{1,0:T(8,128)(2,1)S(1)}, bf16[1024,256]{1,0:T(8,128)(2,1)S(1)}, u32[]{:S(2)}, u32[]{:S(2)}) collective-permute-start(bf16[1024,256]{1,0:T(8,128)(2,1)S(1)} %get-tuple-element.98), channel_id=1, source_target_pairs={{0,2},{1,3},{2,0},{3,1},{4,6},{5,7},{6,4},{7,5},{8,10},{9,11},{10,... | collective-permute-start | bytes 1572872 | tf_op jit(solution)/shard_map/far_2/ppermute | solution.py:370
  57.8 6.9 %collective-permute-start.16 = (bf16[1024,1024]{1,0:T(8,128)(2,1)S(1)}, bf16[1024,1024]{1,0:T(8,128)(2,1)S(1)}, u32[]{:S(2)}, u32[]{:S(2)}) collective-permute-start(bf16[1024,1024]{1,0:T(8,128)(2,1)S(1)} %get-tuple-element.95.refs_0_.refs_1_), channel_id=1, source_target_pairs={{0,1},{1,0},{2,3},{3,2},{4,5},{5,4},{6,7},{7,6},{8,9},{9,8},{10,11... | collective-permute-start | bytes 6291464 | tf_op jit(solution)/shard_map/near/ppermute | solution.py:374
  60.5 4.2 %collective-permute-start.17 = (bf16[1024,512]{1,0:T(8,128)(2,1)S(1)}, bf16[1024,512]{1,0:T(8,128)(2,1)S(1)}, u32[]{:S(2)}, u32[]{:S(2)}) collective-permute-start(bf16[1024,512]{1,0:T(8,128)(2,1)S(1)} %get-tuple-element.97.refs_0_), channel_id=1, source_target_pairs={{0,1},{1,0},{2,3},{3,2},{4,5},{5,4},{6,7},{7,6},{8,9},{9,8},{10,11... | collective-permute-start | bytes 3145736 | tf_op jit(solution)/shard_map/far_near/ppermute | solution.py:374
  61.1 11.3 %collective-permute-start.15 = (bf16[784,256]{1,0:T(8,128)(2,1)S(1)}, bf16[784,256]{1,0:T(8,128)(2,1)S(1)}, u32[]{:S(2)}, u32[]{:S(2)}) collective-permute-start(bf16[784,256]{1,0:T(8,128)(2,1)S(1)} %get-tuple-element.96), channel_id=1, source_target_pairs={{0,2},{1,3},{2,0},{3,1},{4,6},{5,7},{6,4},{7,5},{8,10},{9,11},{10,... | collective-permute-start | bytes 1204232 | tf_op jit(solution)/shard_map/ppermute | solution.py:370
  61.9 2.9 %collective-permute-start.19 = (bf16[1024,256]{1,0:T(8,128)(2,1)S(1)}, bf16[1024,256]{1,0:T(8,128)(2,1)S(1)}, u32[]{:S(2)}, u32[]{:S(2)}) collective-permute-start(bf16[1024,256]{1,0:T(8,128)(2,1)S(1)} %collective-permute-done.18.refs_1_), channel_id=1, source_target_pairs={{0,1},{1,0},{2,3},{3,2},{4,5},{5,4},{6,7},{7,6},{8,9},{9,8},{10,11... | collective-permute-start | bytes 1572872 | tf_op jit(solution)/shard_map/far_near_2/ppermute | solution.py:374
  72.6 2.0 %collective-permute-start.20 = (bf16[1024,256]{1,0:T(8,128)(2,1)S(1)}, bf16[1024,256]{1,0:T(8,128)(2,1)S(1)}, u32[]{:S(2)}, u32[]{:S(2)}) collective-permute-start(bf16[1024,256]{1,0:T(8,128)(2,1)S(1)} %finish.1.refs_0_), channel_id=1, source_target_pairs={{0,1},{1,0},{2,3},{3,2},{4,5},{5,4},{6,7},{7,6},{8,9},{9,8},{10,11... | collective-permute-start | bytes 1572872 | tf_op jit(solution)/shard_map/far_near_3/ppermute | solution.py:374

commit v19 on v18

--- a/solution.py
+++ b/solution.py
@@ -149,6 +149,12 @@
         scaled_ref[j * cap : (j + 1) * cap, :] = scaled.astype(jnp.bfloat16)
         work[j * cap : (j + 1) * cap, :] = scaled
     slots = types * cap
+    columns = pl.ds(start, width)
+    copies.append(pltpu.make_async_copy(scaled_ref, all_ref.at[:, columns], sems.at[0]))
+    copies[-1].start()
+    turned[...] = jnp.transpose(work[...]).astype(jnp.bfloat16)
+    copies.append(pltpu.make_async_copy(turned, turned_ref.at[columns, :], sems.at[1]))
+    copies[-1].start()
     if late:
         sent_ref = joined_refs[-1]
         sent_ref[0 : slots - cap, :] = scaled_ref[cap:slots, :]
@@ -157,12 +163,6 @@
         for i, part in enumerate(thirds(center) + thirds(scale) + thirds(mean)):
             notes = jnp.where(row == i, part, notes)
         sent_ref[slots - cap : slots - cap + TILE, :] = notes.astype(jnp.bfloat16)
-    columns = pl.ds(start, width)
-    copies.append(pltpu.make_async_copy(scaled_ref, all_ref.at[:, columns], sems.at[0]))
-    copies[-1].start()
-    turned[...] = jnp.transpose(work[...]).astype(jnp.bfloat16)
-    copies.append(pltpu.make_async_copy(turned, turned_ref.at[columns, :], sems.at[1]))
-    copies[-1].start()
     for copy in copies:
         copy.wait()
     count_ref[...] = jnp.broadcast_to(count, count_ref.shape)

time: 76.5 us -> 76.5 us (level)
  no operation moved by 1% of the time
where the time goes in v19:
time: 76.5 us; the launch traced here: 76.3 us
  starting transfers between devices  27 us (35%)
  Pallas kernels  25.7 us (34%)
  waiting for transfers between devices  19.9 us (26%)
  local copies, waits for them, and re-layouts  3.27 us (4%)
    ppermute x12, starting transfers between devices, swap(): return lax.ppermute(block, 'cells', [(s, s ^ by) for s in range(types)])  19.6 us
    pallas_call x6, Pallas kernels, gram(): pl.pallas_call(functools.partial(gram_kernel, blocks, cores, strip, layou...  16.9 us
    ppermute x12, waiting for transfers between devices, swap(): return lax.ppermute(block, 'cells', [(s, s ^ by) for s in range(types)])  14.7 us
    pallas_call x4, Pallas kernels, standardize(): pl.pallas_call(functools.partial(standardize_kernel, types, cap, lead, se...  6.95 us
    ppermute x5, starting transfers between devices, across(): lax.ppermute(panel_, 'blk', [(b, (b + by * cores) % blocks) for b in rang...  6.66 us
    ppermute x5, waiting for transfers between devices, across(): lax.ppermute(panel_, 'blk', [(b, (b + by * cores) % blocks) for b in rang...  4.84 us
    unnamed x6, local copies, waits for them, and re-layouts  2.58 us
    pallas_call x1, Pallas kernels, pack(): pl.pallas_call(functools.partial(pack_kernel, types, cap, widths), out_sh...  1.71 us
  transfers between devices with their start and end apart: 21, of which 7 were waited for; matrix products, arithmetic and copies ran while one was open for 1% of the time, Pallas kernels for 29%

profile of v19, /device:TPU:0, one launch (start us, length us, event | category | flops | bytes accessed | tf_op | source)
XLA Modules:
  0.0 76.3 jit_solution(7871181926024792123)
XLA Ops:
  0.0 1.2 %copy-done = bf16[512,1024]{1,0:T(8,128)(2,1)S(1)} copy-done((bf16[512,1024]{1,0:T(8,128)(2,1)S(1)}, bf16[512,1024]{1,0:T(8,128)(2,1)}, u32[]{:S(2)}) %copy-start) | copy-done | bytes 1048600
  1.2 0.7 copy-done.1
  1.9 0.7 copy-done.2
  2.6 1.7 %pack.1 = (bf16[272,256]{1,0:T(8,128)(2,1)S(1)}, bf16[272,256]{1,0:T(8,128)(2,1)S(1)}, bf16[272,256]{1,0:T(8,128)(2,1)S(1)}, bf16[272,256]{1,0:T(8,128)(2,1)S(1)...) custom-call(s32[512]{0:T(512)S(1)} %copy-done.1, ...), custom_call_target="tpu_custom_call" | custom-call | flops 1024 | bytes 1024 | tf_op jit(solution)/shard_map/pack/pallas_call | solution.py:68
  4.3 5.1 %collective-permute-start.5 = (bf16[272,256]{1,0:T(8,128)(2,1)S(1)}, bf16[272,256]{1,0:T(8,128)(2,1)S(1)}, u32[]{:S(2)}, u32[]{:S(2)}) collective-permute-start(bf16[272,256]{1,0:T(8,128)(2,1)S(1)} %get-tuple-element.65), channel_id=1, source_target_pairs={{0,12},{4,8},{8,4},{12,0},{1,13},{5,9},{9,5},{13,1},{2,14},{6,10},... | collective-permute-start | bytes 417800 | tf_op jit(solution)/shard_map/cells_3_chunk_0/ppermute | solution.py:367
  9.4 0.0 collective-permute-start.3
  9.4 0.6 collective-permute-start.1
  10.1 1.6 %collective-permute-start = (bf16[256,256]{1,0:T(8,128)(2,1)S(1)}, bf16[256,256]{1,0:T(8,128)(2,1)S(1)}, u32[]{:S(2)}, u32[]{:S(2)}) collective-permute-start(bf16[256,256]{1,0:T(8,128)(2,1)S(1)} %get-tuple-element.85.refs_0_), channel_id=1, source_target_pairs={{0,2},{1,3},{2,0},{3,1},{4,6},{5,7},{6,4},{7,5},{8,10},{9,11},{10,... | collective-permute-start | bytes 393224 | tf_op jit(solution)/shard_map/far_local/ppermute | solution.py:370
  11.7 3.3 %collective-permute-done.local_ref = bf16[256,256]{1,0:T(8,128)(2,1)S(1)} collective-permute-done((bf16[256,256]{1,0:T(8,128)(2,1)S(1)}, bf16[256,256]{1,0:T(8,128)(2,1)S(1)}, u32[]{:S(2)}, u32[]{:S(2)}) %collective-permute-start) | collective-permute-done | bytes 131104 | tf_op jit(solution)/shard_map/far_local/ppermute | solution.py:370
  15.0 0.0 collective-permute-done.5.refs_3_.refs_7_
  15.0 0.7 broadcast_in_dim.3.mean_ref
  15.7 3.7 %collective-permute-start.6 = (bf16[256,256]{1,0:T(8,128)(2,1)S(1)}, bf16[256,256]{1,0:T(8,128)(2,1)S(1)}, u32[]{:S(2)}, u32[]{:S(2)}) collective-permute-start(bf16[256,256]{1,0:T(8,128)(2,1)S(1)} %get-tuple-element.66), channel_id=1, source_target_pairs={{0,12},{4,8},{8,4},{12,0},{1,13},{5,9},{9,5},{13,1},{2,14},{6,10},... | collective-permute-start | bytes 393224 | tf_op jit(solution)/shard_map/cells_3_chunk_1/ppermute | solution.py:367
  19.5 0.0 collective-permute-done.3.refs_2_.refs_6_
  19.5 6.9 %collective-permute-done.1.refs_1_.refs_5_ = bf16[272,256]{1,0:T(8,128)(2,1)S(1)} collective-permute-done((bf16[272,256]{1,0:T(8,128)(2,1)S(1)}, bf16[272,256]{1,0:T(8,128)(2,1)S(1)}, u32[]{:S(2)}, u32[]{:S(2)}) %collective-permute-start.1) | collective-permute-done | bytes 139296 | tf_op jit(solution)/shard_map/cells_2_chunk_0/ppermute | solution.py:367
  26.4 0.0 collective-permute-start.2
  26.4 1.8 %standardize.4 = (bf16[1024,256]{1,0:T(8,128)(2,1)S(1)}, bf16[1024,1024]{1,0:T(8,128)(2,1)S(1)}, f32[8,128]{1,0:T(8,128)}, bf16[1024,1024]{1,0:T(8,128)(2,1)S(1)}) custom-call(f32[8,1024]{1,0:T(8,128)S(1)} %broadcast_in_dim.3.mean_ref, bf16[272,256]{1,0:T(8,128)(2,1)S(1)} %get-tuple-element.53.refs_0_.refs_4_.tail_ref, ...), custom_call_target="tpu_custom_call" | custom-call | flops 20000000000 | bytes 1024 | tf_op jit(solution)/shard_map/standardize/pallas_call | solution.py:198
  28.2 1.6 %collective-permute-start.8 = (bf16[1024,256]{1,0:T(8,128)(2,1)S(1)}, bf16[1024,256]{1,0:T(8,128)(2,1)S(1)}, u32[]{:S(2)}, u32[]{:S(2)}) collective-permute-start(bf16[1024,256]{1,0:T(8,128)(2,1)S(1)} %get-tuple-element.72), channel_id=1, source_target_pairs={{0,2},{1,3},{2,0},{3,1},{4,6},{5,7},{6,4},{7,5},{8,10},{9,11},{10,... | collective-permute-start | bytes 1572872 | tf_op jit(solution)/shard_map/far_0/ppermute | solution.py:370
  29.8 0.0 collective-permute-done.6.refs_3_
  29.8 1.5 %collective-permute-start.11 = (bf16[256,256]{1,0:T(8,128)(2,1)S(1)}, bf16[256,256]{1,0:T(8,128)(2,1)S(1)}, u32[]{:S(2)}, u32[]{:S(2)}) collective-permute-start(bf16[256,256]{1,0:T(8,128)(2,1)S(1)} %get-tuple-element.79), channel_id=1, source_target_pairs={{0,12},{4,8},{8,4},{12,0},{1,13},{5,9},{9,5},{13,1},{2,14},{6,10},... | collective-permute-start | bytes 393224 | tf_op jit(solution)/shard_map/cells_3_chunk_2/ppermute | solution.py:367
  31.3 2.8 %collective-permute-start.10 = (bf16[256,256]{1,0:T(8,128)(2,1)S(1)}, bf16[256,256]{1,0:T(8,128)(2,1)S(1)}, u32[]{:S(2)}, u32[]{:S(2)}) collective-permute-start(bf16[256,256]{1,0:T(8,128)(2,1)S(1)} %get-tuple-element.77), channel_id=1, source_target_pairs={{0,4},{4,0},{8,12},{12,8},{1,5},{5,1},{9,13},{13,9},{2,6},{6,2},{1... | collective-permute-start | bytes 393224 | tf_op jit(solution)/shard_map/cells_1_chunk_2/ppermute | solution.py:367
  34.1 1.0 %collective-permute-done.2.refs_1_ = bf16[256,256]{1,0:T(8,128)(2,1)S(1)} collective-permute-done((bf16[256,256]{1,0:T(8,128)(2,1)S(1)}, bf16[256,256]{1,0:T(8,128)(2,1)S(1)}, u32[]{:S(2)}, u32[]{:S(2)}) %collective-permute-start.2) | collective-permute-done | bytes 131104 | tf_op jit(solution)/shard_map/cells_2_chunk_1/ppermute | solution.py:367
  35.2 1.8 %standardize.5 = (bf16[1024,256]{1,0:T(8,128)(2,1)S(1)}, bf16[1024,1024]{1,0:T(8,128)(2,1)S(1)}, f32[8,128]{1,0:T(8,128)}, bf16[1024,1024]{1,0:T(8,128)(2,1)S(1)}) custom-call(f32[8,1024]{1,0:T(8,128)S(1)} %broadcast_in_dim.3.mean_ref, bf16[256,256]{1,0:T(8,128)(2,1)S(1)} %get-tuple-element.57.refs_0_, ...), custom_call_target="tpu_custom_call", output_to_operand_aliasing={{1}: (9, {}), {3}: (10, {})} | custom-call | flops 20000000000 | bytes 1024 | tf_op jit(solution)/shard_map/standardize/pallas_call | solution.py:198
  37.0 2.6 %collective-permute-start.7 = (bf16[1024,256]{1,0:T(8,128)(2,1)S(1)}, bf16[1024,256]{1,0:T(8,128)(2,1)S(1)}, u32[]{:S(2)}, u32[]{:S(2)}) collective-permute-start(bf16[1024,256]{1,0:T(8,128)(2,1)S(1)} %get-tuple-element.69), channel_id=1, source_target_pairs={{0,2},{1,3},{2,0},{3,1},{4,6},{5,7},{6,4},{7,5},{8,10},{9,11},{10,... | collective-permute-start | bytes 1572872 | tf_op jit(solution)/shard_map/far_1/ppermute | solution.py:370
  39.6 3.8 %collective-permute-start.14 = (bf16[256,256]{1,0:T(8,128)(2,1)S(1)}, bf16[256,256]{1,0:T(8,128)(2,1)S(1)}, u32[]{:S(2)}, u32[]{:S(2)}) collective-permute-start(bf16[256,256]{1,0:T(8,128)(2,1)S(1)} %get-tuple-element.91), channel_id=1, source_target_pairs={{0,12},{4,8},{8,4},{12,0},{1,13},{5,9},{9,5},{13,1},{2,14},{6,10},... | collective-permute-start | bytes 393224 | tf_op jit(solution)/shard_map/cells_3_chunk_3/ppermute | solution.py:367
  43.4 1.9 %collective-permute-start.13 = (bf16[256,256]{1,0:T(8,128)(2,1)S(1)}, bf16[256,256]{1,0:T(8,128)(2,1)S(1)}, u32[]{:S(2)}, u32[]{:S(2)}) collective-permute-start(bf16[256,256]{1,0:T(8,128)(2,1)S(1)} %get-tuple-element.89), channel_id=1, source_target_pairs={{0,4},{4,0},{8,12},{12,8},{1,5},{5,1},{9,13},{13,9},{2,6},{6,2},{1... | collective-permute-start | bytes 393224 | tf_op jit(solution)/shard_map/cells_1_chunk_3/ppermute | solution.py:367
  45.4 3.6 %collective-permute-done.9.refs_1_ = bf16[256,256]{1,0:T(8,128)(2,1)S(1)} collective-permute-done((bf16[256,256]{1,0:T(8,128)(2,1)S(1)}, bf16[256,256]{1,0:T(8,128)(2,1)S(1)}, u32[]{:S(2)}, u32[]{:S(2)}) %collective-permute-start.9) | collective-permute-done | bytes 131104 | tf_op jit(solution)/shard_map/cells_2_chunk_2/ppermute | solution.py:367
  49.0 0.0 collective-permute-start.12
  49.0 0.0 collective-permute-done.8.refs_8_
  49.0 1.2 %standardize.6 = (bf16[1024,256]{1,0:T(8,128)(2,1)S(1)}, bf16[1024,1024]{1,0:T(8,128)(2,1)S(1)}, f32[8,128]{1,0:T(8,128)S(1)}, bf16[1024,1024]{1,0:T(8,128)(2,1)S(1)}) custom-call(f32[8,1024]{1,0:T(8,128)S(1)} %broadcast_in_dim.3.mean_ref, bf16[256,256]{1,0:T(8,128)(2,1)S(1)} %get-tuple-element.73.refs_0_, ...), custom_call_target="tpu_custom_call", output_to_operand_aliasing={{1}: (9, {}), {3}: (10, {})} | custom-call | flops 20000000000 | bytes 1024 | tf_op jit(solution)/shard_map/standardize/pallas_call | solution.py:198
  50.2 0.1 collective-permute-start.18
  50.3 2.2 %gram.6.refs_2_ = bf16[1,1024,4096]{2,1,0:T(8,128)(2,1)} custom-call(f32[8,128]{1,0:T(8,128)S(1)} %get-tuple-element.82.count_ref, bf16[1024,1024]{1,0:T(8,128)(2,1)S(1)} %get-tuple-element.83.left_ref.refs_10_, bf16[1024,1024]{1,0:T(8,128)(2,1)S(1)} %get-tuple-element.84.refs_0_.refs_11_), custom_call_target="tpu_custom_call" | custom-call | flops 1024 | bytes 1024 | tf_op jit(solution)/shard_map/gram/pallas_call | solution.py:329
  52.5 0.0 collective-permute-done.13.refs_2_
  52.5 3.1 %collective-permute-done.12.refs_1_ = bf16[256,256]{1,0:T(8,128)(2,1)S(1)} collective-permute-done((bf16[256,256]{1,0:T(8,128)(2,1)S(1)}, bf16[256,256]{1,0:T(8,128)(2,1)S(1)}, u32[]{:S(2)}, u32[]{:S(2)}) %collective-permute-start.12) | collective-permute-done | bytes 131104 | tf_op jit(solution)/shard_map/cells_2_chunk_3/ppermute | solution.py:367
  55.7 2.1 %standardize.7 = (bf16[1024,256]{1,0:T(8,128)(2,1)}, bf16[1024,1024]{1,0:T(8,128)(2,1)S(1)}, f32[8,128]{1,0:T(8,128)S(1)}, bf16[1024,1024]{1,0:T(8,128)(2,1)S(1)...) custom-call(f32[8,1024]{1,0:T(8,128)S(1)} %broadcast_in_dim.3.mean_r, ...), custom_call_target="tpu_custom_call", output_to_operand_aliasing={{1}: (11, {}), {3}: (12, {})} | custom-call | flops 20000000000 | bytes 1024 | tf_op jit(solution)/shard_map/standardize/pallas_call | solution.py:198
  57.8 0.1 collective-permute-start.16
  57.9 2.6 %gram.7.refs_2_ = bf16[1,1024,4096]{2,1,0:T(8,128)(2,1)} custom-call(f32[8,128]{1,0:T(8,128)S(1)} %get-tuple-element.92.count_ref, bf16[1024,1024]{1,0:T(8,128)(2,1)S(1)} %get-tuple-element.93.left_ref, bf16[1024,1024]{1,0:T(8,128)(2,1)S(1)} %get-tuple-element.95.refs_0_.refs_1_, ...), custom_call_target="tpu_custom_call", output_to_operand_aliasing={{}: (4, {})} | custom-call | flops 1024 | bytes 1024 | tf_op jit(solution)/shard_map/gram/pallas_call | solution.py:329
  60.5 0.6 collective-permute-start.17
  61.1 0.8 %collective-permute-start.15 = (bf16[784,256]{1,0:T(8,128)(2,1)S(1)}, bf16[784,256]{1,0:T(8,128)(2,1)S(1)}, u32[]{:S(2)}, u32[]{:S(2)}) collective-permute-start(bf16[784,256]{1,0:T(8,128)(2,1)S(1)} %get-tuple-element.96), channel_id=1, source_target_pairs={{0,2},{1,3},{2,0},{3,1},{4,6},{5,7},{6,4},{7,5},{8,10},{9,11},{10,... | collective-permute-start | bytes 1204232 | tf_op jit(solution)/shard_map/ppermute | solution.py:370
  61.9 0.0 collective-permute-start.19
  61.9 2.9 %gram.8.refs_3_ = bf16[1,1024,4096]{2,1,0:T(8,128)(2,1)} custom-call(f32[8,128]{1,0:T(8,128)S(1)} %get-tuple-element.92.count_ref, bf16[1024,1024]{1,0:T(8,128)(2,1)S(1)} %get-tuple-element.93.left_ref, bf16[1024,512]{1,0:T(8,128)(2,1)S(1)} %get-tuple-element.97.refs_0_, ...), custom_call_target="tpu_custom_call", output_to_operand_aliasing={{}: (4, {})} | custom-call | flops 20000000000 | bytes 1024 | tf_op jit(solution)/shard_map/gram/pallas_call | solution.py:329
  64.8 0.0 collective-permute-done.16.refs_0_
  64.8 6.1 %gram.9.refs_1_ = bf16[1,1024,4096]{2,1,0:T(8,128)(2,1)} custom-call(f32[8,128]{1,0:T(8,128)S(1)} %get-tuple-element.92.count_ref, bf16[1024,1024]{1,0:T(8,128)(2,1)S(1)} %get-tuple-element.93.left_ref, bf16[1024,1024]{1,0:T(8,128)(2,1)S(1)} %collective-permute-done.16.refs_0_, ...), custom_call_target="tpu_custom_call", output_to_operand_aliasing={{}: (5, {})} | custom-call | flops 1024 | bytes 1024 | tf_op jit(solution)/shard_map/gram/pallas_call | solution.py:329
  70.9 1.5 %collective-permute-done.15.sent_ref = bf16[784,256]{1,0:T(8,128)(2,1)S(1)} collective-permute-done((bf16[784,256]{1,0:T(8,128)(2,1)S(1)}, bf16[784,256]{1,0:T(8,128)(2,1)S(1)}, u32[]{:S(2)}, u32[]{:S(2)}) %collective-permute-start.15) | collective-permute-done | bytes 401440 | tf_op jit(solution)/shard_map/ppermute | solution.py:370
  72.4 0.2 finish.1.refs_0_
  72.6 0.1 collective-permute-start.20
  72.7 1.5 %gram.10.refs_1_ = bf16[1,1024,4096]{2,1,0:T(8,128)(2,1)} custom-call(f32[8,128]{1,0:T(8,128)S(1)} %get-tuple-element.92.count_ref, bf16[1024,1024]{1,0:T(8,128)(2,1)S(1)} %get-tuple-element.93.left_ref, bf16[1024,256]{1,0:T(8,128)(2,1)S(1)} %finish.1.refs_0_, bf16[1,1024,4096]{2,1,0:T(8,128)(2,1)} %gram.9.refs_1_), custom_call_target="tpu_custom_call", output_to_operand_aliasing={{}: (3, {})} | custom-call | flops 1024 | bytes 1024 | tf_op jit(solution)/shard_map/gram/pallas_call | solution.py:329
  74.2 0.3 collective-permute-done.20.refs_0_
  74.6 1.5 %gram.11 = bf16[1,1024,4096]{2,1,0:T(8,128)(2,1)} custom-call(f32[8,128]{1,0:T(8,128)S(1)} %get-tuple-element.92.count_ref, bf16[1024,1024]{1,0:T(8,128)(2,1)S(1)} %get-tuple-element.93.left_ref, bf16[1024,256]{1,0:T(8,128)(2,1)S(1)} %collective-permute-done.20.refs_0_, bf16[1,1024,4096]{2,1,0:T(8,128)(2,1)} %gram.10.refs_1_), custom_call_target="tpu_custom_call", output_to_operand_aliasing={{}: (3, {})} | custom-call | flops 1024 | bytes 1024 | tf_op jit(solution)/shard_map/gram/pallas_call | solution.py:329
  (13 shorter events, 0.0 us)
Async XLA Ops:
  0.0 1.2 %copy-start = (bf16[512,1024]{1,0:T(8,128)(2,1)S(1)}, bf16[512,1024]{1,0:T(8,128)(2,1)}, u32[]{:S(2)}) copy-start(bf16[512,1024]{1,0:T(8,128)(2,1)} %expr_ref.1) | copy-start | bytes 3145732
  1.2 0.7 copy-start.1
  1.9 0.7 copy-start.2
  4.3 10.7 %collective-permute-start.5 = (bf16[272,256]{1,0:T(8,128)(2,1)S(1)}, bf16[272,256]{1,0:T(8,128)(2,1)S(1)}, u32[]{:S(2)}, u32[]{:S(2)}) collective-permute-start(bf16[272,256]{1,0:T(8,128)(2,1)S(1)} %get-tuple-element.65), channel_id=1, source_target_pairs={{0,12},{4,8},{8,4},{12,0},{1,13},{5,9},{9,5},{13,1},{2,14},{6,10},... | collective-permute-start | bytes 417800 | tf_op jit(solution)/shard_map/cells_3_chunk_0/ppermute | solution.py:367
  9.4 10.1 %collective-permute-start.3 = (bf16[272,256]{1,0:T(8,128)(2,1)S(1)}, bf16[272,256]{1,0:T(8,128)(2,1)S(1)}, u32[]{:S(2)}, u32[]{:S(2)}) collective-permute-start(bf16[272,256]{1,0:T(8,128)(2,1)S(1)} %get-tuple-element.62), channel_id=1, source_target_pairs={{0,4},{4,0},{8,12},{12,8},{1,5},{5,1},{9,13},{13,9},{2,6},{6,2},{1... | collective-permute-start | bytes 417800 | tf_op jit(solution)/shard_map/cells_1_chunk_0/ppermute | solution.py:367
  9.4 17.0 %collective-permute-start.1 = (bf16[272,256]{1,0:T(8,128)(2,1)S(1)}, bf16[272,256]{1,0:T(8,128)(2,1)S(1)}, u32[]{:S(2)}, u32[]{:S(2)}) collective-permute-start(bf16[272,256]{1,0:T(8,128)(2,1)S(1)} %get-tuple-element.59), channel_id=1, source_target_pairs={{0,8},{4,12},{8,0},{12,4},{1,9},{5,13},{9,1},{13,5},{2,10},{6,14},... | collective-permute-start | bytes 417800 | tf_op jit(solution)/shard_map/cells_2_chunk_0/ppermute | solution.py:367
  10.1 5.0 %collective-permute-start = (bf16[256,256]{1,0:T(8,128)(2,1)S(1)}, bf16[256,256]{1,0:T(8,128)(2,1)S(1)}, u32[]{:S(2)}, u32[]{:S(2)}) collective-permute-start(bf16[256,256]{1,0:T(8,128)(2,1)S(1)} %get-tuple-element.85.refs_0_), channel_id=1, source_target_pairs={{0,2},{1,3},{2,0},{3,1},{4,6},{5,7},{6,4},{7,5},{8,10},{9,11},{10,... | collective-permute-start | bytes 393224 | tf_op jit(solution)/shard_map/far_local/ppermute | solution.py:370
  15.7 14.1 %collective-permute-start.6 = (bf16[256,256]{1,0:T(8,128)(2,1)S(1)}, bf16[256,256]{1,0:T(8,128)(2,1)S(1)}, u32[]{:S(2)}, u32[]{:S(2)}) collective-permute-start(bf16[256,256]{1,0:T(8,128)(2,1)S(1)} %get-tuple-element.66), channel_id=1, source_target_pairs={{0,12},{4,8},{8,4},{12,0},{1,13},{5,9},{9,5},{13,1},{2,14},{6,10},... | collective-permute-start | bytes 393224 | tf_op jit(solution)/shard_map/cells_3_chunk_1/ppermute | solution.py:367
  19.5 11.8 %collective-permute-start.4 = (bf16[256,256]{1,0:T(8,128)(2,1)S(1)}, bf16[256,256]{1,0:T(8,128)(2,1)S(1)}, u32[]{:S(2)}, u32[]{:S(2)}) collective-permute-start(bf16[256,256]{1,0:T(8,128)(2,1)S(1)} %get-tuple-element.63), channel_id=1, source_target_pairs={{0,4},{4,0},{8,12},{12,8},{1,5},{5,1},{9,13},{13,9},{2,6},{6,2},{1... | collective-permute-start | bytes 393224 | tf_op jit(solution)/shard_map/cells_1_chunk_1/ppermute | solution.py:367
  26.4 8.8 %collective-permute-start.2 = (bf16[256,256]{1,0:T(8,128)(2,1)S(1)}, bf16[256,256]{1,0:T(8,128)(2,1)S(1)}, u32[]{:S(2)}, u32[]{:S(2)}) collective-permute-start(bf16[256,256]{1,0:T(8,128)(2,1)S(1)} %get-tuple-element.60), channel_id=1, source_target_pairs={{0,8},{4,12},{8,0},{12,4},{1,9},{5,13},{9,1},{13,5},{2,10},{6,14},... | collective-permute-start | bytes 393224 | tf_op jit(solution)/shard_map/cells_2_chunk_1/ppermute | solution.py:367
  28.2 20.8 %collective-permute-start.8 = (bf16[1024,256]{1,0:T(8,128)(2,1)S(1)}, bf16[1024,256]{1,0:T(8,128)(2,1)S(1)}, u32[]{:S(2)}, u32[]{:S(2)}) collective-permute-start(bf16[1024,256]{1,0:T(8,128)(2,1)S(1)} %get-tuple-element.72), channel_id=1, source_target_pairs={{0,2},{1,3},{2,0},{3,1},{4,6},{5,7},{6,4},{7,5},{8,10},{9,11},{10,... | collective-permute-start | bytes 1572872 | tf_op jit(solution)/shard_map/far_0/ppermute | solution.py:370
  29.8 9.8 %collective-permute-start.11 = (bf16[256,256]{1,0:T(8,128)(2,1)S(1)}, bf16[256,256]{1,0:T(8,128)(2,1)S(1)}, u32[]{:S(2)}, u32[]{:S(2)}) collective-permute-start(bf16[256,256]{1,0:T(8,128)(2,1)S(1)} %get-tuple-element.79), channel_id=1, source_target_pairs={{0,12},{4,8},{8,4},{12,0},{1,13},{5,9},{9,5},{13,1},{2,14},{6,10},... | collective-permute-start | bytes 393224 | tf_op jit(solution)/shard_map/cells_3_chunk_2/ppermute | solution.py:367
  31.3 12.1 %collective-permute-start.10 = (bf16[256,256]{1,0:T(8,128)(2,1)S(1)}, bf16[256,256]{1,0:T(8,128)(2,1)S(1)}, u32[]{:S(2)}, u32[]{:S(2)}) collective-permute-start(bf16[256,256]{1,0:T(8,128)(2,1)S(1)} %get-tuple-element.77), channel_id=1, source_target_pairs={{0,4},{4,0},{8,12},{12,8},{1,5},{5,1},{9,13},{13,9},{2,6},{6,2},{1... | collective-permute-start | bytes 393224 | tf_op jit(solution)/shard_map/cells_1_chunk_2/ppermute | solution.py:367
  35.2 13.8 %collective-permute-start.9 = (bf16[256,256]{1,0:T(8,128)(2,1)S(1)}, bf16[256,256]{1,0:T(8,128)(2,1)S(1)}, u32[]{:S(2)}, u32[]{:S(2)}) collective-permute-start(bf16[256,256]{1,0:T(8,128)(2,1)S(1)} %get-tuple-element.75), channel_id=1, source_target_pairs={{0,8},{4,12},{8,0},{12,4},{1,9},{5,13},{9,1},{13,5},{2,10},{6,14},... | collective-permute-start | bytes 393224 | tf_op jit(solution)/shard_map/cells_2_chunk_2/ppermute | solution.py:367
  37.0 15.5 %collective-permute-start.7 = (bf16[1024,256]{1,0:T(8,128)(2,1)S(1)}, bf16[1024,256]{1,0:T(8,128)(2,1)S(1)}, u32[]{:S(2)}, u32[]{:S(2)}) collective-permute-start(bf16[1024,256]{1,0:T(8,128)(2,1)S(1)} %get-tuple-element.69), channel_id=1, source_target_pairs={{0,2},{1,3},{2,0},{3,1},{4,6},{5,7},{6,4},{7,5},{8,10},{9,11},{10,... | collective-permute-start | bytes 1572872 | tf_op jit(solution)/shard_map/far_1/ppermute | solution.py:370
  39.6 12.9 %collective-permute-start.14 = (bf16[256,256]{1,0:T(8,128)(2,1)S(1)}, bf16[256,256]{1,0:T(8,128)(2,1)S(1)}, u32[]{:S(2)}, u32[]{:S(2)}) collective-permute-start(bf16[256,256]{1,0:T(8,128)(2,1)S(1)} %get-tuple-element.91), channel_id=1, source_target_pairs={{0,12},{4,8},{8,4},{12,0},{1,13},{5,9},{9,5},{13,1},{2,14},{6,10},... | collective-permute-start | bytes 393224 | tf_op jit(solution)/shard_map/cells_3_chunk_3/ppermute | solution.py:367
  43.4 9.1 %collective-permute-start.13 = (bf16[256,256]{1,0:T(8,128)(2,1)S(1)}, bf16[256,256]{1,0:T(8,128)(2,1)S(1)}, u32[]{:S(2)}, u32[]{:S(2)}) collective-permute-start(bf16[256,256]{1,0:T(8,128)(2,1)S(1)} %get-tuple-element.89), channel_id=1, source_target_pairs={{0,4},{4,0},{8,12},{12,8},{1,5},{5,1},{9,13},{13,9},{2,6},{6,2},{1... | collective-permute-start | bytes 393224 | tf_op jit(solution)/shard_map/cells_1_chunk_3/ppermute | solution.py:367
  49.0 6.7 %collective-permute-start.12 = (bf16[256,256]{1,0:T(8,128)(2,1)S(1)}, bf16[256,256]{1,0:T(8,128)(2,1)S(1)}, u32[]{:S(2)}, u32[]{:S(2)}) collective-permute-start(bf16[256,256]{1,0:T(8,128)(2,1)S(1)} %get-tuple-element.87), channel_id=1, source_target_pairs={{0,8},{4,12},{8,0},{12,4},{1,9},{5,13},{9,1},{13,5},{2,10},{6,14},... | collective-permute-start | bytes 393224 | tf_op jit(solution)/shard_map/cells_2_chunk_3/ppermute | solution.py:367
  50.2 11.7 %collective-permute-start.18 = (bf16[1024,256]{1,0:T(8,128)(2,1)S(1)}, bf16[1024,256]{1,0:T(8,128)(2,1)S(1)}, u32[]{:S(2)}, u32[]{:S(2)}) collective-permute-start(bf16[1024,256]{1,0:T(8,128)(2,1)S(1)} %get-tuple-element.98), channel_id=1, source_target_pairs={{0,2},{1,3},{2,0},{3,1},{4,6},{5,7},{6,4},{7,5},{8,10},{9,11},{10,... | collective-permute-start | bytes 1572872 | tf_op jit(solution)/shard_map/far_2/ppermute | solution.py:370
  57.8 7.0 %collective-permute-start.16 = (bf16[1024,1024]{1,0:T(8,128)(2,1)S(1)}, bf16[1024,1024]{1,0:T(8,128)(2,1)S(1)}, u32[]{:S(2)}, u32[]{:S(2)}) collective-permute-start(bf16[1024,1024]{1,0:T(8,128)(2,1)S(1)} %get-tuple-element.95.refs_0_.refs_1_), channel_id=1, source_target_pairs={{0,1},{1,0},{2,3},{3,2},{4,5},{5,4},{6,7},{7,6},{8,9},{9,8},{10,11... | collective-permute-start | bytes 6291464 | tf_op jit(solution)/shard_map/near/ppermute | solution.py:374
  60.5 4.2 %collective-permute-start.17 = (bf16[1024,512]{1,0:T(8,128)(2,1)S(1)}, bf16[1024,512]{1,0:T(8,128)(2,1)S(1)}, u32[]{:S(2)}, u32[]{:S(2)}) collective-permute-start(bf16[1024,512]{1,0:T(8,128)(2,1)S(1)} %get-tuple-element.97.refs_0_), channel_id=1, source_target_pairs={{0,1},{1,0},{2,3},{3,2},{4,5},{5,4},{6,7},{7,6},{8,9},{9,8},{10,11... | collective-permute-start | bytes 3145736 | tf_op jit(solution)/shard_map/far_near/ppermute | solution.py:374
  61.1 11.3 %collective-permute-start.15 = (bf16[784,256]{1,0:T(8,128)(2,1)S(1)}, bf16[784,256]{1,0:T(8,128)(2,1)S(1)}, u32[]{:S(2)}, u32[]{:S(2)}) collective-permute-start(bf16[784,256]{1,0:T(8,128)(2,1)S(1)} %get-tuple-element.96), channel_id=1, source_target_pairs={{0,2},{1,3},{2,0},{3,1},{4,6},{5,7},{6,4},{7,5},{8,10},{9,11},{10,... | collective-permute-start | bytes 1204232 | tf_op jit(solution)/shard_map/ppermute | solution.py:370
  61.9 2.9 %collective-permute-start.19 = (bf16[1024,256]{1,0:T(8,128)(2,1)S(1)}, bf16[1024,256]{1,0:T(8,128)(2,1)S(1)}, u32[]{:S(2)}, u32[]{:S(2)}) collective-permute-start(bf16[1024,256]{1,0:T(8,128)(2,1)S(1)} %collective-permute-done.18.refs_1_), channel_id=1, source_target_pairs={{0,1},{1,0},{2,3},{3,2},{4,5},{5,4},{6,7},{7,6},{8,9},{9,8},{10,11... | collective-permute-start | bytes 1572872 | tf_op jit(solution)/shard_map/far_near_2/ppermute | solution.py:374
  72.6 2.0 %collective-permute-start.20 = (bf16[1024,256]{1,0:T(8,128)(2,1)S(1)}, bf16[1024,256]{1,0:T(8,128)(2,1)S(1)}, u32[]{:S(2)}, u32[]{:S(2)}) collective-permute-start(bf16[1024,256]{1,0:T(8,128)(2,1)S(1)} %finish.1.refs_0_), channel_id=1, source_target_pairs={{0,1},{1,0},{2,3},{3,2},{4,5},{5,4},{6,7},{7,6},{8,9},{9,8},{10,11... | collective-permute-start | bytes 1572872 | tf_op jit(solution)/shard_map/far_near_3/ppermute | solution.py:374

commit v20 on v19

--- a/solution.py
+++ b/solution.py
@@ -109,14 +109,21 @@
     return parts
 
 
-def standardize_kernel(types, cap, lead, separate, start, gathered, late, mean_ref, *refs):
+def standardize_kernel(types, cap, lead, separate, start, gathered, late, counts, mean_ref, *refs):
     blocks = refs[:types]
     tails = refs[types : 2 * types] if separate else blocks
     base = 0 if separate else cap
     refs = refs[2 * types :] if separate else refs[types:]
-    work, turned, sems = refs[-3:]
-    more = (gathered[0] if gathered else 0) + (1 if late else 0)
-    scaled_ref, turned_ref, count_ref, all_ref, *joined_refs = refs[-7 - more : -3]
+    outputs = 3 + counts + (gathered[0] if gathered else 0)
+    outs, scratch = list(refs[: len(refs) - (4 if late else 3)]), refs[-4 if late else -3 :]
+    outs = outs[len(outs) - outputs :]
+    turned_ref, all_ref = outs[:2]
+    count_ref = outs[2] if counts else None
+    joined_refs = outs[2 + counts : outputs - 1]
+    if late:
+        sent_ref, (work, turned, sems, scaled_ref) = outs[-1], scratch
+    else:
+        scaled_ref, (work, turned, sems) = outs[-1], scratch
     copies = []
     if gathered:
         sources = refs[: len(gathered[1])]
@@ -156,7 +163,6 @@
     copies.append(pltpu.make_async_copy(turned, turned_ref.at[columns, :], sems.at[1]))
     copies[-1].start()
     if late:
-        sent_ref = joined_refs[-1]
         sent_ref[0 : slots - cap, :] = scaled_ref[cap:slots, :]
         row = lax.broadcasted_iota(jnp.int32, (TILE, 1), 0)
         notes = jnp.zeros((TILE, width), jnp.float32)
@@ -165,10 +171,11 @@
         sent_ref[slots - cap : slots - cap + TILE, :] = notes.astype(jnp.bfloat16)
     for copy in copies:
         copy.wait()
-    count_ref[...] = jnp.broadcast_to(count, count_ref.shape)
-
-
-def standardize(types, cap, mean, start, blocks, first, left, own, gather, late):
+    if counts:
+        count_ref[...] = jnp.broadcast_to(count, count_ref.shape)
+
+
+def standardize(types, cap, mean, start, blocks, first, left, own, gather, late, counts):
     lead, width = first[0].shape[1], blocks[0].shape[1]
     panel = mean.shape[1]
     separate = first is not blocks
@@ -178,7 +185,13 @@
     if separate:
         specs += [pl.BlockSpec((TILE, lead), lambda i: (cap // TILE, 0))] * types
         args += list(first)
-    gathered, shapes = [], []
+    shapes = [
+        jax.ShapeDtypeStruct((panel, slots), jnp.bfloat16),
+        jax.ShapeDtypeStruct((slots, panel), jnp.bfloat16),
+    ]
+    if counts:
+        shapes.append(jax.ShapeDtypeStruct((8, 128), jnp.float32))
+    gathered = []
     for i, panels in enumerate(gather):
         column = 0
         for array in panels:
@@ -187,14 +200,21 @@
             specs.append(whole)
             args.append(array)
         shapes.append(jax.ShapeDtypeStruct((slots, column), jnp.bfloat16))
-    if late:
-        shapes.append(jax.ShapeDtypeStruct((slots - cap + TILE, width), jnp.bfloat16))
+    rows = slots - cap + TILE if late else slots
+    shapes.append(jax.ShapeDtypeStruct((rows, width), jnp.bfloat16))
     aliases = {}
-    for value, output in ((left, 1), (own, 3)):
+    for value, output in ((left, 0), (own, 1)):
         if value is not None:
             aliases[len(args)] = output
             specs.append(anywhere)
             args.append(value)
+    scratch = [
+        pltpu.VMEM((slots, width), jnp.float32),
+        pltpu.VMEM((width, slots), jnp.bfloat16),
+        pltpu.SemaphoreType.DMA((2 + len(gathered),)),
+    ]
+    if late:
+        scratch.append(pltpu.VMEM((slots, width), jnp.bfloat16))
     return pl.pallas_call(
         functools.partial(
             standardize_kernel,
@@ -205,22 +225,13 @@
             start,
             (len(gather), gathered) if gathered else None,
             late,
+            int(counts),
         ),
         grid=(1,),
-        out_shape=[
-            jax.ShapeDtypeStruct((slots, width), jnp.bfloat16),
-            jax.ShapeDtypeStruct((panel, slots), jnp.bfloat16),
-            jax.ShapeDtypeStruct((8, 128), jnp.float32),
-            jax.ShapeDtypeStruct((slots, panel), jnp.bfloat16),
-            *shapes,
-        ],
+        out_shape=shapes,
         in_specs=specs,
-        out_specs=[whole, anywhere, whole, anywhere] + [whole] * len(shapes),
-        scratch_shapes=[
-            pltpu.VMEM((slots, width), jnp.float32),
-            pltpu.VMEM((width, slots), jnp.bfloat16),
-            pltpu.SemaphoreType.DMA((2 + len(gathered),)),
-        ],
+        out_specs=[anywhere, anywhere] + [whole] * (len(shapes) - 2),
+        scratch_shapes=scratch,
         input_output_aliases=aliases,
         compiler_params=pltpu.CompilerParams(vmem_limit_bytes=VMEM),
         cost_estimate=lengthy,
@@ -375,7 +386,7 @@
 
     mean = jnp.broadcast_to(after(gene_mean, packed[0][0]), (8, panel))
 
-    order = sorted(range(1, types), key=lambda j: (j == 3, j == 1, j))
+    order = sorted(range(1, types), key=lambda j: (j == 2, j == 1, -j))
     left, own, out, far, before = None, None, None, [], None
     for k in range(chunks):
         arrived = [packed[k][0]]
@@ -400,9 +411,13 @@
             out = gram(blocks, cores, count, left, groups, None, brief)
             arrived[0] = after(arrived[0], out)
             gather = [[got[d] for got in far[: k - 1]] for d in range(chips - 1)]
-        scaled, left, count, own, *joined = standardize(
-            types, cap, mean, starts[k], arrived, first, left, own, gather, k == chunks - 1
+        counts, late = k == chunks - 2, k == chunks - 1
+        left, own, *rest = standardize(
+            types, cap, mean, starts[k], arrived, first, left, own, gather, late, counts
         )
+        if counts:
+            count = rest.pop(0)
+        scaled, joined = rest[-1], rest[:-1]
         if k < chunks - 1:
             with jax.named_scope(f"far_{k}"):
                 far.append([across(scaled, d) for d in range(1, chips)])
@@ -410,7 +425,7 @@
     multiply = functools.partial(gram, blocks, cores, count, left)
     last = chunks - 1
     near = side("near", own)
-    sent = joined.pop()
+    sent = scaled
     joined_near = [[side("far_near", p)] for p in joined] or [[]] * (chips - 1)
     joined = [[p] for p in joined] or [[]] * (chips - 1)
     if out is None:

time: 76.5 us -> 75.1 us (0.982)
  Pallas kernels: 25.7 us -> 23.7 us
  waiting for transfers between devices: 19.9 us -> 20.8 us
    pallas_call x4, Pallas kernels: 6.95 us -> 4.96 us  [standardize(): pl.pallas_call(functools.partial(standardize_kernel, types, cap, lead, se...]
    ppermute x12, waiting for transfers between devices: 14.7 us -> 16.3 us  [swap(): return lax.ppermute(block, 'cells', [(s, s ^ by) for s in range(types)])]
    ppermute x12, starting transfers between devices: 19.6 us -> 18.3 us  [swap(): return lax.ppermute(block, 'cells', [(s, s ^ by) for s in range(types)])]
    ppermute x5, starting transfers between devices: 6.66 us -> 7.8 us  [across(): lax.ppermute(panel_, 'blk', [(b, (b + by * cores) % blocks) for b in rang...]
  transfers between devices with their start and end apart: 21 -> 21, of which waited for: 7 -> 7; matrix products, arithmetic and copies ran while one was open for 1% -> 1% of each run, Pallas kernels for 29% -> 27%
where the time goes in v20:
time: 75.1 us; the launch traced here: 74.9 us
  starting transfers between devices  26.8 us (36%)
  Pallas kernels  23.7 us (32%)
  waiting for transfers between devices  20.8 us (28%)
  local copies, waits for them, and re-layouts  3.27 us (4%)
    ppermute x12, starting transfers between devices, swap(): return lax.ppermute(block, 'cells', [(s, s ^ by) for s in range(types)])  18.3 us
    pallas_call x6, Pallas kernels, gram(): pl.pallas_call(functools.partial(gram_kernel, blocks, cores, strip, layou...  16.9 us
    ppermute x12, waiting for transfers between devices, swap(): return lax.ppermute(block, 'cells', [(s, s ^ by) for s in range(types)])  16.3 us
    ppermute x5, starting transfers between devices, across(): lax.ppermute(panel_, 'blk', [(b, (b + by * cores) % blocks) for b in rang...  7.8 us
    pallas_call x4, Pallas kernels, standardize(): pl.pallas_call(functools.partial(standardize_kernel, types, cap, lead, se...  4.96 us
    ppermute x5, waiting for transfers between devices, across(): lax.ppermute(panel_, 'blk', [(b, (b + by * cores) % blocks) for b in rang...  4.11 us
    unnamed x6, local copies, waits for them, and re-layouts  2.58 us
    pallas_call x1, Pallas kernels, pack(): pl.pallas_call(functools.partial(pack_kernel, types, cap, widths), out_sh...  1.71 us
  transfers between devices with their start and end apart: 21, of which 7 were waited for; matrix products, arithmetic and copies ran while one was open for 1% of the time, Pallas kernels for 27%

profile of v20, /device:TPU:0, one launch (start us, length us, event | category | flops | bytes accessed | tf_op | source)
XLA Modules:
  0.0 74.9 jit_solution(16382608834101449706)
XLA Ops:
  0.0 1.2 %copy-done = bf16[512,1024]{1,0:T(8,128)(2,1)S(1)} copy-done((bf16[512,1024]{1,0:T(8,128)(2,1)S(1)}, bf16[512,1024]{1,0:T(8,128)(2,1)}, u32[]{:S(2)}) %copy-start) | copy-done | bytes 1048600
  1.2 0.7 copy-done.1
  1.9 0.7 copy-done.2
  2.6 1.7 %pack.1 = (bf16[272,256]{1,0:T(8,128)(2,1)S(1)}, bf16[272,256]{1,0:T(8,128)(2,1)S(1)}, bf16[272,256]{1,0:T(8,128)(2,1)S(1)}, bf16[272,256]{1,0:T(8,128)(2,1)S(1)...) custom-call(s32[512]{0:T(512)S(1)} %copy-done.1, ...), custom_call_target="tpu_custom_call" | custom-call | flops 1024 | bytes 1024 | tf_op jit(solution)/shard_map/pack/pallas_call | solution.py:68
  4.3 5.1 %collective-permute-start = (bf16[272,256]{1,0:T(8,128)(2,1)S(1)}, bf16[272,256]{1,0:T(8,128)(2,1)S(1)}, u32[]{:S(2)}, u32[]{:S(2)}) collective-permute-start(bf16[272,256]{1,0:T(8,128)(2,1)S(1)} %get-tuple-element.55), channel_id=1, source_target_pairs={{0,12},{4,8},{8,4},{12,0},{1,13},{5,9},{9,5},{13,1},{2,14},{6,10},... | collective-permute-start | bytes 417800 | tf_op jit(solution)/shard_map/cells_3_chunk_0/ppermute | solution.py:378
  9.4 0.0 collective-permute-start.1
  9.4 0.6 collective-permute-start.2
  10.1 1.6 %collective-permute-start.10 = (bf16[256,256]{1,0:T(8,128)(2,1)S(1)}, bf16[256,256]{1,0:T(8,128)(2,1)S(1)}, u32[]{:S(2)}, u32[]{:S(2)}) collective-permute-start(bf16[256,256]{1,0:T(8,128)(2,1)S(1)} %get-tuple-element.84.refs_0_), channel_id=1, source_target_pairs={{0,2},{1,3},{2,0},{3,1},{4,6},{5,7},{6,4},{7,5},{8,10},{9,11},{10,... | collective-permute-start | bytes 393224 | tf_op jit(solution)/shard_map/far_local/ppermute | solution.py:381
  11.7 3.3 %collective-permute-done.10.local_ref = bf16[256,256]{1,0:T(8,128)(2,1)S(1)} collective-permute-done((bf16[256,256]{1,0:T(8,128)(2,1)S(1)}, bf16[256,256]{1,0:T(8,128)(2,1)S(1)}, u32[]{:S(2)}, u32[]{:S(2)}) %collective-permute-start.10) | collective-permute-done | bytes 131104 | tf_op jit(solution)/shard_map/far_local/ppermute | solution.py:381
  15.0 0.0 collective-permute-done.refs_1_.refs_5_
  15.0 0.7 broadcast_in_dim.3.mean_ref
  15.7 3.7 %collective-permute-start.4 = (bf16[256,256]{1,0:T(8,128)(2,1)S(1)}, bf16[256,256]{1,0:T(8,128)(2,1)S(1)}, u32[]{:S(2)}, u32[]{:S(2)}) collective-permute-start(bf16[256,256]{1,0:T(8,128)(2,1)S(1)} %get-tuple-element.62), channel_id=1, source_target_pairs={{0,12},{4,8},{8,4},{12,0},{1,13},{5,9},{9,5},{13,1},{2,14},{6,10},... | collective-permute-start | bytes 393224 | tf_op jit(solution)/shard_map/cells_3_chunk_1/ppermute | solution.py:378
  19.5 6.9 %collective-permute-done.2.refs_3_.refs_7_ = bf16[272,256]{1,0:T(8,128)(2,1)S(1)} collective-permute-done((bf16[272,256]{1,0:T(8,128)(2,1)S(1)}, bf16[272,256]{1,0:T(8,128)(2,1)S(1)}, u32[]{:S(2)}, u32[]{:S(2)}) %collective-permute-start.2) | collective-permute-done | bytes 139296 | tf_op jit(solution)/shard_map/cells_2_chunk_0/ppermute | solution.py:378
  26.4 0.0 collective-permute-start.8
  26.4 1.2 %standardize.4 = (bf16[1024,1024]{1,0:T(8,128)(2,1)S(1)}, bf16[1024,1024]{1,0:T(8,128)(2,1)S(1)}, bf16[1024,256]{1,0:T(8,128)(2,1)S(1)}) custom-call(f32[8,1024]{1,0:T(8,128)S(1)} %broadcast_in_dim.3.mean_ref, bf16[272,256]{1,0:T(8,128)(2,1)S(1)} %get-tuple-element.52.refs_0_.refs_4_.tail_ref, bf16[272,256]{1,0:T(8,128)(2,1)S(1)} %collective-permute-done.refs_1_.refs_5_, ...), custom_call_target="tpu_custom_call" | custom-call | flops 20000000000 | bytes 1024 | tf_op jit(solution)/shard_map/standardize/pallas_call | solution.py:218
  27.6 1.6 %collective-permute-start.3 = (bf16[1024,256]{1,0:T(8,128)(2,1)S(1)}, bf16[1024,256]{1,0:T(8,128)(2,1)S(1)}, u32[]{:S(2)}, u32[]{:S(2)}) collective-permute-start(bf16[1024,256]{1,0:T(8,128)(2,1)S(1)} %get-tuple-element.58), channel_id=1, source_target_pairs={{0,2},{1,3},{2,0},{3,1},{4,6},{5,7},{6,4},{7,5},{8,10},{9,11},{10,... | collective-permute-start | bytes 1572872 | tf_op jit(solution)/shard_map/far_0/ppermute | solution.py:381
  29.2 3.3 %collective-permute-done.8.refs_3_ = bf16[256,256]{1,0:T(8,128)(2,1)S(1)} collective-permute-done((bf16[256,256]{1,0:T(8,128)(2,1)S(1)}, bf16[256,256]{1,0:T(8,128)(2,1)S(1)}, u32[]{:S(2)}, u32[]{:S(2)}) %collective-permute-start.8) | collective-permute-done | bytes 131104 | tf_op jit(solution)/shard_map/cells_2_chunk_1/ppermute | solution.py:378
  32.5 3.0 %collective-permute-start.7 = (bf16[256,256]{1,0:T(8,128)(2,1)S(1)}, bf16[256,256]{1,0:T(8,128)(2,1)S(1)}, u32[]{:S(2)}, u32[]{:S(2)}) collective-permute-start(bf16[256,256]{1,0:T(8,128)(2,1)S(1)} %get-tuple-element.67), channel_id=1, source_target_pairs={{0,4},{4,0},{8,12},{12,8},{1,5},{5,1},{9,13},{13,9},{2,6},{6,2},{1... | collective-permute-start | bytes 393224 | tf_op jit(solution)/shard_map/cells_1_chunk_2/ppermute | solution.py:378
  35.5 0.0 collective-permute-done.4.refs_1_
  35.5 1.4 %collective-permute-start.5 = (bf16[256,256]{1,0:T(8,128)(2,1)S(1)}, bf16[256,256]{1,0:T(8,128)(2,1)S(1)}, u32[]{:S(2)}, u32[]{:S(2)}) collective-permute-start(bf16[256,256]{1,0:T(8,128)(2,1)S(1)} %get-tuple-element.63), channel_id=1, source_target_pairs={{0,12},{4,8},{8,4},{12,0},{1,13},{5,9},{9,5},{13,1},{2,14},{6,10},... | collective-permute-start | bytes 393224 | tf_op jit(solution)/shard_map/cells_3_chunk_2/ppermute | solution.py:378
  36.9 1.2 %standardize.5 = (bf16[1024,1024]{1,0:T(8,128)(2,1)S(1)}, bf16[1024,1024]{1,0:T(8,128)(2,1)S(1)}, bf16[1024,256]{1,0:T(8,128)(2,1)S(1)}) custom-call(f32[8,1024]{1,0:T(8,128)S(1)} %broadcast_in_dim.3.mean_ref, bf16[256,256]{1,0:T(8,128)(2,1)S(1)} %get-tuple-element.74.refs_0_, ...), custom_call_target="tpu_custom_call", output_to_operand_aliasing={{0}: (9, {}), {1}: (10, {})} | custom-call | flops 20000000000 | bytes 1024 | tf_op jit(solution)/shard_map/standardize/pallas_call | solution.py:218
  38.1 1.6 %collective-permute-start.11 = (bf16[1024,256]{1,0:T(8,128)(2,1)S(1)}, bf16[1024,256]{1,0:T(8,128)(2,1)S(1)}, u32[]{:S(2)}, u32[]{:S(2)}) collective-permute-start(bf16[1024,256]{1,0:T(8,128)(2,1)S(1)} %get-tuple-element.80), channel_id=1, source_target_pairs={{0,2},{1,3},{2,0},{3,1},{4,6},{5,7},{6,4},{7,5},{8,10},{9,11},{10,... | collective-permute-start | bytes 1572872 | tf_op jit(solution)/shard_map/far_1/ppermute | solution.py:381
  39.6 5.6 %collective-permute-done.9.refs_3_ = bf16[256,256]{1,0:T(8,128)(2,1)S(1)} collective-permute-done((bf16[256,256]{1,0:T(8,128)(2,1)S(1)}, bf16[256,256]{1,0:T(8,128)(2,1)S(1)}, u32[]{:S(2)}, u32[]{:S(2)}) %collective-permute-start.9) | collective-permute-done | bytes 131104 | tf_op jit(solution)/shard_map/cells_2_chunk_2/ppermute | solution.py:378
  45.2 0.0 collective-permute-done.7.refs_2_
  45.2 0.8 %collective-permute-start.13 = (bf16[256,256]{1,0:T(8,128)(2,1)S(1)}, bf16[256,256]{1,0:T(8,128)(2,1)S(1)}, u32[]{:S(2)}, u32[]{:S(2)}) collective-permute-start(bf16[256,256]{1,0:T(8,128)(2,1)S(1)} %get-tuple-element.88), channel_id=1, source_target_pairs={{0,4},{4,0},{8,12},{12,8},{1,5},{5,1},{9,13},{13,9},{2,6},{6,2},{1... | collective-permute-start | bytes 393224 | tf_op jit(solution)/shard_map/cells_1_chunk_3/ppermute | solution.py:378
  46.0 3.6 %collective-permute-start.12 = (bf16[256,256]{1,0:T(8,128)(2,1)S(1)}, bf16[256,256]{1,0:T(8,128)(2,1)S(1)}, u32[]{:S(2)}, u32[]{:S(2)}) collective-permute-start(bf16[256,256]{1,0:T(8,128)(2,1)S(1)} %get-tuple-element.86), channel_id=1, source_target_pairs={{0,12},{4,8},{8,4},{12,0},{1,13},{5,9},{9,5},{13,1},{2,14},{6,10},... | collective-permute-start | bytes 393224 | tf_op jit(solution)/shard_map/cells_3_chunk_3/ppermute | solution.py:378
  49.6 0.0 collective-permute-done.3.refs_8_
  49.6 1.2 %standardize.6 = (bf16[1024,1024]{1,0:T(8,128)(2,1)S(1)}, bf16[1024,1024]{1,0:T(8,128)(2,1)S(1)}, f32[8,128]{1,0:T(8,128)S(1)}, bf16[1024,256]{1,0:T(8,128)(2,1)S(1)}) custom-call(f32[8,1024]{1,0:T(8,128)S(1)} %broadcast_in_dim.3.mean_ref, bf16[256,256]{1,0:T(8,128)(2,1)S(1)} %get-tuple-element.59.refs_0_, ...), custom_call_target="tpu_custom_call", output_to_operand_aliasing={{0}: (9, {}), {1}: (10, {})} | custom-call | flops 20000000000 | bytes 1024 | tf_op jit(solution)/shard_map/standardize/pallas_call | solution.py:218
  50.8 1.6 %collective-permute-start.18 = (bf16[1024,256]{1,0:T(8,128)(2,1)S(1)}, bf16[1024,256]{1,0:T(8,128)(2,1)S(1)}, u32[]{:S(2)}, u32[]{:S(2)}) collective-permute-start(bf16[1024,256]{1,0:T(8,128)(2,1)S(1)} %get-tuple-element.96), channel_id=1, source_target_pairs={{0,2},{1,3},{2,0},{3,1},{4,6},{5,7},{6,4},{7,5},{8,10},{9,11},{10,... | collective-permute-start | bytes 1572872 | tf_op jit(solution)/shard_map/far_2/ppermute | solution.py:381
  52.4 2.2 %gram.6.refs_2_ = bf16[1,1024,4096]{2,1,0:T(8,128)(2,1)} custom-call(f32[8,128]{1,0:T(8,128)S(1)} %get-tuple-element.79.count_ref, bf16[1024,1024]{1,0:T(8,128)(2,1)S(1)} %get-tuple-element.82.left_ref.refs_10_, bf16[1024,1024]{1,0:T(8,128)(2,1)S(1)} %get-tuple-element.83.refs_0_.refs_11_), custom_call_target="tpu_custom_call" | custom-call | flops 1024 | bytes 1024 | tf_op jit(solution)/shard_map/gram/pallas_call | solution.py:340
  54.6 0.5 collective-permute-done.14.refs_3_
  55.1 0.0 collective-permute-done.13.refs_2_
  55.1 0.0 collective-permute-done.12.refs_1_
  55.1 1.3 %standardize.7 = (bf16[1024,1024]{1,0:T(8,128)(2,1)S(1)}, bf16[1024,1024]{1,0:T(8,128)(2,1)S(1)}, bf16[1024,512]{1,0:T(8,128)(2,1)S(1)}, bf16[784,256]{1,0:T(8,128)(2,1)S(1)}) custom-call(f32[8,1024]{1,0:T(8,128)S(1)} %broadcast_in_dim.3.mean_ref, bf16[256,256]{1,0:T(8,128)(2,1)S(1)} %get-tuple-element.84.refs_0_, ...), custom_call_target="tpu_custom_call", output_to_operand_aliasing={{0}: (11, {}), {1}: (12, {})} | custom-call | flops 20000000000 | bytes 1024 | tf_op jit(solution)/shard_map/standardize/pallas_call | solution.py:218
  56.4 0.1 collective-permute-start.16
  56.5 2.6 %gram.7.refs_2_ = bf16[1,1024,4096]{2,1,0:T(8,128)(2,1)} custom-call(f32[8,128]{1,0:T(8,128)S(1)} %get-tuple-element.79.count_ref, bf16[1024,1024]{1,0:T(8,128)(2,1)S(1)} %get-tuple-element.91.left_ref, bf16[1024,1024]{1,0:T(8,128)(2,1)S(1)} %get-tuple-element.93.refs_0_.refs_1_, ...), custom_call_target="tpu_custom_call", output_to_operand_aliasing={{}: (4, {})} | custom-call | flops 1024 | bytes 1024 | tf_op jit(solution)/shard_map/gram/pallas_call | solution.py:340
  59.2 0.6 collective-permute-start.17
  59.7 1.5 %collective-permute-start.15 = (bf16[784,256]{1,0:T(8,128)(2,1)S(1)}, bf16[784,256]{1,0:T(8,128)(2,1)S(1)}, u32[]{:S(2)}, u32[]{:S(2)}) collective-permute-start(bf16[784,256]{1,0:T(8,128)(2,1)S(1)} %get-tuple-element.94), channel_id=1, source_target_pairs={{0,2},{1,3},{2,0},{3,1},{4,6},{5,7},{6,4},{7,5},{8,10},{9,11},{10,... | collective-permute-start | bytes 1204232 | tf_op jit(solution)/shard_map/ppermute | solution.py:381
  61.2 0.0 collective-permute-done.18.refs_1_
  61.2 2.9 %gram.8.refs_3_ = bf16[1,1024,4096]{2,1,0:T(8,128)(2,1)} custom-call(f32[8,128]{1,0:T(8,128)S(1)} %get-tuple-element.79.count_ref, bf16[1024,1024]{1,0:T(8,128)(2,1)S(1)} %get-tuple-element.91.left_ref, bf16[1024,512]{1,0:T(8,128)(2,1)S(1)} %get-tuple-element.95.refs_0_, ...), custom_call_target="tpu_custom_call", output_to_operand_aliasing={{}: (4, {})} | custom-call | flops 20000000000 | bytes 1024 | tf_op jit(solution)/shard_map/gram/pallas_call | solution.py:340
  64.1 0.0 collective-permute-done.19.refs_2_
  64.1 6.1 %gram.9.refs_1_ = bf16[1,1024,4096]{2,1,0:T(8,128)(2,1)} custom-call(f32[8,128]{1,0:T(8,128)S(1)} %get-tuple-element.79.count_ref, bf16[1024,1024]{1,0:T(8,128)(2,1)S(1)} %get-tuple-element.91.left_ref, bf16[1024,1024]{1,0:T(8,128)(2,1)S(1)} %collective-permute-done.16.refs_0_, ...), custom_call_target="tpu_custom_call", output_to_operand_aliasing={{}: (5, {})} | custom-call | flops 1024 | bytes 1024 | tf_op jit(solution)/shard_map/gram/pallas_call | solution.py:340
  70.2 0.8 %collective-permute-done.15.sent_ref = bf16[784,256]{1,0:T(8,128)(2,1)S(1)} collective-permute-done((bf16[784,256]{1,0:T(8,128)(2,1)S(1)}, bf16[784,256]{1,0:T(8,128)(2,1)S(1)}, u32[]{:S(2)}, u32[]{:S(2)}) %collective-permute-start.15) | collective-permute-done | bytes 401440 | tf_op jit(solution)/shard_map/ppermute | solution.py:381
  71.0 0.2 finish.1.refs_0_
  71.2 0.1 collective-permute-start.20
  71.3 1.5 %gram.10.refs_1_ = bf16[1,1024,4096]{2,1,0:T(8,128)(2,1)} custom-call(f32[8,128]{1,0:T(8,128)S(1)} %get-tuple-element.79.count_ref, bf16[1024,1024]{1,0:T(8,128)(2,1)S(1)} %get-tuple-element.91.left_ref, bf16[1024,256]{1,0:T(8,128)(2,1)S(1)} %finish.1.refs_0_, bf16[1,1024,4096]{2,1,0:T(8,128)(2,1)} %gram.9.refs_1_), custom_call_target="tpu_custom_call", output_to_operand_aliasing={{}: (3, {})} | custom-call | flops 1024 | bytes 1024 | tf_op jit(solution)/shard_map/gram/pallas_call | solution.py:340
  72.8 0.3 collective-permute-done.20.refs_0_
  73.2 1.5 %gram.11 = bf16[1,1024,4096]{2,1,0:T(8,128)(2,1)} custom-call(f32[8,128]{1,0:T(8,128)S(1)} %get-tuple-element.79.count_ref, bf16[1024,1024]{1,0:T(8,128)(2,1)S(1)} %get-tuple-element.91.left_ref, bf16[1024,256]{1,0:T(8,128)(2,1)S(1)} %collective-permute-done.20.refs_0_, bf16[1,1024,4096]{2,1,0:T(8,128)(2,1)} %gram.10.refs_1_), custom_call_target="tpu_custom_call", output_to_operand_aliasing={{}: (3, {})} | custom-call | flops 1024 | bytes 1024 | tf_op jit(solution)/shard_map/gram/pallas_call | solution.py:340
  (13 shorter events, 0.0 us)
Async XLA Ops:
  0.0 1.2 %copy-start = (bf16[512,1024]{1,0:T(8,128)(2,1)S(1)}, bf16[512,1024]{1,0:T(8,128)(2,1)}, u32[]{:S(2)}) copy-start(bf16[512,1024]{1,0:T(8,128)(2,1)} %expr_ref.1) | copy-start | bytes 3145732
  1.2 0.7 copy-start.1
  1.9 0.7 copy-start.2
  4.3 10.7 %collective-permute-start = (bf16[272,256]{1,0:T(8,128)(2,1)S(1)}, bf16[272,256]{1,0:T(8,128)(2,1)S(1)}, u32[]{:S(2)}, u32[]{:S(2)}) collective-permute-start(bf16[272,256]{1,0:T(8,128)(2,1)S(1)} %get-tuple-element.55), channel_id=1, source_target_pairs={{0,12},{4,8},{8,4},{12,0},{1,13},{5,9},{9,5},{13,1},{2,14},{6,10},... | collective-permute-start | bytes 417800 | tf_op jit(solution)/shard_map/cells_3_chunk_0/ppermute | solution.py:378
  9.4 10.1 %collective-permute-start.1 = (bf16[272,256]{1,0:T(8,128)(2,1)S(1)}, bf16[272,256]{1,0:T(8,128)(2,1)S(1)}, u32[]{:S(2)}, u32[]{:S(2)}) collective-permute-start(bf16[272,256]{1,0:T(8,128)(2,1)S(1)} %get-tuple-element.56), channel_id=1, source_target_pairs={{0,4},{4,0},{8,12},{12,8},{1,5},{5,1},{9,13},{13,9},{2,6},{6,2},{1... | collective-permute-start | bytes 417800 | tf_op jit(solution)/shard_map/cells_1_chunk_0/ppermute | solution.py:378
  9.4 17.0 %collective-permute-start.2 = (bf16[272,256]{1,0:T(8,128)(2,1)S(1)}, bf16[272,256]{1,0:T(8,128)(2,1)S(1)}, u32[]{:S(2)}, u32[]{:S(2)}) collective-permute-start(bf16[272,256]{1,0:T(8,128)(2,1)S(1)} %get-tuple-element.57), channel_id=1, source_target_pairs={{0,8},{4,12},{8,0},{12,4},{1,9},{5,13},{9,1},{13,5},{2,10},{6,14},... | collective-permute-start | bytes 417800 | tf_op jit(solution)/shard_map/cells_2_chunk_0/ppermute | solution.py:378
  10.1 5.0 %collective-permute-start.10 = (bf16[256,256]{1,0:T(8,128)(2,1)S(1)}, bf16[256,256]{1,0:T(8,128)(2,1)S(1)}, u32[]{:S(2)}, u32[]{:S(2)}) collective-permute-start(bf16[256,256]{1,0:T(8,128)(2,1)S(1)} %get-tuple-element.84.refs_0_), channel_id=1, source_target_pairs={{0,2},{1,3},{2,0},{3,1},{4,6},{5,7},{6,4},{7,5},{8,10},{9,11},{10,... | collective-permute-start | bytes 393224 | tf_op jit(solution)/shard_map/far_local/ppermute | solution.py:381
  15.7 19.8 %collective-permute-start.4 = (bf16[256,256]{1,0:T(8,128)(2,1)S(1)}, bf16[256,256]{1,0:T(8,128)(2,1)S(1)}, u32[]{:S(2)}, u32[]{:S(2)}) collective-permute-start(bf16[256,256]{1,0:T(8,128)(2,1)S(1)} %get-tuple-element.62), channel_id=1, source_target_pairs={{0,12},{4,8},{8,4},{12,0},{1,13},{5,9},{9,5},{13,1},{2,14},{6,10},... | collective-permute-start | bytes 393224 | tf_op jit(solution)/shard_map/cells_3_chunk_1/ppermute | solution.py:378
  19.5 13.0 %collective-permute-start.6 = (bf16[256,256]{1,0:T(8,128)(2,1)S(1)}, bf16[256,256]{1,0:T(8,128)(2,1)S(1)}, u32[]{:S(2)}, u32[]{:S(2)}) collective-permute-start(bf16[256,256]{1,0:T(8,128)(2,1)S(1)} %get-tuple-element.66), channel_id=1, source_target_pairs={{0,4},{4,0},{8,12},{12,8},{1,5},{5,1},{9,13},{13,9},{2,6},{6,2},{1... | collective-permute-start | bytes 393224 | tf_op jit(solution)/shard_map/cells_1_chunk_1/ppermute | solution.py:378
  26.4 6.1 %collective-permute-start.8 = (bf16[256,256]{1,0:T(8,128)(2,1)S(1)}, bf16[256,256]{1,0:T(8,128)(2,1)S(1)}, u32[]{:S(2)}, u32[]{:S(2)}) collective-permute-start(bf16[256,256]{1,0:T(8,128)(2,1)S(1)} %get-tuple-element.70), channel_id=1, source_target_pairs={{0,8},{4,12},{8,0},{12,4},{1,9},{5,13},{9,1},{13,5},{2,10},{6,14},... | collective-permute-start | bytes 393224 | tf_op jit(solution)/shard_map/cells_2_chunk_1/ppermute | solution.py:378
  27.6 22.0 %collective-permute-start.3 = (bf16[1024,256]{1,0:T(8,128)(2,1)S(1)}, bf16[1024,256]{1,0:T(8,128)(2,1)S(1)}, u32[]{:S(2)}, u32[]{:S(2)}) collective-permute-start(bf16[1024,256]{1,0:T(8,128)(2,1)S(1)} %get-tuple-element.58), channel_id=1, source_target_pairs={{0,2},{1,3},{2,0},{3,1},{4,6},{5,7},{6,4},{7,5},{8,10},{9,11},{10,... | collective-permute-start | bytes 1572872 | tf_op jit(solution)/shard_map/far_0/ppermute | solution.py:381
  32.5 12.7 %collective-permute-start.9 = (bf16[256,256]{1,0:T(8,128)(2,1)S(1)}, bf16[256,256]{1,0:T(8,128)(2,1)S(1)}, u32[]{:S(2)}, u32[]{:S(2)}) collective-permute-start(bf16[256,256]{1,0:T(8,128)(2,1)S(1)} %get-tuple-element.71), channel_id=1, source_target_pairs={{0,8},{4,12},{8,0},{12,4},{1,9},{5,13},{9,1},{13,5},{2,10},{6,14},... | collective-permute-start | bytes 393224 | tf_op jit(solution)/shard_map/cells_2_chunk_2/ppermute | solution.py:378
  32.5 12.7 %collective-permute-start.7 = (bf16[256,256]{1,0:T(8,128)(2,1)S(1)}, bf16[256,256]{1,0:T(8,128)(2,1)S(1)}, u32[]{:S(2)}, u32[]{:S(2)}) collective-permute-start(bf16[256,256]{1,0:T(8,128)(2,1)S(1)} %get-tuple-element.67), channel_id=1, source_target_pairs={{0,4},{4,0},{8,12},{12,8},{1,5},{5,1},{9,13},{13,9},{2,6},{6,2},{1... | collective-permute-start | bytes 393224 | tf_op jit(solution)/shard_map/cells_1_chunk_2/ppermute | solution.py:378
  35.5 10.5 %collective-permute-start.5 = (bf16[256,256]{1,0:T(8,128)(2,1)S(1)}, bf16[256,256]{1,0:T(8,128)(2,1)S(1)}, u32[]{:S(2)}, u32[]{:S(2)}) collective-permute-start(bf16[256,256]{1,0:T(8,128)(2,1)S(1)} %get-tuple-element.63), channel_id=1, source_target_pairs={{0,12},{4,8},{8,4},{12,0},{1,13},{5,9},{9,5},{13,1},{2,14},{6,10},... | collective-permute-start | bytes 393224 | tf_op jit(solution)/shard_map/cells_3_chunk_2/ppermute | solution.py:378
  38.1 16.5 %collective-permute-start.11 = (bf16[1024,256]{1,0:T(8,128)(2,1)S(1)}, bf16[1024,256]{1,0:T(8,128)(2,1)S(1)}, u32[]{:S(2)}, u32[]{:S(2)}) collective-permute-start(bf16[1024,256]{1,0:T(8,128)(2,1)S(1)} %get-tuple-element.80), channel_id=1, source_target_pairs={{0,2},{1,3},{2,0},{3,1},{4,6},{5,7},{6,4},{7,5},{8,10},{9,11},{10,... | collective-permute-start | bytes 1572872 | tf_op jit(solution)/shard_map/far_1/ppermute | solution.py:381
  45.2 9.9 %collective-permute-start.14 = (bf16[256,256]{1,0:T(8,128)(2,1)S(1)}, bf16[256,256]{1,0:T(8,128)(2,1)S(1)}, u32[]{:S(2)}, u32[]{:S(2)}) collective-permute-start(bf16[256,256]{1,0:T(8,128)(2,1)S(1)} %get-tuple-element.90), channel_id=1, source_target_pairs={{0,8},{4,12},{8,0},{12,4},{1,9},{5,13},{9,1},{13,5},{2,10},{6,14},... | collective-permute-start | bytes 393224 | tf_op jit(solution)/shard_map/cells_2_chunk_3/ppermute | solution.py:378
  45.2 9.9 %collective-permute-start.13 = (bf16[256,256]{1,0:T(8,128)(2,1)S(1)}, bf16[256,256]{1,0:T(8,128)(2,1)S(1)}, u32[]{:S(2)}, u32[]{:S(2)}) collective-permute-start(bf16[256,256]{1,0:T(8,128)(2,1)S(1)} %get-tuple-element.88), channel_id=1, source_target_pairs={{0,4},{4,0},{8,12},{12,8},{1,5},{5,1},{9,13},{13,9},{2,6},{6,2},{1... | collective-permute-start | bytes 393224 | tf_op jit(solution)/shard_map/cells_1_chunk_3/ppermute | solution.py:378
  46.0 9.1 %collective-permute-start.12 = (bf16[256,256]{1,0:T(8,128)(2,1)S(1)}, bf16[256,256]{1,0:T(8,128)(2,1)S(1)}, u32[]{:S(2)}, u32[]{:S(2)}) collective-permute-start(bf16[256,256]{1,0:T(8,128)(2,1)S(1)} %get-tuple-element.86), channel_id=1, source_target_pairs={{0,12},{4,8},{8,4},{12,0},{1,13},{5,9},{9,5},{13,1},{2,14},{6,10},... | collective-permute-start | bytes 393224 | tf_op jit(solution)/shard_map/cells_3_chunk_3/ppermute | solution.py:378
  50.8 10.4 %collective-permute-start.18 = (bf16[1024,256]{1,0:T(8,128)(2,1)S(1)}, bf16[1024,256]{1,0:T(8,128)(2,1)S(1)}, u32[]{:S(2)}, u32[]{:S(2)}) collective-permute-start(bf16[1024,256]{1,0:T(8,128)(2,1)S(1)} %get-tuple-element.96), channel_id=1, source_target_pairs={{0,2},{1,3},{2,0},{3,1},{4,6},{5,7},{6,4},{7,5},{8,10},{9,11},{10,... | collective-permute-start | bytes 1572872 | tf_op jit(solution)/shard_map/far_2/ppermute | solution.py:381
  56.4 7.7 %collective-permute-start.16 = (bf16[1024,1024]{1,0:T(8,128)(2,1)S(1)}, bf16[1024,1024]{1,0:T(8,128)(2,1)S(1)}, u32[]{:S(2)}, u32[]{:S(2)}) collective-permute-start(bf16[1024,1024]{1,0:T(8,128)(2,1)S(1)} %get-tuple-element.93.refs_0_.refs_1_), channel_id=1, source_target_pairs={{0,1},{1,0},{2,3},{3,2},{4,5},{5,4},{6,7},{7,6},{8,9},{9,8},{10,11... | collective-permute-start | bytes 6291464 | tf_op jit(solution)/shard_map/near/ppermute | solution.py:385
  59.2 5.0 %collective-permute-start.17 = (bf16[1024,512]{1,0:T(8,128)(2,1)S(1)}, bf16[1024,512]{1,0:T(8,128)(2,1)S(1)}, u32[]{:S(2)}, u32[]{:S(2)}) collective-permute-start(bf16[1024,512]{1,0:T(8,128)(2,1)S(1)} %get-tuple-element.95.refs_0_), channel_id=1, source_target_pairs={{0,1},{1,0},{2,3},{3,2},{4,5},{5,4},{6,7},{7,6},{8,9},{9,8},{10,11... | collective-permute-start | bytes 3145736 | tf_op jit(solution)/shard_map/far_near/ppermute | solution.py:385
  59.7 11.3 %collective-permute-start.15 = (bf16[784,256]{1,0:T(8,128)(2,1)S(1)}, bf16[784,256]{1,0:T(8,128)(2,1)S(1)}, u32[]{:S(2)}, u32[]{:S(2)}) collective-permute-start(bf16[784,256]{1,0:T(8,128)(2,1)S(1)} %get-tuple-element.94), channel_id=1, source_target_pairs={{0,2},{1,3},{2,0},{3,1},{4,6},{5,7},{6,4},{7,5},{8,10},{9,11},{10,... | collective-permute-start | bytes 1204232 | tf_op jit(solution)/shard_map/ppermute | solution.py:381
  61.2 2.9 %collective-permute-start.19 = (bf16[1024,256]{1,0:T(8,128)(2,1)S(1)}, bf16[1024,256]{1,0:T(8,128)(2,1)S(1)}, u32[]{:S(2)}, u32[]{:S(2)}) collective-permute-start(bf16[1024,256]{1,0:T(8,128)(2,1)S(1)} %collective-permute-done.18.refs_1_), channel_id=1, source_target_pairs={{0,1},{1,0},{2,3},{3,2},{4,5},{5,4},{6,7},{7,6},{8,9},{9,8},{10,11... | collective-permute-start | bytes 1572872 | tf_op jit(solution)/shard_map/far_near_2/ppermute | solution.py:385
  71.2 2.0 %collective-permute-start.20 = (bf16[1024,256]{1,0:T(8,128)(2,1)S(1)}, bf16[1024,256]{1,0:T(8,128)(2,1)S(1)}, u32[]{:S(2)}, u32[]{:S(2)}) collective-permute-start(bf16[1024,256]{1,0:T(8,128)(2,1)S(1)} %finish.1.refs_0_), channel_id=1, source_target_pairs={{0,1},{1,0},{2,3},{3,2},{4,5},{5,4},{6,7},{7,6},{8,9},{9,8},{10,11... | collective-permute-start | bytes 1572872 | tf_op jit(solution)/shard_map/far_near_3/ppermute | solution.py:385

commit v21 on v20

--- a/solution.py
+++ b/solution.py
@@ -305,7 +305,7 @@
             if parts:
                 right = joined[:, parts[0][0] : parts[0][0] + width]
             else:
-                skip = first if part else 0
+                skip = first if sources[panels[0]].shape[1] == rows else 0
                 right = sources[panels[0]][:, skip : skip + width]
             product = jnp.dot(
                 left_ref[row : row + size, :], right, preferred_element_type=jnp.float32
@@ -393,10 +393,24 @@
         for j in order:
             block = packed[k][j]
             if k:
-                block = after(block, before[len(arrived)], *([mean] if k == 1 else []))
+                waits = [mean] if k == 1 else [out] if out is not None and j == 2 else []
+                block = after(block, before[len(arrived)], *waits)
             with jax.named_scope(f"cells_{j}_chunk_{k}"):
                 arrived.append(swap(block, j))
         before = list(arrived)
+        if k >= 2 and chunks == 4:
+            low, high = starts[k - 1], starts[k]
+            if k == 2:
+                groups = [([own], (0, 0, 0, high, 0, high))]
+                groups += [([p], (d, 0, 0, widths[0], 0, high)) for d, p in enumerate(far[0], 1)]
+            else:
+                groups = [([own], (0, 0, low, high - low, 0, high))]
+                groups += [([own], (0, 0, 0, low, low, high))]
+                for d in range(1, chips):
+                    groups.append(([far[0][d - 1]], (d, 0, 0, widths[0], low, high)))
+                    groups.append(([far[1][d - 1]], (d, 0, starts[1], widths[1], 0, high)))
+            out = gram(blocks, cores, count, left, groups, out, brief)
+            arrived[0] = after(arrived[0], out)
         if k == 1:
             with jax.named_scope("far_local"):
                 local = [across(packed[-1][0], d) for d in range(1, chips)]
@@ -407,11 +421,8 @@
             first = arrived
         gather = []
         if k == chunks - 1 and k > 1:
-            groups = [([own], (0, 0, 0, starts[k], 0, starts[k]))]
-            out = gram(blocks, cores, count, left, groups, None, brief)
-            arrived[0] = after(arrived[0], out)
             gather = [[got[d] for got in far[: k - 1]] for d in range(chips - 1)]
-        counts, late = k == chunks - 2, k == chunks - 1
+        counts, late = k == min(1, chunks - 2), k == chunks - 1
         left, own, *rest = standardize(
             types, cap, mean, starts[k], arrived, first, left, own, gather, late, counts
         )
@@ -439,7 +450,13 @@
         out = multiply(groups, out, brief)
     final = [across(after(sent, out), d) for d in range(1, chips)]
     second = [side(f"far_near_{last - 1}", p, own) for p in far[last - 1]]
-    groups = [([*p, far[last - 1][i]], (i + 1, 0, 0)) for i, p in enumerate(joined)]
+    if chunks == 4:
+        groups = []
+        for i, p in enumerate(joined):
+            groups.append((p, (i + 1, 0, 0, starts[2], starts[3], panel)))
+            groups.append(([far[2][i]], (i + 1, 0, starts[2])))
+    else:
+        groups = [([*p, far[last - 1][i]], (i + 1, 0, 0)) for i, p in enumerate(joined)]
     out = multiply(groups, out, lengthy)
     groups = [([near], (0, 1, 0))]
     groups += [([*p, second[i]], (i + 1, 1, 0)) for i, p in enumerate(joined_near)]

time: 75.1 us -> 76.2 us (1.015)
  the two profiles are of different devices: /device:TPU:0 before, /device:TPU:13 now
where the time goes in v21:
time: 76.2 us; the launch traced here: 76 us
  starting transfers between devices  31.6 us (41%)
  Pallas kernels  26.6 us (35%)
  waiting for transfers between devices  14.2 us (19%)
  local copies, waits for them, and re-layouts  3.27 us (4%)
    pallas_call x7, Pallas kernels, gram(): pl.pallas_call(functools.partial(gram_kernel, blocks, cores, strip, layou...  19.7 us
    ppermute x12, starting transfers between devices, swap(): return lax.ppermute(block, 'cells', [(s, s ^ by) for s in range(types)])  17.8 us
    ppermute x12, waiting for transfers between devices, swap(): return lax.ppermute(block, 'cells', [(s, s ^ by) for s in range(types)])  8.9 us
    ppermute x4, starting transfers between devices, side(): lax.ppermute(after(panel_, *waits), 'blk', [(b, b ^ 1) for b in range(blo...  7.17 us
    ppermute x5, starting transfers between devices, across(): lax.ppermute(panel_, 'blk', [(b, (b + by * cores) % blocks) for b in rang...  6.58 us
    pallas_call x4, Pallas kernels, standardize(): pl.pallas_call(functools.partial(standardize_kernel, types, cap, lead, se...  4.96 us
    ppermute x5, waiting for transfers between devices, across(): lax.ppermute(panel_, 'blk', [(b, (b + by * cores) % blocks) for b in rang...  4.26 us
    unnamed x6, local copies, waits for them, and re-layouts  2.58 us
  transfers between devices with their start and end apart: 21, of which 8 were waited for; matrix products, arithmetic and copies ran while one was open for 1% of the time, Pallas kernels for 30%

profile of v21, /device:TPU:13, one launch (start us, length us, event | category | flops | bytes accessed | tf_op | source)
XLA Modules:
  0.0 76.0 jit_solution(4257879387557799656)
XLA Ops:
  0.0 1.2 %copy-done = bf16[512,1024]{1,0:T(8,128)(2,1)S(1)} copy-done((bf16[512,1024]{1,0:T(8,128)(2,1)S(1)}, bf16[512,1024]{1,0:T(8,128)(2,1)}, u32[]{:S(2)}) %copy-start) | copy-done | bytes 1048600
  1.2 0.7 copy-done.1
  1.9 0.7 copy-done.2
  2.6 1.7 %pack.1 = (bf16[272,256]{1,0:T(8,128)(2,1)S(1)}, bf16[272,256]{1,0:T(8,128)(2,1)S(1)}, bf16[272,256]{1,0:T(8,128)(2,1)S(1)}, bf16[272,256]{1,0:T(8,128)(2,1)S(1)...) custom-call(s32[512]{0:T(512)S(1)} %copy-done.1, ...), custom_call_target="tpu_custom_call" | custom-call | flops 1024 | bytes 1024 | tf_op jit(solution)/shard_map/pack/pallas_call | solution.py:68
  4.3 1.4 %collective-permute-start.1 = (bf16[272,256]{1,0:T(8,128)(2,1)S(1)}, bf16[272,256]{1,0:T(8,128)(2,1)S(1)}, u32[]{:S(2)}, u32[]{:S(2)}) collective-permute-start(bf16[272,256]{1,0:T(8,128)(2,1)S(1)} %get-tuple-element.59), channel_id=1, source_target_pairs={{0,12},{4,8},{8,4},{12,0},{1,13},{5,9},{9,5},{13,1},{2,14},{6,10},... | collective-permute-start | bytes 417800 | tf_op jit(solution)/shard_map/cells_3_chunk_0/ppermute | solution.py:378
  5.7 2.2 %collective-permute-start.3 = (bf16[272,256]{1,0:T(8,128)(2,1)S(1)}, bf16[272,256]{1,0:T(8,128)(2,1)S(1)}, u32[]{:S(2)}, u32[]{:S(2)}) collective-permute-start(bf16[272,256]{1,0:T(8,128)(2,1)S(1)} %get-tuple-element.62), channel_id=1, source_target_pairs={{0,4},{4,0},{8,12},{12,8},{1,5},{5,1},{9,13},{13,9},{2,6},{6,2},{1... | collective-permute-start | bytes 417800 | tf_op jit(solution)/shard_map/cells_1_chunk_0/ppermute | solution.py:378
  7.9 0.0 collective-permute-start.5
  7.9 1.2 %collective-permute-start = (bf16[256,256]{1,0:T(8,128)(2,1)S(1)}, bf16[256,256]{1,0:T(8,128)(2,1)S(1)}, u32[]{:S(2)}, u32[]{:S(2)}) collective-permute-start(bf16[256,256]{1,0:T(8,128)(2,1)S(1)} %get-tuple-element.86.refs_0_), channel_id=1, source_target_pairs={{0,2},{1,3},{2,0},{3,1},{4,6},{5,7},{6,4},{7,5},{8,10},{9,11},{10,... | collective-permute-start | bytes 393224 | tf_op jit(solution)/shard_map/far_local/ppermute | solution.py:381
  9.1 2.9 %collective-permute-done.local_ref = bf16[256,256]{1,0:T(8,128)(2,1)S(1)} collective-permute-done((bf16[256,256]{1,0:T(8,128)(2,1)S(1)}, bf16[256,256]{1,0:T(8,128)(2,1)S(1)}, u32[]{:S(2)}, u32[]{:S(2)}) %collective-permute-start) | collective-permute-done | bytes 131104 | tf_op jit(solution)/shard_map/far_local/ppermute | solution.py:381
  12.0 0.1 collective-permute-done.1.refs_1_.refs_5_
  12.1 0.7 broadcast_in_dim.3.mean_ref
  12.8 1.1 %collective-permute-start.2 = (bf16[256,256]{1,0:T(8,128)(2,1)S(1)}, bf16[256,256]{1,0:T(8,128)(2,1)S(1)}, u32[]{:S(2)}, u32[]{:S(2)}) collective-permute-start(bf16[256,256]{1,0:T(8,128)(2,1)S(1)} %get-tuple-element.60), channel_id=1, source_target_pairs={{0,12},{4,8},{8,4},{12,0},{1,13},{5,9},{9,5},{13,1},{2,14},{6,10},... | collective-permute-start | bytes 393224 | tf_op jit(solution)/shard_map/cells_3_chunk_1/ppermute | solution.py:378
  13.9 0.2 collective-permute-done.3.refs_2_.refs_6_
  14.0 2.2 %collective-permute-start.4 = (bf16[256,256]{1,0:T(8,128)(2,1)S(1)}, bf16[256,256]{1,0:T(8,128)(2,1)S(1)}, u32[]{:S(2)}, u32[]{:S(2)}) collective-permute-start(bf16[256,256]{1,0:T(8,128)(2,1)S(1)} %get-tuple-element.63), channel_id=1, source_target_pairs={{0,4},{4,0},{8,12},{12,8},{1,5},{5,1},{9,13},{13,9},{2,6},{6,2},{1... | collective-permute-start | bytes 393224 | tf_op jit(solution)/shard_map/cells_1_chunk_1/ppermute | solution.py:378
  16.2 0.0 collective-permute-done.5.refs_3_.refs_7_
  16.2 2.1 %collective-permute-start.6 = (bf16[256,256]{1,0:T(8,128)(2,1)S(1)}, bf16[256,256]{1,0:T(8,128)(2,1)S(1)}, u32[]{:S(2)}, u32[]{:S(2)}) collective-permute-start(bf16[256,256]{1,0:T(8,128)(2,1)S(1)} %get-tuple-element.66), channel_id=1, source_target_pairs={{0,8},{4,12},{8,0},{12,4},{1,9},{5,13},{9,1},{13,5},{2,10},{6,14},... | collective-permute-start | bytes 393224 | tf_op jit(solution)/shard_map/cells_2_chunk_1/ppermute | solution.py:378
  18.4 1.2 %standardize.4 = (bf16[1024,1024]{1,0:T(8,128)(2,1)S(1)}, bf16[1024,1024]{1,0:T(8,128)(2,1)S(1)}, bf16[1024,256]{1,0:T(8,128)(2,1)S(1)}) custom-call(f32[8,1024]{1,0:T(8,128)S(1)} %broadcast_in_dim.3.mean_ref, bf16[272,256]{1,0:T(8,128)(2,1)S(1)} %get-tuple-element.53.refs_0_.refs_4_.tail_ref, bf16[272,256]{1,0:T(8,128)(2,1)S(1)} %collective-permute-done.1.refs_1_.refs_5_, ...), custom_call_target="tpu_custom_call" | custom-call | flops 20000000000 | bytes 1024 | tf_op jit(solution)/shard_map/standardize/pallas_call | solution.py:218
  19.6 1.3 %collective-permute-start.7 = (bf16[1024,256]{1,0:T(8,128)(2,1)S(1)}, bf16[1024,256]{1,0:T(8,128)(2,1)S(1)}, u32[]{:S(2)}, u32[]{:S(2)}) collective-permute-start(bf16[1024,256]{1,0:T(8,128)(2,1)S(1)} %get-tuple-element.73), channel_id=1, source_target_pairs={{0,2},{1,3},{2,0},{3,1},{4,6},{5,7},{6,4},{7,5},{8,10},{9,11},{10,... | collective-permute-start | bytes 1572872 | tf_op jit(solution)/shard_map/far_0/ppermute | solution.py:381
  20.9 4.2 %collective-permute-done.2.refs_1_ = bf16[256,256]{1,0:T(8,128)(2,1)S(1)} collective-permute-done((bf16[256,256]{1,0:T(8,128)(2,1)S(1)}, bf16[256,256]{1,0:T(8,128)(2,1)S(1)}, u32[]{:S(2)}, u32[]{:S(2)}) %collective-permute-start.2) | collective-permute-done | bytes 131104 | tf_op jit(solution)/shard_map/cells_3_chunk_1/ppermute | solution.py:378
  25.1 1.4 %collective-permute-start.8 = (bf16[256,256]{1,0:T(8,128)(2,1)S(1)}, bf16[256,256]{1,0:T(8,128)(2,1)S(1)}, u32[]{:S(2)}, u32[]{:S(2)}) collective-permute-start(bf16[256,256]{1,0:T(8,128)(2,1)S(1)} %get-tuple-element.77), channel_id=1, source_target_pairs={{0,12},{4,8},{8,4},{12,0},{1,13},{5,9},{9,5},{13,1},{2,14},{6,10},... | collective-permute-start | bytes 393224 | tf_op jit(solution)/shard_map/cells_3_chunk_2/ppermute | solution.py:378
  26.5 0.0 collective-permute-done.4.refs_2_
  26.5 0.0 collective-permute-start.9
  26.5 3.3 %collective-permute-done.6.refs_3_ = bf16[256,256]{1,0:T(8,128)(2,1)S(1)} collective-permute-done((bf16[256,256]{1,0:T(8,128)(2,1)S(1)}, bf16[256,256]{1,0:T(8,128)(2,1)S(1)}, u32[]{:S(2)}, u32[]{:S(2)}) %collective-permute-start.6) | collective-permute-done | bytes 131104 | tf_op jit(solution)/shard_map/cells_2_chunk_1/ppermute | solution.py:378
  29.8 3.1 %collective-permute-start.10 = (bf16[256,256]{1,0:T(8,128)(2,1)S(1)}, bf16[256,256]{1,0:T(8,128)(2,1)S(1)}, u32[]{:S(2)}, u32[]{:S(2)}) collective-permute-start(bf16[256,256]{1,0:T(8,128)(2,1)S(1)} %get-tuple-element.81), channel_id=1, source_target_pairs={{0,8},{4,12},{8,0},{12,4},{1,9},{5,13},{9,1},{13,5},{2,10},{6,14},... | collective-permute-start | bytes 393224 | tf_op jit(solution)/shard_map/cells_2_chunk_2/ppermute | solution.py:378
  32.9 1.2 %standardize.5 = (bf16[1024,1024]{1,0:T(8,128)(2,1)S(1)}, bf16[1024,1024]{1,0:T(8,128)(2,1)S(1)}, f32[8,128]{1,0:T(8,128)S(1)}, bf16[1024,256]{1,0:T(8,128)(2,1)S(1)}) custom-call(f32[8,1024]{1,0:T(8,128)S(1)} %broadcast_in_dim.3.mean_ref, bf16[256,256]{1,0:T(8,128)(2,1)S(1)} %get-tuple-element.57.refs_0_, ...), custom_call_target="tpu_custom_call", output_to_operand_aliasing={{0}: (9, {}), {1}: (10, {})} | custom-call | flops 20000000000 | bytes 1024 | tf_op jit(solution)/shard_map/standardize/pallas_call | solution.py:218
  34.1 2.7 %collective-permute-start.11 = (bf16[1024,256]{1,0:T(8,128)(2,1)S(1)}, bf16[1024,256]{1,0:T(8,128)(2,1)S(1)}, u32[]{:S(2)}, u32[]{:S(2)}) collective-permute-start(bf16[1024,256]{1,0:T(8,128)(2,1)S(1)} %get-tuple-element.84), channel_id=1, source_target_pairs={{0,2},{1,3},{2,0},{3,1},{4,6},{5,7},{6,4},{7,5},{8,10},{9,11},{10,... | collective-permute-start | bytes 1572872 | tf_op jit(solution)/shard_map/far_1/ppermute | solution.py:381
  36.8 0.8 %collective-permute-start.12 = (bf16[256,256]{1,0:T(8,128)(2,1)S(1)}, bf16[256,256]{1,0:T(8,128)(2,1)S(1)}, u32[]{:S(2)}, u32[]{:S(2)}) collective-permute-start(bf16[256,256]{1,0:T(8,128)(2,1)S(1)} %get-tuple-element.88), channel_id=1, source_target_pairs={{0,12},{4,8},{8,4},{12,0},{1,13},{5,9},{9,5},{13,1},{2,14},{6,10},... | collective-permute-start | bytes 393224 | tf_op jit(solution)/shard_map/cells_3_chunk_3/ppermute | solution.py:378
  37.6 0.4 collective-permute-start.13
  38.0 1.9 %gram.7.refs_4_ = bf16[1,1024,4096]{2,1,0:T(8,128)(2,1)} custom-call(f32[8,128]{1,0:T(8,128)S(1)} %get-tuple-element.69.count_ref, bf16[1024,1024]{1,0:T(8,128)(2,1)S(1)} %get-tuple-element.71.left_ref.refs_8_, bf16[1024,1024]{1,0:T(8,128)(2,1)S(1)} %get-tuple-element.72.refs_0_.refs_9_, bf16[1024,256]{1,0:T(8,128)(2,1)S(1)} %collective-permute-done.7.refs_1_.refs_2_.refs_8_), custom_call_target="tpu_custom_call" | custom-call | flops 1024 | bytes 1024 | tf_op jit(solution)/shard_map/gram/pallas_call | solution.py:340
  39.9 1.1 %collective-permute-done.10.refs_3_ = bf16[256,256]{1,0:T(8,128)(2,1)S(1)} collective-permute-done((bf16[256,256]{1,0:T(8,128)(2,1)S(1)}, bf16[256,256]{1,0:T(8,128)(2,1)S(1)}, u32[]{:S(2)}, u32[]{:S(2)}) %collective-permute-start.10) | collective-permute-done | bytes 131104 | tf_op jit(solution)/shard_map/cells_2_chunk_2/ppermute | solution.py:378
  41.0 3.1 %collective-permute-start.14 = (bf16[256,256]{1,0:T(8,128)(2,1)S(1)}, bf16[256,256]{1,0:T(8,128)(2,1)S(1)}, u32[]{:S(2)}, u32[]{:S(2)}) collective-permute-start(bf16[256,256]{1,0:T(8,128)(2,1)S(1)} %get-tuple-element.92), channel_id=1, source_target_pairs={{0,8},{4,12},{8,0},{12,4},{1,9},{5,13},{9,1},{13,5},{2,10},{6,14},... | collective-permute-start | bytes 393224 | tf_op jit(solution)/shard_map/cells_2_chunk_3/ppermute | solution.py:378
  44.1 1.2 %standardize.6 = (bf16[1024,1024]{1,0:T(8,128)(2,1)S(1)}, bf16[1024,1024]{1,0:T(8,128)(2,1)S(1)}, bf16[1024,256]{1,0:T(8,128)(2,1)S(1)}) custom-call(f32[8,1024]{1,0:T(8,128)S(1)} %broadcast_in_dim.3.mean_ref, bf16[256,256]{1,0:T(8,128)(2,1)S(1)} %get-tuple-element.75.refs_0_, ...), custom_call_target="tpu_custom_call", output_to_operand_aliasing={{0}: (9, {}), {1}: (10, {})} | custom-call | flops 20000000000 | bytes 1024 | tf_op jit(solution)/shard_map/standardize/pallas_call | solution.py:218
  45.3 1.3 %collective-permute-start.18 = (bf16[1024,256]{1,0:T(8,128)(2,1)S(1)}, bf16[1024,256]{1,0:T(8,128)(2,1)S(1)}, u32[]{:S(2)}, u32[]{:S(2)}) collective-permute-start(bf16[1024,256]{1,0:T(8,128)(2,1)S(1)} %get-tuple-element.98), channel_id=1, source_target_pairs={{0,2},{1,3},{2,0},{3,1},{4,6},{5,7},{6,4},{7,5},{8,10},{9,11},{10,... | collective-permute-start | bytes 1572872 | tf_op jit(solution)/shard_map/far_2/ppermute | solution.py:381
  46.6 4.2 %gram.8.refs_2_ = bf16[1,1024,4096]{2,1,0:T(8,128)(2,1)} custom-call(f32[8,128]{1,0:T(8,128)S(1)} %get-tuple-element.69.count_ref, bf16[1024,1024]{1,0:T(8,128)(2,1)S(1)} %get-tuple-element.82.left_ref.refs_10_, bf16[1024,1024]{1,0:T(8,128)(2,1)S(1)} %get-tuple-element.83.refs_0_.refs_1_.refs_11_, ...), custom_call_target="tpu_custom_call", output_to_operand_aliasing={{}: (6, {})} | custom-call | flops 1024 | bytes 1024 | tf_op jit(solution)/shard_map/gram/pallas_call | solution.py:340
  50.9 1.3 %standardize.7 = (bf16[1024,1024]{1,0:T(8,128)(2,1)S(1)}, bf16[1024,1024]{1,0:T(8,128)(2,1)S(1)}, bf16[1024,512]{1,0:T(8,128)(2,1)S(1)}, bf16[784,256]{1,0:T(8,128)(2,1)S(1)}) custom-call(f32[8,1024]{1,0:T(8,128)S(1)} %broadcast_in_dim.3.mean_ref, bf16[256,256]{1,0:T(8,128)(2,1)S(1)} %get-tuple-element.86.refs_0_, ...), custom_call_target="tpu_custom_call", output_to_operand_aliasing={{0}: (11, {}), {1}: (12, {})} | custom-call | flops 20000000000 | bytes 1024 | tf_op jit(solution)/shard_map/standardize/pallas_call | solution.py:218
  52.3 5.8 %collective-permute-start.16 = (bf16[1024,1024]{1,0:T(8,128)(2,1)S(1)}, bf16[1024,1024]{1,0:T(8,128)(2,1)S(1)}, u32[]{:S(2)}, u32[]{:S(2)}) collective-permute-start(bf16[1024,1024]{1,0:T(8,128)(2,1)S(1)} %get-tuple-element.95.refs_0_.refs_1_), channel_id=1, source_target_pairs={{0,1},{1,0},{2,3},{3,2},{4,5},{5,4},{6,7},{7,6},{8,9},{9,8},{10,11... | collective-permute-start | bytes 6291464 | tf_op jit(solution)/shard_map/near/ppermute | solution.py:385
  58.0 2.6 %gram.9.refs_2_ = bf16[1,1024,4096]{2,1,0:T(8,128)(2,1)} custom-call(f32[8,128]{1,0:T(8,128)S(1)} %get-tuple-element.69.count_ref, bf16[1024,1024]{1,0:T(8,128)(2,1)S(1)} %get-tuple-element.93.left_ref, bf16[1024,1024]{1,0:T(8,128)(2,1)S(1)} %get-tuple-element.95.refs_0_.refs_1_, ...), custom_call_target="tpu_custom_call", output_to_operand_aliasing={{}: (4, {})} | custom-call | flops 1024 | bytes 1024 | tf_op jit(solution)/shard_map/gram/pallas_call | solution.py:340
  60.7 0.1 collective-permute-start.15
  60.8 0.3 collective-permute-start.17
  61.1 0.2 collective-permute-start.19
  61.4 1.8 %gram.10.refs_3_ = bf16[1,1024,4096]{2,1,0:T(8,128)(2,1)} custom-call(f32[8,128]{1,0:T(8,128)S(1)} %get-tuple-element.69.count_ref, bf16[1024,1024]{1,0:T(8,128)(2,1)S(1)} %get-tuple-element.93.left_ref, bf16[1024,512]{1,0:T(8,128)(2,1)S(1)} %get-tuple-element.97.refs_0_, ...), custom_call_target="tpu_custom_call", output_to_operand_aliasing={{}: (4, {})} | custom-call | flops 20000000000 | bytes 1024 | tf_op jit(solution)/shard_map/gram/pallas_call | solution.py:340
  63.2 1.1 %collective-permute-done.19.refs_2_ = bf16[1024,256]{1,0:T(8,128)(2,1)S(1)} collective-permute-done((bf16[1024,256]{1,0:T(8,128)(2,1)S(1)}, bf16[1024,256]{1,0:T(8,128)(2,1)S(1)}, u32[]{:S(2)}, u32[]{:S(2)}) %collective-permute-start.19) | collective-permute-done | bytes 524320 | tf_op jit(solution)/shard_map/far_near_2/ppermute | solution.py:385
  64.3 6.1 %gram.11.refs_1_ = bf16[1,1024,4096]{2,1,0:T(8,128)(2,1)} custom-call(f32[8,128]{1,0:T(8,128)S(1)} %get-tuple-element.69.count_ref, bf16[1024,1024]{1,0:T(8,128)(2,1)S(1)} %get-tuple-element.93.left_ref, bf16[1024,1024]{1,0:T(8,128)(2,1)S(1)} %collective-permute-done.16.refs_0_, ...), custom_call_target="tpu_custom_call", output_to_operand_aliasing={{}: (5, {})} | custom-call | flops 1024 | bytes 1024 | tf_op jit(solution)/shard_map/gram/pallas_call | solution.py:340
  70.3 1.3 %collective-permute-done.15.sent_ref = bf16[784,256]{1,0:T(8,128)(2,1)S(1)} collective-permute-done((bf16[784,256]{1,0:T(8,128)(2,1)S(1)}, bf16[784,256]{1,0:T(8,128)(2,1)S(1)}, u32[]{:S(2)}, u32[]{:S(2)}) %collective-permute-start.15) | collective-permute-done | bytes 401440 | tf_op jit(solution)/shard_map/ppermute | solution.py:381
  71.7 0.2 finish.1.refs_0_
  71.9 0.9 %collective-permute-start.20 = (bf16[1024,256]{1,0:T(8,128)(2,1)S(1)}, bf16[1024,256]{1,0:T(8,128)(2,1)S(1)}, u32[]{:S(2)}, u32[]{:S(2)}) collective-permute-start(bf16[1024,256]{1,0:T(8,128)(2,1)S(1)} %finish.1.refs_0_), channel_id=1, source_target_pairs={{0,1},{1,0},{2,3},{3,2},{4,5},{5,4},{6,7},{7,6},{8,9},{9,8},{10,11... | collective-permute-start | bytes 1572872 | tf_op jit(solution)/shard_map/far_near_3/ppermute | solution.py:385
  72.7 1.5 %gram.12.refs_1_ = bf16[1,1024,4096]{2,1,0:T(8,128)(2,1)} custom-call(f32[8,128]{1,0:T(8,128)S(1)} %get-tuple-element.69.count_ref, bf16[1024,1024]{1,0:T(8,128)(2,1)S(1)} %get-tuple-element.93.left_ref, bf16[1024,256]{1,0:T(8,128)(2,1)S(1)} %finish.1.refs_0_, bf16[1,1024,4096]{2,1,0:T(8,128)(2,1)} %gram.11.refs_1_), custom_call_target="tpu_custom_call", output_to_operand_aliasing={{}: (3, {})} | custom-call | flops 1024 | bytes 1024 | tf_op jit(solution)/shard_map/gram/pallas_call | solution.py:340
  74.3 1.5 %gram.13 = bf16[1,1024,4096]{2,1,0:T(8,128)(2,1)} custom-call(f32[8,128]{1,0:T(8,128)S(1)} %get-tuple-element.69.count_ref, bf16[1024,1024]{1,0:T(8,128)(2,1)S(1)} %get-tuple-element.93.left_ref, bf16[1024,256]{1,0:T(8,128)(2,1)S(1)} %collective-permute-done.20.refs_0_, bf16[1,1024,4096]{2,1,0:T(8,128)(2,1)} %gram.12.refs_1_), custom_call_target="tpu_custom_call", output_to_operand_aliasing={{}: (3, {})} | custom-call | flops 1024 | bytes 1024 | tf_op jit(solution)/shard_map/gram/pallas_call | solution.py:340
  (14 shorter events, 0.0 us)
Async XLA Ops:
  0.0 1.2 %copy-start = (bf16[512,1024]{1,0:T(8,128)(2,1)S(1)}, bf16[512,1024]{1,0:T(8,128)(2,1)}, u32[]{:S(2)}) copy-start(bf16[512,1024]{1,0:T(8,128)(2,1)} %expr_ref.1) | copy-start | bytes 3145732
  1.2 0.7 copy-start.1
  1.9 0.7 copy-start.2
  4.3 7.8 %collective-permute-start.1 = (bf16[272,256]{1,0:T(8,128)(2,1)S(1)}, bf16[272,256]{1,0:T(8,128)(2,1)S(1)}, u32[]{:S(2)}, u32[]{:S(2)}) collective-permute-start(bf16[272,256]{1,0:T(8,128)(2,1)S(1)} %get-tuple-element.59), channel_id=1, source_target_pairs={{0,12},{4,8},{8,4},{12,0},{1,13},{5,9},{9,5},{13,1},{2,14},{6,10},... | collective-permute-start | bytes 417800 | tf_op jit(solution)/shard_map/cells_3_chunk_0/ppermute | solution.py:378
  5.7 8.3 %collective-permute-start.3 = (bf16[272,256]{1,0:T(8,128)(2,1)S(1)}, bf16[272,256]{1,0:T(8,128)(2,1)S(1)}, u32[]{:S(2)}, u32[]{:S(2)}) collective-permute-start(bf16[272,256]{1,0:T(8,128)(2,1)S(1)} %get-tuple-element.62), channel_id=1, source_target_pairs={{0,4},{4,0},{8,12},{12,8},{1,5},{5,1},{9,13},{13,9},{2,6},{6,2},{1... | collective-permute-start | bytes 417800 | tf_op jit(solution)/shard_map/cells_1_chunk_0/ppermute | solution.py:378
  7.9 8.4 %collective-permute-start.5 = (bf16[272,256]{1,0:T(8,128)(2,1)S(1)}, bf16[272,256]{1,0:T(8,128)(2,1)S(1)}, u32[]{:S(2)}, u32[]{:S(2)}) collective-permute-start(bf16[272,256]{1,0:T(8,128)(2,1)S(1)} %get-tuple-element.65), channel_id=1, source_target_pairs={{0,8},{4,12},{8,0},{12,4},{1,9},{5,13},{9,1},{13,5},{2,10},{6,14},... | collective-permute-start | bytes 417800 | tf_op jit(solution)/shard_map/cells_2_chunk_0/ppermute | solution.py:378
  7.9 4.1 %collective-permute-start = (bf16[256,256]{1,0:T(8,128)(2,1)S(1)}, bf16[256,256]{1,0:T(8,128)(2,1)S(1)}, u32[]{:S(2)}, u32[]{:S(2)}) collective-permute-start(bf16[256,256]{1,0:T(8,128)(2,1)S(1)} %get-tuple-element.86.refs_0_), channel_id=1, source_target_pairs={{0,2},{1,3},{2,0},{3,1},{4,6},{5,7},{6,4},{7,5},{8,10},{9,11},{10,... | collective-permute-start | bytes 393224 | tf_op jit(solution)/shard_map/far_local/ppermute | solution.py:381
  12.8 12.3 %collective-permute-start.2 = (bf16[256,256]{1,0:T(8,128)(2,1)S(1)}, bf16[256,256]{1,0:T(8,128)(2,1)S(1)}, u32[]{:S(2)}, u32[]{:S(2)}) collective-permute-start(bf16[256,256]{1,0:T(8,128)(2,1)S(1)} %get-tuple-element.60), channel_id=1, source_target_pairs={{0,12},{4,8},{8,4},{12,0},{1,13},{5,9},{9,5},{13,1},{2,14},{6,10},... | collective-permute-start | bytes 393224 | tf_op jit(solution)/shard_map/cells_3_chunk_1/ppermute | solution.py:378
  14.0 12.5 %collective-permute-start.4 = (bf16[256,256]{1,0:T(8,128)(2,1)S(1)}, bf16[256,256]{1,0:T(8,128)(2,1)S(1)}, u32[]{:S(2)}, u32[]{:S(2)}) collective-permute-start(bf16[256,256]{1,0:T(8,128)(2,1)S(1)} %get-tuple-element.63), channel_id=1, source_target_pairs={{0,4},{4,0},{8,12},{12,8},{1,5},{5,1},{9,13},{13,9},{2,6},{6,2},{1... | collective-permute-start | bytes 393224 | tf_op jit(solution)/shard_map/cells_1_chunk_1/ppermute | solution.py:378
  16.2 13.6 %collective-permute-start.6 = (bf16[256,256]{1,0:T(8,128)(2,1)S(1)}, bf16[256,256]{1,0:T(8,128)(2,1)S(1)}, u32[]{:S(2)}, u32[]{:S(2)}) collective-permute-start(bf16[256,256]{1,0:T(8,128)(2,1)S(1)} %get-tuple-element.66), channel_id=1, source_target_pairs={{0,8},{4,12},{8,0},{12,4},{1,9},{5,13},{9,1},{13,5},{2,10},{6,14},... | collective-permute-start | bytes 393224 | tf_op jit(solution)/shard_map/cells_2_chunk_1/ppermute | solution.py:378
  19.6 18.4 %collective-permute-start.7 = (bf16[1024,256]{1,0:T(8,128)(2,1)S(1)}, bf16[1024,256]{1,0:T(8,128)(2,1)S(1)}, u32[]{:S(2)}, u32[]{:S(2)}) collective-permute-start(bf16[1024,256]{1,0:T(8,128)(2,1)S(1)} %get-tuple-element.73), channel_id=1, source_target_pairs={{0,2},{1,3},{2,0},{3,1},{4,6},{5,7},{6,4},{7,5},{8,10},{9,11},{10,... | collective-permute-start | bytes 1572872 | tf_op jit(solution)/shard_map/far_0/ppermute | solution.py:381
  25.1 11.7 %collective-permute-start.8 = (bf16[256,256]{1,0:T(8,128)(2,1)S(1)}, bf16[256,256]{1,0:T(8,128)(2,1)S(1)}, u32[]{:S(2)}, u32[]{:S(2)}) collective-permute-start(bf16[256,256]{1,0:T(8,128)(2,1)S(1)} %get-tuple-element.77), channel_id=1, source_target_pairs={{0,12},{4,8},{8,4},{12,0},{1,13},{5,9},{9,5},{13,1},{2,14},{6,10},... | collective-permute-start | bytes 393224 | tf_op jit(solution)/shard_map/cells_3_chunk_2/ppermute | solution.py:378
  26.5 11.1 %collective-permute-start.9 = (bf16[256,256]{1,0:T(8,128)(2,1)S(1)}, bf16[256,256]{1,0:T(8,128)(2,1)S(1)}, u32[]{:S(2)}, u32[]{:S(2)}) collective-permute-start(bf16[256,256]{1,0:T(8,128)(2,1)S(1)} %get-tuple-element.79), channel_id=1, source_target_pairs={{0,4},{4,0},{8,12},{12,8},{1,5},{5,1},{9,13},{13,9},{2,6},{6,2},{1... | collective-permute-start | bytes 393224 | tf_op jit(solution)/shard_map/cells_1_chunk_2/ppermute | solution.py:378
  29.8 11.2 %collective-permute-start.10 = (bf16[256,256]{1,0:T(8,128)(2,1)S(1)}, bf16[256,256]{1,0:T(8,128)(2,1)S(1)}, u32[]{:S(2)}, u32[]{:S(2)}) collective-permute-start(bf16[256,256]{1,0:T(8,128)(2,1)S(1)} %get-tuple-element.81), channel_id=1, source_target_pairs={{0,8},{4,12},{8,0},{12,4},{1,9},{5,13},{9,1},{13,5},{2,10},{6,14},... | collective-permute-start | bytes 393224 | tf_op jit(solution)/shard_map/cells_2_chunk_2/ppermute | solution.py:378
  34.1 12.5 %collective-permute-start.11 = (bf16[1024,256]{1,0:T(8,128)(2,1)S(1)}, bf16[1024,256]{1,0:T(8,128)(2,1)S(1)}, u32[]{:S(2)}, u32[]{:S(2)}) collective-permute-start(bf16[1024,256]{1,0:T(8,128)(2,1)S(1)} %get-tuple-element.84), channel_id=1, source_target_pairs={{0,2},{1,3},{2,0},{3,1},{4,6},{5,7},{6,4},{7,5},{8,10},{9,11},{10,... | collective-permute-start | bytes 1572872 | tf_op jit(solution)/shard_map/far_1/ppermute | solution.py:381
  36.8 14.1 %collective-permute-start.12 = (bf16[256,256]{1,0:T(8,128)(2,1)S(1)}, bf16[256,256]{1,0:T(8,128)(2,1)S(1)}, u32[]{:S(2)}, u32[]{:S(2)}) collective-permute-start(bf16[256,256]{1,0:T(8,128)(2,1)S(1)} %get-tuple-element.88), channel_id=1, source_target_pairs={{0,12},{4,8},{8,4},{12,0},{1,13},{5,9},{9,5},{13,1},{2,14},{6,10},... | collective-permute-start | bytes 393224 | tf_op jit(solution)/shard_map/cells_3_chunk_3/ppermute | solution.py:378
  37.6 13.3 %collective-permute-start.13 = (bf16[256,256]{1,0:T(8,128)(2,1)S(1)}, bf16[256,256]{1,0:T(8,128)(2,1)S(1)}, u32[]{:S(2)}, u32[]{:S(2)}) collective-permute-start(bf16[256,256]{1,0:T(8,128)(2,1)S(1)} %get-tuple-element.90), channel_id=1, source_target_pairs={{0,4},{4,0},{8,12},{12,8},{1,5},{5,1},{9,13},{13,9},{2,6},{6,2},{1... | collective-permute-start | bytes 393224 | tf_op jit(solution)/shard_map/cells_1_chunk_3/ppermute | solution.py:378
  41.0 9.9 %collective-permute-start.14 = (bf16[256,256]{1,0:T(8,128)(2,1)S(1)}, bf16[256,256]{1,0:T(8,128)(2,1)S(1)}, u32[]{:S(2)}, u32[]{:S(2)}) collective-permute-start(bf16[256,256]{1,0:T(8,128)(2,1)S(1)} %get-tuple-element.92), channel_id=1, source_target_pairs={{0,8},{4,12},{8,0},{12,4},{1,9},{5,13},{9,1},{13,5},{2,10},{6,14},... | collective-permute-start | bytes 393224 | tf_op jit(solution)/shard_map/cells_2_chunk_3/ppermute | solution.py:378
  45.3 15.8 %collective-permute-start.18 = (bf16[1024,256]{1,0:T(8,128)(2,1)S(1)}, bf16[1024,256]{1,0:T(8,128)(2,1)S(1)}, u32[]{:S(2)}, u32[]{:S(2)}) collective-permute-start(bf16[1024,256]{1,0:T(8,128)(2,1)S(1)} %get-tuple-element.98), channel_id=1, source_target_pairs={{0,2},{1,3},{2,0},{3,1},{4,6},{5,7},{6,4},{7,5},{8,10},{9,11},{10,... | collective-permute-start | bytes 1572872 | tf_op jit(solution)/shard_map/far_2/ppermute | solution.py:381
  52.3 12.0 %collective-permute-start.16 = (bf16[1024,1024]{1,0:T(8,128)(2,1)S(1)}, bf16[1024,1024]{1,0:T(8,128)(2,1)S(1)}, u32[]{:S(2)}, u32[]{:S(2)}) collective-permute-start(bf16[1024,1024]{1,0:T(8,128)(2,1)S(1)} %get-tuple-element.95.refs_0_.refs_1_), channel_id=1, source_target_pairs={{0,1},{1,0},{2,3},{3,2},{4,5},{5,4},{6,7},{7,6},{8,9},{9,8},{10,11... | collective-permute-start | bytes 6291464 | tf_op jit(solution)/shard_map/near/ppermute | solution.py:385
  60.7 11.0 %collective-permute-start.15 = (bf16[784,256]{1,0:T(8,128)(2,1)S(1)}, bf16[784,256]{1,0:T(8,128)(2,1)S(1)}, u32[]{:S(2)}, u32[]{:S(2)}) collective-permute-start(bf16[784,256]{1,0:T(8,128)(2,1)S(1)} %get-tuple-element.96), channel_id=1, source_target_pairs={{0,2},{1,3},{2,0},{3,1},{4,6},{5,7},{6,4},{7,5},{8,10},{9,11},{10,... | collective-permute-start | bytes 1204232 | tf_op jit(solution)/shard_map/ppermute | solution.py:381
  60.8 3.4 %collective-permute-start.17 = (bf16[1024,512]{1,0:T(8,128)(2,1)S(1)}, bf16[1024,512]{1,0:T(8,128)(2,1)S(1)}, u32[]{:S(2)}, u32[]{:S(2)}) collective-permute-start(bf16[1024,512]{1,0:T(8,128)(2,1)S(1)} %get-tuple-element.97.refs_0_), channel_id=1, source_target_pairs={{0,1},{1,0},{2,3},{3,2},{4,5},{5,4},{6,7},{7,6},{8,9},{9,8},{10,11... | collective-permute-start | bytes 3145736 | tf_op jit(solution)/shard_map/far_near/ppermute | solution.py:385
  61.1 3.1 %collective-permute-start.19 = (bf16[1024,256]{1,0:T(8,128)(2,1)S(1)}, bf16[1024,256]{1,0:T(8,128)(2,1)S(1)}, u32[]{:S(2)}, u32[]{:S(2)}) collective-permute-start(bf16[1024,256]{1,0:T(8,128)(2,1)S(1)} %collective-permute-done.18.refs_1_), channel_id=1, source_target_pairs={{0,1},{1,0},{2,3},{3,2},{4,5},{5,4},{6,7},{7,6},{8,9},{9,8},{10,11... | collective-permute-start | bytes 1572872 | tf_op jit(solution)/shard_map/far_near_2/ppermute | solution.py:385
  71.9 2.4 %collective-permute-start.20 = (bf16[1024,256]{1,0:T(8,128)(2,1)S(1)}, bf16[1024,256]{1,0:T(8,128)(2,1)S(1)}, u32[]{:S(2)}, u32[]{:S(2)}) collective-permute-start(bf16[1024,256]{1,0:T(8,128)(2,1)S(1)} %finish.1.refs_0_), channel_id=1, source_target_pairs={{0,1},{1,0},{2,3},{3,2},{4,5},{5,4},{6,7},{7,6},{8,9},{9,8},{10,11... | collective-permute-start | bytes 1572872 | tf_op jit(solution)/shard_map/far_near_3/ppermute | solution.py:385

commit v22 on v20

--- a/solution.py
+++ b/solution.py
@@ -266,7 +266,11 @@
     )(sent, local, first)
 
 
-def gram_kernel(blocks, cores, strip, groups, arrays, count_ref, left_ref, *refs):
+def strip_rows(width, rows):
+    return rows if width <= 512 or rows <= 768 else 512
+
+
+def gram_kernel(blocks, cores, groups, arrays, count_ref, left_ref, *refs):
     sources = refs[:arrays]
     out_ref, joined, tile, join_sems, sems = refs[-5:]
     rows, slots = left_ref.shape
@@ -297,6 +301,7 @@
         owner = lax.rem(me + (blocks - chip * cores), blocks)
         owner = jnp.bitwise_xor(owner, flip)
         column = pl.multiple_of(owner * rows + first, 128)
+        strip = strip_rows(width, high - low)
         for row in range(low, high, strip):
             size = min(strip, high - row)
             slot = len(stores) % 2
@@ -331,20 +336,19 @@
         arrays += panels
     joined = [array for panels, _ in groups if len(panels) > 1 for array in panels]
     widest = max(sum(array.shape[1] for array in panels) for panels, _ in groups)
-    strip = min(rows, 512 if widest > 512 else 1024)
     args = [count, left, *arrays]
     specs = [whole] * len(args)
     if before is not None:
         args.append(before)
         specs.append(anywhere)
     return pl.pallas_call(
-        functools.partial(gram_kernel, blocks, cores, strip, layout, len(arrays)),
+        functools.partial(gram_kernel, blocks, cores, layout, len(arrays)),
         in_specs=specs,
         out_specs=anywhere,
         out_shape=jax.ShapeDtypeStruct((1, rows, rows * blocks), jnp.bfloat16),
         scratch_shapes=[
             pltpu.VMEM((slots, max(sum(array.shape[1] for array in joined), 128)), jnp.bfloat16),
-            pltpu.VMEM((2, strip, widest), jnp.bfloat16),
+            pltpu.VMEM((2, rows, widest), jnp.bfloat16),
             pltpu.SemaphoreType.DMA((max(len(joined), 1),)),
             pltpu.SemaphoreType.DMA((2,)),
         ],

time: 75.1 us -> 74.5 us (level)
  no operation moved by 1% of the time
where the time goes in v22:
time: 74.5 us; the launch traced here: 74.2 us
  starting transfers between devices  27.2 us (37%)
  Pallas kernels  23.3 us (31%)
  waiting for transfers between devices  20.2 us (27%)
  local copies, waits for them, and re-layouts  3.27 us (4%)
    ppermute x12, starting transfers between devices, swap(): return lax.ppermute(block, 'cells', [(s, s ^ by) for s in range(types)])  18.3 us
    pallas_call x6, Pallas kernels, gram(): pl.pallas_call(functools.partial(gram_kernel, blocks, cores, layout, len(...  16.4 us
    ppermute x12, waiting for transfers between devices, swap(): return lax.ppermute(block, 'cells', [(s, s ^ by) for s in range(types)])  16 us
    ppermute x5, starting transfers between devices, across(): lax.ppermute(panel_, 'blk', [(b, (b + by * cores) % blocks) for b in rang...  7.8 us
    pallas_call x4, Pallas kernels, standardize(): pl.pallas_call(functools.partial(standardize_kernel, types, cap, lead, se...  4.96 us
    ppermute x5, waiting for transfers between devices, across(): lax.ppermute(panel_, 'blk', [(b, (b + by * cores) % blocks) for b in rang...  4.11 us
    unnamed x6, local copies, waits for them, and re-layouts  2.58 us
    pallas_call x1, Pallas kernels, pack(): pl.pallas_call(functools.partial(pack_kernel, types, cap, widths), out_sh...  1.71 us
  transfers between devices with their start and end apart: 21, of which 7 were waited for; matrix products, arithmetic and copies ran while one was open for 1% of the time, Pallas kernels for 27%

profile of v22, /device:TPU:0, one launch (start us, length us, event | category | flops | bytes accessed | tf_op | source)
XLA Modules:
  0.0 74.2 jit_solution(3298419987548716704)
XLA Ops:
  0.0 1.2 %copy-done = bf16[512,1024]{1,0:T(8,128)(2,1)S(1)} copy-done((bf16[512,1024]{1,0:T(8,128)(2,1)S(1)}, bf16[512,1024]{1,0:T(8,128)(2,1)}, u32[]{:S(2)}) %copy-start) | copy-done | bytes 1048600
  1.2 0.7 copy-done.1
  1.9 0.7 copy-done.2
  2.6 1.7 %pack.1 = (bf16[272,256]{1,0:T(8,128)(2,1)S(1)}, bf16[272,256]{1,0:T(8,128)(2,1)S(1)}, bf16[272,256]{1,0:T(8,128)(2,1)S(1)}, bf16[272,256]{1,0:T(8,128)(2,1)S(1)...) custom-call(s32[512]{0:T(512)S(1)} %copy-done.1, ...), custom_call_target="tpu_custom_call" | custom-call | flops 1024 | bytes 1024 | tf_op jit(solution)/shard_map/pack/pallas_call | solution.py:68
  4.3 5.1 %collective-permute-start = (bf16[272,256]{1,0:T(8,128)(2,1)S(1)}, bf16[272,256]{1,0:T(8,128)(2,1)S(1)}, u32[]{:S(2)}, u32[]{:S(2)}) collective-permute-start(bf16[272,256]{1,0:T(8,128)(2,1)S(1)} %get-tuple-element.55), channel_id=1, source_target_pairs={{0,12},{4,8},{8,4},{12,0},{1,13},{5,9},{9,5},{13,1},{2,14},{6,10},... | collective-permute-start | bytes 417800 | tf_op jit(solution)/shard_map/cells_3_chunk_0/ppermute | solution.py:382
  9.4 0.0 collective-permute-start.1
  9.4 0.6 collective-permute-start.2
  10.1 1.6 %collective-permute-start.10 = (bf16[256,256]{1,0:T(8,128)(2,1)S(1)}, bf16[256,256]{1,0:T(8,128)(2,1)S(1)}, u32[]{:S(2)}, u32[]{:S(2)}) collective-permute-start(bf16[256,256]{1,0:T(8,128)(2,1)S(1)} %get-tuple-element.84.refs_0_), channel_id=1, source_target_pairs={{0,2},{1,3},{2,0},{3,1},{4,6},{5,7},{6,4},{7,5},{8,10},{9,11},{10,... | collective-permute-start | bytes 393224 | tf_op jit(solution)/shard_map/far_local/ppermute | solution.py:385
  11.7 3.3 %collective-permute-done.10.local_ref = bf16[256,256]{1,0:T(8,128)(2,1)S(1)} collective-permute-done((bf16[256,256]{1,0:T(8,128)(2,1)S(1)}, bf16[256,256]{1,0:T(8,128)(2,1)S(1)}, u32[]{:S(2)}, u32[]{:S(2)}) %collective-permute-start.10) | collective-permute-done | bytes 131104 | tf_op jit(solution)/shard_map/far_local/ppermute | solution.py:385
  15.0 0.0 collective-permute-done.refs_1_.refs_5_
  15.0 0.7 broadcast_in_dim.3.mean_ref
  15.7 3.7 %collective-permute-start.4 = (bf16[256,256]{1,0:T(8,128)(2,1)S(1)}, bf16[256,256]{1,0:T(8,128)(2,1)S(1)}, u32[]{:S(2)}, u32[]{:S(2)}) collective-permute-start(bf16[256,256]{1,0:T(8,128)(2,1)S(1)} %get-tuple-element.62), channel_id=1, source_target_pairs={{0,12},{4,8},{8,4},{12,0},{1,13},{5,9},{9,5},{13,1},{2,14},{6,10},... | collective-permute-start | bytes 393224 | tf_op jit(solution)/shard_map/cells_3_chunk_1/ppermute | solution.py:382
  19.5 6.9 %collective-permute-done.2.refs_3_.refs_7_ = bf16[272,256]{1,0:T(8,128)(2,1)S(1)} collective-permute-done((bf16[272,256]{1,0:T(8,128)(2,1)S(1)}, bf16[272,256]{1,0:T(8,128)(2,1)S(1)}, u32[]{:S(2)}, u32[]{:S(2)}) %collective-permute-start.2) | collective-permute-done | bytes 139296 | tf_op jit(solution)/shard_map/cells_2_chunk_0/ppermute | solution.py:382
  26.4 1.2 %standardize.4 = (bf16[1024,1024]{1,0:T(8,128)(2,1)S(1)}, bf16[1024,1024]{1,0:T(8,128)(2,1)S(1)}, bf16[1024,256]{1,0:T(8,128)(2,1)S(1)}) custom-call(f32[8,1024]{1,0:T(8,128)S(1)} %broadcast_in_dim.3.mean_ref, bf16[272,256]{1,0:T(8,128)(2,1)S(1)} %get-tuple-element.52.refs_0_.refs_4_.tail_ref, bf16[272,256]{1,0:T(8,128)(2,1)S(1)} %collective-permute-done.refs_1_.refs_5_, ...), custom_call_target="tpu_custom_call" | custom-call | flops 20000000000 | bytes 1024 | tf_op jit(solution)/shard_map/standardize/pallas_call | solution.py:218
  27.6 1.6 %collective-permute-start.3 = (bf16[1024,256]{1,0:T(8,128)(2,1)S(1)}, bf16[1024,256]{1,0:T(8,128)(2,1)S(1)}, u32[]{:S(2)}, u32[]{:S(2)}) collective-permute-start(bf16[1024,256]{1,0:T(8,128)(2,1)S(1)} %get-tuple-element.58), channel_id=1, source_target_pairs={{0,2},{1,3},{2,0},{3,1},{4,6},{5,7},{6,4},{7,5},{8,10},{9,11},{10,... | collective-permute-start | bytes 1572872 | tf_op jit(solution)/shard_map/far_0/ppermute | solution.py:385
  29.2 3.3 %collective-permute-done.8.refs_3_ = bf16[256,256]{1,0:T(8,128)(2,1)S(1)} collective-permute-done((bf16[256,256]{1,0:T(8,128)(2,1)S(1)}, bf16[256,256]{1,0:T(8,128)(2,1)S(1)}, u32[]{:S(2)}, u32[]{:S(2)}) %collective-permute-start.8) | collective-permute-done | bytes 131104 | tf_op jit(solution)/shard_map/cells_2_chunk_1/ppermute | solution.py:382
  32.5 0.0 collective-permute-start.9
  32.5 0.0 collective-permute-done.6.refs_2_
  32.5 3.0 %collective-permute-start.7 = (bf16[256,256]{1,0:T(8,128)(2,1)S(1)}, bf16[256,256]{1,0:T(8,128)(2,1)S(1)}, u32[]{:S(2)}, u32[]{:S(2)}) collective-permute-start(bf16[256,256]{1,0:T(8,128)(2,1)S(1)} %get-tuple-element.67), channel_id=1, source_target_pairs={{0,4},{4,0},{8,12},{12,8},{1,5},{5,1},{9,13},{13,9},{2,6},{6,2},{1... | collective-permute-start | bytes 393224 | tf_op jit(solution)/shard_map/cells_1_chunk_2/ppermute | solution.py:382
  35.5 1.4 %collective-permute-start.5 = (bf16[256,256]{1,0:T(8,128)(2,1)S(1)}, bf16[256,256]{1,0:T(8,128)(2,1)S(1)}, u32[]{:S(2)}, u32[]{:S(2)}) collective-permute-start(bf16[256,256]{1,0:T(8,128)(2,1)S(1)} %get-tuple-element.63), channel_id=1, source_target_pairs={{0,12},{4,8},{8,4},{12,0},{1,13},{5,9},{9,5},{13,1},{2,14},{6,10},... | collective-permute-start | bytes 393224 | tf_op jit(solution)/shard_map/cells_3_chunk_2/ppermute | solution.py:382
  36.9 1.2 %standardize.5 = (bf16[1024,1024]{1,0:T(8,128)(2,1)S(1)}, bf16[1024,1024]{1,0:T(8,128)(2,1)S(1)}, bf16[1024,256]{1,0:T(8,128)(2,1)S(1)}) custom-call(f32[8,1024]{1,0:T(8,128)S(1)} %broadcast_in_dim.3.mean_ref, bf16[256,256]{1,0:T(8,128)(2,1)S(1)} %get-tuple-element.74.refs_0_, ...), custom_call_target="tpu_custom_call", output_to_operand_aliasing={{0}: (9, {}), {1}: (10, {})} | custom-call | flops 20000000000 | bytes 1024 | tf_op jit(solution)/shard_map/standardize/pallas_call | solution.py:218
  38.1 1.6 %collective-permute-start.11 = (bf16[1024,256]{1,0:T(8,128)(2,1)S(1)}, bf16[1024,256]{1,0:T(8,128)(2,1)S(1)}, u32[]{:S(2)}, u32[]{:S(2)}) collective-permute-start(bf16[1024,256]{1,0:T(8,128)(2,1)S(1)} %get-tuple-element.80), channel_id=1, source_target_pairs={{0,2},{1,3},{2,0},{3,1},{4,6},{5,7},{6,4},{7,5},{8,10},{9,11},{10,... | collective-permute-start | bytes 1572872 | tf_op jit(solution)/shard_map/far_1/ppermute | solution.py:385
  39.6 5.6 %collective-permute-done.9.refs_3_ = bf16[256,256]{1,0:T(8,128)(2,1)S(1)} collective-permute-done((bf16[256,256]{1,0:T(8,128)(2,1)S(1)}, bf16[256,256]{1,0:T(8,128)(2,1)S(1)}, u32[]{:S(2)}, u32[]{:S(2)}) %collective-permute-start.9) | collective-permute-done | bytes 131104 | tf_op jit(solution)/shard_map/cells_2_chunk_2/ppermute | solution.py:382
  45.2 0.8 %collective-permute-start.13 = (bf16[256,256]{1,0:T(8,128)(2,1)S(1)}, bf16[256,256]{1,0:T(8,128)(2,1)S(1)}, u32[]{:S(2)}, u32[]{:S(2)}) collective-permute-start(bf16[256,256]{1,0:T(8,128)(2,1)S(1)} %get-tuple-element.88), channel_id=1, source_target_pairs={{0,4},{4,0},{8,12},{12,8},{1,5},{5,1},{9,13},{13,9},{2,6},{6,2},{1... | collective-permute-start | bytes 393224 | tf_op jit(solution)/shard_map/cells_1_chunk_3/ppermute | solution.py:382
  46.0 3.6 %collective-permute-start.12 = (bf16[256,256]{1,0:T(8,128)(2,1)S(1)}, bf16[256,256]{1,0:T(8,128)(2,1)S(1)}, u32[]{:S(2)}, u32[]{:S(2)}) collective-permute-start(bf16[256,256]{1,0:T(8,128)(2,1)S(1)} %get-tuple-element.86), channel_id=1, source_target_pairs={{0,12},{4,8},{8,4},{12,0},{1,13},{5,9},{9,5},{13,1},{2,14},{6,10},... | collective-permute-start | bytes 393224 | tf_op jit(solution)/shard_map/cells_3_chunk_3/ppermute | solution.py:382
  49.6 0.0 collective-permute-done.3.refs_8_
  49.6 1.2 %standardize.6 = (bf16[1024,1024]{1,0:T(8,128)(2,1)S(1)}, bf16[1024,1024]{1,0:T(8,128)(2,1)S(1)}, f32[8,128]{1,0:T(8,128)S(1)}, bf16[1024,256]{1,0:T(8,128)(2,1)S(1)}) custom-call(f32[8,1024]{1,0:T(8,128)S(1)} %broadcast_in_dim.3.mean_ref, bf16[256,256]{1,0:T(8,128)(2,1)S(1)} %get-tuple-element.59.refs_0_, ...), custom_call_target="tpu_custom_call", output_to_operand_aliasing={{0}: (9, {}), {1}: (10, {})} | custom-call | flops 20000000000 | bytes 1024 | tf_op jit(solution)/shard_map/standardize/pallas_call | solution.py:218
  50.8 1.6 %collective-permute-start.18 = (bf16[1024,256]{1,0:T(8,128)(2,1)S(1)}, bf16[1024,256]{1,0:T(8,128)(2,1)S(1)}, u32[]{:S(2)}, u32[]{:S(2)}) collective-permute-start(bf16[1024,256]{1,0:T(8,128)(2,1)S(1)} %get-tuple-element.96), channel_id=1, source_target_pairs={{0,2},{1,3},{2,0},{3,1},{4,6},{5,7},{6,4},{7,5},{8,10},{9,11},{10,... | collective-permute-start | bytes 1572872 | tf_op jit(solution)/shard_map/far_2/ppermute | solution.py:385
  52.4 2.4 %gram.6.refs_2_ = bf16[1,1024,4096]{2,1,0:T(8,128)(2,1)} custom-call(f32[8,128]{1,0:T(8,128)S(1)} %get-tuple-element.79.count_ref, bf16[1024,1024]{1,0:T(8,128)(2,1)S(1)} %get-tuple-element.82.left_ref.refs_10_, bf16[1024,1024]{1,0:T(8,128)(2,1)S(1)} %get-tuple-element.83.refs_0_.refs_11_), custom_call_target="tpu_custom_call" | custom-call | flops 1024 | bytes 1024 | tf_op jit(solution)/shard_map/gram/pallas_call | solution.py:344
  54.8 0.0 collective-permute-done.11.refs_9_
  54.9 0.2 collective-permute-done.14.refs_3_
  55.1 0.0 collective-permute-done.12.refs_1_
  55.1 1.3 %standardize.7 = (bf16[1024,1024]{1,0:T(8,128)(2,1)S(1)}, bf16[1024,1024]{1,0:T(8,128)(2,1)S(1)}, bf16[1024,512]{1,0:T(8,128)(2,1)S(1)}, bf16[784,256]{1,0:T(8,128)(2,1)S(1)}) custom-call(f32[8,1024]{1,0:T(8,128)S(1)} %broadcast_in_dim.3.mean_ref, bf16[256,256]{1,0:T(8,128)(2,1)S(1)} %get-tuple-element.84.refs_0_, ...), custom_call_target="tpu_custom_call", output_to_operand_aliasing={{0}: (11, {}), {1}: (12, {})} | custom-call | flops 20000000000 | bytes 1024 | tf_op jit(solution)/shard_map/standardize/pallas_call | solution.py:218
  56.4 0.1 collective-permute-start.16
  56.5 1.9 %gram.7.refs_2_ = bf16[1,1024,4096]{2,1,0:T(8,128)(2,1)} custom-call(f32[8,128]{1,0:T(8,128)S(1)} %get-tuple-element.79.count_ref, bf16[1024,1024]{1,0:T(8,128)(2,1)S(1)} %get-tuple-element.91.left_ref, bf16[1024,1024]{1,0:T(8,128)(2,1)S(1)} %get-tuple-element.93.refs_0_.refs_1_, ...), custom_call_target="tpu_custom_call", output_to_operand_aliasing={{}: (4, {})} | custom-call | flops 1024 | bytes 1024 | tf_op jit(solution)/shard_map/gram/pallas_call | solution.py:344
  58.4 0.6 collective-permute-start.17
  59.0 1.5 %collective-permute-start.15 = (bf16[784,256]{1,0:T(8,128)(2,1)S(1)}, bf16[784,256]{1,0:T(8,128)(2,1)S(1)}, u32[]{:S(2)}, u32[]{:S(2)}) collective-permute-start(bf16[784,256]{1,0:T(8,128)(2,1)S(1)} %get-tuple-element.94), channel_id=1, source_target_pairs={{0,2},{1,3},{2,0},{3,1},{4,6},{5,7},{6,4},{7,5},{8,10},{9,11},{10,... | collective-permute-start | bytes 1204232 | tf_op jit(solution)/shard_map/ppermute | solution.py:385
  60.5 0.7 collective-permute-done.18.refs_1_
  61.2 0.0 collective-permute-start.19
  61.2 2.9 %gram.8.refs_3_ = bf16[1,1024,4096]{2,1,0:T(8,128)(2,1)} custom-call(f32[8,128]{1,0:T(8,128)S(1)} %get-tuple-element.79.count_ref, bf16[1024,1024]{1,0:T(8,128)(2,1)S(1)} %get-tuple-element.91.left_ref, bf16[1024,512]{1,0:T(8,128)(2,1)S(1)} %get-tuple-element.95.refs_0_, ...), custom_call_target="tpu_custom_call", output_to_operand_aliasing={{}: (4, {})} | custom-call | flops 20000000000 | bytes 1024 | tf_op jit(solution)/shard_map/gram/pallas_call | solution.py:344
  64.1 0.0 collective-permute-done.19.refs_2_
  64.1 0.0 collective-permute-done.17.refs_1_
  64.1 6.1 %gram.9.refs_1_ = bf16[1,1024,4096]{2,1,0:T(8,128)(2,1)} custom-call(f32[8,128]{1,0:T(8,128)S(1)} %get-tuple-element.79.count_ref, bf16[1024,1024]{1,0:T(8,128)(2,1)S(1)} %get-tuple-element.91.left_ref, bf16[1024,1024]{1,0:T(8,128)(2,1)S(1)} %collective-permute-done.16.refs_0_, ...), custom_call_target="tpu_custom_call", output_to_operand_aliasing={{}: (5, {})} | custom-call | flops 1024 | bytes 1024 | tf_op jit(solution)/shard_map/gram/pallas_call | solution.py:344
  70.2 0.1 collective-permute-done.15.sent_ref
  70.3 0.2 finish.1.refs_0_
  70.5 0.5 collective-permute-start.20
  71.0 1.5 %gram.10.refs_1_ = bf16[1,1024,4096]{2,1,0:T(8,128)(2,1)} custom-call(f32[8,128]{1,0:T(8,128)S(1)} %get-tuple-element.79.count_ref, bf16[1024,1024]{1,0:T(8,128)(2,1)S(1)} %get-tuple-element.91.left_ref, bf16[1024,256]{1,0:T(8,128)(2,1)S(1)} %finish.1.refs_0_, bf16[1,1024,4096]{2,1,0:T(8,128)(2,1)} %gram.9.refs_1_), custom_call_target="tpu_custom_call", output_to_operand_aliasing={{}: (3, {})} | custom-call | flops 1024 | bytes 1024 | tf_op jit(solution)/shard_map/gram/pallas_call | solution.py:344
  72.5 1.5 %gram.11 = bf16[1,1024,4096]{2,1,0:T(8,128)(2,1)} custom-call(f32[8,128]{1,0:T(8,128)S(1)} %get-tuple-element.79.count_ref, bf16[1024,1024]{1,0:T(8,128)(2,1)S(1)} %get-tuple-element.91.left_ref, bf16[1024,256]{1,0:T(8,128)(2,1)S(1)} %collective-permute-done.20.refs_0_, bf16[1,1024,4096]{2,1,0:T(8,128)(2,1)} %gram.10.refs_1_), custom_call_target="tpu_custom_call", output_to_operand_aliasing={{}: (3, {})} | custom-call | flops 1024 | bytes 1024 | tf_op jit(solution)/shard_map/gram/pallas_call | solution.py:344
  (13 shorter events, 0.0 us)
Async XLA Ops:
  0.0 1.2 %copy-start = (bf16[512,1024]{1,0:T(8,128)(2,1)S(1)}, bf16[512,1024]{1,0:T(8,128)(2,1)}, u32[]{:S(2)}) copy-start(bf16[512,1024]{1,0:T(8,128)(2,1)} %expr_ref.1) | copy-start | bytes 3145732
  1.2 0.7 copy-start.1
  1.9 0.7 copy-start.2
  4.3 10.7 %collective-permute-start = (bf16[272,256]{1,0:T(8,128)(2,1)S(1)}, bf16[272,256]{1,0:T(8,128)(2,1)S(1)}, u32[]{:S(2)}, u32[]{:S(2)}) collective-permute-start(bf16[272,256]{1,0:T(8,128)(2,1)S(1)} %get-tuple-element.55), channel_id=1, source_target_pairs={{0,12},{4,8},{8,4},{12,0},{1,13},{5,9},{9,5},{13,1},{2,14},{6,10},... | collective-permute-start | bytes 417800 | tf_op jit(solution)/shard_map/cells_3_chunk_0/ppermute | solution.py:382
  9.4 10.1 %collective-permute-start.1 = (bf16[272,256]{1,0:T(8,128)(2,1)S(1)}, bf16[272,256]{1,0:T(8,128)(2,1)S(1)}, u32[]{:S(2)}, u32[]{:S(2)}) collective-permute-start(bf16[272,256]{1,0:T(8,128)(2,1)S(1)} %get-tuple-element.56), channel_id=1, source_target_pairs={{0,4},{4,0},{8,12},{12,8},{1,5},{5,1},{9,13},{13,9},{2,6},{6,2},{1... | collective-permute-start | bytes 417800 | tf_op jit(solution)/shard_map/cells_1_chunk_0/ppermute | solution.py:382
  9.4 17.0 %collective-permute-start.2 = (bf16[272,256]{1,0:T(8,128)(2,1)S(1)}, bf16[272,256]{1,0:T(8,128)(2,1)S(1)}, u32[]{:S(2)}, u32[]{:S(2)}) collective-permute-start(bf16[272,256]{1,0:T(8,128)(2,1)S(1)} %get-tuple-element.57), channel_id=1, source_target_pairs={{0,8},{4,12},{8,0},{12,4},{1,9},{5,13},{9,1},{13,5},{2,10},{6,14},... | collective-permute-start | bytes 417800 | tf_op jit(solution)/shard_map/cells_2_chunk_0/ppermute | solution.py:382
  10.1 5.0 %collective-permute-start.10 = (bf16[256,256]{1,0:T(8,128)(2,1)S(1)}, bf16[256,256]{1,0:T(8,128)(2,1)S(1)}, u32[]{:S(2)}, u32[]{:S(2)}) collective-permute-start(bf16[256,256]{1,0:T(8,128)(2,1)S(1)} %get-tuple-element.84.refs_0_), channel_id=1, source_target_pairs={{0,2},{1,3},{2,0},{3,1},{4,6},{5,7},{6,4},{7,5},{8,10},{9,11},{10,... | collective-permute-start | bytes 393224 | tf_op jit(solution)/shard_map/far_local/ppermute | solution.py:385
  15.7 19.8 %collective-permute-start.4 = (bf16[256,256]{1,0:T(8,128)(2,1)S(1)}, bf16[256,256]{1,0:T(8,128)(2,1)S(1)}, u32[]{:S(2)}, u32[]{:S(2)}) collective-permute-start(bf16[256,256]{1,0:T(8,128)(2,1)S(1)} %get-tuple-element.62), channel_id=1, source_target_pairs={{0,12},{4,8},{8,4},{12,0},{1,13},{5,9},{9,5},{13,1},{2,14},{6,10},... | collective-permute-start | bytes 393224 | tf_op jit(solution)/shard_map/cells_3_chunk_1/ppermute | solution.py:382
  19.5 13.0 %collective-permute-start.6 = (bf16[256,256]{1,0:T(8,128)(2,1)S(1)}, bf16[256,256]{1,0:T(8,128)(2,1)S(1)}, u32[]{:S(2)}, u32[]{:S(2)}) collective-permute-start(bf16[256,256]{1,0:T(8,128)(2,1)S(1)} %get-tuple-element.66), channel_id=1, source_target_pairs={{0,4},{4,0},{8,12},{12,8},{1,5},{5,1},{9,13},{13,9},{2,6},{6,2},{1... | collective-permute-start | bytes 393224 | tf_op jit(solution)/shard_map/cells_1_chunk_1/ppermute | solution.py:382
  26.4 6.1 %collective-permute-start.8 = (bf16[256,256]{1,0:T(8,128)(2,1)S(1)}, bf16[256,256]{1,0:T(8,128)(2,1)S(1)}, u32[]{:S(2)}, u32[]{:S(2)}) collective-permute-start(bf16[256,256]{1,0:T(8,128)(2,1)S(1)} %get-tuple-element.70), channel_id=1, source_target_pairs={{0,8},{4,12},{8,0},{12,4},{1,9},{5,13},{9,1},{13,5},{2,10},{6,14},... | collective-permute-start | bytes 393224 | tf_op jit(solution)/shard_map/cells_2_chunk_1/ppermute | solution.py:382
  27.6 22.0 %collective-permute-start.3 = (bf16[1024,256]{1,0:T(8,128)(2,1)S(1)}, bf16[1024,256]{1,0:T(8,128)(2,1)S(1)}, u32[]{:S(2)}, u32[]{:S(2)}) collective-permute-start(bf16[1024,256]{1,0:T(8,128)(2,1)S(1)} %get-tuple-element.58), channel_id=1, source_target_pairs={{0,2},{1,3},{2,0},{3,1},{4,6},{5,7},{6,4},{7,5},{8,10},{9,11},{10,... | collective-permute-start | bytes 1572872 | tf_op jit(solution)/shard_map/far_0/ppermute | solution.py:385
  32.5 12.7 %collective-permute-start.9 = (bf16[256,256]{1,0:T(8,128)(2,1)S(1)}, bf16[256,256]{1,0:T(8,128)(2,1)S(1)}, u32[]{:S(2)}, u32[]{:S(2)}) collective-permute-start(bf16[256,256]{1,0:T(8,128)(2,1)S(1)} %get-tuple-element.71), channel_id=1, source_target_pairs={{0,8},{4,12},{8,0},{12,4},{1,9},{5,13},{9,1},{13,5},{2,10},{6,14},... | collective-permute-start | bytes 393224 | tf_op jit(solution)/shard_map/cells_2_chunk_2/ppermute | solution.py:382
  32.5 12.7 %collective-permute-start.7 = (bf16[256,256]{1,0:T(8,128)(2,1)S(1)}, bf16[256,256]{1,0:T(8,128)(2,1)S(1)}, u32[]{:S(2)}, u32[]{:S(2)}) collective-permute-start(bf16[256,256]{1,0:T(8,128)(2,1)S(1)} %get-tuple-element.67), channel_id=1, source_target_pairs={{0,4},{4,0},{8,12},{12,8},{1,5},{5,1},{9,13},{13,9},{2,6},{6,2},{1... | collective-permute-start | bytes 393224 | tf_op jit(solution)/shard_map/cells_1_chunk_2/ppermute | solution.py:382
  35.5 10.5 %collective-permute-start.5 = (bf16[256,256]{1,0:T(8,128)(2,1)S(1)}, bf16[256,256]{1,0:T(8,128)(2,1)S(1)}, u32[]{:S(2)}, u32[]{:S(2)}) collective-permute-start(bf16[256,256]{1,0:T(8,128)(2,1)S(1)} %get-tuple-element.63), channel_id=1, source_target_pairs={{0,12},{4,8},{8,4},{12,0},{1,13},{5,9},{9,5},{13,1},{2,14},{6,10},... | collective-permute-start | bytes 393224 | tf_op jit(solution)/shard_map/cells_3_chunk_2/ppermute | solution.py:382
  38.1 16.8 %collective-permute-start.11 = (bf16[1024,256]{1,0:T(8,128)(2,1)S(1)}, bf16[1024,256]{1,0:T(8,128)(2,1)S(1)}, u32[]{:S(2)}, u32[]{:S(2)}) collective-permute-start(bf16[1024,256]{1,0:T(8,128)(2,1)S(1)} %get-tuple-element.80), channel_id=1, source_target_pairs={{0,2},{1,3},{2,0},{3,1},{4,6},{5,7},{6,4},{7,5},{8,10},{9,11},{10,... | collective-permute-start | bytes 1572872 | tf_op jit(solution)/shard_map/far_1/ppermute | solution.py:385
  45.2 9.9 %collective-permute-start.14 = (bf16[256,256]{1,0:T(8,128)(2,1)S(1)}, bf16[256,256]{1,0:T(8,128)(2,1)S(1)}, u32[]{:S(2)}, u32[]{:S(2)}) collective-permute-start(bf16[256,256]{1,0:T(8,128)(2,1)S(1)} %get-tuple-element.90), channel_id=1, source_target_pairs={{0,8},{4,12},{8,0},{12,4},{1,9},{5,13},{9,1},{13,5},{2,10},{6,14},... | collective-permute-start | bytes 393224 | tf_op jit(solution)/shard_map/cells_2_chunk_3/ppermute | solution.py:382
  45.2 9.9 %collective-permute-start.13 = (bf16[256,256]{1,0:T(8,128)(2,1)S(1)}, bf16[256,256]{1,0:T(8,128)(2,1)S(1)}, u32[]{:S(2)}, u32[]{:S(2)}) collective-permute-start(bf16[256,256]{1,0:T(8,128)(2,1)S(1)} %get-tuple-element.88), channel_id=1, source_target_pairs={{0,4},{4,0},{8,12},{12,8},{1,5},{5,1},{9,13},{13,9},{2,6},{6,2},{1... | collective-permute-start | bytes 393224 | tf_op jit(solution)/shard_map/cells_1_chunk_3/ppermute | solution.py:382
  46.0 9.1 %collective-permute-start.12 = (bf16[256,256]{1,0:T(8,128)(2,1)S(1)}, bf16[256,256]{1,0:T(8,128)(2,1)S(1)}, u32[]{:S(2)}, u32[]{:S(2)}) collective-permute-start(bf16[256,256]{1,0:T(8,128)(2,1)S(1)} %get-tuple-element.86), channel_id=1, source_target_pairs={{0,12},{4,8},{8,4},{12,0},{1,13},{5,9},{9,5},{13,1},{2,14},{6,10},... | collective-permute-start | bytes 393224 | tf_op jit(solution)/shard_map/cells_3_chunk_3/ppermute | solution.py:382
  50.8 10.4 %collective-permute-start.18 = (bf16[1024,256]{1,0:T(8,128)(2,1)S(1)}, bf16[1024,256]{1,0:T(8,128)(2,1)S(1)}, u32[]{:S(2)}, u32[]{:S(2)}) collective-permute-start(bf16[1024,256]{1,0:T(8,128)(2,1)S(1)} %get-tuple-element.96), channel_id=1, source_target_pairs={{0,2},{1,3},{2,0},{3,1},{4,6},{5,7},{6,4},{7,5},{8,10},{9,11},{10,... | collective-permute-start | bytes 1572872 | tf_op jit(solution)/shard_map/far_2/ppermute | solution.py:385
  56.4 7.7 %collective-permute-start.16 = (bf16[1024,1024]{1,0:T(8,128)(2,1)S(1)}, bf16[1024,1024]{1,0:T(8,128)(2,1)S(1)}, u32[]{:S(2)}, u32[]{:S(2)}) collective-permute-start(bf16[1024,1024]{1,0:T(8,128)(2,1)S(1)} %get-tuple-element.93.refs_0_.refs_1_), channel_id=1, source_target_pairs={{0,1},{1,0},{2,3},{3,2},{4,5},{5,4},{6,7},{7,6},{8,9},{9,8},{10,11... | collective-permute-start | bytes 6291464 | tf_op jit(solution)/shard_map/near/ppermute | solution.py:389
  58.4 5.7 %collective-permute-start.17 = (bf16[1024,512]{1,0:T(8,128)(2,1)S(1)}, bf16[1024,512]{1,0:T(8,128)(2,1)S(1)}, u32[]{:S(2)}, u32[]{:S(2)}) collective-permute-start(bf16[1024,512]{1,0:T(8,128)(2,1)S(1)} %get-tuple-element.95.refs_0_), channel_id=1, source_target_pairs={{0,1},{1,0},{2,3},{3,2},{4,5},{5,4},{6,7},{7,6},{8,9},{9,8},{10,11... | collective-permute-start | bytes 3145736 | tf_op jit(solution)/shard_map/far_near/ppermute | solution.py:389
  59.0 11.3 %collective-permute-start.15 = (bf16[784,256]{1,0:T(8,128)(2,1)S(1)}, bf16[784,256]{1,0:T(8,128)(2,1)S(1)}, u32[]{:S(2)}, u32[]{:S(2)}) collective-permute-start(bf16[784,256]{1,0:T(8,128)(2,1)S(1)} %get-tuple-element.94), channel_id=1, source_target_pairs={{0,2},{1,3},{2,0},{3,1},{4,6},{5,7},{6,4},{7,5},{8,10},{9,11},{10,... | collective-permute-start | bytes 1204232 | tf_op jit(solution)/shard_map/ppermute | solution.py:385
  61.2 2.9 %collective-permute-start.19 = (bf16[1024,256]{1,0:T(8,128)(2,1)S(1)}, bf16[1024,256]{1,0:T(8,128)(2,1)S(1)}, u32[]{:S(2)}, u32[]{:S(2)}) collective-permute-start(bf16[1024,256]{1,0:T(8,128)(2,1)S(1)} %collective-permute-done.18.refs_1_), channel_id=1, source_target_pairs={{0,1},{1,0},{2,3},{3,2},{4,5},{5,4},{6,7},{7,6},{8,9},{9,8},{10,11... | collective-permute-start | bytes 1572872 | tf_op jit(solution)/shard_map/far_near_2/ppermute | solution.py:389
  70.5 2.1 %collective-permute-start.20 = (bf16[1024,256]{1,0:T(8,128)(2,1)S(1)}, bf16[1024,256]{1,0:T(8,128)(2,1)S(1)}, u32[]{:S(2)}, u32[]{:S(2)}) collective-permute-start(bf16[1024,256]{1,0:T(8,128)(2,1)S(1)} %finish.1.refs_0_), channel_id=1, source_target_pairs={{0,1},{1,0},{2,3},{3,2},{4,5},{5,4},{6,7},{7,6},{8,9},{9,8},{10,11... | collective-permute-start | bytes 1572872 | tf_op jit(solution)/shard_map/far_near_3/ppermute | solution.py:389

commit v23 on v22

--- a/solution.py
+++ b/solution.py
@@ -267,7 +267,7 @@
 
 
 def strip_rows(width, rows):
-    return rows if width <= 512 or rows <= 768 else 512
+    return rows if width <= 512 else 512
 
 
 def gram_kernel(blocks, cores, groups, arrays, count_ref, left_ref, *refs):

time: 74.5 us -> 74.5 us (level)
  transfers between devices with their start and end apart: 21 -> 21, of which waited for: 7 -> 7; matrix products, arithmetic and copies ran while one was open for 1% -> 1% of each run, Pallas kernels for 27% -> 26%
where the time goes in v23:
time: 74.5 us; the launch traced here: 74.2 us
  starting transfers between devices  27.2 us (37%)
  Pallas kernels  23 us (31%)
  waiting for transfers between devices  20.4 us (27%)
  local copies, waits for them, and re-layouts  3.27 us (4%)
    ppermute x12, starting transfers between devices, swap(): return lax.ppermute(block, 'cells', [(s, s ^ by) for s in range(types)])  18.3 us
    ppermute x12, waiting for transfers between devices, swap(): return lax.ppermute(block, 'cells', [(s, s ^ by) for s in range(types)])  16.3 us
    pallas_call x6, Pallas kernels, gram(): pl.pallas_call(functools.partial(gram_kernel, blocks, cores, layout, len(...  16.1 us
    ppermute x5, starting transfers between devices, across(): lax.ppermute(panel_, 'blk', [(b, (b + by * cores) % blocks) for b in rang...  7.8 us
    pallas_call x4, Pallas kernels, standardize(): pl.pallas_call(functools.partial(standardize_kernel, types, cap, lead, se...  4.96 us
    ppermute x5, waiting for transfers between devices, across(): lax.ppermute(panel_, 'blk', [(b, (b + by * cores) % blocks) for b in rang...  4.11 us
    unnamed x6, local copies, waits for them, and re-layouts  2.58 us
    pallas_call x1, Pallas kernels, pack(): pl.pallas_call(functools.partial(pack_kernel, types, cap, widths), out_sh...  1.71 us
  transfers between devices with their start and end apart: 21, of which 7 were waited for; matrix products, arithmetic and copies ran while one was open for 1% of the time, Pallas kernels for 26%

profile of v23, /device:TPU:0, one launch (start us, length us, event | category | flops | bytes accessed | tf_op | source)
XLA Modules:
  0.0 74.2 jit_solution(4657171528768183488)
XLA Ops:
  0.0 1.2 %copy-done = bf16[512,1024]{1,0:T(8,128)(2,1)S(1)} copy-done((bf16[512,1024]{1,0:T(8,128)(2,1)S(1)}, bf16[512,1024]{1,0:T(8,128)(2,1)}, u32[]{:S(2)}) %copy-start) | copy-done | bytes 1048600
  1.2 0.7 copy-done.1
  1.9 0.7 copy-done.2
  2.6 1.7 %pack.1 = (bf16[272,256]{1,0:T(8,128)(2,1)S(1)}, bf16[272,256]{1,0:T(8,128)(2,1)S(1)}, bf16[272,256]{1,0:T(8,128)(2,1)S(1)}, bf16[272,256]{1,0:T(8,128)(2,1)S(1)...) custom-call(s32[512]{0:T(512)S(1)} %copy-done.1, ...), custom_call_target="tpu_custom_call" | custom-call | flops 1024 | bytes 1024 | tf_op jit(solution)/shard_map/pack/pallas_call | solution.py:68
  4.3 5.1 %collective-permute-start = (bf16[272,256]{1,0:T(8,128)(2,1)S(1)}, bf16[272,256]{1,0:T(8,128)(2,1)S(1)}, u32[]{:S(2)}, u32[]{:S(2)}) collective-permute-start(bf16[272,256]{1,0:T(8,128)(2,1)S(1)} %get-tuple-element.55), channel_id=1, source_target_pairs={{0,12},{4,8},{8,4},{12,0},{1,13},{5,9},{9,5},{13,1},{2,14},{6,10},... | collective-permute-start | bytes 417800 | tf_op jit(solution)/shard_map/cells_3_chunk_0/ppermute | solution.py:382
  9.4 0.0 collective-permute-start.1
  9.4 0.6 collective-permute-start.2
  10.1 1.6 %collective-permute-start.10 = (bf16[256,256]{1,0:T(8,128)(2,1)S(1)}, bf16[256,256]{1,0:T(8,128)(2,1)S(1)}, u32[]{:S(2)}, u32[]{:S(2)}) collective-permute-start(bf16[256,256]{1,0:T(8,128)(2,1)S(1)} %get-tuple-element.84.refs_0_), channel_id=1, source_target_pairs={{0,2},{1,3},{2,0},{3,1},{4,6},{5,7},{6,4},{7,5},{8,10},{9,11},{10,... | collective-permute-start | bytes 393224 | tf_op jit(solution)/shard_map/far_local/ppermute | solution.py:385
  11.7 3.3 %collective-permute-done.10.local_ref = bf16[256,256]{1,0:T(8,128)(2,1)S(1)} collective-permute-done((bf16[256,256]{1,0:T(8,128)(2,1)S(1)}, bf16[256,256]{1,0:T(8,128)(2,1)S(1)}, u32[]{:S(2)}, u32[]{:S(2)}) %collective-permute-start.10) | collective-permute-done | bytes 131104 | tf_op jit(solution)/shard_map/far_local/ppermute | solution.py:385
  15.0 0.0 collective-permute-done.refs_1_.refs_5_
  15.0 0.7 broadcast_in_dim.3.mean_ref
  15.7 3.7 %collective-permute-start.4 = (bf16[256,256]{1,0:T(8,128)(2,1)S(1)}, bf16[256,256]{1,0:T(8,128)(2,1)S(1)}, u32[]{:S(2)}, u32[]{:S(2)}) collective-permute-start(bf16[256,256]{1,0:T(8,128)(2,1)S(1)} %get-tuple-element.62), channel_id=1, source_target_pairs={{0,12},{4,8},{8,4},{12,0},{1,13},{5,9},{9,5},{13,1},{2,14},{6,10},... | collective-permute-start | bytes 393224 | tf_op jit(solution)/shard_map/cells_3_chunk_1/ppermute | solution.py:382
  19.5 6.9 %collective-permute-done.2.refs_3_.refs_7_ = bf16[272,256]{1,0:T(8,128)(2,1)S(1)} collective-permute-done((bf16[272,256]{1,0:T(8,128)(2,1)S(1)}, bf16[272,256]{1,0:T(8,128)(2,1)S(1)}, u32[]{:S(2)}, u32[]{:S(2)}) %collective-permute-start.2) | collective-permute-done | bytes 139296 | tf_op jit(solution)/shard_map/cells_2_chunk_0/ppermute | solution.py:382
  26.4 1.2 %standardize.4 = (bf16[1024,1024]{1,0:T(8,128)(2,1)S(1)}, bf16[1024,1024]{1,0:T(8,128)(2,1)S(1)}, bf16[1024,256]{1,0:T(8,128)(2,1)S(1)}) custom-call(f32[8,1024]{1,0:T(8,128)S(1)} %broadcast_in_dim.3.mean_ref, bf16[272,256]{1,0:T(8,128)(2,1)S(1)} %get-tuple-element.52.refs_0_.refs_4_.tail_ref, bf16[272,256]{1,0:T(8,128)(2,1)S(1)} %collective-permute-done.refs_1_.refs_5_, ...), custom_call_target="tpu_custom_call" | custom-call | flops 20000000000 | bytes 1024 | tf_op jit(solution)/shard_map/standardize/pallas_call | solution.py:218
  27.6 1.6 %collective-permute-start.3 = (bf16[1024,256]{1,0:T(8,128)(2,1)S(1)}, bf16[1024,256]{1,0:T(8,128)(2,1)S(1)}, u32[]{:S(2)}, u32[]{:S(2)}) collective-permute-start(bf16[1024,256]{1,0:T(8,128)(2,1)S(1)} %get-tuple-element.58), channel_id=1, source_target_pairs={{0,2},{1,3},{2,0},{3,1},{4,6},{5,7},{6,4},{7,5},{8,10},{9,11},{10,... | collective-permute-start | bytes 1572872 | tf_op jit(solution)/shard_map/far_0/ppermute | solution.py:385
  29.2 3.3 %collective-permute-done.8.refs_3_ = bf16[256,256]{1,0:T(8,128)(2,1)S(1)} collective-permute-done((bf16[256,256]{1,0:T(8,128)(2,1)S(1)}, bf16[256,256]{1,0:T(8,128)(2,1)S(1)}, u32[]{:S(2)}, u32[]{:S(2)}) %collective-permute-start.8) | collective-permute-done | bytes 131104 | tf_op jit(solution)/shard_map/cells_2_chunk_1/ppermute | solution.py:382
  32.5 0.0 collective-permute-start.9
  32.5 0.0 collective-permute-done.6.refs_2_
  32.5 3.0 %collective-permute-start.7 = (bf16[256,256]{1,0:T(8,128)(2,1)S(1)}, bf16[256,256]{1,0:T(8,128)(2,1)S(1)}, u32[]{:S(2)}, u32[]{:S(2)}) collective-permute-start(bf16[256,256]{1,0:T(8,128)(2,1)S(1)} %get-tuple-element.67), channel_id=1, source_target_pairs={{0,4},{4,0},{8,12},{12,8},{1,5},{5,1},{9,13},{13,9},{2,6},{6,2},{1... | collective-permute-start | bytes 393224 | tf_op jit(solution)/shard_map/cells_1_chunk_2/ppermute | solution.py:382
  35.5 1.4 %collective-permute-start.5 = (bf16[256,256]{1,0:T(8,128)(2,1)S(1)}, bf16[256,256]{1,0:T(8,128)(2,1)S(1)}, u32[]{:S(2)}, u32[]{:S(2)}) collective-permute-start(bf16[256,256]{1,0:T(8,128)(2,1)S(1)} %get-tuple-element.63), channel_id=1, source_target_pairs={{0,12},{4,8},{8,4},{12,0},{1,13},{5,9},{9,5},{13,1},{2,14},{6,10},... | collective-permute-start | bytes 393224 | tf_op jit(solution)/shard_map/cells_3_chunk_2/ppermute | solution.py:382
  36.9 1.2 %standardize.5 = (bf16[1024,1024]{1,0:T(8,128)(2,1)S(1)}, bf16[1024,1024]{1,0:T(8,128)(2,1)S(1)}, bf16[1024,256]{1,0:T(8,128)(2,1)S(1)}) custom-call(f32[8,1024]{1,0:T(8,128)S(1)} %broadcast_in_dim.3.mean_ref, bf16[256,256]{1,0:T(8,128)(2,1)S(1)} %get-tuple-element.74.refs_0_, ...), custom_call_target="tpu_custom_call", output_to_operand_aliasing={{0}: (9, {}), {1}: (10, {})} | custom-call | flops 20000000000 | bytes 1024 | tf_op jit(solution)/shard_map/standardize/pallas_call | solution.py:218
  38.1 1.6 %collective-permute-start.11 = (bf16[1024,256]{1,0:T(8,128)(2,1)S(1)}, bf16[1024,256]{1,0:T(8,128)(2,1)S(1)}, u32[]{:S(2)}, u32[]{:S(2)}) collective-permute-start(bf16[1024,256]{1,0:T(8,128)(2,1)S(1)} %get-tuple-element.80), channel_id=1, source_target_pairs={{0,2},{1,3},{2,0},{3,1},{4,6},{5,7},{6,4},{7,5},{8,10},{9,11},{10,... | collective-permute-start | bytes 1572872 | tf_op jit(solution)/shard_map/far_1/ppermute | solution.py:385
  39.6 5.6 %collective-permute-done.9.refs_3_ = bf16[256,256]{1,0:T(8,128)(2,1)S(1)} collective-permute-done((bf16[256,256]{1,0:T(8,128)(2,1)S(1)}, bf16[256,256]{1,0:T(8,128)(2,1)S(1)}, u32[]{:S(2)}, u32[]{:S(2)}) %collective-permute-start.9) | collective-permute-done | bytes 131104 | tf_op jit(solution)/shard_map/cells_2_chunk_2/ppermute | solution.py:382
  45.2 0.8 %collective-permute-start.13 = (bf16[256,256]{1,0:T(8,128)(2,1)S(1)}, bf16[256,256]{1,0:T(8,128)(2,1)S(1)}, u32[]{:S(2)}, u32[]{:S(2)}) collective-permute-start(bf16[256,256]{1,0:T(8,128)(2,1)S(1)} %get-tuple-element.88), channel_id=1, source_target_pairs={{0,4},{4,0},{8,12},{12,8},{1,5},{5,1},{9,13},{13,9},{2,6},{6,2},{1... | collective-permute-start | bytes 393224 | tf_op jit(solution)/shard_map/cells_1_chunk_3/ppermute | solution.py:382
  46.0 3.6 %collective-permute-start.12 = (bf16[256,256]{1,0:T(8,128)(2,1)S(1)}, bf16[256,256]{1,0:T(8,128)(2,1)S(1)}, u32[]{:S(2)}, u32[]{:S(2)}) collective-permute-start(bf16[256,256]{1,0:T(8,128)(2,1)S(1)} %get-tuple-element.86), channel_id=1, source_target_pairs={{0,12},{4,8},{8,4},{12,0},{1,13},{5,9},{9,5},{13,1},{2,14},{6,10},... | collective-permute-start | bytes 393224 | tf_op jit(solution)/shard_map/cells_3_chunk_3/ppermute | solution.py:382
  49.6 0.0 collective-permute-done.3.refs_8_
  49.6 1.2 %standardize.6 = (bf16[1024,1024]{1,0:T(8,128)(2,1)S(1)}, bf16[1024,1024]{1,0:T(8,128)(2,1)S(1)}, f32[8,128]{1,0:T(8,128)S(1)}, bf16[1024,256]{1,0:T(8,128)(2,1)S(1)}) custom-call(f32[8,1024]{1,0:T(8,128)S(1)} %broadcast_in_dim.3.mean_ref, bf16[256,256]{1,0:T(8,128)(2,1)S(1)} %get-tuple-element.59.refs_0_, ...), custom_call_target="tpu_custom_call", output_to_operand_aliasing={{0}: (9, {}), {1}: (10, {})} | custom-call | flops 20000000000 | bytes 1024 | tf_op jit(solution)/shard_map/standardize/pallas_call | solution.py:218
  50.8 1.6 %collective-permute-start.18 = (bf16[1024,256]{1,0:T(8,128)(2,1)S(1)}, bf16[1024,256]{1,0:T(8,128)(2,1)S(1)}, u32[]{:S(2)}, u32[]{:S(2)}) collective-permute-start(bf16[1024,256]{1,0:T(8,128)(2,1)S(1)} %get-tuple-element.96), channel_id=1, source_target_pairs={{0,2},{1,3},{2,0},{3,1},{4,6},{5,7},{6,4},{7,5},{8,10},{9,11},{10,... | collective-permute-start | bytes 1572872 | tf_op jit(solution)/shard_map/far_2/ppermute | solution.py:385
  52.4 2.2 %gram.6.refs_2_ = bf16[1,1024,4096]{2,1,0:T(8,128)(2,1)} custom-call(f32[8,128]{1,0:T(8,128)S(1)} %get-tuple-element.79.count_ref, bf16[1024,1024]{1,0:T(8,128)(2,1)S(1)} %get-tuple-element.82.left_ref.refs_10_, bf16[1024,1024]{1,0:T(8,128)(2,1)S(1)} %get-tuple-element.83.refs_0_.refs_11_), custom_call_target="tpu_custom_call" | custom-call | flops 1024 | bytes 1024 | tf_op jit(solution)/shard_map/gram/pallas_call | solution.py:344
  54.6 0.5 collective-permute-done.14.refs_3_
  55.1 0.0 collective-permute-done.12.refs_1_
  55.1 1.3 %standardize.7 = (bf16[1024,1024]{1,0:T(8,128)(2,1)S(1)}, bf16[1024,1024]{1,0:T(8,128)(2,1)S(1)}, bf16[1024,512]{1,0:T(8,128)(2,1)S(1)}, bf16[784,256]{1,0:T(8,128)(2,1)S(1)}) custom-call(f32[8,1024]{1,0:T(8,128)S(1)} %broadcast_in_dim.3.mean_ref, bf16[256,256]{1,0:T(8,128)(2,1)S(1)} %get-tuple-element.84.refs_0_, ...), custom_call_target="tpu_custom_call", output_to_operand_aliasing={{0}: (11, {}), {1}: (12, {})} | custom-call | flops 20000000000 | bytes 1024 | tf_op jit(solution)/shard_map/standardize/pallas_call | solution.py:218
  56.4 0.1 collective-permute-start.16
  56.5 1.9 %gram.7.refs_2_ = bf16[1,1024,4096]{2,1,0:T(8,128)(2,1)} custom-call(f32[8,128]{1,0:T(8,128)S(1)} %get-tuple-element.79.count_ref, bf16[1024,1024]{1,0:T(8,128)(2,1)S(1)} %get-tuple-element.91.left_ref, bf16[1024,1024]{1,0:T(8,128)(2,1)S(1)} %get-tuple-element.93.refs_0_.refs_1_, ...), custom_call_target="tpu_custom_call", output_to_operand_aliasing={{}: (4, {})} | custom-call | flops 1024 | bytes 1024 | tf_op jit(solution)/shard_map/gram/pallas_call | solution.py:344
  58.4 0.6 collective-permute-start.17
  59.0 1.5 %collective-permute-start.15 = (bf16[784,256]{1,0:T(8,128)(2,1)S(1)}, bf16[784,256]{1,0:T(8,128)(2,1)S(1)}, u32[]{:S(2)}, u32[]{:S(2)}) collective-permute-start(bf16[784,256]{1,0:T(8,128)(2,1)S(1)} %get-tuple-element.94), channel_id=1, source_target_pairs={{0,2},{1,3},{2,0},{3,1},{4,6},{5,7},{6,4},{7,5},{8,10},{9,11},{10,... | collective-permute-start | bytes 1204232 | tf_op jit(solution)/shard_map/ppermute | solution.py:385
  60.5 0.7 collective-permute-done.18.refs_1_
  61.2 0.0 collective-permute-start.19
  61.2 2.9 %gram.8.refs_3_ = bf16[1,1024,4096]{2,1,0:T(8,128)(2,1)} custom-call(f32[8,128]{1,0:T(8,128)S(1)} %get-tuple-element.79.count_ref, bf16[1024,1024]{1,0:T(8,128)(2,1)S(1)} %get-tuple-element.91.left_ref, bf16[1024,512]{1,0:T(8,128)(2,1)S(1)} %get-tuple-element.95.refs_0_, ...), custom_call_target="tpu_custom_call", output_to_operand_aliasing={{}: (4, {})} | custom-call | flops 20000000000 | bytes 1024 | tf_op jit(solution)/shard_map/gram/pallas_call | solution.py:344
  64.1 0.0 collective-permute-done.19.refs_2_
  64.1 0.0 collective-permute-done.17.refs_1_
  64.1 6.1 %gram.9.refs_1_ = bf16[1,1024,4096]{2,1,0:T(8,128)(2,1)} custom-call(f32[8,128]{1,0:T(8,128)S(1)} %get-tuple-element.79.count_ref, bf16[1024,1024]{1,0:T(8,128)(2,1)S(1)} %get-tuple-element.91.left_ref, bf16[1024,1024]{1,0:T(8,128)(2,1)S(1)} %collective-permute-done.16.refs_0_, ...), custom_call_target="tpu_custom_call", output_to_operand_aliasing={{}: (5, {})} | custom-call | flops 1024 | bytes 1024 | tf_op jit(solution)/shard_map/gram/pallas_call | solution.py:344
  70.2 0.1 collective-permute-done.15.sent_ref
  70.3 0.2 finish.1.refs_0_
  70.5 0.5 collective-permute-start.20
  71.0 1.5 %gram.10.refs_1_ = bf16[1,1024,4096]{2,1,0:T(8,128)(2,1)} custom-call(f32[8,128]{1,0:T(8,128)S(1)} %get-tuple-element.79.count_ref, bf16[1024,1024]{1,0:T(8,128)(2,1)S(1)} %get-tuple-element.91.left_ref, bf16[1024,256]{1,0:T(8,128)(2,1)S(1)} %finish.1.refs_0_, bf16[1,1024,4096]{2,1,0:T(8,128)(2,1)} %gram.9.refs_1_), custom_call_target="tpu_custom_call", output_to_operand_aliasing={{}: (3, {})} | custom-call | flops 1024 | bytes 1024 | tf_op jit(solution)/shard_map/gram/pallas_call | solution.py:344
  72.5 0.0 collective-permute-done.20.refs_0_
  72.5 1.5 %gram.11 = bf16[1,1024,4096]{2,1,0:T(8,128)(2,1)} custom-call(f32[8,128]{1,0:T(8,128)S(1)} %get-tuple-element.79.count_ref, bf16[1024,1024]{1,0:T(8,128)(2,1)S(1)} %get-tuple-element.91.left_ref, bf16[1024,256]{1,0:T(8,128)(2,1)S(1)} %collective-permute-done.20.refs_0_, bf16[1,1024,4096]{2,1,0:T(8,128)(2,1)} %gram.10.refs_1_), custom_call_target="tpu_custom_call", output_to_operand_aliasing={{}: (3, {})} | custom-call | flops 1024 | bytes 1024 | tf_op jit(solution)/shard_map/gram/pallas_call | solution.py:344
  (13 shorter events, 0.0 us)
Async XLA Ops:
  0.0 1.2 %copy-start = (bf16[512,1024]{1,0:T(8,128)(2,1)S(1)}, bf16[512,1024]{1,0:T(8,128)(2,1)}, u32[]{:S(2)}) copy-start(bf16[512,1024]{1,0:T(8,128)(2,1)} %expr_ref.1) | copy-start | bytes 3145732
  1.2 0.7 copy-start.1
  1.9 0.7 copy-start.2
  4.3 10.7 %collective-permute-start = (bf16[272,256]{1,0:T(8,128)(2,1)S(1)}, bf16[272,256]{1,0:T(8,128)(2,1)S(1)}, u32[]{:S(2)}, u32[]{:S(2)}) collective-permute-start(bf16[272,256]{1,0:T(8,128)(2,1)S(1)} %get-tuple-element.55), channel_id=1, source_target_pairs={{0,12},{4,8},{8,4},{12,0},{1,13},{5,9},{9,5},{13,1},{2,14},{6,10},... | collective-permute-start | bytes 417800 | tf_op jit(solution)/shard_map/cells_3_chunk_0/ppermute | solution.py:382
  9.4 10.1 %collective-permute-start.1 = (bf16[272,256]{1,0:T(8,128)(2,1)S(1)}, bf16[272,256]{1,0:T(8,128)(2,1)S(1)}, u32[]{:S(2)}, u32[]{:S(2)}) collective-permute-start(bf16[272,256]{1,0:T(8,128)(2,1)S(1)} %get-tuple-element.56), channel_id=1, source_target_pairs={{0,4},{4,0},{8,12},{12,8},{1,5},{5,1},{9,13},{13,9},{2,6},{6,2},{1... | collective-permute-start | bytes 417800 | tf_op jit(solution)/shard_map/cells_1_chunk_0/ppermute | solution.py:382
  9.4 17.0 %collective-permute-start.2 = (bf16[272,256]{1,0:T(8,128)(2,1)S(1)}, bf16[272,256]{1,0:T(8,128)(2,1)S(1)}, u32[]{:S(2)}, u32[]{:S(2)}) collective-permute-start(bf16[272,256]{1,0:T(8,128)(2,1)S(1)} %get-tuple-element.57), channel_id=1, source_target_pairs={{0,8},{4,12},{8,0},{12,4},{1,9},{5,13},{9,1},{13,5},{2,10},{6,14},... | collective-permute-start | bytes 417800 | tf_op jit(solution)/shard_map/cells_2_chunk_0/ppermute | solution.py:382
  10.1 5.0 %collective-permute-start.10 = (bf16[256,256]{1,0:T(8,128)(2,1)S(1)}, bf16[256,256]{1,0:T(8,128)(2,1)S(1)}, u32[]{:S(2)}, u32[]{:S(2)}) collective-permute-start(bf16[256,256]{1,0:T(8,128)(2,1)S(1)} %get-tuple-element.84.refs_0_), channel_id=1, source_target_pairs={{0,2},{1,3},{2,0},{3,1},{4,6},{5,7},{6,4},{7,5},{8,10},{9,11},{10,... | collective-permute-start | bytes 393224 | tf_op jit(solution)/shard_map/far_local/ppermute | solution.py:385
  15.7 19.8 %collective-permute-start.4 = (bf16[256,256]{1,0:T(8,128)(2,1)S(1)}, bf16[256,256]{1,0:T(8,128)(2,1)S(1)}, u32[]{:S(2)}, u32[]{:S(2)}) collective-permute-start(bf16[256,256]{1,0:T(8,128)(2,1)S(1)} %get-tuple-element.62), channel_id=1, source_target_pairs={{0,12},{4,8},{8,4},{12,0},{1,13},{5,9},{9,5},{13,1},{2,14},{6,10},... | collective-permute-start | bytes 393224 | tf_op jit(solution)/shard_map/cells_3_chunk_1/ppermute | solution.py:382
  19.5 13.0 %collective-permute-start.6 = (bf16[256,256]{1,0:T(8,128)(2,1)S(1)}, bf16[256,256]{1,0:T(8,128)(2,1)S(1)}, u32[]{:S(2)}, u32[]{:S(2)}) collective-permute-start(bf16[256,256]{1,0:T(8,128)(2,1)S(1)} %get-tuple-element.66), channel_id=1, source_target_pairs={{0,4},{4,0},{8,12},{12,8},{1,5},{5,1},{9,13},{13,9},{2,6},{6,2},{1... | collective-permute-start | bytes 393224 | tf_op jit(solution)/shard_map/cells_1_chunk_1/ppermute | solution.py:382
  26.4 6.1 %collective-permute-start.8 = (bf16[256,256]{1,0:T(8,128)(2,1)S(1)}, bf16[256,256]{1,0:T(8,128)(2,1)S(1)}, u32[]{:S(2)}, u32[]{:S(2)}) collective-permute-start(bf16[256,256]{1,0:T(8,128)(2,1)S(1)} %get-tuple-element.70), channel_id=1, source_target_pairs={{0,8},{4,12},{8,0},{12,4},{1,9},{5,13},{9,1},{13,5},{2,10},{6,14},... | collective-permute-start | bytes 393224 | tf_op jit(solution)/shard_map/cells_2_chunk_1/ppermute | solution.py:382
  27.6 22.0 %collective-permute-start.3 = (bf16[1024,256]{1,0:T(8,128)(2,1)S(1)}, bf16[1024,256]{1,0:T(8,128)(2,1)S(1)}, u32[]{:S(2)}, u32[]{:S(2)}) collective-permute-start(bf16[1024,256]{1,0:T(8,128)(2,1)S(1)} %get-tuple-element.58), channel_id=1, source_target_pairs={{0,2},{1,3},{2,0},{3,1},{4,6},{5,7},{6,4},{7,5},{8,10},{9,11},{10,... | collective-permute-start | bytes 1572872 | tf_op jit(solution)/shard_map/far_0/ppermute | solution.py:385
  32.5 12.7 %collective-permute-start.9 = (bf16[256,256]{1,0:T(8,128)(2,1)S(1)}, bf16[256,256]{1,0:T(8,128)(2,1)S(1)}, u32[]{:S(2)}, u32[]{:S(2)}) collective-permute-start(bf16[256,256]{1,0:T(8,128)(2,1)S(1)} %get-tuple-element.71), channel_id=1, source_target_pairs={{0,8},{4,12},{8,0},{12,4},{1,9},{5,13},{9,1},{13,5},{2,10},{6,14},... | collective-permute-start | bytes 393224 | tf_op jit(solution)/shard_map/cells_2_chunk_2/ppermute | solution.py:382
  32.5 12.7 %collective-permute-start.7 = (bf16[256,256]{1,0:T(8,128)(2,1)S(1)}, bf16[256,256]{1,0:T(8,128)(2,1)S(1)}, u32[]{:S(2)}, u32[]{:S(2)}) collective-permute-start(bf16[256,256]{1,0:T(8,128)(2,1)S(1)} %get-tuple-element.67), channel_id=1, source_target_pairs={{0,4},{4,0},{8,12},{12,8},{1,5},{5,1},{9,13},{13,9},{2,6},{6,2},{1... | collective-permute-start | bytes 393224 | tf_op jit(solution)/shard_map/cells_1_chunk_2/ppermute | solution.py:382
  35.5 10.5 %collective-permute-start.5 = (bf16[256,256]{1,0:T(8,128)(2,1)S(1)}, bf16[256,256]{1,0:T(8,128)(2,1)S(1)}, u32[]{:S(2)}, u32[]{:S(2)}) collective-permute-start(bf16[256,256]{1,0:T(8,128)(2,1)S(1)} %get-tuple-element.63), channel_id=1, source_target_pairs={{0,12},{4,8},{8,4},{12,0},{1,13},{5,9},{9,5},{13,1},{2,14},{6,10},... | collective-permute-start | bytes 393224 | tf_op jit(solution)/shard_map/cells_3_chunk_2/ppermute | solution.py:382
  38.1 16.5 %collective-permute-start.11 = (bf16[1024,256]{1,0:T(8,128)(2,1)S(1)}, bf16[1024,256]{1,0:T(8,128)(2,1)S(1)}, u32[]{:S(2)}, u32[]{:S(2)}) collective-permute-start(bf16[1024,256]{1,0:T(8,128)(2,1)S(1)} %get-tuple-element.80), channel_id=1, source_target_pairs={{0,2},{1,3},{2,0},{3,1},{4,6},{5,7},{6,4},{7,5},{8,10},{9,11},{10,... | collective-permute-start | bytes 1572872 | tf_op jit(solution)/shard_map/far_1/ppermute | solution.py:385
  45.2 9.9 %collective-permute-start.14 = (bf16[256,256]{1,0:T(8,128)(2,1)S(1)}, bf16[256,256]{1,0:T(8,128)(2,1)S(1)}, u32[]{:S(2)}, u32[]{:S(2)}) collective-permute-start(bf16[256,256]{1,0:T(8,128)(2,1)S(1)} %get-tuple-element.90), channel_id=1, source_target_pairs={{0,8},{4,12},{8,0},{12,4},{1,9},{5,13},{9,1},{13,5},{2,10},{6,14},... | collective-permute-start | bytes 393224 | tf_op jit(solution)/shard_map/cells_2_chunk_3/ppermute | solution.py:382
  45.2 9.9 %collective-permute-start.13 = (bf16[256,256]{1,0:T(8,128)(2,1)S(1)}, bf16[256,256]{1,0:T(8,128)(2,1)S(1)}, u32[]{:S(2)}, u32[]{:S(2)}) collective-permute-start(bf16[256,256]{1,0:T(8,128)(2,1)S(1)} %get-tuple-element.88), channel_id=1, source_target_pairs={{0,4},{4,0},{8,12},{12,8},{1,5},{5,1},{9,13},{13,9},{2,6},{6,2},{1... | collective-permute-start | bytes 393224 | tf_op jit(solution)/shard_map/cells_1_chunk_3/ppermute | solution.py:382
  46.0 9.1 %collective-permute-start.12 = (bf16[256,256]{1,0:T(8,128)(2,1)S(1)}, bf16[256,256]{1,0:T(8,128)(2,1)S(1)}, u32[]{:S(2)}, u32[]{:S(2)}) collective-permute-start(bf16[256,256]{1,0:T(8,128)(2,1)S(1)} %get-tuple-element.86), channel_id=1, source_target_pairs={{0,12},{4,8},{8,4},{12,0},{1,13},{5,9},{9,5},{13,1},{2,14},{6,10},... | collective-permute-start | bytes 393224 | tf_op jit(solution)/shard_map/cells_3_chunk_3/ppermute | solution.py:382
  50.8 10.4 %collective-permute-start.18 = (bf16[1024,256]{1,0:T(8,128)(2,1)S(1)}, bf16[1024,256]{1,0:T(8,128)(2,1)S(1)}, u32[]{:S(2)}, u32[]{:S(2)}) collective-permute-start(bf16[1024,256]{1,0:T(8,128)(2,1)S(1)} %get-tuple-element.96), channel_id=1, source_target_pairs={{0,2},{1,3},{2,0},{3,1},{4,6},{5,7},{6,4},{7,5},{8,10},{9,11},{10,... | collective-permute-start | bytes 1572872 | tf_op jit(solution)/shard_map/far_2/ppermute | solution.py:385
  56.4 7.7 %collective-permute-start.16 = (bf16[1024,1024]{1,0:T(8,128)(2,1)S(1)}, bf16[1024,1024]{1,0:T(8,128)(2,1)S(1)}, u32[]{:S(2)}, u32[]{:S(2)}) collective-permute-start(bf16[1024,1024]{1,0:T(8,128)(2,1)S(1)} %get-tuple-element.93.refs_0_.refs_1_), channel_id=1, source_target_pairs={{0,1},{1,0},{2,3},{3,2},{4,5},{5,4},{6,7},{7,6},{8,9},{9,8},{10,11... | collective-permute-start | bytes 6291464 | tf_op jit(solution)/shard_map/near/ppermute | solution.py:389
  58.4 5.7 %collective-permute-start.17 = (bf16[1024,512]{1,0:T(8,128)(2,1)S(1)}, bf16[1024,512]{1,0:T(8,128)(2,1)S(1)}, u32[]{:S(2)}, u32[]{:S(2)}) collective-permute-start(bf16[1024,512]{1,0:T(8,128)(2,1)S(1)} %get-tuple-element.95.refs_0_), channel_id=1, source_target_pairs={{0,1},{1,0},{2,3},{3,2},{4,5},{5,4},{6,7},{7,6},{8,9},{9,8},{10,11... | collective-permute-start | bytes 3145736 | tf_op jit(solution)/shard_map/far_near/ppermute | solution.py:389
  59.0 11.3 %collective-permute-start.15 = (bf16[784,256]{1,0:T(8,128)(2,1)S(1)}, bf16[784,256]{1,0:T(8,128)(2,1)S(1)}, u32[]{:S(2)}, u32[]{:S(2)}) collective-permute-start(bf16[784,256]{1,0:T(8,128)(2,1)S(1)} %get-tuple-element.94), channel_id=1, source_target_pairs={{0,2},{1,3},{2,0},{3,1},{4,6},{5,7},{6,4},{7,5},{8,10},{9,11},{10,... | collective-permute-start | bytes 1204232 | tf_op jit(solution)/shard_map/ppermute | solution.py:385
  61.2 2.9 %collective-permute-start.19 = (bf16[1024,256]{1,0:T(8,128)(2,1)S(1)}, bf16[1024,256]{1,0:T(8,128)(2,1)S(1)}, u32[]{:S(2)}, u32[]{:S(2)}) collective-permute-start(bf16[1024,256]{1,0:T(8,128)(2,1)S(1)} %collective-permute-done.18.refs_1_), channel_id=1, source_target_pairs={{0,1},{1,0},{2,3},{3,2},{4,5},{5,4},{6,7},{7,6},{8,9},{9,8},{10,11... | collective-permute-start | bytes 1572872 | tf_op jit(solution)/shard_map/far_near_2/ppermute | solution.py:389
  70.5 2.1 %collective-permute-start.20 = (bf16[1024,256]{1,0:T(8,128)(2,1)S(1)}, bf16[1024,256]{1,0:T(8,128)(2,1)S(1)}, u32[]{:S(2)}, u32[]{:S(2)}) collective-permute-start(bf16[1024,256]{1,0:T(8,128)(2,1)S(1)} %finish.1.refs_0_), channel_id=1, source_target_pairs={{0,1},{1,0},{2,3},{3,2},{4,5},{5,4},{6,7},{7,6},{8,9},{9,8},{10,11... | collective-permute-start | bytes 1572872 | tf_op jit(solution)/shard_map/far_near_3/ppermute | solution.py:389
